TPU v7x, 32 devices: a whole 2x2x4 slice. The times are simulated.
32 devices in a mesh: stn: 2 (over core), tm: 8 (over z, x), ct: 2 (over y).
Axes of the slice: x: 2, y: 2, z: 4, core: 2. Of those that a mesh axis runs over, the one named last changes fastest.
Arguments:
- voltages: bfloat16 [2, 32, 524288], P(None, ('stn', 'ct'), 'tm'), may hold values from -128 to 127, as said below
- delays: int32 [32], P(('stn', 'ct')), may hold values from 0 to 4095
Outputs:
- visibilities: float32 [2, 4096, 32, 32], P(None, ('tm', 'ct'), 'stn')
Inputs may be any that keep to these rules, and one draw needn't show every extreme that they name: `voltages`: every entry is a whole number.
All inputs are finite; a program needn't handle non-finite values.
Results may differ from a plain program's by a relative error of at most 0.0037.
Values may be sent and summed in bfloat16 or wider, within the bound.
No kernel may reach another device: no remote copies, remote signals or barrier semaphores. Data moves between devices by JAX's collectives and lax.ppermute only.
A program may use at most 128 MiB of HBM per device.

v0:
```python
import math

import jax
import jax.numpy as jnp
from jax import lax
from jax.sharding import PartitionSpec as P

CHANNELS = 4096
RADIX = 64
TAPS = 16


def passed_along(block, axis, distance):
    devices = range(lax.axis_size(axis))
    route = [(i - distance, i) for i in devices if i - distance in devices]
    return lax.ppermute(block, axis, route)


def filter_table():
    length = TAPS * CHANNELS
    index = jnp.arange(length, dtype=jnp.int32).astype(jnp.float32)
    centred = (index - length / 2) / CHANNELS
    window = 0.5 - 0.5 * jnp.cos(2.0 * math.pi * index / length)
    factor = 1.0 / (48.0 * math.sqrt(CHANNELS))
    return (jnp.sinc(centred) * window * factor).reshape(TAPS, CHANNELS)


def dft_block(radix):
    steps = jnp.arange(radix, dtype=jnp.int32)
    grid = steps[:, None] * steps[None, :] % radix
    angle = 2.0 * math.pi * grid.astype(jnp.float32) / radix
    cosine = jnp.cos(angle)
    sine = jnp.sin(angle)
    upper = jnp.concatenate([cosine, sine], axis=1)
    lower = jnp.concatenate([-sine, cosine], axis=1)
    return jnp.concatenate([upper, lower], axis=0).astype(jnp.bfloat16)


def twiddles():
    second = CHANNELS // RADIX
    rows = jnp.arange(second, dtype=jnp.int32)
    cols = jnp.arange(RADIX, dtype=jnp.int32)
    grid = rows[:, None] * cols[None, :] % CHANNELS
    angle = 2.0 * math.pi * grid.astype(jnp.float32) / CHANNELS
    return (jnp.cos(angle), jnp.sin(angle))


def filtered(framed, table):
    count = framed.shape[-2] - TAPS + 1
    total = jnp.zeros(framed.shape[:-2] + (count, CHANNELS), jnp.float32)
    for tap in range(TAPS):
        begin = TAPS - 1 - tap
        total = total + table[tap] * framed[..., begin : begin + count, :].astype(jnp.float32)
    return total.astype(jnp.bfloat16)


def transform(branches):
    second = CHANNELS // RADIX
    number = branches.shape[0]
    stacked = branches.reshape(number, 2 * second, RADIX)
    inner = jnp.einsum(
        "kj,nja->nka", dft_block(second), stacked, preferred_element_type=jnp.float32
    )
    inner = inner.reshape(number, 2, second, RADIX)
    tw_cos, tw_sin = twiddles()
    real_part = inner[:, 0] * tw_cos + inner[:, 1] * tw_sin
    imag_part = inner[:, 1] * tw_cos - inner[:, 0] * tw_sin
    turned = (
        jnp.stack([real_part, imag_part], axis=2)
        .reshape(number, second, 2 * RADIX)
        .astype(jnp.bfloat16)
    )
    result = jnp.einsum("lj,nkj->nlk", dft_block(RADIX), turned, preferred_element_type=jnp.float32)
    return result.reshape(number, 2, CHANNELS).astype(jnp.bfloat16)


def pick_span(row, offset, span):
    return lax.dynamic_slice_in_dim(row, CHANNELS - offset, span, 1)


def on_device(voltages, delays):
    in_count = voltages.shape[1]
    frame_count = voltages.shape[2] // CHANNELS
    prior = passed_along(voltages, "tm", 1)
    extended = jnp.concatenate([prior, voltages], axis=2)
    span = (frame_count + TAPS - 1) * CHANNELS
    shifted = jax.vmap(
        lambda row, offset: pick_span(row, offset, span), in_axes=(1, 0), out_axes=1
    )(extended, delays)
    framed = shifted.reshape(2, in_count, frame_count + TAPS - 1, CHANNELS)
    branches = jnp.moveaxis(filtered(framed, filter_table()), 0, 2)
    spectra = transform(branches.reshape(in_count * frame_count, 2, CHANNELS))
    spectra = spectra.reshape(in_count, frame_count, 2, CHANNELS)
    moved = lax.all_to_all(
        lax.all_to_all(spectra, "tm", split_axis=3, concat_axis=1, tiled=True),
        "ct",
        split_axis=3,
        concat_axis=0,
        tiled=True,
    )
    local = moved.transpose(3, 2, 0, 1)
    total_frames = local.shape[3]
    swapped = jnp.stack([local[:, 1], -local[:, 0]], axis=1)
    left = jnp.stack([local, swapped], axis=0)
    summed = jnp.einsum(
        "ocjaf,cjbf->ocab",
        left,
        lax.all_gather(local, "stn", axis=2, tiled=True),
        preferred_element_type=jnp.float32,
    )
    return summed * (1.0 / total_frames)


def solution(mesh):
    return jax.shard_map(
        on_device,
        mesh=mesh,
        in_specs=(P(None, ("stn", "ct"), "tm"), P(("stn", "ct"))),
        out_specs=P(None, ("tm", "ct"), "stn", None),
        check_vma=False,
    )
```

profile of v0, /device:TPU:0, one launch (start us, length us, event | category | flops | bytes accessed | tf_op | source)
XLA Modules:
  0.0 328.2 jit_solution(3180392282420654220)
XLA Ops:
  6.5 3.8 %copy.57 = bf16[2,8,65536]{2,0,1:T(2,128)(2,1)S(1)} copy(bf16[2,8,65536]{2,1,0:T(8,128)(2,1)} %param.2) | data formatting | bytes 4194304 | tf_op args[0]
  10.3 6.2 %collective-permute-start = (bf16[2,8,65536]{2,0,1:T(2,128)(2,1)S(1)}, bf16[2,8,65536]{2,0,1:T(2,128)(2,1)}, u32[]{:S(2)}, u32[]{:S(2)}) collective-permute-start(bf16[2,8,65536]{2,0,1:T(2,128)(2,1)S(1)} %copy.57), channel_id=1, source_target_pairs={{0,2},{2,4},{4,6},{6,8},{8,10},{10,12},{12,14},{1,3},{3,5},{5,7},{... | collective-permute-start | bytes 6291464 | tf_op jit(solution)/shard_map/ppermute | solution.py:16
  17.0 1.2 fusion.24
  18.2 41.8 %collective-permute-done = bf16[2,8,65536]{2,0,1:T(2,128)(2,1)} collective-permute-done((bf16[2,8,65536]{2,0,1:T(2,128)(2,1)S(1)}, bf16[2,8,65536]{2,0,1:T(2,128)(2,1)}, u32[]{:S(2)}, u32[]{:S(2)}) %collective-permute-start) | collective-permute-done | bytes 2097184 | tf_op jit(solution)/shard_map/ppermute | solution.py:16
  60.0 7.1 %maximum_bitcast_fusion = bf16[8,2,131072]{2,1,0:T(2,128)(2,1)} fusion(bf16[2,8,65536]{2,0,1:T(2,128)(2,1)S(1)} %copy.57, bf16[2,8,65536]{2,0,1:T(2,128)(2,1)} %collective-permute-done), kind=kLoop, calls=%fused_computation.2 | loop fusion | flops 8388608 | bytes 8388608 | tf_op jit(solution)/shard_map/vmap()/transpose | solution.py:78
  67.2 34.8 %while.1 = (s32[]{:T(128)}, bf16[8,2,131072]{2,1,0:T(2,128)(2,1)}, s32[8,3]{0,1:T(4,128)S(1)}, bf16[8,2,126976]{2,1,0:T(2,128)(2,1)}, s32[]{:T(128)}) while((s32[]{:T(128)}, bf16[8,2,131072]{2,1,0:T(2,128)(2,1)}, s32[8,3]{0,1:T(4,128)S(1)}, bf16[8,2,126976]{2,1,0:T(2,128)(2,1)}, s32[]{:T(128)}) %tuple.41), condition=%wide.while_cond, body=%wide.while_body.sunk | while | flops 2 | bytes 1016949 | solution.py:78
  67.2 0.6 fusion.52
  67.8 3.7 %dynamic-slice_dynamic-update-slice_fusion.2 = bf16[8,2,126976]{2,1,0:T(2,128)(2,1)} fusion(bf16[8,2,126976]{2,1,0:T(2,128)(2,1)} %get-tuple-element.88, s32[]{:T(128)S(6)} %copy.97, bf16[8,2,131072]{2,1,0:T(2,128)(2,1)} %get-tuple-element.91, s32[]{:T(128)} %bitcast.73, s32[]{:T(128)} %bitcast.74), kind=kLoop, calls=%fused_computation.clone.1 | loop fusion | bytes 1016836 | tf_op jit(solution)/shard_map/vmap()/gather
  71.6 0.6 fusion.52
  72.2 3.7 %dynamic-slice_dynamic-update-slice_fusion.2 = bf16[8,2,126976]{2,1,0:T(2,128)(2,1)} fusion(bf16[8,2,126976]{2,1,0:T(2,128)(2,1)} %get-tuple-element.88, s32[]{:T(128)S(6)} %copy.97, bf16[8,2,131072]{2,1,0:T(2,128)(2,1)} %get-tuple-element.91, s32[]{:T(128)} %bitcast.73, s32[]{:T(128)} %bitcast.74), kind=kLoop, calls=%fused_computation.clone.1 | loop fusion | bytes 1016836 | tf_op jit(solution)/shard_map/vmap()/gather
  75.9 0.6 fusion.52
  76.5 3.7 %dynamic-slice_dynamic-update-slice_fusion.2 = bf16[8,2,126976]{2,1,0:T(2,128)(2,1)} fusion(bf16[8,2,126976]{2,1,0:T(2,128)(2,1)} %get-tuple-element.88, s32[]{:T(128)S(6)} %copy.97, bf16[8,2,131072]{2,1,0:T(2,128)(2,1)} %get-tuple-element.91, s32[]{:T(128)} %bitcast.73, s32[]{:T(128)} %bitcast.74), kind=kLoop, calls=%fused_computation.clone.1 | loop fusion | bytes 1016836 | tf_op jit(solution)/shard_map/vmap()/gather
  80.3 0.6 fusion.52
  80.9 3.7 %dynamic-slice_dynamic-update-slice_fusion.2 = bf16[8,2,126976]{2,1,0:T(2,128)(2,1)} fusion(bf16[8,2,126976]{2,1,0:T(2,128)(2,1)} %get-tuple-element.88, s32[]{:T(128)S(6)} %copy.97, bf16[8,2,131072]{2,1,0:T(2,128)(2,1)} %get-tuple-element.91, s32[]{:T(128)} %bitcast.73, s32[]{:T(128)} %bitcast.74), kind=kLoop, calls=%fused_computation.clone.1 | loop fusion | bytes 1016836 | tf_op jit(solution)/shard_map/vmap()/gather
  84.6 0.6 fusion.52
  85.2 3.7 %dynamic-slice_dynamic-update-slice_fusion.2 = bf16[8,2,126976]{2,1,0:T(2,128)(2,1)} fusion(bf16[8,2,126976]{2,1,0:T(2,128)(2,1)} %get-tuple-element.88, s32[]{:T(128)S(6)} %copy.97, bf16[8,2,131072]{2,1,0:T(2,128)(2,1)} %get-tuple-element.91, s32[]{:T(128)} %bitcast.73, s32[]{:T(128)} %bitcast.74), kind=kLoop, calls=%fused_computation.clone.1 | loop fusion | bytes 1016836 | tf_op jit(solution)/shard_map/vmap()/gather
  89.0 0.6 fusion.52
  89.6 3.7 %dynamic-slice_dynamic-update-slice_fusion.2 = bf16[8,2,126976]{2,1,0:T(2,128)(2,1)} fusion(bf16[8,2,126976]{2,1,0:T(2,128)(2,1)} %get-tuple-element.88, s32[]{:T(128)S(6)} %copy.97, bf16[8,2,131072]{2,1,0:T(2,128)(2,1)} %get-tuple-element.91, s32[]{:T(128)} %bitcast.73, s32[]{:T(128)} %bitcast.74), kind=kLoop, calls=%fused_computation.clone.1 | loop fusion | bytes 1016836 | tf_op jit(solution)/shard_map/vmap()/gather
  93.3 0.6 fusion.52
  93.9 3.7 %dynamic-slice_dynamic-update-slice_fusion.2 = bf16[8,2,126976]{2,1,0:T(2,128)(2,1)} fusion(bf16[8,2,126976]{2,1,0:T(2,128)(2,1)} %get-tuple-element.88, s32[]{:T(128)S(6)} %copy.97, bf16[8,2,131072]{2,1,0:T(2,128)(2,1)} %get-tuple-element.91, s32[]{:T(128)} %bitcast.73, s32[]{:T(128)} %bitcast.74), kind=kLoop, calls=%fused_computation.clone.1 | loop fusion | bytes 1016836 | tf_op jit(solution)/shard_map/vmap()/gather
  97.7 0.6 fusion.52
  98.3 3.7 %dynamic-slice_dynamic-update-slice_fusion.2 = bf16[8,2,126976]{2,1,0:T(2,128)(2,1)} fusion(bf16[8,2,126976]{2,1,0:T(2,128)(2,1)} %get-tuple-element.88, s32[]{:T(128)S(6)} %copy.97, bf16[8,2,131072]{2,1,0:T(2,128)(2,1)} %get-tuple-element.91, s32[]{:T(128)} %bitcast.73, s32[]{:T(128)} %bitcast.74), kind=kLoop, calls=%fused_computation.clone.1 | loop fusion | bytes 1016836 | tf_op jit(solution)/shard_map/vmap()/gather
  102.0 4.4 %copy.59 = bf16[8,2,126976]{2,0,1:T(8,128)(2,1)S(1)} copy(bf16[8,2,126976]{2,1,0:T(2,128)(2,1)} %get-tuple-element.12) | data formatting | bytes 8126464 | tf_op jit(solution)/shard_map/vmap()/gather | solution.py:78
  106.4 8.8 %fusion.10 = bf16[8,16,2,4096]{3,0,1,2:T(8,128)(2,1)S(1)} fusion(bf16[2,8,31,4096]{3,1,2,0:T(8,128)(2,1)S(1)} %bitcast.75, f32[4096]{0:T(1024)S(1)} %get-tuple-element.32, f32[4096]{0:T(1024)S(1)} %get-tuple-element.33, f32[4096]{0:T(1024)S(1)} %get-tuple-element.34, f32[4096]{0:T(1024)S(1)} %get-tuple-element.35, f32[4096]{0:T(1024)S(1)} %get-tuple-element.36, ...), kind=kLoop, calls=%fused_computation.18 | loop fusion | flops 50331648 | bytes 35913728 | tf_op jit(solution)/shard_map/transpose | solution.py:91
  115.2 2.2 copy.60
  117.4 4.2 %reshape_reshape.3 = bf16[128,128,64]{2,1,0:T(8,128)(2,1)} reshape(bf16[8,16,2,4096]{3,2,1,0:T(2,128)(2,1)S(1)} %copy.60) | data formatting | bytes 4194304 | tf_op jit(solution)/shard_map/reshape;reshape | solution.py:60
  121.5 4.8 %copy.61 = bf16[128,128,64]{1,0,2:T(8,128)(2,1)S(1)} copy(bf16[128,128,64]{2,1,0:T(8,128)(2,1)} %reshape_reshape.3) | data formatting | bytes 4194304 | tf_op jit(solution)/shard_map/reshape;reshape | solution.py:60
  126.3 0.8 fusion.40
  127.1 0.6 fusion.46
  127.7 5.0 %add_convert_fusion.1 = (bf16[128,64,1,64]{0,3,2,1:T(8,128)(2,1)S(1)}, bf16[128,64,1,64]{0,3,2,1:T(8,128)(2,1)S(1)}) fusion(f32[128,1,64,64]{0,2,1,3:T(8,128)S(1)} %get-tuple-element.26, f32[128,1,64,64]{0,2,1,3:T(8,128)S(1)} %get-tuple-element.25, f32[64,64]{1,0:T(8,128)S(1)} %get-tuple-element.49, f32[64,64]{1,0:T(8,128)S(1)} %get-tuple-element.50), kind=kLoop, calls=%fused_computation.17 | loop fusion | flops 4194304 | bytes 6324224 | tf_op jit(solution)/shard_map/convert
  132.7 0.2 pad_maximum_fusion
  132.9 0.8 convert_bitcast_fusion
  133.7 3.9 %copy.65 = bf16[128,128,64]{2,1,0:T(8,128)(2,1)} copy(bf16[128,128,64]{1,0,2:T(8,128)(2,1)S(1)} %convert_bitcast_fusion) | data formatting | bytes 4194304 | tf_op jit(solution)/shard_map/convert_element_type | solution.py:74
  137.6 6.7 %convert_element_type.154 = bf16[8,16,2,4096]{3,2,1,0:T(2,128)(2,1)S(1)} reshape(bf16[128,128,64]{2,1,0:T(8,128)(2,1)} %copy.65) | data formatting | bytes 4194304 | tf_op jit(solution)/shard_map/convert_element_type | solution.py:74
  144.3 16.7 %copy.66 = bf16[8,16,2,4096]{1,0,2,3:T(8,128)(2,1)} copy(bf16[8,16,2,4096]{3,2,1,0:T(2,128)(2,1)S(1)} %convert_element_type.154) | data formatting | bytes 4194304 | tf_op jit(solution)/shard_map/convert_element_type | solution.py:74
  161.0 18.8 %reshape.171 = bf16[8,2,65536]{2,1,0:T(2,128)(2,1)S(1)} reshape(bf16[4096,2,8,16]{3,2,1,0:T(8,128)(2,1)} %bitcast.76) | data formatting | bytes 4194304
  179.9 54.3 %all_to_all.36 = bf16[8,2,65536]{2,1,0:T(2,128)(2,1)} all-to-all(bf16[8,2,65536]{2,1,0:T(2,128)(2,1)S(1)} %reshape.171), channel_id=1, replica_groups=mesh['stn'=2,'tm'=8,'ct'=2] {'tm'}, dimensions={0} | all-to-all | bytes 4194304 | tf_op jit(solution)/shard_map/all_to_all | solution.py:95
  234.2 13.9 %reshape.172 = bf16[4096,2,8,16]{3,2,1,0:T(8,128)(2,1)} reshape(bf16[8,2,65536]{2,1,0:T(2,128)(2,1)} %all_to_all.36) | data formatting | bytes 4194304
  248.1 16.0 %copy.68 = bf16[8,8,16,2,512]{4,2,1,3,0:T(8,128)(2,1)S(1)} copy(bf16[8,8,16,2,512]{2,0,3,4,1:T(8,128)(2,1)} %bitcast.77) | data formatting | bytes 4194304 | tf_op jit(solution)/shard_map/all_to_all | solution.py:95
  264.1 4.0 %copy.69 = bf16[8,128,2,512]{1,2,0,3:T(2,128)(2,1)} copy(bf16[8,128,2,512]{3,1,2,0:T(8,128)(2,1)S(1)} %bitcast.82) | data formatting | bytes 4194304 | tf_op jit(solution)/shard_map/all_to_all | solution.py:95
  268.1 27.6 %all_to_all.37 = bf16[8,128,2,512]{1,2,0,3:T(2,128)(2,1)S(1)} all-to-all(bf16[8,128,2,512]{1,2,0,3:T(2,128)(2,1)} %copy.69), channel_id=1, replica_groups=mesh['stn'=2,'tm'=8,'ct'=2] {'ct'}, dimensions={3} | all-to-all | bytes 4194304 | tf_op jit(solution)/shard_map/all_to_all | solution.py:94
  295.7 0.5 copy.70
  296.2 2.7 copy.93
  298.9 1.9 fusion.47
  300.8 1.5 maximum_bitcast_fusion.1
  302.4 8.5 %all-gather.2.cloned.1.call-done = bf16[256,2,32,128]{3,2,1,0:T(8,128)(2,1)} async-done(((bf16[256,2,16,128]{3,2,1,0:T(8,128)(2,1)}), bf16[256,2,32,128]{3,2,1,0:T(8,128)(2,1)}) %all-gather.2.cloned.1.call-update) | async-done | bytes 4194320 | tf_op jit(solution)/shard_map/all_gather | solution.py:108
  310.9 6.1 %fusion.5 = f32[2,256,16,32]{3,2,0,1:T(8,128)} fusion(bf16[1,256,2,16,128]{4,3,2,0,1:T(8,128)(2,1)} %maximum_bitcast_fusion.1, bf16[1,256,2,16,128]{4,3,2,0,1:T(8,128)(2,1)S(1)} %bitcast.80, bf16[256,2,32,128]{3,2,1,0:T(8,128)(2,1)} %all-gather.2.cloned.1.call-done), kind=kOutput, calls=%fused_computation.9 | convolution fusion | flops 142868480 | bytes 9437184 | tf_op jit(solution)/shard_map/ocjaf,cjbf->ocab/dot_general | solution.py:105
  317.0 4.3 %copy.73 = f32[2,256,16,32]{1,3,2,0:T(8,128)} copy(f32[2,256,16,32]{3,2,0,1:T(8,128)} %fusion.5) | data formatting | bytes 2097152 | tf_op jit(solution)/shard_map/mul | solution.py:111
  (22 shorter events, 1.1 us)
Async XLA Ops:
  6.5 10.0 %copy-start.1 = (s32[8]{0:T(128)S(1)}, s32[8]{0:T(128)}, u32[]{:S(2)}) copy-start(s32[8]{0:T(128)} %param.3) | copy-start | bytes 100
  6.5 304.4 %all-gather.2.cloned.1.call-start = ((), (), s32[]{:S(2)}) async-start(), calls=%async_computation.2 | async-start | bytes 6291456 | tf_op jit(solution)/shard_map/all_gather | solution.py:108
  10.3 49.7 %collective-permute-start = (bf16[2,8,65536]{2,0,1:T(2,128)(2,1)S(1)}, bf16[2,8,65536]{2,0,1:T(2,128)(2,1)}, u32[]{:S(2)}, u32[]{:S(2)}) collective-permute-start(bf16[2,8,65536]{2,0,1:T(2,128)(2,1)S(1)} %copy.57), channel_id=1, source_target_pairs={{0,2},{2,4},{4,6},{6,8},{8,10},{10,12},{12,14},{1,3},{3,5},{5,7},{... | collective-permute-start | bytes 6291464 | tf_op jit(solution)/shard_map/ppermute | solution.py:16
  298.9 12.0 %copy-start = (bf16[2,8,128,2,256]{2,1,0,3,4:T(8,128)(2,1)S(1)}, bf16[2,8,128,2,256]{2,1,0,3,4:T(8,128)(2,1)}, u32[]{:S(2)}) copy-start(bf16[2,8,128,2,256]{2,1,0,3,4:T(8,128)(2,1)} %copy.93) | copy-start | bytes 6291460
Sparse Core Ops, SparseCore 0:
  299.0 11.8 all-gather.1
where the time goes:
time: 330 us; the launch traced here: 328 us
  local copies, waits for them, and re-layouts  142 us (43%)
  blocking collectives  81.8 us (25%)
  waiting for transfers between devices  50.3 us (15%)
  other arithmetic  26.2 us (8%)
  between operations  13.5 us (4%)
  matrix products  7.62 us (2%)
  starting transfers between devices  6.22 us (2%)
    all_to_all x1, blocking collectives, on_device(): lax.all_to_all(spectra, 'tm', split_axis=3, concat_axis=1, tiled=True)  54.3 us
    ppermute x1, waiting for transfers between devices, passed_along(): return lax.ppermute(block, axis, route)  41.8 us
    unnamed x8, local copies, waits for them, and re-layouts  36.5 us
    gather x24, local copies, waits for them, and re-layouts  34.8 us
    all_to_all x1, blocking collectives, on_device(): lax.all_to_all(lax.all_to_all(spectra, 'tm', split_axis=3, concat_axis=1,...  27.6 us
    convert_element_type x3, local copies, waits for them, and re-layouts, transform(): return result.reshape(number, 2, CHANNELS).astype(jnp.bfloat16)  27.4 us
    all_to_all x2, local copies, waits for them, and re-layouts, on_device(): lax.all_to_all(spectra, 'tm', split_axis=3, concat_axis=1, tiled=True)  20 us
    another operation x2, local copies, waits for them, and re-layouts, transform(): stacked = branches.reshape(number, 2 * second, RADIX)  8.97 us
  transfers between devices with their start and end apart: 2, of which 2 were waited for; matrix products, arithmetic and copies ran while one was open for 2% of the time, Pallas kernels for 0%

commit v1 on v0

v1 whole, which is shorter than its diff:
```python
import functools
import math

import jax
import jax.numpy as jnp
import numpy as np
from jax import lax
from jax.experimental import pallas as pl
from jax.experimental.pallas import tpu as pltpu
from jax.sharding import PartitionSpec as P

CHANNELS = 4096
RADIX = 64
TAPS = 16
LANES = 128
ROWS = CHANNELS // LANES
PAIR = 2
TILE = 4
CHUNKS = 2

VMEM = pl.BlockSpec(memory_space=pltpu.VMEM)
SMEM = pl.BlockSpec(memory_space=pltpu.SMEM)


def params(mib):
    return pltpu.CompilerParams(vmem_limit_bytes=mib * 2**20)


def cost(flops, size):
    return pl.CostEstimate(flops=flops, bytes_accessed=size, transcendentals=0)


def filter_table():
    length = TAPS * CHANNELS
    index = np.arange(length, dtype=np.float64)
    centred = (index - length / 2) / CHANNELS
    window = 0.5 - 0.5 * np.cos(2.0 * math.pi * index / length)
    factor = 1.0 / (48.0 * math.sqrt(CHANNELS))
    table = np.sinc(centred) * window * factor
    return table.reshape(TAPS, ROWS, LANES).astype(np.float32)


def dft_parts(radix):
    steps = np.arange(radix)
    angle = 2.0 * math.pi * (steps[:, None] * steps[None, :] % radix) / radix
    return np.cos(angle).astype(jnp.bfloat16), np.sin(angle).astype(jnp.bfloat16)


def first_table():
    cosine, sine = dft_parts(CHANNELS // RADIX)
    order = [2 * row + half for half in range(2) for row in range(ROWS)]
    cosine, sine = cosine[:, order], sine[:, order]
    upper = np.concatenate([cosine, sine], axis=1)
    lower = np.concatenate([-sine, cosine], axis=1)
    return np.concatenate([upper, lower], axis=0)


def last_table(outer, per_ct, span):
    cosine, sine = dft_parts(RADIX)
    blocks = []
    for g in range(PAIR):
        for ct in range(per_ct):
            steps = [
                ((o * PAIR + g) * per_ct + ct) * span + j for o in range(outer) for j in range(span)
            ]
            real = np.concatenate([cosine[steps], sine[steps]], axis=1)
            imag = np.concatenate([-sine[steps], cosine[steps]], axis=1)
            blocks.append(np.concatenate([real, imag], axis=0))
    return np.stack(blocks).reshape(PAIR, per_ct, -1, 2 * RADIX)


def twiddle_tables():
    rows = np.arange(CHANNELS // RADIX)
    cols = np.arange(RADIX)
    angle = 2.0 * math.pi * (rows[:, None] * cols[None, :] % CHANNELS) / CHANNELS
    cosine = np.cos(angle).astype(np.float32)
    sine = np.sin(angle).astype(np.float32)
    return np.concatenate([cosine, cosine], axis=1), np.concatenate([sine, sine], axis=1)


def filterbank_kernel(count, frames, dests, *refs):
    scal, keep, recv, halo, coef, first, tw_cos, tw_sin, last = refs[:9]
    outs = refs[9 : 9 + dests]
    samples, shifted, grouped = refs[9 + dests :]
    block_rows = frames * ROWS
    all_rows = (PAIR + 1) * block_rows
    first_row = (frames - (TAPS - 1)) * ROWS
    total = PAIR * frames
    me = scal[count]
    lane = lax.broadcasted_iota(jnp.int32, (1, LANES), 1)

    step = 8
    for source, place in ((halo, 0), (keep, 1 + me), (recv, 2 - me)):
        for part in range(2):

            def unpack(n, carry, source=source, place=place, part=part):
                wide = source[part, :, pl.ds(pl.multiple_of(n * step * LANES, step * LANES), step * LANES)]
                wide = wide.astype(jnp.float32)
                base = (part * all_rows + place * block_rows + n * step) * count
                for u in range(step):
                    at = pl.multiple_of(base + u * count, count)
                    samples[pl.ds(at, count), :] = wide[:, u * LANES : (u + 1) * LANES]
                return carry

            lax.fori_loop(0, block_rows // step, unpack, 0)

    kept_rows = all_rows - first_row
    high = lane < RADIX
    for item in range(count):
        delay = scal[item]
        down = delay // LANES
        across = delay % LANES
        inside = lane < LANES - across
        piece = ROWS
        for part in range(2):

            def shift(n, carry, part=part, item=item):
                row = part * all_rows + first_row + n * piece - down
                at = row * count + item
                here = samples[pl.ds(at, piece, stride=count), :]
                before = samples[pl.ds(at - count, piece, stride=count), :]
                moved = pltpu.roll(jnp.where(inside, here, before), across, 1)
                shifted[pl.ds(pl.multiple_of(part * kept_rows + n * piece, piece), piece), :] = moved
                return carry

            lax.fori_loop(0, kept_rows // piece, shift, 0)

        group = 4

        def filt(n, carry):
            base = n * group
            for band in range(ROWS // 16):
                sums = [[None] * group for _ in range(2)]
                for part in range(2):
                    values = []
                    for u in range(group + TAPS - 1):
                        at = part * kept_rows + (base + u) * ROWS + band * 16
                        values.append(shifted[pl.ds(pl.multiple_of(at, 16), 16), :])
                    for tap in range(TAPS):
                        weight = coef[tap, band * 16 : band * 16 + 16, :]
                        for u in range(group):
                            term = weight * values[u + TAPS - 1 - tap]
                            old = sums[part][u]
                            sums[part][u] = term if old is None else old + term
                for u in range(group):
                    real, imag = sums[0][u], sums[1][u]
                    real_turned = pltpu.roll(real, RADIX, 1)
                    imag_turned = pltpu.roll(imag, RADIX, 1)
                    parts = (
                        jnp.where(high, real, imag_turned),
                        jnp.where(high, real_turned, imag),
                        jnp.where(high, imag, -real_turned),
                        jnp.where(high, imag_turned, -real),
                    )
                    for index, value in enumerate(parts):
                        low = index * ROWS + band * 16
                        grouped[base + u, low : low + 16, :] = value.astype(jnp.bfloat16)
            return carry

        lax.fori_loop(0, total // group, filt, 0)

        def turn(n, carry, item=item):
            base = n * group
            wide = jnp.concatenate([grouped[base + u] for u in range(group)], axis=1)
            inner = jnp.dot(first[...], wide, preferred_element_type=jnp.float32)
            rows = []
            for u in range(group):
                cut = slice(u * LANES, (u + 1) * LANES)
                turned = inner[:RADIX, cut] * tw_cos[...] + inner[RADIX:, cut] * tw_sin[...]
                rows.append(turned.astype(jnp.bfloat16))
            inner = jnp.concatenate(rows, axis=0)
            result = lax.dot_general(
                last[...], inner, (((1,), (1,)), ((), ())), preferred_element_type=jnp.float32
            ).astype(jnp.bfloat16)
            size = result.shape[0] // (2 * dests)
            for dest in range(dests):
                for part in range(2):
                    low = (dest * 2 + part) * size
                    for u in range(group // 2):
                        outs[dest][item, n * (group // 2) + u, part] = result[
                            low : low + size, u * LANES : (u + 1) * LANES
                        ]
            return carry

        lax.fori_loop(0, total // group, turn, 0)


def filterbank(scal, keep, recv, halo, tables, last, dests):
    count = keep.shape[1]
    frames = keep.shape[2] // CHANNELS
    size = last.shape[0] // (2 * dests)
    all_rows = (PAIR + 1) * frames * ROWS
    kept_rows = (PAIR * frames + TAPS - 1) * ROWS
    shape = jax.ShapeDtypeStruct((count, PAIR * frames // 2, 2, size, LANES), jnp.bfloat16)
    return pl.pallas_call(
        functools.partial(filterbank_kernel, count, frames, dests),
        out_shape=[shape] * dests,
        in_specs=[SMEM] + [VMEM] * 8,
        out_specs=[VMEM] * dests,
        scratch_shapes=[
            pltpu.VMEM((2 * all_rows * count, LANES), jnp.float32),
            pltpu.VMEM((2 * kept_rows, LANES), jnp.float32),
            pltpu.VMEM((PAIR * frames, LANES, LANES), jnp.bfloat16),
        ],
        compiler_params=params(40),
        cost_estimate=cost(2 * 10**9, 8 * 2**20),
        name="filterbank",
    )(scal, keep, recv, halo, *tables, last)


def pair_blocks(own):
    tiles = own // TILE
    inside = [(i, j) for i in range(tiles) for j in range(i, tiles)]
    across = [(i, j) for i in range(tiles // 2) for j in range(tiles)]
    return inside, across


def correlate_kernel(layout, *refs):
    count, own, outer, span, pairs, blocks_in, blocks_all = layout
    sources, (place, starts, where_outer) = refs[: len(pairs)], refs[len(pairs) : len(pairs) + 3]
    rest = refs[len(pairs) + 3 :]
    outs, (spectra, sums) = rest[:-2], rest[-2:]
    halves = outer * span // 8
    pair_count = blocks_in[1], blocks_all
    steps = spectra.shape[1]

    for index, source in enumerate(sources):
        for item in range(count):

            def spread(n, carry, index=index, source=source, item=item):
                for part in range(2):
                    spectra[place[index] + item, n, part] = source[item, n, part].astype(jnp.float32)
                return carry

            lax.fori_loop(0, steps, spread, 0)

    lane = lax.broadcasted_iota(jnp.int32, (8, LANES), 1)
    high = lane < RADIX
    rows_outer = blocks_all * TILE * TILE * span

    def block(t, carry):
        left, right = starts[2 * t], starts[2 * t + 1]
        for half in range(halves):
            cut = slice(half * 8, half * 8 + 8)

            def frame(n, acc):
                a = [[spectra[left + p, n, part, cut, :] for part in range(2)] for p in range(TILE)]
                b = [[spectra[right + q, n, part, cut, :] for part in range(2)] for q in range(TILE)]
                new = []
                for p in range(TILE):
                    for q in range(TILE):
                        real, imag = acc[2 * (p * TILE + q)], acc[2 * (p * TILE + q) + 1]
                        real = real + a[p][0] * b[q][0] + a[p][1] * b[q][1]
                        imag = imag + a[p][1] * b[q][0] - a[p][0] * b[q][1]
                        new += [real, imag]
                return tuple(new)

            zero = jnp.zeros((8, LANES), jnp.float32)
            acc = lax.fori_loop(0, steps, frame, (zero,) * (2 * TILE * TILE))
            for p in range(TILE * TILE):
                real = acc[2 * p] + pltpu.roll(acc[2 * p], RADIX, 1)
                imag = acc[2 * p + 1] + pltpu.roll(acc[2 * p + 1], RADIX, 1)
                both = jnp.where(high, real, imag)
                for u in range(8 // span):
                    o = half * (8 // span) + u
                    at = o * rows_outer + (t * TILE * TILE + p) * span
                    sums[pl.ds(pl.multiple_of(at, span), span), :] = both[u * span : (u + 1) * span]
        return carry

    lax.fori_loop(0, blocks_all, block, 0)

    rows_in = blocks_in[0] * TILE * TILE * span
    for r in range(outer):
        base = lax.rem(where_outer[0] + r, outer) * rows_outer
        for low, high_row, out in ((0, rows_in, outs[2 * r]), (rows_in, rows_outer, outs[2 * r + 1])):
            at = pl.multiple_of(base + low, 16)
            out[...] = sums[pl.ds(at, high_row - low), :].astype(out.dtype)


def correlate(arrays, place, starts, where_outer, own, outer, span):
    count, steps, _, size, _ = arrays[0].shape
    inside, across = pair_blocks(own)
    total = len(inside) + len(across)
    rows = TILE * TILE * span
    shapes = []
    for r in range(outer):
        dtype = jnp.float32 if r == 0 else jnp.bfloat16
        shapes.append(jax.ShapeDtypeStruct((len(inside) * rows, LANES), dtype))
        shapes.append(jax.ShapeDtypeStruct((len(across) * rows, LANES), dtype))
    layout = (count, own, outer, span, tuple(range(len(arrays))), (len(inside), 0), total)
    return pl.pallas_call(
        functools.partial(correlate_kernel, layout),
        out_shape=shapes,
        in_specs=[VMEM] * len(arrays) + [SMEM] * 3,
        out_specs=[VMEM] * len(shapes),
        scratch_shapes=[
            pltpu.VMEM((2 * own, steps, 2, size, LANES), jnp.float32),
            pltpu.VMEM((outer * total * rows, LANES), jnp.float32),
        ],
        compiler_params=params(40),
        cost_estimate=cost(10**10, 16 * 2**20),
        name="correlate",
    )(*arrays, place, starts, where_outer)


def assemble_kernel(own, outer, span, scale, *refs):
    core = refs[0]
    mine_in = refs[1 : 1 + outer]
    mine_across = refs[1 + outer : 1 + 2 * outer]
    far_across = refs[1 + 2 * outer : 1 + 3 * outer]
    out, joined = refs[1 + 3 * outer :]
    inside, across = pair_blocks(own)
    rows = TILE * TILE * span
    lane = lax.broadcasted_iota(jnp.int32, (1, LANES), 1)
    high = lane < RADIX
    mirror = jnp.where(high, 1.0, -1.0).astype(jnp.float32)
    me = core[0]

    def added(sources, t):
        total = sources[0][t * rows : (t + 1) * rows, :].astype(jnp.float32)
        for source in sources[1:]:
            total = total + source[t * rows : (t + 1) * rows, :].astype(jnp.float32)
        return total * scale

    def put(value, row, col):
        at = pl.multiple_of((row * 2 * own + col) * span, span)
        joined[pl.ds(at, span), :] = value

    for t, (i, j) in enumerate(inside):
        total = added(mine_in, t)
        turned = total * mirror
        for p in range(TILE):
            for q in range(TILE):
                low = (p * TILE + q) * span
                a, b = i * TILE + p, j * TILE + q
                put(total[low : low + span], a, me * own + b)
                if i < j:
                    put(turned[low : low + span], b, me * own + a)
    sign = jnp.where(me == 0, jnp.ones_like(mirror), mirror)
    for sources, part in ((mine_across, me), (far_across, 1 - me)):
        for t, (i, j) in enumerate(across):
            total = added(sources, t) * sign
            for p in range(TILE):
                for q in range(TILE):
                    low = (p * TILE + q) * span
                    a = part * (own // 2) + i * TILE + p
                    b = j * TILE + q
                    row = jnp.where(me == 0, a, b)
                    col = jnp.where(me == 0, own + b, a)
                    put(total[low : low + span], row, col)

    def emit(a, carry):
        for tile in range(2 * own // 8):
            for pair in range(span // 2):
                loads = []
                for u in range(2):
                    at = (a * 2 * own + tile * 8) * span + pair * 2 + u
                    loads.append(joined[pl.ds(at, 8, stride=span), :])
                turned = [pltpu.roll(x, RADIX, 1) for x in loads]
                cut = slice(pair * LANES, (pair + 1) * LANES)
                out[0, a, tile * 8 : tile * 8 + 8, cut] = jnp.where(high, loads[0], turned[1])
                out[1, a, tile * 8 : tile * 8 + 8, cut] = jnp.where(high, turned[0], loads[1])
        return carry

    lax.fori_loop(0, own, emit, 0)


def assemble(core, mine_in, mine_across, far_across, own, span, scale):
    outer = len(mine_in)
    return pl.pallas_call(
        functools.partial(assemble_kernel, own, outer, span, scale),
        out_shape=jax.ShapeDtypeStruct((2, own, 2 * own, span * RADIX), jnp.float32),
        in_specs=[SMEM] + [VMEM] * (3 * outer),
        out_specs=VMEM,
        scratch_shapes=[pltpu.VMEM((own * 2 * own * span, LANES), jnp.float32)],
        compiler_params=params(24),
        cost_estimate=cost(10**8, 8 * 2**20),
        name="assemble",
    )(core, *mine_in, *mine_across, *far_across)


def fast_fits(in_count, frame_count):
    stn, tm, per_ct = (lax.axis_size(a) for a in ("stn", "tm", "ct"))
    groups = tm * per_ct
    if stn != 2 or tm % PAIR or in_count % (PAIR * CHUNKS) or RADIX % groups:
        return False
    outer, span = tm // PAIR, RADIX // groups
    own = in_count * per_ct
    return (
        frame_count >= TAPS
        and frame_count % 4 == 0
        and span in (2, 4, 8)
        and outer * span % 16 == 0
        and own % (2 * TILE) == 0
    )


def fast(voltages, delays):
    tm, per_ct = lax.axis_size("tm"), lax.axis_size("ct")
    in_count = voltages.shape[1]
    frame_count = voltages.shape[2] // CHANNELS
    outer = tm // PAIR
    span = RADIX // (tm * per_ct)
    own = in_count * per_ct
    half = in_count // PAIR
    part = half // CHUNKS
    place_tm, place_ct = lax.axis_index("tm"), lax.axis_index("ct")
    core = lax.axis_index("stn")
    g, o = place_tm % PAIR, place_tm // PAIR

    swap = [(i, i ^ 1) for i in range(tm)]
    onward = [(i, i + PAIR) for i in range(tm - PAIR)]
    cores = [(0, 1), (1, 0)]

    dests = [(dg, dc) for dg in range(PAIR) for dc in range(per_ct)]
    base = jnp.asarray(last_table(outer, per_ct, span))
    base = jnp.where(g == 0, base, base[::-1])
    base = lax.dynamic_slice_in_dim(jnp.concatenate([base, base], axis=1), place_ct, per_ct, 1)
    last = base.reshape(-1, 2 * RADIX)
    tables = [jnp.asarray(filter_table()), jnp.asarray(first_table())]
    tables += [jnp.asarray(t) for t in twiddle_tables()]

    def rows_of(start):
        return lax.dynamic_slice_in_dim(voltages, start, part, 1)

    keeps, recvs, halos = [], [], []
    for c in range(CHUNKS):
        keeps.append(rows_of(g * half + c * part))
        recvs.append(lax.ppermute(rows_of((1 - g) * half + c * part), "tm", swap))
    for c in range(CHUNKS):
        halos.append(lax.ppermute(jnp.where(g == 1, keeps[c], recvs[c]), "tm", onward))

    arrays, place = [], []
    for c in range(CHUNKS):
        offsets = lax.dynamic_slice_in_dim(delays, g * half + c * part, part, 0)
        scal = jnp.concatenate([offsets, g.astype(jnp.int32)[None]])
        spectra = filterbank(scal, keeps[c], recvs[c], halos[c], tables, last, len(dests))
        for (dg, dc), block in zip(dests, spectra):
            route = []
            for i in range(tm):
                for j in range(per_ct):
                    target = (i ^ dg) * per_ct + (j + dc) % per_ct
                    route.append((i * per_ct + j, target))
            if dg or dc:
                block = lax.ppermute(block, ("tm", "ct"), route)
            other = lax.ppermute(block, "stn", cores)
            start = ((place_ct - dc) % per_ct) * in_count + (g ^ dg) * half + c * part
            arrays += [block, other]
            place += [core * own + start, (1 - core) * own + start]

    inside, across = pair_blocks(own)
    starts = [core * own + TILE * s for block in inside for s in block]
    for i, j in across:
        starts += [core * (own // 2) + TILE * i, own + TILE * j]

    def stacked(values):
        return jnp.stack([jnp.asarray(v, jnp.int32) for v in values])

    parts = correlate(arrays, stacked(place), stacked(starts), stacked([o]), own, outer, span)
    mine_in, mine_across, far_across = [], [], []
    for r in range(outer):
        a, b = parts[2 * r], parts[2 * r + 1]
        if r:
            route = [(i, (i + r * PAIR) % tm) for i in range(tm)]
            a, b = lax.ppermute(a, "tm", route), lax.ppermute(b, "tm", route)
        mine_in.append(a)
        mine_across.append(b)
        far_across.append(lax.ppermute(b, "stn", cores))
    scale = 1.0 / (tm * frame_count)
    result = assemble(stacked([core]), mine_in, mine_across, far_across, own, span, scale)
    return result.transpose(0, 3, 1, 2)


def general(voltages, delays):
    in_count = voltages.shape[1]
    frame_count = voltages.shape[2] // CHANNELS
    route = [(i, i + 1) for i in range(lax.axis_size("tm") - 1)]
    extended = jnp.concatenate([lax.ppermute(voltages, "tm", route), voltages], axis=2)
    span = (frame_count + TAPS - 1) * CHANNELS
    shifted = jax.vmap(
        lambda row, offset: lax.dynamic_slice_in_dim(row, CHANNELS - offset, span, 1),
        in_axes=(1, 0),
        out_axes=1,
    )(extended, delays)
    framed = shifted.reshape(2, in_count, frame_count + TAPS - 1, CHANNELS)
    table = jnp.asarray(filter_table()).reshape(TAPS, CHANNELS)
    total = jnp.zeros((2, in_count, frame_count, CHANNELS), jnp.float32)
    for tap in range(TAPS):
        low = TAPS - 1 - tap
        total = total + table[tap] * framed[:, :, low : low + frame_count].astype(jnp.float32)
    branches = jnp.moveaxis(total.astype(jnp.bfloat16), 0, 2)

    number = in_count * frame_count
    cosine, sine = dft_parts(RADIX)
    block = np.concatenate(
        [np.concatenate([cosine, sine], axis=1), np.concatenate([-sine, cosine], axis=1)], axis=0
    )
    block = jnp.asarray(block)
    stacked = branches.reshape(number, 2 * RADIX, RADIX)
    inner = jnp.einsum("kj,nja->nka", block, stacked, preferred_element_type=jnp.float32)
    inner = inner.reshape(number, 2, RADIX, RADIX)
    tw_cos, tw_sin = (jnp.asarray(t[:, :RADIX]) for t in twiddle_tables())
    real = inner[:, 0] * tw_cos + inner[:, 1] * tw_sin
    imag = inner[:, 1] * tw_cos - inner[:, 0] * tw_sin
    turned = jnp.stack([real, imag], axis=2).reshape(number, RADIX, 2 * RADIX)
    turned = turned.astype(jnp.bfloat16)
    result = jnp.einsum("lj,nkj->nlk", block, turned, preferred_element_type=jnp.float32)
    spectra = result.reshape(in_count, frame_count, 2, CHANNELS).astype(jnp.bfloat16)
    moved = lax.all_to_all(spectra, "tm", split_axis=3, concat_axis=1, tiled=True)
    moved = lax.all_to_all(moved, "ct", split_axis=3, concat_axis=0, tiled=True)
    local = moved.transpose(3, 2, 0, 1)
    swapped = jnp.stack([local[:, 1], -local[:, 0]], axis=1)
    summed = jnp.einsum(
        "ocjaf,cjbf->ocab",
        jnp.stack([local, swapped], axis=0),
        lax.all_gather(local, "stn", axis=2, tiled=True),
        preferred_element_type=jnp.float32,
    )
    return summed * (1.0 / local.shape[3])


def on_device(voltages, delays):
    if fast_fits(voltages.shape[1], voltages.shape[2] // CHANNELS):
        return fast(voltages, delays)
    return general(voltages, delays)


def solution(mesh):
    return jax.shard_map(
        on_device,
        mesh=mesh,
        in_specs=(P(None, ("stn", "ct"), "tm"), P(("stn", "ct"))),
        out_specs=P(None, ("tm", "ct"), "stn", None),
        check_vma=False,
    )
```

time: 330 us -> 177 us (0.54)
  local copies, waits for them, and re-layouts: 142 us -> 2.46 us
  blocking collectives: 81.8 us -> 0 us
  Pallas kernels: 0 us -> 80.3 us
  starting transfers between devices: 6.22 us -> 28.9 us
  other arithmetic: 26.2 us -> 7.23 us
  between operations: 13.5 us -> 0.17 us
  matrix products: 7.62 us -> 0 us
  waiting for transfers between devices: 50.3 us -> 56.7 us
    all_to_all x2 -> x0, blocking collectives: 81.8 us -> none  [the longest x1 54.3 us: on_device(): lax.all_to_all(spectra, 'tm', split_axis=3, concat_axis=1, tiled=True)]
    pallas_call x0 -> x4, Pallas kernels: none -> 80.3 us  [the longest x2 53.2 us: filterbank(): pl.pallas_call(functools.partial(filterbank_kernel, count, frames, dests)...]
    gather x25 -> x0, local copies, waits for them, and re-layouts: 39.2 us -> none
    unnamed x8 -> x14, local copies, waits for them, and re-layouts: 36.5 us -> 0.03 us
    convert_element_type x3 -> x0, local copies, waits for them, and re-layouts: 27.4 us -> none  [transform(): return result.reshape(number, 2, CHANNELS).astype(jnp.bfloat16)]
    all_to_all x4 -> x0, local copies, waits for them, and re-layouts: 23.3 us -> none  [the longest x2 20 us: on_device(): lax.all_to_all(spectra, 'tm', split_axis=3, concat_axis=1, tiled=True)]
    ppermute x1 -> x28, starting transfers between devices: 6.21 us -> 28.9 us  [the longest x6 9.07 us: fast(): a, b = (lax.ppermute(a, 'tm', route), lax.ppermute(b, 'tm', route))]
    transpose x2 -> x0, other arithmetic: 15.9 us -> none  [the longest x1 8.79 us: on_device(): branches = jnp.moveaxis(filtered(framed, filter_table()), 0, 2)]
  transfers between devices with their start and end apart: 2 -> 28, of which waited for: 2 -> 12; matrix products, arithmetic and copies ran while one was open for 2% -> 2% of each run, Pallas kernels for 0% -> 30%
where the time goes in v1:
time: 177 us; the launch traced here: 176 us
  Pallas kernels  80.3 us (45%)
  waiting for transfers between devices  56.7 us (32%)
  starting transfers between devices  28.9 us (16%)
  other arithmetic  7.23 us (4%)
  local copies, waits for them, and re-layouts  2.46 us (1%)
    pallas_call x2, Pallas kernels, filterbank(): pl.pallas_call(functools.partial(filterbank_kernel, count, frames, dests)...  53.2 us
    pallas_call x1, Pallas kernels, correlate(): pl.pallas_call(functools.partial(correlate_kernel, layout), out_shape=sha...  23.9 us
    ppermute x2, waiting for transfers between devices, fast(): recvs.append(lax.ppermute(rows_of((1 - g) * half + c * part), 'tm', swap))  19.8 us
    ppermute x6, waiting for transfers between devices, fast(): block = lax.ppermute(block, ('tm', 'ct'), route)  18 us
    ppermute x6, waiting for transfers between devices, fast(): a, b = (lax.ppermute(a, 'tm', route), lax.ppermute(b, 'tm', route))  17.5 us
    ppermute x6, starting transfers between devices, fast(): a, b = (lax.ppermute(a, 'tm', route), lax.ppermute(b, 'tm', route))  9.07 us
    ppermute x6, starting transfers between devices, fast(): block = lax.ppermute(block, ('tm', 'ct'), route)  7.11 us
    select_n x2, other arithmetic, fast(): jnp.where(g == 1, keeps[c], recvs[c])  7.04 us
  transfers between devices with their start and end apart: 28, of which 12 were waited for; matrix products, arithmetic and copies ran while one was open for 2% of the time, Pallas kernels for 30%

profile of v1, /device:TPU:0, one launch (start us, length us, event | category | flops | bytes accessed | tf_op | source)
XLA Modules:
  0.0 175.8 jit_solution(14920794940329313310)
XLA Ops:
  0.0 2.2 %constant_dynamic-slice_fusion = bf16[2,2,65536]{2,1,0:T(2,128)(2,1)S(1)} fusion(bf16[2,8,65536]{2,1,0:T(8,128)(2,1)} %param.7, s32[]{:T(128)S(6)} %select_n.77), kind=kLoop, calls=%fused_computation.6 | loop fusion | bytes 1048580 | tf_op jit(solution)/shard_map/dynamic_slice | solution.py:424
  2.2 3.0 %collective-permute-start.9 = (bf16[2,2,65536]{2,1,0:T(2,128)(2,1)S(1)}, bf16[2,2,65536]{2,1,0:T(2,128)(2,1)S(1)}, u32[]{:S(2)}, u32[]{:S(2)}) collective-permute-start(bf16[2,2,65536]{2,1,0:T(2,128)(2,1)S(1)} %constant_dynamic-slice_fusion), channel_id=1, source_target_pairs={{0,2},{2,0},{4,6},{6,4},{8,10},{10,8},{12,14},{14,12},{1,3},{3,1},... | collective-permute-start | bytes 1572872 | tf_op jit(solution)/shard_map/ppermute | solution.py:429
  5.2 11.9 %collective-permute-done.9.refs_2_ = bf16[2,2,65536]{2,1,0:T(2,128)(2,1)S(1)} collective-permute-done((bf16[2,2,65536]{2,1,0:T(2,128)(2,1)S(1)}, bf16[2,2,65536]{2,1,0:T(2,128)(2,1)S(1)}, u32[]{:S(2)}, u32[]{:S(2)}) %collective-permute-start.9) | collective-permute-done | bytes 524320 | tf_op jit(solution)/shard_map/ppermute | solution.py:429
  17.1 4.5 %broadcast_select_fusion = (bf16[2,2,65536]{2,1,0:T(2,128)(2,1)S(1)}, bf16[2,2,65536]{2,1,0:T(2,128)(2,1)S(1)}, bf16[2,2,65536]{2,1,0:T(2,128)(2,1)}) fusion(bf16[2,2,65536]{2,1,0:T(2,128)(2,1)S(1)} %collective-permute-done.9.refs_2_, pred[]{:T(512)S(6)} %eq.17, bf16[2,8,65536]{2,1,0:T(8,128)(2,1)} %param.7, s32[]{:T(128)S(6)} %select_n.76, s32[]{:T(128)S(6)} %select_n.70), kind=kLoop, calls=%fused_computation | loop fusion | flops 262144 | bytes 3145737 | tf_op jit(solution)/shard_map/jit(_where)/select_n | solution.py:431
  21.6 1.7 collective-permute-start
  23.4 0.1 fusion.1
  23.5 3.5 %collective-permute-start.10 = (bf16[2,2,65536]{2,1,0:T(2,128)(2,1)S(1)}, bf16[2,2,65536]{2,1,0:T(2,128)(2,1)S(1)}, u32[]{:S(2)}, u32[]{:S(2)}) collective-permute-start(bf16[2,2,65536]{2,1,0:T(2,128)(2,1)S(1)} %get-tuple-element.37), channel_id=1, source_target_pairs={{0,4},{2,6},{4,8},{6,10},{8,12},{10,14},{1,5},{3,7},{5,9},{7,11},{... | collective-permute-start | bytes 1572872 | tf_op jit(solution)/shard_map/ppermute | solution.py:431
  27.0 7.9 %collective-permute-done.refs_2_ = bf16[2,2,65536]{2,1,0:T(2,128)(2,1)S(1)} collective-permute-done((bf16[2,2,65536]{2,1,0:T(2,128)(2,1)}, bf16[2,2,65536]{2,1,0:T(2,128)(2,1)S(1)}, u32[]{:S(2)}, u32[]{:S(2)}) %collective-permute-start) | collective-permute-done | bytes 524320 | tf_op jit(solution)/shard_map/ppermute | solution.py:429
  34.9 2.5 %broadcast_select_fusion.1 = (bf16[2,2,65536]{2,1,0:T(2,128)(2,1)S(1)}, bf16[2,2,65536]{2,1,0:T(2,128)(2,1)S(1)}) fusion(bf16[2,2,65536]{2,1,0:T(2,128)(2,1)S(1)} %collective-permute-done.refs_2_, pred[]{:T(512)S(6)} %eq.17, bf16[2,8,65536]{2,1,0:T(8,128)(2,1)} %param.7, s32[]{:T(128)S(6)} %select_n.69), kind=kLoop, calls=%fused_computation.1 | loop fusion | flops 262144 | bytes 2097157 | tf_op jit(solution)/shard_map/jit(_where)/select_n | solution.py:431
  37.5 3.4 %collective-permute-start.1 = (bf16[2,2,65536]{2,1,0:T(2,128)(2,1)S(1)}, bf16[2,2,65536]{2,1,0:T(2,128)(2,1)S(1)}, u32[]{:S(2)}, u32[]{:S(2)}) collective-permute-start(bf16[2,2,65536]{2,1,0:T(2,128)(2,1)S(1)} %get-tuple-element.39), channel_id=1, source_target_pairs={{0,4},{2,6},{4,8},{6,10},{8,12},{10,14},{1,5},{3,7},{5,9},{7,11},{... | collective-permute-start | bytes 1572872 | tf_op jit(solution)/shard_map/ppermute | solution.py:431
  40.9 0.1 pad_add_fusion.1.refs_0_
  41.0 0.0 collective-permute-done.10.refs_3_
  41.0 26.6 %filterbank.3 = (bf16[2,16,2,16,128]{4,3,2,1,0:T(8,128)(2,1)S(1)}, bf16[2,16,2,16,128]{4,3,2,1,0:T(8,128)(2,1)S(1)}, bf16[2,16,2,16,128]{4,3,2,1,0:T(8,128)(2,1)S(1)}, bf16[2,16,2,16,128]{4,3,2,1,0:T(8,128)(2,1)S(1)}) custom-call(s32[3]{0:T(128)S(1)} %pad_add_fusion.1.refs_0_, bf16[2,2,65536]{2,1,0:T(2,128)(2,1)S(1)} %get-tuple-element.38.refs_1_, ...), custom_call_target="tpu_custom_call" | custom-call | flops 2000000000 | bytes 8388608 | tf_op jit(solution)/shard_map/filterbank/pallas_call | solution.py:195
  67.6 1.6 collective-permute-start.12
  69.2 1.5 collective-permute-start.14
  70.7 0.5 collective-permute-start.16
  71.2 0.1 pad_add_fusion.refs_0_
  71.3 5.6 %collective-permute-done.12.refs_10_ = bf16[2,16,2,16,128]{4,3,2,1,0:T(8,128)(2,1)S(1)} collective-permute-done((bf16[2,16,2,16,128]{4,3,2,1,0:T(8,128)(2,1)S(1)}, bf16[2,16,2,16,128]{4,3,2,1,0:T(8,128)(2,1)S(1)}, u32[]{:S(2)}, u32[]{:S(2)}) %collective-permute-start.12) | collective-permute-done | bytes 262176 | tf_op jit(solution)/shard_map/ppermute | solution.py:445
  76.8 0.0 collective-permute-start.13
  76.8 0.9 collective-permute-done.14.refs_12_
  77.7 0.0 collective-permute-start.15
  77.7 0.0 collective-permute-done.1.refs_3_
  77.7 26.6 %filterbank.2 = (bf16[2,16,2,16,128]{4,3,2,1,0:T(8,128)(2,1)S(1)}, bf16[2,16,2,16,128]{4,3,2,1,0:T(8,128)(2,1)S(1)}, bf16[2,16,2,16,128]{4,3,2,1,0:T(8,128)(2,1)S(1)}, bf16[2,16,2,16,128]{4,3,2,1,0:T(8,128)(2,1)S(1)}) custom-call(s32[3]{0:T(128)S(1)} %pad_add_fusion.refs_0_, bf16[2,2,65536]{2,1,0:T(2,128)(2,1)S(1)} %get-tuple-element.40.refs_1_, ...), custom_call_target="tpu_custom_call" | custom-call | flops 2000000000 | bytes 8388608 | tf_op jit(solution)/shard_map/filterbank/pallas_call | solution.py:195
  104.3 1.2 collective-permute-start.3
  105.5 0.0 collective-permute-done.16.refs_14_
  105.5 1.5 collective-permute-start.5
  107.0 0.0 collective-permute-done.11.refs_9_
  107.0 0.8 collective-permute-start.7
  107.9 0.5 collective-permute-start.2
  108.4 4.7 %collective-permute-done.3.refs_2_ = bf16[2,16,2,16,128]{4,3,2,1,0:T(8,128)(2,1)S(1)} collective-permute-done((bf16[2,16,2,16,128]{4,3,2,1,0:T(8,128)(2,1)S(1)}, bf16[2,16,2,16,128]{4,3,2,1,0:T(8,128)(2,1)S(1)}, u32[]{:S(2)}, u32[]{:S(2)}) %collective-permute-start.3) | collective-permute-done | bytes 262176 | tf_op jit(solution)/shard_map/ppermute | solution.py:445
  113.1 1.6 collective-permute-done.5.refs_4_
  114.7 5.2 %collective-permute-done.7.refs_6_ = bf16[2,16,2,16,128]{4,3,2,1,0:T(8,128)(2,1)S(1)} collective-permute-done((bf16[2,16,2,16,128]{4,3,2,1,0:T(8,128)(2,1)S(1)}, bf16[2,16,2,16,128]{4,3,2,1,0:T(8,128)(2,1)S(1)}, u32[]{:S(2)}, u32[]{:S(2)}) %collective-permute-start.7) | collective-permute-done | bytes 262176 | tf_op jit(solution)/shard_map/ppermute | solution.py:445
  119.9 0.1 stack.124.refs_17_
  120.0 0.1 stack.117.refs_16_
  120.2 1.4 collective-permute-done.8.refs_7_
  121.6 23.9 %correlate.1 = (f32[640,128]{1,0:T(8,128)S(1)}, f32[512,128]{1,0:T(8,128)S(1)}, bf16[640,128]{1,0:T(8,128)(2,1)S(1)}, bf16[512,128]{1,0:T(8,128)(2,1)S(1)}, bf16...) custom-call(bf16[2,16,2,16,128]{4,3,2,1,0:T(8,128)(2,1)S(1)} %get-tu, ...), custom_call_target="tpu_custom_call" | custom-call | flops 10000000000 | bytes 16777216 | tf_op jit(solution)/shard_map/correlate/pallas_call | solution.py:291
  145.5 1.6 collective-permute-start.21
  147.1 1.1 collective-permute-start.22
  148.2 1.8 collective-permute-start.18
  150.0 1.7 collective-permute-start.19
  151.6 1.3 collective-permute-start.23
  153.0 0.8 collective-permute-done.21.refs_6_
  153.8 11.9 %collective-permute-done.22.refs_7_ = bf16[512,128]{1,0:T(8,128)(2,1)S(1)} collective-permute-done((bf16[512,128]{1,0:T(8,128)(2,1)S(1)}, bf16[512,128]{1,0:T(8,128)(2,1)S(1)}, u32[]{:S(2)}, u32[]{:S(2)}) %collective-permute-start.22) | collective-permute-done | bytes 131104 | tf_op jit(solution)/shard_map/ppermute | solution.py:465
  165.7 1.6 collective-permute-start.20
  167.3 0.5 collective-permute-start.26
  167.8 1.4 collective-permute-done.19.refs_3_
  169.2 3.4 %collective-permute-done.20.refs_4_ = bf16[640,128]{1,0:T(8,128)(2,1)S(1)} collective-permute-done((bf16[640,128]{1,0:T(8,128)(2,1)S(1)}, bf16[640,128]{1,0:T(8,128)(2,1)S(1)}, u32[]{:S(2)}, u32[]{:S(2)}) %collective-permute-start.20) | collective-permute-done | bytes 163872 | tf_op jit(solution)/shard_map/ppermute | solution.py:465
  172.6 3.2 %assemble.1 = f32[2,16,32,256]{3,2,1,0:T(8,128)} custom-call(s32[1]{0:T(128)} %bitcast.refs_0_, f32[640,128]{1,0:T(8,128)S(1)} %get-tuple-element.29.refs_1_, bf16[640,128]{1,0:T(8,128)(2,1)S(1)} %collective-permute-done.18.refs_2_, bf16[640,128]{1,0:T(8,128)(2,1)S(1)} %collective-permute-done.19.refs_3_, ...), custom_call_target="tpu_custom_call" | custom-call | flops 100000000 | bytes 8388608 | tf_op jit(solution)/shard_map/assemble/pallas_call | solution.py:370
  (36 shorter events, 0.1 us)
Async XLA Ops:
  0.0 23.4 %copy-start.6 = (s32[8]{0:T(128)S(1)}, s32[8]{0:T(128)}, u32[]{:S(2)}) copy-start(s32[8]{0:T(128)} %param.8) | copy-start | bytes 100
  0.0 23.4 %copy-start.4 = (bf16[2,2,32,128]{3,2,1,0:T(8,128)(2,1)S(1)}, bf16[2,2,32,128]{3,2,1,0:T(8,128)(2,1)}, u32[]{:S(2)}) copy-start(bf16[2,2,32,128]{3,2,1,0:T(8,128)(2,1)} %constant.93) | copy-start | bytes 98308
  0.0 23.4 %copy-start.5 = (bf16[2,2,32,128]{3,2,1,0:T(8,128)(2,1)S(1)}, bf16[2,2,32,128]{3,2,1,0:T(8,128)(2,1)}, u32[]{:S(2)}) copy-start(bf16[2,2,32,128]{3,2,1,0:T(8,128)(2,1)} %constant.88.clone) | copy-start | bytes 98308
  2.2 14.9 %collective-permute-start.9 = (bf16[2,2,65536]{2,1,0:T(2,128)(2,1)S(1)}, bf16[2,2,65536]{2,1,0:T(2,128)(2,1)S(1)}, u32[]{:S(2)}, u32[]{:S(2)}) collective-permute-start(bf16[2,2,65536]{2,1,0:T(2,128)(2,1)S(1)} %constant_dynamic-slice_fusion), channel_id=1, source_target_pairs={{0,2},{2,0},{4,6},{6,4},{8,10},{10,8},{12,14},{14,12},{1,3},{3,1},... | collective-permute-start | bytes 1572872 | tf_op jit(solution)/shard_map/ppermute | solution.py:429
  5.2 35.8 %copy-start = (f32[16,32,128]{2,1,0:T(8,128)S(1)}, f32[16,32,128]{2,1,0:T(8,128)}, u32[]{:S(2)}) copy-start(f32[16,32,128]{2,1,0:T(8,128)} %constant.89.clone.refs_4_) | copy-start | bytes 786436
  5.2 35.8 %copy-start.1 = (f32[64,128]{1,0:T(8,128)S(1)}, f32[64,128]{1,0:T(8,128)}, u32[]{:S(2)}) copy-start(f32[64,128]{1,0:T(8,128)} %constant.92.clone.refs_7_) | copy-start | bytes 98308
  5.2 35.8 %copy-start.2 = (f32[64,128]{1,0:T(8,128)S(1)}, f32[64,128]{1,0:T(8,128)}, u32[]{:S(2)}) copy-start(f32[64,128]{1,0:T(8,128)} %constant.91.clone.refs_6_) | copy-start | bytes 98308
  5.2 35.8 %copy-start.3 = (bf16[128,128]{1,0:T(8,128)(2,1)S(1)}, bf16[128,128]{1,0:T(8,128)(2,1)}, u32[]{:S(2)}) copy-start(bf16[128,128]{1,0:T(8,128)(2,1)} %constant.90.clone.refs_5_) | copy-start | bytes 98308
  21.6 13.3 %collective-permute-start = (bf16[2,2,65536]{2,1,0:T(2,128)(2,1)}, bf16[2,2,65536]{2,1,0:T(2,128)(2,1)S(1)}, u32[]{:S(2)}, u32[]{:S(2)}) collective-permute-start(bf16[2,2,65536]{2,1,0:T(2,128)(2,1)} %get-tuple-element.41), channel_id=1, source_target_pairs={{0,2},{2,0},{4,6},{6,4},{8,10},{10,8},{12,14},{14,12},{1,3},{3,1},... | collective-permute-start | bytes 1572872 | tf_op jit(solution)/shard_map/ppermute | solution.py:429
  23.5 17.5 %collective-permute-start.10 = (bf16[2,2,65536]{2,1,0:T(2,128)(2,1)S(1)}, bf16[2,2,65536]{2,1,0:T(2,128)(2,1)S(1)}, u32[]{:S(2)}, u32[]{:S(2)}) collective-permute-start(bf16[2,2,65536]{2,1,0:T(2,128)(2,1)S(1)} %get-tuple-element.37), channel_id=1, source_target_pairs={{0,4},{2,6},{4,8},{6,10},{8,12},{10,14},{1,5},{3,7},{5,9},{7,11},{... | collective-permute-start | bytes 1572872 | tf_op jit(solution)/shard_map/ppermute | solution.py:431
  37.5 40.2 %collective-permute-start.1 = (bf16[2,2,65536]{2,1,0:T(2,128)(2,1)S(1)}, bf16[2,2,65536]{2,1,0:T(2,128)(2,1)S(1)}, u32[]{:S(2)}, u32[]{:S(2)}) collective-permute-start(bf16[2,2,65536]{2,1,0:T(2,128)(2,1)S(1)} %get-tuple-element.39), channel_id=1, source_target_pairs={{0,4},{2,6},{4,8},{6,10},{8,12},{10,14},{1,5},{3,7},{5,9},{7,11},{... | collective-permute-start | bytes 1572872 | tf_op jit(solution)/shard_map/ppermute | solution.py:431
  67.6 9.2 %collective-permute-start.12 = (bf16[2,16,2,16,128]{4,3,2,1,0:T(8,128)(2,1)S(1)}, bf16[2,16,2,16,128]{4,3,2,1,0:T(8,128)(2,1)S(1)}, u32[]{:S(2)}, u32[]{:S(2)}) collective-permute-start(bf16[2,16,2,16,128]{4,3,2,1,0:T(8,128)(2,1)S(1)} %get-tuple-element.26), channel_id=1, source_target_pairs={{0,1},{1,0},{2,3},{3,2},{4,5},{5,4},{6,7},{7,6},{8,9},{9,8},{10,11... | collective-permute-start | bytes 786440 | tf_op jit(solution)/shard_map/ppermute | solution.py:445
  69.2 8.5 %collective-permute-start.14 = (bf16[2,16,2,16,128]{4,3,2,1,0:T(8,128)(2,1)S(1)}, bf16[2,16,2,16,128]{4,3,2,1,0:T(8,128)(2,1)S(1)}, u32[]{:S(2)}, u32[]{:S(2)}) collective-permute-start(bf16[2,16,2,16,128]{4,3,2,1,0:T(8,128)(2,1)S(1)} %get-tuple-element.27), channel_id=1, source_target_pairs={{0,2},{1,3},{2,0},{3,1},{4,6},{5,7},{6,4},{7,5},{8,10},{9,11},{10,... | collective-permute-start | bytes 786440 | tf_op jit(solution)/shard_map/ppermute | solution.py:445
  70.7 34.8 %collective-permute-start.16 = (bf16[2,16,2,16,128]{4,3,2,1,0:T(8,128)(2,1)S(1)}, bf16[2,16,2,16,128]{4,3,2,1,0:T(8,128)(2,1)S(1)}, u32[]{:S(2)}, u32[]{:S(2)}) collective-permute-start(bf16[2,16,2,16,128]{4,3,2,1,0:T(8,128)(2,1)S(1)} %get-tuple-element.28), channel_id=1, source_target_pairs={{0,3},{1,2},{2,1},{3,0},{4,7},{5,6},{6,5},{7,4},{8,11},{9,10},{10,... | collective-permute-start | bytes 786440 | tf_op jit(solution)/shard_map/ppermute | solution.py:445
  71.2 35.9 %collective-permute-start.11 = (bf16[2,16,2,16,128]{4,3,2,1,0:T(8,128)(2,1)S(1)}, bf16[2,16,2,16,128]{4,3,2,1,0:T(8,128)(2,1)S(1)}, u32[]{:S(2)}, u32[]{:S(2)}) collective-permute-start(bf16[2,16,2,16,128]{4,3,2,1,0:T(8,128)(2,1)S(1)} %get-tuple-element.25.refs_8_), channel_id=1, source_target_pairs={{0,16},{16,0},{1,17},{17,1},{2,18},{18,2},{3,19},{19,3},{4,20},{20... | collective-permute-start | bytes 786440 | tf_op jit(solution)/shard_map/ppermute | solution.py:446
  76.8 31.0 %collective-permute-start.13 = (bf16[2,16,2,16,128]{4,3,2,1,0:T(8,128)(2,1)S(1)}, bf16[2,16,2,16,128]{4,3,2,1,0:T(8,128)(2,1)S(1)}, u32[]{:S(2)}, u32[]{:S(2)}) collective-permute-start(bf16[2,16,2,16,128]{4,3,2,1,0:T(8,128)(2,1)S(1)} %collective-permute-done.12.refs_10_), channel_id=1, source_target_pairs={{0,16},{16,0},{1,17},{17,1},{2,18},{18,2},{3,19},{19,3},{4,20},{20... | collective-permute-start | bytes 786440 | tf_op jit(solution)/shard_map/ppermute | solution.py:446
  77.7 30.2 %collective-permute-start.15 = (bf16[2,16,2,16,128]{4,3,2,1,0:T(8,128)(2,1)S(1)}, bf16[2,16,2,16,128]{4,3,2,1,0:T(8,128)(2,1)S(1)}, u32[]{:S(2)}, u32[]{:S(2)}) collective-permute-start(bf16[2,16,2,16,128]{4,3,2,1,0:T(8,128)(2,1)S(1)} %collective-permute-done.14.refs_12_), channel_id=1, source_target_pairs={{0,16},{16,0},{1,17},{17,1},{2,18},{18,2},{3,19},{19,3},{4,20},{20... | collective-permute-start | bytes 786440 | tf_op jit(solution)/shard_map/ppermute | solution.py:446
  104.3 8.8 %collective-permute-start.3 = (bf16[2,16,2,16,128]{4,3,2,1,0:T(8,128)(2,1)S(1)}, bf16[2,16,2,16,128]{4,3,2,1,0:T(8,128)(2,1)S(1)}, u32[]{:S(2)}, u32[]{:S(2)}) collective-permute-start(bf16[2,16,2,16,128]{4,3,2,1,0:T(8,128)(2,1)S(1)} %get-tuple-element.22), channel_id=1, source_target_pairs={{0,1},{1,0},{2,3},{3,2},{4,5},{5,4},{6,7},{7,6},{8,9},{9,8},{10,11... | collective-permute-start | bytes 786440 | tf_op jit(solution)/shard_map/ppermute | solution.py:445
  105.5 9.2 %collective-permute-start.5 = (bf16[2,16,2,16,128]{4,3,2,1,0:T(8,128)(2,1)S(1)}, bf16[2,16,2,16,128]{4,3,2,1,0:T(8,128)(2,1)S(1)}, u32[]{:S(2)}, u32[]{:S(2)}) collective-permute-start(bf16[2,16,2,16,128]{4,3,2,1,0:T(8,128)(2,1)S(1)} %get-tuple-element.23), channel_id=1, source_target_pairs={{0,2},{1,3},{2,0},{3,1},{4,6},{5,7},{6,4},{7,5},{8,10},{9,11},{10,... | collective-permute-start | bytes 786440 | tf_op jit(solution)/shard_map/ppermute | solution.py:445
  107.0 12.9 %collective-permute-start.7 = (bf16[2,16,2,16,128]{4,3,2,1,0:T(8,128)(2,1)S(1)}, bf16[2,16,2,16,128]{4,3,2,1,0:T(8,128)(2,1)S(1)}, u32[]{:S(2)}, u32[]{:S(2)}) collective-permute-start(bf16[2,16,2,16,128]{4,3,2,1,0:T(8,128)(2,1)S(1)} %get-tuple-element.24), channel_id=1, source_target_pairs={{0,3},{1,2},{2,1},{3,0},{4,7},{5,6},{6,5},{7,4},{8,11},{9,10},{10,... | collective-permute-start | bytes 786440 | tf_op jit(solution)/shard_map/ppermute | solution.py:445
  107.9 12.2 %collective-permute-start.17 = (bf16[2,16,2,16,128]{4,3,2,1,0:T(8,128)(2,1)S(1)}, bf16[2,16,2,16,128]{4,3,2,1,0:T(8,128)(2,1)S(1)}, u32[]{:S(2)}, u32[]{:S(2)}) collective-permute-start(bf16[2,16,2,16,128]{4,3,2,1,0:T(8,128)(2,1)S(1)} %collective-permute-done.16.refs_14_), channel_id=1, source_target_pairs={{0,16},{16,0},{1,17},{17,1},{2,18},{18,2},{3,19},{19,3},{4,20},{20... | collective-permute-start | bytes 786440 | tf_op jit(solution)/shard_map/ppermute | solution.py:446
  107.9 12.2 %collective-permute-start.2 = (bf16[2,16,2,16,128]{4,3,2,1,0:T(8,128)(2,1)S(1)}, bf16[2,16,2,16,128]{4,3,2,1,0:T(8,128)(2,1)}, u32[]{:S(2)}, u32[]{:S(2)}) collective-permute-start(bf16[2,16,2,16,128]{4,3,2,1,0:T(8,128)(2,1)S(1)} %get-tuple-element.21.refs_0_), channel_id=1, source_target_pairs={{0,16},{16,0},{1,17},{17,1},{2,18},{18,2},{3,19},{19,3},{4,20},{20... | collective-permute-start | bytes 786440 | tf_op jit(solution)/shard_map/ppermute | solution.py:446
  113.1 7.0 %collective-permute-start.4 = (bf16[2,16,2,16,128]{4,3,2,1,0:T(8,128)(2,1)S(1)}, bf16[2,16,2,16,128]{4,3,2,1,0:T(8,128)(2,1)}, u32[]{:S(2)}, u32[]{:S(2)}) collective-permute-start(bf16[2,16,2,16,128]{4,3,2,1,0:T(8,128)(2,1)S(1)} %collective-permute-done.3.refs_2_), channel_id=1, source_target_pairs={{0,16},{16,0},{1,17},{17,1},{2,18},{18,2},{3,19},{19,3},{4,20},{20... | collective-permute-start | bytes 786440 | tf_op jit(solution)/shard_map/ppermute | solution.py:446
  114.7 5.4 %collective-permute-start.6 = (bf16[2,16,2,16,128]{4,3,2,1,0:T(8,128)(2,1)S(1)}, bf16[2,16,2,16,128]{4,3,2,1,0:T(8,128)(2,1)}, u32[]{:S(2)}, u32[]{:S(2)}) collective-permute-start(bf16[2,16,2,16,128]{4,3,2,1,0:T(8,128)(2,1)S(1)} %collective-permute-done.5.refs_4_), channel_id=1, source_target_pairs={{0,16},{16,0},{1,17},{17,1},{2,18},{18,2},{3,19},{19,3},{4,20},{20... | collective-permute-start | bytes 786440 | tf_op jit(solution)/shard_map/ppermute | solution.py:446
  119.9 1.7 collective-permute-start.8
  145.5 8.3 %collective-permute-start.21 = (bf16[512,128]{1,0:T(8,128)(2,1)S(1)}, bf16[512,128]{1,0:T(8,128)(2,1)S(1)}, u32[]{:S(2)}, u32[]{:S(2)}) collective-permute-start(bf16[512,128]{1,0:T(8,128)(2,1)S(1)} %get-tuple-element.34), channel_id=1, source_target_pairs={{0,4},{2,6},{4,8},{6,10},{8,12},{10,14},{12,0},{14,2},{1,5},{3,7},... | collective-permute-start | bytes 393224 | tf_op jit(solution)/shard_map/ppermute | solution.py:465
  147.1 18.6 %collective-permute-start.22 = (bf16[512,128]{1,0:T(8,128)(2,1)S(1)}, bf16[512,128]{1,0:T(8,128)(2,1)S(1)}, u32[]{:S(2)}, u32[]{:S(2)}) collective-permute-start(bf16[512,128]{1,0:T(8,128)(2,1)S(1)} %get-tuple-element.35), channel_id=1, source_target_pairs={{0,8},{2,10},{4,12},{6,14},{8,0},{10,2},{12,4},{14,6},{1,9},{3,11}... | collective-permute-start | bytes 393224 | tf_op jit(solution)/shard_map/ppermute | solution.py:465
  148.2 19.1 %collective-permute-start.18 = (bf16[640,128]{1,0:T(8,128)(2,1)S(1)}, bf16[640,128]{1,0:T(8,128)(2,1)S(1)}, u32[]{:S(2)}, u32[]{:S(2)}) collective-permute-start(bf16[640,128]{1,0:T(8,128)(2,1)S(1)} %get-tuple-element.30), channel_id=1, source_target_pairs={{0,4},{2,6},{4,8},{6,10},{8,12},{10,14},{12,0},{14,2},{1,5},{3,7},... | collective-permute-start | bytes 491528 | tf_op jit(solution)/shard_map/ppermute | solution.py:465
  150.0 19.2 %collective-permute-start.19 = (bf16[640,128]{1,0:T(8,128)(2,1)S(1)}, bf16[640,128]{1,0:T(8,128)(2,1)S(1)}, u32[]{:S(2)}, u32[]{:S(2)}) collective-permute-start(bf16[640,128]{1,0:T(8,128)(2,1)S(1)} %get-tuple-element.31), channel_id=1, source_target_pairs={{0,8},{2,10},{4,12},{6,14},{8,0},{10,2},{12,4},{14,6},{1,9},{3,11}... | collective-permute-start | bytes 491528 | tf_op jit(solution)/shard_map/ppermute | solution.py:465
  151.6 15.7 %collective-permute-start.23 = (bf16[512,128]{1,0:T(8,128)(2,1)S(1)}, bf16[512,128]{1,0:T(8,128)(2,1)S(1)}, u32[]{:S(2)}, u32[]{:S(2)}) collective-permute-start(bf16[512,128]{1,0:T(8,128)(2,1)S(1)} %get-tuple-element.36), channel_id=1, source_target_pairs={{0,12},{2,14},{4,0},{6,2},{8,4},{10,6},{12,8},{14,10},{1,13},{3,15... | collective-permute-start | bytes 393224 | tf_op jit(solution)/shard_map/ppermute | solution.py:465
  153.8 18.8 %collective-permute-start.24 = (f32[512,128]{1,0:T(8,128)S(1)}, f32[512,128]{1,0:T(8,128)S(1)}, u32[]{:S(2)}, u32[]{:S(2)}) collective-permute-start(f32[512,128]{1,0:T(8,128)S(1)} %get-tuple-element.33.refs_5_), channel_id=1, source_target_pairs={{0,16},{16,0},{1,17},{17,1},{2,18},{18,2},{3,19},{19,3},{4,20},{20... | collective-permute-start | bytes 786440 | tf_op jit(solution)/shard_map/ppermute | solution.py:468
  165.7 6.9 %collective-permute-start.20 = (bf16[640,128]{1,0:T(8,128)(2,1)S(1)}, bf16[640,128]{1,0:T(8,128)(2,1)S(1)}, u32[]{:S(2)}, u32[]{:S(2)}) collective-permute-start(bf16[640,128]{1,0:T(8,128)(2,1)S(1)} %get-tuple-element.32), channel_id=1, source_target_pairs={{0,12},{2,14},{4,0},{6,2},{8,4},{10,6},{12,8},{14,10},{1,13},{3,15... | collective-permute-start | bytes 491528 | tf_op jit(solution)/shard_map/ppermute | solution.py:465
  167.3 5.3 %collective-permute-start.25 = (bf16[512,128]{1,0:T(8,128)(2,1)S(1)}, bf16[512,128]{1,0:T(8,128)(2,1)S(1)}, u32[]{:S(2)}, u32[]{:S(2)}) collective-permute-start(bf16[512,128]{1,0:T(8,128)(2,1)S(1)} %collective-permute-done.21.refs_6_), channel_id=1, source_target_pairs={{0,16},{16,0},{1,17},{17,1},{2,18},{18,2},{3,19},{19,3},{4,20},{20... | collective-permute-start | bytes 393224 | tf_op jit(solution)/shard_map/ppermute | solution.py:468
  167.3 5.3 %collective-permute-start.26 = (bf16[512,128]{1,0:T(8,128)(2,1)S(1)}, bf16[512,128]{1,0:T(8,128)(2,1)S(1)}, u32[]{:S(2)}, u32[]{:S(2)}) collective-permute-start(bf16[512,128]{1,0:T(8,128)(2,1)S(1)} %collective-permute-done.22.refs_7_), channel_id=1, source_target_pairs={{0,16},{16,0},{1,17},{17,1},{2,18},{18,2},{3,19},{19,3},{4,20},{20... | collective-permute-start | bytes 393224 | tf_op jit(solution)/shard_map/ppermute | solution.py:468
  169.2 3.4 %collective-permute-start.27 = (bf16[512,128]{1,0:T(8,128)(2,1)S(1)}, bf16[512,128]{1,0:T(8,128)(2,1)S(1)}, u32[]{:S(2)}, u32[]{:S(2)}) collective-permute-start(bf16[512,128]{1,0:T(8,128)(2,1)S(1)} %collective-permute-done.23.refs_8_), channel_id=1, source_target_pairs={{0,16},{16,0},{1,17},{17,1},{2,18},{18,2},{3,19},{19,3},{4,20},{20... | collective-permute-start | bytes 393224 | tf_op jit(solution)/shard_map/ppermute | solution.py:468

commit v2 on v1

--- a/solution.py
+++ b/solution.py
@@ -78,93 +78,110 @@
     return np.concatenate([cosine, cosine], axis=1), np.concatenate([sine, sine], axis=1)
 
 
+def pick_kernel(count, scal, block, out, rows):
+    inputs, samples = block.shape[1], block.shape[2]
+    step = 16
+    for part in range(2):
+
+        def spread(n, carry, part=part):
+            low = pl.multiple_of(n * step * LANES, step * LANES)
+            wide = block[part, :, pl.ds(low, step * LANES)].astype(jnp.float32)
+            for u in range(step):
+                at = pl.multiple_of((n * step + u) * inputs, inputs)
+                rows[part, pl.ds(at, inputs), :] = wide[:, u * LANES : (u + 1) * LANES]
+            return carry
+
+        lax.fori_loop(0, samples // LANES // step, spread, 0)
+    first = scal[0]
+    tall = 128
+    for part in range(2):
+        for item in range(count):
+
+            def gather(n, carry, part=part, item=item):
+                low = pl.multiple_of(n * tall, tall)
+                value = rows[part, pl.ds(low * inputs + first + item, tall, stride=inputs), :]
+                out[item, part, pl.ds(low, tall), :] = value.astype(jnp.bfloat16)
+                return carry
+
+            lax.fori_loop(0, samples // LANES // tall, gather, 0)
+
+
+def pick(block, first, count):
+    _, inputs, samples = block.shape
+    return pl.pallas_call(
+        functools.partial(pick_kernel, count),
+        out_shape=jax.ShapeDtypeStruct((count, 2, samples // LANES, LANES), jnp.bfloat16),
+        in_specs=[SMEM, VMEM],
+        out_specs=VMEM,
+        scratch_shapes=[pltpu.VMEM((2, samples // LANES * inputs, LANES), jnp.float32)],
+        compiler_params=params(24),
+        cost_estimate=cost(10**6, 8 * 2**20),
+        name="pick",
+    )(first, block)
+
+
+FRONT = 40
+GROUP = 8
+
+
 def filterbank_kernel(count, frames, dests, *refs):
-    scal, keep, recv, halo, coef, first, tw_cos, tw_sin, last = refs[:9]
-    outs = refs[9 : 9 + dests]
-    samples, shifted, grouped = refs[9 + dests :]
+    scal, keep, recv, halo_far, halo_own, coef, first, tw_cos, tw_sin, last = refs[:10]
+    outs = refs[10 : 10 + dests]
+    samples, shifted, grouped = refs[10 + dests :]
     block_rows = frames * ROWS
-    all_rows = (PAIR + 1) * block_rows
-    first_row = (frames - (TAPS - 1)) * ROWS
     total = PAIR * frames
     me = scal[count]
     lane = lax.broadcasted_iota(jnp.int32, (1, LANES), 1)
-
-    step = 8
-    for source, place in ((halo, 0), (keep, 1 + me), (recv, 2 - me)):
-        for part in range(2):
-
-            def unpack(n, carry, source=source, place=place, part=part):
-                wide = source[part, :, pl.ds(pl.multiple_of(n * step * LANES, step * LANES), step * LANES)]
-                wide = wide.astype(jnp.float32)
-                base = (part * all_rows + place * block_rows + n * step) * count
-                for u in range(step):
-                    at = pl.multiple_of(base + u * count, count)
-                    samples[pl.ds(at, count), :] = wide[:, u * LANES : (u + 1) * LANES]
-                return carry
-
-            lax.fori_loop(0, block_rows // step, unpack, 0)
-
-    kept_rows = all_rows - first_row
     high = lane < RADIX
-    for item in range(count):
-        delay = scal[item]
-        down = delay // LANES
-        across = delay % LANES
-        inside = lane < LANES - across
-        piece = ROWS
-        for part in range(2):
-
-            def shift(n, carry, part=part, item=item):
-                row = part * all_rows + first_row + n * piece - down
-                at = row * count + item
-                here = samples[pl.ds(at, piece, stride=count), :]
-                before = samples[pl.ds(at - count, piece, stride=count), :]
-                moved = pltpu.roll(jnp.where(inside, here, before), across, 1)
-                shifted[pl.ds(pl.multiple_of(part * kept_rows + n * piece, piece), piece), :] = moved
-                return carry
-
-            lax.fori_loop(0, kept_rows // piece, shift, 0)
-
-        group = 4
-
-        def filt(n, carry):
-            base = n * group
-            for band in range(ROWS // 16):
-                sums = [[None] * group for _ in range(2)]
-                for part in range(2):
-                    values = []
-                    for u in range(group + TAPS - 1):
-                        at = part * kept_rows + (base + u) * ROWS + band * 16
-                        values.append(shifted[pl.ds(pl.multiple_of(at, 16), 16), :])
-                    for tap in range(TAPS):
-                        weight = coef[tap, band * 16 : band * 16 + 16, :]
-                        for u in range(group):
-                            term = weight * values[u + TAPS - 1 - tap]
-                            old = sums[part][u]
-                            sums[part][u] = term if old is None else old + term
-                for u in range(group):
-                    real, imag = sums[0][u], sums[1][u]
-                    real_turned = pltpu.roll(real, RADIX, 1)
-                    imag_turned = pltpu.roll(imag, RADIX, 1)
-                    parts = (
-                        jnp.where(high, real, imag_turned),
-                        jnp.where(high, real_turned, imag),
-                        jnp.where(high, imag, -real_turned),
-                        jnp.where(high, imag_turned, -real),
-                    )
-                    for index, value in enumerate(parts):
-                        low = index * ROWS + band * 16
-                        grouped[base + u, low : low + 16, :] = value.astype(jnp.bfloat16)
+    tall = 128
+
+    def unpack(source, place, item):
+        def step(n, carry):
+            low = pl.multiple_of(n * tall, tall)
+            for part in range(2):
+                at = pl.multiple_of(FRONT + place * block_rows + low, 8)
+                value = source[item, part, pl.ds(low, tall), :]
+                samples[part, pl.ds(at, tall), :] = value.astype(jnp.float32)
             return carry
 
-        lax.fori_loop(0, total // group, filt, 0)
-
-        def turn(n, carry, item=item):
-            base = n * group
-            wide = jnp.concatenate([grouped[base + u] for u in range(group)], axis=1)
+        lax.fori_loop(0, block_rows // tall, step, 0)
+
+    def filt(m):
+        for band in range(ROWS // 16):
+            sums = [[None] * GROUP for _ in range(2)]
+            for part in range(2):
+                values = []
+                for u in range(GROUP + TAPS - 1):
+                    at = (m * GROUP + frames - TAPS + 1 + u) * ROWS + band * 16
+                    values.append(shifted[part, at : at + 16, :])
+                for tap in range(TAPS):
+                    weight = coef[tap, band * 16 : band * 16 + 16, :]
+                    for u in range(GROUP):
+                        term = weight * values[u + TAPS - 1 - tap]
+                        old = sums[part][u]
+                        sums[part][u] = term if old is None else old + term
+            for u in range(GROUP):
+                real, imag = sums[0][u], sums[1][u]
+                real_turned = pltpu.roll(real, RADIX, 1)
+                imag_turned = pltpu.roll(imag, RADIX, 1)
+                parts = (
+                    jnp.where(high, real, imag_turned),
+                    jnp.where(high, real_turned, imag),
+                    jnp.where(high, imag, -real_turned),
+                    jnp.where(high, imag_turned, -real),
+                )
+                for index, value in enumerate(parts):
+                    low = index * ROWS + band * 16
+                    grouped[m % 2, u, low : low + 16, :] = value.astype(jnp.bfloat16)
+
+    def turn(m, item):
+        some = 4
+        for piece in range(GROUP // some):
+            base = piece * some
+            wide = jnp.concatenate([grouped[m % 2, base + u] for u in range(some)], axis=1)
             inner = jnp.dot(first[...], wide, preferred_element_type=jnp.float32)
             rows = []
-            for u in range(group):
+            for u in range(some):
                 cut = slice(u * LANES, (u + 1) * LANES)
                 turned = inner[:RADIX, cut] * tw_cos[...] + inner[RADIX:, cut] * tw_sin[...]
                 rows.append(turned.astype(jnp.bfloat16))
@@ -176,36 +193,70 @@
             for dest in range(dests):
                 for part in range(2):
                     low = (dest * 2 + part) * size
-                    for u in range(group // 2):
-                        outs[dest][item, n * (group // 2) + u, part] = result[
+                    for u in range(some // 2):
+                        at = (m * GROUP + base) // 2 + u
+                        outs[dest][item, at, part] = result[
                             low : low + size, u * LANES : (u + 1) * LANES
                         ]
+
+    def one(item, carry):
+        @pl.when(me == 0)
+        def _():
+            unpack(halo_far, 0, item)
+
+        @pl.when(me != 0)
+        def _():
+            unpack(halo_own, 0, item)
+
+        unpack(keep, 1 + me, item)
+        unpack(recv, 2 - me, item)
+        delay = scal[item]
+        down = delay // LANES
+        across = delay % LANES
+        inside = lane < LANES - across
+
+        def shift(n, carry):
+            low = pl.multiple_of(n * GROUP * ROWS, GROUP * ROWS)
+            for part in range(2):
+                at = FRONT + low - down
+                here = samples[part, pl.ds(at, GROUP * ROWS), :]
+                before = samples[part, pl.ds(at - 1, GROUP * ROWS), :]
+                moved = pltpu.roll(jnp.where(inside, here, before), across, 1)
+                shifted[part, pl.ds(low, GROUP * ROWS), :] = moved
             return carry
 
-        lax.fori_loop(0, total // group, turn, 0)
-
-
-def filterbank(scal, keep, recv, halo, tables, last, dests):
-    count = keep.shape[1]
-    frames = keep.shape[2] // CHANNELS
+        lax.fori_loop(0, (PAIR + 1) * frames // GROUP, shift, 0)
+        steps = total // GROUP
+        for m in range(steps + 1):
+            if m < steps:
+                filt(m)
+            if m:
+                turn(m - 1, item)
+        return carry
+
+    lax.fori_loop(0, count, one, 0)
+
+
+def filterbank(scal, keep, recv, halo_far, halo_own, tables, last, dests):
+    count = keep.shape[0]
+    frames = keep.shape[2] // ROWS
     size = last.shape[0] // (2 * dests)
     all_rows = (PAIR + 1) * frames * ROWS
-    kept_rows = (PAIR * frames + TAPS - 1) * ROWS
     shape = jax.ShapeDtypeStruct((count, PAIR * frames // 2, 2, size, LANES), jnp.bfloat16)
     return pl.pallas_call(
         functools.partial(filterbank_kernel, count, frames, dests),
         out_shape=[shape] * dests,
-        in_specs=[SMEM] + [VMEM] * 8,
+        in_specs=[SMEM] + [VMEM] * 9,
         out_specs=[VMEM] * dests,
         scratch_shapes=[
-            pltpu.VMEM((2 * all_rows * count, LANES), jnp.float32),
-            pltpu.VMEM((2 * kept_rows, LANES), jnp.float32),
-            pltpu.VMEM((PAIR * frames, LANES, LANES), jnp.bfloat16),
+            pltpu.VMEM((2, FRONT + all_rows, LANES), jnp.float32),
+            pltpu.VMEM((2, all_rows, LANES), jnp.float32),
+            pltpu.VMEM((2, GROUP, LANES, LANES), jnp.bfloat16),
         ],
         compiler_params=params(40),
-        cost_estimate=cost(2 * 10**9, 8 * 2**20),
+        cost_estimate=cost(2 * 10**9, 32 * 2**20),
         name="filterbank",
-    )(scal, keep, recv, halo, *tables, last)
+    )(scal, keep, recv, halo_far, halo_own, *tables, last)
 
 
 def pair_blocks(own):
@@ -216,50 +267,52 @@
 
 
 def correlate_kernel(layout, *refs):
-    count, own, outer, span, pairs, blocks_in, blocks_all = layout
-    sources, (place, starts, where_outer) = refs[: len(pairs)], refs[len(pairs) : len(pairs) + 3]
-    rest = refs[len(pairs) + 3 :]
+    arrays, blocks, outer, span = layout
+    sources, (place, starts, where_outer) = refs[:arrays], refs[arrays : arrays + 3]
+    rest = refs[arrays + 3 :]
     outs, (spectra, sums) = rest[:-2], rest[-2:]
     halves = outer * span // 8
-    pair_count = blocks_in[1], blocks_all
     steps = spectra.shape[1]
+    some = 8
 
     for index, source in enumerate(sources):
-        for item in range(count):
+        for item in range(source.shape[0]):
 
             def spread(n, carry, index=index, source=source, item=item):
-                for part in range(2):
-                    spectra[place[index] + item, n, part] = source[item, n, part].astype(jnp.float32)
+                for u in range(some):
+                    real = source[item, n * some + u, 0].astype(jnp.float32)
+                    imag = source[item, n * some + u, 1].astype(jnp.float32)
+                    for which, value in enumerate((real, imag, real + imag, imag - real)):
+                        spectra[place[index] + item, n * some + u, which] = value
                 return carry
 
-            lax.fori_loop(0, steps, spread, 0)
-
-    lane = lax.broadcasted_iota(jnp.int32, (8, LANES), 1)
-    high = lane < RADIX
-    rows_outer = blocks_all * TILE * TILE * span
+            lax.fori_loop(0, steps // some, spread, 0)
+
+    high = lax.broadcasted_iota(jnp.int32, (1, LANES), 1) < RADIX
+    rows_outer = blocks * TILE * TILE * span
 
     def block(t, carry):
         left, right = starts[2 * t], starts[2 * t + 1]
         for half in range(halves):
             cut = slice(half * 8, half * 8 + 8)
-
-            def frame(n, acc):
-                a = [[spectra[left + p, n, part, cut, :] for part in range(2)] for p in range(TILE)]
-                b = [[spectra[right + q, n, part, cut, :] for part in range(2)] for q in range(TILE)]
-                new = []
-                for p in range(TILE):
-                    for q in range(TILE):
-                        real, imag = acc[2 * (p * TILE + q)], acc[2 * (p * TILE + q) + 1]
-                        real = real + a[p][0] * b[q][0] + a[p][1] * b[q][1]
-                        imag = imag + a[p][1] * b[q][0] - a[p][0] * b[q][1]
-                        new += [real, imag]
-                return tuple(new)
-
-            zero = jnp.zeros((8, LANES), jnp.float32)
-            acc = lax.fori_loop(0, steps, frame, (zero,) * (2 * TILE * TILE))
+            products = []
+            for one, two in ((2, 0), (0, 2), (1, 3)):
+                acc = [None] * (TILE * TILE)
+                for n in range(steps):
+                    a = [spectra[left + p, n, one, cut, :] for p in range(TILE)]
+                    b = [spectra[right + q, n, two, cut, :] for q in range(TILE)]
+                    for p in range(TILE):
+                        for q in range(TILE):
+                            term = a[p] * b[q]
+                            at = p * TILE + q
+                            acc[at] = term if acc[at] is None else acc[at] + term
+                products.append(acc)
             for p in range(TILE * TILE):
-                real = acc[2 * p] + pltpu.roll(acc[2 * p], RADIX, 1)
-                imag = acc[2 * p + 1] + pltpu.roll(acc[2 * p + 1], RADIX, 1)
+                first, second, third = (acc[p] for acc in products)
+                real = first + third
+                imag = first - second
+                real = real + pltpu.roll(real, RADIX, 1)
+                imag = imag + pltpu.roll(imag, RADIX, 1)
                 both = jnp.where(high, real, imag)
                 for u in range(8 // span):
                     o = half * (8 // span) + u
@@ -267,39 +320,33 @@
                     sums[pl.ds(pl.multiple_of(at, span), span), :] = both[u * span : (u + 1) * span]
         return carry
 
-    lax.fori_loop(0, blocks_all, block, 0)
-
-    rows_in = blocks_in[0] * TILE * TILE * span
+    lax.fori_loop(0, blocks, block, 0)
     for r in range(outer):
-        base = lax.rem(where_outer[0] + r, outer) * rows_outer
-        for low, high_row, out in ((0, rows_in, outs[2 * r]), (rows_in, rows_outer, outs[2 * r + 1])):
-            at = pl.multiple_of(base + low, 16)
-            out[...] = sums[pl.ds(at, high_row - low), :].astype(out.dtype)
-
-
-def correlate(arrays, place, starts, where_outer, own, outer, span):
-    count, steps, _, size, _ = arrays[0].shape
-    inside, across = pair_blocks(own)
-    total = len(inside) + len(across)
-    rows = TILE * TILE * span
+        base = pl.multiple_of(lax.rem(where_outer[0] + r, outer) * rows_outer, 16)
+        outs[r][...] = sums[pl.ds(base, rows_outer), :].astype(outs[r].dtype)
+
+
+def correlate(arrays, place, starts, where_outer, inputs, outer, span, name):
+    _, steps, _, size, _ = arrays[0].shape
+    blocks = starts.shape[0] // 2
+    rows = blocks * TILE * TILE * span
     shapes = []
     for r in range(outer):
         dtype = jnp.float32 if r == 0 else jnp.bfloat16
-        shapes.append(jax.ShapeDtypeStruct((len(inside) * rows, LANES), dtype))
-        shapes.append(jax.ShapeDtypeStruct((len(across) * rows, LANES), dtype))
-    layout = (count, own, outer, span, tuple(range(len(arrays))), (len(inside), 0), total)
+        shapes.append(jax.ShapeDtypeStruct((rows, LANES), dtype))
+    layout = (len(arrays), blocks, outer, span)
     return pl.pallas_call(
         functools.partial(correlate_kernel, layout),
         out_shape=shapes,
         in_specs=[VMEM] * len(arrays) + [SMEM] * 3,
         out_specs=[VMEM] * len(shapes),
         scratch_shapes=[
-            pltpu.VMEM((2 * own, steps, 2, size, LANES), jnp.float32),
-            pltpu.VMEM((outer * total * rows, LANES), jnp.float32),
+            pltpu.VMEM((inputs, steps, 4, size, LANES), jnp.float32),
+            pltpu.VMEM((outer * rows, LANES), jnp.float32),
         ],
         compiler_params=params(40),
-        cost_estimate=cost(10**10, 16 * 2**20),
-        name="correlate",
+        cost_estimate=cost(10**9, 20 * 2**20),
+        name=name,
     )(*arrays, place, starts, where_outer)
 
 
@@ -388,7 +435,7 @@
     own = in_count * per_ct
     return (
         frame_count >= TAPS
-        and frame_count % 4 == 0
+        and frame_count % GROUP == 0
         and span in (2, 4, 8)
         and outer * span % 16 == 0
         and own % (2 * TILE) == 0
@@ -412,6 +459,9 @@
     onward = [(i, i + PAIR) for i in range(tm - PAIR)]
     cores = [(0, 1), (1, 0)]
 
+    def stacked(values):
+        return jnp.stack([jnp.asarray(v, jnp.int32) for v in values])
+
     dests = [(dg, dc) for dg in range(PAIR) for dc in range(per_ct)]
     base = jnp.asarray(last_table(outer, per_ct, span))
     base = jnp.where(g == 0, base, base[::-1])
@@ -420,21 +470,21 @@
     tables = [jnp.asarray(filter_table()), jnp.asarray(first_table())]
     tables += [jnp.asarray(t) for t in twiddle_tables()]
 
-    def rows_of(start):
-        return lax.dynamic_slice_in_dim(voltages, start, part, 1)
-
-    keeps, recvs, halos = [], [], []
+    sends = [pick(voltages, stacked([(1 - g) * half + c * part]), part) for c in range(CHUNKS)]
+    keeps = [pick(voltages, stacked([g * half + c * part]), part) for c in range(CHUNKS)]
+    recvs, fars, owns = [], [], []
     for c in range(CHUNKS):
-        keeps.append(rows_of(g * half + c * part))
-        recvs.append(lax.ppermute(rows_of((1 - g) * half + c * part), "tm", swap))
-    for c in range(CHUNKS):
-        halos.append(lax.ppermute(jnp.where(g == 1, keeps[c], recvs[c]), "tm", onward))
-
-    arrays, place = [], []
+        recvs.append(lax.ppermute(sends[c], "tm", swap))
+        owns.append(lax.ppermute(keeps[c], "tm", [p for p in onward if p[0] % PAIR == 1]))
+        fars.append(lax.ppermute(recvs[c], "tm", [p for p in onward if p[0] % PAIR == 0]))
+
+    arrays, others, place = [], [], []
     for c in range(CHUNKS):
         offsets = lax.dynamic_slice_in_dim(delays, g * half + c * part, part, 0)
         scal = jnp.concatenate([offsets, g.astype(jnp.int32)[None]])
-        spectra = filterbank(scal, keeps[c], recvs[c], halos[c], tables, last, len(dests))
+        spectra = filterbank(
+            scal, keeps[c], recvs[c], fars[c], owns[c], tables, last, len(dests)
+        )
         for (dg, dc), block in zip(dests, spectra):
             route = []
             for i in range(tm):
@@ -443,29 +493,32 @@
                     route.append((i * per_ct + j, target))
             if dg or dc:
                 block = lax.ppermute(block, ("tm", "ct"), route)
-            other = lax.ppermute(block, "stn", cores)
-            start = ((place_ct - dc) % per_ct) * in_count + (g ^ dg) * half + c * part
-            arrays += [block, other]
-            place += [core * own + start, (1 - core) * own + start]
+            arrays.append(block)
+            others.append(lax.ppermute(block, "stn", cores))
+            place.append(((place_ct - dc) % per_ct) * in_count + (g ^ dg) * half + c * part)
 
     inside, across = pair_blocks(own)
-    starts = [core * own + TILE * s for block in inside for s in block]
+    starts = stacked([TILE * s for block in inside for s in block])
+    mine_in = correlate(
+        arrays, stacked(place), starts, stacked([o]), own, outer, span, "correlate_own"
+    )
+    starts = []
     for i, j in across:
         starts += [core * (own // 2) + TILE * i, own + TILE * j]
-
-    def stacked(values):
-        return jnp.stack([jnp.asarray(v, jnp.int32) for v in values])
-
-    parts = correlate(arrays, stacked(place), stacked(starts), stacked([o]), own, outer, span)
-    mine_in, mine_across, far_across = [], [], []
+    place = [core * own + s for s in place] + [(1 - core) * own + s for s in place]
+    mine_across = correlate(
+        arrays + others, stacked(place), stacked(starts), stacked([o]), 2 * own, outer, span,
+        "correlate_cross",
+    )
+    mine_in, mine_across, far_across = list(mine_in), list(mine_across), []
+    for r in range(1, outer):
+        route = [(i, (i + r * PAIR) % tm) for i in range(tm)]
+        mine_in[r] = lax.ppermute(mine_in[r], "tm", route)
     for r in range(outer):
-        a, b = parts[2 * r], parts[2 * r + 1]
         if r:
             route = [(i, (i + r * PAIR) % tm) for i in range(tm)]
-            a, b = lax.ppermute(a, "tm", route), lax.ppermute(b, "tm", route)
-        mine_in.append(a)
-        mine_across.append(b)
-        far_across.append(lax.ppermute(b, "stn", cores))
+            mine_across[r] = lax.ppermute(mine_across[r], "tm", route)
+        far_across.append(lax.ppermute(mine_across[r], "stn", cores))
     scale = 1.0 / (tm * frame_count)
     result = assemble(stacked([core]), mine_in, mine_across, far_across, own, span, scale)
     return result.transpose(0, 3, 1, 2)

time: 177 us -> 118 us (0.67)
  Pallas kernels: 80.3 us -> 45.7 us
  waiting for transfers between devices: 56.7 us -> 34.5 us
  other arithmetic: 7.23 us -> 0.94 us
  local copies, waits for them, and re-layouts: 2.46 us -> 5.15 us
    pallas_call x2, Pallas kernels: 53.2 us -> 15.5 us  [filterbank(): pl.pallas_call(functools.partial(filterbank_kernel, count, frames, dests)...]
    ppermute x22 -> x24, waiting for transfers between devices: 38.8 us -> 23 us  [the longest x2 12.8 us: fast(): recvs.append(lax.ppermute(sends[c], 'tm', swap))]
    select_n x2 -> x0, other arithmetic: 7.04 us -> none  [fast(): jnp.where(g == 1, keeps[c], recvs[c])]
    ppermute x6, waiting for transfers between devices: 18 us -> 11.5 us  [fast(): block = lax.ppermute(block, ('tm', 'ct'), route)]
    pallas_call x0 -> x4, Pallas kernels: none -> 5.15 us  [pick(): pl.pallas_call(functools.partial(pick_kernel, count), out_shape=jax.Shape...]
    unnamed x14 -> x28, local copies, waits for them, and re-layouts: 0.03 us -> 4.8 us
    pallas_call x1 -> x2, Pallas kernels: 23.9 us -> 21 us  [correlate(): pl.pallas_call(functools.partial(correlate_kernel, layout), out_shape=sha...]
    dynamic_slice x1 -> x0, local copies, waits for them, and re-layouts: 2.15 us -> none  [rows_of(): return lax.dynamic_slice_in_dim(voltages, start, part, 1)]
  transfers between devices with their start and end apart: 28 -> 30, of which waited for: 12 -> 8; matrix products, arithmetic and copies ran while one was open for 2% -> 1% of each run, Pallas kernels for 30% -> 34%
where the time goes in v2:
time: 118 us; the launch traced here: 117 us
  Pallas kernels  45.7 us (39%)
  waiting for transfers between devices  34.5 us (29%)
  starting transfers between devices  30.6 us (26%)
  local copies, waits for them, and re-layouts  5.15 us (4%)
    pallas_call x2, Pallas kernels, correlate(): pl.pallas_call(functools.partial(correlate_kernel, layout), out_shape=sha...  21 us
    pallas_call x2, Pallas kernels, filterbank(): pl.pallas_call(functools.partial(filterbank_kernel, count, frames, dests)...  15.5 us
    ppermute x2, waiting for transfers between devices, fast(): recvs.append(lax.ppermute(sends[c], 'tm', swap))  12.8 us
    ppermute x6, waiting for transfers between devices, fast(): block = lax.ppermute(block, ('tm', 'ct'), route)  11.5 us
    ppermute x3, waiting for transfers between devices, fast(): mine_across[r] = lax.ppermute(mine_across[r], 'tm', route)  8.15 us
    ppermute x2, starting transfers between devices, fast(): lax.ppermute(recvs[c], 'tm', [p for p in onward if p[0] % PAIR == 0])  7.82 us
    ppermute x6, starting transfers between devices, fast(): block = lax.ppermute(block, ('tm', 'ct'), route)  7.11 us
    pallas_call x4, Pallas kernels, pick(): pl.pallas_call(functools.partial(pick_kernel, count), out_shape=jax.Shape...  5.15 us
  transfers between devices with their start and end apart: 30, of which 8 were waited for; matrix products, arithmetic and copies ran while one was open for 1% of the time, Pallas kernels for 34%

profile of v2, /device:TPU:0, one launch (start us, length us, event | category | flops | bytes accessed | tf_op | source)
XLA Modules:
  0.0 117.2 jit_solution(3564331090412634682)
XLA Ops:
  0.0 1.6 %copy-done = bf16[2,8,65536]{2,1,0:T(8,128)(2,1)S(1)} copy-done((bf16[2,8,65536]{2,1,0:T(8,128)(2,1)S(1)}, bf16[2,8,65536]{2,1,0:T(8,128)(2,1)}, u32[]{:S(2)}) %copy-start) | copy-done | bytes 2097176
  1.6 1.7 %pick.7 = bf16[2,2,512,128]{3,2,1,0:T(8,128)(2,1)} custom-call(s32[1]{0:T(128)} %bitcast.6.scal, bf16[2,8,65536]{2,1,0:T(8,128)(2,1)S(1)} %copy-done), custom_call_target="tpu_custom_call" | custom-call | flops 1000000 | bytes 8388608 | tf_op jit(solution)/shard_map/pick/pallas_call | solution.py:111
  3.3 2.9 %collective-permute-start.6 = (bf16[2,2,512,128]{3,2,1,0:T(8,128)(2,1)}, bf16[2,2,512,128]{3,2,1,0:T(8,128)(2,1)}, u32[]{:S(2)}, u32[]{:S(2)}) collective-permute-start(bf16[2,2,512,128]{3,2,1,0:T(8,128)(2,1)} %pick.7), channel_id=1, source_target_pairs={{0,2},{2,0},{4,6},{6,4},{8,10},{10,8},{12,14},{14,12},{1,3},{3,1},... | collective-permute-start | bytes 1572872 | tf_op jit(solution)/shard_map/ppermute | solution.py:477
  6.2 1.7 %pick.5 = bf16[2,2,512,128]{3,2,1,0:T(8,128)(2,1)} custom-call(s32[1]{0:T(128)} %bitcast.3.scal, bf16[2,8,65536]{2,1,0:T(8,128)(2,1)S(1)} %copy-done), custom_call_target="tpu_custom_call" | custom-call | flops 1000000 | bytes 8388608 | tf_op jit(solution)/shard_map/pick/pallas_call | solution.py:111
  8.0 0.9 pick.6.refs_1_
  8.9 1.5 %collective-permute-start.8 = (bf16[2,2,512,128]{3,2,1,0:T(8,128)(2,1)S(1)}, bf16[2,2,512,128]{3,2,1,0:T(8,128)(2,1)}, u32[]{:S(2)}, u32[]{:S(2)}) collective-permute-start(bf16[2,2,512,128]{3,2,1,0:T(8,128)(2,1)S(1)} %pick.6.refs_1_), channel_id=1, source_target_pairs={{2,6},{6,10},{10,14},{3,7},{7,11},{11,15},{18,22},{22,26},{26,30},... | collective-permute-start | bytes 1572872 | tf_op jit(solution)/shard_map/ppermute | solution.py:478
  10.4 0.9 pick.4.refs_1_
  11.3 0.7 collective-permute-start.2
  12.0 7.3 %collective-permute-done.6.refs_2_ = bf16[2,2,512,128]{3,2,1,0:T(8,128)(2,1)} collective-permute-done((bf16[2,2,512,128]{3,2,1,0:T(8,128)(2,1)}, bf16[2,2,512,128]{3,2,1,0:T(8,128)(2,1)}, u32[]{:S(2)}, u32[]{:S(2)}) %collective-permute-start.6) | collective-permute-done | bytes 524320 | tf_op jit(solution)/shard_map/ppermute | solution.py:477
  19.3 4.1 %collective-permute-start.7 = (bf16[2,2,512,128]{3,2,1,0:T(8,128)(2,1)}, bf16[2,2,512,128]{3,2,1,0:T(8,128)(2,1)S(1)}, u32[]{:S(2)}, u32[]{:S(2)}) collective-permute-start(bf16[2,2,512,128]{3,2,1,0:T(8,128)(2,1)} %collective-permute-done.6.refs_2_), channel_id=1, source_target_pairs={{0,4},{4,8},{8,12},{1,5},{5,9},{9,13},{16,20},{20,24},{24,28},{17,... | collective-permute-start | bytes 1572872 | tf_op jit(solution)/shard_map/ppermute | solution.py:479
  23.4 0.8 broadcast_select_fusion
  24.2 0.1 fusion.1
  24.2 5.5 %collective-permute-done.refs_2_ = bf16[2,2,512,128]{3,2,1,0:T(8,128)(2,1)} collective-permute-done((bf16[2,2,512,128]{3,2,1,0:T(8,128)(2,1)}, bf16[2,2,512,128]{3,2,1,0:T(8,128)(2,1)}, u32[]{:S(2)}, u32[]{:S(2)}) %collective-permute-start) | collective-permute-done | bytes 524320 | tf_op jit(solution)/shard_map/ppermute | solution.py:477
  29.7 3.8 %collective-permute-start.1 = (bf16[2,2,512,128]{3,2,1,0:T(8,128)(2,1)}, bf16[2,2,512,128]{3,2,1,0:T(8,128)(2,1)S(1)}, u32[]{:S(2)}, u32[]{:S(2)}) collective-permute-start(bf16[2,2,512,128]{3,2,1,0:T(8,128)(2,1)} %collective-permute-done.refs_2_), channel_id=1, source_target_pairs={{0,4},{4,8},{8,12},{1,5},{5,9},{9,13},{16,20},{20,24},{24,28},{17,... | collective-permute-start | bytes 1572872 | tf_op jit(solution)/shard_map/ppermute | solution.py:479
  33.5 0.1 pad_add_fusion.1.refs_0_
  33.6 7.8 %filterbank.3 = (bf16[2,16,2,16,128]{4,3,2,1,0:T(8,128)(2,1)S(1)}, bf16[2,16,2,16,128]{4,3,2,1,0:T(8,128)(2,1)S(1)}, bf16[2,16,2,16,128]{4,3,2,1,0:T(8,128)(2,1)S(1)}, bf16[2,16,2,16,128]{4,3,2,1,0:T(8,128)(2,1)S(1)}) custom-call(s32[3]{0:T(128)S(1)} %pad_add_fusion.1.refs_0_, bf16[2,2,512,128]{3,2,1,0:T(8,128)(2,1)S(1)} %pick.6.refs_1_, ...), custom_call_target="tpu_custom_call" | custom-call | flops 2000000000 | bytes 33554432 | tf_op jit(solution)/shard_map/filterbank/pallas_call | solution.py:246
  41.5 1.6 %collective-permute-start.9 = (bf16[2,16,2,16,128]{4,3,2,1,0:T(8,128)(2,1)S(1)}, bf16[2,16,2,16,128]{4,3,2,1,0:T(8,128)(2,1)S(1)}, u32[]{:S(2)}, u32[]{:S(2)}) collective-permute-start(bf16[2,16,2,16,128]{4,3,2,1,0:T(8,128)(2,1)S(1)} %get-tuple-element.26), channel_id=1, source_target_pairs={{0,1},{1,0},{2,3},{3,2},{4,5},{5,4},{6,7},{7,6},{8,9},{9,8},{10,11... | collective-permute-start | bytes 786440 | tf_op jit(solution)/shard_map/ppermute | solution.py:495
  43.0 2.0 %collective-permute-start.11 = (bf16[2,16,2,16,128]{4,3,2,1,0:T(8,128)(2,1)S(1)}, bf16[2,16,2,16,128]{4,3,2,1,0:T(8,128)(2,1)S(1)}, u32[]{:S(2)}, u32[]{:S(2)}) collective-permute-start(bf16[2,16,2,16,128]{4,3,2,1,0:T(8,128)(2,1)S(1)} %get-tuple-element.28), channel_id=1, source_target_pairs={{0,3},{1,2},{2,1},{3,0},{4,7},{5,6},{6,5},{7,4},{8,11},{9,10},{10,... | collective-permute-start | bytes 786440 | tf_op jit(solution)/shard_map/ppermute | solution.py:495
  45.0 0.8 copy-done.2
  45.8 0.1 pad_add_fusion.refs_0_
  45.9 1.0 copy-done.3
  46.9 7.7 %filterbank.2 = (bf16[2,16,2,16,128]{4,3,2,1,0:T(8,128)(2,1)S(1)}, bf16[2,16,2,16,128]{4,3,2,1,0:T(8,128)(2,1)S(1)}, bf16[2,16,2,16,128]{4,3,2,1,0:T(8,128)(2,1)S(1)}, bf16[2,16,2,16,128]{4,3,2,1,0:T(8,128)(2,1)S(1)}) custom-call(s32[3]{0:T(128)S(1)} %pad_add_fusion.refs_0_, bf16[2,2,512,128]{3,2,1,0:T(8,128)(2,1)S(1)} %pick.4.refs_1_, ...), custom_call_target="tpu_custom_call" | custom-call | flops 2000000000 | bytes 33554432 | tf_op jit(solution)/shard_map/filterbank/pallas_call | solution.py:246
  54.6 1.6 %collective-permute-start.3 = (bf16[2,16,2,16,128]{4,3,2,1,0:T(8,128)(2,1)S(1)}, bf16[2,16,2,16,128]{4,3,2,1,0:T(8,128)(2,1)S(1)}, u32[]{:S(2)}, u32[]{:S(2)}) collective-permute-start(bf16[2,16,2,16,128]{4,3,2,1,0:T(8,128)(2,1)S(1)} %get-tuple-element.22), channel_id=1, source_target_pairs={{0,1},{1,0},{2,3},{3,2},{4,5},{5,4},{6,7},{7,6},{8,9},{9,8},{10,11... | collective-permute-start | bytes 786440 | tf_op jit(solution)/shard_map/ppermute | solution.py:495
  56.2 2.0 %collective-permute-start.5 = (bf16[2,16,2,16,128]{4,3,2,1,0:T(8,128)(2,1)S(1)}, bf16[2,16,2,16,128]{4,3,2,1,0:T(8,128)(2,1)S(1)}, u32[]{:S(2)}, u32[]{:S(2)}) collective-permute-start(bf16[2,16,2,16,128]{4,3,2,1,0:T(8,128)(2,1)S(1)} %get-tuple-element.24), channel_id=1, source_target_pairs={{0,3},{1,2},{2,1},{3,0},{4,7},{5,6},{6,5},{7,4},{8,11},{9,10},{10,... | collective-permute-start | bytes 786440 | tf_op jit(solution)/shard_map/ppermute | solution.py:495
  58.2 0.5 collective-permute-start.20
  58.7 4.7 %collective-permute-done.3.refs_1_ = bf16[2,16,2,16,128]{4,3,2,1,0:T(8,128)(2,1)S(1)} collective-permute-done((bf16[2,16,2,16,128]{4,3,2,1,0:T(8,128)(2,1)S(1)}, bf16[2,16,2,16,128]{4,3,2,1,0:T(8,128)(2,1)S(1)}, u32[]{:S(2)}, u32[]{:S(2)}) %collective-permute-start.3) | collective-permute-done | bytes 262176 | tf_op jit(solution)/shard_map/ppermute | solution.py:495
  63.4 1.9 %collective-permute-done.4.refs_2_ = bf16[2,16,2,16,128]{4,3,2,1,0:T(8,128)(2,1)S(1)} collective-permute-done((bf16[2,16,2,16,128]{4,3,2,1,0:T(8,128)(2,1)S(1)}, bf16[2,16,2,16,128]{4,3,2,1,0:T(8,128)(2,1)S(1)}, u32[]{:S(2)}, u32[]{:S(2)}) %collective-permute-start.4) | collective-permute-done | bytes 262176 | tf_op jit(solution)/shard_map/ppermute | solution.py:495
  65.3 4.9 %collective-permute-done.5.refs_3_ = bf16[2,16,2,16,128]{4,3,2,1,0:T(8,128)(2,1)S(1)} collective-permute-done((bf16[2,16,2,16,128]{4,3,2,1,0:T(8,128)(2,1)S(1)}, bf16[2,16,2,16,128]{4,3,2,1,0:T(8,128)(2,1)S(1)}, u32[]{:S(2)}, u32[]{:S(2)}) %collective-permute-start.5) | collective-permute-done | bytes 262176 | tf_op jit(solution)/shard_map/ppermute | solution.py:495
  70.2 0.5 collective-permute-start.17
  70.7 0.1 collective-permute-start.18
  70.8 0.1 stack.125.refs_8_
  70.9 11.0 %correlate_own.1 = (f32[640,128]{1,0:T(8,128)S(1)}, bf16[640,128]{1,0:T(8,128)(2,1)}, bf16[640,128]{1,0:T(8,128)(2,1)S(1)}, bf16[640,128]{1,0:T(8,128)(2,1)S(1)}) custom-call(bf16[2,16,2,16,128]{4,3,2,1,0:T(8,128)(2,1)S(1)} %get-tuple-element.21.refs_0_, bf16[2,16,2,16,128]{4,3,2,1,0:T(8,128)(2,1)S(1)} %collective-permute-done.3.refs_1_, ...), custom_call_target="tpu_custom_call" | custom-call | flops 1000000000 | bytes 20971520 | tf_op jit(solution)/shard_map/correlate_own/pallas_call | solution.py:338
  81.9 0.7 copy-done.4
  82.6 0.7 copy-done.6
  83.2 1.6 %collective-permute-start.12 = (bf16[640,128]{1,0:T(8,128)(2,1)}, bf16[640,128]{1,0:T(8,128)(2,1)}, u32[]{:S(2)}, u32[]{:S(2)}) collective-permute-start(bf16[640,128]{1,0:T(8,128)(2,1)} %get-tuple-element.30), channel_id=1, source_target_pairs={{0,4},{2,6},{4,8},{6,10},{8,12},{10,14},{12,0},{14,2},{1,5},{3,7},... | collective-permute-start | bytes 491528 | tf_op jit(solution)/shard_map/ppermute | solution.py:516
  84.8 0.1 stack.146.refs_17_
  84.9 0.1 stack.143.refs_16_
  85.0 2.7 %collective-permute-start.13 = (bf16[640,128]{1,0:T(8,128)(2,1)}, bf16[640,128]{1,0:T(8,128)(2,1)S(1)}, u32[]{:S(2)}, u32[]{:S(2)}) collective-permute-start(bf16[640,128]{1,0:T(8,128)(2,1)} %copy-done.6), channel_id=1, source_target_pairs={{0,8},{2,10},{4,12},{6,14},{8,0},{10,2},{12,4},{14,6},{1,9},{3,11}... | collective-permute-start | bytes 491528 | tf_op jit(solution)/shard_map/ppermute | solution.py:516
  87.7 9.9 %correlate_cross.1 = (f32[512,128]{1,0:T(8,128)S(1)}, bf16[512,128]{1,0:T(8,128)(2,1)S(1)}, bf16[512,128]{1,0:T(8,128)(2,1)S(1)}, bf16[512,128]{1,0:T(8,128)(2,1)S(1)}) custom-call(bf16[2,16,2,16,128]{4,3,2,1,0:T(8,128)(2,1)S(1)} %get-tuple-element.21.refs_0_, bf16[2,16,2,16,128]{4,3,2,1,0:T(8,128)(2,1)S(1)} %collective-permute-done.3.refs_1_, ...), custom_call_target="tpu_custom_call" | custom-call | flops 1000000000 | bytes 20971520 | tf_op jit(solution)/shard_map/correlate_cross/pallas_call | solution.py:338
  97.6 0.3 collective-permute-start.23
  97.9 1.7 %collective-permute-start.24 = (bf16[512,128]{1,0:T(8,128)(2,1)S(1)}, bf16[512,128]{1,0:T(8,128)(2,1)S(1)}, u32[]{:S(2)}, u32[]{:S(2)}) collective-permute-start(bf16[512,128]{1,0:T(8,128)(2,1)S(1)} %get-tuple-element.35), channel_id=1, source_target_pairs={{0,8},{2,10},{4,12},{6,14},{8,0},{10,2},{12,4},{14,6},{1,9},{3,11}... | collective-permute-start | bytes 393224 | tf_op jit(solution)/shard_map/ppermute | solution.py:520
  99.6 1.9 %collective-permute-start.25 = (bf16[512,128]{1,0:T(8,128)(2,1)S(1)}, bf16[512,128]{1,0:T(8,128)(2,1)S(1)}, u32[]{:S(2)}, u32[]{:S(2)}) collective-permute-start(bf16[512,128]{1,0:T(8,128)(2,1)S(1)} %get-tuple-element.36), channel_id=1, source_target_pairs={{0,12},{2,14},{4,0},{6,2},{8,4},{10,6},{12,8},{14,10},{1,13},{3,15... | collective-permute-start | bytes 393224 | tf_op jit(solution)/shard_map/ppermute | solution.py:520
  101.5 0.8 collective-permute-start.14
  102.4 3.6 %collective-permute-done.23.refs_6_ = bf16[512,128]{1,0:T(8,128)(2,1)S(1)} collective-permute-done((bf16[512,128]{1,0:T(8,128)(2,1)S(1)}, bf16[512,128]{1,0:T(8,128)(2,1)S(1)}, u32[]{:S(2)}, u32[]{:S(2)}) %collective-permute-start.23) | collective-permute-done | bytes 131104 | tf_op jit(solution)/shard_map/ppermute | solution.py:520
  105.9 4.6 %collective-permute-done.24.refs_7_ = bf16[512,128]{1,0:T(8,128)(2,1)S(1)} collective-permute-done((bf16[512,128]{1,0:T(8,128)(2,1)S(1)}, bf16[512,128]{1,0:T(8,128)(2,1)S(1)}, u32[]{:S(2)}, u32[]{:S(2)}) %collective-permute-start.24) | collective-permute-done | bytes 131104 | tf_op jit(solution)/shard_map/ppermute | solution.py:520
  110.5 0.5 collective-permute-start.29
  111.0 2.0 %collective-permute-done.14.refs_4_ = bf16[640,128]{1,0:T(8,128)(2,1)S(1)} collective-permute-done((bf16[640,128]{1,0:T(8,128)(2,1)S(1)}, bf16[640,128]{1,0:T(8,128)(2,1)S(1)}, u32[]{:S(2)}, u32[]{:S(2)}) %collective-permute-start.14) | collective-permute-done | bytes 163872 | tf_op jit(solution)/shard_map/ppermute | solution.py:516
  113.1 4.1 %assemble.1 = f32[2,16,32,256]{3,2,1,0:T(8,128)} custom-call(s32[1]{0:T(128)} %bitcast.refs_0_, f32[640,128]{1,0:T(8,128)S(1)} %get-tuple-element.29.refs_1_, bf16[640,128]{1,0:T(8,128)(2,1)} %collective-permute-done.12.refs_2_, bf16[640,128]{1,0:T(8,128)(2,1)S(1)} %collective-permute-done.13.refs_3_, bf16[640,128]{1,0:T(8,128)(2,1)S(1)} %collective-permute-done.14.refs_4_, ...), custom_call_target="tpu_custom_call" | custom-call | flops 100000000 | bytes 8388608 | tf_op jit(solution)/shard_map/assemble/pallas_call | solution.py:417
  (57 shorter events, 0.2 us)
Async XLA Ops:
  0.0 1.6 %copy-start = (bf16[2,8,65536]{2,1,0:T(8,128)(2,1)S(1)}, bf16[2,8,65536]{2,1,0:T(8,128)(2,1)}, u32[]{:S(2)}) copy-start(bf16[2,8,65536]{2,1,0:T(8,128)(2,1)} %block.7) | copy-start | bytes 6291460
  1.6 6.3 %copy-start.1 = (bf16[2,8,65536]{2,1,0:T(8,128)(2,1)S(1)}, bf16[2,8,65536]{2,1,0:T(8,128)(2,1)}, u32[]{:S(2)}) copy-start(bf16[2,8,65536]{2,1,0:T(8,128)(2,1)} %block.7) | copy-start | bytes 6291460
  3.3 16.0 %collective-permute-start.6 = (bf16[2,2,512,128]{3,2,1,0:T(8,128)(2,1)}, bf16[2,2,512,128]{3,2,1,0:T(8,128)(2,1)}, u32[]{:S(2)}, u32[]{:S(2)}) collective-permute-start(bf16[2,2,512,128]{3,2,1,0:T(8,128)(2,1)} %pick.7), channel_id=1, source_target_pairs={{0,2},{2,0},{4,6},{6,4},{8,10},{10,8},{12,14},{14,12},{1,3},{3,1},... | collective-permute-start | bytes 1572872 | tf_op jit(solution)/shard_map/ppermute | solution.py:477
  7.9 21.8 %collective-permute-start = (bf16[2,2,512,128]{3,2,1,0:T(8,128)(2,1)}, bf16[2,2,512,128]{3,2,1,0:T(8,128)(2,1)}, u32[]{:S(2)}, u32[]{:S(2)}) collective-permute-start(bf16[2,2,512,128]{3,2,1,0:T(8,128)(2,1)} %pick.5), channel_id=1, source_target_pairs={{0,2},{2,0},{4,6},{6,4},{8,10},{10,8},{12,14},{14,12},{1,3},{3,1},... | collective-permute-start | bytes 1572872 | tf_op jit(solution)/shard_map/ppermute | solution.py:477
  7.9 15.5 %copy-start.12 = (bf16[2,2,32,128]{3,2,1,0:T(8,128)(2,1)S(1)}, bf16[2,2,32,128]{3,2,1,0:T(8,128)(2,1)}, u32[]{:S(2)}) copy-start(bf16[2,2,32,128]{3,2,1,0:T(8,128)(2,1)} %constant.92) | copy-start | bytes 98308
  7.9 16.2 %copy-start.13 = (s32[8]{0:T(128)S(1)}, s32[8]{0:T(128)}, u32[]{:S(2)}) copy-start(s32[8]{0:T(128)} %param.8) | copy-start | bytes 100
  7.9 25.7 %copy-start.7 = (f32[16,32,128]{2,1,0:T(8,128)S(1)}, f32[16,32,128]{2,1,0:T(8,128)}, u32[]{:S(2)}) copy-start(f32[16,32,128]{2,1,0:T(8,128)} %constant.88.clone.refs_5_) | copy-start | bytes 786436
  7.9 25.7 %copy-start.8 = (f32[64,128]{1,0:T(8,128)S(1)}, f32[64,128]{1,0:T(8,128)}, u32[]{:S(2)}) copy-start(f32[64,128]{1,0:T(8,128)} %constant.91.clone.refs_8_) | copy-start | bytes 98308
  8.0 25.7 %copy-start.9 = (f32[64,128]{1,0:T(8,128)S(1)}, f32[64,128]{1,0:T(8,128)}, u32[]{:S(2)}) copy-start(f32[64,128]{1,0:T(8,128)} %constant.90.clone.refs_7_) | copy-start | bytes 98308
  8.0 25.7 %copy-start.10 = (bf16[128,128]{1,0:T(8,128)(2,1)S(1)}, bf16[128,128]{1,0:T(8,128)(2,1)}, u32[]{:S(2)}) copy-start(bf16[128,128]{1,0:T(8,128)(2,1)} %constant.89.clone.refs_6_) | copy-start | bytes 98308
  8.9 24.7 %collective-permute-start.8 = (bf16[2,2,512,128]{3,2,1,0:T(8,128)(2,1)S(1)}, bf16[2,2,512,128]{3,2,1,0:T(8,128)(2,1)}, u32[]{:S(2)}, u32[]{:S(2)}) collective-permute-start(bf16[2,2,512,128]{3,2,1,0:T(8,128)(2,1)S(1)} %pick.6.refs_1_), channel_id=1, source_target_pairs={{2,6},{6,10},{10,14},{3,7},{7,11},{11,15},{18,22},{22,26},{26,30},... | collective-permute-start | bytes 1572872 | tf_op jit(solution)/shard_map/ppermute | solution.py:478
  11.3 33.8 %collective-permute-start.2 = (bf16[2,2,512,128]{3,2,1,0:T(8,128)(2,1)S(1)}, bf16[2,2,512,128]{3,2,1,0:T(8,128)(2,1)S(1)}, u32[]{:S(2)}, u32[]{:S(2)}) collective-permute-start(bf16[2,2,512,128]{3,2,1,0:T(8,128)(2,1)S(1)} %pick.4.refs_1_), channel_id=1, source_target_pairs={{2,6},{6,10},{10,14},{3,7},{7,11},{11,15},{18,22},{22,26},{26,30},... | collective-permute-start | bytes 1572872 | tf_op jit(solution)/shard_map/ppermute | solution.py:478
  19.3 14.3 %collective-permute-start.7 = (bf16[2,2,512,128]{3,2,1,0:T(8,128)(2,1)}, bf16[2,2,512,128]{3,2,1,0:T(8,128)(2,1)S(1)}, u32[]{:S(2)}, u32[]{:S(2)}) collective-permute-start(bf16[2,2,512,128]{3,2,1,0:T(8,128)(2,1)} %collective-permute-done.6.refs_2_), channel_id=1, source_target_pairs={{0,4},{4,8},{8,12},{1,5},{5,9},{9,13},{16,20},{20,24},{24,28},{17,... | collective-permute-start | bytes 1572872 | tf_op jit(solution)/shard_map/ppermute | solution.py:479
  29.7 16.2 %collective-permute-start.1 = (bf16[2,2,512,128]{3,2,1,0:T(8,128)(2,1)}, bf16[2,2,512,128]{3,2,1,0:T(8,128)(2,1)S(1)}, u32[]{:S(2)}, u32[]{:S(2)}) collective-permute-start(bf16[2,2,512,128]{3,2,1,0:T(8,128)(2,1)} %collective-permute-done.refs_2_), channel_id=1, source_target_pairs={{0,4},{4,8},{8,12},{1,5},{5,9},{9,13},{16,20},{20,24},{24,28},{17,... | collective-permute-start | bytes 1572872 | tf_op jit(solution)/shard_map/ppermute | solution.py:479
  41.5 14.7 %collective-permute-start.9 = (bf16[2,16,2,16,128]{4,3,2,1,0:T(8,128)(2,1)S(1)}, bf16[2,16,2,16,128]{4,3,2,1,0:T(8,128)(2,1)S(1)}, u32[]{:S(2)}, u32[]{:S(2)}) collective-permute-start(bf16[2,16,2,16,128]{4,3,2,1,0:T(8,128)(2,1)S(1)} %get-tuple-element.26), channel_id=1, source_target_pairs={{0,1},{1,0},{2,3},{3,2},{4,5},{5,4},{6,7},{7,6},{8,9},{9,8},{10,11... | collective-permute-start | bytes 786440 | tf_op jit(solution)/shard_map/ppermute | solution.py:495
  43.0 13.2 %collective-permute-start.10 = (bf16[2,16,2,16,128]{4,3,2,1,0:T(8,128)(2,1)S(1)}, bf16[2,16,2,16,128]{4,3,2,1,0:T(8,128)(2,1)S(1)}, u32[]{:S(2)}, u32[]{:S(2)}) collective-permute-start(bf16[2,16,2,16,128]{4,3,2,1,0:T(8,128)(2,1)S(1)} %get-tuple-element.27), channel_id=1, source_target_pairs={{0,2},{1,3},{2,0},{3,1},{4,6},{5,7},{6,4},{7,5},{8,10},{9,11},{10,... | collective-permute-start | bytes 786440 | tf_op jit(solution)/shard_map/ppermute | solution.py:495
  43.0 15.1 %collective-permute-start.11 = (bf16[2,16,2,16,128]{4,3,2,1,0:T(8,128)(2,1)S(1)}, bf16[2,16,2,16,128]{4,3,2,1,0:T(8,128)(2,1)S(1)}, u32[]{:S(2)}, u32[]{:S(2)}) collective-permute-start(bf16[2,16,2,16,128]{4,3,2,1,0:T(8,128)(2,1)S(1)} %get-tuple-element.28), channel_id=1, source_target_pairs={{0,3},{1,2},{2,1},{3,0},{4,7},{5,6},{6,5},{7,4},{8,11},{9,10},{10,... | collective-permute-start | bytes 786440 | tf_op jit(solution)/shard_map/ppermute | solution.py:495
  45.0 0.8 copy-start.2
  45.8 12.4 %collective-permute-start.19 = (bf16[2,16,2,16,128]{4,3,2,1,0:T(8,128)(2,1)S(1)}, bf16[2,16,2,16,128]{4,3,2,1,0:T(8,128)(2,1)S(1)}, u32[]{:S(2)}, u32[]{:S(2)}) collective-permute-start(bf16[2,16,2,16,128]{4,3,2,1,0:T(8,128)(2,1)S(1)} %get-tuple-element.25.refs_4_), channel_id=1, source_target_pairs={{0,16},{16,0},{1,17},{17,1},{2,18},{18,2},{3,19},{19,3},{4,20},{20... | collective-permute-start | bytes 786440 | tf_op jit(solution)/shard_map/ppermute | solution.py:497
  45.9 1.0 copy-start.3
  46.9 23.9 %copy-start.11 = (s32[20]{0:T(128)S(1)}, s32[20]{0:T(128)}, u32[]{:S(2)}) copy-start(s32[20]{0:T(128)} %constant.81.clone.1.refs_9_) | copy-start | bytes 244
  54.6 8.8 %collective-permute-start.3 = (bf16[2,16,2,16,128]{4,3,2,1,0:T(8,128)(2,1)S(1)}, bf16[2,16,2,16,128]{4,3,2,1,0:T(8,128)(2,1)S(1)}, u32[]{:S(2)}, u32[]{:S(2)}) collective-permute-start(bf16[2,16,2,16,128]{4,3,2,1,0:T(8,128)(2,1)S(1)} %get-tuple-element.22), channel_id=1, source_target_pairs={{0,1},{1,0},{2,3},{3,2},{4,5},{5,4},{6,7},{7,6},{8,9},{9,8},{10,11... | collective-permute-start | bytes 786440 | tf_op jit(solution)/shard_map/ppermute | solution.py:495
  56.2 9.1 %collective-permute-start.4 = (bf16[2,16,2,16,128]{4,3,2,1,0:T(8,128)(2,1)S(1)}, bf16[2,16,2,16,128]{4,3,2,1,0:T(8,128)(2,1)S(1)}, u32[]{:S(2)}, u32[]{:S(2)}) collective-permute-start(bf16[2,16,2,16,128]{4,3,2,1,0:T(8,128)(2,1)S(1)} %get-tuple-element.23), channel_id=1, source_target_pairs={{0,2},{1,3},{2,0},{3,1},{4,6},{5,7},{6,4},{7,5},{8,10},{9,11},{10,... | collective-permute-start | bytes 786440 | tf_op jit(solution)/shard_map/ppermute | solution.py:495
  56.2 14.0 %collective-permute-start.5 = (bf16[2,16,2,16,128]{4,3,2,1,0:T(8,128)(2,1)S(1)}, bf16[2,16,2,16,128]{4,3,2,1,0:T(8,128)(2,1)S(1)}, u32[]{:S(2)}, u32[]{:S(2)}) collective-permute-start(bf16[2,16,2,16,128]{4,3,2,1,0:T(8,128)(2,1)S(1)} %get-tuple-element.24), channel_id=1, source_target_pairs={{0,3},{1,2},{2,1},{3,0},{4,7},{5,6},{6,5},{7,4},{8,11},{9,10},{10,... | collective-permute-start | bytes 786440 | tf_op jit(solution)/shard_map/ppermute | solution.py:495
  58.2 12.0 %collective-permute-start.15 = (bf16[2,16,2,16,128]{4,3,2,1,0:T(8,128)(2,1)S(1)}, bf16[2,16,2,16,128]{4,3,2,1,0:T(8,128)(2,1)S(1)}, u32[]{:S(2)}, u32[]{:S(2)}) collective-permute-start(bf16[2,16,2,16,128]{4,3,2,1,0:T(8,128)(2,1)S(1)} %get-tuple-element.21.refs_0_), channel_id=1, source_target_pairs={{0,16},{16,0},{1,17},{17,1},{2,18},{18,2},{3,19},{19,3},{4,20},{20... | collective-permute-start | bytes 786440 | tf_op jit(solution)/shard_map/ppermute | solution.py:497
  58.2 12.5 %collective-permute-start.20 = (bf16[2,16,2,16,128]{4,3,2,1,0:T(8,128)(2,1)S(1)}, bf16[2,16,2,16,128]{4,3,2,1,0:T(8,128)(2,1)S(1)}, u32[]{:S(2)}, u32[]{:S(2)}) collective-permute-start(bf16[2,16,2,16,128]{4,3,2,1,0:T(8,128)(2,1)S(1)} %collective-permute-done.9.refs_5_), channel_id=1, source_target_pairs={{0,16},{16,0},{1,17},{17,1},{2,18},{18,2},{3,19},{19,3},{4,20},{20... | collective-permute-start | bytes 786440 | tf_op jit(solution)/shard_map/ppermute | solution.py:497
  63.4 19.2 %collective-permute-start.21 = (bf16[2,16,2,16,128]{4,3,2,1,0:T(8,128)(2,1)S(1)}, bf16[2,16,2,16,128]{4,3,2,1,0:T(8,128)(2,1)S(1)}, u32[]{:S(2)}, u32[]{:S(2)}) collective-permute-start(bf16[2,16,2,16,128]{4,3,2,1,0:T(8,128)(2,1)S(1)} %collective-permute-done.10.refs_6_), channel_id=1, source_target_pairs={{0,16},{16,0},{1,17},{17,1},{2,18},{18,2},{3,19},{19,3},{4,20},{20... | collective-permute-start | bytes 786440 | tf_op jit(solution)/shard_map/ppermute | solution.py:497
  65.3 19.7 %collective-permute-start.22 = (bf16[2,16,2,16,128]{4,3,2,1,0:T(8,128)(2,1)S(1)}, bf16[2,16,2,16,128]{4,3,2,1,0:T(8,128)(2,1)}, u32[]{:S(2)}, u32[]{:S(2)}) collective-permute-start(bf16[2,16,2,16,128]{4,3,2,1,0:T(8,128)(2,1)S(1)} %collective-permute-done.11.refs_7_), channel_id=1, source_target_pairs={{0,16},{16,0},{1,17},{17,1},{2,18},{18,2},{3,19},{19,3},{4,20},{20... | collective-permute-start | bytes 786440 | tf_op jit(solution)/shard_map/ppermute | solution.py:497
  70.2 17.5 %collective-permute-start.16 = (bf16[2,16,2,16,128]{4,3,2,1,0:T(8,128)(2,1)S(1)}, bf16[2,16,2,16,128]{4,3,2,1,0:T(8,128)(2,1)}, u32[]{:S(2)}, u32[]{:S(2)}) collective-permute-start(bf16[2,16,2,16,128]{4,3,2,1,0:T(8,128)(2,1)S(1)} %collective-permute-done.3.refs_1_), channel_id=1, source_target_pairs={{0,16},{16,0},{1,17},{17,1},{2,18},{18,2},{3,19},{19,3},{4,20},{20... | collective-permute-start | bytes 786440 | tf_op jit(solution)/shard_map/ppermute | solution.py:497
  70.2 17.5 %collective-permute-start.17 = (bf16[2,16,2,16,128]{4,3,2,1,0:T(8,128)(2,1)S(1)}, bf16[2,16,2,16,128]{4,3,2,1,0:T(8,128)(2,1)}, u32[]{:S(2)}, u32[]{:S(2)}) collective-permute-start(bf16[2,16,2,16,128]{4,3,2,1,0:T(8,128)(2,1)S(1)} %collective-permute-done.4.refs_2_), channel_id=1, source_target_pairs={{0,16},{16,0},{1,17},{17,1},{2,18},{18,2},{3,19},{19,3},{4,20},{20... | collective-permute-start | bytes 786440 | tf_op jit(solution)/shard_map/ppermute | solution.py:497
  70.7 17.0 %collective-permute-start.18 = (bf16[2,16,2,16,128]{4,3,2,1,0:T(8,128)(2,1)S(1)}, bf16[2,16,2,16,128]{4,3,2,1,0:T(8,128)(2,1)}, u32[]{:S(2)}, u32[]{:S(2)}) collective-permute-start(bf16[2,16,2,16,128]{4,3,2,1,0:T(8,128)(2,1)S(1)} %collective-permute-done.5.refs_3_), channel_id=1, source_target_pairs={{0,16},{16,0},{1,17},{17,1},{2,18},{18,2},{3,19},{19,3},{4,20},{20... | collective-permute-start | bytes 786440 | tf_op jit(solution)/shard_map/ppermute | solution.py:497
  81.9 0.7 copy-start.4
  82.6 0.7 copy-start.6
  83.2 18.3 %collective-permute-start.12 = (bf16[640,128]{1,0:T(8,128)(2,1)}, bf16[640,128]{1,0:T(8,128)(2,1)}, u32[]{:S(2)}, u32[]{:S(2)}) collective-permute-start(bf16[640,128]{1,0:T(8,128)(2,1)} %get-tuple-element.30), channel_id=1, source_target_pairs={{0,4},{2,6},{4,8},{6,10},{8,12},{10,14},{12,0},{14,2},{1,5},{3,7},... | collective-permute-start | bytes 491528 | tf_op jit(solution)/shard_map/ppermute | solution.py:516
  85.0 16.5 %copy-start.5 = (bf16[640,128]{1,0:T(8,128)(2,1)S(1)}, bf16[640,128]{1,0:T(8,128)(2,1)}, u32[]{:S(2)}) copy-start(bf16[640,128]{1,0:T(8,128)(2,1)} %copy-done.4) | copy-start | bytes 491524
  85.0 16.5 %collective-permute-start.13 = (bf16[640,128]{1,0:T(8,128)(2,1)}, bf16[640,128]{1,0:T(8,128)(2,1)S(1)}, u32[]{:S(2)}, u32[]{:S(2)}) collective-permute-start(bf16[640,128]{1,0:T(8,128)(2,1)} %copy-done.6), channel_id=1, source_target_pairs={{0,8},{2,10},{4,12},{6,14},{8,0},{10,2},{12,4},{14,6},{1,9},{3,11}... | collective-permute-start | bytes 491528 | tf_op jit(solution)/shard_map/ppermute | solution.py:516
  97.6 8.3 %collective-permute-start.23 = (bf16[512,128]{1,0:T(8,128)(2,1)S(1)}, bf16[512,128]{1,0:T(8,128)(2,1)S(1)}, u32[]{:S(2)}, u32[]{:S(2)}) collective-permute-start(bf16[512,128]{1,0:T(8,128)(2,1)S(1)} %get-tuple-element.34), channel_id=1, source_target_pairs={{0,4},{2,6},{4,8},{6,10},{8,12},{10,14},{12,0},{14,2},{1,5},{3,7},... | collective-permute-start | bytes 393224 | tf_op jit(solution)/shard_map/ppermute | solution.py:520
  97.9 12.6 %collective-permute-start.24 = (bf16[512,128]{1,0:T(8,128)(2,1)S(1)}, bf16[512,128]{1,0:T(8,128)(2,1)S(1)}, u32[]{:S(2)}, u32[]{:S(2)}) collective-permute-start(bf16[512,128]{1,0:T(8,128)(2,1)S(1)} %get-tuple-element.35), channel_id=1, source_target_pairs={{0,8},{2,10},{4,12},{6,14},{8,0},{10,2},{12,4},{14,6},{1,9},{3,11}... | collective-permute-start | bytes 393224 | tf_op jit(solution)/shard_map/ppermute | solution.py:520
  99.6 10.9 %collective-permute-start.25 = (bf16[512,128]{1,0:T(8,128)(2,1)S(1)}, bf16[512,128]{1,0:T(8,128)(2,1)S(1)}, u32[]{:S(2)}, u32[]{:S(2)}) collective-permute-start(bf16[512,128]{1,0:T(8,128)(2,1)S(1)} %get-tuple-element.36), channel_id=1, source_target_pairs={{0,12},{2,14},{4,0},{6,2},{8,4},{10,6},{12,8},{14,10},{1,13},{3,15... | collective-permute-start | bytes 393224 | tf_op jit(solution)/shard_map/ppermute | solution.py:520
  101.5 11.6 %collective-permute-start.26 = (f32[512,128]{1,0:T(8,128)S(1)}, f32[512,128]{1,0:T(8,128)S(1)}, u32[]{:S(2)}, u32[]{:S(2)}) collective-permute-start(f32[512,128]{1,0:T(8,128)S(1)} %get-tuple-element.33.refs_5_), channel_id=1, source_target_pairs={{0,16},{16,0},{1,17},{17,1},{2,18},{18,2},{3,19},{19,3},{4,20},{20... | collective-permute-start | bytes 786440 | tf_op jit(solution)/shard_map/ppermute | solution.py:521
  101.5 11.5 %collective-permute-start.14 = (bf16[640,128]{1,0:T(8,128)(2,1)S(1)}, bf16[640,128]{1,0:T(8,128)(2,1)S(1)}, u32[]{:S(2)}, u32[]{:S(2)}) collective-permute-start(bf16[640,128]{1,0:T(8,128)(2,1)S(1)} %copy-done.5), channel_id=1, source_target_pairs={{0,12},{2,14},{4,0},{6,2},{8,4},{10,6},{12,8},{14,10},{1,13},{3,15... | collective-permute-start | bytes 491528 | tf_op jit(solution)/shard_map/ppermute | solution.py:516
  105.9 7.1 %collective-permute-start.27 = (bf16[512,128]{1,0:T(8,128)(2,1)S(1)}, bf16[512,128]{1,0:T(8,128)(2,1)S(1)}, u32[]{:S(2)}, u32[]{:S(2)}) collective-permute-start(bf16[512,128]{1,0:T(8,128)(2,1)S(1)} %collective-permute-done.23.refs_6_), channel_id=1, source_target_pairs={{0,16},{16,0},{1,17},{17,1},{2,18},{18,2},{3,19},{19,3},{4,20},{20... | collective-permute-start | bytes 393224 | tf_op jit(solution)/shard_map/ppermute | solution.py:521
  110.5 2.6 %collective-permute-start.28 = (bf16[512,128]{1,0:T(8,128)(2,1)S(1)}, bf16[512,128]{1,0:T(8,128)(2,1)S(1)}, u32[]{:S(2)}, u32[]{:S(2)}) collective-permute-start(bf16[512,128]{1,0:T(8,128)(2,1)S(1)} %collective-permute-done.24.refs_7_), channel_id=1, source_target_pairs={{0,16},{16,0},{1,17},{17,1},{2,18},{18,2},{3,19},{19,3},{4,20},{20... | collective-permute-start | bytes 393224 | tf_op jit(solution)/shard_map/ppermute | solution.py:521
  110.5 2.6 %collective-permute-start.29 = (bf16[512,128]{1,0:T(8,128)(2,1)S(1)}, bf16[512,128]{1,0:T(8,128)(2,1)S(1)}, u32[]{:S(2)}, u32[]{:S(2)}) collective-permute-start(bf16[512,128]{1,0:T(8,128)(2,1)S(1)} %collective-permute-done.25.refs_8_), channel_id=1, source_target_pairs={{0,16},{16,0},{1,17},{17,1},{2,18},{18,2},{3,19},{19,3},{4,20},{20... | collective-permute-start | bytes 393224 | tf_op jit(solution)/shard_map/ppermute | solution.py:521

commit v3 on v2

--- a/solution.py
+++ b/solution.py
@@ -16,10 +16,11 @@
 ROWS = CHANNELS // LANES
 PAIR = 2
 TILE = 4
-CHUNKS = 2
+JOIN = 2
 
 VMEM = pl.BlockSpec(memory_space=pltpu.VMEM)
 SMEM = pl.BlockSpec(memory_space=pltpu.SMEM)
+ANY = pl.BlockSpec(memory_space=pl.ANY)
 
 
 def params(mib):
@@ -78,7 +79,8 @@
     return np.concatenate([cosine, cosine], axis=1), np.concatenate([sine, sine], axis=1)
 
 
-def pick_kernel(count, scal, block, out, rows):
+def pick_kernel(count, joined, scal, block, *refs):
+    outs, rows = refs[:-1], refs[-1]
     inputs, samples = block.shape[1], block.shape[2]
     step = 16
     for part in range(2):
@@ -94,169 +96,176 @@
         lax.fori_loop(0, samples // LANES // step, spread, 0)
     first = scal[0]
     tall = 128
-    for part in range(2):
-        for item in range(count):
-
-            def gather(n, carry, part=part, item=item):
-                low = pl.multiple_of(n * tall, tall)
+    for item in range(count):
+        out = outs[0].at[item] if joined else outs[item]
+
+        def gather(n, carry, item=item, out=out):
+            low = pl.multiple_of(n * tall, tall)
+            for part in range(2):
                 value = rows[part, pl.ds(low * inputs + first + item, tall, stride=inputs), :]
-                out[item, part, pl.ds(low, tall), :] = value.astype(jnp.bfloat16)
-                return carry
-
-            lax.fori_loop(0, samples // LANES // tall, gather, 0)
-
-
-def pick(block, first, count):
+                out[part, pl.ds(low, tall), :] = value.astype(jnp.bfloat16)
+            return carry
+
+        lax.fori_loop(0, samples // LANES // tall, gather, 0)
+
+
+def pick(block, first, count, joined):
     _, inputs, samples = block.shape
+    one = (2, samples // LANES, LANES)
+    shapes = [(count,) + one] if joined else [one] * count
     return pl.pallas_call(
-        functools.partial(pick_kernel, count),
-        out_shape=jax.ShapeDtypeStruct((count, 2, samples // LANES, LANES), jnp.bfloat16),
+        functools.partial(pick_kernel, count, joined),
+        out_shape=[jax.ShapeDtypeStruct(s, jnp.bfloat16) for s in shapes],
         in_specs=[SMEM, VMEM],
-        out_specs=VMEM,
+        out_specs=[VMEM] * len(shapes),
         scratch_shapes=[pltpu.VMEM((2, samples // LANES * inputs, LANES), jnp.float32)],
-        compiler_params=params(24),
-        cost_estimate=cost(10**6, 8 * 2**20),
+        compiler_params=params(16),
+        cost_estimate=cost(10**6, 4 * 2**20),
         name="pick",
     )(first, block)
 
 
-FRONT = 40
-GROUP = 8
-
-
-def filterbank_kernel(count, frames, dests, *refs):
-    scal, keep, recv, halo_far, halo_own, coef, first, tw_cos, tw_sin, last = refs[:10]
-    outs = refs[10 : 10 + dests]
-    samples, shifted, grouped = refs[10 + dests :]
+HALF = 16
+SOME = 4
+
+
+def filterbank_kernel(index, before, frames, dests, *refs):
+    scal, keep, halo_own, recv, halo_far, coef, first, tw_cos, tw_sin, last = refs[:10]
+    earlier = refs[10 : 10 + dests * (before > 0)]
+    refs = refs[10 + len(earlier) :]
+    outs = refs[:dests]
+    raw, weights, grouped, sems = refs[dests : dests + 4]
+    filtered = refs[dests + 4 :]
     block_rows = frames * ROWS
     total = PAIR * frames
-    me = scal[count]
+    delay, me = scal[0], scal[1]
+    down = delay // LANES
+    across = delay % LANES
     lane = lax.broadcasted_iota(jnp.int32, (1, LANES), 1)
+    inside = lane < LANES - across
+    turned_in = lane >= across
     high = lane < RADIX
-    tall = 128
-
-    def unpack(source, place, item):
-        def step(n, carry):
-            low = pl.multiple_of(n * tall, tall)
+
+    def bring(source, place, sem):
+        at = pl.multiple_of(place * block_rows, block_rows)
+        return pltpu.make_async_copy(source, raw.at[:, pl.ds(at, block_rows), :], sems.at[sem])
+
+    @pl.when(me == 0)
+    def _():
+        bring(halo_far, 0, 0).start()
+
+    @pl.when(me != 0)
+    def _():
+        bring(halo_own.at[index], 0, 0).start()
+
+    bring(keep.at[index], 1 + me, 1).start()
+    bring(recv, 2 - me, 2).start()
+
+    back = lax.rem(LANES - across, LANES)
+    for tap in range(TAPS):
+        here = coef[tap, pl.ds(down, ROWS), :]
+        after = coef[tap, pl.ds(down + 1, ROWS), :]
+        weights[tap] = pltpu.roll(jnp.where(turned_in, here, after), back, 1)
+    for dest, old in zip(outs, earlier):
+        dest[:before] = old[...]
+
+    bring(halo_far, 0, 0).wait()
+    bring(keep.at[index], 1 + me, 1).wait()
+    bring(recv, 2 - me, 2).wait()
+
+    def filt(half):
+        for low, high_frame in ((0, 9), (9, HALF + 1)):
+            size = high_frame - low
+            for band in range(ROWS // 16):
+                for part in range(2):
+                    values = []
+                    for u in range(size + TAPS - 1):
+                        at = (half * HALF + low + u + frames - TAPS) * ROWS + band * 16
+                        values.append(raw[part, at : at + 16, :].astype(jnp.float32))
+                    sums = [None] * size
+                    for tap in range(TAPS):
+                        weight = weights[tap, band * 16 : band * 16 + 16, :]
+                        for u in range(size):
+                            term = weight * values[u + TAPS - 1 - tap]
+                            sums[u] = term if sums[u] is None else sums[u] + term
+                    for u in range(size):
+                        at = (low + u) * ROWS + band * 16
+                        filtered[half][part, at : at + 16, :] = sums[u]
+
+    twice = lax.rem(across + RADIX, LANES)
+
+    def place(half, u):
+        for band in range(ROWS // 16):
+            at = (u + 1) * ROWS + band * 16 - down
+            moved, turned = [], []
             for part in range(2):
-                at = pl.multiple_of(FRONT + place * block_rows + low, 8)
-                value = source[item, part, pl.ds(low, tall), :]
-                samples[part, pl.ds(at, tall), :] = value.astype(jnp.float32)
-            return carry
-
-        lax.fori_loop(0, block_rows // tall, step, 0)
-
-    def filt(m):
-        for band in range(ROWS // 16):
-            sums = [[None] * GROUP for _ in range(2)]
+                here = filtered[half][part, pl.ds(at, 16), :]
+                above = filtered[half][part, pl.ds(at - 1, 16), :]
+                value = jnp.where(inside, here, above)
+                moved.append(pltpu.roll(value, across, 1))
+                turned.append(pltpu.roll(value, twice, 1))
+            parts = (
+                jnp.where(high, moved[0], turned[1]),
+                jnp.where(high, turned[0], moved[1]),
+                jnp.where(high, moved[1], -turned[0]),
+                jnp.where(high, turned[1], -moved[0]),
+            )
+            for which, value in enumerate(parts):
+                low = which * ROWS + band * 16
+                grouped[half * HALF + u, low : low + 16, :] = value.astype(jnp.bfloat16)
+
+    def turn(base):
+        wide = jnp.concatenate([grouped[base + u] for u in range(SOME)], axis=1)
+        inner = jnp.dot(first[...], wide, preferred_element_type=jnp.float32)
+        rows = []
+        for u in range(SOME):
+            cut = slice(u * LANES, (u + 1) * LANES)
+            value = inner[:RADIX, cut] * tw_cos[...] + inner[RADIX:, cut] * tw_sin[...]
+            rows.append(value.astype(jnp.bfloat16))
+        inner = jnp.concatenate(rows, axis=0)
+        result = lax.dot_general(
+            last[...], inner, (((1,), (1,)), ((), ())), preferred_element_type=jnp.float32
+        ).astype(jnp.bfloat16)
+        size = result.shape[0] // (2 * dests)
+        for dest in range(dests):
             for part in range(2):
-                values = []
-                for u in range(GROUP + TAPS - 1):
-                    at = (m * GROUP + frames - TAPS + 1 + u) * ROWS + band * 16
-                    values.append(shifted[part, at : at + 16, :])
-                for tap in range(TAPS):
-                    weight = coef[tap, band * 16 : band * 16 + 16, :]
-                    for u in range(GROUP):
-                        term = weight * values[u + TAPS - 1 - tap]
-                        old = sums[part][u]
-                        sums[part][u] = term if old is None else old + term
-            for u in range(GROUP):
-                real, imag = sums[0][u], sums[1][u]
-                real_turned = pltpu.roll(real, RADIX, 1)
-                imag_turned = pltpu.roll(imag, RADIX, 1)
-                parts = (
-                    jnp.where(high, real, imag_turned),
-                    jnp.where(high, real_turned, imag),
-                    jnp.where(high, imag, -real_turned),
-                    jnp.where(high, imag_turned, -real),
-                )
-                for index, value in enumerate(parts):
-                    low = index * ROWS + band * 16
-                    grouped[m % 2, u, low : low + 16, :] = value.astype(jnp.bfloat16)
-
-    def turn(m, item):
-        some = 4
-        for piece in range(GROUP // some):
-            base = piece * some
-            wide = jnp.concatenate([grouped[m % 2, base + u] for u in range(some)], axis=1)
-            inner = jnp.dot(first[...], wide, preferred_element_type=jnp.float32)
-            rows = []
-            for u in range(some):
-                cut = slice(u * LANES, (u + 1) * LANES)
-                turned = inner[:RADIX, cut] * tw_cos[...] + inner[RADIX:, cut] * tw_sin[...]
-                rows.append(turned.astype(jnp.bfloat16))
-            inner = jnp.concatenate(rows, axis=0)
-            result = lax.dot_general(
-                last[...], inner, (((1,), (1,)), ((), ())), preferred_element_type=jnp.float32
-            ).astype(jnp.bfloat16)
-            size = result.shape[0] // (2 * dests)
-            for dest in range(dests):
-                for part in range(2):
-                    low = (dest * 2 + part) * size
-                    for u in range(some // 2):
-                        at = (m * GROUP + base) // 2 + u
-                        outs[dest][item, at, part] = result[
-                            low : low + size, u * LANES : (u + 1) * LANES
-                        ]
-
-    def one(item, carry):
-        @pl.when(me == 0)
-        def _():
-            unpack(halo_far, 0, item)
-
-        @pl.when(me != 0)
-        def _():
-            unpack(halo_own, 0, item)
-
-        unpack(keep, 1 + me, item)
-        unpack(recv, 2 - me, item)
-        delay = scal[item]
-        down = delay // LANES
-        across = delay % LANES
-        inside = lane < LANES - across
-
-        def shift(n, carry):
-            low = pl.multiple_of(n * GROUP * ROWS, GROUP * ROWS)
-            for part in range(2):
-                at = FRONT + low - down
-                here = samples[part, pl.ds(at, GROUP * ROWS), :]
-                before = samples[part, pl.ds(at - 1, GROUP * ROWS), :]
-                moved = pltpu.roll(jnp.where(inside, here, before), across, 1)
-                shifted[part, pl.ds(low, GROUP * ROWS), :] = moved
-            return carry
-
-        lax.fori_loop(0, (PAIR + 1) * frames // GROUP, shift, 0)
-        steps = total // GROUP
-        for m in range(steps + 1):
-            if m < steps:
-                filt(m)
-            if m:
-                turn(m - 1, item)
-        return carry
-
-    lax.fori_loop(0, count, one, 0)
-
-
-def filterbank(scal, keep, recv, halo_far, halo_own, tables, last, dests):
-    count = keep.shape[0]
+                low = (dest * 2 + part) * size
+                for u in range(SOME // 2):
+                    outs[dest][before, base // 2 + u, part] = result[
+                        low : low + size, u * LANES : (u + 1) * LANES
+                    ]
+
+    for half in range(total // HALF):
+        filt(half)
+    for half in range(total // HALF):
+        for base in range(0, HALF, SOME):
+            for u in range(SOME):
+                place(half, base + u)
+            turn(half * HALF + base)
+
+
+def filterbank(index, scal, keep, halo_own, recv, halo_far, tables, last, earlier, dests):
     frames = keep.shape[2] // ROWS
     size = last.shape[0] // (2 * dests)
+    before = earlier[0].shape[0] if earlier else 0
     all_rows = (PAIR + 1) * frames * ROWS
-    shape = jax.ShapeDtypeStruct((count, PAIR * frames // 2, 2, size, LANES), jnp.bfloat16)
+    shape = (before + 1, PAIR * frames // 2, 2, size, LANES)
     return pl.pallas_call(
-        functools.partial(filterbank_kernel, count, frames, dests),
-        out_shape=[shape] * dests,
-        in_specs=[SMEM] + [VMEM] * 9,
+        functools.partial(filterbank_kernel, index, before, frames, dests),
+        out_shape=[jax.ShapeDtypeStruct(shape, jnp.bfloat16)] * dests,
+        in_specs=[SMEM] + [ANY] * 4 + [VMEM] * (5 + len(earlier)),
         out_specs=[VMEM] * dests,
         scratch_shapes=[
-            pltpu.VMEM((2, FRONT + all_rows, LANES), jnp.float32),
-            pltpu.VMEM((2, all_rows, LANES), jnp.float32),
-            pltpu.VMEM((2, GROUP, LANES, LANES), jnp.bfloat16),
-        ],
-        compiler_params=params(40),
-        cost_estimate=cost(2 * 10**9, 32 * 2**20),
+            pltpu.VMEM((2, all_rows, LANES), jnp.bfloat16),
+            pltpu.VMEM((TAPS, ROWS, LANES), jnp.float32),
+            pltpu.VMEM((PAIR * frames, LANES, LANES), jnp.bfloat16),
+            pltpu.SemaphoreType.DMA((3,)),
+        ]
+        + [pltpu.VMEM((2, (HALF + 1) * ROWS, LANES), jnp.float32)] * (PAIR * frames // HALF),
+        compiler_params=params(16),
+        cost_estimate=cost(10**9, 10 * 2**20),
         name="filterbank",
-    )(scal, keep, recv, halo_far, halo_own, *tables, last)
+    )(scal, keep, halo_own, recv, halo_far, *tables, last, *earlier)
 
 
 def pair_blocks(own):
@@ -270,8 +279,7 @@
     arrays, blocks, outer, span = layout
     sources, (place, starts, where_outer) = refs[:arrays], refs[arrays : arrays + 3]
     rest = refs[arrays + 3 :]
-    outs, (spectra, sums) = rest[:-2], rest[-2:]
-    halves = outer * span // 8
+    outs, (spectra, sums, held) = rest[:-3], rest[-3:]
     steps = spectra.shape[1]
     some = 8
 
@@ -290,34 +298,41 @@
 
     high = lax.broadcasted_iota(jnp.int32, (1, LANES), 1) < RADIX
     rows_outer = blocks * TILE * TILE * span
+    size = outer * span
+    unroll = 4
 
     def block(t, carry):
         left, right = starts[2 * t], starts[2 * t + 1]
-        for half in range(halves):
-            cut = slice(half * 8, half * 8 + 8)
-            products = []
-            for one, two in ((2, 0), (0, 2), (1, 3)):
-                acc = [None] * (TILE * TILE)
-                for n in range(steps):
-                    a = [spectra[left + p, n, one, cut, :] for p in range(TILE)]
-                    b = [spectra[right + q, n, two, cut, :] for q in range(TILE)]
+
+        def over(one, two, acc, sign):
+            def frame(n, acc):
+                acc = list(acc)
+                for u in range(unroll):
+                    a = [spectra[left + p, n * unroll + u, one] for p in range(TILE)]
+                    b = [spectra[right + q, n * unroll + u, two] for q in range(TILE)]
                     for p in range(TILE):
                         for q in range(TILE):
+                            at = p * TILE + q
                             term = a[p] * b[q]
-                            at = p * TILE + q
-                            acc[at] = term if acc[at] is None else acc[at] + term
-                products.append(acc)
-            for p in range(TILE * TILE):
-                first, second, third = (acc[p] for acc in products)
-                real = first + third
-                imag = first - second
-                real = real + pltpu.roll(real, RADIX, 1)
-                imag = imag + pltpu.roll(imag, RADIX, 1)
-                both = jnp.where(high, real, imag)
-                for u in range(8 // span):
-                    o = half * (8 // span) + u
-                    at = o * rows_outer + (t * TILE * TILE + p) * span
-                    sums[pl.ds(pl.multiple_of(at, span), span), :] = both[u * span : (u + 1) * span]
+                            acc[at] = acc[at] + term if sign > 0 else acc[at] - term
+                return tuple(acc)
+
+            return lax.fori_loop(0, steps // unroll, frame, tuple(acc))
+
+        zero = jnp.zeros((size, LANES), jnp.float32)
+        first = over(2, 0, [zero] * (TILE * TILE), 1)
+        for p in range(TILE * TILE):
+            held[0, p] = first[p]
+        real = over(1, 3, first, 1)
+        for p in range(TILE * TILE):
+            held[1, p] = real[p] + pltpu.roll(real[p], RADIX, 1)
+        imag = over(0, 2, [held[0, p] for p in range(TILE * TILE)], -1)
+        for p in range(TILE * TILE):
+            folded = imag[p] + pltpu.roll(imag[p], RADIX, 1)
+            both = jnp.where(high, held[1, p], folded)
+            for o in range(outer):
+                at = o * rows_outer + (t * TILE * TILE + p) * span
+                sums[pl.ds(pl.multiple_of(at, span), span), :] = both[o * span : (o + 1) * span]
         return carry
 
     lax.fori_loop(0, blocks, block, 0)
@@ -343,9 +358,10 @@
         scratch_shapes=[
             pltpu.VMEM((inputs, steps, 4, size, LANES), jnp.float32),
             pltpu.VMEM((outer * rows, LANES), jnp.float32),
+            pltpu.VMEM((2, TILE * TILE, outer * span, LANES), jnp.float32),
         ],
-        compiler_params=params(40),
-        cost_estimate=cost(10**9, 20 * 2**20),
+        compiler_params=params(14 + inputs * steps * 4 * size * LANES * 4 // 2**20),
+        cost_estimate=cost(10**9, 22 * 2**20),
         name=name,
     )(*arrays, place, starts, where_outer)
 
@@ -429,13 +445,13 @@
 def fast_fits(in_count, frame_count):
     stn, tm, per_ct = (lax.axis_size(a) for a in ("stn", "tm", "ct"))
     groups = tm * per_ct
-    if stn != 2 or tm % PAIR or in_count % (PAIR * CHUNKS) or RADIX % groups:
+    if stn != 2 or tm % PAIR or in_count % (PAIR * JOIN) or RADIX % groups:
         return False
     outer, span = tm // PAIR, RADIX // groups
     own = in_count * per_ct
     return (
         frame_count >= TAPS
-        and frame_count % GROUP == 0
+        and frame_count % HALF == 0
         and span in (2, 4, 8)
         and outer * span % 16 == 0
         and own % (2 * TILE) == 0
@@ -450,7 +466,6 @@
     span = RADIX // (tm * per_ct)
     own = in_count * per_ct
     half = in_count // PAIR
-    part = half // CHUNKS
     place_tm, place_ct = lax.axis_index("tm"), lax.axis_index("ct")
     core = lax.axis_index("stn")
     g, o = place_tm % PAIR, place_tm // PAIR
@@ -467,24 +482,25 @@
     base = jnp.where(g == 0, base, base[::-1])
     base = lax.dynamic_slice_in_dim(jnp.concatenate([base, base], axis=1), place_ct, per_ct, 1)
     last = base.reshape(-1, 2 * RADIX)
-    tables = [jnp.asarray(filter_table()), jnp.asarray(first_table())]
+    twice = np.concatenate([filter_table()] * 2, axis=1)
+    tables = [jnp.asarray(twice), jnp.asarray(first_table())]
     tables += [jnp.asarray(t) for t in twiddle_tables()]
 
-    sends = [pick(voltages, stacked([(1 - g) * half + c * part]), part) for c in range(CHUNKS)]
-    keeps = [pick(voltages, stacked([g * half + c * part]), part) for c in range(CHUNKS)]
-    recvs, fars, owns = [], [], []
-    for c in range(CHUNKS):
-        recvs.append(lax.ppermute(sends[c], "tm", swap))
-        owns.append(lax.ppermute(keeps[c], "tm", [p for p in onward if p[0] % PAIR == 1]))
-        fars.append(lax.ppermute(recvs[c], "tm", [p for p in onward if p[0] % PAIR == 0]))
+    sends = pick(voltages, stacked([(1 - g) * half]), half, False)
+    keep = pick(voltages, stacked([g * half]), half, True)[0]
+    recvs = [lax.ppermute(block, "tm", swap) for block in sends]
+    halo_own = lax.ppermute(keep, "tm", [p for p in onward if p[0] % PAIR == 1])
+    fars = [lax.ppermute(block, "tm", [p for p in onward if p[0] % PAIR == 0]) for block in recvs]
 
     arrays, others, place = [], [], []
-    for c in range(CHUNKS):
-        offsets = lax.dynamic_slice_in_dim(delays, g * half + c * part, part, 0)
-        scal = jnp.concatenate([offsets, g.astype(jnp.int32)[None]])
+    spectra = []
+    for c in range(half):
+        scal = stacked([lax.dynamic_index_in_dim(delays, g * half + c, 0, False), g])
         spectra = filterbank(
-            scal, keeps[c], recvs[c], fars[c], owns[c], tables, last, len(dests)
+            c, scal, keep, halo_own, recvs[c], fars[c], tables, last, spectra, len(dests)
         )
+        if c % JOIN < JOIN - 1:
+            continue
         for (dg, dc), block in zip(dests, spectra):
             route = []
             for i in range(tm):
@@ -495,7 +511,9 @@
                 block = lax.ppermute(block, ("tm", "ct"), route)
             arrays.append(block)
             others.append(lax.ppermute(block, "stn", cores))
-            place.append(((place_ct - dc) % per_ct) * in_count + (g ^ dg) * half + c * part)
+            start = ((place_ct - dc) % per_ct) * in_count + (g ^ dg) * half
+            place.append(start + c - JOIN + 1)
+        spectra = []
 
     inside, across = pair_blocks(own)
     starts = stacked([TILE * s for block in inside for s in block])

time: 118 us -> 127 us (1.076)
  waiting for transfers between devices: 34.5 us -> 41.4 us
  Pallas kernels: 45.7 us -> 40.2 us
  starting transfers between devices: 30.6 us -> 35.1 us
  other arithmetic: 0.94 us -> 3.65 us
    ppermute x6 -> x9, starting transfers between devices: 12.9 us -> 19.6 us  [the longest x4 10.1 us: fast(): lax.ppermute(block, 'tm', [p for p in onward if p[0] % PAIR == 0])]
    ppermute x6 -> x9, waiting for transfers between devices: 12.8 us -> 19.3 us  [the longest x4 19.3 us: fast(): recvs = [lax.ppermute(block, 'tm', swap) for block in sends]]
    ppermute x3, waiting for transfers between devices: 2.05 us -> 6.62 us  [fast(): mine_in[r] = lax.ppermute(mine_in[r], 'tm', route)]
    ppermute x3, waiting for transfers between devices: 8.15 us -> 3.87 us  [fast(): mine_across[r] = lax.ppermute(mine_across[r], 'tm', route)]
    ppermute x3, starting transfers between devices: 5.07 us -> 1.44 us  [fast(): mine_in[r] = lax.ppermute(mine_in[r], 'tm', route)]
    another operation x0 -> x4, other arithmetic: none -> 2.86 us  [stacked(): return jnp.stack([jnp.asarray(v, jnp.int32) for v in values])]
    pallas_call x2, Pallas kernels: 21 us -> 18.2 us  [correlate(): pl.pallas_call(functools.partial(correlate_kernel, layout), out_shape=sha...]
    pallas_call x6, Pallas kernels: 20.6 us -> 18.8 us  [the longest x4 15.6 us: filterbank(): pl.pallas_call(functools.partial(filterbank_kernel, index, before, frames...]
  transfers between devices with their start and end apart: 30 -> 33, of which waited for: 8 -> 8; matrix products, arithmetic and copies ran while one was open for 1% -> 4% of each run, Pallas kernels for 34% -> 29%
where the time goes in v3:
time: 127 us; the launch traced here: 126 us
  waiting for transfers between devices  41.4 us (33%)
  Pallas kernels  40.2 us (32%)
  starting transfers between devices  35.1 us (28%)
  local copies, waits for them, and re-layouts  4.96 us (4%)
  other arithmetic  3.65 us (3%)
    ppermute x4, waiting for transfers between devices, fast(): recvs = [lax.ppermute(block, 'tm', swap) for block in sends]  19.3 us
    pallas_call x2, Pallas kernels, correlate(): pl.pallas_call(functools.partial(correlate_kernel, layout), out_shape=sha...  18.2 us
    pallas_call x4, Pallas kernels, filterbank(): pl.pallas_call(functools.partial(filterbank_kernel, index, before, frames...  15.6 us
    ppermute x6, waiting for transfers between devices, fast(): block = lax.ppermute(block, ('tm', 'ct'), route)  11.5 us
    ppermute x4, starting transfers between devices, fast(): lax.ppermute(block, 'tm', [p for p in onward if p[0] % PAIR == 0])  10.1 us
    ppermute x4, starting transfers between devices, fast(): recvs = [lax.ppermute(block, 'tm', swap) for block in sends]  7.83 us
    ppermute x6, starting transfers between devices, fast(): block = lax.ppermute(block, ('tm', 'ct'), route)  7.11 us
    ppermute x3, waiting for transfers between devices, fast(): mine_in[r] = lax.ppermute(mine_in[r], 'tm', route)  6.62 us
  transfers between devices with their start and end apart: 33, of which 8 were waited for; matrix products, arithmetic and copies ran while one was open for 4% of the time, Pallas kernels for 29%

profile of v3, /device:TPU:0, one launch (start us, length us, event | category | flops | bytes accessed | tf_op | source)
XLA Modules:
  0.0 125.6 jit_solution(11508020200307400776)
XLA Ops:
  0.0 1.6 %copy-done = bf16[2,8,65536]{2,1,0:T(8,128)(2,1)S(1)} copy-done((bf16[2,8,65536]{2,1,0:T(8,128)(2,1)S(1)}, bf16[2,8,65536]{2,1,0:T(8,128)(2,1)}, u32[]{:S(2)}) %copy-start) | copy-done | bytes 2097176
  1.6 1.2 pick.2.refs_1_
  2.8 1.7 %collective-permute-start = (bf16[4,2,512,128]{3,2,1,0:T(8,128)(2,1)S(1)}, bf16[4,2,512,128]{3,2,1,0:T(8,128)(2,1)}, u32[]{:S(2)}, u32[]{:S(2)}) collective-permute-start(bf16[4,2,512,128]{3,2,1,0:T(8,128)(2,1)S(1)} %pick.2.refs_1_), channel_id=1, source_target_pairs={{2,6},{6,10},{10,14},{3,7},{7,11},{11,15},{18,22},{22,26},{26,30},... | collective-permute-start | bytes 3145736 | tf_op jit(solution)/shard_map/ppermute | solution.py:492
  4.5 2.0 %pick.3 = (bf16[2,512,128]{2,1,0:T(8,128)(2,1)}, bf16[2,512,128]{2,1,0:T(8,128)(2,1)S(1)}, bf16[2,512,128]{2,1,0:T(8,128)(2,1)}, bf16[2,512,128]{2,1,0:T(8,128)(2,1)}) custom-call(s32[1]{0:T(128)} %bitcast.3.scal, bf16[2,8,65536]{2,1,0:T(8,128)(2,1)S(1)} %copy-done.1), custom_call_target="tpu_custom_call" | custom-call | flops 1000000 | bytes 4194304 | tf_op jit(solution)/shard_map/pick/pallas_call | solution.py:116
  6.5 5.8 %collective-permute-start.1 = (bf16[2,512,128]{2,1,0:T(8,128)(2,1)S(1)}, bf16[2,512,128]{2,1,0:T(8,128)(2,1)S(1)}, u32[]{:S(2)}, u32[]{:S(2)}) collective-permute-start(bf16[2,512,128]{2,1,0:T(8,128)(2,1)S(1)} %get-tuple-element.33), channel_id=1, source_target_pairs={{0,2},{2,0},{4,6},{6,4},{8,10},{10,8},{12,14},{14,12},{1,3},{3,1},... | collective-permute-start | bytes 786440 | tf_op jit(solution)/shard_map/ppermute | solution.py:491
  12.3 2.0 %collective-permute-start.8 = (bf16[2,512,128]{2,1,0:T(8,128)(2,1)}, bf16[2,512,128]{2,1,0:T(8,128)(2,1)S(1)}, u32[]{:S(2)}, u32[]{:S(2)}) collective-permute-start(bf16[2,512,128]{2,1,0:T(8,128)(2,1)} %get-tuple-element.43), channel_id=1, source_target_pairs={{0,2},{2,0},{4,6},{6,4},{8,10},{10,8},{12,14},{14,12},{1,3},{3,1},... | collective-permute-start | bytes 786440 | tf_op jit(solution)/shard_map/ppermute | solution.py:491
  14.3 0.8 broadcast_select_fusion
  15.1 0.7 fusion.1
  15.8 19.3 %collective-permute-done.10.refs_3_ = bf16[2,512,128]{2,1,0:T(8,128)(2,1)S(1)} collective-permute-done((bf16[2,512,128]{2,1,0:T(8,128)(2,1)}, bf16[2,512,128]{2,1,0:T(8,128)(2,1)S(1)}, u32[]{:S(2)}, u32[]{:S(2)}) %collective-permute-start.10) | collective-permute-done | bytes 262176 | tf_op jit(solution)/shard_map/ppermute | solution.py:491
  35.1 2.5 %collective-permute-start.11 = (bf16[2,512,128]{2,1,0:T(8,128)(2,1)S(1)}, bf16[2,512,128]{2,1,0:T(8,128)(2,1)S(1)}, u32[]{:S(2)}, u32[]{:S(2)}) collective-permute-start(bf16[2,512,128]{2,1,0:T(8,128)(2,1)S(1)} %collective-permute-done.10.refs_3_), channel_id=1, source_target_pairs={{0,4},{4,8},{8,12},{1,5},{5,9},{9,13},{16,20},{20,24},{24,28},{17,... | collective-permute-start | bytes 786440 | tf_op jit(solution)/shard_map/ppermute | solution.py:493
  37.6 0.7 pad_add_fusion.3.refs_0_
  38.4 3.5 %collective-permute-start.9 = (bf16[2,512,128]{2,1,0:T(8,128)(2,1)S(1)}, bf16[2,512,128]{2,1,0:T(8,128)(2,1)S(1)}, u32[]{:S(2)}, u32[]{:S(2)}) collective-permute-start(bf16[2,512,128]{2,1,0:T(8,128)(2,1)S(1)} %collective-permute-done.8.refs_3_), channel_id=1, source_target_pairs={{0,4},{4,8},{8,12},{1,5},{5,9},{9,13},{16,20},{20,24},{24,28},{17,... | collective-permute-start | bytes 786440 | tf_op jit(solution)/shard_map/ppermute | solution.py:493
  41.8 0.7 pad_add_fusion.1.refs_0_
  42.5 2.2 %collective-permute-start.4 = (bf16[2,512,128]{2,1,0:T(8,128)(2,1)S(1)}, bf16[2,512,128]{2,1,0:T(8,128)(2,1)S(1)}, u32[]{:S(2)}, u32[]{:S(2)}) collective-permute-start(bf16[2,512,128]{2,1,0:T(8,128)(2,1)S(1)} %collective-permute-done.3.refs_3_), channel_id=1, source_target_pairs={{0,4},{4,8},{8,12},{1,5},{5,9},{9,13},{16,20},{20,24},{24,28},{17,... | collective-permute-start | bytes 786440 | tf_op jit(solution)/shard_map/ppermute | solution.py:493
  44.7 0.8 pad_add_fusion.2.refs_0_
  45.5 1.9 %collective-permute-start.2 = (bf16[2,512,128]{2,1,0:T(8,128)(2,1)S(1)}, bf16[2,512,128]{2,1,0:T(8,128)(2,1)S(1)}, u32[]{:S(2)}, u32[]{:S(2)}) collective-permute-start(bf16[2,512,128]{2,1,0:T(8,128)(2,1)S(1)} %collective-permute-done.1.refs_3_), channel_id=1, source_target_pairs={{0,4},{4,8},{8,12},{1,5},{5,9},{9,13},{16,20},{20,24},{24,28},{17,... | collective-permute-start | bytes 786440 | tf_op jit(solution)/shard_map/ppermute | solution.py:493
  47.4 1.0 copy-done.2
  48.5 3.8 %filterbank.6 = (bf16[1,16,2,16,128]{4,3,2,1,0:T(8,128)(2,1)S(1)}, bf16[1,16,2,16,128]{4,3,2,1,0:T(8,128)(2,1)S(1)}, bf16[1,16,2,16,128]{4,3,2,1,0:T(8,128)(2,1)S(1)}, bf16[1,16,2,16,128]{4,3,2,1,0:T(8,128)(2,1)S(1)}) custom-call(s32[2]{0:T(128)S(1)} %pad_add_fusion.3.refs_0_, bf16[4,2,512,128]{3,2,1,0:T(8,128)(2,1)S(1)} %pick.2.refs_1_, ...), custom_call_target="tpu_custom_call" | custom-call | flops 1000000000 | bytes 10485760 | tf_op jit(solution)/shard_map/filterbank/pallas_call | solution.py:253
  52.4 3.9 %filterbank.7 = (bf16[2,16,2,16,128]{4,3,2,1,0:T(8,128)(2,1)S(1)}, bf16[2,16,2,16,128]{4,3,2,1,0:T(8,128)(2,1)S(1)}, bf16[2,16,2,16,128]{4,3,2,1,0:T(8,128)(2,1)S(1)}, bf16[2,16,2,16,128]{4,3,2,1,0:T(8,128)(2,1)S(1)}) custom-call(s32[2]{0:T(128)S(1)} %pad_add_fusion.2.refs_0_, bf16[4,2,512,128]{3,2,1,0:T(8,128)(2,1)S(1)} %pick.2.refs_1_, ...), custom_call_target="tpu_custom_call" | custom-call | flops 1000000000 | bytes 10485760 | tf_op jit(solution)/shard_map/filterbank/pallas_call | solution.py:253
  56.2 1.6 %collective-permute-start.12 = (bf16[2,16,2,16,128]{4,3,2,1,0:T(8,128)(2,1)S(1)}, bf16[2,16,2,16,128]{4,3,2,1,0:T(8,128)(2,1)S(1)}, u32[]{:S(2)}, u32[]{:S(2)}) collective-permute-start(bf16[2,16,2,16,128]{4,3,2,1,0:T(8,128)(2,1)S(1)} %get-tuple-element.50), channel_id=1, source_target_pairs={{0,1},{1,0},{2,3},{3,2},{4,5},{5,4},{6,7},{7,6},{8,9},{9,8},{10,11... | collective-permute-start | bytes 786440 | tf_op jit(solution)/shard_map/ppermute | solution.py:511
  57.8 2.0 %collective-permute-start.14 = (bf16[2,16,2,16,128]{4,3,2,1,0:T(8,128)(2,1)S(1)}, bf16[2,16,2,16,128]{4,3,2,1,0:T(8,128)(2,1)S(1)}, u32[]{:S(2)}, u32[]{:S(2)}) collective-permute-start(bf16[2,16,2,16,128]{4,3,2,1,0:T(8,128)(2,1)S(1)} %get-tuple-element.52), channel_id=1, source_target_pairs={{0,3},{1,2},{2,1},{3,0},{4,7},{5,6},{6,5},{7,4},{8,11},{9,10},{10,... | collective-permute-start | bytes 786440 | tf_op jit(solution)/shard_map/ppermute | solution.py:511
  59.8 0.7 pad_add_fusion.refs_0_
  60.5 3.8 %filterbank.4 = (bf16[1,16,2,16,128]{4,3,2,1,0:T(8,128)(2,1)S(1)}, bf16[1,16,2,16,128]{4,3,2,1,0:T(8,128)(2,1)S(1)}, bf16[1,16,2,16,128]{4,3,2,1,0:T(8,128)(2,1)S(1)}, bf16[1,16,2,16,128]{4,3,2,1,0:T(8,128)(2,1)S(1)}) custom-call(s32[2]{0:T(128)S(1)} %pad_add_fusion.1.refs_0_, bf16[4,2,512,128]{3,2,1,0:T(8,128)(2,1)S(1)} %pick.2.refs_1_, ...), custom_call_target="tpu_custom_call" | custom-call | flops 1000000000 | bytes 10485760 | tf_op jit(solution)/shard_map/filterbank/pallas_call | solution.py:253
  64.4 4.0 %filterbank.5 = (bf16[2,16,2,16,128]{4,3,2,1,0:T(8,128)(2,1)S(1)}, bf16[2,16,2,16,128]{4,3,2,1,0:T(8,128)(2,1)S(1)}, bf16[2,16,2,16,128]{4,3,2,1,0:T(8,128)(2,1)S(1)}, bf16[2,16,2,16,128]{4,3,2,1,0:T(8,128)(2,1)S(1)}) custom-call(s32[2]{0:T(128)S(1)} %pad_add_fusion.refs_0_, bf16[4,2,512,128]{3,2,1,0:T(8,128)(2,1)S(1)} %pick.2.refs_1_, ...), custom_call_target="tpu_custom_call" | custom-call | flops 1000000000 | bytes 10485760 | tf_op jit(solution)/shard_map/filterbank/pallas_call | solution.py:253
  68.4 1.6 %collective-permute-start.5 = (bf16[2,16,2,16,128]{4,3,2,1,0:T(8,128)(2,1)S(1)}, bf16[2,16,2,16,128]{4,3,2,1,0:T(8,128)(2,1)S(1)}, u32[]{:S(2)}, u32[]{:S(2)}) collective-permute-start(bf16[2,16,2,16,128]{4,3,2,1,0:T(8,128)(2,1)S(1)} %get-tuple-element.40), channel_id=1, source_target_pairs={{0,1},{1,0},{2,3},{3,2},{4,5},{5,4},{6,7},{7,6},{8,9},{9,8},{10,11... | collective-permute-start | bytes 786440 | tf_op jit(solution)/shard_map/ppermute | solution.py:511
  70.0 1.5 %collective-permute-start.6 = (bf16[2,16,2,16,128]{4,3,2,1,0:T(8,128)(2,1)S(1)}, bf16[2,16,2,16,128]{4,3,2,1,0:T(8,128)(2,1)S(1)}, u32[]{:S(2)}, u32[]{:S(2)}) collective-permute-start(bf16[2,16,2,16,128]{4,3,2,1,0:T(8,128)(2,1)S(1)} %get-tuple-element.41), channel_id=1, source_target_pairs={{0,2},{1,3},{2,0},{3,1},{4,6},{5,7},{6,4},{7,5},{8,10},{9,11},{10,... | collective-permute-start | bytes 786440 | tf_op jit(solution)/shard_map/ppermute | solution.py:511
  71.5 0.5 collective-permute-start.7
  72.0 0.5 collective-permute-start.23
  72.5 4.7 %collective-permute-done.5.refs_1_ = bf16[2,16,2,16,128]{4,3,2,1,0:T(8,128)(2,1)S(1)} collective-permute-done((bf16[2,16,2,16,128]{4,3,2,1,0:T(8,128)(2,1)S(1)}, bf16[2,16,2,16,128]{4,3,2,1,0:T(8,128)(2,1)S(1)}, u32[]{:S(2)}, u32[]{:S(2)}) %collective-permute-start.5) | collective-permute-done | bytes 262176 | tf_op jit(solution)/shard_map/ppermute | solution.py:511
  77.2 1.9 %collective-permute-done.6.refs_2_ = bf16[2,16,2,16,128]{4,3,2,1,0:T(8,128)(2,1)S(1)} collective-permute-done((bf16[2,16,2,16,128]{4,3,2,1,0:T(8,128)(2,1)S(1)}, bf16[2,16,2,16,128]{4,3,2,1,0:T(8,128)(2,1)S(1)}, u32[]{:S(2)}, u32[]{:S(2)}) %collective-permute-start.6) | collective-permute-done | bytes 262176 | tf_op jit(solution)/shard_map/ppermute | solution.py:511
  79.1 4.9 %collective-permute-done.7.refs_3_ = bf16[2,16,2,16,128]{4,3,2,1,0:T(8,128)(2,1)S(1)} collective-permute-done((bf16[2,16,2,16,128]{4,3,2,1,0:T(8,128)(2,1)S(1)}, bf16[2,16,2,16,128]{4,3,2,1,0:T(8,128)(2,1)S(1)}, u32[]{:S(2)}, u32[]{:S(2)}) %collective-permute-start.7) | collective-permute-done | bytes 262176 | tf_op jit(solution)/shard_map/ppermute | solution.py:511
  84.0 0.5 collective-permute-start.20
  84.7 9.5 %correlate_own.1 = (f32[640,128]{1,0:T(8,128)S(1)}, bf16[640,128]{1,0:T(8,128)(2,1)}, bf16[640,128]{1,0:T(8,128)(2,1)S(1)}, bf16[640,128]{1,0:T(8,128)(2,1)S(1)}) custom-call(bf16[2,16,2,16,128]{4,3,2,1,0:T(8,128)(2,1)S(1)} %get-tuple-element.39.refs_0_, bf16[2,16,2,16,128]{4,3,2,1,0:T(8,128)(2,1)S(1)} %collective-permute-done.5.refs_1_, ...), custom_call_target="tpu_custom_call" | custom-call | flops 1000000000 | bytes 23068672 | tf_op jit(solution)/shard_map/correlate_own/pallas_call | solution.py:353
  94.2 0.7 copy-done.7
  94.8 0.7 copy-done.9
  95.5 0.1 stack.165.refs_17_
  95.6 0.1 stack.162.refs_16_
  95.7 1.4 %collective-permute-start.16 = (bf16[640,128]{1,0:T(8,128)(2,1)}, bf16[640,128]{1,0:T(8,128)(2,1)S(1)}, u32[]{:S(2)}, u32[]{:S(2)}) collective-permute-start(bf16[640,128]{1,0:T(8,128)(2,1)} %copy-done.9), channel_id=1, source_target_pairs={{0,8},{2,10},{4,12},{6,14},{8,0},{10,2},{12,4},{14,6},{1,9},{3,11}... | collective-permute-start | bytes 491528 | tf_op jit(solution)/shard_map/ppermute | solution.py:534
  97.2 8.8 %correlate_cross.1 = (f32[512,128]{1,0:T(8,128)S(1)}, bf16[512,128]{1,0:T(8,128)(2,1)S(1)}, bf16[512,128]{1,0:T(8,128)(2,1)S(1)}, bf16[512,128]{1,0:T(8,128)(2,1)S(1)}) custom-call(bf16[2,16,2,16,128]{4,3,2,1,0:T(8,128)(2,1)S(1)} %get-tuple-element.39.refs_0_, bf16[2,16,2,16,128]{4,3,2,1,0:T(8,128)(2,1)S(1)} %collective-permute-done.5.refs_1_, ...), custom_call_target="tpu_custom_call" | custom-call | flops 1000000000 | bytes 23068672 | tf_op jit(solution)/shard_map/correlate_cross/pallas_call | solution.py:353
  105.9 3.1 %collective-permute-start.26 = (bf16[512,128]{1,0:T(8,128)(2,1)S(1)}, bf16[512,128]{1,0:T(8,128)(2,1)S(1)}, u32[]{:S(2)}, u32[]{:S(2)}) collective-permute-start(bf16[512,128]{1,0:T(8,128)(2,1)S(1)} %get-tuple-element.58), channel_id=1, source_target_pairs={{0,4},{2,6},{4,8},{6,10},{8,12},{10,14},{12,0},{14,2},{1,5},{3,7},... | collective-permute-start | bytes 393224 | tf_op jit(solution)/shard_map/ppermute | solution.py:538
  109.0 0.2 collective-permute-start.27
  109.2 2.2 %collective-permute-start.28 = (bf16[512,128]{1,0:T(8,128)(2,1)S(1)}, bf16[512,128]{1,0:T(8,128)(2,1)S(1)}, u32[]{:S(2)}, u32[]{:S(2)}) collective-permute-start(bf16[512,128]{1,0:T(8,128)(2,1)S(1)} %get-tuple-element.60), channel_id=1, source_target_pairs={{0,12},{2,14},{4,0},{6,2},{8,4},{10,6},{12,8},{14,10},{1,13},{3,15... | collective-permute-start | bytes 393224 | tf_op jit(solution)/shard_map/ppermute | solution.py:538
  111.4 3.7 %collective-permute-done.16.refs_3_ = bf16[640,128]{1,0:T(8,128)(2,1)S(1)} collective-permute-done((bf16[640,128]{1,0:T(8,128)(2,1)}, bf16[640,128]{1,0:T(8,128)(2,1)S(1)}, u32[]{:S(2)}, u32[]{:S(2)}) %collective-permute-start.16) | collective-permute-done | bytes 163872 | tf_op jit(solution)/shard_map/ppermute | solution.py:534
  115.3 3.7 %collective-permute-done.27.refs_7_ = bf16[512,128]{1,0:T(8,128)(2,1)S(1)} collective-permute-done((bf16[512,128]{1,0:T(8,128)(2,1)S(1)}, bf16[512,128]{1,0:T(8,128)(2,1)S(1)}, u32[]{:S(2)}, u32[]{:S(2)}) %collective-permute-start.27) | collective-permute-done | bytes 131104 | tf_op jit(solution)/shard_map/ppermute | solution.py:538
  119.0 0.2 collective-permute-done.28.refs_8_
  119.2 0.3 collective-permute-start.32
  119.5 2.9 %collective-permute-done.17.refs_4_ = bf16[640,128]{1,0:T(8,128)(2,1)S(1)} collective-permute-done((bf16[640,128]{1,0:T(8,128)(2,1)S(1)}, bf16[640,128]{1,0:T(8,128)(2,1)S(1)}, u32[]{:S(2)}, u32[]{:S(2)}) %collective-permute-start.17) | collective-permute-done | bytes 163872 | tf_op jit(solution)/shard_map/ppermute | solution.py:534
  122.4 3.2 %assemble.1 = f32[2,16,32,256]{3,2,1,0:T(8,128)} custom-call(s32[1]{0:T(128)} %bitcast.refs_0_, f32[640,128]{1,0:T(8,128)S(1)} %get-tuple-element.53.refs_1_, bf16[640,128]{1,0:T(8,128)(2,1)S(1)} %collective-permute-done.15.refs_2_, bf16[640,128]{1,0:T(8,128)(2,1)S(1)} %collective-permute-done.16.refs_3_, ...), custom_call_target="tpu_custom_call" | custom-call | flops 100000000 | bytes 8388608 | tf_op jit(solution)/shard_map/assemble/pallas_call | solution.py:433
  (63 shorter events, 0.5 us)
Async XLA Ops:
  0.0 1.6 %copy-start = (bf16[2,8,65536]{2,1,0:T(8,128)(2,1)S(1)}, bf16[2,8,65536]{2,1,0:T(8,128)(2,1)}, u32[]{:S(2)}) copy-start(bf16[2,8,65536]{2,1,0:T(8,128)(2,1)} %block.3) | copy-start | bytes 6291460
  1.6 2.9 %copy-start.1 = (bf16[2,8,65536]{2,1,0:T(8,128)(2,1)S(1)}, bf16[2,8,65536]{2,1,0:T(8,128)(2,1)}, u32[]{:S(2)}) copy-start(bf16[2,8,65536]{2,1,0:T(8,128)(2,1)} %block.3) | copy-start | bytes 6291460
  1.6 12.7 %copy-start.11 = (bf16[2,2,32,128]{3,2,1,0:T(8,128)(2,1)S(1)}, bf16[2,2,32,128]{3,2,1,0:T(8,128)(2,1)}, u32[]{:S(2)}) copy-start(bf16[2,2,32,128]{3,2,1,0:T(8,128)(2,1)} %constant.132) | copy-start | bytes 98308
  1.6 13.5 %copy-start.12 = (s32[8]{0:T(128)S(1)}, s32[8]{0:T(128)}, u32[]{:S(2)}) copy-start(s32[8]{0:T(128)} %param.8) | copy-start | bytes 100
  1.6 45.8 %copy-start.4 = (f32[64,128]{1,0:T(8,128)S(1)}, f32[64,128]{1,0:T(8,128)}, u32[]{:S(2)}) copy-start(f32[64,128]{1,0:T(8,128)} %constant.131.clone.refs_8_) | copy-start | bytes 98308
  1.6 45.8 %copy-start.5 = (f32[64,128]{1,0:T(8,128)S(1)}, f32[64,128]{1,0:T(8,128)}, u32[]{:S(2)}) copy-start(f32[64,128]{1,0:T(8,128)} %constant.130.clone.refs_7_) | copy-start | bytes 98308
  1.6 45.8 %copy-start.6 = (bf16[128,128]{1,0:T(8,128)(2,1)S(1)}, bf16[128,128]{1,0:T(8,128)(2,1)}, u32[]{:S(2)}) copy-start(bf16[128,128]{1,0:T(8,128)(2,1)} %constant.129.clone.refs_6_) | copy-start | bytes 98308
  2.8 44.6 %collective-permute-start = (bf16[4,2,512,128]{3,2,1,0:T(8,128)(2,1)S(1)}, bf16[4,2,512,128]{3,2,1,0:T(8,128)(2,1)}, u32[]{:S(2)}, u32[]{:S(2)}) collective-permute-start(bf16[4,2,512,128]{3,2,1,0:T(8,128)(2,1)S(1)} %pick.2.refs_1_), channel_id=1, source_target_pairs={{2,6},{6,10},{10,14},{3,7},{7,11},{11,15},{18,22},{22,26},{26,30},... | collective-permute-start | bytes 3145736 | tf_op jit(solution)/shard_map/ppermute | solution.py:492
  6.5 39.0 %collective-permute-start.1 = (bf16[2,512,128]{2,1,0:T(8,128)(2,1)S(1)}, bf16[2,512,128]{2,1,0:T(8,128)(2,1)S(1)}, u32[]{:S(2)}, u32[]{:S(2)}) collective-permute-start(bf16[2,512,128]{2,1,0:T(8,128)(2,1)S(1)} %get-tuple-element.33), channel_id=1, source_target_pairs={{0,2},{2,0},{4,6},{6,4},{8,10},{10,8},{12,14},{14,12},{1,3},{3,1},... | collective-permute-start | bytes 786440 | tf_op jit(solution)/shard_map/ppermute | solution.py:491
  12.2 30.3 %collective-permute-start.3 = (bf16[2,512,128]{2,1,0:T(8,128)(2,1)}, bf16[2,512,128]{2,1,0:T(8,128)(2,1)S(1)}, u32[]{:S(2)}, u32[]{:S(2)}) collective-permute-start(bf16[2,512,128]{2,1,0:T(8,128)(2,1)} %get-tuple-element.34), channel_id=1, source_target_pairs={{0,2},{2,0},{4,6},{6,4},{8,10},{10,8},{12,14},{14,12},{1,3},{3,1},... | collective-permute-start | bytes 786440 | tf_op jit(solution)/shard_map/ppermute | solution.py:491
  12.3 26.1 %collective-permute-start.8 = (bf16[2,512,128]{2,1,0:T(8,128)(2,1)}, bf16[2,512,128]{2,1,0:T(8,128)(2,1)S(1)}, u32[]{:S(2)}, u32[]{:S(2)}) collective-permute-start(bf16[2,512,128]{2,1,0:T(8,128)(2,1)} %get-tuple-element.43), channel_id=1, source_target_pairs={{0,2},{2,0},{4,6},{6,4},{8,10},{10,8},{12,14},{14,12},{1,3},{3,1},... | collective-permute-start | bytes 786440 | tf_op jit(solution)/shard_map/ppermute | solution.py:491
  14.3 20.9 %collective-permute-start.10 = (bf16[2,512,128]{2,1,0:T(8,128)(2,1)}, bf16[2,512,128]{2,1,0:T(8,128)(2,1)S(1)}, u32[]{:S(2)}, u32[]{:S(2)}) collective-permute-start(bf16[2,512,128]{2,1,0:T(8,128)(2,1)} %get-tuple-element.44), channel_id=1, source_target_pairs={{0,2},{2,0},{4,6},{6,4},{8,10},{10,8},{12,14},{14,12},{1,3},{3,1},... | collective-permute-start | bytes 786440 | tf_op jit(solution)/shard_map/ppermute | solution.py:491
  35.1 12.3 %collective-permute-start.11 = (bf16[2,512,128]{2,1,0:T(8,128)(2,1)S(1)}, bf16[2,512,128]{2,1,0:T(8,128)(2,1)S(1)}, u32[]{:S(2)}, u32[]{:S(2)}) collective-permute-start(bf16[2,512,128]{2,1,0:T(8,128)(2,1)S(1)} %collective-permute-done.10.refs_3_), channel_id=1, source_target_pairs={{0,4},{4,8},{8,12},{1,5},{5,9},{9,13},{16,20},{20,24},{24,28},{17,... | collective-permute-start | bytes 786440 | tf_op jit(solution)/shard_map/ppermute | solution.py:493
  38.4 14.0 %collective-permute-start.9 = (bf16[2,512,128]{2,1,0:T(8,128)(2,1)S(1)}, bf16[2,512,128]{2,1,0:T(8,128)(2,1)S(1)}, u32[]{:S(2)}, u32[]{:S(2)}) collective-permute-start(bf16[2,512,128]{2,1,0:T(8,128)(2,1)S(1)} %collective-permute-done.8.refs_3_), channel_id=1, source_target_pairs={{0,4},{4,8},{8,12},{1,5},{5,9},{9,13},{16,20},{20,24},{24,28},{17,... | collective-permute-start | bytes 786440 | tf_op jit(solution)/shard_map/ppermute | solution.py:493
  42.5 17.2 %collective-permute-start.4 = (bf16[2,512,128]{2,1,0:T(8,128)(2,1)S(1)}, bf16[2,512,128]{2,1,0:T(8,128)(2,1)S(1)}, u32[]{:S(2)}, u32[]{:S(2)}) collective-permute-start(bf16[2,512,128]{2,1,0:T(8,128)(2,1)S(1)} %collective-permute-done.3.refs_3_), channel_id=1, source_target_pairs={{0,4},{4,8},{8,12},{1,5},{5,9},{9,13},{16,20},{20,24},{24,28},{17,... | collective-permute-start | bytes 786440 | tf_op jit(solution)/shard_map/ppermute | solution.py:493
  45.5 18.9 %collective-permute-start.2 = (bf16[2,512,128]{2,1,0:T(8,128)(2,1)S(1)}, bf16[2,512,128]{2,1,0:T(8,128)(2,1)S(1)}, u32[]{:S(2)}, u32[]{:S(2)}) collective-permute-start(bf16[2,512,128]{2,1,0:T(8,128)(2,1)S(1)} %collective-permute-done.1.refs_3_), channel_id=1, source_target_pairs={{0,4},{4,8},{8,12},{1,5},{5,9},{9,13},{16,20},{20,24},{24,28},{17,... | collective-permute-start | bytes 786440 | tf_op jit(solution)/shard_map/ppermute | solution.py:493
  47.4 1.0 copy-start.2
  52.3 8.2 %copy-start.3 = (f32[16,64,128]{2,1,0:T(8,128)S(1)}, f32[16,64,128]{2,1,0:T(8,128)}, u32[]{:S(2)}) copy-start(f32[16,64,128]{2,1,0:T(8,128)} %constant.128.clone.refs_5_) | copy-start | bytes 1572868
  56.2 13.8 %collective-permute-start.12 = (bf16[2,16,2,16,128]{4,3,2,1,0:T(8,128)(2,1)S(1)}, bf16[2,16,2,16,128]{4,3,2,1,0:T(8,128)(2,1)S(1)}, u32[]{:S(2)}, u32[]{:S(2)}) collective-permute-start(bf16[2,16,2,16,128]{4,3,2,1,0:T(8,128)(2,1)S(1)} %get-tuple-element.50), channel_id=1, source_target_pairs={{0,1},{1,0},{2,3},{3,2},{4,5},{5,4},{6,7},{7,6},{8,9},{9,8},{10,11... | collective-permute-start | bytes 786440 | tf_op jit(solution)/shard_map/ppermute | solution.py:511
  57.8 13.7 %collective-permute-start.13 = (bf16[2,16,2,16,128]{4,3,2,1,0:T(8,128)(2,1)S(1)}, bf16[2,16,2,16,128]{4,3,2,1,0:T(8,128)(2,1)S(1)}, u32[]{:S(2)}, u32[]{:S(2)}) collective-permute-start(bf16[2,16,2,16,128]{4,3,2,1,0:T(8,128)(2,1)S(1)} %get-tuple-element.51), channel_id=1, source_target_pairs={{0,2},{1,3},{2,0},{3,1},{4,6},{5,7},{6,4},{7,5},{8,10},{9,11},{10,... | collective-permute-start | bytes 786440 | tf_op jit(solution)/shard_map/ppermute | solution.py:511
  57.8 14.2 %collective-permute-start.14 = (bf16[2,16,2,16,128]{4,3,2,1,0:T(8,128)(2,1)S(1)}, bf16[2,16,2,16,128]{4,3,2,1,0:T(8,128)(2,1)S(1)}, u32[]{:S(2)}, u32[]{:S(2)}) collective-permute-start(bf16[2,16,2,16,128]{4,3,2,1,0:T(8,128)(2,1)S(1)} %get-tuple-element.52), channel_id=1, source_target_pairs={{0,3},{1,2},{2,1},{3,0},{4,7},{5,6},{6,5},{7,4},{8,11},{9,10},{10,... | collective-permute-start | bytes 786440 | tf_op jit(solution)/shard_map/ppermute | solution.py:511
  59.8 12.2 %collective-permute-start.22 = (bf16[2,16,2,16,128]{4,3,2,1,0:T(8,128)(2,1)S(1)}, bf16[2,16,2,16,128]{4,3,2,1,0:T(8,128)(2,1)S(1)}, u32[]{:S(2)}, u32[]{:S(2)}) collective-permute-start(bf16[2,16,2,16,128]{4,3,2,1,0:T(8,128)(2,1)S(1)} %get-tuple-element.49.refs_4_), channel_id=1, source_target_pairs={{0,16},{16,0},{1,17},{17,1},{2,18},{18,2},{3,19},{19,3},{4,20},{20... | collective-permute-start | bytes 786440 | tf_op jit(solution)/shard_map/ppermute | solution.py:513
  64.3 20.3 %copy-start.10 = (s32[20]{0:T(128)S(1)}, s32[20]{0:T(128)}, u32[]{:S(2)}) copy-start(s32[20]{0:T(128)} %constant.121.clone.1.refs_9_) | copy-start | bytes 244
  68.4 8.8 %collective-permute-start.5 = (bf16[2,16,2,16,128]{4,3,2,1,0:T(8,128)(2,1)S(1)}, bf16[2,16,2,16,128]{4,3,2,1,0:T(8,128)(2,1)S(1)}, u32[]{:S(2)}, u32[]{:S(2)}) collective-permute-start(bf16[2,16,2,16,128]{4,3,2,1,0:T(8,128)(2,1)S(1)} %get-tuple-element.40), channel_id=1, source_target_pairs={{0,1},{1,0},{2,3},{3,2},{4,5},{5,4},{6,7},{7,6},{8,9},{9,8},{10,11... | collective-permute-start | bytes 786440 | tf_op jit(solution)/shard_map/ppermute | solution.py:511
  70.0 9.1 %collective-permute-start.6 = (bf16[2,16,2,16,128]{4,3,2,1,0:T(8,128)(2,1)S(1)}, bf16[2,16,2,16,128]{4,3,2,1,0:T(8,128)(2,1)S(1)}, u32[]{:S(2)}, u32[]{:S(2)}) collective-permute-start(bf16[2,16,2,16,128]{4,3,2,1,0:T(8,128)(2,1)S(1)} %get-tuple-element.41), channel_id=1, source_target_pairs={{0,2},{1,3},{2,0},{3,1},{4,6},{5,7},{6,4},{7,5},{8,10},{9,11},{10,... | collective-permute-start | bytes 786440 | tf_op jit(solution)/shard_map/ppermute | solution.py:511
  71.5 12.5 %collective-permute-start.7 = (bf16[2,16,2,16,128]{4,3,2,1,0:T(8,128)(2,1)S(1)}, bf16[2,16,2,16,128]{4,3,2,1,0:T(8,128)(2,1)S(1)}, u32[]{:S(2)}, u32[]{:S(2)}) collective-permute-start(bf16[2,16,2,16,128]{4,3,2,1,0:T(8,128)(2,1)S(1)} %get-tuple-element.42), channel_id=1, source_target_pairs={{0,3},{1,2},{2,1},{3,0},{4,7},{5,6},{6,5},{7,4},{8,11},{9,10},{10,... | collective-permute-start | bytes 786440 | tf_op jit(solution)/shard_map/ppermute | solution.py:511
  72.0 12.0 %collective-permute-start.18 = (bf16[2,16,2,16,128]{4,3,2,1,0:T(8,128)(2,1)S(1)}, bf16[2,16,2,16,128]{4,3,2,1,0:T(8,128)(2,1)S(1)}, u32[]{:S(2)}, u32[]{:S(2)}) collective-permute-start(bf16[2,16,2,16,128]{4,3,2,1,0:T(8,128)(2,1)S(1)} %get-tuple-element.39.refs_0_), channel_id=1, source_target_pairs={{0,16},{16,0},{1,17},{17,1},{2,18},{18,2},{3,19},{19,3},{4,20},{20... | collective-permute-start | bytes 786440 | tf_op jit(solution)/shard_map/ppermute | solution.py:513
  72.0 12.5 %collective-permute-start.23 = (bf16[2,16,2,16,128]{4,3,2,1,0:T(8,128)(2,1)S(1)}, bf16[2,16,2,16,128]{4,3,2,1,0:T(8,128)(2,1)S(1)}, u32[]{:S(2)}, u32[]{:S(2)}) collective-permute-start(bf16[2,16,2,16,128]{4,3,2,1,0:T(8,128)(2,1)S(1)} %collective-permute-done.12.refs_5_), channel_id=1, source_target_pairs={{0,16},{16,0},{1,17},{17,1},{2,18},{18,2},{3,19},{19,3},{4,20},{20... | collective-permute-start | bytes 786440 | tf_op jit(solution)/shard_map/ppermute | solution.py:513
  77.2 17.6 %collective-permute-start.24 = (bf16[2,16,2,16,128]{4,3,2,1,0:T(8,128)(2,1)S(1)}, bf16[2,16,2,16,128]{4,3,2,1,0:T(8,128)(2,1)}, u32[]{:S(2)}, u32[]{:S(2)}) collective-permute-start(bf16[2,16,2,16,128]{4,3,2,1,0:T(8,128)(2,1)S(1)} %collective-permute-done.13.refs_6_), channel_id=1, source_target_pairs={{0,16},{16,0},{1,17},{17,1},{2,18},{18,2},{3,19},{19,3},{4,20},{20... | collective-permute-start | bytes 786440 | tf_op jit(solution)/shard_map/ppermute | solution.py:513
  79.1 16.5 %collective-permute-start.25 = (bf16[2,16,2,16,128]{4,3,2,1,0:T(8,128)(2,1)S(1)}, bf16[2,16,2,16,128]{4,3,2,1,0:T(8,128)(2,1)}, u32[]{:S(2)}, u32[]{:S(2)}) collective-permute-start(bf16[2,16,2,16,128]{4,3,2,1,0:T(8,128)(2,1)S(1)} %collective-permute-done.14.refs_7_), channel_id=1, source_target_pairs={{0,16},{16,0},{1,17},{17,1},{2,18},{18,2},{3,19},{19,3},{4,20},{20... | collective-permute-start | bytes 786440 | tf_op jit(solution)/shard_map/ppermute | solution.py:513
  84.0 13.1 %collective-permute-start.19 = (bf16[2,16,2,16,128]{4,3,2,1,0:T(8,128)(2,1)S(1)}, bf16[2,16,2,16,128]{4,3,2,1,0:T(8,128)(2,1)}, u32[]{:S(2)}, u32[]{:S(2)}) collective-permute-start(bf16[2,16,2,16,128]{4,3,2,1,0:T(8,128)(2,1)S(1)} %collective-permute-done.5.refs_1_), channel_id=1, source_target_pairs={{0,16},{16,0},{1,17},{17,1},{2,18},{18,2},{3,19},{19,3},{4,20},{20... | collective-permute-start | bytes 786440 | tf_op jit(solution)/shard_map/ppermute | solution.py:513
  84.0 13.1 %collective-permute-start.20 = (bf16[2,16,2,16,128]{4,3,2,1,0:T(8,128)(2,1)S(1)}, bf16[2,16,2,16,128]{4,3,2,1,0:T(8,128)(2,1)}, u32[]{:S(2)}, u32[]{:S(2)}) collective-permute-start(bf16[2,16,2,16,128]{4,3,2,1,0:T(8,128)(2,1)S(1)} %collective-permute-done.6.refs_2_), channel_id=1, source_target_pairs={{0,16},{16,0},{1,17},{17,1},{2,18},{18,2},{3,19},{19,3},{4,20},{20... | collective-permute-start | bytes 786440 | tf_op jit(solution)/shard_map/ppermute | solution.py:513
  84.5 12.6 %collective-permute-start.21 = (bf16[2,16,2,16,128]{4,3,2,1,0:T(8,128)(2,1)S(1)}, bf16[2,16,2,16,128]{4,3,2,1,0:T(8,128)(2,1)}, u32[]{:S(2)}, u32[]{:S(2)}) collective-permute-start(bf16[2,16,2,16,128]{4,3,2,1,0:T(8,128)(2,1)S(1)} %collective-permute-done.7.refs_3_), channel_id=1, source_target_pairs={{0,16},{16,0},{1,17},{17,1},{2,18},{18,2},{3,19},{19,3},{4,20},{20... | collective-permute-start | bytes 786440 | tf_op jit(solution)/shard_map/ppermute | solution.py:513
  94.2 0.7 copy-start.7
  94.8 0.7 copy-start.9
  95.5 16.0 %collective-permute-start.15 = (bf16[640,128]{1,0:T(8,128)(2,1)}, bf16[640,128]{1,0:T(8,128)(2,1)S(1)}, u32[]{:S(2)}, u32[]{:S(2)}) collective-permute-start(bf16[640,128]{1,0:T(8,128)(2,1)} %get-tuple-element.54), channel_id=1, source_target_pairs={{0,4},{2,6},{4,8},{6,10},{8,12},{10,14},{12,0},{14,2},{1,5},{3,7},... | collective-permute-start | bytes 491528 | tf_op jit(solution)/shard_map/ppermute | solution.py:534
  95.7 19.5 %copy-start.8 = (bf16[640,128]{1,0:T(8,128)(2,1)S(1)}, bf16[640,128]{1,0:T(8,128)(2,1)}, u32[]{:S(2)}) copy-start(bf16[640,128]{1,0:T(8,128)(2,1)} %copy-done.7) | copy-start | bytes 491524
  95.7 19.5 %collective-permute-start.16 = (bf16[640,128]{1,0:T(8,128)(2,1)}, bf16[640,128]{1,0:T(8,128)(2,1)S(1)}, u32[]{:S(2)}, u32[]{:S(2)}) collective-permute-start(bf16[640,128]{1,0:T(8,128)(2,1)} %copy-done.9), channel_id=1, source_target_pairs={{0,8},{2,10},{4,12},{6,14},{8,0},{10,2},{12,4},{14,6},{1,9},{3,11}... | collective-permute-start | bytes 491528 | tf_op jit(solution)/shard_map/ppermute | solution.py:534
  105.9 9.3 %collective-permute-start.26 = (bf16[512,128]{1,0:T(8,128)(2,1)S(1)}, bf16[512,128]{1,0:T(8,128)(2,1)S(1)}, u32[]{:S(2)}, u32[]{:S(2)}) collective-permute-start(bf16[512,128]{1,0:T(8,128)(2,1)S(1)} %get-tuple-element.58), channel_id=1, source_target_pairs={{0,4},{2,6},{4,8},{6,10},{8,12},{10,14},{12,0},{14,2},{1,5},{3,7},... | collective-permute-start | bytes 393224 | tf_op jit(solution)/shard_map/ppermute | solution.py:538
  109.0 10.0 %collective-permute-start.27 = (bf16[512,128]{1,0:T(8,128)(2,1)S(1)}, bf16[512,128]{1,0:T(8,128)(2,1)S(1)}, u32[]{:S(2)}, u32[]{:S(2)}) collective-permute-start(bf16[512,128]{1,0:T(8,128)(2,1)S(1)} %get-tuple-element.59), channel_id=1, source_target_pairs={{0,8},{2,10},{4,12},{6,14},{8,0},{10,2},{12,4},{14,6},{1,9},{3,11}... | collective-permute-start | bytes 393224 | tf_op jit(solution)/shard_map/ppermute | solution.py:538
  109.2 10.0 %collective-permute-start.28 = (bf16[512,128]{1,0:T(8,128)(2,1)S(1)}, bf16[512,128]{1,0:T(8,128)(2,1)S(1)}, u32[]{:S(2)}, u32[]{:S(2)}) collective-permute-start(bf16[512,128]{1,0:T(8,128)(2,1)S(1)} %get-tuple-element.60), channel_id=1, source_target_pairs={{0,12},{2,14},{4,0},{6,2},{8,4},{10,6},{12,8},{14,10},{1,13},{3,15... | collective-permute-start | bytes 393224 | tf_op jit(solution)/shard_map/ppermute | solution.py:538
  111.4 11.0 %collective-permute-start.29 = (f32[512,128]{1,0:T(8,128)S(1)}, f32[512,128]{1,0:T(8,128)S(1)}, u32[]{:S(2)}, u32[]{:S(2)}) collective-permute-start(f32[512,128]{1,0:T(8,128)S(1)} %get-tuple-element.57.refs_5_), channel_id=1, source_target_pairs={{0,16},{16,0},{1,17},{17,1},{2,18},{18,2},{3,19},{19,3},{4,20},{20... | collective-permute-start | bytes 786440 | tf_op jit(solution)/shard_map/ppermute | solution.py:539
  115.2 7.2 %collective-permute-start.17 = (bf16[640,128]{1,0:T(8,128)(2,1)S(1)}, bf16[640,128]{1,0:T(8,128)(2,1)S(1)}, u32[]{:S(2)}, u32[]{:S(2)}) collective-permute-start(bf16[640,128]{1,0:T(8,128)(2,1)S(1)} %copy-done.8), channel_id=1, source_target_pairs={{0,12},{2,14},{4,0},{6,2},{8,4},{10,6},{12,8},{14,10},{1,13},{3,15... | collective-permute-start | bytes 491528 | tf_op jit(solution)/shard_map/ppermute | solution.py:534
  115.2 7.2 %collective-permute-start.30 = (bf16[512,128]{1,0:T(8,128)(2,1)S(1)}, bf16[512,128]{1,0:T(8,128)(2,1)S(1)}, u32[]{:S(2)}, u32[]{:S(2)}) collective-permute-start(bf16[512,128]{1,0:T(8,128)(2,1)S(1)} %collective-permute-done.26.refs_6_), channel_id=1, source_target_pairs={{0,16},{16,0},{1,17},{17,1},{2,18},{18,2},{3,19},{19,3},{4,20},{20... | collective-permute-start | bytes 393224 | tf_op jit(solution)/shard_map/ppermute | solution.py:539
  119.0 3.4 %collective-permute-start.31 = (bf16[512,128]{1,0:T(8,128)(2,1)S(1)}, bf16[512,128]{1,0:T(8,128)(2,1)S(1)}, u32[]{:S(2)}, u32[]{:S(2)}) collective-permute-start(bf16[512,128]{1,0:T(8,128)(2,1)S(1)} %collective-permute-done.27.refs_7_), channel_id=1, source_target_pairs={{0,16},{16,0},{1,17},{17,1},{2,18},{18,2},{3,19},{19,3},{4,20},{20... | collective-permute-start | bytes 393224 | tf_op jit(solution)/shard_map/ppermute | solution.py:539
  119.2 3.2 %collective-permute-start.32 = (bf16[512,128]{1,0:T(8,128)(2,1)S(1)}, bf16[512,128]{1,0:T(8,128)(2,1)S(1)}, u32[]{:S(2)}, u32[]{:S(2)}) collective-permute-start(bf16[512,128]{1,0:T(8,128)(2,1)S(1)} %collective-permute-done.28.refs_8_), channel_id=1, source_target_pairs={{0,16},{16,0},{1,17},{17,1},{2,18},{18,2},{3,19},{19,3},{4,20},{20... | collective-permute-start | bytes 393224 | tf_op jit(solution)/shard_map/ppermute | solution.py:539

commit v4 on v3

--- a/solution.py
+++ b/solution.py
@@ -17,6 +17,8 @@
 PAIR = 2
 TILE = 4
 JOIN = 2
+
+G_AT, O_AT, CORE_AT, CT_AT, DELAY_AT = range(5)
 
 VMEM = pl.BlockSpec(memory_space=pltpu.VMEM)
 SMEM = pl.BlockSpec(memory_space=pltpu.SMEM)
@@ -79,7 +81,7 @@
     return np.concatenate([cosine, cosine], axis=1), np.concatenate([sine, sine], axis=1)
 
 
-def pick_kernel(count, joined, scal, block, *refs):
+def pick_kernel(count, joined, own, meta, block, *refs):
     outs, rows = refs[:-1], refs[-1]
     inputs, samples = block.shape[1], block.shape[2]
     step = 16
@@ -94,7 +96,7 @@
             return carry
 
         lax.fori_loop(0, samples // LANES // step, spread, 0)
-    first = scal[0]
+    first = (meta[G_AT] if own else 1 - meta[G_AT]) * count
     tall = 128
     for item in range(count):
         out = outs[0].at[item] if joined else outs[item]
@@ -109,12 +111,12 @@
         lax.fori_loop(0, samples // LANES // tall, gather, 0)
 
 
-def pick(block, first, count, joined):
+def pick(meta, block, count, joined, own):
     _, inputs, samples = block.shape
     one = (2, samples // LANES, LANES)
     shapes = [(count,) + one] if joined else [one] * count
     return pl.pallas_call(
-        functools.partial(pick_kernel, count, joined),
+        functools.partial(pick_kernel, count, joined, own),
         out_shape=[jax.ShapeDtypeStruct(s, jnp.bfloat16) for s in shapes],
         in_specs=[SMEM, VMEM],
         out_specs=[VMEM] * len(shapes),
@@ -122,23 +124,38 @@
         compiler_params=params(16),
         cost_estimate=cost(10**6, 4 * 2**20),
         name="pick",
-    )(first, block)
+    )(meta, block)
+
+
+def follow(block, after):
+    def hand_on(block, after, out):
+        pass
+
+    return pl.pallas_call(
+        hand_on,
+        out_shape=jax.ShapeDtypeStruct(block.shape, block.dtype),
+        in_specs=[ANY, ANY],
+        out_specs=ANY,
+        input_output_aliases={0: 0},
+        name="follow",
+    )(block, after)
 
 
 HALF = 16
 SOME = 4
 
 
-def filterbank_kernel(index, before, frames, dests, *refs):
-    scal, keep, halo_own, recv, halo_far, coef, first, tw_cos, tw_sin, last = refs[:10]
-    earlier = refs[10 : 10 + dests * (before > 0)]
-    refs = refs[10 + len(earlier) :]
+def filterbank_kernel(index, before, frames, dests, per_ct, half_count, *refs):
+    meta, keep, halo_own, recv, halo_far, after, coef, first, tw_cos, tw_sin, last = refs[:11]
+    earlier = refs[11 : 11 + dests * (before > 0)]
+    refs = refs[11 + len(earlier) :]
     outs = refs[:dests]
     raw, weights, grouped, sems = refs[dests : dests + 4]
     filtered = refs[dests + 4 :]
     block_rows = frames * ROWS
     total = PAIR * frames
-    delay, me = scal[0], scal[1]
+    me, ct = meta[G_AT], meta[CT_AT]
+    delay = meta[DELAY_AT + me * half_count + index]
     down = delay // LANES
     across = delay % LANES
     lane = lax.broadcasted_iota(jnp.int32, (1, LANES), 1)
@@ -173,24 +190,21 @@
     bring(keep.at[index], 1 + me, 1).wait()
     bring(recv, 2 - me, 2).wait()
 
-    def filt(half):
-        for low, high_frame in ((0, 9), (9, HALF + 1)):
-            size = high_frame - low
-            for band in range(ROWS // 16):
-                for part in range(2):
-                    values = []
-                    for u in range(size + TAPS - 1):
-                        at = (half * HALF + low + u + frames - TAPS) * ROWS + band * 16
-                        values.append(raw[part, at : at + 16, :].astype(jnp.float32))
-                    sums = [None] * size
-                    for tap in range(TAPS):
-                        weight = weights[tap, band * 16 : band * 16 + 16, :]
-                        for u in range(size):
-                            term = weight * values[u + TAPS - 1 - tap]
-                            sums[u] = term if sums[u] is None else sums[u] + term
-                    for u in range(size):
-                        at = (low + u) * ROWS + band * 16
-                        filtered[half][part, at : at + 16, :] = sums[u]
+    def filt(half, low, high_frame, band, part):
+        size = high_frame - low
+        values = []
+        for u in range(size + TAPS - 1):
+            at = (half * HALF + low + u + frames - TAPS) * ROWS + band * 16
+            values.append(raw[part, at : at + 16, :].astype(jnp.float32))
+        sums = [None] * size
+        for tap in range(TAPS):
+            weight = weights[tap, band * 16 : band * 16 + 16, :]
+            for u in range(size):
+                term = weight * values[u + TAPS - 1 - tap]
+                sums[u] = term if sums[u] is None else sums[u] + term
+        for u in range(size):
+            at = (low + u) * ROWS + band * 16
+            filtered[half][part, at : at + 16, :] = sums[u]
 
     twice = lax.rem(across + RADIX, LANES)
 
@@ -224,7 +238,7 @@
             rows.append(value.astype(jnp.bfloat16))
         inner = jnp.concatenate(rows, axis=0)
         result = lax.dot_general(
-            last[...], inner, (((1,), (1,)), ((), ())), preferred_element_type=jnp.float32
+            rows_out, inner, (((1,), (1,)), ((), ())), preferred_element_type=jnp.float32
         ).astype(jnp.bfloat16)
         size = result.shape[0] // (2 * dests)
         for dest in range(dests):
@@ -235,25 +249,41 @@
                         low : low + size, u * LANES : (u + 1) * LANES
                     ]
 
-    for half in range(total // HALF):
-        filt(half)
-    for half in range(total // HALF):
-        for base in range(0, HALF, SOME):
-            for u in range(SOME):
-                place(half, base + u)
-            turn(half * HALF + base)
-
-
-def filterbank(index, scal, keep, halo_own, recv, halo_far, tables, last, earlier, dests):
+    rows_out = jnp.concatenate(
+        [last[me ^ dg, ct + dc] for dg in range(PAIR) for dc in range(per_ct)], axis=0
+    )
+    pieces = [
+        (low, high_frame, band, part)
+        for low, high_frame in ((0, 9), (9, HALF + 1))
+        for band in range(ROWS // 16)
+        for part in range(2)
+    ]
+    each = len(pieces) // (HALF // SOME)
+    halves = total // HALF
+    for half in range(halves + 1):
+        for n in range(HALF // SOME):
+            if half < halves:
+                for piece in pieces[n * each : (n + 1) * each]:
+                    filt(half, *piece)
+            if half:
+                for u in range(SOME):
+                    place(half - 1, n * SOME + u)
+                turn((half - 1) * HALF + n * SOME)
+
+
+def filterbank(index, meta, keep, halo_own, recv, halo_far, after, tables, earlier, dests):
     frames = keep.shape[2] // ROWS
-    size = last.shape[0] // (2 * dests)
+    size = tables[-1].shape[2] // 2
+    per_ct = tables[-1].shape[1] // 2
     before = earlier[0].shape[0] if earlier else 0
     all_rows = (PAIR + 1) * frames * ROWS
     shape = (before + 1, PAIR * frames // 2, 2, size, LANES)
     return pl.pallas_call(
-        functools.partial(filterbank_kernel, index, before, frames, dests),
+        functools.partial(
+            filterbank_kernel, index, before, frames, dests, per_ct, keep.shape[0]
+        ),
         out_shape=[jax.ShapeDtypeStruct(shape, jnp.bfloat16)] * dests,
-        in_specs=[SMEM] + [ANY] * 4 + [VMEM] * (5 + len(earlier)),
+        in_specs=[SMEM] + [ANY] * 5 + [VMEM] * (5 + len(earlier)),
         out_specs=[VMEM] * dests,
         scratch_shapes=[
             pltpu.VMEM((2, all_rows, LANES), jnp.bfloat16),
@@ -265,95 +295,141 @@
         compiler_params=params(16),
         cost_estimate=cost(10**9, 10 * 2**20),
         name="filterbank",
-    )(scal, keep, halo_own, recv, halo_far, *tables, last, *earlier)
-
-
-def pair_blocks(own):
+    )(meta, keep, halo_own, recv, halo_far, after, *tables, *earlier)
+
+
+SQUARE = [(p, q) for p in range(TILE) for q in range(TILE)]
+CORNER = [(p, q) for p in range(TILE) for q in range(p, TILE)]
+
+
+def own_blocks(own):
     tiles = own // TILE
-    inside = [(i, j) for i in range(tiles) for j in range(i, tiles)]
-    across = [(i, j) for i in range(tiles // 2) for j in range(tiles)]
-    return inside, across
+    whole = [(i, j, SQUARE) for i in range(tiles) for j in range(i + 1, tiles)]
+    return whole + [(i, i, CORNER) for i in range(tiles)]
+
+
+def cross_blocks(own):
+    tiles = own // TILE
+    return [(i, j, SQUARE) for i in range(tiles // 2) for j in range(tiles)]
+
+
+def pairs_in(blocks):
+    return sum(len(block[2]) for block in blocks)
+
+
+def chosen(t, values):
+    result = jnp.int32(values[0])
+    for n, value in enumerate(values[1:], 1):
+        result = jnp.where(t == n, jnp.int32(value), result)
+    return result
 
 
 def correlate_kernel(layout, *refs):
-    arrays, blocks, outer, span = layout
-    sources, (place, starts, where_outer) = refs[:arrays], refs[arrays : arrays + 3]
-    rest = refs[arrays + 3 :]
+    sources_at, blocks, own, cross, outer, span, per_ct, in_count, half_count = layout
+    meta, sources = refs[0], refs[1 : 1 + len(sources_at)]
+    rest = refs[1 + len(sources_at) :]
     outs, (spectra, sums, held) = rest[:-3], rest[-3:]
     steps = spectra.shape[1]
     some = 8
-
-    for index, source in enumerate(sources):
-        for item in range(source.shape[0]):
-
-            def spread(n, carry, index=index, source=source, item=item):
-                for u in range(some):
-                    real = source[item, n * some + u, 0].astype(jnp.float32)
-                    imag = source[item, n * some + u, 1].astype(jnp.float32)
-                    for which, value in enumerate((real, imag, real + imag, imag - real)):
-                        spectra[place[index] + item, n * some + u, which] = value
-                return carry
-
-            lax.fori_loop(0, steps // some, spread, 0)
+    core, g, ct = meta[CORE_AT], meta[G_AT], meta[CT_AT]
+
+    for source, (far, dg, dc, start) in zip(sources, sources_at):
+        base = lax.rem(ct - dc + per_ct, per_ct) * in_count + (g ^ dg) * half_count + start
+        wanted = None
+        if cross:
+            side = 1 - core if far else core
+            low = core * (own // 2)
+            wanted = (side == 1) | ((base >= low) & (base < low + own // 2))
+            base = base + side * own
+
+        def bring(source=source, base=base):
+            for item in range(source.shape[0]):
+
+                def spread(n, carry, item=item):
+                    for u in range(some):
+                        real = source[item, n * some + u, 0].astype(jnp.float32)
+                        imag = source[item, n * some + u, 1].astype(jnp.float32)
+                        for which, value in enumerate((real, imag, real + imag, imag - real)):
+                            spectra[base + item, n * some + u, which] = value
+                    return carry
+
+                lax.fori_loop(0, steps // some, spread, 0)
+
+        if wanted is None:
+            bring()
+        else:
+            pl.when(wanted)(bring)
 
     high = lax.broadcasted_iota(jnp.int32, (1, LANES), 1) < RADIX
-    rows_outer = blocks * TILE * TILE * span
+    rows_outer = pairs_in(blocks) * span
     size = outer * span
     unroll = 4
 
-    def block(t, carry):
-        left, right = starts[2 * t], starts[2 * t + 1]
-
+    def block(left, right, pairs, first_row):
         def over(one, two, acc, sign):
             def frame(n, acc):
                 acc = list(acc)
                 for u in range(unroll):
                     a = [spectra[left + p, n * unroll + u, one] for p in range(TILE)]
                     b = [spectra[right + q, n * unroll + u, two] for q in range(TILE)]
-                    for p in range(TILE):
-                        for q in range(TILE):
-                            at = p * TILE + q
-                            term = a[p] * b[q]
-                            acc[at] = acc[at] + term if sign > 0 else acc[at] - term
+                    for at, (p, q) in enumerate(pairs):
+                        term = a[p] * b[q]
+                        acc[at] = acc[at] + term if sign > 0 else acc[at] - term
                 return tuple(acc)
 
             return lax.fori_loop(0, steps // unroll, frame, tuple(acc))
 
-        zero = jnp.zeros((size, LANES), jnp.float32)
-        first = over(2, 0, [zero] * (TILE * TILE), 1)
-        for p in range(TILE * TILE):
-            held[0, p] = first[p]
+        count = len(pairs)
+        first = over(2, 0, [jnp.zeros((size, LANES), jnp.float32)] * count, 1)
+        for at in range(count):
+            held[0, at] = first[at]
         real = over(1, 3, first, 1)
-        for p in range(TILE * TILE):
-            held[1, p] = real[p] + pltpu.roll(real[p], RADIX, 1)
-        imag = over(0, 2, [held[0, p] for p in range(TILE * TILE)], -1)
-        for p in range(TILE * TILE):
-            folded = imag[p] + pltpu.roll(imag[p], RADIX, 1)
-            both = jnp.where(high, held[1, p], folded)
+        for at in range(count):
+            held[1, at] = real[at] + pltpu.roll(real[at], RADIX, 1)
+        imag = over(0, 2, [held[0, at] for at in range(count)], -1)
+        for at in range(count):
+            folded = imag[at] + pltpu.roll(imag[at], RADIX, 1)
+            both = jnp.where(high, held[1, at], folded)
             for o in range(outer):
-                at = o * rows_outer + (t * TILE * TILE + p) * span
-                sums[pl.ds(pl.multiple_of(at, span), span), :] = both[o * span : (o + 1) * span]
-        return carry
-
-    lax.fori_loop(0, blocks, block, 0)
+                row = o * rows_outer + first_row + at * span
+                sums[pl.ds(pl.multiple_of(row, span), span), :] = both[o * span : (o + 1) * span]
+
+    done = 0
+    for pairs in (SQUARE, CORNER):
+        some_blocks = [b for b in blocks if b[2] is pairs]
+        if not some_blocks:
+            continue
+
+        def step(t, carry, some_blocks=some_blocks, pairs=pairs, done=done):
+            left = TILE * chosen(t, [b[0] for b in some_blocks])
+            right = TILE * chosen(t, [b[1] for b in some_blocks])
+            if cross:
+                left, right = left + core * (own // 2), right + own
+            block(left, right, pairs, done + t * len(pairs) * span)
+            return carry
+
+        lax.fori_loop(0, len(some_blocks), step, 0)
+        done += pairs_in(some_blocks) * span
+
     for r in range(outer):
-        base = pl.multiple_of(lax.rem(where_outer[0] + r, outer) * rows_outer, 16)
+        base = pl.multiple_of(lax.rem(meta[O_AT] + r, outer) * rows_outer, 16)
         outs[r][...] = sums[pl.ds(base, rows_outer), :].astype(outs[r].dtype)
 
 
-def correlate(arrays, place, starts, where_outer, inputs, outer, span, name):
+def correlate(meta, arrays, sources_at, blocks, own, cross, sizes, name):
+    outer, span, per_ct, in_count, half_count = sizes
     _, steps, _, size, _ = arrays[0].shape
-    blocks = starts.shape[0] // 2
-    rows = blocks * TILE * TILE * span
+    inputs = 2 * own if cross else own
+    rows = pairs_in(blocks) * span
     shapes = []
     for r in range(outer):
         dtype = jnp.float32 if r == 0 else jnp.bfloat16
         shapes.append(jax.ShapeDtypeStruct((rows, LANES), dtype))
-    layout = (len(arrays), blocks, outer, span)
+    layout = (sources_at, blocks, own, cross) + sizes
     return pl.pallas_call(
         functools.partial(correlate_kernel, layout),
         out_shape=shapes,
-        in_specs=[VMEM] * len(arrays) + [SMEM] * 3,
+        in_specs=[SMEM] + [VMEM] * len(arrays),
         out_specs=[VMEM] * len(shapes),
         scratch_shapes=[
             pltpu.VMEM((inputs, steps, 4, size, LANES), jnp.float32),
@@ -363,54 +439,53 @@
         compiler_params=params(14 + inputs * steps * 4 * size * LANES * 4 // 2**20),
         cost_estimate=cost(10**9, 22 * 2**20),
         name=name,
-    )(*arrays, place, starts, where_outer)
+    )(meta, *arrays)
 
 
 def assemble_kernel(own, outer, span, scale, *refs):
-    core = refs[0]
+    meta = refs[0]
     mine_in = refs[1 : 1 + outer]
     mine_across = refs[1 + outer : 1 + 2 * outer]
     far_across = refs[1 + 2 * outer : 1 + 3 * outer]
     out, joined = refs[1 + 3 * outer :]
-    inside, across = pair_blocks(own)
-    rows = TILE * TILE * span
     lane = lax.broadcasted_iota(jnp.int32, (1, LANES), 1)
     high = lane < RADIX
     mirror = jnp.where(high, 1.0, -1.0).astype(jnp.float32)
-    me = core[0]
-
-    def added(sources, t):
-        total = sources[0][t * rows : (t + 1) * rows, :].astype(jnp.float32)
+    me = meta[CORE_AT]
+
+    def added(sources, low, rows):
+        total = sources[0][low : low + rows, :].astype(jnp.float32)
         for source in sources[1:]:
-            total = total + source[t * rows : (t + 1) * rows, :].astype(jnp.float32)
+            total = total + source[low : low + rows, :].astype(jnp.float32)
         return total * scale
 
     def put(value, row, col):
         at = pl.multiple_of((row * 2 * own + col) * span, span)
         joined[pl.ds(at, span), :] = value
 
-    for t, (i, j) in enumerate(inside):
-        total = added(mine_in, t)
+    done = 0
+    for i, j, pairs in own_blocks(own):
+        total = added(mine_in, done, len(pairs) * span)
         turned = total * mirror
-        for p in range(TILE):
-            for q in range(TILE):
-                low = (p * TILE + q) * span
-                a, b = i * TILE + p, j * TILE + q
-                put(total[low : low + span], a, me * own + b)
-                if i < j:
-                    put(turned[low : low + span], b, me * own + a)
+        for at, (p, q) in enumerate(pairs):
+            cut = slice(at * span, (at + 1) * span)
+            a, b = i * TILE + p, j * TILE + q
+            put(total[cut], a, me * own + b)
+            if a != b:
+                put(turned[cut], b, me * own + a)
+        done += len(pairs) * span
     sign = jnp.where(me == 0, jnp.ones_like(mirror), mirror)
     for sources, part in ((mine_across, me), (far_across, 1 - me)):
-        for t, (i, j) in enumerate(across):
-            total = added(sources, t) * sign
-            for p in range(TILE):
-                for q in range(TILE):
-                    low = (p * TILE + q) * span
-                    a = part * (own // 2) + i * TILE + p
-                    b = j * TILE + q
-                    row = jnp.where(me == 0, a, b)
-                    col = jnp.where(me == 0, own + b, a)
-                    put(total[low : low + span], row, col)
+        done = 0
+        for i, j, pairs in cross_blocks(own):
+            total = added(sources, done, len(pairs) * span) * sign
+            for at, (p, q) in enumerate(pairs):
+                a = part * (own // 2) + i * TILE + p
+                b = j * TILE + q
+                row = jnp.where(me == 0, a, b)
+                col = jnp.where(me == 0, own + b, a)
+                put(total[at * span : (at + 1) * span], row, col)
+            done += len(pairs) * span
 
     def emit(a, carry):
         for tile in range(2 * own // 8):
@@ -428,7 +503,7 @@
     lax.fori_loop(0, own, emit, 0)
 
 
-def assemble(core, mine_in, mine_across, far_across, own, span, scale):
+def assemble(meta, mine_in, mine_across, far_across, own, span, scale):
     outer = len(mine_in)
     return pl.pallas_call(
         functools.partial(assemble_kernel, own, outer, span, scale),
@@ -439,7 +514,7 @@
         compiler_params=params(24),
         cost_estimate=cost(10**8, 8 * 2**20),
         name="assemble",
-    )(core, *mine_in, *mine_across, *far_across)
+    )(meta, *mine_in, *mine_across, *far_across)
 
 
 def fast_fits(in_count, frame_count):
@@ -455,6 +530,7 @@
         and span in (2, 4, 8)
         and outer * span % 16 == 0
         and own % (2 * TILE) == 0
+        and (own * (own + 1) // 2 * span) % 16 == 0
     )
 
 
@@ -474,31 +550,31 @@
     onward = [(i, i + PAIR) for i in range(tm - PAIR)]
     cores = [(0, 1), (1, 0)]
 
-    def stacked(values):
-        return jnp.stack([jnp.asarray(v, jnp.int32) for v in values])
+    scalars = [None] * DELAY_AT
+    scalars[G_AT], scalars[O_AT], scalars[CORE_AT], scalars[CT_AT] = g, o, core, place_ct
+    meta = jnp.concatenate([jnp.stack(scalars).astype(jnp.int32), delays])
 
     dests = [(dg, dc) for dg in range(PAIR) for dc in range(per_ct)]
-    base = jnp.asarray(last_table(outer, per_ct, span))
-    base = jnp.where(g == 0, base, base[::-1])
-    base = lax.dynamic_slice_in_dim(jnp.concatenate([base, base], axis=1), place_ct, per_ct, 1)
-    last = base.reshape(-1, 2 * RADIX)
-    twice = np.concatenate([filter_table()] * 2, axis=1)
-    tables = [jnp.asarray(twice), jnp.asarray(first_table())]
-    tables += [jnp.asarray(t) for t in twiddle_tables()]
-
-    sends = pick(voltages, stacked([(1 - g) * half]), half, False)
-    keep = pick(voltages, stacked([g * half]), half, True)[0]
-    recvs = [lax.ppermute(block, "tm", swap) for block in sends]
+    base = last_table(outer, per_ct, span)
+    tables = [np.concatenate([filter_table()] * 2, axis=1), first_table(), *twiddle_tables()]
+    tables = [jnp.asarray(t) for t in tables + [np.concatenate([base, base], axis=1)]]
+
+    sends = list(pick(meta, voltages, half, False, False))
+    recvs = []
+    for c in range(half):
+        block = sends[c] if c < 2 else follow(sends[c], recvs[c - 2])
+        recvs.append(lax.ppermute(block, "tm", swap))
+    keep = pick(meta, voltages, half, True, True)[0]
     halo_own = lax.ppermute(keep, "tm", [p for p in onward if p[0] % PAIR == 1])
     fars = [lax.ppermute(block, "tm", [p for p in onward if p[0] % PAIR == 0]) for block in recvs]
 
-    arrays, others, place = [], [], []
-    spectra = []
+    arrays, others, places = [], [], []
+    spectra, after = [], meta
     for c in range(half):
-        scal = stacked([lax.dynamic_index_in_dim(delays, g * half + c, 0, False), g])
         spectra = filterbank(
-            c, scal, keep, halo_own, recvs[c], fars[c], tables, last, spectra, len(dests)
+            c, meta, keep, halo_own, recvs[c], fars[c], after, tables, spectra, len(dests)
         )
+        after = spectra[0]
         if c % JOIN < JOIN - 1:
             continue
         for (dg, dc), block in zip(dests, spectra):
@@ -511,22 +587,17 @@
                 block = lax.ppermute(block, ("tm", "ct"), route)
             arrays.append(block)
             others.append(lax.ppermute(block, "stn", cores))
-            start = ((place_ct - dc) % per_ct) * in_count + (g ^ dg) * half
-            place.append(start + c - JOIN + 1)
+            places.append((dg, dc, c - JOIN + 1))
         spectra = []
 
-    inside, across = pair_blocks(own)
-    starts = stacked([TILE * s for block in inside for s in block])
+    sizes = (outer, span, per_ct, in_count, half)
+    near = [(False,) + place for place in places]
+    far = [(True,) + place for place in places]
     mine_in = correlate(
-        arrays, stacked(place), starts, stacked([o]), own, outer, span, "correlate_own"
+        meta, arrays, near, own_blocks(own), own, False, sizes, "correlate_own"
     )
-    starts = []
-    for i, j in across:
-        starts += [core * (own // 2) + TILE * i, own + TILE * j]
-    place = [core * own + s for s in place] + [(1 - core) * own + s for s in place]
     mine_across = correlate(
-        arrays + others, stacked(place), stacked(starts), stacked([o]), 2 * own, outer, span,
-        "correlate_cross",
+        meta, arrays + others, near + far, cross_blocks(own), own, True, sizes, "correlate_cross"
     )
     mine_in, mine_across, far_across = list(mine_in), list(mine_across), []
     for r in range(1, outer):
@@ -538,7 +609,7 @@
             mine_across[r] = lax.ppermute(mine_across[r], "tm", route)
         far_across.append(lax.ppermute(mine_across[r], "stn", cores))
     scale = 1.0 / (tm * frame_count)
-    result = assemble(stacked([core]), mine_in, mine_across, far_across, own, span, scale)
+    result = assemble(meta, mine_in, mine_across, far_across, own, span, scale)
     return result.transpose(0, 3, 1, 2)
 
 

time: 127 us -> 123 us (0.969)
  waiting for transfers between devices: 41.4 us -> 34.8 us
  starting transfers between devices: 35.1 us -> 40 us
  other arithmetic: 3.65 us -> 0 us
    ppermute x4, waiting for transfers between devices: 19.3 us -> 10 us  [fast(): recvs.append(lax.ppermute(block, 'tm', swap))]
    ppermute x3, waiting for transfers between devices: 6.62 us -> 2.34 us  [fast(): mine_in[r] = lax.ppermute(mine_in[r], 'tm', route)]
    ppermute x6, waiting for transfers between devices: 11.5 us -> 15.4 us  [fast(): block = lax.ppermute(block, ('tm', 'ct'), route)]
    another operation x4 -> x0, other arithmetic: 2.86 us -> none  [stacked(): return jnp.stack([jnp.asarray(v, jnp.int32) for v in values])]
    pallas_call x2, Pallas kernels: 18.2 us -> 15.5 us  [correlate(): pl.pallas_call(functools.partial(correlate_kernel, layout), out_shape=sha...]
    ppermute x4, starting transfers between devices: 7.83 us -> 9.91 us  [fast(): recvs.append(lax.ppermute(block, 'tm', swap))]
    ppermute x3, waiting for transfers between devices: 3.87 us -> 5.82 us  [fast(): mine_across[r] = lax.ppermute(mine_across[r], 'tm', route)]
    ppermute x3, starting transfers between devices: 1.44 us -> 3.03 us  [fast(): mine_in[r] = lax.ppermute(mine_in[r], 'tm', route)]
  transfers between devices with their start and end apart: 33 -> 33, of which waited for: 8 -> 13; matrix products, arithmetic and copies ran while one was open for 4% -> 0% of each run, Pallas kernels for 29% -> 25%
where the time goes in v4:
time: 123 us; the launch traced here: 121 us
  starting transfers between devices  40 us (33%)
  Pallas kernels  39.7 us (32%)
  waiting for transfers between devices  34.8 us (28%)
  local copies, waits for them, and re-layouts  6.1 us (5%)
    pallas_call x4, Pallas kernels, filterbank(): pl.pallas_call(functools.partial(filterbank_kernel, index, before, frames...  16.4 us
    pallas_call x2, Pallas kernels, correlate(): pl.pallas_call(functools.partial(correlate_kernel, layout), out_shape=sha...  15.5 us
    ppermute x6, waiting for transfers between devices, fast(): block = lax.ppermute(block, ('tm', 'ct'), route)  15.4 us
    ppermute x4, starting transfers between devices, fast(): lax.ppermute(block, 'tm', [p for p in onward if p[0] % PAIR == 0])  10.7 us
    ppermute x4, waiting for transfers between devices, fast(): recvs.append(lax.ppermute(block, 'tm', swap))  10 us
    ppermute x4, starting transfers between devices, fast(): recvs.append(lax.ppermute(block, 'tm', swap))  9.91 us
    ppermute x6, starting transfers between devices, fast(): block = lax.ppermute(block, ('tm', 'ct'), route)  7.96 us
    ppermute x3, starting transfers between devices, fast(): mine_across[r] = lax.ppermute(mine_across[r], 'tm', route)  5.89 us
  transfers between devices with their start and end apart: 33, of which 13 were waited for; matrix products, arithmetic and copies ran while one was open for 0% of the time, Pallas kernels for 25%

profile of v4, /device:TPU:0, one launch (start us, length us, event | category | flops | bytes accessed | tf_op | source)
XLA Modules:
  0.0 121.0 jit_solution(6833037480428520337)
XLA Ops:
  0.0 0.7 concatenate.3.meta.refs_0_.refs_5_
  0.7 1.6 %copy-done = bf16[2,8,65536]{2,1,0:T(8,128)(2,1)S(1)} copy-done((bf16[2,8,65536]{2,1,0:T(8,128)(2,1)S(1)}, bf16[2,8,65536]{2,1,0:T(8,128)(2,1)}, u32[]{:S(2)}) %copy-start) | copy-done | bytes 2097176
  2.3 1.7 %pick.2.refs_1_ = bf16[4,2,512,128]{3,2,1,0:T(8,128)(2,1)S(1)} custom-call(s32[12]{0:T(128)S(1)} %concatenate.3.meta.refs_0_.refs_5_, bf16[2,8,65536]{2,1,0:T(8,128)(2,1)S(1)} %copy-done), custom_call_target="tpu_custom_call" | custom-call | flops 1000000 | bytes 4194304 | tf_op jit(solution)/shard_map/pick/pallas_call | solution.py:118
  4.1 0.9 collective-permute-start
  5.0 2.4 %pick.3 = (bf16[2,512,128]{2,1,0:T(8,128)(2,1)S(1)}, bf16[2,512,128]{2,1,0:T(8,128)(2,1)}, bf16[2,512,128]{2,1,0:T(8,128)(2,1)S(1)}, bf16[2,512,128]{2,1,0:T(8,128)(2,1)S(1)}) custom-call(s32[12]{0:T(128)S(1)} %concatenate.3.meta.refs_0_.refs_5_, bf16[2,8,65536]{2,1,0:T(8,128)(2,1)S(1)} %copy-done), custom_call_target="tpu_custom_call" | custom-call | flops 1000000 | bytes 4194304 | tf_op jit(solution)/shard_map/pick/pallas_call | solution.py:118
  7.4 0.7 copy-done.7
  8.1 0.7 copy-done.8
  8.8 5.8 %collective-permute-start.3 = (bf16[2,512,128]{2,1,0:T(8,128)(2,1)S(1)}, bf16[2,512,128]{2,1,0:T(8,128)(2,1)S(1)}, u32[]{:S(2)}, u32[]{:S(2)}) collective-permute-start(bf16[2,512,128]{2,1,0:T(8,128)(2,1)S(1)} %get-tuple-element.34), channel_id=1, source_target_pairs={{0,2},{2,0},{4,6},{6,4},{8,10},{10,8},{12,14},{14,12},{1,3},{3,1},... | collective-permute-start | bytes 786440 | tf_op jit(solution)/shard_map/ppermute | solution.py:566
  14.6 7.1 %collective-permute-done.3.refs_3_.after = bf16[2,512,128]{2,1,0:T(8,128)(2,1)S(1)} collective-permute-done((bf16[2,512,128]{2,1,0:T(8,128)(2,1)S(1)}, bf16[2,512,128]{2,1,0:T(8,128)(2,1)S(1)}, u32[]{:S(2)}, u32[]{:S(2)}) %collective-permute-start.3) | collective-permute-done | bytes 262176 | tf_op jit(solution)/shard_map/ppermute | solution.py:566
  21.7 0.7 copy-done.5
  22.4 2.1 %collective-permute-start.10 = (bf16[2,512,128]{2,1,0:T(8,128)(2,1)}, bf16[2,512,128]{2,1,0:T(8,128)(2,1)}, u32[]{:S(2)}, u32[]{:S(2)}) collective-permute-start(bf16[2,512,128]{2,1,0:T(8,128)(2,1)} %follow.3), channel_id=1, source_target_pairs={{0,2},{2,0},{4,6},{6,4},{8,10},{10,8},{12,14},{14,12},{1,3},{3,1},... | collective-permute-start | bytes 786440 | tf_op jit(solution)/shard_map/ppermute | solution.py:566
  24.5 2.9 %collective-permute-done.1.refs_3_.after = bf16[2,512,128]{2,1,0:T(8,128)(2,1)S(1)} collective-permute-done((bf16[2,512,128]{2,1,0:T(8,128)(2,1)}, bf16[2,512,128]{2,1,0:T(8,128)(2,1)S(1)}, u32[]{:S(2)}, u32[]{:S(2)}) %collective-permute-start.1) | collective-permute-done | bytes 262176 | tf_op jit(solution)/shard_map/ppermute | solution.py:566
  27.3 0.7 copy-done.2
  28.0 2.1 %collective-permute-start.8 = (bf16[2,512,128]{2,1,0:T(8,128)(2,1)}, bf16[2,512,128]{2,1,0:T(8,128)(2,1)S(1)}, u32[]{:S(2)}, u32[]{:S(2)}) collective-permute-start(bf16[2,512,128]{2,1,0:T(8,128)(2,1)} %follow.2), channel_id=1, source_target_pairs={{0,2},{2,0},{4,6},{6,4},{8,10},{10,8},{12,14},{14,12},{1,3},{3,1},... | collective-permute-start | bytes 786440 | tf_op jit(solution)/shard_map/ppermute | solution.py:566
  30.1 3.4 %collective-permute-start.4 = (bf16[2,512,128]{2,1,0:T(8,128)(2,1)}, bf16[2,512,128]{2,1,0:T(8,128)(2,1)S(1)}, u32[]{:S(2)}, u32[]{:S(2)}) collective-permute-start(bf16[2,512,128]{2,1,0:T(8,128)(2,1)} %copy-done.5), channel_id=1, source_target_pairs={{0,4},{4,8},{8,12},{1,5},{5,9},{9,13},{16,20},{20,24},{24,28},{17,... | collective-permute-start | bytes 786440 | tf_op jit(solution)/shard_map/ppermute | solution.py:569
  33.5 3.5 %collective-permute-start.2 = (bf16[2,512,128]{2,1,0:T(8,128)(2,1)}, bf16[2,512,128]{2,1,0:T(8,128)(2,1)S(1)}, u32[]{:S(2)}, u32[]{:S(2)}) collective-permute-start(bf16[2,512,128]{2,1,0:T(8,128)(2,1)} %copy-done.2), channel_id=1, source_target_pairs={{0,4},{4,8},{8,12},{1,5},{5,9},{9,13},{16,20},{20,24},{24,28},{17,... | collective-permute-start | bytes 786440 | tf_op jit(solution)/shard_map/ppermute | solution.py:569
  37.0 1.9 %collective-permute-start.11 = (bf16[2,512,128]{2,1,0:T(8,128)(2,1)}, bf16[2,512,128]{2,1,0:T(8,128)(2,1)S(1)}, u32[]{:S(2)}, u32[]{:S(2)}) collective-permute-start(bf16[2,512,128]{2,1,0:T(8,128)(2,1)} %collective-permute-done.10.refs_3_), channel_id=1, source_target_pairs={{0,4},{4,8},{8,12},{1,5},{5,9},{9,13},{16,20},{20,24},{24,28},{17,... | collective-permute-start | bytes 786440 | tf_op jit(solution)/shard_map/ppermute | solution.py:569
  39.0 1.9 %collective-permute-start.9 = (bf16[2,512,128]{2,1,0:T(8,128)(2,1)S(1)}, bf16[2,512,128]{2,1,0:T(8,128)(2,1)S(1)}, u32[]{:S(2)}, u32[]{:S(2)}) collective-permute-start(bf16[2,512,128]{2,1,0:T(8,128)(2,1)S(1)} %collective-permute-done.8.refs_3_), channel_id=1, source_target_pairs={{0,4},{4,8},{8,12},{1,5},{5,9},{9,13},{16,20},{20,24},{24,28},{17,... | collective-permute-start | bytes 786440 | tf_op jit(solution)/shard_map/ppermute | solution.py:569
  41.0 0.9 copy-done.6
  41.9 3.9 %filterbank.4 = (bf16[1,16,2,16,128]{4,3,2,1,0:T(8,128)(2,1)S(1)}, bf16[1,16,2,16,128]{4,3,2,1,0:T(8,128)(2,1)S(1)}, bf16[1,16,2,16,128]{4,3,2,1,0:T(8,128)(2,1)S(1)}, bf16[1,16,2,16,128]{4,3,2,1,0:T(8,128)(2,1)S(1)}) custom-call(s32[12]{0:T(128)S(1)} %concatenate.3.meta.refs_0_.refs_5_, bf16[4,2,512,128]{3,2,1,0:T(8,128)(2,1)S(1)} %pick.2.refs_1_, ...), custom_call_target="tpu_custom_call" | custom-call | flops 1000000000 | bytes 10485760 | tf_op jit(solution)/shard_map/filterbank/pallas_call | solution.py:281
  45.8 0.3 collective-permute-done.2.refs_4_
  46.1 3.9 %filterbank.5 = (bf16[2,16,2,16,128]{4,3,2,1,0:T(8,128)(2,1)S(1)}, bf16[2,16,2,16,128]{4,3,2,1,0:T(8,128)(2,1)S(1)}, bf16[2,16,2,16,128]{4,3,2,1,0:T(8,128)(2,1)S(1)}, bf16[2,16,2,16,128]{4,3,2,1,0:T(8,128)(2,1)S(1)}) custom-call(s32[12]{0:T(128)S(1)} %concatenate.3.meta.refs_0_.refs_5_, bf16[4,2,512,128]{3,2,1,0:T(8,128)(2,1)S(1)} %pick.2.refs_1_, ...), custom_call_target="tpu_custom_call" | custom-call | flops 1000000000 | bytes 10485760 | tf_op jit(solution)/shard_map/filterbank/pallas_call | solution.py:281
  50.0 0.9 collective-permute-done.11.refs_4_
  50.9 4.7 %filterbank.6 = (bf16[1,16,2,16,128]{4,3,2,1,0:T(8,128)(2,1)S(1)}, bf16[1,16,2,16,128]{4,3,2,1,0:T(8,128)(2,1)S(1)}, bf16[1,16,2,16,128]{4,3,2,1,0:T(8,128)(2,1)S(1)}, bf16[1,16,2,16,128]{4,3,2,1,0:T(8,128)(2,1)S(1)}) custom-call(s32[12]{0:T(128)S(1)} %concatenate.3.meta.refs_0_.refs_5_, bf16[4,2,512,128]{3,2,1,0:T(8,128)(2,1)S(1)} %pick.2.refs_1_, ...), custom_call_target="tpu_custom_call" | custom-call | flops 1000000000 | bytes 10485760 | tf_op jit(solution)/shard_map/filterbank/pallas_call | solution.py:281
  55.6 4.1 %filterbank.7 = (bf16[2,16,2,16,128]{4,3,2,1,0:T(8,128)(2,1)S(1)}, bf16[2,16,2,16,128]{4,3,2,1,0:T(8,128)(2,1)S(1)}, bf16[2,16,2,16,128]{4,3,2,1,0:T(8,128)(2,1)S(1)}, bf16[2,16,2,16,128]{4,3,2,1,0:T(8,128)(2,1)S(1)}) custom-call(s32[12]{0:T(128)S(1)} %concatenate.3.meta.refs_0_.refs_5_, bf16[4,2,512,128]{3,2,1,0:T(8,128)(2,1)S(1)} %pick.2.refs_1_, ...), custom_call_target="tpu_custom_call" | custom-call | flops 1000000000 | bytes 10485760 | tf_op jit(solution)/shard_map/filterbank/pallas_call | solution.py:281
  59.6 1.6 %collective-permute-start.12 = (bf16[2,16,2,16,128]{4,3,2,1,0:T(8,128)(2,1)S(1)}, bf16[2,16,2,16,128]{4,3,2,1,0:T(8,128)(2,1)S(1)}, u32[]{:S(2)}, u32[]{:S(2)}) collective-permute-start(bf16[2,16,2,16,128]{4,3,2,1,0:T(8,128)(2,1)S(1)} %get-tuple-element.50), channel_id=1, source_target_pairs={{0,1},{1,0},{2,3},{3,2},{4,5},{5,4},{6,7},{7,6},{8,9},{9,8},{10,11... | collective-permute-start | bytes 786440 | tf_op jit(solution)/shard_map/ppermute | solution.py:587
  61.2 2.0 %collective-permute-start.14 = (bf16[2,16,2,16,128]{4,3,2,1,0:T(8,128)(2,1)S(1)}, bf16[2,16,2,16,128]{4,3,2,1,0:T(8,128)(2,1)S(1)}, u32[]{:S(2)}, u32[]{:S(2)}) collective-permute-start(bf16[2,16,2,16,128]{4,3,2,1,0:T(8,128)(2,1)S(1)} %get-tuple-element.52), channel_id=1, source_target_pairs={{0,3},{1,2},{2,1},{3,0},{4,7},{5,6},{6,5},{7,4},{8,11},{9,10},{10,... | collective-permute-start | bytes 786440 | tf_op jit(solution)/shard_map/ppermute | solution.py:587
  63.2 1.5 %collective-permute-start.5 = (bf16[2,16,2,16,128]{4,3,2,1,0:T(8,128)(2,1)S(1)}, bf16[2,16,2,16,128]{4,3,2,1,0:T(8,128)(2,1)S(1)}, u32[]{:S(2)}, u32[]{:S(2)}) collective-permute-start(bf16[2,16,2,16,128]{4,3,2,1,0:T(8,128)(2,1)S(1)} %get-tuple-element.40), channel_id=1, source_target_pairs={{0,1},{1,0},{2,3},{3,2},{4,5},{5,4},{6,7},{7,6},{8,9},{9,8},{10,11... | collective-permute-start | bytes 786440 | tf_op jit(solution)/shard_map/ppermute | solution.py:587
  64.7 5.7 %collective-permute-done.12.refs_6_ = bf16[2,16,2,16,128]{4,3,2,1,0:T(8,128)(2,1)S(1)} collective-permute-done((bf16[2,16,2,16,128]{4,3,2,1,0:T(8,128)(2,1)S(1)}, bf16[2,16,2,16,128]{4,3,2,1,0:T(8,128)(2,1)S(1)}, u32[]{:S(2)}, u32[]{:S(2)}) %collective-permute-start.12) | collective-permute-done | bytes 262176 | tf_op jit(solution)/shard_map/ppermute | solution.py:587
  70.5 2.9 %collective-permute-start.7 = (bf16[2,16,2,16,128]{4,3,2,1,0:T(8,128)(2,1)S(1)}, bf16[2,16,2,16,128]{4,3,2,1,0:T(8,128)(2,1)S(1)}, u32[]{:S(2)}, u32[]{:S(2)}) collective-permute-start(bf16[2,16,2,16,128]{4,3,2,1,0:T(8,128)(2,1)S(1)} %get-tuple-element.42), channel_id=1, source_target_pairs={{0,3},{1,2},{2,1},{3,0},{4,7},{5,6},{6,5},{7,4},{8,11},{9,10},{10,... | collective-permute-start | bytes 786440 | tf_op jit(solution)/shard_map/ppermute | solution.py:587
  73.3 2.8 %collective-permute-done.14.refs_8_ = bf16[2,16,2,16,128]{4,3,2,1,0:T(8,128)(2,1)S(1)} collective-permute-done((bf16[2,16,2,16,128]{4,3,2,1,0:T(8,128)(2,1)S(1)}, bf16[2,16,2,16,128]{4,3,2,1,0:T(8,128)(2,1)S(1)}, u32[]{:S(2)}, u32[]{:S(2)}) %collective-permute-start.14) | collective-permute-done | bytes 262176 | tf_op jit(solution)/shard_map/ppermute | solution.py:587
  76.1 0.5 collective-permute-start.23
  76.6 3.5 %collective-permute-done.5.refs_2_ = bf16[2,16,2,16,128]{4,3,2,1,0:T(8,128)(2,1)S(1)} collective-permute-done((bf16[2,16,2,16,128]{4,3,2,1,0:T(8,128)(2,1)S(1)}, bf16[2,16,2,16,128]{4,3,2,1,0:T(8,128)(2,1)S(1)}, u32[]{:S(2)}, u32[]{:S(2)}) %collective-permute-start.5) | collective-permute-done | bytes 262176 | tf_op jit(solution)/shard_map/ppermute | solution.py:587
  80.1 0.6 collective-permute-done.6.refs_3_
  80.7 2.7 %collective-permute-done.7.refs_4_ = bf16[2,16,2,16,128]{4,3,2,1,0:T(8,128)(2,1)S(1)} collective-permute-done((bf16[2,16,2,16,128]{4,3,2,1,0:T(8,128)(2,1)S(1)}, bf16[2,16,2,16,128]{4,3,2,1,0:T(8,128)(2,1)S(1)}, u32[]{:S(2)}, u32[]{:S(2)}) %collective-permute-start.7) | collective-permute-done | bytes 262176 | tf_op jit(solution)/shard_map/ppermute | solution.py:587
  83.5 0.5 collective-permute-start.20
  84.1 7.8 %correlate_own.1 = (f32[544,128]{1,0:T(8,128)S(1)}, bf16[544,128]{1,0:T(8,128)(2,1)S(1)}, bf16[544,128]{1,0:T(8,128)(2,1)S(1)}, bf16[544,128]{1,0:T(8,128)(2,1)S(1)}) custom-call(s32[12]{0:T(128)S(1)} %concatenate.3.meta.refs_0_.refs_5_, bf16[2,16,2,16,128]{4,3,2,1,0:T(8,128)(2,1)S(1)} %get-tuple-element.39.refs_5_.refs_1_, ...), custom_call_target="tpu_custom_call" | custom-call | flops 1000000000 | bytes 23068672 | tf_op jit(solution)/shard_map/correlate_own/pallas_call | solution.py:429
  91.9 1.6 %collective-permute-start.15 = (bf16[544,128]{1,0:T(8,128)(2,1)S(1)}, bf16[544,128]{1,0:T(8,128)(2,1)S(1)}, u32[]{:S(2)}, u32[]{:S(2)}) collective-permute-start(bf16[544,128]{1,0:T(8,128)(2,1)S(1)} %get-tuple-element.54), channel_id=1, source_target_pairs={{0,4},{2,6},{4,8},{6,10},{8,12},{10,14},{12,0},{14,2},{1,5},{3,7},... | collective-permute-start | bytes 417800 | tf_op jit(solution)/shard_map/ppermute | solution.py:605
  93.5 7.7 %correlate_cross.1 = (f32[512,128]{1,0:T(8,128)S(1)}, bf16[512,128]{1,0:T(8,128)(2,1)S(1)}, bf16[512,128]{1,0:T(8,128)(2,1)S(1)}, bf16[512,128]{1,0:T(8,128)(2,1)S(1)}) custom-call(s32[12]{0:T(128)S(1)} %concatenate.3.meta.refs_0_.refs_5_, bf16[2,16,2,16,128]{4,3,2,1,0:T(8,128)(2,1)S(1)} %get-tuple-element.39.refs_5_.refs_1_, ...), custom_call_target="tpu_custom_call" | custom-call | flops 1000000000 | bytes 23068672 | tf_op jit(solution)/shard_map/correlate_cross/pallas_call | solution.py:429
  101.2 2.9 %collective-permute-start.26 = (bf16[512,128]{1,0:T(8,128)(2,1)S(1)}, bf16[512,128]{1,0:T(8,128)(2,1)S(1)}, u32[]{:S(2)}, u32[]{:S(2)}) collective-permute-start(bf16[512,128]{1,0:T(8,128)(2,1)S(1)} %get-tuple-element.58), channel_id=1, source_target_pairs={{0,4},{2,6},{4,8},{6,10},{8,12},{10,14},{12,0},{14,2},{1,5},{3,7},... | collective-permute-start | bytes 393224 | tf_op jit(solution)/shard_map/ppermute | solution.py:609
  104.1 0.4 collective-permute-start.27
  104.5 2.6 %collective-permute-start.28 = (bf16[512,128]{1,0:T(8,128)(2,1)S(1)}, bf16[512,128]{1,0:T(8,128)(2,1)S(1)}, u32[]{:S(2)}, u32[]{:S(2)}) collective-permute-start(bf16[512,128]{1,0:T(8,128)(2,1)S(1)} %get-tuple-element.60), channel_id=1, source_target_pairs={{0,12},{2,14},{4,0},{6,2},{8,4},{10,6},{12,8},{14,10},{1,13},{3,15... | collective-permute-start | bytes 393224 | tf_op jit(solution)/shard_map/ppermute | solution.py:609
  107.1 1.4 %collective-permute-start.17 = (bf16[544,128]{1,0:T(8,128)(2,1)S(1)}, bf16[544,128]{1,0:T(8,128)(2,1)S(1)}, u32[]{:S(2)}, u32[]{:S(2)}) collective-permute-start(bf16[544,128]{1,0:T(8,128)(2,1)S(1)} %get-tuple-element.56), channel_id=1, source_target_pairs={{0,12},{2,14},{4,0},{6,2},{8,4},{10,6},{12,8},{14,10},{1,13},{3,15... | collective-permute-start | bytes 417800 | tf_op jit(solution)/shard_map/ppermute | solution.py:605
  108.6 0.9 collective-permute-done.26.refs_6_
  109.5 4.9 %collective-permute-done.27.refs_7_ = bf16[512,128]{1,0:T(8,128)(2,1)S(1)} collective-permute-done((bf16[512,128]{1,0:T(8,128)(2,1)S(1)}, bf16[512,128]{1,0:T(8,128)(2,1)S(1)}, u32[]{:S(2)}, u32[]{:S(2)}) %collective-permute-start.27) | collective-permute-done | bytes 131104 | tf_op jit(solution)/shard_map/ppermute | solution.py:609
  114.4 0.5 collective-permute-start.32
  114.9 2.3 %collective-permute-done.17.refs_4_ = bf16[544,128]{1,0:T(8,128)(2,1)S(1)} collective-permute-done((bf16[544,128]{1,0:T(8,128)(2,1)S(1)}, bf16[544,128]{1,0:T(8,128)(2,1)S(1)}, u32[]{:S(2)}, u32[]{:S(2)}) %collective-permute-start.17) | collective-permute-done | bytes 139296 | tf_op jit(solution)/shard_map/ppermute | solution.py:605
  117.3 3.7 %assemble.1 = f32[2,16,32,256]{3,2,1,0:T(8,128)} custom-call(s32[12]{0:T(128)S(1)} %concatenate.3.meta.refs_0_.refs_5_, f32[544,128]{1,0:T(8,128)S(1)} %get-tuple-element.53.refs_1_, bf16[544,128]{1,0:T(8,128)(2,1)S(1)} %collective-permute-done.15.refs_2_, bf16[544,128]{1,0:T(8,128)(2,1)S(1)} %collective-permute-done.16.refs_3_, ...), custom_call_target="tpu_custom_call" | custom-call | flops 100000000 | bytes 8388608 | tf_op jit(solution)/shard_map/assemble/pallas_call | solution.py:508
  (54 shorter events, 0.3 us)
Async XLA Ops:
  0.7 1.6 %copy-start = (bf16[2,8,65536]{2,1,0:T(8,128)(2,1)S(1)}, bf16[2,8,65536]{2,1,0:T(8,128)(2,1)}, u32[]{:S(2)}) copy-start(bf16[2,8,65536]{2,1,0:T(8,128)(2,1)} %block.3) | copy-start | bytes 6291460
  4.0 36.9 %copy-start.1 = (f32[16,64,128]{2,1,0:T(8,128)S(1)}, f32[16,64,128]{2,1,0:T(8,128)}, u32[]{:S(2)}) copy-start(f32[16,64,128]{2,1,0:T(8,128)} %constant.46.clone.refs_6_) | copy-start | bytes 1572868
  4.0 36.9 %copy-start.4 = (bf16[2,4,32,128]{3,2,1,0:T(8,128)(2,1)S(1)}, bf16[2,4,32,128]{3,2,1,0:T(8,128)(2,1)}, u32[]{:S(2)}) copy-start(bf16[2,4,32,128]{3,2,1,0:T(8,128)(2,1)} %constant.50.clone.refs_10_) | copy-start | bytes 196612
  4.1 36.9 %copy-start.9 = (f32[64,128]{1,0:T(8,128)S(1)}, f32[64,128]{1,0:T(8,128)}, u32[]{:S(2)}) copy-start(f32[64,128]{1,0:T(8,128)} %constant.49.clone.refs_9_) | copy-start | bytes 98308
  4.1 36.9 %copy-start.10 = (f32[64,128]{1,0:T(8,128)S(1)}, f32[64,128]{1,0:T(8,128)}, u32[]{:S(2)}) copy-start(f32[64,128]{1,0:T(8,128)} %constant.48.clone.refs_8_) | copy-start | bytes 98308
  4.1 36.9 %copy-start.11 = (bf16[128,128]{1,0:T(8,128)(2,1)S(1)}, bf16[128,128]{1,0:T(8,128)(2,1)}, u32[]{:S(2)}) copy-start(bf16[128,128]{1,0:T(8,128)(2,1)} %constant.47.clone.refs_7_) | copy-start | bytes 98308
  4.1 36.8 %collective-permute-start = (bf16[4,2,512,128]{3,2,1,0:T(8,128)(2,1)S(1)}, bf16[4,2,512,128]{3,2,1,0:T(8,128)(2,1)S(1)}, u32[]{:S(2)}, u32[]{:S(2)}) collective-permute-start(bf16[4,2,512,128]{3,2,1,0:T(8,128)(2,1)S(1)} %pick.2.refs_1_), channel_id=1, source_target_pairs={{2,6},{6,10},{10,14},{3,7},{7,11},{11,15},{18,22},{22,26},{26,30},... | collective-permute-start | bytes 3145736 | tf_op jit(solution)/shard_map/ppermute | solution.py:568
  7.4 0.7 copy-start.7
  8.1 0.7 copy-start.8
  8.8 12.9 %collective-permute-start.3 = (bf16[2,512,128]{2,1,0:T(8,128)(2,1)S(1)}, bf16[2,512,128]{2,1,0:T(8,128)(2,1)S(1)}, u32[]{:S(2)}, u32[]{:S(2)}) collective-permute-start(bf16[2,512,128]{2,1,0:T(8,128)(2,1)S(1)} %get-tuple-element.34), channel_id=1, source_target_pairs={{0,2},{2,0},{4,6},{6,4},{8,10},{10,8},{12,14},{14,12},{1,3},{3,1},... | collective-permute-start | bytes 786440 | tf_op jit(solution)/shard_map/ppermute | solution.py:566
  14.5 12.8 %collective-permute-start.1 = (bf16[2,512,128]{2,1,0:T(8,128)(2,1)}, bf16[2,512,128]{2,1,0:T(8,128)(2,1)S(1)}, u32[]{:S(2)}, u32[]{:S(2)}) collective-permute-start(bf16[2,512,128]{2,1,0:T(8,128)(2,1)} %get-tuple-element.33), channel_id=1, source_target_pairs={{0,2},{2,0},{4,6},{6,4},{8,10},{10,8},{12,14},{14,12},{1,3},{3,1},... | collective-permute-start | bytes 786440 | tf_op jit(solution)/shard_map/ppermute | solution.py:566
  21.7 0.7 copy-start.5
  22.4 14.6 %collective-permute-start.10 = (bf16[2,512,128]{2,1,0:T(8,128)(2,1)}, bf16[2,512,128]{2,1,0:T(8,128)(2,1)}, u32[]{:S(2)}, u32[]{:S(2)}) collective-permute-start(bf16[2,512,128]{2,1,0:T(8,128)(2,1)} %follow.3), channel_id=1, source_target_pairs={{0,2},{2,0},{4,6},{6,4},{8,10},{10,8},{12,14},{14,12},{1,3},{3,1},... | collective-permute-start | bytes 786440 | tf_op jit(solution)/shard_map/ppermute | solution.py:566
  27.3 0.7 copy-start.2
  28.0 18.1 %copy-start.3 = (bf16[2,512,128]{2,1,0:T(8,128)(2,1)S(1)}, bf16[2,512,128]{2,1,0:T(8,128)(2,1)}, u32[]{:S(2)}) copy-start(bf16[2,512,128]{2,1,0:T(8,128)(2,1)} %copy-done.2) | copy-start | bytes 786436
  28.0 10.9 %collective-permute-start.8 = (bf16[2,512,128]{2,1,0:T(8,128)(2,1)}, bf16[2,512,128]{2,1,0:T(8,128)(2,1)S(1)}, u32[]{:S(2)}, u32[]{:S(2)}) collective-permute-start(bf16[2,512,128]{2,1,0:T(8,128)(2,1)} %follow.2), channel_id=1, source_target_pairs={{0,2},{2,0},{4,6},{6,4},{8,10},{10,8},{12,14},{14,12},{1,3},{3,1},... | collective-permute-start | bytes 786440 | tf_op jit(solution)/shard_map/ppermute | solution.py:566
  30.1 10.8 %collective-permute-start.4 = (bf16[2,512,128]{2,1,0:T(8,128)(2,1)}, bf16[2,512,128]{2,1,0:T(8,128)(2,1)S(1)}, u32[]{:S(2)}, u32[]{:S(2)}) collective-permute-start(bf16[2,512,128]{2,1,0:T(8,128)(2,1)} %copy-done.5), channel_id=1, source_target_pairs={{0,4},{4,8},{8,12},{1,5},{5,9},{9,13},{16,20},{20,24},{24,28},{17,... | collective-permute-start | bytes 786440 | tf_op jit(solution)/shard_map/ppermute | solution.py:569
  33.5 12.6 %collective-permute-start.2 = (bf16[2,512,128]{2,1,0:T(8,128)(2,1)}, bf16[2,512,128]{2,1,0:T(8,128)(2,1)S(1)}, u32[]{:S(2)}, u32[]{:S(2)}) collective-permute-start(bf16[2,512,128]{2,1,0:T(8,128)(2,1)} %copy-done.2), channel_id=1, source_target_pairs={{0,4},{4,8},{8,12},{1,5},{5,9},{9,13},{16,20},{20,24},{24,28},{17,... | collective-permute-start | bytes 786440 | tf_op jit(solution)/shard_map/ppermute | solution.py:569
  37.0 13.9 %collective-permute-start.11 = (bf16[2,512,128]{2,1,0:T(8,128)(2,1)}, bf16[2,512,128]{2,1,0:T(8,128)(2,1)S(1)}, u32[]{:S(2)}, u32[]{:S(2)}) collective-permute-start(bf16[2,512,128]{2,1,0:T(8,128)(2,1)} %collective-permute-done.10.refs_3_), channel_id=1, source_target_pairs={{0,4},{4,8},{8,12},{1,5},{5,9},{9,13},{16,20},{20,24},{24,28},{17,... | collective-permute-start | bytes 786440 | tf_op jit(solution)/shard_map/ppermute | solution.py:569
  39.0 16.6 %collective-permute-start.9 = (bf16[2,512,128]{2,1,0:T(8,128)(2,1)S(1)}, bf16[2,512,128]{2,1,0:T(8,128)(2,1)S(1)}, u32[]{:S(2)}, u32[]{:S(2)}) collective-permute-start(bf16[2,512,128]{2,1,0:T(8,128)(2,1)S(1)} %collective-permute-done.8.refs_3_), channel_id=1, source_target_pairs={{0,4},{4,8},{8,12},{1,5},{5,9},{9,13},{16,20},{20,24},{24,28},{17,... | collective-permute-start | bytes 786440 | tf_op jit(solution)/shard_map/ppermute | solution.py:569
  41.0 1.0 copy-start.6
  59.6 10.7 %collective-permute-start.12 = (bf16[2,16,2,16,128]{4,3,2,1,0:T(8,128)(2,1)S(1)}, bf16[2,16,2,16,128]{4,3,2,1,0:T(8,128)(2,1)S(1)}, u32[]{:S(2)}, u32[]{:S(2)}) collective-permute-start(bf16[2,16,2,16,128]{4,3,2,1,0:T(8,128)(2,1)S(1)} %get-tuple-element.50), channel_id=1, source_target_pairs={{0,1},{1,0},{2,3},{3,2},{4,5},{5,4},{6,7},{7,6},{8,9},{9,8},{10,11... | collective-permute-start | bytes 786440 | tf_op jit(solution)/shard_map/ppermute | solution.py:587
  61.2 9.3 %collective-permute-start.13 = (bf16[2,16,2,16,128]{4,3,2,1,0:T(8,128)(2,1)S(1)}, bf16[2,16,2,16,128]{4,3,2,1,0:T(8,128)(2,1)S(1)}, u32[]{:S(2)}, u32[]{:S(2)}) collective-permute-start(bf16[2,16,2,16,128]{4,3,2,1,0:T(8,128)(2,1)S(1)} %get-tuple-element.51), channel_id=1, source_target_pairs={{0,2},{1,3},{2,0},{3,1},{4,6},{5,7},{6,4},{7,5},{8,10},{9,11},{10,... | collective-permute-start | bytes 786440 | tf_op jit(solution)/shard_map/ppermute | solution.py:587
  61.2 14.9 %collective-permute-start.14 = (bf16[2,16,2,16,128]{4,3,2,1,0:T(8,128)(2,1)S(1)}, bf16[2,16,2,16,128]{4,3,2,1,0:T(8,128)(2,1)S(1)}, u32[]{:S(2)}, u32[]{:S(2)}) collective-permute-start(bf16[2,16,2,16,128]{4,3,2,1,0:T(8,128)(2,1)S(1)} %get-tuple-element.52), channel_id=1, source_target_pairs={{0,3},{1,2},{2,1},{3,0},{4,7},{5,6},{6,5},{7,4},{8,11},{9,10},{10,... | collective-permute-start | bytes 786440 | tf_op jit(solution)/shard_map/ppermute | solution.py:587
  63.2 13.0 %collective-permute-start.22 = (bf16[2,16,2,16,128]{4,3,2,1,0:T(8,128)(2,1)S(1)}, bf16[2,16,2,16,128]{4,3,2,1,0:T(8,128)(2,1)S(1)}, u32[]{:S(2)}, u32[]{:S(2)}) collective-permute-start(bf16[2,16,2,16,128]{4,3,2,1,0:T(8,128)(2,1)S(1)} %get-tuple-element.49.refs_5_), channel_id=1, source_target_pairs={{0,16},{16,0},{1,17},{17,1},{2,18},{18,2},{3,19},{19,3},{4,20},{20... | collective-permute-start | bytes 786440 | tf_op jit(solution)/shard_map/ppermute | solution.py:589
  63.2 16.9 %collective-permute-start.5 = (bf16[2,16,2,16,128]{4,3,2,1,0:T(8,128)(2,1)S(1)}, bf16[2,16,2,16,128]{4,3,2,1,0:T(8,128)(2,1)S(1)}, u32[]{:S(2)}, u32[]{:S(2)}) collective-permute-start(bf16[2,16,2,16,128]{4,3,2,1,0:T(8,128)(2,1)S(1)} %get-tuple-element.40), channel_id=1, source_target_pairs={{0,1},{1,0},{2,3},{3,2},{4,5},{5,4},{6,7},{7,6},{8,9},{9,8},{10,11... | collective-permute-start | bytes 786440 | tf_op jit(solution)/shard_map/ppermute | solution.py:587
  70.4 10.4 %collective-permute-start.6 = (bf16[2,16,2,16,128]{4,3,2,1,0:T(8,128)(2,1)S(1)}, bf16[2,16,2,16,128]{4,3,2,1,0:T(8,128)(2,1)S(1)}, u32[]{:S(2)}, u32[]{:S(2)}) collective-permute-start(bf16[2,16,2,16,128]{4,3,2,1,0:T(8,128)(2,1)S(1)} %get-tuple-element.41), channel_id=1, source_target_pairs={{0,2},{1,3},{2,0},{3,1},{4,6},{5,7},{6,4},{7,5},{8,10},{9,11},{10,... | collective-permute-start | bytes 786440 | tf_op jit(solution)/shard_map/ppermute | solution.py:587
  70.5 13.0 %collective-permute-start.7 = (bf16[2,16,2,16,128]{4,3,2,1,0:T(8,128)(2,1)S(1)}, bf16[2,16,2,16,128]{4,3,2,1,0:T(8,128)(2,1)S(1)}, u32[]{:S(2)}, u32[]{:S(2)}) collective-permute-start(bf16[2,16,2,16,128]{4,3,2,1,0:T(8,128)(2,1)S(1)} %get-tuple-element.42), channel_id=1, source_target_pairs={{0,3},{1,2},{2,1},{3,0},{4,7},{5,6},{6,5},{7,4},{8,11},{9,10},{10,... | collective-permute-start | bytes 786440 | tf_op jit(solution)/shard_map/ppermute | solution.py:587
  76.1 7.4 %collective-permute-start.18 = (bf16[2,16,2,16,128]{4,3,2,1,0:T(8,128)(2,1)S(1)}, bf16[2,16,2,16,128]{4,3,2,1,0:T(8,128)(2,1)S(1)}, u32[]{:S(2)}, u32[]{:S(2)}) collective-permute-start(bf16[2,16,2,16,128]{4,3,2,1,0:T(8,128)(2,1)S(1)} %get-tuple-element.39.refs_5_.refs_1_), channel_id=1, source_target_pairs={{0,16},{16,0},{1,17},{17,1},{2,18},{18,2},{3,19},{19,3},{4,20},{20... | collective-permute-start | bytes 786440 | tf_op jit(solution)/shard_map/ppermute | solution.py:589
  76.1 7.9 %collective-permute-start.23 = (bf16[2,16,2,16,128]{4,3,2,1,0:T(8,128)(2,1)S(1)}, bf16[2,16,2,16,128]{4,3,2,1,0:T(8,128)(2,1)S(1)}, u32[]{:S(2)}, u32[]{:S(2)}) collective-permute-start(bf16[2,16,2,16,128]{4,3,2,1,0:T(8,128)(2,1)S(1)} %collective-permute-done.12.refs_6_), channel_id=1, source_target_pairs={{0,16},{16,0},{1,17},{17,1},{2,18},{18,2},{3,19},{19,3},{4,20},{20... | collective-permute-start | bytes 786440 | tf_op jit(solution)/shard_map/ppermute | solution.py:589
  80.1 11.7 %collective-permute-start.24 = (bf16[2,16,2,16,128]{4,3,2,1,0:T(8,128)(2,1)S(1)}, bf16[2,16,2,16,128]{4,3,2,1,0:T(8,128)(2,1)S(1)}, u32[]{:S(2)}, u32[]{:S(2)}) collective-permute-start(bf16[2,16,2,16,128]{4,3,2,1,0:T(8,128)(2,1)S(1)} %collective-permute-done.13.refs_7_), channel_id=1, source_target_pairs={{0,16},{16,0},{1,17},{17,1},{2,18},{18,2},{3,19},{19,3},{4,20},{20... | collective-permute-start | bytes 786440 | tf_op jit(solution)/shard_map/ppermute | solution.py:589
  80.7 12.7 %collective-permute-start.25 = (bf16[2,16,2,16,128]{4,3,2,1,0:T(8,128)(2,1)S(1)}, bf16[2,16,2,16,128]{4,3,2,1,0:T(8,128)(2,1)S(1)}, u32[]{:S(2)}, u32[]{:S(2)}) collective-permute-start(bf16[2,16,2,16,128]{4,3,2,1,0:T(8,128)(2,1)S(1)} %collective-permute-done.14.refs_8_), channel_id=1, source_target_pairs={{0,16},{16,0},{1,17},{17,1},{2,18},{18,2},{3,19},{19,3},{4,20},{20... | collective-permute-start | bytes 786440 | tf_op jit(solution)/shard_map/ppermute | solution.py:589
  83.5 10.0 %collective-permute-start.19 = (bf16[2,16,2,16,128]{4,3,2,1,0:T(8,128)(2,1)S(1)}, bf16[2,16,2,16,128]{4,3,2,1,0:T(8,128)(2,1)S(1)}, u32[]{:S(2)}, u32[]{:S(2)}) collective-permute-start(bf16[2,16,2,16,128]{4,3,2,1,0:T(8,128)(2,1)S(1)} %collective-permute-done.5.refs_2_), channel_id=1, source_target_pairs={{0,16},{16,0},{1,17},{17,1},{2,18},{18,2},{3,19},{19,3},{4,20},{20... | collective-permute-start | bytes 786440 | tf_op jit(solution)/shard_map/ppermute | solution.py:589
  83.5 10.0 %collective-permute-start.20 = (bf16[2,16,2,16,128]{4,3,2,1,0:T(8,128)(2,1)S(1)}, bf16[2,16,2,16,128]{4,3,2,1,0:T(8,128)(2,1)S(1)}, u32[]{:S(2)}, u32[]{:S(2)}) collective-permute-start(bf16[2,16,2,16,128]{4,3,2,1,0:T(8,128)(2,1)S(1)} %collective-permute-done.6.refs_3_), channel_id=1, source_target_pairs={{0,16},{16,0},{1,17},{17,1},{2,18},{18,2},{3,19},{19,3},{4,20},{20... | collective-permute-start | bytes 786440 | tf_op jit(solution)/shard_map/ppermute | solution.py:589
  84.0 9.5 %collective-permute-start.21 = (bf16[2,16,2,16,128]{4,3,2,1,0:T(8,128)(2,1)S(1)}, bf16[2,16,2,16,128]{4,3,2,1,0:T(8,128)(2,1)S(1)}, u32[]{:S(2)}, u32[]{:S(2)}) collective-permute-start(bf16[2,16,2,16,128]{4,3,2,1,0:T(8,128)(2,1)S(1)} %collective-permute-done.7.refs_4_), channel_id=1, source_target_pairs={{0,16},{16,0},{1,17},{17,1},{2,18},{18,2},{3,19},{19,3},{4,20},{20... | collective-permute-start | bytes 786440 | tf_op jit(solution)/shard_map/ppermute | solution.py:589
  91.9 15.3 %collective-permute-start.15 = (bf16[544,128]{1,0:T(8,128)(2,1)S(1)}, bf16[544,128]{1,0:T(8,128)(2,1)S(1)}, u32[]{:S(2)}, u32[]{:S(2)}) collective-permute-start(bf16[544,128]{1,0:T(8,128)(2,1)S(1)} %get-tuple-element.54), channel_id=1, source_target_pairs={{0,4},{2,6},{4,8},{6,10},{8,12},{10,14},{12,0},{14,2},{1,5},{3,7},... | collective-permute-start | bytes 417800 | tf_op jit(solution)/shard_map/ppermute | solution.py:605
  93.4 13.7 %collective-permute-start.16 = (bf16[544,128]{1,0:T(8,128)(2,1)S(1)}, bf16[544,128]{1,0:T(8,128)(2,1)S(1)}, u32[]{:S(2)}, u32[]{:S(2)}) collective-permute-start(bf16[544,128]{1,0:T(8,128)(2,1)S(1)} %get-tuple-element.55), channel_id=1, source_target_pairs={{0,8},{2,10},{4,12},{6,14},{8,0},{10,2},{12,4},{14,6},{1,9},{3,11}... | collective-permute-start | bytes 417800 | tf_op jit(solution)/shard_map/ppermute | solution.py:605
  101.2 8.3 %collective-permute-start.26 = (bf16[512,128]{1,0:T(8,128)(2,1)S(1)}, bf16[512,128]{1,0:T(8,128)(2,1)S(1)}, u32[]{:S(2)}, u32[]{:S(2)}) collective-permute-start(bf16[512,128]{1,0:T(8,128)(2,1)S(1)} %get-tuple-element.58), channel_id=1, source_target_pairs={{0,4},{2,6},{4,8},{6,10},{8,12},{10,14},{12,0},{14,2},{1,5},{3,7},... | collective-permute-start | bytes 393224 | tf_op jit(solution)/shard_map/ppermute | solution.py:609
  104.1 10.3 %collective-permute-start.27 = (bf16[512,128]{1,0:T(8,128)(2,1)S(1)}, bf16[512,128]{1,0:T(8,128)(2,1)S(1)}, u32[]{:S(2)}, u32[]{:S(2)}) collective-permute-start(bf16[512,128]{1,0:T(8,128)(2,1)S(1)} %get-tuple-element.59), channel_id=1, source_target_pairs={{0,8},{2,10},{4,12},{6,14},{8,0},{10,2},{12,4},{14,6},{1,9},{3,11}... | collective-permute-start | bytes 393224 | tf_op jit(solution)/shard_map/ppermute | solution.py:609
  104.5 9.9 %collective-permute-start.28 = (bf16[512,128]{1,0:T(8,128)(2,1)S(1)}, bf16[512,128]{1,0:T(8,128)(2,1)S(1)}, u32[]{:S(2)}, u32[]{:S(2)}) collective-permute-start(bf16[512,128]{1,0:T(8,128)(2,1)S(1)} %get-tuple-element.60), channel_id=1, source_target_pairs={{0,12},{2,14},{4,0},{6,2},{8,4},{10,6},{12,8},{14,10},{1,13},{3,15... | collective-permute-start | bytes 393224 | tf_op jit(solution)/shard_map/ppermute | solution.py:609
  107.1 10.1 %collective-permute-start.29 = (f32[512,128]{1,0:T(8,128)S(1)}, f32[512,128]{1,0:T(8,128)S(1)}, u32[]{:S(2)}, u32[]{:S(2)}) collective-permute-start(f32[512,128]{1,0:T(8,128)S(1)} %get-tuple-element.57.refs_5_), channel_id=1, source_target_pairs={{0,16},{16,0},{1,17},{17,1},{2,18},{18,2},{3,19},{19,3},{4,20},{20... | collective-permute-start | bytes 786440 | tf_op jit(solution)/shard_map/ppermute | solution.py:610
  107.1 10.1 %collective-permute-start.17 = (bf16[544,128]{1,0:T(8,128)(2,1)S(1)}, bf16[544,128]{1,0:T(8,128)(2,1)S(1)}, u32[]{:S(2)}, u32[]{:S(2)}) collective-permute-start(bf16[544,128]{1,0:T(8,128)(2,1)S(1)} %get-tuple-element.56), channel_id=1, source_target_pairs={{0,12},{2,14},{4,0},{6,2},{8,4},{10,6},{12,8},{14,10},{1,13},{3,15... | collective-permute-start | bytes 417800 | tf_op jit(solution)/shard_map/ppermute | solution.py:605
  109.5 7.7 %collective-permute-start.30 = (bf16[512,128]{1,0:T(8,128)(2,1)S(1)}, bf16[512,128]{1,0:T(8,128)(2,1)S(1)}, u32[]{:S(2)}, u32[]{:S(2)}) collective-permute-start(bf16[512,128]{1,0:T(8,128)(2,1)S(1)} %collective-permute-done.26.refs_6_), channel_id=1, source_target_pairs={{0,16},{16,0},{1,17},{17,1},{2,18},{18,2},{3,19},{19,3},{4,20},{20... | collective-permute-start | bytes 393224 | tf_op jit(solution)/shard_map/ppermute | solution.py:610
  114.4 2.9 %collective-permute-start.31 = (bf16[512,128]{1,0:T(8,128)(2,1)S(1)}, bf16[512,128]{1,0:T(8,128)(2,1)S(1)}, u32[]{:S(2)}, u32[]{:S(2)}) collective-permute-start(bf16[512,128]{1,0:T(8,128)(2,1)S(1)} %collective-permute-done.27.refs_7_), channel_id=1, source_target_pairs={{0,16},{16,0},{1,17},{17,1},{2,18},{18,2},{3,19},{19,3},{4,20},{20... | collective-permute-start | bytes 393224 | tf_op jit(solution)/shard_map/ppermute | solution.py:610
  114.4 2.8 %collective-permute-start.32 = (bf16[512,128]{1,0:T(8,128)(2,1)S(1)}, bf16[512,128]{1,0:T(8,128)(2,1)S(1)}, u32[]{:S(2)}, u32[]{:S(2)}) collective-permute-start(bf16[512,128]{1,0:T(8,128)(2,1)S(1)} %collective-permute-done.28.refs_8_), channel_id=1, source_target_pairs={{0,16},{16,0},{1,17},{17,1},{2,18},{18,2},{3,19},{19,3},{4,20},{20... | collective-permute-start | bytes 393224 | tf_op jit(solution)/shard_map/ppermute | solution.py:610

commit v5 on v4

--- a/solution.py
+++ b/solution.py
@@ -122,7 +122,7 @@
         out_specs=[VMEM] * len(shapes),
         scratch_shapes=[pltpu.VMEM((2, samples // LANES * inputs, LANES), jnp.float32)],
         compiler_params=params(16),
-        cost_estimate=cost(10**6, 4 * 2**20),
+        cost_estimate=cost(10**6, 2**18),
         name="pick",
     )(meta, block)
 
@@ -293,7 +293,7 @@
         ]
         + [pltpu.VMEM((2, (HALF + 1) * ROWS, LANES), jnp.float32)] * (PAIR * frames // HALF),
         compiler_params=params(16),
-        cost_estimate=cost(10**9, 10 * 2**20),
+        cost_estimate=cost(10**6, 2**18),
         name="filterbank",
     )(meta, keep, halo_own, recv, halo_far, after, *tables, *earlier)
 
@@ -437,7 +437,7 @@
             pltpu.VMEM((2, TILE * TILE, outer * span, LANES), jnp.float32),
         ],
         compiler_params=params(14 + inputs * steps * 4 * size * LANES * 4 // 2**20),
-        cost_estimate=cost(10**9, 22 * 2**20),
+        cost_estimate=cost(10**6, 2**18),
         name=name,
     )(meta, *arrays)
 
@@ -512,7 +512,7 @@
         out_specs=VMEM,
         scratch_shapes=[pltpu.VMEM((own * 2 * own * span, LANES), jnp.float32)],
         compiler_params=params(24),
-        cost_estimate=cost(10**8, 8 * 2**20),
+        cost_estimate=cost(10**6, 2**18),
         name="assemble",
     )(meta, *mine_in, *mine_across, *far_across)
 
@@ -560,21 +560,24 @@
     tables = [jnp.asarray(t) for t in tables + [np.concatenate([base, base], axis=1)]]
 
     sends = list(pick(meta, voltages, half, False, False))
+    forward = [p for p in onward if p[0] % PAIR == 0]
     recvs = []
     for c in range(half):
-        block = sends[c] if c < 2 else follow(sends[c], recvs[c - 2])
+        block = follow(sends[c], recvs[c - 2]) if c >= 2 else sends[c]
         recvs.append(lax.ppermute(block, "tm", swap))
     keep = pick(meta, voltages, half, True, True)[0]
     halo_own = lax.ppermute(keep, "tm", [p for p in onward if p[0] % PAIR == 1])
-    fars = [lax.ppermute(block, "tm", [p for p in onward if p[0] % PAIR == 0]) for block in recvs]
 
     arrays, others, places = [], [], []
-    spectra, after = [], meta
+    spectra, done = [], []
     for c in range(half):
+        block = follow(recvs[c], done[c - 2]) if c >= 2 else recvs[c]
+        far = lax.ppermute(block, "tm", forward)
+        after = done[c - 1] if c else meta
         spectra = filterbank(
-            c, meta, keep, halo_own, recvs[c], fars[c], after, tables, spectra, len(dests)
+            c, meta, keep, halo_own, recvs[c], far, after, tables, spectra, len(dests)
         )
-        after = spectra[0]
+        done.append(spectra[0])
         if c % JOIN < JOIN - 1:
             continue
         for (dg, dc), block in zip(dests, spectra):
@@ -584,6 +587,8 @@
                     target = (i ^ dg) * per_ct + (j + dc) % per_ct
                     route.append((i * per_ct + j, target))
             if dg or dc:
+                if len(arrays) >= len(dests):
+                    block = follow(block, arrays[-len(dests)])
                 block = lax.ppermute(block, ("tm", "ct"), route)
             arrays.append(block)
             others.append(lax.ppermute(block, "stn", cores))
@@ -606,7 +611,8 @@
     for r in range(outer):
         if r:
             route = [(i, (i + r * PAIR) % tm) for i in range(tm)]
-            mine_across[r] = lax.ppermute(mine_across[r], "tm", route)
+            block = follow(mine_across[r], mine_in[r])
+            mine_across[r] = lax.ppermute(block, "tm", route)
         far_across.append(lax.ppermute(mine_across[r], "stn", cores))
     scale = 1.0 / (tm * frame_count)
     result = assemble(meta, mine_in, mine_across, far_across, own, span, scale)

time: 123 us -> 144 us (1.17)
  local copies, waits for them, and re-layouts: 6.1 us -> 35.3 us
  waiting for transfers between devices: 34.8 us -> 26.6 us
    unnamed x24 -> x112, local copies, waits for them, and re-layouts: 5.37 us -> 34.6 us
    ppermute x6, waiting for transfers between devices: 15.4 us -> 10.1 us  [fast(): block = lax.ppermute(block, ('tm', 'ct'), route)]
    ppermute x4, waiting for transfers between devices: 10 us -> 7.14 us  [fast(): recvs.append(lax.ppermute(block, 'tm', swap))]
    ppermute x7, starting transfers between devices: 16.6 us -> 19.3 us  [the longest x4 14.5 us: fast(): far = lax.ppermute(block, 'tm', forward)]
    ppermute x3, waiting for transfers between devices: 2.34 us -> 0.01 us  [fast(): mine_in[r] = lax.ppermute(mine_in[r], 'tm', route)]
  transfers between devices with their start and end apart: 33 -> 33, of which waited for: 13 -> 7; matrix products, arithmetic and copies ran while one was open for 0% -> 1% of each run, Pallas kernels for 25% -> 25%
where the time goes in v5:
time: 144 us; the launch traced here: 143 us
  Pallas kernels  40.9 us (28%)
  starting transfers between devices  40 us (28%)
  local copies, waits for them, and re-layouts  35.3 us (25%)
  waiting for transfers between devices  26.6 us (18%)
    unnamed x112, local copies, waits for them, and re-layouts  34.6 us
    pallas_call x4, Pallas kernels, filterbank(): pl.pallas_call(functools.partial(filterbank_kernel, index, before, frames...  17.8 us
    pallas_call x2, Pallas kernels, correlate(): pl.pallas_call(functools.partial(correlate_kernel, layout), out_shape=sha...  15.9 us
    ppermute x4, starting transfers between devices, fast(): far = lax.ppermute(block, 'tm', forward)  14.5 us
    ppermute x6, waiting for transfers between devices, fast(): block = lax.ppermute(block, ('tm', 'ct'), route)  10.1 us
    ppermute x4, starting transfers between devices, fast(): recvs.append(lax.ppermute(block, 'tm', swap))  8.61 us
    ppermute x3, waiting for transfers between devices, fast(): mine_across[r] = lax.ppermute(block, 'tm', route)  8.3 us
    ppermute x4, waiting for transfers between devices, fast(): recvs.append(lax.ppermute(block, 'tm', swap))  7.14 us
  transfers between devices with their start and end apart: 33, of which 7 were waited for; matrix products, arithmetic and copies ran while one was open for 1% of the time, Pallas kernels for 25%

profile of v5, /device:TPU:0, one launch (start us, length us, event | category | flops | bytes accessed | tf_op | source)
XLA Modules:
  0.0 143.2 jit_solution(14234686221012630903)
XLA Ops:
  0.0 0.7 concatenate.3.meta.refs_0_.refs_5_
  0.7 1.6 %copy-done = bf16[2,8,65536]{2,1,0:T(8,128)(2,1)S(1)} copy-done((bf16[2,8,65536]{2,1,0:T(8,128)(2,1)S(1)}, bf16[2,8,65536]{2,1,0:T(8,128)(2,1)}, u32[]{:S(2)}) %copy-start) | copy-done | bytes 2097176
  2.3 1.7 %pick.2.refs_1_ = bf16[4,2,512,128]{3,2,1,0:T(8,128)(2,1)S(1)} custom-call(s32[12]{0:T(128)S(1)} %concatenate.3.meta.refs_0_.refs_5_, bf16[2,8,65536]{2,1,0:T(8,128)(2,1)S(1)} %copy-done), custom_call_target="tpu_custom_call" | custom-call | flops 1000000 | bytes 262144 | tf_op jit(solution)/shard_map/pick/pallas_call | solution.py:118
  4.1 0.9 collective-permute-start
  5.0 1.7 %pick.3 = (bf16[2,512,128]{2,1,0:T(8,128)(2,1)S(1)}, bf16[2,512,128]{2,1,0:T(8,128)(2,1)S(1)}, bf16[2,512,128]{2,1,0:T(8,128)(2,1)S(1)}, bf16[2,512,128]{2,1,0:T(8,128)(2,1)S(1)}) custom-call(s32[12]{0:T(128)S(1)} %concatenate.3.meta.refs_0_.refs_5_, bf16[2,8,65536]{2,1,0:T(8,128)(2,1)S(1)} %copy-done), custom_call_target="tpu_custom_call" | custom-call | flops 1000000 | bytes 262144 | tf_op jit(solution)/shard_map/pick/pallas_call | solution.py:118
  8.1 5.8 %collective-permute-start.3 = (bf16[2,512,128]{2,1,0:T(8,128)(2,1)S(1)}, bf16[2,512,128]{2,1,0:T(8,128)(2,1)S(1)}, u32[]{:S(2)}, u32[]{:S(2)}) collective-permute-start(bf16[2,512,128]{2,1,0:T(8,128)(2,1)S(1)} %get-tuple-element.34), channel_id=1, source_target_pairs={{0,2},{2,0},{4,6},{6,4},{8,10},{10,8},{12,14},{14,12},{1,3},{3,1},... | collective-permute-start | bytes 786440 | tf_op jit(solution)/shard_map/ppermute | solution.py:567
  13.9 7.1 %collective-permute-done.3.refs_3_.after = bf16[2,512,128]{2,1,0:T(8,128)(2,1)S(1)} collective-permute-done((bf16[2,512,128]{2,1,0:T(8,128)(2,1)S(1)}, bf16[2,512,128]{2,1,0:T(8,128)(2,1)S(1)}, u32[]{:S(2)}, u32[]{:S(2)}) %collective-permute-start.3) | collective-permute-done | bytes 262176 | tf_op jit(solution)/shard_map/ppermute | solution.py:567
  21.7 2.1 %collective-permute-start.10 = (bf16[2,512,128]{2,1,0:T(8,128)(2,1)}, bf16[2,512,128]{2,1,0:T(8,128)(2,1)S(1)}, u32[]{:S(2)}, u32[]{:S(2)}) collective-permute-start(bf16[2,512,128]{2,1,0:T(8,128)(2,1)} %follow.12), channel_id=1, source_target_pairs={{0,2},{2,0},{4,6},{6,4},{8,10},{10,8},{12,14},{14,12},{1,3},{3,1},... | collective-permute-start | bytes 786440 | tf_op jit(solution)/shard_map/ppermute | solution.py:567
  23.8 4.1 %collective-permute-start.4 = (bf16[2,512,128]{2,1,0:T(8,128)(2,1)}, bf16[2,512,128]{2,1,0:T(8,128)(2,1)}, u32[]{:S(2)}, u32[]{:S(2)}) collective-permute-start(bf16[2,512,128]{2,1,0:T(8,128)(2,1)} %copy-done.21), channel_id=1, source_target_pairs={{0,4},{4,8},{8,12},{1,5},{5,9},{9,13},{16,20},{20,24},{24,28},{17,... | collective-permute-start | bytes 786440 | tf_op jit(solution)/shard_map/ppermute | solution.py:575
  28.6 0.8 collective-permute-start.8
  29.4 4.1 %collective-permute-start.2 = (bf16[2,512,128]{2,1,0:T(8,128)(2,1)}, bf16[2,512,128]{2,1,0:T(8,128)(2,1)}, u32[]{:S(2)}, u32[]{:S(2)}) collective-permute-start(bf16[2,512,128]{2,1,0:T(8,128)(2,1)} %copy-done.19), channel_id=1, source_target_pairs={{0,4},{4,8},{8,12},{1,5},{5,9},{9,13},{16,20},{20,24},{24,28},{17,... | collective-permute-start | bytes 786440 | tf_op jit(solution)/shard_map/ppermute | solution.py:575
  33.5 0.7 copy.21.block
  34.3 1.0 copy-done.22
  35.3 0.8 copy-done.35
  36.1 4.6 %filterbank.4 = (bf16[1,16,2,16,128]{4,3,2,1,0:T(8,128)(2,1)S(1)}, bf16[1,16,2,16,128]{4,3,2,1,0:T(8,128)(2,1)S(1)}, bf16[1,16,2,16,128]{4,3,2,1,0:T(8,128)(2,1)S(1)}, bf16[1,16,2,16,128]{4,3,2,1,0:T(8,128)(2,1)S(1)}) custom-call(s32[12]{0:T(128)S(1)} %concatenate.3.meta.refs_0_.refs_5_, bf16[4,2,512,128]{3,2,1,0:T(8,128)(2,1)S(1)} %pick.2.refs_1_, ...), custom_call_target="tpu_custom_call" | custom-call | flops 1000000 | bytes 262144 | tf_op jit(solution)/shard_map/filterbank/pallas_call | solution.py:281
  43.3 3.5 %collective-permute-start.11 = (bf16[2,512,128]{2,1,0:T(8,128)(2,1)}, bf16[2,512,128]{2,1,0:T(8,128)(2,1)}, u32[]{:S(2)}, u32[]{:S(2)}) collective-permute-start(bf16[2,512,128]{2,1,0:T(8,128)(2,1)} %follow.13), channel_id=1, source_target_pairs={{0,4},{4,8},{8,12},{1,5},{5,9},{9,13},{16,20},{20,24},{24,28},{17,... | collective-permute-start | bytes 786440 | tf_op jit(solution)/shard_map/ppermute | solution.py:575
  47.5 0.9 copy-done.15
  48.4 0.8 copy-done.36
  49.2 0.9 copy-done.46
  50.1 0.9 copy-done.48
  51.0 0.9 copy-done.50
  51.9 4.6 %filterbank.5 = (bf16[2,16,2,16,128]{4,3,2,1,0:T(8,128)(2,1)S(1)}, bf16[2,16,2,16,128]{4,3,2,1,0:T(8,128)(2,1)S(1)}, bf16[2,16,2,16,128]{4,3,2,1,0:T(8,128)(2,1)S(1)}, bf16[2,16,2,16,128]{4,3,2,1,0:T(8,128)(2,1)S(1)}) custom-call(s32[12]{0:T(128)S(1)} %concatenate.3.meta.refs_0_.refs_5_, bf16[4,2,512,128]{3,2,1,0:T(8,128)(2,1)S(1)} %pick.2.refs_1_, ...), custom_call_target="tpu_custom_call" | custom-call | flops 1000000 | bytes 262144 | tf_op jit(solution)/shard_map/filterbank/pallas_call | solution.py:281
  59.4 2.7 %collective-permute-start.9 = (bf16[2,512,128]{2,1,0:T(8,128)(2,1)}, bf16[2,512,128]{2,1,0:T(8,128)(2,1)S(1)}, u32[]{:S(2)}, u32[]{:S(2)}) collective-permute-start(bf16[2,512,128]{2,1,0:T(8,128)(2,1)} %follow.11), channel_id=1, source_target_pairs={{0,4},{4,8},{8,12},{1,5},{5,9},{9,13},{16,20},{20,24},{24,28},{17,... | collective-permute-start | bytes 786440 | tf_op jit(solution)/shard_map/ppermute | solution.py:575
  62.2 3.0 %collective-permute-start.6 = (bf16[2,16,2,16,128]{4,3,2,1,0:T(8,128)(2,1)}, bf16[2,16,2,16,128]{4,3,2,1,0:T(8,128)(2,1)S(1)}, u32[]{:S(2)}, u32[]{:S(2)}) collective-permute-start(bf16[2,16,2,16,128]{4,3,2,1,0:T(8,128)(2,1)} %copy-done.53), channel_id=1, source_target_pairs={{0,2},{1,3},{2,0},{3,1},{4,6},{5,7},{6,4},{7,5},{8,10},{9,11},{10,... | collective-permute-start | bytes 786440 | tf_op jit(solution)/shard_map/ppermute | solution.py:592
  65.6 0.9 copy-done.3
  66.6 0.9 copy-done.26
  67.5 0.8 copy-done.37
  68.3 4.6 %filterbank.6 = (bf16[1,16,2,16,128]{4,3,2,1,0:T(8,128)(2,1)S(1)}, bf16[1,16,2,16,128]{4,3,2,1,0:T(8,128)(2,1)S(1)}, bf16[1,16,2,16,128]{4,3,2,1,0:T(8,128)(2,1)S(1)}, bf16[1,16,2,16,128]{4,3,2,1,0:T(8,128)(2,1)S(1)}) custom-call(s32[12]{0:T(128)S(1)} %concatenate.3.meta.refs_0_.refs_5_, bf16[4,2,512,128]{3,2,1,0:T(8,128)(2,1)S(1)} %pick.2.refs_1_, ...), custom_call_target="tpu_custom_call" | custom-call | flops 1000000 | bytes 262144 | tf_op jit(solution)/shard_map/filterbank/pallas_call | solution.py:281
  72.9 4.1 %filterbank.7 = (bf16[2,16,2,16,128]{4,3,2,1,0:T(8,128)(2,1)S(1)}, bf16[2,16,2,16,128]{4,3,2,1,0:T(8,128)(2,1)S(1)}, bf16[2,16,2,16,128]{4,3,2,1,0:T(8,128)(2,1)S(1)}, bf16[2,16,2,16,128]{4,3,2,1,0:T(8,128)(2,1)S(1)}) custom-call(s32[12]{0:T(128)S(1)} %concatenate.3.meta.refs_0_.refs_5_, bf16[4,2,512,128]{3,2,1,0:T(8,128)(2,1)S(1)} %pick.2.refs_1_, ...), custom_call_target="tpu_custom_call" | custom-call | flops 1000000 | bytes 262144 | tf_op jit(solution)/shard_map/filterbank/pallas_call | solution.py:281
  81.5 2.8 %collective-permute-start.13 = (bf16[2,16,2,16,128]{4,3,2,1,0:T(8,128)(2,1)}, bf16[2,16,2,16,128]{4,3,2,1,0:T(8,128)(2,1)S(1)}, u32[]{:S(2)}, u32[]{:S(2)}) collective-permute-start(bf16[2,16,2,16,128]{4,3,2,1,0:T(8,128)(2,1)} %follow.15), channel_id=1, source_target_pairs={{0,2},{1,3},{2,0},{3,1},{4,6},{5,7},{6,4},{7,5},{8,10},{9,11},{10,... | collective-permute-start | bytes 786440 | tf_op jit(solution)/shard_map/ppermute | solution.py:592
  84.2 0.7 copy-done.11
  86.0 4.8 %collective-permute-done.14.refs_8_ = bf16[2,16,2,16,128]{4,3,2,1,0:T(8,128)(2,1)S(1)} collective-permute-done((bf16[2,16,2,16,128]{4,3,2,1,0:T(8,128)(2,1)}, bf16[2,16,2,16,128]{4,3,2,1,0:T(8,128)(2,1)S(1)}, u32[]{:S(2)}, u32[]{:S(2)}) %collective-permute-start.14) | collective-permute-done | bytes 262176 | tf_op jit(solution)/shard_map/ppermute | solution.py:592
  90.8 5.3 %collective-permute-done.13.refs_7_ = bf16[2,16,2,16,128]{4,3,2,1,0:T(8,128)(2,1)S(1)} collective-permute-done((bf16[2,16,2,16,128]{4,3,2,1,0:T(8,128)(2,1)}, bf16[2,16,2,16,128]{4,3,2,1,0:T(8,128)(2,1)S(1)}, u32[]{:S(2)}, u32[]{:S(2)}) %collective-permute-start.13) | collective-permute-done | bytes 262176 | tf_op jit(solution)/shard_map/ppermute | solution.py:592
  97.1 0.9 copy-done.6
  98.1 0.9 copy-done.9
  99.0 0.9 copy-done.12
  100.0 7.8 %correlate_own.1 = (f32[544,128]{1,0:T(8,128)S(1)}, bf16[544,128]{1,0:T(8,128)(2,1)S(1)}, bf16[544,128]{1,0:T(8,128)(2,1)S(1)}, bf16[544,128]{1,0:T(8,128)(2,1)S(1)}) custom-call(s32[12]{0:T(128)S(1)} %concatenate.3.meta.refs_0_.refs_5_, bf16[2,16,2,16,128]{4,3,2,1,0:T(8,128)(2,1)S(1)} %copy-done.4, bf16[2,16,2,16,128]{4,3,2,1,0:T(8,128)(2,1)S(1)} %copy-done.12, ...), custom_call_target="tpu_custom_call" | custom-call | flops 1000000 | bytes 262144 | tf_op jit(solution)/shard_map/correlate_own/pallas_call | solution.py:429
  107.9 1.4 %collective-permute-start.16 = (bf16[544,128]{1,0:T(8,128)(2,1)S(1)}, bf16[544,128]{1,0:T(8,128)(2,1)S(1)}, u32[]{:S(2)}, u32[]{:S(2)}) collective-permute-start(bf16[544,128]{1,0:T(8,128)(2,1)S(1)} %get-tuple-element.55), channel_id=1, source_target_pairs={{0,8},{2,10},{4,12},{6,14},{8,0},{10,2},{12,4},{14,6},{1,9},{3,11}... | collective-permute-start | bytes 417800 | tf_op jit(solution)/shard_map/ppermute | solution.py:610
  110.0 8.1 %correlate_cross.1 = (f32[512,128]{1,0:T(8,128)S(1)}, bf16[512,128]{1,0:T(8,128)(2,1)S(1)}, bf16[512,128]{1,0:T(8,128)(2,1)S(1)}, bf16[512,128]{1,0:T(8,128)(2,1)S(1)}) custom-call(s32[12]{0:T(128)S(1)} %concatenate.3.meta.refs_0_.refs_5_, bf16[2,16,2,16,128]{4,3,2,1,0:T(8,128)(2,1)S(1)} %copy-done.4, bf16[2,16,2,16,128]{4,3,2,1,0:T(8,128)(2,1)S(1)} %copy-done.13, ...), custom_call_target="tpu_custom_call" | custom-call | flops 1000000 | bytes 262144 | tf_op jit(solution)/shard_map/correlate_cross/pallas_call | solution.py:429
  120.7 3.2 %collective-permute-start.28 = (bf16[512,128]{1,0:T(8,128)(2,1)}, bf16[512,128]{1,0:T(8,128)(2,1)S(1)}, u32[]{:S(2)}, u32[]{:S(2)}) collective-permute-start(bf16[512,128]{1,0:T(8,128)(2,1)} %follow.19), channel_id=1, source_target_pairs={{0,12},{2,14},{4,0},{6,2},{8,4},{10,6},{12,8},{14,10},{1,13},{3,15... | collective-permute-start | bytes 393224 | tf_op jit(solution)/shard_map/ppermute | solution.py:615
  125.3 1.7 %collective-permute-start.26 = (bf16[512,128]{1,0:T(8,128)(2,1)}, bf16[512,128]{1,0:T(8,128)(2,1)S(1)}, u32[]{:S(2)}, u32[]{:S(2)}) collective-permute-start(bf16[512,128]{1,0:T(8,128)(2,1)} %follow.17), channel_id=1, source_target_pairs={{0,4},{2,6},{4,8},{6,10},{8,12},{10,14},{12,0},{14,2},{1,5},{3,7},... | collective-permute-start | bytes 393224 | tf_op jit(solution)/shard_map/ppermute | solution.py:615
  127.0 0.9 collective-permute-done.28.refs_8_
  127.9 7.4 %collective-permute-done.27.refs_7_ = bf16[512,128]{1,0:T(8,128)(2,1)S(1)} collective-permute-done((bf16[512,128]{1,0:T(8,128)(2,1)}, bf16[512,128]{1,0:T(8,128)(2,1)S(1)}, u32[]{:S(2)}, u32[]{:S(2)}) %collective-permute-start.27) | collective-permute-done | bytes 131104 | tf_op jit(solution)/shard_map/ppermute | solution.py:615
  135.8 0.8 collective-permute-done.31.refs_11_
  136.8 0.9 copy-done.28
  137.7 0.9 copy-done.30
  138.6 0.9 copy-done.32
  139.5 3.7 %assemble.1 = f32[2,16,32,256]{3,2,1,0:T(8,128)} custom-call(s32[12]{0:T(128)S(1)} %concatenate.3.meta.refs_0_.refs_5_, f32[544,128]{1,0:T(8,128)S(1)} %get-tuple-element.53.refs_1_, bf16[544,128]{1,0:T(8,128)(2,1)S(1)} %copy-done.32, bf16[544,128]{1,0:T(8,128)(2,1)S(1)} %copy-done.30, bf16[544,128]{1,0:T(8,128)(2,1)S(1)} %copy-done.28, ...), custom_call_target="tpu_custom_call" | custom-call | flops 1000000 | bytes 262144 | tf_op jit(solution)/shard_map/assemble/pallas_call | solution.py:508
  (150 shorter events, 21.6 us)
Async XLA Ops:
  0.7 1.6 %copy-start = (bf16[2,8,65536]{2,1,0:T(8,128)(2,1)S(1)}, bf16[2,8,65536]{2,1,0:T(8,128)(2,1)}, u32[]{:S(2)}) copy-start(bf16[2,8,65536]{2,1,0:T(8,128)(2,1)} %block.3) | copy-start | bytes 6291460
  4.0 30.2 %copy-start.1 = (f32[16,64,128]{2,1,0:T(8,128)S(1)}, f32[16,64,128]{2,1,0:T(8,128)}, u32[]{:S(2)}) copy-start(f32[16,64,128]{2,1,0:T(8,128)} %constant.46.clone.refs_6_) | copy-start | bytes 1572868
  4.0 30.2 %copy-start.16 = (bf16[2,4,32,128]{3,2,1,0:T(8,128)(2,1)S(1)}, bf16[2,4,32,128]{3,2,1,0:T(8,128)(2,1)}, u32[]{:S(2)}) copy-start(bf16[2,4,32,128]{3,2,1,0:T(8,128)(2,1)} %constant.50.clone.refs_10_) | copy-start | bytes 196612
  4.1 30.2 %copy-start.33 = (bf16[128,128]{1,0:T(8,128)(2,1)S(1)}, bf16[128,128]{1,0:T(8,128)(2,1)}, u32[]{:S(2)}) copy-start(bf16[128,128]{1,0:T(8,128)(2,1)} %constant.47.clone.refs_7_) | copy-start | bytes 98308
  4.1 30.2 %copy-start.34 = (f32[64,128]{1,0:T(8,128)S(1)}, f32[64,128]{1,0:T(8,128)}, u32[]{:S(2)}) copy-start(f32[64,128]{1,0:T(8,128)} %constant.48.clone.refs_8_) | copy-start | bytes 98308
  4.1 30.2 %collective-permute-start = (bf16[4,2,512,128]{3,2,1,0:T(8,128)(2,1)S(1)}, bf16[4,2,512,128]{3,2,1,0:T(8,128)(2,1)S(1)}, u32[]{:S(2)}, u32[]{:S(2)}) collective-permute-start(bf16[4,2,512,128]{3,2,1,0:T(8,128)(2,1)S(1)} %pick.2.refs_1_), channel_id=1, source_target_pairs={{2,6},{6,10},{10,14},{3,7},{7,11},{11,15},{18,22},{22,26},{26,30},... | collective-permute-start | bytes 3145736 | tf_op jit(solution)/shard_map/ppermute | solution.py:569
  8.1 12.9 %collective-permute-start.3 = (bf16[2,512,128]{2,1,0:T(8,128)(2,1)S(1)}, bf16[2,512,128]{2,1,0:T(8,128)(2,1)S(1)}, u32[]{:S(2)}, u32[]{:S(2)}) collective-permute-start(bf16[2,512,128]{2,1,0:T(8,128)(2,1)S(1)} %get-tuple-element.34), channel_id=1, source_target_pairs={{0,2},{2,0},{4,6},{6,4},{8,10},{10,8},{12,14},{14,12},{1,3},{3,1},... | collective-permute-start | bytes 786440 | tf_op jit(solution)/shard_map/ppermute | solution.py:567
  13.8 14.1 %collective-permute-start.1 = (bf16[2,512,128]{2,1,0:T(8,128)(2,1)S(1)}, bf16[2,512,128]{2,1,0:T(8,128)(2,1)S(1)}, u32[]{:S(2)}, u32[]{:S(2)}) collective-permute-start(bf16[2,512,128]{2,1,0:T(8,128)(2,1)S(1)} %get-tuple-element.33), channel_id=1, source_target_pairs={{0,2},{2,0},{4,6},{6,4},{8,10},{10,8},{12,14},{14,12},{1,3},{3,1},... | collective-permute-start | bytes 786440 | tf_op jit(solution)/shard_map/ppermute | solution.py:567
  21.7 11.8 %collective-permute-start.10 = (bf16[2,512,128]{2,1,0:T(8,128)(2,1)}, bf16[2,512,128]{2,1,0:T(8,128)(2,1)S(1)}, u32[]{:S(2)}, u32[]{:S(2)}) collective-permute-start(bf16[2,512,128]{2,1,0:T(8,128)(2,1)} %follow.12), channel_id=1, source_target_pairs={{0,2},{2,0},{4,6},{6,4},{8,10},{10,8},{12,14},{14,12},{1,3},{3,1},... | collective-permute-start | bytes 786440 | tf_op jit(solution)/shard_map/ppermute | solution.py:567
  23.8 10.5 %collective-permute-start.4 = (bf16[2,512,128]{2,1,0:T(8,128)(2,1)}, bf16[2,512,128]{2,1,0:T(8,128)(2,1)}, u32[]{:S(2)}, u32[]{:S(2)}) collective-permute-start(bf16[2,512,128]{2,1,0:T(8,128)(2,1)} %copy-done.21), channel_id=1, source_target_pairs={{0,4},{4,8},{8,12},{1,5},{5,9},{9,13},{16,20},{20,24},{24,28},{17,... | collective-permute-start | bytes 786440 | tf_op jit(solution)/shard_map/ppermute | solution.py:575
  28.6 18.2 %collective-permute-start.8 = (bf16[2,512,128]{2,1,0:T(8,128)(2,1)}, bf16[2,512,128]{2,1,0:T(8,128)(2,1)S(1)}, u32[]{:S(2)}, u32[]{:S(2)}) collective-permute-start(bf16[2,512,128]{2,1,0:T(8,128)(2,1)} %follow.10), channel_id=1, source_target_pairs={{0,2},{2,0},{4,6},{6,4},{8,10},{10,8},{12,14},{14,12},{1,3},{3,1},... | collective-permute-start | bytes 786440 | tf_op jit(solution)/shard_map/ppermute | solution.py:567
  29.4 18.1 %collective-permute-start.2 = (bf16[2,512,128]{2,1,0:T(8,128)(2,1)}, bf16[2,512,128]{2,1,0:T(8,128)(2,1)}, u32[]{:S(2)}, u32[]{:S(2)}) collective-permute-start(bf16[2,512,128]{2,1,0:T(8,128)(2,1)} %copy-done.19), channel_id=1, source_target_pairs={{0,4},{4,8},{8,12},{1,5},{5,9},{9,13},{16,20},{20,24},{24,28},{17,... | collective-permute-start | bytes 786440 | tf_op jit(solution)/shard_map/ppermute | solution.py:575
  33.5 9.8 %copy-start.25 = (bf16[2,512,128]{2,1,0:T(8,128)(2,1)}, bf16[2,512,128]{2,1,0:T(8,128)(2,1)S(1)}, u32[]{:S(2)}) copy-start(bf16[2,512,128]{2,1,0:T(8,128)(2,1)S(1)} %collective-permute-done.10.refs_3_) | copy-start | bytes 786436
  34.3 13.3 %copy-start.20 = (bf16[2,512,128]{2,1,0:T(8,128)(2,1)S(1)}, bf16[2,512,128]{2,1,0:T(8,128)(2,1)}, u32[]{:S(2)}) copy-start(bf16[2,512,128]{2,1,0:T(8,128)(2,1)} %copy-done.19) | copy-start | bytes 786436
  34.3 1.0 copy-start.22
  43.3 22.3 %collective-permute-start.11 = (bf16[2,512,128]{2,1,0:T(8,128)(2,1)}, bf16[2,512,128]{2,1,0:T(8,128)(2,1)}, u32[]{:S(2)}, u32[]{:S(2)}) collective-permute-start(bf16[2,512,128]{2,1,0:T(8,128)(2,1)} %follow.13), channel_id=1, source_target_pairs={{0,4},{4,8},{8,12},{1,5},{5,9},{9,13},{16,20},{20,24},{24,28},{17,... | collective-permute-start | bytes 786440 | tf_op jit(solution)/shard_map/ppermute | solution.py:575
  46.8 9.7 %copy-start.23 = (bf16[2,512,128]{2,1,0:T(8,128)(2,1)}, bf16[2,512,128]{2,1,0:T(8,128)(2,1)S(1)}, u32[]{:S(2)}) copy-start(bf16[2,512,128]{2,1,0:T(8,128)(2,1)S(1)} %collective-permute-done.8.refs_3_) | copy-start | bytes 786436
  59.4 13.5 %collective-permute-start.9 = (bf16[2,512,128]{2,1,0:T(8,128)(2,1)}, bf16[2,512,128]{2,1,0:T(8,128)(2,1)S(1)}, u32[]{:S(2)}, u32[]{:S(2)}) collective-permute-start(bf16[2,512,128]{2,1,0:T(8,128)(2,1)} %follow.11), channel_id=1, source_target_pairs={{0,4},{4,8},{8,12},{1,5},{5,9},{9,13},{16,20},{20,24},{24,28},{17,... | collective-permute-start | bytes 786440 | tf_op jit(solution)/shard_map/ppermute | solution.py:575
  62.1 17.7 %collective-permute-start.7 = (bf16[2,16,2,16,128]{4,3,2,1,0:T(8,128)(2,1)}, bf16[2,16,2,16,128]{4,3,2,1,0:T(8,128)(2,1)S(1)}, u32[]{:S(2)}, u32[]{:S(2)}) collective-permute-start(bf16[2,16,2,16,128]{4,3,2,1,0:T(8,128)(2,1)} %copy-done.54), channel_id=1, source_target_pairs={{0,3},{1,2},{2,1},{3,0},{4,7},{5,6},{6,5},{7,4},{8,11},{9,10},{10,... | collective-permute-start | bytes 786440 | tf_op jit(solution)/shard_map/ppermute | solution.py:592
  62.2 18.6 %collective-permute-start.6 = (bf16[2,16,2,16,128]{4,3,2,1,0:T(8,128)(2,1)}, bf16[2,16,2,16,128]{4,3,2,1,0:T(8,128)(2,1)S(1)}, u32[]{:S(2)}, u32[]{:S(2)}) collective-permute-start(bf16[2,16,2,16,128]{4,3,2,1,0:T(8,128)(2,1)} %copy-done.53), channel_id=1, source_target_pairs={{0,2},{1,3},{2,0},{3,1},{4,6},{5,7},{6,4},{7,5},{8,10},{9,11},{10,... | collective-permute-start | bytes 786440 | tf_op jit(solution)/shard_map/ppermute | solution.py:592
  65.1 19.1 %collective-permute-start.5 = (bf16[2,16,2,16,128]{4,3,2,1,0:T(8,128)(2,1)}, bf16[2,16,2,16,128]{4,3,2,1,0:T(8,128)(2,1)S(1)}, u32[]{:S(2)}, u32[]{:S(2)}) collective-permute-start(bf16[2,16,2,16,128]{4,3,2,1,0:T(8,128)(2,1)} %copy-done.52), channel_id=1, source_target_pairs={{0,1},{1,0},{2,3},{3,2},{4,5},{5,4},{6,7},{7,6},{8,9},{9,8},{10,11... | collective-permute-start | bytes 786440 | tf_op jit(solution)/shard_map/ppermute | solution.py:592
  65.6 19.8 %collective-permute-start.18 = (bf16[2,16,2,16,128]{4,3,2,1,0:T(8,128)(2,1)}, bf16[2,16,2,16,128]{4,3,2,1,0:T(8,128)(2,1)}, u32[]{:S(2)}, u32[]{:S(2)}) collective-permute-start(bf16[2,16,2,16,128]{4,3,2,1,0:T(8,128)(2,1)} %copy-done.2), channel_id=1, source_target_pairs={{0,16},{16,0},{1,17},{17,1},{2,18},{18,2},{3,19},{19,3},{4,20},{20... | collective-permute-start | bytes 786440 | tf_op jit(solution)/shard_map/ppermute | solution.py:594
  68.3 4.6 %copy-start.24 = (bf16[2,512,128]{2,1,0:T(8,128)(2,1)S(1)}, bf16[2,512,128]{2,1,0:T(8,128)(2,1)}, u32[]{:S(2)}) copy-start(bf16[2,512,128]{2,1,0:T(8,128)(2,1)} %copy-done.23) | copy-start | bytes 786436
  79.8 17.3 %copy-start.4 = (bf16[2,16,2,16,128]{4,3,2,1,0:T(8,128)(2,1)S(1)}, bf16[2,16,2,16,128]{4,3,2,1,0:T(8,128)(2,1)}, u32[]{:S(2)}) copy-start(bf16[2,16,2,16,128]{4,3,2,1,0:T(8,128)(2,1)} %copy-done.2) | copy-start | bytes 786436
  79.8 5.6 %copy-start.18 = (bf16[2,16,2,16,128]{4,3,2,1,0:T(8,128)(2,1)S(1)}, bf16[2,16,2,16,128]{4,3,2,1,0:T(8,128)(2,1)}, u32[]{:S(2)}) copy-start(bf16[2,16,2,16,128]{4,3,2,1,0:T(8,128)(2,1)} %copy-done.17) | copy-start | bytes 786436
  80.5 29.4 %copy-start.7 = (bf16[2,16,2,16,128]{4,3,2,1,0:T(8,128)(2,1)S(1)}, bf16[2,16,2,16,128]{4,3,2,1,0:T(8,128)(2,1)}, u32[]{:S(2)}) copy-start(bf16[2,16,2,16,128]{4,3,2,1,0:T(8,128)(2,1)} %copy-done.5) | copy-start | bytes 786436
  80.5 10.3 %collective-permute-start.14 = (bf16[2,16,2,16,128]{4,3,2,1,0:T(8,128)(2,1)}, bf16[2,16,2,16,128]{4,3,2,1,0:T(8,128)(2,1)S(1)}, u32[]{:S(2)}, u32[]{:S(2)}) collective-permute-start(bf16[2,16,2,16,128]{4,3,2,1,0:T(8,128)(2,1)} %follow.16), channel_id=1, source_target_pairs={{0,3},{1,2},{2,1},{3,0},{4,7},{5,6},{6,5},{7,4},{8,11},{9,10},{10,... | collective-permute-start | bytes 786440 | tf_op jit(solution)/shard_map/ppermute | solution.py:592
  81.5 28.5 %copy-start.10 = (bf16[2,16,2,16,128]{4,3,2,1,0:T(8,128)(2,1)S(1)}, bf16[2,16,2,16,128]{4,3,2,1,0:T(8,128)(2,1)}, u32[]{:S(2)}) copy-start(bf16[2,16,2,16,128]{4,3,2,1,0:T(8,128)(2,1)} %copy-done.8) | copy-start | bytes 786436
  81.5 14.6 %collective-permute-start.13 = (bf16[2,16,2,16,128]{4,3,2,1,0:T(8,128)(2,1)}, bf16[2,16,2,16,128]{4,3,2,1,0:T(8,128)(2,1)S(1)}, u32[]{:S(2)}, u32[]{:S(2)}) collective-permute-start(bf16[2,16,2,16,128]{4,3,2,1,0:T(8,128)(2,1)} %follow.15), channel_id=1, source_target_pairs={{0,2},{1,3},{2,0},{3,1},{4,6},{5,7},{6,4},{7,5},{8,10},{9,11},{10,... | collective-permute-start | bytes 786440 | tf_op jit(solution)/shard_map/ppermute | solution.py:592
  85.0 11.1 %collective-permute-start.12 = (bf16[2,16,2,16,128]{4,3,2,1,0:T(8,128)(2,1)}, bf16[2,16,2,16,128]{4,3,2,1,0:T(8,128)(2,1)S(1)}, u32[]{:S(2)}, u32[]{:S(2)}) collective-permute-start(bf16[2,16,2,16,128]{4,3,2,1,0:T(8,128)(2,1)} %follow.14), channel_id=1, source_target_pairs={{0,1},{1,0},{2,3},{3,2},{4,5},{5,4},{6,7},{7,6},{8,9},{9,8},{10,11... | collective-permute-start | bytes 786440 | tf_op jit(solution)/shard_map/ppermute | solution.py:592
  85.5 11.1 %collective-permute-start.22 = (bf16[2,16,2,16,128]{4,3,2,1,0:T(8,128)(2,1)S(1)}, bf16[2,16,2,16,128]{4,3,2,1,0:T(8,128)(2,1)S(1)}, u32[]{:S(2)}, u32[]{:S(2)}) collective-permute-start(bf16[2,16,2,16,128]{4,3,2,1,0:T(8,128)(2,1)S(1)} %copy-done.18), channel_id=1, source_target_pairs={{0,16},{16,0},{1,17},{17,1},{2,18},{18,2},{3,19},{19,3},{4,20},{20... | collective-permute-start | bytes 786440 | tf_op jit(solution)/shard_map/ppermute | solution.py:594
  85.5 11.2 %collective-permute-start.19 = (bf16[2,16,2,16,128]{4,3,2,1,0:T(8,128)(2,1)}, bf16[2,16,2,16,128]{4,3,2,1,0:T(8,128)(2,1)S(1)}, u32[]{:S(2)}, u32[]{:S(2)}) collective-permute-start(bf16[2,16,2,16,128]{4,3,2,1,0:T(8,128)(2,1)} %copy-done.11), channel_id=1, source_target_pairs={{0,16},{16,0},{1,17},{17,1},{2,18},{18,2},{3,19},{19,3},{4,20},{20... | collective-permute-start | bytes 786440 | tf_op jit(solution)/shard_map/ppermute | solution.py:594
  90.8 17.0 %collective-permute-start.20 = (bf16[2,16,2,16,128]{4,3,2,1,0:T(8,128)(2,1)}, bf16[2,16,2,16,128]{4,3,2,1,0:T(8,128)(2,1)S(1)}, u32[]{:S(2)}, u32[]{:S(2)}) collective-permute-start(bf16[2,16,2,16,128]{4,3,2,1,0:T(8,128)(2,1)} %copy-done.8), channel_id=1, source_target_pairs={{0,16},{16,0},{1,17},{17,1},{2,18},{18,2},{3,19},{19,3},{4,20},{20... | collective-permute-start | bytes 786440 | tf_op jit(solution)/shard_map/ppermute | solution.py:594
  96.1 11.8 %collective-permute-start.21 = (bf16[2,16,2,16,128]{4,3,2,1,0:T(8,128)(2,1)}, bf16[2,16,2,16,128]{4,3,2,1,0:T(8,128)(2,1)S(1)}, u32[]{:S(2)}, u32[]{:S(2)}) collective-permute-start(bf16[2,16,2,16,128]{4,3,2,1,0:T(8,128)(2,1)} %copy-done.5), channel_id=1, source_target_pairs={{0,16},{16,0},{1,17},{17,1},{2,18},{18,2},{3,19},{19,3},{4,20},{20... | collective-permute-start | bytes 786440 | tf_op jit(solution)/shard_map/ppermute | solution.py:594
  96.1 13.2 %collective-permute-start.25 = (bf16[2,16,2,16,128]{4,3,2,1,0:T(8,128)(2,1)S(1)}, bf16[2,16,2,16,128]{4,3,2,1,0:T(8,128)(2,1)S(1)}, u32[]{:S(2)}, u32[]{:S(2)}) collective-permute-start(bf16[2,16,2,16,128]{4,3,2,1,0:T(8,128)(2,1)S(1)} %collective-permute-done.14.refs_8_), channel_id=1, source_target_pairs={{0,16},{16,0},{1,17},{17,1},{2,18},{18,2},{3,19},{19,3},{4,20},{20... | collective-permute-start | bytes 786440 | tf_op jit(solution)/shard_map/ppermute | solution.py:594
  96.6 13.3 %collective-permute-start.24 = (bf16[2,16,2,16,128]{4,3,2,1,0:T(8,128)(2,1)S(1)}, bf16[2,16,2,16,128]{4,3,2,1,0:T(8,128)(2,1)S(1)}, u32[]{:S(2)}, u32[]{:S(2)}) collective-permute-start(bf16[2,16,2,16,128]{4,3,2,1,0:T(8,128)(2,1)S(1)} %collective-permute-done.13.refs_7_), channel_id=1, source_target_pairs={{0,16},{16,0},{1,17},{17,1},{2,18},{18,2},{3,19},{19,3},{4,20},{20... | collective-permute-start | bytes 786440 | tf_op jit(solution)/shard_map/ppermute | solution.py:594
  96.7 13.3 %collective-permute-start.23 = (bf16[2,16,2,16,128]{4,3,2,1,0:T(8,128)(2,1)S(1)}, bf16[2,16,2,16,128]{4,3,2,1,0:T(8,128)(2,1)S(1)}, u32[]{:S(2)}, u32[]{:S(2)}) collective-permute-start(bf16[2,16,2,16,128]{4,3,2,1,0:T(8,128)(2,1)S(1)} %collective-permute-done.12.refs_6_), channel_id=1, source_target_pairs={{0,16},{16,0},{1,17},{17,1},{2,18},{18,2},{3,19},{19,3},{4,20},{20... | collective-permute-start | bytes 786440 | tf_op jit(solution)/shard_map/ppermute | solution.py:594
  100.0 10.0 %copy-start.13 = (bf16[2,16,2,16,128]{4,3,2,1,0:T(8,128)(2,1)S(1)}, bf16[2,16,2,16,128]{4,3,2,1,0:T(8,128)(2,1)}, u32[]{:S(2)}) copy-start(bf16[2,16,2,16,128]{4,3,2,1,0:T(8,128)(2,1)} %copy-done.11) | copy-start | bytes 786436
  107.8 12.3 %collective-permute-start.17 = (bf16[544,128]{1,0:T(8,128)(2,1)S(1)}, bf16[544,128]{1,0:T(8,128)(2,1)S(1)}, u32[]{:S(2)}, u32[]{:S(2)}) collective-permute-start(bf16[544,128]{1,0:T(8,128)(2,1)S(1)} %get-tuple-element.56), channel_id=1, source_target_pairs={{0,12},{2,14},{4,0},{6,2},{8,4},{10,6},{12,8},{14,10},{1,13},{3,15... | collective-permute-start | bytes 417800 | tf_op jit(solution)/shard_map/ppermute | solution.py:610
  107.9 16.1 %collective-permute-start.16 = (bf16[544,128]{1,0:T(8,128)(2,1)S(1)}, bf16[544,128]{1,0:T(8,128)(2,1)S(1)}, u32[]{:S(2)}, u32[]{:S(2)}) collective-permute-start(bf16[544,128]{1,0:T(8,128)(2,1)S(1)} %get-tuple-element.55), channel_id=1, source_target_pairs={{0,8},{2,10},{4,12},{6,14},{8,0},{10,2},{12,4},{14,6},{1,9},{3,11}... | collective-permute-start | bytes 417800 | tf_op jit(solution)/shard_map/ppermute | solution.py:610
  109.3 15.3 %collective-permute-start.15 = (bf16[544,128]{1,0:T(8,128)(2,1)S(1)}, bf16[544,128]{1,0:T(8,128)(2,1)S(1)}, u32[]{:S(2)}, u32[]{:S(2)}) collective-permute-start(bf16[544,128]{1,0:T(8,128)(2,1)S(1)} %get-tuple-element.54), channel_id=1, source_target_pairs={{0,4},{2,6},{4,8},{6,10},{8,12},{10,14},{12,0},{14,2},{1,5},{3,7},... | collective-permute-start | bytes 417800 | tf_op jit(solution)/shard_map/ppermute | solution.py:610
  120.7 7.1 %collective-permute-start.28 = (bf16[512,128]{1,0:T(8,128)(2,1)}, bf16[512,128]{1,0:T(8,128)(2,1)S(1)}, u32[]{:S(2)}, u32[]{:S(2)}) collective-permute-start(bf16[512,128]{1,0:T(8,128)(2,1)} %follow.19), channel_id=1, source_target_pairs={{0,12},{2,14},{4,0},{6,2},{8,4},{10,6},{12,8},{14,10},{1,13},{3,15... | collective-permute-start | bytes 393224 | tf_op jit(solution)/shard_map/ppermute | solution.py:615
  124.6 10.7 %collective-permute-start.27 = (bf16[512,128]{1,0:T(8,128)(2,1)}, bf16[512,128]{1,0:T(8,128)(2,1)S(1)}, u32[]{:S(2)}, u32[]{:S(2)}) collective-permute-start(bf16[512,128]{1,0:T(8,128)(2,1)} %follow.18), channel_id=1, source_target_pairs={{0,8},{2,10},{4,12},{6,14},{8,0},{10,2},{12,4},{14,6},{1,9},{3,11}... | collective-permute-start | bytes 393224 | tf_op jit(solution)/shard_map/ppermute | solution.py:615
  124.6 11.2 %collective-permute-start.29 = (f32[512,128]{1,0:T(8,128)S(1)}, f32[512,128]{1,0:T(8,128)S(1)}, u32[]{:S(2)}, u32[]{:S(2)}) collective-permute-start(f32[512,128]{1,0:T(8,128)S(1)} %get-tuple-element.57.refs_5_), channel_id=1, source_target_pairs={{0,16},{16,0},{1,17},{17,1},{2,18},{18,2},{3,19},{19,3},{4,20},{20... | collective-permute-start | bytes 786440 | tf_op jit(solution)/shard_map/ppermute | solution.py:616
  125.3 10.0 %collective-permute-start.26 = (bf16[512,128]{1,0:T(8,128)(2,1)}, bf16[512,128]{1,0:T(8,128)(2,1)S(1)}, u32[]{:S(2)}, u32[]{:S(2)}) collective-permute-start(bf16[512,128]{1,0:T(8,128)(2,1)} %follow.17), channel_id=1, source_target_pairs={{0,4},{2,6},{4,8},{6,10},{8,12},{10,14},{12,0},{14,2},{1,5},{3,7},... | collective-permute-start | bytes 393224 | tf_op jit(solution)/shard_map/ppermute | solution.py:615
  127.9 7.9 %collective-permute-start.32 = (bf16[512,128]{1,0:T(8,128)(2,1)S(1)}, bf16[512,128]{1,0:T(8,128)(2,1)S(1)}, u32[]{:S(2)}, u32[]{:S(2)}) collective-permute-start(bf16[512,128]{1,0:T(8,128)(2,1)S(1)} %collective-permute-done.28.refs_8_), channel_id=1, source_target_pairs={{0,16},{16,0},{1,17},{17,1},{2,18},{18,2},{3,19},{19,3},{4,20},{20... | collective-permute-start | bytes 393224 | tf_op jit(solution)/shard_map/ppermute | solution.py:616
  135.3 1.3 collective-permute-start.31
  135.3 1.5 %collective-permute-start.30 = (bf16[512,128]{1,0:T(8,128)(2,1)S(1)}, bf16[512,128]{1,0:T(8,128)(2,1)S(1)}, u32[]{:S(2)}, u32[]{:S(2)}) collective-permute-start(bf16[512,128]{1,0:T(8,128)(2,1)S(1)} %collective-permute-done.26.refs_6_), channel_id=1, source_target_pairs={{0,16},{16,0},{1,17},{17,1},{2,18},{18,2},{3,19},{19,3},{4,20},{20... | collective-permute-start | bytes 393224 | tf_op jit(solution)/shard_map/ppermute | solution.py:616
  (40 other events, 30.6 us)

commit v6 on v5

--- a/solution.py
+++ b/solution.py
@@ -22,7 +22,7 @@
 
 VMEM = pl.BlockSpec(memory_space=pltpu.VMEM)
 SMEM = pl.BlockSpec(memory_space=pltpu.SMEM)
-ANY = pl.BlockSpec(memory_space=pl.ANY)
+HBM = pl.BlockSpec(memory_space=pltpu.HBM)
 
 
 def params(mib):
@@ -82,33 +82,50 @@
 
 
 def pick_kernel(count, joined, own, meta, block, *refs):
-    outs, rows = refs[:-1], refs[-1]
+    outs, (held, rows, staged, in_sems, out_sems) = refs[:-5], refs[-5:]
     inputs, samples = block.shape[1], block.shape[2]
     step = 16
-    for part in range(2):
-
-        def spread(n, carry, part=part):
-            low = pl.multiple_of(n * step * LANES, step * LANES)
-            wide = block[part, :, pl.ds(low, step * LANES)].astype(jnp.float32)
-            for u in range(step):
-                at = pl.multiple_of((n * step + u) * inputs, inputs)
-                rows[part, pl.ds(at, inputs), :] = wide[:, u * LANES : (u + 1) * LANES]
+    parts = in_sems.shape[0]
+    size = samples // parts
+
+    def bring(n):
+        cut = slice(n * size, (n + 1) * size)
+        return pltpu.make_async_copy(block.at[:, :, cut], held.at[:, :, cut], in_sems.at[n])
+
+    def send(item):
+        out = outs[0].at[item] if joined else outs[item]
+        return pltpu.make_async_copy(staged.at[item], out, out_sems.at[item])
+
+    for n in range(parts):
+        bring(n).start()
+    for m in range(parts):
+        bring(m).wait()
+
+        def spread(n, carry, m=m):
+            low = pl.multiple_of(m * size + n * step * LANES, step * LANES)
+            for part in range(2):
+                wide = held[part, :, pl.ds(low, step * LANES)].astype(jnp.float32)
+                for u in range(step):
+                    at = pl.multiple_of((m * size // LANES + n * step + u) * inputs, inputs)
+                    rows[part, pl.ds(at, inputs), :] = wide[:, u * LANES : (u + 1) * LANES]
             return carry
 
-        lax.fori_loop(0, samples // LANES // step, spread, 0)
+        lax.fori_loop(0, size // LANES // step, spread, 0)
     first = (meta[G_AT] if own else 1 - meta[G_AT]) * count
     tall = 128
     for item in range(count):
-        out = outs[0].at[item] if joined else outs[item]
-
-        def gather(n, carry, item=item, out=out):
+
+        def gather(n, carry, item=item):
             low = pl.multiple_of(n * tall, tall)
             for part in range(2):
                 value = rows[part, pl.ds(low * inputs + first + item, tall, stride=inputs), :]
-                out[part, pl.ds(low, tall), :] = value.astype(jnp.bfloat16)
+                staged[item, part, pl.ds(low, tall), :] = value.astype(jnp.bfloat16)
             return carry
 
         lax.fori_loop(0, samples // LANES // tall, gather, 0)
+        send(item).start()
+    for item in range(count):
+        send(item).wait()
 
 
 def pick(meta, block, count, joined, own):
@@ -118,9 +135,15 @@
     return pl.pallas_call(
         functools.partial(pick_kernel, count, joined, own),
         out_shape=[jax.ShapeDtypeStruct(s, jnp.bfloat16) for s in shapes],
-        in_specs=[SMEM, VMEM],
-        out_specs=[VMEM] * len(shapes),
-        scratch_shapes=[pltpu.VMEM((2, samples // LANES * inputs, LANES), jnp.float32)],
+        in_specs=[SMEM, HBM],
+        out_specs=[HBM] * len(shapes),
+        scratch_shapes=[
+            pltpu.VMEM(block.shape, jnp.bfloat16),
+            pltpu.VMEM((2, samples // LANES * inputs, LANES), jnp.float32),
+            pltpu.VMEM((count,) + one, jnp.bfloat16),
+            pltpu.SemaphoreType.DMA((4,)),
+            pltpu.SemaphoreType.DMA((count,)),
+        ],
         compiler_params=params(16),
         cost_estimate=cost(10**6, 2**18),
         name="pick",
@@ -134,8 +157,8 @@
     return pl.pallas_call(
         hand_on,
         out_shape=jax.ShapeDtypeStruct(block.shape, block.dtype),
-        in_specs=[ANY, ANY],
-        out_specs=ANY,
+        in_specs=[HBM, HBM],
+        out_specs=HBM,
         input_output_aliases={0: 0},
         name="follow",
     )(block, after)
@@ -145,13 +168,12 @@
 SOME = 4
 
 
-def filterbank_kernel(index, before, frames, dests, per_ct, half_count, *refs):
+def filterbank_kernel(index, frames, dests, per_ct, half_count, *refs):
     meta, keep, halo_own, recv, halo_far, after, coef, first, tw_cos, tw_sin, last = refs[:11]
-    earlier = refs[11 : 11 + dests * (before > 0)]
-    refs = refs[11 + len(earlier) :]
-    outs = refs[:dests]
-    raw, weights, grouped, sems = refs[dests : dests + 4]
-    filtered = refs[dests + 4 :]
+    raw, weights, grouped, staged, sems, out_sems = refs[-6 - PAIR * frames // HALF :][:6]
+    filtered = refs[-(PAIR * frames // HALF) :]
+    outs = refs[-7 - PAIR * frames // HALF - dests :][:dests]
+    slot = index % JOIN
     block_rows = frames * ROWS
     total = PAIR * frames
     me, ct = meta[G_AT], meta[CT_AT]
@@ -183,8 +205,12 @@
         here = coef[tap, pl.ds(down, ROWS), :]
         after = coef[tap, pl.ds(down + 1, ROWS), :]
         weights[tap] = pltpu.roll(jnp.where(turned_in, here, after), back, 1)
-    for dest, old in zip(outs, earlier):
-        dest[:before] = old[...]
+
+    def send(dest, half):
+        cut = pl.ds(half * HALF // 2, HALF // 2)
+        return pltpu.make_async_copy(
+            staged.at[dest, cut], outs[dest].at[slot, cut], out_sems.at[dest, half]
+        )
 
     bring(halo_far, 0, 0).wait()
     bring(keep.at[index], 1 + me, 1).wait()
@@ -245,7 +271,7 @@
             for part in range(2):
                 low = (dest * 2 + part) * size
                 for u in range(SOME // 2):
-                    outs[dest][before, base // 2 + u, part] = result[
+                    staged[dest, base // 2 + u, part] = result[
                         low : low + size, u * LANES : (u + 1) * LANES
                     ]
 
@@ -269,30 +295,39 @@
                 for u in range(SOME):
                     place(half - 1, n * SOME + u)
                 turn((half - 1) * HALF + n * SOME)
+        if half:
+            for dest in range(dests):
+                send(dest, half - 1).start()
+    for half in range(halves):
+        for dest in range(dests):
+            send(dest, half).wait()
 
 
 def filterbank(index, meta, keep, halo_own, recv, halo_far, after, tables, earlier, dests):
     frames = keep.shape[2] // ROWS
     size = tables[-1].shape[2] // 2
     per_ct = tables[-1].shape[1] // 2
-    before = earlier[0].shape[0] if earlier else 0
     all_rows = (PAIR + 1) * frames * ROWS
-    shape = (before + 1, PAIR * frames // 2, 2, size, LANES)
+    halves = PAIR * frames // HALF
+    shape = (PAIR * frames // 2, 2, size, LANES)
+    spectra = jax.ShapeDtypeStruct((JOIN,) + shape, jnp.bfloat16)
+    token = jax.ShapeDtypeStruct((8, LANES), jnp.float32)
     return pl.pallas_call(
-        functools.partial(
-            filterbank_kernel, index, before, frames, dests, per_ct, keep.shape[0]
-        ),
-        out_shape=[jax.ShapeDtypeStruct(shape, jnp.bfloat16)] * dests,
-        in_specs=[SMEM] + [ANY] * 5 + [VMEM] * (5 + len(earlier)),
-        out_specs=[VMEM] * dests,
+        functools.partial(filterbank_kernel, index, frames, dests, per_ct, keep.shape[0]),
+        out_shape=[spectra] * dests + [token],
+        in_specs=[SMEM] + [HBM] * 5 + [VMEM] * 5 + [HBM] * len(earlier),
+        out_specs=[HBM] * (dests + 1),
+        input_output_aliases={11 + n: n for n in range(len(earlier))},
         scratch_shapes=[
             pltpu.VMEM((2, all_rows, LANES), jnp.bfloat16),
             pltpu.VMEM((TAPS, ROWS, LANES), jnp.float32),
             pltpu.VMEM((PAIR * frames, LANES, LANES), jnp.bfloat16),
+            pltpu.VMEM((dests,) + shape, jnp.bfloat16),
             pltpu.SemaphoreType.DMA((3,)),
+            pltpu.SemaphoreType.DMA((dests, halves)),
         ]
-        + [pltpu.VMEM((2, (HALF + 1) * ROWS, LANES), jnp.float32)] * (PAIR * frames // HALF),
-        compiler_params=params(16),
+        + [pltpu.VMEM((2, (HALF + 1) * ROWS, LANES), jnp.float32)] * halves,
+        compiler_params=params(12),
         cost_estimate=cost(10**6, 2**18),
         name="filterbank",
     )(meta, keep, halo_own, recv, halo_far, after, *tables, *earlier)
@@ -328,37 +363,47 @@
     sources_at, blocks, own, cross, outer, span, per_ct, in_count, half_count = layout
     meta, sources = refs[0], refs[1 : 1 + len(sources_at)]
     rest = refs[1 + len(sources_at) :]
-    outs, (spectra, sums, held) = rest[:-3], rest[-3:]
+    outs, (raw, spectra, sums, held, first_out, staged, sems, out_sems) = rest[:-8], rest[-8:]
     steps = spectra.shape[1]
     some = 8
     core, g, ct = meta[CORE_AT], meta[G_AT], meta[CT_AT]
 
-    for source, (far, dg, dc, start) in zip(sources, sources_at):
+    def bring(n):
+        return pltpu.make_async_copy(sources[n], raw.at[n], sems.at[n])
+
+    def fill(n, base):
+        bring(n).wait()
+        for item in range(sources[n].shape[0]):
+
+            def spread(m, carry, item=item):
+                for u in range(some):
+                    real = raw[n, item, m * some + u, 0].astype(jnp.float32)
+                    imag = raw[n, item, m * some + u, 1].astype(jnp.float32)
+                    for which, value in enumerate((real, imag, real + imag, imag - real)):
+                        spectra[base + item, m * some + u, which] = value
+                return carry
+
+            lax.fori_loop(0, steps // some, spread, 0)
+
+    bases, wanted = [], []
+    for far, dg, dc, start in sources_at:
         base = lax.rem(ct - dc + per_ct, per_ct) * in_count + (g ^ dg) * half_count + start
-        wanted = None
         if cross:
             side = 1 - core if far else core
             low = core * (own // 2)
-            wanted = (side == 1) | ((base >= low) & (base < low + own // 2))
+            wanted.append((side == 1) | ((base >= low) & (base < low + own // 2)))
             base = base + side * own
-
-        def bring(source=source, base=base):
-            for item in range(source.shape[0]):
-
-                def spread(n, carry, item=item):
-                    for u in range(some):
-                        real = source[item, n * some + u, 0].astype(jnp.float32)
-                        imag = source[item, n * some + u, 1].astype(jnp.float32)
-                        for which, value in enumerate((real, imag, real + imag, imag - real)):
-                            spectra[base + item, n * some + u, which] = value
-                    return carry
-
-                lax.fori_loop(0, steps // some, spread, 0)
-
-        if wanted is None:
-            bring()
+        bases.append(base)
+    for n in range(len(sources)):
+        if cross:
+            pl.when(wanted[n])(lambda n=n: bring(n).start())
         else:
-            pl.when(wanted)(bring)
+            bring(n).start()
+    for n in range(len(sources)):
+        if cross:
+            pl.when(wanted[n])(functools.partial(fill, n, bases[n]))
+        else:
+            fill(n, bases[n])
 
     high = lax.broadcasted_iota(jnp.int32, (1, LANES), 1) < RADIX
     rows_outer = pairs_in(blocks) * span
@@ -411,9 +456,19 @@
         lax.fori_loop(0, len(some_blocks), step, 0)
         done += pairs_in(some_blocks) * span
 
+    def send(r):
+        return pltpu.make_async_copy(staged.at[r - 1] if r else first_out, outs[r], out_sems.at[r])
+
+    for r in list(range(1, outer)) + [0]:
+        base = pl.multiple_of(lax.rem(meta[O_AT] + r, outer) * rows_outer, 16)
+        value = sums[pl.ds(base, rows_outer), :]
+        if r:
+            staged[r - 1] = value.astype(staged.dtype)
+        else:
+            first_out[...] = value
+        send(r).start()
     for r in range(outer):
-        base = pl.multiple_of(lax.rem(meta[O_AT] + r, outer) * rows_outer, 16)
-        outs[r][...] = sums[pl.ds(base, rows_outer), :].astype(outs[r].dtype)
+        send(r).wait()
 
 
 def correlate(meta, arrays, sources_at, blocks, own, cross, sizes, name):
@@ -429,14 +484,19 @@
     return pl.pallas_call(
         functools.partial(correlate_kernel, layout),
         out_shape=shapes,
-        in_specs=[SMEM] + [VMEM] * len(arrays),
-        out_specs=[VMEM] * len(shapes),
+        in_specs=[SMEM] + [HBM] * len(arrays),
+        out_specs=[HBM] * len(shapes),
         scratch_shapes=[
+            pltpu.VMEM((len(arrays),) + arrays[0].shape, jnp.bfloat16),
             pltpu.VMEM((inputs, steps, 4, size, LANES), jnp.float32),
             pltpu.VMEM((outer * rows, LANES), jnp.float32),
             pltpu.VMEM((2, TILE * TILE, outer * span, LANES), jnp.float32),
+            pltpu.VMEM((rows, LANES), jnp.float32),
+            pltpu.VMEM((outer - 1, rows, LANES), jnp.bfloat16),
+            pltpu.SemaphoreType.DMA((len(arrays),)),
+            pltpu.SemaphoreType.DMA((outer,)),
         ],
-        compiler_params=params(14 + inputs * steps * 4 * size * LANES * 4 // 2**20),
+        compiler_params=params(12 + inputs * steps * 4 * size * LANES * 4 // 2**20),
         cost_estimate=cost(10**6, 2**18),
         name=name,
     )(meta, *arrays)
@@ -444,10 +504,19 @@
 
 def assemble_kernel(own, outer, span, scale, *refs):
     meta = refs[0]
-    mine_in = refs[1 : 1 + outer]
-    mine_across = refs[1 + outer : 1 + 2 * outer]
-    far_across = refs[1 + 2 * outer : 1 + 3 * outer]
-    out, joined = refs[1 + 3 * outer :]
+    sources = refs[1 : 1 + 3 * outer]
+    out = refs[1 + 3 * outer]
+    kept = refs[2 + 3 * outer : 2 + 6 * outer]
+    joined, staged, sems, out_sems = refs[2 + 6 * outer :]
+    mine_in, mine_across, far_across = (kept[n * outer : (n + 1) * outer] for n in range(3))
+
+    def bring(n):
+        return pltpu.make_async_copy(sources[n], kept[n], sems.at[n])
+
+    for n in range(len(sources)):
+        bring(n).start()
+    for n in range(len(sources)):
+        bring(n).wait()
     lane = lax.broadcasted_iota(jnp.int32, (1, LANES), 1)
     high = lane < RADIX
     mirror = jnp.where(high, 1.0, -1.0).astype(jnp.float32)
@@ -496,25 +565,44 @@
                     loads.append(joined[pl.ds(at, 8, stride=span), :])
                 turned = [pltpu.roll(x, RADIX, 1) for x in loads]
                 cut = slice(pair * LANES, (pair + 1) * LANES)
-                out[0, a, tile * 8 : tile * 8 + 8, cut] = jnp.where(high, loads[0], turned[1])
-                out[1, a, tile * 8 : tile * 8 + 8, cut] = jnp.where(high, turned[0], loads[1])
+                staged[0, a, tile * 8 : tile * 8 + 8, cut] = jnp.where(high, loads[0], turned[1])
+                staged[1, a, tile * 8 : tile * 8 + 8, cut] = jnp.where(high, turned[0], loads[1])
         return carry
 
-    lax.fori_loop(0, own, emit, 0)
+    groups = out_sems.shape[0]
+    size = own // groups
+
+    def send(n):
+        cut = pl.ds(n * size, size)
+        return pltpu.make_async_copy(staged.at[:, cut], out.at[:, cut], out_sems.at[n])
+
+    for n in range(groups):
+        lax.fori_loop(n * size, (n + 1) * size, emit, 0)
+        send(n).start()
+    for n in range(groups):
+        send(n).wait()
 
 
 def assemble(meta, mine_in, mine_across, far_across, own, span, scale):
     outer = len(mine_in)
+    sources = [*mine_in, *mine_across, *far_across]
+    shape = (2, own, 2 * own, span * RADIX)
     return pl.pallas_call(
         functools.partial(assemble_kernel, own, outer, span, scale),
-        out_shape=jax.ShapeDtypeStruct((2, own, 2 * own, span * RADIX), jnp.float32),
-        in_specs=[SMEM] + [VMEM] * (3 * outer),
-        out_specs=VMEM,
-        scratch_shapes=[pltpu.VMEM((own * 2 * own * span, LANES), jnp.float32)],
-        compiler_params=params(24),
+        out_shape=jax.ShapeDtypeStruct(shape, jnp.float32),
+        in_specs=[SMEM] + [HBM] * len(sources),
+        out_specs=HBM,
+        scratch_shapes=[pltpu.VMEM(x.shape, x.dtype) for x in sources]
+        + [
+            pltpu.VMEM((own * 2 * own * span, LANES), jnp.float32),
+            pltpu.VMEM(shape, jnp.float32),
+            pltpu.SemaphoreType.DMA((len(sources),)),
+            pltpu.SemaphoreType.DMA((4,)),
+        ],
+        compiler_params=params(12),
         cost_estimate=cost(10**6, 2**18),
         name="assemble",
-    )(meta, *mine_in, *mine_across, *far_across)
+    )(meta, *sources)
 
 
 def fast_fits(in_count, frame_count):
@@ -571,13 +659,13 @@
     arrays, others, places = [], [], []
     spectra, done = [], []
     for c in range(half):
-        block = follow(recvs[c], done[c - 2]) if c >= 2 else recvs[c]
-        far = lax.ppermute(block, "tm", forward)
-        after = done[c - 1] if c else meta
-        spectra = filterbank(
-            c, meta, keep, halo_own, recvs[c], far, after, tables, spectra, len(dests)
+        recv = follow(recvs[c], done[c - 2]) if c >= 2 else recvs[c]
+        far = lax.ppermute(recv, "tm", forward)
+        *spectra, token = filterbank(
+            c, meta, keep, halo_own, recv, far, done[c - 1] if c else keep, tables, spectra,
+            len(dests),
         )
-        done.append(spectra[0])
+        done.append(token)
         if c % JOIN < JOIN - 1:
             continue
         for (dg, dc), block in zip(dests, spectra):

time: 144 us -> 150 us (1.042)
  Pallas kernels: 40.9 us -> 49.1 us
  local copies, waits for them, and re-layouts: 35.3 us -> 33.3 us
    pallas_call x4, Pallas kernels: 17.8 us -> 22.3 us  [filterbank(): pl.pallas_call(functools.partial(filterbank_kernel, index, frames, dests,...]
    ppermute x4, starting transfers between devices: 8.61 us -> 5.8 us  [fast(): recvs.append(lax.ppermute(block, 'tm', swap))]
    unnamed x112 -> x108, local copies, waits for them, and re-layouts: 34.6 us -> 32.6 us
    pallas_call x2, Pallas kernels: 15.9 us -> 17.9 us  [correlate(): pl.pallas_call(functools.partial(correlate_kernel, layout), out_shape=sha...]
    ppermute x3, starting transfers between devices: 2.12 us -> 3.92 us  [fast(): mine_in[r] = lax.ppermute(mine_in[r], 'tm', route)]
    pallas_call x1, Pallas kernels: 3.68 us -> 5.18 us  [assemble(): pl.pallas_call(functools.partial(assemble_kernel, own, outer, span, scale...]
  transfers between devices with their start and end apart: 33 -> 33, of which waited for: 7 -> 10; matrix products, arithmetic and copies ran while one was open for 1% -> 0% of each run, Pallas kernels for 25% -> 28%
where the time goes in v6:
time: 150 us; the launch traced here: 149 us
  Pallas kernels  49.1 us (33%)
  starting transfers between devices  38.7 us (26%)
  local copies, waits for them, and re-layouts  33.3 us (22%)
  waiting for transfers between devices  27.7 us (18%)
    unnamed x108, local copies, waits for them, and re-layouts  32.6 us
    pallas_call x4, Pallas kernels, filterbank(): pl.pallas_call(functools.partial(filterbank_kernel, index, frames, dests,...  22.3 us
    pallas_call x2, Pallas kernels, correlate(): pl.pallas_call(functools.partial(correlate_kernel, layout), out_shape=sha...  17.9 us
    ppermute x4, starting transfers between devices, fast(): far = lax.ppermute(recv, 'tm', forward)  15.1 us
    ppermute x6, waiting for transfers between devices, fast(): block = lax.ppermute(block, ('tm', 'ct'), route)  11 us
    ppermute x4, waiting for transfers between devices, fast(): recvs.append(lax.ppermute(block, 'tm', swap))  8.1 us
    ppermute x3, waiting for transfers between devices, fast(): mine_across[r] = lax.ppermute(block, 'tm', route)  7.18 us
    ppermute x6, starting transfers between devices, fast(): block = lax.ppermute(block, ('tm', 'ct'), route)  7.04 us
  transfers between devices with their start and end apart: 33, of which 10 were waited for; matrix products, arithmetic and copies ran while one was open for 0% of the time, Pallas kernels for 28%

profile of v6, /device:TPU:0, one launch (start us, length us, event | category | flops | bytes accessed | tf_op | source)
XLA Modules:
  0.0 149.4 jit_solution(6341233506435409098)
XLA Ops:
  0.0 0.7 concatenate.3.meta.refs_0_
  0.7 1.6 %copy-done = bf16[2,8,65536]{2,1,0:T(8,128)(2,1)S(1)} copy-done((bf16[2,8,65536]{2,1,0:T(8,128)(2,1)S(1)}, bf16[2,8,65536]{2,1,0:T(8,128)(2,1)}, u32[]{:S(2)}) %copy-start) | copy-done | bytes 2097176
  2.3 1.9 %pick.2.refs_1_.refs_5_ = bf16[4,2,512,128]{3,2,1,0:T(8,128)(2,1)S(1)} custom-call(s32[12]{0:T(128)S(1)} %concatenate.3.meta.refs_0_, bf16[2,8,65536]{2,1,0:T(8,128)(2,1)S(1)} %copy-done), custom_call_target="tpu_custom_call" | custom-call | flops 1000000 | bytes 262144 | tf_op jit(solution)/shard_map/pick/pallas_call | solution.py:135
  4.3 0.9 collective-permute-start
  5.1 1.9 %pick.3 = (bf16[2,512,128]{2,1,0:T(8,128)(2,1)S(1)}, bf16[2,512,128]{2,1,0:T(8,128)(2,1)S(1)}, bf16[2,512,128]{2,1,0:T(8,128)(2,1)S(1)}, bf16[2,512,128]{2,1,0:T(8,128)(2,1)S(1)}) custom-call(s32[12]{0:T(128)S(1)} %concatenate.3.meta.refs_0_, bf16[2,8,65536]{2,1,0:T(8,128)(2,1)S(1)} %copy-done), custom_call_target="tpu_custom_call" | custom-call | flops 1000000 | bytes 262144 | tf_op jit(solution)/shard_map/pick/pallas_call | solution.py:135
  8.4 5.8 %collective-permute-start.3 = (bf16[2,512,128]{2,1,0:T(8,128)(2,1)S(1)}, bf16[2,512,128]{2,1,0:T(8,128)(2,1)S(1)}, u32[]{:S(2)}, u32[]{:S(2)}) collective-permute-start(bf16[2,512,128]{2,1,0:T(8,128)(2,1)S(1)} %get-tuple-element.37), channel_id=1, source_target_pairs={{0,2},{2,0},{4,6},{6,4},{8,10},{10,8},{12,14},{14,12},{1,3},{3,1},... | collective-permute-start | bytes 786440 | tf_op jit(solution)/shard_map/ppermute | solution.py:655
  14.2 7.1 %collective-permute-done.3.refs_3_.after = bf16[2,512,128]{2,1,0:T(8,128)(2,1)S(1)} collective-permute-done((bf16[2,512,128]{2,1,0:T(8,128)(2,1)S(1)}, bf16[2,512,128]{2,1,0:T(8,128)(2,1)S(1)}, u32[]{:S(2)}, u32[]{:S(2)}) %collective-permute-start.3) | collective-permute-done | bytes 262176 | tf_op jit(solution)/shard_map/ppermute | solution.py:655
  21.3 4.1 %collective-permute-start.4 = (bf16[2,512,128]{2,1,0:T(8,128)(2,1)S(1)}, bf16[2,512,128]{2,1,0:T(8,128)(2,1)}, u32[]{:S(2)}, u32[]{:S(2)}) collective-permute-start(bf16[2,512,128]{2,1,0:T(8,128)(2,1)S(1)} %collective-permute-done.3.refs_3_.after), channel_id=1, source_target_pairs={{0,4},{4,8},{8,12},{1,5},{5,9},{9,13},{16,20},{20,24},{24,28},{17,... | collective-permute-start | bytes 786440 | tf_op jit(solution)/shard_map/ppermute | solution.py:663
  25.5 1.0 collective-permute-done.1.refs_3_.after
  26.5 4.2 %collective-permute-start.2 = (bf16[2,512,128]{2,1,0:T(8,128)(2,1)}, bf16[2,512,128]{2,1,0:T(8,128)(2,1)}, u32[]{:S(2)}, u32[]{:S(2)}) collective-permute-start(bf16[2,512,128]{2,1,0:T(8,128)(2,1)} %collective-permute-done.1.refs_3_.after), channel_id=1, source_target_pairs={{0,4},{4,8},{8,12},{1,5},{5,9},{9,13},{16,20},{20,24},{24,28},{17,... | collective-permute-start | bytes 786440 | tf_op jit(solution)/shard_map/ppermute | solution.py:663
  30.7 0.9 copy-done.17
  31.7 0.8 copy-done.33
  32.4 5.7 %filterbank.4 = (bf16[2,16,2,16,128]{4,3,2,1,0:T(8,128)(2,1)S(1)}, bf16[2,16,2,16,128]{4,3,2,1,0:T(8,128)(2,1)S(1)}, bf16[2,16,2,16,128]{4,3,2,1,0:T(8,128)(2,1)...) custom-call(s32[12]{0:T(128)S(1)} %concatenate.3.meta.refs_0_, ...), custom_call_target="tpu_custom_call" | custom-call | flops 1000000 | bytes 262144 | tf_op jit(solution)/shard_map/filterbank/pallas_call | solution.py:315
  41.6 4.1 %collective-permute-start.11 = (bf16[2,512,128]{2,1,0:T(8,128)(2,1)}, bf16[2,512,128]{2,1,0:T(8,128)(2,1)}, u32[]{:S(2)}, u32[]{:S(2)}) collective-permute-start(bf16[2,512,128]{2,1,0:T(8,128)(2,1)} %follow.13.refs_3_), channel_id=1, source_target_pairs={{0,4},{4,8},{8,12},{1,5},{5,9},{9,13},{16,20},{20,24},{24,28},{17,... | collective-permute-start | bytes 786440 | tf_op jit(solution)/shard_map/ppermute | solution.py:663
  45.7 0.8 copy-done.34
  46.4 0.9 copy-done.39
  47.4 0.9 copy-done.42
  48.3 0.9 copy-done.45
  49.9 5.8 %filterbank.5 = (bf16[2,16,2,16,128]{4,3,2,1,0:T(8,128)(2,1)S(1)}, bf16[2,16,2,16,128]{4,3,2,1,0:T(8,128)(2,1)S(1)}, bf16[2,16,2,16,128]{4,3,2,1,0:T(8,128)(2,1)...) custom-call(s32[12]{0:T(128)S(1)} %concatenate.3.meta.refs_0_, ...), custom_call_target="tpu_custom_call", output_to_operand_aliasing={{0}: (11, {}), {1}: (12, {}), {2}: (13, {}), {3}: (14, {})} | custom-call | flops 1000000 | bytes 262144 | tf_op jit(solution)/shard_map/filterbank/pallas_call | solution.py:315
  58.4 0.7 copy-done.23
  59.2 2.6 %collective-permute-start.9 = (bf16[2,512,128]{2,1,0:T(8,128)(2,1)}, bf16[2,512,128]{2,1,0:T(8,128)(2,1)S(1)}, u32[]{:S(2)}, u32[]{:S(2)}) collective-permute-start(bf16[2,512,128]{2,1,0:T(8,128)(2,1)} %follow.11.refs_3_), channel_id=1, source_target_pairs={{0,4},{4,8},{8,12},{1,5},{5,9},{9,13},{16,20},{20,24},{24,28},{17,... | collective-permute-start | bytes 786440 | tf_op jit(solution)/shard_map/ppermute | solution.py:663
  61.8 1.6 %collective-permute-start.5 = (bf16[2,16,2,16,128]{4,3,2,1,0:T(8,128)(2,1)}, bf16[2,16,2,16,128]{4,3,2,1,0:T(8,128)(2,1)S(1)}, u32[]{:S(2)}, u32[]{:S(2)}) collective-permute-start(bf16[2,16,2,16,128]{4,3,2,1,0:T(8,128)(2,1)} %copy-done.40), channel_id=1, source_target_pairs={{0,1},{1,0},{2,3},{3,2},{4,5},{5,4},{6,7},{7,6},{8,9},{9,8},{10,11... | collective-permute-start | bytes 786440 | tf_op jit(solution)/shard_map/ppermute | solution.py:680
  63.4 2.0 %collective-permute-start.7 = (bf16[2,16,2,16,128]{4,3,2,1,0:T(8,128)(2,1)}, bf16[2,16,2,16,128]{4,3,2,1,0:T(8,128)(2,1)S(1)}, u32[]{:S(2)}, u32[]{:S(2)}) collective-permute-start(bf16[2,16,2,16,128]{4,3,2,1,0:T(8,128)(2,1)} %copy-done.46), channel_id=1, source_target_pairs={{0,3},{1,2},{2,1},{3,0},{4,7},{5,6},{6,5},{7,4},{8,11},{9,10},{10,... | collective-permute-start | bytes 786440 | tf_op jit(solution)/shard_map/ppermute | solution.py:680
  65.4 0.9 copy-done.19
  66.3 0.8 copy-done.35
  67.8 5.7 %filterbank.6 = (bf16[2,16,2,16,128]{4,3,2,1,0:T(8,128)(2,1)S(1)}, bf16[2,16,2,16,128]{4,3,2,1,0:T(8,128)(2,1)S(1)}, bf16[2,16,2,16,128]{4,3,2,1,0:T(8,128)(2,1)...) custom-call(s32[12]{0:T(128)S(1)} %concatenate.3.meta.refs_0_, ...), custom_call_target="tpu_custom_call" | custom-call | flops 1000000 | bytes 262144 | tf_op jit(solution)/shard_map/filterbank/pallas_call | solution.py:315
  73.5 5.2 %filterbank.7 = (bf16[2,16,2,16,128]{4,3,2,1,0:T(8,128)(2,1)S(1)}, bf16[2,16,2,16,128]{4,3,2,1,0:T(8,128)(2,1)S(1)}, bf16[2,16,2,16,128]{4,3,2,1,0:T(8,128)(2,1)...) custom-call(s32[12]{0:T(128)S(1)} %concatenate.3.meta.refs_0_, ...), custom_call_target="tpu_custom_call", output_to_operand_aliasing={{0}: (11, {}), {1}: (12, {}), {2}: (13, {}), {3}: (14, {})} | custom-call | flops 1000000 | bytes 262144 | tf_op jit(solution)/shard_map/filterbank/pallas_call | solution.py:315
  82.2 1.5 %collective-permute-start.12 = (bf16[2,16,2,16,128]{4,3,2,1,0:T(8,128)(2,1)}, bf16[2,16,2,16,128]{4,3,2,1,0:T(8,128)(2,1)S(1)}, u32[]{:S(2)}, u32[]{:S(2)}) collective-permute-start(bf16[2,16,2,16,128]{4,3,2,1,0:T(8,128)(2,1)} %follow.14), channel_id=1, source_target_pairs={{0,1},{1,0},{2,3},{3,2},{4,5},{5,4},{6,7},{7,6},{8,9},{9,8},{10,11... | collective-permute-start | bytes 786440 | tf_op jit(solution)/shard_map/ppermute | solution.py:680
  85.2 1.9 %collective-permute-start.14 = (bf16[2,16,2,16,128]{4,3,2,1,0:T(8,128)(2,1)}, bf16[2,16,2,16,128]{4,3,2,1,0:T(8,128)(2,1)S(1)}, u32[]{:S(2)}, u32[]{:S(2)}) collective-permute-start(bf16[2,16,2,16,128]{4,3,2,1,0:T(8,128)(2,1)} %follow.16), channel_id=1, source_target_pairs={{0,3},{1,2},{2,1},{3,0},{4,7},{5,6},{6,5},{7,4},{8,11},{9,10},{10,... | collective-permute-start | bytes 786440 | tf_op jit(solution)/shard_map/ppermute | solution.py:680
  87.6 3.5 %collective-permute-done.12.refs_6_ = bf16[2,16,2,16,128]{4,3,2,1,0:T(8,128)(2,1)S(1)} collective-permute-done((bf16[2,16,2,16,128]{4,3,2,1,0:T(8,128)(2,1)}, bf16[2,16,2,16,128]{4,3,2,1,0:T(8,128)(2,1)S(1)}, u32[]{:S(2)}, u32[]{:S(2)}) %collective-permute-start.12) | collective-permute-done | bytes 262176 | tf_op jit(solution)/shard_map/ppermute | solution.py:680
  91.1 2.7 %collective-permute-done.13.refs_7_ = bf16[2,16,2,16,128]{4,3,2,1,0:T(8,128)(2,1)S(1)} collective-permute-done((bf16[2,16,2,16,128]{4,3,2,1,0:T(8,128)(2,1)}, bf16[2,16,2,16,128]{4,3,2,1,0:T(8,128)(2,1)S(1)}, u32[]{:S(2)}, u32[]{:S(2)}) %collective-permute-start.13) | collective-permute-done | bytes 262176 | tf_op jit(solution)/shard_map/ppermute | solution.py:680
  93.8 4.8 %collective-permute-done.14.refs_8_ = bf16[2,16,2,16,128]{4,3,2,1,0:T(8,128)(2,1)S(1)} collective-permute-done((bf16[2,16,2,16,128]{4,3,2,1,0:T(8,128)(2,1)}, bf16[2,16,2,16,128]{4,3,2,1,0:T(8,128)(2,1)S(1)}, u32[]{:S(2)}, u32[]{:S(2)}) %collective-permute-start.14) | collective-permute-done | bytes 262176 | tf_op jit(solution)/shard_map/ppermute | solution.py:680
  99.2 0.9 copy-done.3
  100.2 0.9 copy-done.6
  101.1 0.9 copy-done.9
  102.1 8.6 %correlate_own.1 = (f32[544,128]{1,0:T(8,128)S(1)}, bf16[544,128]{1,0:T(8,128)(2,1)S(1)}, bf16[544,128]{1,0:T(8,128)(2,1)S(1)}, bf16[544,128]{1,0:T(8,128)(2,1)S(1)}) custom-call(s32[12]{0:T(128)S(1)} %concatenate.3.meta.refs_0_, bf16[2,16,2,16,128]{4,3,2,1,0:T(8,128)(2,1)S(1)} %copy-done.12, bf16[2,16,2,16,128]{4,3,2,1,0:T(8,128)(2,1)S(1)} %copy-done.3, ...), custom_call_target="tpu_custom_call" | custom-call | flops 1000000 | bytes 262144 | tf_op jit(solution)/shard_map/correlate_own/pallas_call | solution.py:484
  111.0 3.6 %collective-permute-start.17 = (bf16[544,128]{1,0:T(8,128)(2,1)S(1)}, bf16[544,128]{1,0:T(8,128)(2,1)S(1)}, u32[]{:S(2)}, u32[]{:S(2)}) collective-permute-start(bf16[544,128]{1,0:T(8,128)(2,1)S(1)} %get-tuple-element.62), channel_id=1, source_target_pairs={{0,12},{2,14},{4,0},{6,2},{8,4},{10,6},{12,8},{14,10},{1,13},{3,15... | collective-permute-start | bytes 417800 | tf_op jit(solution)/shard_map/ppermute | solution.py:698
  114.7 9.2 %correlate_cross.1 = (f32[512,128]{1,0:T(8,128)S(1)}, bf16[512,128]{1,0:T(8,128)(2,1)S(1)}, bf16[512,128]{1,0:T(8,128)(2,1)S(1)}, bf16[512,128]{1,0:T(8,128)(2,1)S(1)}) custom-call(s32[12]{0:T(128)S(1)} %concatenate.3.meta.refs_0_, bf16[2,16,2,16,128]{4,3,2,1,0:T(8,128)(2,1)S(1)} %copy-done.12, bf16[2,16,2,16,128]{4,3,2,1,0:T(8,128)(2,1)S(1)} %copy-done.4, ...), custom_call_target="tpu_custom_call" | custom-call | flops 1000000 | bytes 262144 | tf_op jit(solution)/shard_map/correlate_cross/pallas_call | solution.py:484
  127.7 1.4 collective-permute-start.27
  129.8 2.9 %collective-permute-start.28 = (bf16[512,128]{1,0:T(8,128)(2,1)}, bf16[512,128]{1,0:T(8,128)(2,1)S(1)}, u32[]{:S(2)}, u32[]{:S(2)}) collective-permute-start(bf16[512,128]{1,0:T(8,128)(2,1)} %follow.19), channel_id=1, source_target_pairs={{0,12},{2,14},{4,0},{6,2},{8,4},{10,6},{12,8},{14,10},{1,13},{3,15... | collective-permute-start | bytes 393224 | tf_op jit(solution)/shard_map/ppermute | solution.py:703
  132.8 2.3 %collective-permute-done.26.refs_6_ = bf16[512,128]{1,0:T(8,128)(2,1)S(1)} collective-permute-done((bf16[512,128]{1,0:T(8,128)(2,1)}, bf16[512,128]{1,0:T(8,128)(2,1)S(1)}, u32[]{:S(2)}, u32[]{:S(2)}) %collective-permute-start.26) | collective-permute-done | bytes 131104 | tf_op jit(solution)/shard_map/ppermute | solution.py:703
  135.1 4.0 %collective-permute-done.27.refs_7_ = bf16[512,128]{1,0:T(8,128)(2,1)S(1)} collective-permute-done((bf16[512,128]{1,0:T(8,128)(2,1)}, bf16[512,128]{1,0:T(8,128)(2,1)S(1)}, u32[]{:S(2)}, u32[]{:S(2)}) %collective-permute-start.27) | collective-permute-done | bytes 131104 | tf_op jit(solution)/shard_map/ppermute | solution.py:703
  139.1 0.8 collective-permute-done.28.refs_8_
  140.5 0.8 collective-permute-done.32.refs_12_
  141.3 0.9 copy-done.26
  142.2 0.9 copy-done.28
  143.1 0.9 copy-done.30
  144.0 5.2 %assemble.1 = f32[2,16,32,256]{3,2,1,0:T(8,128)} custom-call(s32[12]{0:T(128)S(1)} %concatenate.3.meta.refs_0_, f32[544,128]{1,0:T(8,128)S(1)} %get-tuple-element.59.refs_1_, bf16[544,128]{1,0:T(8,128)(2,1)S(1)} %copy-done.26, bf16[544,128]{1,0:T(8,128)(2,1)S(1)} %copy-done.28, bf16[544,128]{1,0:T(8,128)(2,1)S(1)} %copy-done.30, ...), custom_call_target="tpu_custom_call" | custom-call | flops 1000000 | bytes 262144 | tf_op jit(solution)/shard_map/assemble/pallas_call | solution.py:590
  (146 shorter events, 20.3 us)
Async XLA Ops:
  0.7 1.6 %copy-start = (bf16[2,8,65536]{2,1,0:T(8,128)(2,1)S(1)}, bf16[2,8,65536]{2,1,0:T(8,128)(2,1)}, u32[]{:S(2)}) copy-start(bf16[2,8,65536]{2,1,0:T(8,128)(2,1)} %block.3) | copy-start | bytes 6291460
  4.2 26.5 %copy-start.1 = (f32[16,64,128]{2,1,0:T(8,128)S(1)}, f32[16,64,128]{2,1,0:T(8,128)}, u32[]{:S(2)}) copy-start(f32[16,64,128]{2,1,0:T(8,128)} %constant.46.clone.refs_6_) | copy-start | bytes 1572868
  4.2 26.5 %copy-start.15 = (bf16[2,4,32,128]{3,2,1,0:T(8,128)(2,1)S(1)}, bf16[2,4,32,128]{3,2,1,0:T(8,128)(2,1)}, u32[]{:S(2)}) copy-start(bf16[2,4,32,128]{3,2,1,0:T(8,128)(2,1)} %constant.50.clone.refs_10_) | copy-start | bytes 196612
  4.2 26.5 %copy-start.31 = (bf16[128,128]{1,0:T(8,128)(2,1)S(1)}, bf16[128,128]{1,0:T(8,128)(2,1)}, u32[]{:S(2)}) copy-start(bf16[128,128]{1,0:T(8,128)(2,1)} %constant.47.clone.refs_7_) | copy-start | bytes 98308
  4.2 26.5 %copy-start.32 = (f32[64,128]{1,0:T(8,128)S(1)}, f32[64,128]{1,0:T(8,128)}, u32[]{:S(2)}) copy-start(f32[64,128]{1,0:T(8,128)} %constant.48.clone.refs_8_) | copy-start | bytes 98308
  4.3 26.4 %collective-permute-start = (bf16[4,2,512,128]{3,2,1,0:T(8,128)(2,1)S(1)}, bf16[4,2,512,128]{3,2,1,0:T(8,128)(2,1)S(1)}, u32[]{:S(2)}, u32[]{:S(2)}) collective-permute-start(bf16[4,2,512,128]{3,2,1,0:T(8,128)(2,1)S(1)} %pick.2.refs_1_.refs_5_), channel_id=1, source_target_pairs={{2,6},{6,10},{10,14},{3,7},{7,11},{11,15},{18,22},{22,26},{26,30},... | collective-permute-start | bytes 3145736 | tf_op jit(solution)/shard_map/ppermute | solution.py:657
  8.4 12.9 %collective-permute-start.3 = (bf16[2,512,128]{2,1,0:T(8,128)(2,1)S(1)}, bf16[2,512,128]{2,1,0:T(8,128)(2,1)S(1)}, u32[]{:S(2)}, u32[]{:S(2)}) collective-permute-start(bf16[2,512,128]{2,1,0:T(8,128)(2,1)S(1)} %get-tuple-element.37), channel_id=1, source_target_pairs={{0,2},{2,0},{4,6},{6,4},{8,10},{10,8},{12,14},{14,12},{1,3},{3,1},... | collective-permute-start | bytes 786440 | tf_op jit(solution)/shard_map/ppermute | solution.py:655
  14.2 12.3 %collective-permute-start.1 = (bf16[2,512,128]{2,1,0:T(8,128)(2,1)S(1)}, bf16[2,512,128]{2,1,0:T(8,128)(2,1)}, u32[]{:S(2)}, u32[]{:S(2)}) collective-permute-start(bf16[2,512,128]{2,1,0:T(8,128)(2,1)S(1)} %get-tuple-element.36), channel_id=1, source_target_pairs={{0,2},{2,0},{4,6},{6,4},{8,10},{10,8},{12,14},{14,12},{1,3},{3,1},... | collective-permute-start | bytes 786440 | tf_op jit(solution)/shard_map/ppermute | solution.py:655
  21.3 4.1 %copy-start.16 = (bf16[2,512,128]{2,1,0:T(8,128)(2,1)}, bf16[2,512,128]{2,1,0:T(8,128)(2,1)S(1)}, u32[]{:S(2)}) copy-start(bf16[2,512,128]{2,1,0:T(8,128)(2,1)S(1)} %collective-permute-done.3.refs_3_.after) | copy-start | bytes 786436
  21.3 9.3 %collective-permute-start.4 = (bf16[2,512,128]{2,1,0:T(8,128)(2,1)S(1)}, bf16[2,512,128]{2,1,0:T(8,128)(2,1)}, u32[]{:S(2)}, u32[]{:S(2)}) collective-permute-start(bf16[2,512,128]{2,1,0:T(8,128)(2,1)S(1)} %collective-permute-done.3.refs_3_.after), channel_id=1, source_target_pairs={{0,4},{4,8},{8,12},{1,5},{5,9},{9,13},{16,20},{20,24},{24,28},{17,... | collective-permute-start | bytes 786440 | tf_op jit(solution)/shard_map/ppermute | solution.py:663
  25.5 15.3 %collective-permute-start.10 = (bf16[2,512,128]{2,1,0:T(8,128)(2,1)}, bf16[2,512,128]{2,1,0:T(8,128)(2,1)S(1)}, u32[]{:S(2)}, u32[]{:S(2)}) collective-permute-start(bf16[2,512,128]{2,1,0:T(8,128)(2,1)} %follow.12), channel_id=1, source_target_pairs={{0,2},{2,0},{4,6},{6,4},{8,10},{10,8},{12,14},{14,12},{1,3},{3,1},... | collective-permute-start | bytes 786440 | tf_op jit(solution)/shard_map/ppermute | solution.py:655
  26.5 19.2 %collective-permute-start.2 = (bf16[2,512,128]{2,1,0:T(8,128)(2,1)}, bf16[2,512,128]{2,1,0:T(8,128)(2,1)}, u32[]{:S(2)}, u32[]{:S(2)}) collective-permute-start(bf16[2,512,128]{2,1,0:T(8,128)(2,1)} %collective-permute-done.1.refs_3_.after), channel_id=1, source_target_pairs={{0,4},{4,8},{8,12},{1,5},{5,9},{9,13},{16,20},{20,24},{24,28},{17,... | collective-permute-start | bytes 786440 | tf_op jit(solution)/shard_map/ppermute | solution.py:663
  30.7 27.8 %collective-permute-start.8 = (bf16[2,512,128]{2,1,0:T(8,128)(2,1)}, bf16[2,512,128]{2,1,0:T(8,128)(2,1)S(1)}, u32[]{:S(2)}, u32[]{:S(2)}) collective-permute-start(bf16[2,512,128]{2,1,0:T(8,128)(2,1)} %follow.10), channel_id=1, source_target_pairs={{0,2},{2,0},{4,6},{6,4},{8,10},{10,8},{12,14},{14,12},{1,3},{3,1},... | collective-permute-start | bytes 786440 | tf_op jit(solution)/shard_map/ppermute | solution.py:655
  30.7 1.0 copy-start.17
  41.6 23.8 %collective-permute-start.11 = (bf16[2,512,128]{2,1,0:T(8,128)(2,1)}, bf16[2,512,128]{2,1,0:T(8,128)(2,1)}, u32[]{:S(2)}, u32[]{:S(2)}) collective-permute-start(bf16[2,512,128]{2,1,0:T(8,128)(2,1)} %follow.13.refs_3_), channel_id=1, source_target_pairs={{0,4},{4,8},{8,12},{1,5},{5,9},{9,13},{16,20},{20,24},{24,28},{17,... | collective-permute-start | bytes 786440 | tf_op jit(solution)/shard_map/ppermute | solution.py:663
  58.4 5.0 %copy-start.11 = (bf16[2,16,2,16,128]{4,3,2,1,0:T(8,128)(2,1)}, bf16[2,16,2,16,128]{4,3,2,1,0:T(8,128)(2,1)S(1)}, u32[]{:S(2)}) copy-start(bf16[2,16,2,16,128]{4,3,2,1,0:T(8,128)(2,1)S(1)} %get-tuple-element.43.refs_1_) | copy-start | bytes 786436
  59.2 14.3 %collective-permute-start.9 = (bf16[2,512,128]{2,1,0:T(8,128)(2,1)}, bf16[2,512,128]{2,1,0:T(8,128)(2,1)S(1)}, u32[]{:S(2)}, u32[]{:S(2)}) collective-permute-start(bf16[2,512,128]{2,1,0:T(8,128)(2,1)} %follow.11.refs_3_), channel_id=1, source_target_pairs={{0,4},{4,8},{8,12},{1,5},{5,9},{9,13},{16,20},{20,24},{24,28},{17,... | collective-permute-start | bytes 786440 | tf_op jit(solution)/shard_map/ppermute | solution.py:663
  61.8 19.7 %collective-permute-start.5 = (bf16[2,16,2,16,128]{4,3,2,1,0:T(8,128)(2,1)}, bf16[2,16,2,16,128]{4,3,2,1,0:T(8,128)(2,1)S(1)}, u32[]{:S(2)}, u32[]{:S(2)}) collective-permute-start(bf16[2,16,2,16,128]{4,3,2,1,0:T(8,128)(2,1)} %copy-done.40), channel_id=1, source_target_pairs={{0,1},{1,0},{2,3},{3,2},{4,5},{5,4},{6,7},{7,6},{8,9},{9,8},{10,11... | collective-permute-start | bytes 786440 | tf_op jit(solution)/shard_map/ppermute | solution.py:680
  63.4 20.3 %collective-permute-start.6 = (bf16[2,16,2,16,128]{4,3,2,1,0:T(8,128)(2,1)}, bf16[2,16,2,16,128]{4,3,2,1,0:T(8,128)(2,1)S(1)}, u32[]{:S(2)}, u32[]{:S(2)}) collective-permute-start(bf16[2,16,2,16,128]{4,3,2,1,0:T(8,128)(2,1)} %copy-done.43), channel_id=1, source_target_pairs={{0,2},{1,3},{2,0},{3,1},{4,6},{5,7},{6,4},{7,5},{8,10},{9,11},{10,... | collective-permute-start | bytes 786440 | tf_op jit(solution)/shard_map/ppermute | solution.py:680
  63.4 21.0 %collective-permute-start.7 = (bf16[2,16,2,16,128]{4,3,2,1,0:T(8,128)(2,1)}, bf16[2,16,2,16,128]{4,3,2,1,0:T(8,128)(2,1)S(1)}, u32[]{:S(2)}, u32[]{:S(2)}) collective-permute-start(bf16[2,16,2,16,128]{4,3,2,1,0:T(8,128)(2,1)} %copy-done.46), channel_id=1, source_target_pairs={{0,3},{1,2},{2,1},{3,0},{4,7},{5,6},{6,5},{7,4},{8,11},{9,10},{10,... | collective-permute-start | bytes 786440 | tf_op jit(solution)/shard_map/ppermute | solution.py:680
  65.4 21.7 %collective-permute-start.18 = (bf16[2,16,2,16,128]{4,3,2,1,0:T(8,128)(2,1)}, bf16[2,16,2,16,128]{4,3,2,1,0:T(8,128)(2,1)}, u32[]{:S(2)}, u32[]{:S(2)}) collective-permute-start(bf16[2,16,2,16,128]{4,3,2,1,0:T(8,128)(2,1)} %copy-done.11), channel_id=1, source_target_pairs={{0,16},{16,0},{1,17},{17,1},{2,18},{18,2},{3,19},{19,3},{4,20},{20... | collective-permute-start | bytes 786440 | tf_op jit(solution)/shard_map/ppermute | solution.py:682
  65.4 1.0 copy-start.19
  67.8 5.7 %copy-start.24 = (bf16[2,512,128]{2,1,0:T(8,128)(2,1)S(1)}, bf16[2,512,128]{2,1,0:T(8,128)(2,1)}, u32[]{:S(2)}) copy-start(bf16[2,512,128]{2,1,0:T(8,128)(2,1)} %follow.11.refs_3_) | copy-start | bytes 786436
  81.5 17.7 %copy-start.12 = (bf16[2,16,2,16,128]{4,3,2,1,0:T(8,128)(2,1)S(1)}, bf16[2,16,2,16,128]{4,3,2,1,0:T(8,128)(2,1)}, u32[]{:S(2)}) copy-start(bf16[2,16,2,16,128]{4,3,2,1,0:T(8,128)(2,1)} %copy-done.11) | copy-start | bytes 786436
  81.5 12.3 %copy-start.14 = (bf16[2,16,2,16,128]{4,3,2,1,0:T(8,128)(2,1)S(1)}, bf16[2,16,2,16,128]{4,3,2,1,0:T(8,128)(2,1)}, u32[]{:S(2)}) copy-start(bf16[2,16,2,16,128]{4,3,2,1,0:T(8,128)(2,1)} %copy-done.13) | copy-start | bytes 786436
  82.2 32.5 %copy-start.4 = (bf16[2,16,2,16,128]{4,3,2,1,0:T(8,128)(2,1)S(1)}, bf16[2,16,2,16,128]{4,3,2,1,0:T(8,128)(2,1)}, u32[]{:S(2)}) copy-start(bf16[2,16,2,16,128]{4,3,2,1,0:T(8,128)(2,1)} %copy-done.2) | copy-start | bytes 786436
  82.2 8.9 %collective-permute-start.12 = (bf16[2,16,2,16,128]{4,3,2,1,0:T(8,128)(2,1)}, bf16[2,16,2,16,128]{4,3,2,1,0:T(8,128)(2,1)S(1)}, u32[]{:S(2)}, u32[]{:S(2)}) collective-permute-start(bf16[2,16,2,16,128]{4,3,2,1,0:T(8,128)(2,1)} %follow.14), channel_id=1, source_target_pairs={{0,1},{1,0},{2,3},{3,2},{4,5},{5,4},{6,7},{7,6},{8,9},{9,8},{10,11... | collective-permute-start | bytes 786440 | tf_op jit(solution)/shard_map/ppermute | solution.py:680
  84.4 30.2 %copy-start.7 = (bf16[2,16,2,16,128]{4,3,2,1,0:T(8,128)(2,1)S(1)}, bf16[2,16,2,16,128]{4,3,2,1,0:T(8,128)(2,1)}, u32[]{:S(2)}) copy-start(bf16[2,16,2,16,128]{4,3,2,1,0:T(8,128)(2,1)} %copy-done.5) | copy-start | bytes 786436
  84.4 9.4 %collective-permute-start.13 = (bf16[2,16,2,16,128]{4,3,2,1,0:T(8,128)(2,1)}, bf16[2,16,2,16,128]{4,3,2,1,0:T(8,128)(2,1)S(1)}, u32[]{:S(2)}, u32[]{:S(2)}) collective-permute-start(bf16[2,16,2,16,128]{4,3,2,1,0:T(8,128)(2,1)} %follow.15), channel_id=1, source_target_pairs={{0,2},{1,3},{2,0},{3,1},{4,6},{5,7},{6,4},{7,5},{8,10},{9,11},{10,... | collective-permute-start | bytes 786440 | tf_op jit(solution)/shard_map/ppermute | solution.py:680
  85.2 13.5 %collective-permute-start.14 = (bf16[2,16,2,16,128]{4,3,2,1,0:T(8,128)(2,1)}, bf16[2,16,2,16,128]{4,3,2,1,0:T(8,128)(2,1)S(1)}, u32[]{:S(2)}, u32[]{:S(2)}) collective-permute-start(bf16[2,16,2,16,128]{4,3,2,1,0:T(8,128)(2,1)} %follow.16), channel_id=1, source_target_pairs={{0,3},{1,2},{2,1},{3,0},{4,7},{5,6},{6,5},{7,4},{8,11},{9,10},{10,... | collective-permute-start | bytes 786440 | tf_op jit(solution)/shard_map/ppermute | solution.py:680
  87.1 11.5 %collective-permute-start.19 = (bf16[2,16,2,16,128]{4,3,2,1,0:T(8,128)(2,1)}, bf16[2,16,2,16,128]{4,3,2,1,0:T(8,128)(2,1)S(1)}, u32[]{:S(2)}, u32[]{:S(2)}) collective-permute-start(bf16[2,16,2,16,128]{4,3,2,1,0:T(8,128)(2,1)} %copy-done.2), channel_id=1, source_target_pairs={{0,16},{16,0},{1,17},{17,1},{2,18},{18,2},{3,19},{19,3},{4,20},{20... | collective-permute-start | bytes 786440 | tf_op jit(solution)/shard_map/ppermute | solution.py:682
  87.1 12.0 %collective-permute-start.20 = (bf16[2,16,2,16,128]{4,3,2,1,0:T(8,128)(2,1)}, bf16[2,16,2,16,128]{4,3,2,1,0:T(8,128)(2,1)S(1)}, u32[]{:S(2)}, u32[]{:S(2)}) collective-permute-start(bf16[2,16,2,16,128]{4,3,2,1,0:T(8,128)(2,1)} %copy-done.5), channel_id=1, source_target_pairs={{0,16},{16,0},{1,17},{17,1},{2,18},{18,2},{3,19},{19,3},{4,20},{20... | collective-permute-start | bytes 786440 | tf_op jit(solution)/shard_map/ppermute | solution.py:682
  91.1 19.6 %collective-permute-start.21 = (bf16[2,16,2,16,128]{4,3,2,1,0:T(8,128)(2,1)}, bf16[2,16,2,16,128]{4,3,2,1,0:T(8,128)(2,1)S(1)}, u32[]{:S(2)}, u32[]{:S(2)}) collective-permute-start(bf16[2,16,2,16,128]{4,3,2,1,0:T(8,128)(2,1)} %copy-done.8), channel_id=1, source_target_pairs={{0,16},{16,0},{1,17},{17,1},{2,18},{18,2},{3,19},{19,3},{4,20},{20... | collective-permute-start | bytes 786440 | tf_op jit(solution)/shard_map/ppermute | solution.py:682
  93.8 17.0 %collective-permute-start.22 = (bf16[2,16,2,16,128]{4,3,2,1,0:T(8,128)(2,1)S(1)}, bf16[2,16,2,16,128]{4,3,2,1,0:T(8,128)(2,1)S(1)}, u32[]{:S(2)}, u32[]{:S(2)}) collective-permute-start(bf16[2,16,2,16,128]{4,3,2,1,0:T(8,128)(2,1)S(1)} %copy-done.14), channel_id=1, source_target_pairs={{0,16},{16,0},{1,17},{17,1},{2,18},{18,2},{3,19},{19,3},{4,20},{20... | collective-permute-start | bytes 786440 | tf_op jit(solution)/shard_map/ppermute | solution.py:682
  98.6 12.4 %collective-permute-start.23 = (bf16[2,16,2,16,128]{4,3,2,1,0:T(8,128)(2,1)S(1)}, bf16[2,16,2,16,128]{4,3,2,1,0:T(8,128)(2,1)S(1)}, u32[]{:S(2)}, u32[]{:S(2)}) collective-permute-start(bf16[2,16,2,16,128]{4,3,2,1,0:T(8,128)(2,1)S(1)} %collective-permute-done.12.refs_6_), channel_id=1, source_target_pairs={{0,16},{16,0},{1,17},{17,1},{2,18},{18,2},{3,19},{19,3},{4,20},{20... | collective-permute-start | bytes 786440 | tf_op jit(solution)/shard_map/ppermute | solution.py:682
  98.6 16.0 %collective-permute-start.24 = (bf16[2,16,2,16,128]{4,3,2,1,0:T(8,128)(2,1)S(1)}, bf16[2,16,2,16,128]{4,3,2,1,0:T(8,128)(2,1)S(1)}, u32[]{:S(2)}, u32[]{:S(2)}) collective-permute-start(bf16[2,16,2,16,128]{4,3,2,1,0:T(8,128)(2,1)S(1)} %collective-permute-done.13.refs_7_), channel_id=1, source_target_pairs={{0,16},{16,0},{1,17},{17,1},{2,18},{18,2},{3,19},{19,3},{4,20},{20... | collective-permute-start | bytes 786440 | tf_op jit(solution)/shard_map/ppermute | solution.py:682
  99.1 15.5 %collective-permute-start.25 = (bf16[2,16,2,16,128]{4,3,2,1,0:T(8,128)(2,1)S(1)}, bf16[2,16,2,16,128]{4,3,2,1,0:T(8,128)(2,1)S(1)}, u32[]{:S(2)}, u32[]{:S(2)}) collective-permute-start(bf16[2,16,2,16,128]{4,3,2,1,0:T(8,128)(2,1)S(1)} %collective-permute-done.14.refs_8_), channel_id=1, source_target_pairs={{0,16},{16,0},{1,17},{17,1},{2,18},{18,2},{3,19},{19,3},{4,20},{20... | collective-permute-start | bytes 786440 | tf_op jit(solution)/shard_map/ppermute | solution.py:682
  102.1 12.6 %copy-start.10 = (bf16[2,16,2,16,128]{4,3,2,1,0:T(8,128)(2,1)S(1)}, bf16[2,16,2,16,128]{4,3,2,1,0:T(8,128)(2,1)}, u32[]{:S(2)}) copy-start(bf16[2,16,2,16,128]{4,3,2,1,0:T(8,128)(2,1)} %copy-done.8) | copy-start | bytes 786436
  110.7 15.2 %collective-permute-start.15 = (bf16[544,128]{1,0:T(8,128)(2,1)S(1)}, bf16[544,128]{1,0:T(8,128)(2,1)S(1)}, u32[]{:S(2)}, u32[]{:S(2)}) collective-permute-start(bf16[544,128]{1,0:T(8,128)(2,1)S(1)} %get-tuple-element.60), channel_id=1, source_target_pairs={{0,4},{2,6},{4,8},{6,10},{8,12},{10,14},{12,0},{14,2},{1,5},{3,7},... | collective-permute-start | bytes 417800 | tf_op jit(solution)/shard_map/ppermute | solution.py:698
  110.8 16.3 %collective-permute-start.16 = (bf16[544,128]{1,0:T(8,128)(2,1)S(1)}, bf16[544,128]{1,0:T(8,128)(2,1)S(1)}, u32[]{:S(2)}, u32[]{:S(2)}) collective-permute-start(bf16[544,128]{1,0:T(8,128)(2,1)S(1)} %get-tuple-element.61), channel_id=1, source_target_pairs={{0,8},{2,10},{4,12},{6,14},{8,0},{10,2},{12,4},{14,6},{1,9},{3,11}... | collective-permute-start | bytes 417800 | tf_op jit(solution)/shard_map/ppermute | solution.py:698
  111.0 18.2 %collective-permute-start.17 = (bf16[544,128]{1,0:T(8,128)(2,1)S(1)}, bf16[544,128]{1,0:T(8,128)(2,1)S(1)}, u32[]{:S(2)}, u32[]{:S(2)}) collective-permute-start(bf16[544,128]{1,0:T(8,128)(2,1)S(1)} %get-tuple-element.62), channel_id=1, source_target_pairs={{0,12},{2,14},{4,0},{6,2},{8,4},{10,6},{12,8},{14,10},{1,13},{3,15... | collective-permute-start | bytes 417800 | tf_op jit(solution)/shard_map/ppermute | solution.py:698
  126.6 8.5 %collective-permute-start.26 = (bf16[512,128]{1,0:T(8,128)(2,1)}, bf16[512,128]{1,0:T(8,128)(2,1)S(1)}, u32[]{:S(2)}, u32[]{:S(2)}) collective-permute-start(bf16[512,128]{1,0:T(8,128)(2,1)} %follow.17), channel_id=1, source_target_pairs={{0,4},{2,6},{4,8},{6,10},{8,12},{10,14},{12,0},{14,2},{1,5},{3,7},... | collective-permute-start | bytes 393224 | tf_op jit(solution)/shard_map/ppermute | solution.py:703
  127.7 11.4 %collective-permute-start.27 = (bf16[512,128]{1,0:T(8,128)(2,1)}, bf16[512,128]{1,0:T(8,128)(2,1)S(1)}, u32[]{:S(2)}, u32[]{:S(2)}) collective-permute-start(bf16[512,128]{1,0:T(8,128)(2,1)} %follow.18), channel_id=1, source_target_pairs={{0,8},{2,10},{4,12},{6,14},{8,0},{10,2},{12,4},{14,6},{1,9},{3,11}... | collective-permute-start | bytes 393224 | tf_op jit(solution)/shard_map/ppermute | solution.py:703
  129.2 10.8 %collective-permute-start.29 = (f32[512,128]{1,0:T(8,128)S(1)}, f32[512,128]{1,0:T(8,128)S(1)}, u32[]{:S(2)}, u32[]{:S(2)}) collective-permute-start(f32[512,128]{1,0:T(8,128)S(1)} %get-tuple-element.63.refs_5_), channel_id=1, source_target_pairs={{0,16},{16,0},{1,17},{17,1},{2,18},{18,2},{3,19},{19,3},{4,20},{20... | collective-permute-start | bytes 786440 | tf_op jit(solution)/shard_map/ppermute | solution.py:704
  129.8 10.1 %collective-permute-start.28 = (bf16[512,128]{1,0:T(8,128)(2,1)}, bf16[512,128]{1,0:T(8,128)(2,1)S(1)}, u32[]{:S(2)}, u32[]{:S(2)}) collective-permute-start(bf16[512,128]{1,0:T(8,128)(2,1)} %follow.19), channel_id=1, source_target_pairs={{0,12},{2,14},{4,0},{6,2},{8,4},{10,6},{12,8},{14,10},{1,13},{3,15... | collective-permute-start | bytes 393224 | tf_op jit(solution)/shard_map/ppermute | solution.py:703
  135.1 4.9 %collective-permute-start.30 = (bf16[512,128]{1,0:T(8,128)(2,1)S(1)}, bf16[512,128]{1,0:T(8,128)(2,1)S(1)}, u32[]{:S(2)}, u32[]{:S(2)}) collective-permute-start(bf16[512,128]{1,0:T(8,128)(2,1)S(1)} %collective-permute-done.26.refs_6_), channel_id=1, source_target_pairs={{0,16},{16,0},{1,17},{17,1},{2,18},{18,2},{3,19},{19,3},{4,20},{20... | collective-permute-start | bytes 393224 | tf_op jit(solution)/shard_map/ppermute | solution.py:704
  139.1 1.3 collective-permute-start.31
  139.9 1.3 collective-permute-start.32
  (39 other events, 29.1 us)

commit v7 on v5

--- a/solution.py
+++ b/solution.py
@@ -22,7 +22,6 @@
 
 VMEM = pl.BlockSpec(memory_space=pltpu.VMEM)
 SMEM = pl.BlockSpec(memory_space=pltpu.SMEM)
-ANY = pl.BlockSpec(memory_space=pl.ANY)
 
 
 def params(mib):
@@ -128,17 +127,7 @@
 
 
 def follow(block, after):
-    def hand_on(block, after, out):
-        pass
-
-    return pl.pallas_call(
-        hand_on,
-        out_shape=jax.ShapeDtypeStruct(block.shape, block.dtype),
-        in_specs=[ANY, ANY],
-        out_specs=ANY,
-        input_output_aliases={0: 0},
-        name="follow",
-    )(block, after)
+    return lax.optimization_barrier((block, after))[0]
 
 
 HALF = 16
@@ -146,12 +135,12 @@
 
 
 def filterbank_kernel(index, before, frames, dests, per_ct, half_count, *refs):
-    meta, keep, halo_own, recv, halo_far, after, coef, first, tw_cos, tw_sin, last = refs[:11]
-    earlier = refs[11 : 11 + dests * (before > 0)]
-    refs = refs[11 + len(earlier) :]
+    meta, keep, halo_own, recv, halo_far, coef, first, tw_cos, tw_sin, last = refs[:10]
+    earlier = refs[10 : 10 + dests * (before > 0)]
+    refs = refs[10 + len(earlier) :]
     outs = refs[:dests]
-    raw, weights, grouped, sems = refs[dests : dests + 4]
-    filtered = refs[dests + 4 :]
+    raw, weights, grouped = refs[dests : dests + 3]
+    filtered = refs[dests + 3 :]
     block_rows = frames * ROWS
     total = PAIR * frames
     me, ct = meta[G_AT], meta[CT_AT]
@@ -163,20 +152,28 @@
     turned_in = lane >= across
     high = lane < RADIX
 
-    def bring(source, place, sem):
-        at = pl.multiple_of(place * block_rows, block_rows)
-        return pltpu.make_async_copy(source, raw.at[:, pl.ds(at, block_rows), :], sems.at[sem])
+    def bring(source, place):
+        tall = 128
+
+        def step(n, carry):
+            for part in range(2):
+                value = source[part, pl.ds(pl.multiple_of(n * tall, tall), tall), :]
+                at = pl.multiple_of(place * block_rows + n * tall, tall)
+                raw[part, pl.ds(at, tall), :] = value
+            return carry
+
+        lax.fori_loop(0, block_rows // tall, step, 0)
 
     @pl.when(me == 0)
     def _():
-        bring(halo_far, 0, 0).start()
+        bring(halo_far, 0)
 
     @pl.when(me != 0)
     def _():
-        bring(halo_own.at[index], 0, 0).start()
-
-    bring(keep.at[index], 1 + me, 1).start()
-    bring(recv, 2 - me, 2).start()
+        bring(halo_own.at[index], 0)
+
+    bring(keep.at[index], 1 + me)
+    bring(recv, 2 - me)
 
     back = lax.rem(LANES - across, LANES)
     for tap in range(TAPS):
@@ -185,10 +182,6 @@
         weights[tap] = pltpu.roll(jnp.where(turned_in, here, after), back, 1)
     for dest, old in zip(outs, earlier):
         dest[:before] = old[...]
-
-    bring(halo_far, 0, 0).wait()
-    bring(keep.at[index], 1 + me, 1).wait()
-    bring(recv, 2 - me, 2).wait()
 
     def filt(half, low, high_frame, band, part):
         size = high_frame - low
@@ -271,7 +264,7 @@
                 turn((half - 1) * HALF + n * SOME)
 
 
-def filterbank(index, meta, keep, halo_own, recv, halo_far, after, tables, earlier, dests):
+def filterbank(index, meta, keep, halo_own, recv, halo_far, tables, earlier, dests):
     frames = keep.shape[2] // ROWS
     size = tables[-1].shape[2] // 2
     per_ct = tables[-1].shape[1] // 2
@@ -283,19 +276,18 @@
             filterbank_kernel, index, before, frames, dests, per_ct, keep.shape[0]
         ),
         out_shape=[jax.ShapeDtypeStruct(shape, jnp.bfloat16)] * dests,
-        in_specs=[SMEM] + [ANY] * 5 + [VMEM] * (5 + len(earlier)),
+        in_specs=[SMEM] + [VMEM] * (9 + len(earlier)),
         out_specs=[VMEM] * dests,
         scratch_shapes=[
             pltpu.VMEM((2, all_rows, LANES), jnp.bfloat16),
             pltpu.VMEM((TAPS, ROWS, LANES), jnp.float32),
             pltpu.VMEM((PAIR * frames, LANES, LANES), jnp.bfloat16),
-            pltpu.SemaphoreType.DMA((3,)),
         ]
         + [pltpu.VMEM((2, (HALF + 1) * ROWS, LANES), jnp.float32)] * (PAIR * frames // HALF),
-        compiler_params=params(16),
+        compiler_params=params(12),
         cost_estimate=cost(10**6, 2**18),
         name="filterbank",
-    )(meta, keep, halo_own, recv, halo_far, after, *tables, *earlier)
+    )(meta, keep, halo_own, recv, halo_far, *tables, *earlier)
 
 
 SQUARE = [(p, q) for p in range(TILE) for q in range(TILE)]
@@ -436,7 +428,7 @@
             pltpu.VMEM((outer * rows, LANES), jnp.float32),
             pltpu.VMEM((2, TILE * TILE, outer * span, LANES), jnp.float32),
         ],
-        compiler_params=params(14 + inputs * steps * 4 * size * LANES * 4 // 2**20),
+        compiler_params=params(8 + inputs * steps * 4 * size * LANES * 4 // 2**20),
         cost_estimate=cost(10**6, 2**18),
         name=name,
     )(meta, *arrays)
@@ -511,7 +503,7 @@
         in_specs=[SMEM] + [VMEM] * (3 * outer),
         out_specs=VMEM,
         scratch_shapes=[pltpu.VMEM((own * 2 * own * span, LANES), jnp.float32)],
-        compiler_params=params(24),
+        compiler_params=params(10),
         cost_estimate=cost(10**6, 2**18),
         name="assemble",
     )(meta, *mine_in, *mine_across, *far_across)
@@ -573,9 +565,9 @@
     for c in range(half):
         block = follow(recvs[c], done[c - 2]) if c >= 2 else recvs[c]
         far = lax.ppermute(block, "tm", forward)
-        after = done[c - 1] if c else meta
+        far = follow(far, done[c - 1]) if c else far
         spectra = filterbank(
-            c, meta, keep, halo_own, recvs[c], far, after, tables, spectra, len(dests)
+            c, meta, keep, halo_own, recvs[c], far, tables, spectra, len(dests)
         )
         done.append(spectra[0])
         if c % JOIN < JOIN - 1:

time: 144 us -> 110 us (0.76)
  local copies, waits for them, and re-layouts: 35.3 us -> 2.35 us
  waiting for transfers between devices: 26.6 us -> 31.7 us
  starting transfers between devices: 40 us -> 37 us
  Pallas kernels: 40.9 us -> 38 us
    unnamed x112 -> x12, local copies, waits for them, and re-layouts: 34.6 us -> 1.61 us
    ppermute x4, starting transfers between devices: 8.61 us -> 6.04 us  [fast(): recvs.append(lax.ppermute(block, 'tm', swap))]
    pallas_call x4, Pallas kernels: 17.8 us -> 15.4 us  [filterbank(): pl.pallas_call(functools.partial(filterbank_kernel, index, before, frames...]
    ppermute x4, waiting for transfers between devices: 7.14 us -> 8.84 us  [fast(): recvs.append(lax.ppermute(block, 'tm', swap))]
  transfers between devices with their start and end apart: 33 -> 33, of which waited for: 7 -> 9; matrix products, arithmetic and copies ran while one was open for 1% -> 0% of each run, Pallas kernels for 25% -> 30%
where the time goes in v7:
time: 110 us; the launch traced here: 109 us
  Pallas kernels  38 us (35%)
  starting transfers between devices  37 us (34%)
  waiting for transfers between devices  31.7 us (29%)
  local copies, waits for them, and re-layouts  2.35 us (2%)
    pallas_call x2, Pallas kernels, correlate(): pl.pallas_call(functools.partial(correlate_kernel, layout), out_shape=sha...  15.5 us
    pallas_call x4, Pallas kernels, filterbank(): pl.pallas_call(functools.partial(filterbank_kernel, index, before, frames...  15.4 us
    ppermute x4, starting transfers between devices, fast(): far = lax.ppermute(block, 'tm', forward)  13.5 us
    ppermute x6, waiting for transfers between devices, fast(): block = lax.ppermute(block, ('tm', 'ct'), route)  11.3 us
    ppermute x3, waiting for transfers between devices, fast(): mine_across[r] = lax.ppermute(block, 'tm', route)  9.67 us
    ppermute x4, waiting for transfers between devices, fast(): recvs.append(lax.ppermute(block, 'tm', swap))  8.84 us
    ppermute x6, starting transfers between devices, fast(): block = lax.ppermute(block, ('tm', 'ct'), route)  7.11 us
    ppermute x4, starting transfers between devices, fast(): recvs.append(lax.ppermute(block, 'tm', swap))  6.04 us
  transfers between devices with their start and end apart: 33, of which 9 were waited for; matrix products, arithmetic and copies ran while one was open for 0% of the time, Pallas kernels for 30%

profile of v7, /device:TPU:0, one launch (start us, length us, event | category | flops | bytes accessed | tf_op | source)
XLA Modules:
  0.0 109.3 jit_solution(10787839276094217577)
XLA Ops:
  0.0 0.7 concatenate.3.meta.refs_0_
  0.7 1.6 %copy-done = bf16[2,8,65536]{2,1,0:T(8,128)(2,1)S(1)} copy-done((bf16[2,8,65536]{2,1,0:T(8,128)(2,1)S(1)}, bf16[2,8,65536]{2,1,0:T(8,128)(2,1)}, u32[]{:S(2)}) %copy-start) | copy-done | bytes 2097176
  2.3 0.0 copy-start.5
  2.4 1.7 %pick.2.refs_1_ = bf16[4,2,512,128]{3,2,1,0:T(8,128)(2,1)S(1)} custom-call(s32[12]{0:T(128)S(1)} %concatenate.3.meta.refs_0_, bf16[2,8,65536]{2,1,0:T(8,128)(2,1)S(1)} %copy-done), custom_call_target="tpu_custom_call" | custom-call | flops 1000000 | bytes 262144 | tf_op jit(solution)/shard_map/pick/pallas_call | solution.py:117
  4.1 0.7 collective-permute-start
  4.8 1.7 %pick.3 = (bf16[2,512,128]{2,1,0:T(8,128)(2,1)S(1)}, bf16[2,512,128]{2,1,0:T(8,128)(2,1)S(1)}, bf16[2,512,128]{2,1,0:T(8,128)(2,1)S(1)}, bf16[2,512,128]{2,1,0:T(8,128)(2,1)S(1)}) custom-call(s32[12]{0:T(128)S(1)} %concatenate.3.meta.refs_0_, bf16[2,8,65536]{2,1,0:T(8,128)(2,1)S(1)} %copy-done), custom_call_target="tpu_custom_call" | custom-call | flops 1000000 | bytes 262144 | tf_op jit(solution)/shard_map/pick/pallas_call | solution.py:117
  6.5 5.8 %collective-permute-start.3 = (bf16[2,512,128]{2,1,0:T(8,128)(2,1)S(1)}, bf16[2,512,128]{2,1,0:T(8,128)(2,1)S(1)}, u32[]{:S(2)}, u32[]{:S(2)}) collective-permute-start(bf16[2,512,128]{2,1,0:T(8,128)(2,1)S(1)} %get-tuple-element.47), channel_id=1, source_target_pairs={{0,2},{2,0},{4,6},{6,4},{8,10},{10,8},{12,14},{14,12},{1,3},{3,1},... | collective-permute-start | bytes 786440 | tf_op jit(solution)/shard_map/ppermute | solution.py:559
  12.3 0.1 collective-permute-start.1
  12.4 7.1 %collective-permute-done.3.refs_3_ = bf16[2,512,128]{2,1,0:T(8,128)(2,1)S(1)} collective-permute-done((bf16[2,512,128]{2,1,0:T(8,128)(2,1)S(1)}, bf16[2,512,128]{2,1,0:T(8,128)(2,1)S(1)}, u32[]{:S(2)}, u32[]{:S(2)}) %collective-permute-start.3) | collective-permute-done | bytes 262176 | tf_op jit(solution)/shard_map/ppermute | solution.py:559
  19.5 3.4 %collective-permute-start.4 = (bf16[2,512,128]{2,1,0:T(8,128)(2,1)S(1)}, bf16[2,512,128]{2,1,0:T(8,128)(2,1)S(1)}, u32[]{:S(2)}, u32[]{:S(2)}) collective-permute-start(bf16[2,512,128]{2,1,0:T(8,128)(2,1)S(1)} %collective-permute-done.3.refs_3_), channel_id=1, source_target_pairs={{0,4},{4,8},{8,12},{1,5},{5,9},{9,13},{16,20},{20,24},{24,28},{17,... | collective-permute-start | bytes 786440 | tf_op jit(solution)/shard_map/ppermute | solution.py:567
  22.9 0.1 collective-permute-start.10
  23.0 1.7 %collective-permute-done.1.refs_3_ = bf16[2,512,128]{2,1,0:T(8,128)(2,1)S(1)} collective-permute-done((bf16[2,512,128]{2,1,0:T(8,128)(2,1)S(1)}, bf16[2,512,128]{2,1,0:T(8,128)(2,1)S(1)}, u32[]{:S(2)}, u32[]{:S(2)}) %collective-permute-start.1) | collective-permute-done | bytes 262176 | tf_op jit(solution)/shard_map/ppermute | solution.py:559
  24.7 3.4 %collective-permute-start.2 = (bf16[2,512,128]{2,1,0:T(8,128)(2,1)S(1)}, bf16[2,512,128]{2,1,0:T(8,128)(2,1)S(1)}, u32[]{:S(2)}, u32[]{:S(2)}) collective-permute-start(bf16[2,512,128]{2,1,0:T(8,128)(2,1)S(1)} %collective-permute-done.1.refs_3_), channel_id=1, source_target_pairs={{0,4},{4,8},{8,12},{1,5},{5,9},{9,13},{16,20},{20,24},{24,28},{17,... | collective-permute-start | bytes 786440 | tf_op jit(solution)/shard_map/ppermute | solution.py:567
  28.1 0.1 collective-permute-start.8
  28.2 0.0 collective-permute-done.refs_2_
  28.3 3.8 %filterbank.4 = (bf16[1,16,2,16,128]{4,3,2,1,0:T(8,128)(2,1)S(1)}, bf16[1,16,2,16,128]{4,3,2,1,0:T(8,128)(2,1)S(1)}, bf16[1,16,2,16,128]{4,3,2,1,0:T(8,128)(2,1)S(1)}, bf16[1,16,2,16,128]{4,3,2,1,0:T(8,128)(2,1)S(1)}) custom-call(s32[12]{0:T(128)S(1)} %concatenate.3.meta.refs_0_, bf16[4,2,512,128]{3,2,1,0:T(8,128)(2,1)S(1)} %pick.2.refs_1_, ...), custom_call_target="tpu_custom_call" | custom-call | flops 1000000 | bytes 262144 | tf_op jit(solution)/shard_map/filterbank/pallas_call | solution.py:274
  32.1 3.9 %collective-permute-start.11 = (bf16[2,512,128]{2,1,0:T(8,128)(2,1)S(1)}, bf16[2,512,128]{2,1,0:T(8,128)(2,1)S(1)}, u32[]{:S(2)}, u32[]{:S(2)}) collective-permute-start(bf16[2,512,128]{2,1,0:T(8,128)(2,1)S(1)} %collective-permute-done.10.refs_3_), channel_id=1, source_target_pairs={{0,4},{4,8},{8,12},{1,5},{5,9},{9,13},{16,20},{20,24},{24,28},{17,... | collective-permute-start | bytes 786440 | tf_op jit(solution)/shard_map/ppermute | solution.py:567
  36.0 3.8 %filterbank.5 = (bf16[2,16,2,16,128]{4,3,2,1,0:T(8,128)(2,1)S(1)}, bf16[2,16,2,16,128]{4,3,2,1,0:T(8,128)(2,1)S(1)}, bf16[2,16,2,16,128]{4,3,2,1,0:T(8,128)(2,1)S(1)}, bf16[2,16,2,16,128]{4,3,2,1,0:T(8,128)(2,1)S(1)}) custom-call(s32[12]{0:T(128)S(1)} %concatenate.3.meta.refs_0_, bf16[4,2,512,128]{3,2,1,0:T(8,128)(2,1)S(1)} %pick.2.refs_1_, ...), custom_call_target="tpu_custom_call" | custom-call | flops 1000000 | bytes 262144 | tf_op jit(solution)/shard_map/filterbank/pallas_call | solution.py:274
  39.9 2.8 %collective-permute-start.9 = (bf16[2,512,128]{2,1,0:T(8,128)(2,1)S(1)}, bf16[2,512,128]{2,1,0:T(8,128)(2,1)S(1)}, u32[]{:S(2)}, u32[]{:S(2)}) collective-permute-start(bf16[2,512,128]{2,1,0:T(8,128)(2,1)S(1)} %collective-permute-done.8.refs_3_), channel_id=1, source_target_pairs={{0,4},{4,8},{8,12},{1,5},{5,9},{9,13},{16,20},{20,24},{24,28},{17,... | collective-permute-start | bytes 786440 | tf_op jit(solution)/shard_map/ppermute | solution.py:567
  42.7 0.3 collective-permute-start.7
  43.0 2.8 %collective-permute-start.6 = (bf16[2,16,2,16,128]{4,3,2,1,0:T(8,128)(2,1)S(1)}, bf16[2,16,2,16,128]{4,3,2,1,0:T(8,128)(2,1)S(1)}, u32[]{:S(2)}, u32[]{:S(2)}) collective-permute-start(bf16[2,16,2,16,128]{4,3,2,1,0:T(8,128)(2,1)S(1)} %get-tuple-element.55), channel_id=1, source_target_pairs={{0,2},{1,3},{2,0},{3,1},{4,6},{5,7},{6,4},{7,5},{8,10},{9,11},{10,... | collective-permute-start | bytes 786440 | tf_op jit(solution)/shard_map/ppermute | solution.py:584
  45.7 0.5 collective-permute-start.5
  46.2 3.8 %filterbank.6 = (bf16[1,16,2,16,128]{4,3,2,1,0:T(8,128)(2,1)S(1)}, bf16[1,16,2,16,128]{4,3,2,1,0:T(8,128)(2,1)S(1)}, bf16[1,16,2,16,128]{4,3,2,1,0:T(8,128)(2,1)S(1)}, bf16[1,16,2,16,128]{4,3,2,1,0:T(8,128)(2,1)S(1)}) custom-call(s32[12]{0:T(128)S(1)} %concatenate.3.meta.refs_0_, bf16[4,2,512,128]{3,2,1,0:T(8,128)(2,1)S(1)} %pick.2.refs_1_, ...), custom_call_target="tpu_custom_call" | custom-call | flops 1000000 | bytes 262144 | tf_op jit(solution)/shard_map/filterbank/pallas_call | solution.py:274
  50.0 0.0 collective-permute-done.9.refs_4_
  50.0 4.0 %filterbank.7 = (bf16[2,16,2,16,128]{4,3,2,1,0:T(8,128)(2,1)S(1)}, bf16[2,16,2,16,128]{4,3,2,1,0:T(8,128)(2,1)S(1)}, bf16[2,16,2,16,128]{4,3,2,1,0:T(8,128)(2,1)S(1)}, bf16[2,16,2,16,128]{4,3,2,1,0:T(8,128)(2,1)S(1)}) custom-call(s32[12]{0:T(128)S(1)} %concatenate.3.meta.refs_0_, bf16[4,2,512,128]{3,2,1,0:T(8,128)(2,1)S(1)} %pick.2.refs_1_, ...), custom_call_target="tpu_custom_call" | custom-call | flops 1000000 | bytes 262144 | tf_op jit(solution)/shard_map/filterbank/pallas_call | solution.py:274
  54.1 1.0 collective-permute-start.14
  55.1 2.0 %collective-permute-start.13 = (bf16[2,16,2,16,128]{4,3,2,1,0:T(8,128)(2,1)S(1)}, bf16[2,16,2,16,128]{4,3,2,1,0:T(8,128)(2,1)S(1)}, u32[]{:S(2)}, u32[]{:S(2)}) collective-permute-start(bf16[2,16,2,16,128]{4,3,2,1,0:T(8,128)(2,1)S(1)} %get-tuple-element.73), channel_id=1, source_target_pairs={{0,2},{1,3},{2,0},{3,1},{4,6},{5,7},{6,4},{7,5},{8,10},{9,11},{10,... | collective-permute-start | bytes 786440 | tf_op jit(solution)/shard_map/ppermute | solution.py:584
  57.1 0.5 collective-permute-start.12
  57.6 0.5 collective-permute-start.19
  58.1 6.0 %collective-permute-done.14.refs_8_ = bf16[2,16,2,16,128]{4,3,2,1,0:T(8,128)(2,1)S(1)} collective-permute-done((bf16[2,16,2,16,128]{4,3,2,1,0:T(8,128)(2,1)S(1)}, bf16[2,16,2,16,128]{4,3,2,1,0:T(8,128)(2,1)S(1)}, u32[]{:S(2)}, u32[]{:S(2)}) %collective-permute-start.14) | collective-permute-done | bytes 262176 | tf_op jit(solution)/shard_map/ppermute | solution.py:584
  64.2 5.3 %collective-permute-done.13.refs_7_ = bf16[2,16,2,16,128]{4,3,2,1,0:T(8,128)(2,1)S(1)} collective-permute-done((bf16[2,16,2,16,128]{4,3,2,1,0:T(8,128)(2,1)S(1)}, bf16[2,16,2,16,128]{4,3,2,1,0:T(8,128)(2,1)S(1)}, u32[]{:S(2)}, u32[]{:S(2)}) %collective-permute-start.13) | collective-permute-done | bytes 262176 | tf_op jit(solution)/shard_map/ppermute | solution.py:584
  69.5 0.5 collective-permute-start.25
  70.0 0.1 collective-permute-start.24
  70.1 0.4 collective-permute-start.23
  70.5 7.8 %correlate_own.1 = (f32[544,128]{1,0:T(8,128)S(1)}, bf16[544,128]{1,0:T(8,128)(2,1)S(1)}, bf16[544,128]{1,0:T(8,128)(2,1)S(1)}, bf16[544,128]{1,0:T(8,128)(2,1)S(1)}) custom-call(s32[12]{0:T(128)S(1)} %concatenate.3.meta.refs_0_, bf16[2,16,2,16,128]{4,3,2,1,0:T(8,128)(2,1)S(1)} %get-tuple-element.53.refs_1_, ...), custom_call_target="tpu_custom_call" | custom-call | flops 1000000 | bytes 262144 | tf_op jit(solution)/shard_map/correlate_own/pallas_call | solution.py:421
  78.3 1.8 %collective-permute-start.17 = (bf16[544,128]{1,0:T(8,128)(2,1)S(1)}, bf16[544,128]{1,0:T(8,128)(2,1)S(1)}, u32[]{:S(2)}, u32[]{:S(2)}) collective-permute-start(bf16[544,128]{1,0:T(8,128)(2,1)S(1)} %get-tuple-element.79), channel_id=1, source_target_pairs={{0,12},{2,14},{4,0},{6,2},{8,4},{10,6},{12,8},{14,10},{1,13},{3,15... | collective-permute-start | bytes 417800 | tf_op jit(solution)/shard_map/ppermute | solution.py:602
  80.1 1.0 collective-permute-start.15
  81.1 7.7 %correlate_cross.1 = (f32[512,128]{1,0:T(8,128)S(1)}, bf16[512,128]{1,0:T(8,128)(2,1)S(1)}, bf16[512,128]{1,0:T(8,128)(2,1)S(1)}, bf16[512,128]{1,0:T(8,128)(2,1)S(1)}) custom-call(s32[12]{0:T(128)S(1)} %concatenate.3.meta.refs_0_, bf16[2,16,2,16,128]{4,3,2,1,0:T(8,128)(2,1)S(1)} %get-tuple-element.53.refs_1_, ...), custom_call_target="tpu_custom_call" | custom-call | flops 1000000 | bytes 262144 | tf_op jit(solution)/shard_map/correlate_cross/pallas_call | solution.py:421
  88.9 2.9 %collective-permute-start.28 = (bf16[512,128]{1,0:T(8,128)(2,1)S(1)}, bf16[512,128]{1,0:T(8,128)(2,1)S(1)}, u32[]{:S(2)}, u32[]{:S(2)}) collective-permute-start(bf16[512,128]{1,0:T(8,128)(2,1)S(1)} %get-tuple-element.86), channel_id=1, source_target_pairs={{0,12},{2,14},{4,0},{6,2},{8,4},{10,6},{12,8},{14,10},{1,13},{3,15... | collective-permute-start | bytes 393224 | tf_op jit(solution)/shard_map/ppermute | solution.py:607
  91.8 0.8 collective-permute-done.16.refs_3_
  92.6 0.3 collective-permute-start.27
  92.9 1.5 %collective-permute-start.26 = (bf16[512,128]{1,0:T(8,128)(2,1)S(1)}, bf16[512,128]{1,0:T(8,128)(2,1)S(1)}, u32[]{:S(2)}, u32[]{:S(2)}) collective-permute-start(bf16[512,128]{1,0:T(8,128)(2,1)S(1)} %get-tuple-element.82), channel_id=1, source_target_pairs={{0,4},{2,6},{4,8},{6,10},{8,12},{10,14},{12,0},{14,2},{1,5},{3,7},... | collective-permute-start | bytes 393224 | tf_op jit(solution)/shard_map/ppermute | solution.py:607
  94.4 1.3 %collective-permute-done.28.refs_8_ = bf16[512,128]{1,0:T(8,128)(2,1)S(1)} collective-permute-done((bf16[512,128]{1,0:T(8,128)(2,1)S(1)}, bf16[512,128]{1,0:T(8,128)(2,1)S(1)}, u32[]{:S(2)}, u32[]{:S(2)}) %collective-permute-start.28) | collective-permute-done | bytes 131104 | tf_op jit(solution)/shard_map/ppermute | solution.py:607
  95.7 8.3 %collective-permute-done.27.refs_7_ = bf16[512,128]{1,0:T(8,128)(2,1)S(1)} collective-permute-done((bf16[512,128]{1,0:T(8,128)(2,1)S(1)}, bf16[512,128]{1,0:T(8,128)(2,1)S(1)}, u32[]{:S(2)}, u32[]{:S(2)}) %collective-permute-start.27) | collective-permute-done | bytes 131104 | tf_op jit(solution)/shard_map/ppermute | solution.py:607
  104.1 0.5 collective-permute-start.30
  104.6 0.8 collective-permute-done.31.refs_11_
  105.4 0.2 collective-permute-done.30.refs_10_
  105.6 3.7 %assemble.1 = f32[2,16,32,256]{3,2,1,0:T(8,128)} custom-call(s32[12]{0:T(128)S(1)} %concatenate.3.meta.refs_0_, f32[544,128]{1,0:T(8,128)S(1)} %get-tuple-element.76.refs_1_, bf16[544,128]{1,0:T(8,128)(2,1)S(1)} %collective-permute-done.15.refs_2_, bf16[544,128]{1,0:T(8,128)(2,1)S(1)} %collective-permute-done.16.refs_3_, ...), custom_call_target="tpu_custom_call" | custom-call | flops 1000000 | bytes 262144 | tf_op jit(solution)/shard_map/assemble/pallas_call | solution.py:500
  (40 shorter events, 0.1 us)
Async XLA Ops:
  0.7 1.6 %copy-start = (bf16[2,8,65536]{2,1,0:T(8,128)(2,1)S(1)}, bf16[2,8,65536]{2,1,0:T(8,128)(2,1)}, u32[]{:S(2)}) copy-start(bf16[2,8,65536]{2,1,0:T(8,128)(2,1)} %block.3) | copy-start | bytes 6291460
  2.3 25.9 %copy-start.1 = (f32[16,64,128]{2,1,0:T(8,128)S(1)}, f32[16,64,128]{2,1,0:T(8,128)}, u32[]{:S(2)}) copy-start(f32[16,64,128]{2,1,0:T(8,128)} %constant.46.clone.refs_5_) | copy-start | bytes 1572868
  2.3 25.9 %copy-start.2 = (bf16[2,4,32,128]{3,2,1,0:T(8,128)(2,1)S(1)}, bf16[2,4,32,128]{3,2,1,0:T(8,128)(2,1)}, u32[]{:S(2)}) copy-start(bf16[2,4,32,128]{3,2,1,0:T(8,128)(2,1)} %constant.50.clone.refs_9_) | copy-start | bytes 196612
  2.3 25.9 %copy-start.3 = (bf16[128,128]{1,0:T(8,128)(2,1)S(1)}, bf16[128,128]{1,0:T(8,128)(2,1)}, u32[]{:S(2)}) copy-start(bf16[128,128]{1,0:T(8,128)(2,1)} %constant.47.clone.refs_6_) | copy-start | bytes 98308
  2.3 25.9 %copy-start.4 = (f32[64,128]{1,0:T(8,128)S(1)}, f32[64,128]{1,0:T(8,128)}, u32[]{:S(2)}) copy-start(f32[64,128]{1,0:T(8,128)} %constant.48.clone.refs_7_) | copy-start | bytes 98308
  2.3 25.9 %copy-start.5 = (f32[64,128]{1,0:T(8,128)S(1)}, f32[64,128]{1,0:T(8,128)}, u32[]{:S(2)}) copy-start(f32[64,128]{1,0:T(8,128)} %constant.49.clone.refs_8_) | copy-start | bytes 98308
  4.1 24.2 %collective-permute-start = (bf16[4,2,512,128]{3,2,1,0:T(8,128)(2,1)S(1)}, bf16[4,2,512,128]{3,2,1,0:T(8,128)(2,1)S(1)}, u32[]{:S(2)}, u32[]{:S(2)}) collective-permute-start(bf16[4,2,512,128]{3,2,1,0:T(8,128)(2,1)S(1)} %pick.2.refs_1_), channel_id=1, source_target_pairs={{2,6},{6,10},{10,14},{3,7},{7,11},{11,15},{18,22},{22,26},{26,30},... | collective-permute-start | bytes 3145736 | tf_op jit(solution)/shard_map/ppermute | solution.py:561
  6.5 13.0 %collective-permute-start.3 = (bf16[2,512,128]{2,1,0:T(8,128)(2,1)S(1)}, bf16[2,512,128]{2,1,0:T(8,128)(2,1)S(1)}, u32[]{:S(2)}, u32[]{:S(2)}) collective-permute-start(bf16[2,512,128]{2,1,0:T(8,128)(2,1)S(1)} %get-tuple-element.47), channel_id=1, source_target_pairs={{0,2},{2,0},{4,6},{6,4},{8,10},{10,8},{12,14},{14,12},{1,3},{3,1},... | collective-permute-start | bytes 786440 | tf_op jit(solution)/shard_map/ppermute | solution.py:559
  12.3 12.4 %collective-permute-start.1 = (bf16[2,512,128]{2,1,0:T(8,128)(2,1)S(1)}, bf16[2,512,128]{2,1,0:T(8,128)(2,1)S(1)}, u32[]{:S(2)}, u32[]{:S(2)}) collective-permute-start(bf16[2,512,128]{2,1,0:T(8,128)(2,1)S(1)} %get-tuple-element.46), channel_id=1, source_target_pairs={{0,2},{2,0},{4,6},{6,4},{8,10},{10,8},{12,14},{14,12},{1,3},{3,1},... | collective-permute-start | bytes 786440 | tf_op jit(solution)/shard_map/ppermute | solution.py:559
  19.5 8.7 %collective-permute-start.4 = (bf16[2,512,128]{2,1,0:T(8,128)(2,1)S(1)}, bf16[2,512,128]{2,1,0:T(8,128)(2,1)S(1)}, u32[]{:S(2)}, u32[]{:S(2)}) collective-permute-start(bf16[2,512,128]{2,1,0:T(8,128)(2,1)S(1)} %collective-permute-done.3.refs_3_), channel_id=1, source_target_pairs={{0,4},{4,8},{8,12},{1,5},{5,9},{9,13},{16,20},{20,24},{24,28},{17,... | collective-permute-start | bytes 786440 | tf_op jit(solution)/shard_map/ppermute | solution.py:567
  22.9 9.2 %collective-permute-start.10 = (bf16[2,512,128]{2,1,0:T(8,128)(2,1)S(1)}, bf16[2,512,128]{2,1,0:T(8,128)(2,1)S(1)}, u32[]{:S(2)}, u32[]{:S(2)}) collective-permute-start(bf16[2,512,128]{2,1,0:T(8,128)(2,1)S(1)} %get-tuple-element.61), channel_id=1, source_target_pairs={{0,2},{2,0},{4,6},{6,4},{8,10},{10,8},{12,14},{14,12},{1,3},{3,1},... | collective-permute-start | bytes 786440 | tf_op jit(solution)/shard_map/ppermute | solution.py:559
  24.7 11.3 %collective-permute-start.2 = (bf16[2,512,128]{2,1,0:T(8,128)(2,1)S(1)}, bf16[2,512,128]{2,1,0:T(8,128)(2,1)S(1)}, u32[]{:S(2)}, u32[]{:S(2)}) collective-permute-start(bf16[2,512,128]{2,1,0:T(8,128)(2,1)S(1)} %collective-permute-done.1.refs_3_), channel_id=1, source_target_pairs={{0,4},{4,8},{8,12},{1,5},{5,9},{9,13},{16,20},{20,24},{24,28},{17,... | collective-permute-start | bytes 786440 | tf_op jit(solution)/shard_map/ppermute | solution.py:567
  28.1 11.7 %collective-permute-start.8 = (bf16[2,512,128]{2,1,0:T(8,128)(2,1)S(1)}, bf16[2,512,128]{2,1,0:T(8,128)(2,1)S(1)}, u32[]{:S(2)}, u32[]{:S(2)}) collective-permute-start(bf16[2,512,128]{2,1,0:T(8,128)(2,1)S(1)} %get-tuple-element.58), channel_id=1, source_target_pairs={{0,2},{2,0},{4,6},{6,4},{8,10},{10,8},{12,14},{14,12},{1,3},{3,1},... | collective-permute-start | bytes 786440 | tf_op jit(solution)/shard_map/ppermute | solution.py:559
  32.1 14.2 %collective-permute-start.11 = (bf16[2,512,128]{2,1,0:T(8,128)(2,1)S(1)}, bf16[2,512,128]{2,1,0:T(8,128)(2,1)S(1)}, u32[]{:S(2)}, u32[]{:S(2)}) collective-permute-start(bf16[2,512,128]{2,1,0:T(8,128)(2,1)S(1)} %collective-permute-done.10.refs_3_), channel_id=1, source_target_pairs={{0,4},{4,8},{8,12},{1,5},{5,9},{9,13},{16,20},{20,24},{24,28},{17,... | collective-permute-start | bytes 786440 | tf_op jit(solution)/shard_map/ppermute | solution.py:567
  39.9 10.2 %collective-permute-start.9 = (bf16[2,512,128]{2,1,0:T(8,128)(2,1)S(1)}, bf16[2,512,128]{2,1,0:T(8,128)(2,1)S(1)}, u32[]{:S(2)}, u32[]{:S(2)}) collective-permute-start(bf16[2,512,128]{2,1,0:T(8,128)(2,1)S(1)} %collective-permute-done.8.refs_3_), channel_id=1, source_target_pairs={{0,4},{4,8},{8,12},{1,5},{5,9},{9,13},{16,20},{20,24},{24,28},{17,... | collective-permute-start | bytes 786440 | tf_op jit(solution)/shard_map/ppermute | solution.py:567
  42.7 11.4 %collective-permute-start.7 = (bf16[2,16,2,16,128]{4,3,2,1,0:T(8,128)(2,1)S(1)}, bf16[2,16,2,16,128]{4,3,2,1,0:T(8,128)(2,1)S(1)}, u32[]{:S(2)}, u32[]{:S(2)}) collective-permute-start(bf16[2,16,2,16,128]{4,3,2,1,0:T(8,128)(2,1)S(1)} %get-tuple-element.56), channel_id=1, source_target_pairs={{0,3},{1,2},{2,1},{3,0},{4,7},{5,6},{6,5},{7,4},{8,11},{9,10},{10,... | collective-permute-start | bytes 786440 | tf_op jit(solution)/shard_map/ppermute | solution.py:584
  43.0 12.1 %collective-permute-start.6 = (bf16[2,16,2,16,128]{4,3,2,1,0:T(8,128)(2,1)S(1)}, bf16[2,16,2,16,128]{4,3,2,1,0:T(8,128)(2,1)S(1)}, u32[]{:S(2)}, u32[]{:S(2)}) collective-permute-start(bf16[2,16,2,16,128]{4,3,2,1,0:T(8,128)(2,1)S(1)} %get-tuple-element.55), channel_id=1, source_target_pairs={{0,2},{1,3},{2,0},{3,1},{4,6},{5,7},{6,4},{7,5},{8,10},{9,11},{10,... | collective-permute-start | bytes 786440 | tf_op jit(solution)/shard_map/ppermute | solution.py:584
  45.7 11.4 %collective-permute-start.5 = (bf16[2,16,2,16,128]{4,3,2,1,0:T(8,128)(2,1)S(1)}, bf16[2,16,2,16,128]{4,3,2,1,0:T(8,128)(2,1)S(1)}, u32[]{:S(2)}, u32[]{:S(2)}) collective-permute-start(bf16[2,16,2,16,128]{4,3,2,1,0:T(8,128)(2,1)S(1)} %get-tuple-element.54), channel_id=1, source_target_pairs={{0,1},{1,0},{2,3},{3,2},{4,5},{5,4},{6,7},{7,6},{8,9},{9,8},{10,11... | collective-permute-start | bytes 786440 | tf_op jit(solution)/shard_map/ppermute | solution.py:584
  46.2 11.4 %collective-permute-start.18 = (bf16[2,16,2,16,128]{4,3,2,1,0:T(8,128)(2,1)S(1)}, bf16[2,16,2,16,128]{4,3,2,1,0:T(8,128)(2,1)S(1)}, u32[]{:S(2)}, u32[]{:S(2)}) collective-permute-start(bf16[2,16,2,16,128]{4,3,2,1,0:T(8,128)(2,1)S(1)} %get-tuple-element.53.refs_1_), channel_id=1, source_target_pairs={{0,16},{16,0},{1,17},{17,1},{2,18},{18,2},{3,19},{19,3},{4,20},{20... | collective-permute-start | bytes 786440 | tf_op jit(solution)/shard_map/ppermute | solution.py:586
  54.1 10.1 %collective-permute-start.14 = (bf16[2,16,2,16,128]{4,3,2,1,0:T(8,128)(2,1)S(1)}, bf16[2,16,2,16,128]{4,3,2,1,0:T(8,128)(2,1)S(1)}, u32[]{:S(2)}, u32[]{:S(2)}) collective-permute-start(bf16[2,16,2,16,128]{4,3,2,1,0:T(8,128)(2,1)S(1)} %get-tuple-element.75), channel_id=1, source_target_pairs={{0,3},{1,2},{2,1},{3,0},{4,7},{5,6},{6,5},{7,4},{8,11},{9,10},{10,... | collective-permute-start | bytes 786440 | tf_op jit(solution)/shard_map/ppermute | solution.py:584
  55.1 14.4 %collective-permute-start.13 = (bf16[2,16,2,16,128]{4,3,2,1,0:T(8,128)(2,1)S(1)}, bf16[2,16,2,16,128]{4,3,2,1,0:T(8,128)(2,1)S(1)}, u32[]{:S(2)}, u32[]{:S(2)}) collective-permute-start(bf16[2,16,2,16,128]{4,3,2,1,0:T(8,128)(2,1)S(1)} %get-tuple-element.73), channel_id=1, source_target_pairs={{0,2},{1,3},{2,0},{3,1},{4,6},{5,7},{6,4},{7,5},{8,10},{9,11},{10,... | collective-permute-start | bytes 786440 | tf_op jit(solution)/shard_map/ppermute | solution.py:584
  57.1 12.4 %collective-permute-start.12 = (bf16[2,16,2,16,128]{4,3,2,1,0:T(8,128)(2,1)S(1)}, bf16[2,16,2,16,128]{4,3,2,1,0:T(8,128)(2,1)S(1)}, u32[]{:S(2)}, u32[]{:S(2)}) collective-permute-start(bf16[2,16,2,16,128]{4,3,2,1,0:T(8,128)(2,1)S(1)} %get-tuple-element.71), channel_id=1, source_target_pairs={{0,1},{1,0},{2,3},{3,2},{4,5},{5,4},{6,7},{7,6},{8,9},{9,8},{10,11... | collective-permute-start | bytes 786440 | tf_op jit(solution)/shard_map/ppermute | solution.py:584
  57.6 12.4 %collective-permute-start.22 = (bf16[2,16,2,16,128]{4,3,2,1,0:T(8,128)(2,1)S(1)}, bf16[2,16,2,16,128]{4,3,2,1,0:T(8,128)(2,1)S(1)}, u32[]{:S(2)}, u32[]{:S(2)}) collective-permute-start(bf16[2,16,2,16,128]{4,3,2,1,0:T(8,128)(2,1)S(1)} %get-tuple-element.69.refs_5_), channel_id=1, source_target_pairs={{0,16},{16,0},{1,17},{17,1},{2,18},{18,2},{3,19},{19,3},{4,20},{20... | collective-permute-start | bytes 786440 | tf_op jit(solution)/shard_map/ppermute | solution.py:586
  57.6 12.4 %collective-permute-start.19 = (bf16[2,16,2,16,128]{4,3,2,1,0:T(8,128)(2,1)S(1)}, bf16[2,16,2,16,128]{4,3,2,1,0:T(8,128)(2,1)S(1)}, u32[]{:S(2)}, u32[]{:S(2)}) collective-permute-start(bf16[2,16,2,16,128]{4,3,2,1,0:T(8,128)(2,1)S(1)} %collective-permute-done.5.refs_2_), channel_id=1, source_target_pairs={{0,16},{16,0},{1,17},{17,1},{2,18},{18,2},{3,19},{19,3},{4,20},{20... | collective-permute-start | bytes 786440 | tf_op jit(solution)/shard_map/ppermute | solution.py:586
  64.2 14.1 %collective-permute-start.20 = (bf16[2,16,2,16,128]{4,3,2,1,0:T(8,128)(2,1)S(1)}, bf16[2,16,2,16,128]{4,3,2,1,0:T(8,128)(2,1)S(1)}, u32[]{:S(2)}, u32[]{:S(2)}) collective-permute-start(bf16[2,16,2,16,128]{4,3,2,1,0:T(8,128)(2,1)S(1)} %collective-permute-done.6.refs_3_), channel_id=1, source_target_pairs={{0,16},{16,0},{1,17},{17,1},{2,18},{18,2},{3,19},{19,3},{4,20},{20... | collective-permute-start | bytes 786440 | tf_op jit(solution)/shard_map/ppermute | solution.py:586
  69.5 10.6 %collective-permute-start.21 = (bf16[2,16,2,16,128]{4,3,2,1,0:T(8,128)(2,1)S(1)}, bf16[2,16,2,16,128]{4,3,2,1,0:T(8,128)(2,1)S(1)}, u32[]{:S(2)}, u32[]{:S(2)}) collective-permute-start(bf16[2,16,2,16,128]{4,3,2,1,0:T(8,128)(2,1)S(1)} %collective-permute-done.7.refs_4_), channel_id=1, source_target_pairs={{0,16},{16,0},{1,17},{17,1},{2,18},{18,2},{3,19},{19,3},{4,20},{20... | collective-permute-start | bytes 786440 | tf_op jit(solution)/shard_map/ppermute | solution.py:586
  69.5 10.6 %collective-permute-start.25 = (bf16[2,16,2,16,128]{4,3,2,1,0:T(8,128)(2,1)S(1)}, bf16[2,16,2,16,128]{4,3,2,1,0:T(8,128)(2,1)S(1)}, u32[]{:S(2)}, u32[]{:S(2)}) collective-permute-start(bf16[2,16,2,16,128]{4,3,2,1,0:T(8,128)(2,1)S(1)} %collective-permute-done.14.refs_8_), channel_id=1, source_target_pairs={{0,16},{16,0},{1,17},{17,1},{2,18},{18,2},{3,19},{19,3},{4,20},{20... | collective-permute-start | bytes 786440 | tf_op jit(solution)/shard_map/ppermute | solution.py:586
  70.0 11.2 %collective-permute-start.24 = (bf16[2,16,2,16,128]{4,3,2,1,0:T(8,128)(2,1)S(1)}, bf16[2,16,2,16,128]{4,3,2,1,0:T(8,128)(2,1)S(1)}, u32[]{:S(2)}, u32[]{:S(2)}) collective-permute-start(bf16[2,16,2,16,128]{4,3,2,1,0:T(8,128)(2,1)S(1)} %collective-permute-done.13.refs_7_), channel_id=1, source_target_pairs={{0,16},{16,0},{1,17},{17,1},{2,18},{18,2},{3,19},{19,3},{4,20},{20... | collective-permute-start | bytes 786440 | tf_op jit(solution)/shard_map/ppermute | solution.py:586
  70.1 11.1 %collective-permute-start.23 = (bf16[2,16,2,16,128]{4,3,2,1,0:T(8,128)(2,1)S(1)}, bf16[2,16,2,16,128]{4,3,2,1,0:T(8,128)(2,1)S(1)}, u32[]{:S(2)}, u32[]{:S(2)}) collective-permute-start(bf16[2,16,2,16,128]{4,3,2,1,0:T(8,128)(2,1)S(1)} %collective-permute-done.12.refs_6_), channel_id=1, source_target_pairs={{0,16},{16,0},{1,17},{17,1},{2,18},{18,2},{3,19},{19,3},{4,20},{20... | collective-permute-start | bytes 786440 | tf_op jit(solution)/shard_map/ppermute | solution.py:586
  78.3 10.6 %collective-permute-start.17 = (bf16[544,128]{1,0:T(8,128)(2,1)S(1)}, bf16[544,128]{1,0:T(8,128)(2,1)S(1)}, u32[]{:S(2)}, u32[]{:S(2)}) collective-permute-start(bf16[544,128]{1,0:T(8,128)(2,1)S(1)} %get-tuple-element.79), channel_id=1, source_target_pairs={{0,12},{2,14},{4,0},{6,2},{8,4},{10,6},{12,8},{14,10},{1,13},{3,15... | collective-permute-start | bytes 417800 | tf_op jit(solution)/shard_map/ppermute | solution.py:602
  80.1 12.5 %collective-permute-start.16 = (bf16[544,128]{1,0:T(8,128)(2,1)S(1)}, bf16[544,128]{1,0:T(8,128)(2,1)S(1)}, u32[]{:S(2)}, u32[]{:S(2)}) collective-permute-start(bf16[544,128]{1,0:T(8,128)(2,1)S(1)} %get-tuple-element.78), channel_id=1, source_target_pairs={{0,8},{2,10},{4,12},{6,14},{8,0},{10,2},{12,4},{14,6},{1,9},{3,11}... | collective-permute-start | bytes 417800 | tf_op jit(solution)/shard_map/ppermute | solution.py:602
  80.1 12.8 %collective-permute-start.15 = (bf16[544,128]{1,0:T(8,128)(2,1)S(1)}, bf16[544,128]{1,0:T(8,128)(2,1)S(1)}, u32[]{:S(2)}, u32[]{:S(2)}) collective-permute-start(bf16[544,128]{1,0:T(8,128)(2,1)S(1)} %get-tuple-element.77), channel_id=1, source_target_pairs={{0,4},{2,6},{4,8},{6,10},{8,12},{10,14},{12,0},{14,2},{1,5},{3,7},... | collective-permute-start | bytes 417800 | tf_op jit(solution)/shard_map/ppermute | solution.py:602
  88.9 6.8 %collective-permute-start.28 = (bf16[512,128]{1,0:T(8,128)(2,1)S(1)}, bf16[512,128]{1,0:T(8,128)(2,1)S(1)}, u32[]{:S(2)}, u32[]{:S(2)}) collective-permute-start(bf16[512,128]{1,0:T(8,128)(2,1)S(1)} %get-tuple-element.86), channel_id=1, source_target_pairs={{0,12},{2,14},{4,0},{6,2},{8,4},{10,6},{12,8},{14,10},{1,13},{3,15... | collective-permute-start | bytes 393224 | tf_op jit(solution)/shard_map/ppermute | solution.py:607
  92.6 11.5 %collective-permute-start.27 = (bf16[512,128]{1,0:T(8,128)(2,1)S(1)}, bf16[512,128]{1,0:T(8,128)(2,1)S(1)}, u32[]{:S(2)}, u32[]{:S(2)}) collective-permute-start(bf16[512,128]{1,0:T(8,128)(2,1)S(1)} %get-tuple-element.84), channel_id=1, source_target_pairs={{0,8},{2,10},{4,12},{6,14},{8,0},{10,2},{12,4},{14,6},{1,9},{3,11}... | collective-permute-start | bytes 393224 | tf_op jit(solution)/shard_map/ppermute | solution.py:607
  92.9 11.7 %collective-permute-start.29 = (f32[512,128]{1,0:T(8,128)S(1)}, f32[512,128]{1,0:T(8,128)S(1)}, u32[]{:S(2)}, u32[]{:S(2)}) collective-permute-start(f32[512,128]{1,0:T(8,128)S(1)} %get-tuple-element.80.refs_5_), channel_id=1, source_target_pairs={{0,16},{16,0},{1,17},{17,1},{2,18},{18,2},{3,19},{19,3},{4,20},{20... | collective-permute-start | bytes 786440 | tf_op jit(solution)/shard_map/ppermute | solution.py:608
  92.9 11.2 %collective-permute-start.26 = (bf16[512,128]{1,0:T(8,128)(2,1)S(1)}, bf16[512,128]{1,0:T(8,128)(2,1)S(1)}, u32[]{:S(2)}, u32[]{:S(2)}) collective-permute-start(bf16[512,128]{1,0:T(8,128)(2,1)S(1)} %get-tuple-element.82), channel_id=1, source_target_pairs={{0,4},{2,6},{4,8},{6,10},{8,12},{10,14},{12,0},{14,2},{1,5},{3,7},... | collective-permute-start | bytes 393224 | tf_op jit(solution)/shard_map/ppermute | solution.py:607
  95.7 8.9 %collective-permute-start.32 = (bf16[512,128]{1,0:T(8,128)(2,1)S(1)}, bf16[512,128]{1,0:T(8,128)(2,1)S(1)}, u32[]{:S(2)}, u32[]{:S(2)}) collective-permute-start(bf16[512,128]{1,0:T(8,128)(2,1)S(1)} %collective-permute-done.28.refs_8_), channel_id=1, source_target_pairs={{0,16},{16,0},{1,17},{17,1},{2,18},{18,2},{3,19},{19,3},{4,20},{20... | collective-permute-start | bytes 393224 | tf_op jit(solution)/shard_map/ppermute | solution.py:608
  104.1 1.3 %collective-permute-start.31 = (bf16[512,128]{1,0:T(8,128)(2,1)S(1)}, bf16[512,128]{1,0:T(8,128)(2,1)S(1)}, u32[]{:S(2)}, u32[]{:S(2)}) collective-permute-start(bf16[512,128]{1,0:T(8,128)(2,1)S(1)} %collective-permute-done.27.refs_7_), channel_id=1, source_target_pairs={{0,16},{16,0},{1,17},{17,1},{2,18},{18,2},{3,19},{19,3},{4,20},{20... | collective-permute-start | bytes 393224 | tf_op jit(solution)/shard_map/ppermute | solution.py:608
  104.1 1.5 %collective-permute-start.30 = (bf16[512,128]{1,0:T(8,128)(2,1)S(1)}, bf16[512,128]{1,0:T(8,128)(2,1)S(1)}, u32[]{:S(2)}, u32[]{:S(2)}) collective-permute-start(bf16[512,128]{1,0:T(8,128)(2,1)S(1)} %collective-permute-done.26.refs_6_), channel_id=1, source_target_pairs={{0,16},{16,0},{1,17},{17,1},{2,18},{18,2},{3,19},{19,3},{4,20},{20... | collective-permute-start | bytes 393224 | tf_op jit(solution)/shard_map/ppermute | solution.py:608

commit v8 on v7

--- a/solution.py
+++ b/solution.py
@@ -80,7 +80,7 @@
     return np.concatenate([cosine, cosine], axis=1), np.concatenate([sine, sine], axis=1)
 
 
-def pick_kernel(count, joined, own, meta, block, *refs):
+def pick_kernel(half, meta, block, *refs):
     outs, rows = refs[:-1], refs[-1]
     inputs, samples = block.shape[1], block.shape[2]
     step = 16
@@ -95,27 +95,30 @@
             return carry
 
         lax.fori_loop(0, samples // LANES // step, spread, 0)
-    first = (meta[G_AT] if own else 1 - meta[G_AT]) * count
+    g = meta[G_AT]
     tall = 128
-    for item in range(count):
-        out = outs[0].at[item] if joined else outs[item]
-
-        def gather(n, carry, item=item, out=out):
+    for item in range(inputs):
+        first = (1 - g) * half + item if item < half else g * half + item - half
+        kept = item - half
+        out = outs[item] if item < half else outs[half + kept // JOIN].at[kept % JOIN]
+
+        def gather(n, carry, first=first, out=out):
             low = pl.multiple_of(n * tall, tall)
             for part in range(2):
-                value = rows[part, pl.ds(low * inputs + first + item, tall, stride=inputs), :]
+                value = rows[part, pl.ds(low * inputs + first, tall, stride=inputs), :]
                 out[part, pl.ds(low, tall), :] = value.astype(jnp.bfloat16)
             return carry
 
         lax.fori_loop(0, samples // LANES // tall, gather, 0)
 
 
-def pick(meta, block, count, joined, own):
+def pick(meta, block):
     _, inputs, samples = block.shape
+    half = inputs // PAIR
     one = (2, samples // LANES, LANES)
-    shapes = [(count,) + one] if joined else [one] * count
+    shapes = [one] * half + [(JOIN,) + one] * (half // JOIN)
     return pl.pallas_call(
-        functools.partial(pick_kernel, count, joined, own),
+        functools.partial(pick_kernel, half),
         out_shape=[jax.ShapeDtypeStruct(s, jnp.bfloat16) for s in shapes],
         in_specs=[SMEM, VMEM],
         out_specs=[VMEM] * len(shapes),
@@ -170,9 +173,9 @@
 
     @pl.when(me != 0)
     def _():
-        bring(halo_own.at[index], 0)
-
-    bring(keep.at[index], 1 + me)
+        bring(halo_own.at[index % JOIN], 0)
+
+    bring(keep.at[index % JOIN], 1 + me)
     bring(recv, 2 - me)
 
     back = lax.rem(LANES - across, LANES)
@@ -264,7 +267,7 @@
                 turn((half - 1) * HALF + n * SOME)
 
 
-def filterbank(index, meta, keep, halo_own, recv, halo_far, tables, earlier, dests):
+def filterbank(index, half, meta, keep, halo_own, recv, halo_far, tables, earlier, dests):
     frames = keep.shape[2] // ROWS
     size = tables[-1].shape[2] // 2
     per_ct = tables[-1].shape[1] // 2
@@ -273,7 +276,7 @@
     shape = (before + 1, PAIR * frames // 2, 2, size, LANES)
     return pl.pallas_call(
         functools.partial(
-            filterbank_kernel, index, before, frames, dests, per_ct, keep.shape[0]
+            filterbank_kernel, index, before, frames, dests, per_ct, half
         ),
         out_shape=[jax.ShapeDtypeStruct(shape, jnp.bfloat16)] * dests,
         in_specs=[SMEM] + [VMEM] * (9 + len(earlier)),
@@ -294,19 +297,25 @@
 CORNER = [(p, q) for p in range(TILE) for q in range(p, TILE)]
 
 
-def own_blocks(own):
+def pair_sets(own, parts):
     tiles = own // TILE
-    whole = [(i, j, SQUARE) for i in range(tiles) for j in range(i + 1, tiles)]
-    return whole + [(i, i, CORNER) for i in range(tiles)]
-
-
-def cross_blocks(own):
-    tiles = own // TILE
-    return [(i, j, SQUARE) for i in range(tiles // 2) for j in range(tiles)]
+    per = tiles // parts
+    whole = [(True, i, j, SQUARE) for i in range(tiles) for j in range(i + 1, tiles)]
+    corner = [(True, i, i, CORNER) for i in range(tiles)]
+    across = [(False, i, j, SQUARE) for i in range(0, tiles, 2) for j in range(tiles)]
+
+    def early(block):
+        return block[1] < per and block[2] < per
+
+    def late(blocks):
+        return [block for block in blocks if not early(block)]
+
+    first = [block for block in whole + across + corner if early(block)]
+    return [first, late(whole + corner), late(across)]
 
 
 def pairs_in(blocks):
-    return sum(len(block[2]) for block in blocks)
+    return sum(len(block[3]) for block in blocks)
 
 
 def chosen(t, values):
@@ -317,21 +326,25 @@
 
 
 def correlate_kernel(layout, *refs):
-    sources_at, blocks, own, cross, outer, span, per_ct, in_count, half_count = layout
+    sources_at, blocks, own, terms, outer, span, per_ct = layout
     meta, sources = refs[0], refs[1 : 1 + len(sources_at)]
     rest = refs[1 + len(sources_at) :]
-    outs, (spectra, sums, held) = rest[:-3], rest[-3:]
+    earlier, outs, (spectra, sums, held) = rest[:terms], rest[terms:-3], rest[-3:]
     steps = spectra.shape[1]
     some = 8
     core, g, ct = meta[CORE_AT], meta[G_AT], meta[CT_AT]
-
-    for source, (far, dg, dc, start) in zip(sources, sources_at):
-        base = lax.rem(ct - dc + per_ct, per_ct) * in_count + (g ^ dg) * half_count + start
+    within = any(block[0] for block in blocks)
+    across = any(not block[0] for block in blocks)
+
+    for source, (far, dg, dc, part) in zip(sources, sources_at):
+        device = lax.rem(ct - dc + per_ct, per_ct) * PAIR + (g ^ dg)
+        base = (part * per_ct * PAIR + device) * JOIN
         wanted = None
-        if cross:
+        if across:
             side = 1 - core if far else core
-            low = core * (own // 2)
-            wanted = (side == 1) | ((base >= low) & (base < low + own // 2))
+            wanted = (side == 1) | (lax.rem(base // TILE, 2) == core)
+            if within and not far:
+                wanted = None
             base = base + side * own
 
         def bring(source=source, base=base):
@@ -387,41 +400,52 @@
                 sums[pl.ds(pl.multiple_of(row, span), span), :] = both[o * span : (o + 1) * span]
 
     done = 0
-    for pairs in (SQUARE, CORNER):
-        some_blocks = [b for b in blocks if b[2] is pairs]
-        if not some_blocks:
-            continue
-
-        def step(t, carry, some_blocks=some_blocks, pairs=pairs, done=done):
-            left = TILE * chosen(t, [b[0] for b in some_blocks])
-            right = TILE * chosen(t, [b[1] for b in some_blocks])
-            if cross:
-                left, right = left + core * (own // 2), right + own
-            block(left, right, pairs, done + t * len(pairs) * span)
+    while done < len(blocks):
+        kind = (blocks[done][0], blocks[done][3])
+        end = done
+        while end < len(blocks) and (blocks[end][0], blocks[end][3]) == kind:
+            end += 1
+        run, row = blocks[done:end], pairs_in(blocks[:done]) * span
+
+        def step(t, carry, run=run, row=row, kind=kind):
+            left, right = chosen(t, [b[1] for b in run]), chosen(t, [b[2] for b in run])
+            if not kind[0]:
+                left, right = TILE * (left + core), own + TILE * right
+            elif across:
+                left, right = core * own + TILE * left, core * own + TILE * right
+            else:
+                left, right = TILE * left, TILE * right
+            block(left, right, kind[1], row + t * len(kind[1]) * span)
             return carry
 
-        lax.fori_loop(0, len(some_blocks), step, 0)
-        done += pairs_in(some_blocks) * span
+        lax.fori_loop(0, len(run), step, 0)
+        done = end
 
     for r in range(outer):
         base = pl.multiple_of(lax.rem(meta[O_AT] + r, outer) * rows_outer, 16)
         outs[r][...] = sums[pl.ds(base, rows_outer), :].astype(outs[r].dtype)
-
-
-def correlate(meta, arrays, sources_at, blocks, own, cross, sizes, name):
-    outer, span, per_ct, in_count, half_count = sizes
+    if terms:
+        total = earlier[0][...].astype(jnp.float32)
+        for term in earlier[1:]:
+            total = total + term[...].astype(jnp.float32)
+        outs[outer][...] = total
+
+
+def correlate(meta, arrays, sources_at, blocks, own, sizes, name, earlier=()):
+    outer, span, _ = sizes
     _, steps, _, size, _ = arrays[0].shape
-    inputs = 2 * own if cross else own
+    inputs = own if all(block[0] for block in blocks) else 2 * own
     rows = pairs_in(blocks) * span
     shapes = []
     for r in range(outer):
         dtype = jnp.float32 if r == 0 else jnp.bfloat16
         shapes.append(jax.ShapeDtypeStruct((rows, LANES), dtype))
-    layout = (sources_at, blocks, own, cross) + sizes
+    shapes += [jax.ShapeDtypeStruct(x.shape, jnp.float32) for x in earlier[:1]]
+    layout = (sources_at, blocks, own, len(earlier)) + sizes
     return pl.pallas_call(
         functools.partial(correlate_kernel, layout),
         out_shape=shapes,
-        in_specs=[SMEM] + [VMEM] * len(arrays),
+        in_specs=[SMEM] + [VMEM] * (len(arrays) + len(earlier)),
         out_specs=[VMEM] * len(shapes),
         scratch_shapes=[
             pltpu.VMEM((inputs, steps, 4, size, LANES), jnp.float32),
@@ -431,53 +455,56 @@
         compiler_params=params(8 + inputs * steps * 4 * size * LANES * 4 // 2**20),
         cost_estimate=cost(10**6, 2**18),
         name=name,
-    )(meta, *arrays)
-
-
-def assemble_kernel(own, outer, span, scale, *refs):
+    )(meta, *arrays, *earlier)
+
+
+def assemble_kernel(own, outer, span, scale, sets, order, counts, *refs):
     meta = refs[0]
-    mine_in = refs[1 : 1 + outer]
-    mine_across = refs[1 + outer : 1 + 2 * outer]
-    far_across = refs[1 + 2 * outer : 1 + 3 * outer]
-    out, joined = refs[1 + 3 * outer :]
+    out, joined = refs[-2:]
+    sources, at = [], 1
+    for count in counts:
+        sources.append(refs[at : at + count])
+        at += count
+    near, far = sources[: len(sets)], sources[len(sets) :]
     lane = lax.broadcasted_iota(jnp.int32, (1, LANES), 1)
     high = lane < RADIX
     mirror = jnp.where(high, 1.0, -1.0).astype(jnp.float32)
     me = meta[CORE_AT]
 
-    def added(sources, low, rows):
-        total = sources[0][low : low + rows, :].astype(jnp.float32)
-        for source in sources[1:]:
-            total = total + source[low : low + rows, :].astype(jnp.float32)
+    def added(parts, low, rows):
+        total = parts[0][low : low + rows, :].astype(jnp.float32)
+        for part in parts[1:]:
+            total = total + part[low : low + rows, :].astype(jnp.float32)
         return total * scale
 
     def put(value, row, col):
         at = pl.multiple_of((row * 2 * own + col) * span, span)
         joined[pl.ds(at, span), :] = value
 
-    done = 0
-    for i, j, pairs in own_blocks(own):
-        total = added(mine_in, done, len(pairs) * span)
-        turned = total * mirror
-        for at, (p, q) in enumerate(pairs):
-            cut = slice(at * span, (at + 1) * span)
-            a, b = i * TILE + p, j * TILE + q
-            put(total[cut], a, me * own + b)
-            if a != b:
-                put(turned[cut], b, me * own + a)
-        done += len(pairs) * span
     sign = jnp.where(me == 0, jnp.ones_like(mirror), mirror)
-    for sources, part in ((mine_across, me), (far_across, 1 - me)):
-        done = 0
-        for i, j, pairs in cross_blocks(own):
-            total = added(sources, done, len(pairs) * span) * sign
-            for at, (p, q) in enumerate(pairs):
-                a = part * (own // 2) + i * TILE + p
-                b = j * TILE + q
-                row = jnp.where(me == 0, a, b)
-                col = jnp.where(me == 0, own + b, a)
-                put(total[at * span : (at + 1) * span], row, col)
-            done += len(pairs) * span
+    for blocks, mine, others in zip(sets, near, far):
+        low = 0
+        for within, i, j, pairs in blocks:
+            rows = len(pairs) * span
+            if within:
+                total = added(mine, low, rows)
+                turned = total * mirror
+                for n, (p, q) in enumerate(pairs):
+                    cut = slice(n * span, (n + 1) * span)
+                    a, b = order[i * TILE + p], order[j * TILE + q]
+                    put(total[cut], a, me * own + b)
+                    if a != b:
+                        put(turned[cut], b, me * own + a)
+            else:
+                for parts, side in ((mine, me), (others, 1 - me)):
+                    total = added(parts, low, rows) * sign
+                    for n, (p, q) in enumerate(pairs):
+                        a = jnp.where(side == 0, order[i * TILE + p], order[(i + 1) * TILE + p])
+                        b = order[j * TILE + q]
+                        row = jnp.where(me == 0, a, b)
+                        col = jnp.where(me == 0, own + b, a)
+                        put(total[n * span : (n + 1) * span], row, col)
+            low += rows
 
     def emit(a, carry):
         for tile in range(2 * own // 8):
@@ -495,18 +522,20 @@
     lax.fori_loop(0, own, emit, 0)
 
 
-def assemble(meta, mine_in, mine_across, far_across, own, span, scale):
-    outer = len(mine_in)
+def assemble(meta, near, far, sets, order, own, span, scale):
+    outer = len(near[1])
+    counts = [len(arrays) for arrays in near + far]
+    sources = [x for arrays in near + far for x in arrays]
     return pl.pallas_call(
-        functools.partial(assemble_kernel, own, outer, span, scale),
+        functools.partial(assemble_kernel, own, outer, span, scale, sets, order, counts),
         out_shape=jax.ShapeDtypeStruct((2, own, 2 * own, span * RADIX), jnp.float32),
-        in_specs=[SMEM] + [VMEM] * (3 * outer),
+        in_specs=[SMEM] + [VMEM] * len(sources),
         out_specs=VMEM,
         scratch_shapes=[pltpu.VMEM((own * 2 * own * span, LANES), jnp.float32)],
         compiler_params=params(10),
         cost_estimate=cost(10**6, 2**18),
         name="assemble",
-    )(meta, *mine_in, *mine_across, *far_across)
+    )(meta, *sources)
 
 
 def fast_fits(in_count, frame_count):
@@ -521,8 +550,10 @@
         and frame_count % HALF == 0
         and span in (2, 4, 8)
         and outer * span % 16 == 0
-        and own % (2 * TILE) == 0
-        and (own * (own + 1) // 2 * span) % 16 == 0
+        and own % (PAIR * JOIN * 2 * TILE // 4) == 0
+        and in_count == PAIR * JOIN * 2
+        and per_ct * PAIR * JOIN % (2 * TILE) == 0
+        and all(pairs_in(s) * span % 16 == 0 for s in pair_sets(own, 2))
     )
 
 
@@ -551,23 +582,30 @@
     tables = [np.concatenate([filter_table()] * 2, axis=1), first_table(), *twiddle_tables()]
     tables = [jnp.asarray(t) for t in tables + [np.concatenate([base, base], axis=1)]]
 
-    sends = list(pick(meta, voltages, half, False, False))
+    picked = pick(meta, voltages)
+    sends, keeps = picked[:half], picked[half:]
     forward = [p for p in onward if p[0] % PAIR == 0]
     recvs = []
     for c in range(half):
         block = follow(sends[c], recvs[c - 2]) if c >= 2 else sends[c]
         recvs.append(lax.ppermute(block, "tm", swap))
-    keep = pick(meta, voltages, half, True, True)[0]
-    halo_own = lax.ppermute(keep, "tm", [p for p in onward if p[0] % PAIR == 1])
-
-    arrays, others, places = [], [], []
+    ahead = [p for p in onward if p[0] % PAIR == 1]
+    halos = []
+    for block in keeps:
+        halos.append(lax.ppermute(follow(block, halos[-1]) if halos else block, "tm", ahead))
+
+    parts = half // JOIN
+    sets = pair_sets(own, parts)
+    sizes = (outer, span, per_ct)
+    arrays, places = [], []
     spectra, done = [], []
     for c in range(half):
         block = follow(recvs[c], done[c - 2]) if c >= 2 else recvs[c]
         far = lax.ppermute(block, "tm", forward)
         far = follow(far, done[c - 1]) if c else far
         spectra = filterbank(
-            c, meta, keep, halo_own, recvs[c], far, tables, spectra, len(dests)
+            c, half, meta, keeps[c // JOIN], halos[c // JOIN], recvs[c], far, tables, spectra,
+            len(dests),
         )
         done.append(spectra[0])
         if c % JOIN < JOIN - 1:
@@ -583,31 +621,42 @@
                     block = follow(block, arrays[-len(dests)])
                 block = lax.ppermute(block, ("tm", "ct"), route)
             arrays.append(block)
-            others.append(lax.ppermute(block, "stn", cores))
-            places.append((dg, dc, c - JOIN + 1))
+            places.append((dg, dc, c // JOIN))
         spectra = []
-
-    sizes = (outer, span, per_ct, in_count, half)
     near = [(False,) + place for place in places]
     far = [(True,) + place for place in places]
-    mine_in = correlate(
-        meta, arrays, near, own_blocks(own), own, False, sizes, "correlate_own"
+    count = len(dests)
+    others = [lax.ppermute(follow(block, done[-1]), "stn", cores) for block in arrays[:count]]
+    early = correlate(
+        meta, arrays[:count] + others, near[:count] + far[:count], sets[0], own // parts, sizes,
+        "correlate_early",
     )
-    mine_across = correlate(
-        meta, arrays + others, near + far, cross_blocks(own), own, True, sizes, "correlate_cross"
+    others += [lax.ppermute(follow(block, early[0]), "stn", cores) for block in arrays[count:]]
+    own_late = correlate(meta, arrays, near, sets[1], own, sizes, "correlate_own")
+
+    def along(parts, after):
+        moved = [parts[0]]
+        for r in range(1, outer):
+            route = [(i, (i + r * PAIR) % tm) for i in range(tm)]
+            moved.append(lax.ppermute(follow(parts[r], after(r)), "tm", route))
+        return moved
+
+    early = along(early, lambda r: others)
+    own_late = along(own_late, lambda r: early[r])
+    *cross_late, early = correlate(
+        meta, arrays + others, near + far, sets[2], own, sizes, "correlate_cross", early
     )
-    mine_in, mine_across, far_across = list(mine_in), list(mine_across), []
-    for r in range(1, outer):
-        route = [(i, (i + r * PAIR) % tm) for i in range(tm)]
-        mine_in[r] = lax.ppermute(mine_in[r], "tm", route)
-    for r in range(outer):
-        if r:
-            route = [(i, (i + r * PAIR) % tm) for i in range(tm)]
-            block = follow(mine_across[r], mine_in[r])
-            mine_across[r] = lax.ppermute(block, "tm", route)
-        far_across.append(lax.ppermute(mine_across[r], "stn", cores))
+    cross_late = along(cross_late, lambda r: own_late[r])
+    mine = [[early], own_late, cross_late]
+    theirs = [[lax.ppermute(block, "stn", cores) for block in part] for part in (mine[0], mine[2])]
+    theirs.insert(1, [])
+    order = []
+    for part in range(parts):
+        for device in range(per_ct * PAIR):
+            start = device // PAIR * in_count + device % PAIR * half + part * JOIN
+            order += range(start, start + JOIN)
     scale = 1.0 / (tm * frame_count)
-    result = assemble(meta, mine_in, mine_across, far_across, own, span, scale)
+    result = assemble(meta, mine, theirs, sets, order, own, span, scale)
     return result.transpose(0, 3, 1, 2)
 
 

time: 110 us -> 111 us (level)
  starting transfers between devices: 37 us -> 42 us
  waiting for transfers between devices: 31.7 us -> 27.7 us
    ppermute x6, waiting for transfers between devices: 11.3 us -> 6.88 us  [fast(): block = lax.ppermute(block, ('tm', 'ct'), route)]
    ppermute x19 -> x24, starting transfers between devices: 10.3 us -> 14.5 us  [the longest x9 10.4 us: along(): moved.append(lax.ppermute(follow(parts[r], after(r)), 'tm', route))]
    pallas_call x2 -> x3, Pallas kernels: 15.5 us -> 16.8 us  [correlate(): pl.pallas_call(functools.partial(correlate_kernel, layout), out_shape=sha...]
    pallas_call x2 -> x1, Pallas kernels: 3.4 us -> 2.32 us  [pick(): pl.pallas_call(functools.partial(pick_kernel, half), out_shape=[jax.Shape...]
    ppermute x19 -> x24, waiting for transfers between devices: 11.5 us -> 12 us  [the longest x9 9.43 us: along(): moved.append(lax.ppermute(follow(parts[r], after(r)), 'tm', route))]
  transfers between devices with their start and end apart: 33 -> 38, of which waited for: 9 -> 12; matrix products, arithmetic and copies ran while one was open for 0% -> 0% of each run, Pallas kernels for 30% -> 29%
where the time goes in v8:
time: 111 us
  starting transfers between devices  42 us (38%)
  Pallas kernels  38.2 us (34%)
  waiting for transfers between devices  27.7 us (25%)
  local copies, waits for them, and re-layouts  2.4 us (2%)
    pallas_call x3, Pallas kernels, correlate(): pl.pallas_call(functools.partial(correlate_kernel, layout), out_shape=sha...  16.8 us
    pallas_call x4, Pallas kernels, filterbank(): pl.pallas_call(functools.partial(filterbank_kernel, index, before, frames...  15.4 us
    ppermute x4, starting transfers between devices, fast(): far = lax.ppermute(block, 'tm', forward)  14.4 us
    ppermute x9, starting transfers between devices, along(): moved.append(lax.ppermute(follow(parts[r], after(r)), 'tm', route))  10.4 us
    ppermute x9, waiting for transfers between devices, along(): moved.append(lax.ppermute(follow(parts[r], after(r)), 'tm', route))  9.43 us
    ppermute x4, waiting for transfers between devices, fast(): recvs.append(lax.ppermute(block, 'tm', swap))  8.77 us
    ppermute x6, starting transfers between devices, fast(): block = lax.ppermute(block, ('tm', 'ct'), route)  7.04 us
    ppermute x6, waiting for transfers between devices, fast(): block = lax.ppermute(block, ('tm', 'ct'), route)  6.88 us
  transfers between devices with their start and end apart: 38, of which 12 were waited for; matrix products, arithmetic and copies ran while one was open for 0% of the time, Pallas kernels for 29%

profile of v8, /device:TPU:0, one launch (start us, length us, event | category | flops | bytes accessed | tf_op | source)
XLA Modules:
  0.0 110.5 jit_solution(806905921751639476)
XLA Ops:
  0.0 0.8 concatenate.3.meta.refs_0_
  0.8 1.6 %copy-done.1 = bf16[2,8,65536]{2,1,0:T(8,128)(2,1)S(1)} copy-done((bf16[2,8,65536]{2,1,0:T(8,128)(2,1)S(1)}, bf16[2,8,65536]{2,1,0:T(8,128)(2,1)}, u32[]{:S(2)}) %copy-start.1) | copy-done | bytes 2097176
  2.4 2.3 %pick.1 = (bf16[2,512,128]{2,1,0:T(8,128)(2,1)S(1)}, bf16[2,512,128]{2,1,0:T(8,128)(2,1)S(1)}, bf16[2,512,128]{2,1,0:T(8,128)(2,1)S(1)}, bf16[2,512,128]{2,1,0:T...) custom-call(s32[12]{0:T(128)S(1)} %concatenate.3.meta.refs_0_, ...), custom_call_target="tpu_custom_call" | custom-call | flops 1000000 | bytes 262144 | tf_op jit(solution)/shard_map/pick/pallas_call | solution.py:120
  4.7 0.7 collective-permute-start
  5.4 5.8 %collective-permute-start.3 = (bf16[2,512,128]{2,1,0:T(8,128)(2,1)S(1)}, bf16[2,512,128]{2,1,0:T(8,128)(2,1)S(1)}, u32[]{:S(2)}, u32[]{:S(2)}) collective-permute-start(bf16[2,512,128]{2,1,0:T(8,128)(2,1)S(1)} %get-tuple-element.70), channel_id=1, source_target_pairs={{0,2},{2,0},{4,6},{6,4},{8,10},{10,8},{12,14},{14,12},{1,3},{3,1},... | collective-permute-start | bytes 786440 | tf_op jit(solution)/shard_map/ppermute | solution.py:591
  11.2 0.1 collective-permute-start.1
  11.3 7.1 %collective-permute-done.3.refs_3_ = bf16[2,512,128]{2,1,0:T(8,128)(2,1)S(1)} collective-permute-done((bf16[2,512,128]{2,1,0:T(8,128)(2,1)S(1)}, bf16[2,512,128]{2,1,0:T(8,128)(2,1)S(1)}, u32[]{:S(2)}, u32[]{:S(2)}) %collective-permute-start.3) | collective-permute-done | bytes 262176 | tf_op jit(solution)/shard_map/ppermute | solution.py:591
  18.4 3.5 %collective-permute-start.4 = (bf16[2,512,128]{2,1,0:T(8,128)(2,1)S(1)}, bf16[2,512,128]{2,1,0:T(8,128)(2,1)S(1)}, u32[]{:S(2)}, u32[]{:S(2)}) collective-permute-start(bf16[2,512,128]{2,1,0:T(8,128)(2,1)S(1)} %collective-permute-done.3.refs_3_), channel_id=1, source_target_pairs={{0,4},{4,8},{8,12},{1,5},{5,9},{9,13},{16,20},{20,24},{24,28},{17,... | collective-permute-start | bytes 786440 | tf_op jit(solution)/shard_map/ppermute | solution.py:604
  22.0 1.7 %collective-permute-done.1.refs_3_ = bf16[2,512,128]{2,1,0:T(8,128)(2,1)S(1)} collective-permute-done((bf16[2,512,128]{2,1,0:T(8,128)(2,1)S(1)}, bf16[2,512,128]{2,1,0:T(8,128)(2,1)S(1)}, u32[]{:S(2)}, u32[]{:S(2)}) %collective-permute-start.1) | collective-permute-done | bytes 262176 | tf_op jit(solution)/shard_map/ppermute | solution.py:591
  23.6 3.4 %collective-permute-start.2 = (bf16[2,512,128]{2,1,0:T(8,128)(2,1)S(1)}, bf16[2,512,128]{2,1,0:T(8,128)(2,1)S(1)}, u32[]{:S(2)}, u32[]{:S(2)}) collective-permute-start(bf16[2,512,128]{2,1,0:T(8,128)(2,1)S(1)} %collective-permute-done.1.refs_3_), channel_id=1, source_target_pairs={{0,4},{4,8},{8,12},{1,5},{5,9},{9,13},{16,20},{20,24},{24,28},{17,... | collective-permute-start | bytes 786440 | tf_op jit(solution)/shard_map/ppermute | solution.py:604
  27.2 0.7 collective-permute-start.8
  27.9 3.8 %filterbank.4 = (bf16[1,16,2,16,128]{4,3,2,1,0:T(8,128)(2,1)S(1)}, bf16[1,16,2,16,128]{4,3,2,1,0:T(8,128)(2,1)S(1)}, bf16[1,16,2,16,128]{4,3,2,1,0:T(8,128)(2,1)S(1)}, bf16[1,16,2,16,128]{4,3,2,1,0:T(8,128)(2,1)S(1)}) custom-call(s32[12]{0:T(128)S(1)} %concatenate.3.meta.refs_0_, bf16[2,2,512,128]{3,2,1,0:T(8,128)(2,1)S(1)} %get-tuple-element.68.refs_1_, ...), custom_call_target="tpu_custom_call" | custom-call | flops 1000000 | bytes 262144 | tf_op jit(solution)/shard_map/filterbank/pallas_call | solution.py:277
  31.8 4.0 %collective-permute-start.12 = (bf16[2,512,128]{2,1,0:T(8,128)(2,1)S(1)}, bf16[2,512,128]{2,1,0:T(8,128)(2,1)S(1)}, u32[]{:S(2)}, u32[]{:S(2)}) collective-permute-start(bf16[2,512,128]{2,1,0:T(8,128)(2,1)S(1)} %collective-permute-done.11.refs_3_), channel_id=1, source_target_pairs={{0,4},{4,8},{8,12},{1,5},{5,9},{9,13},{16,20},{20,24},{24,28},{17,... | collective-permute-start | bytes 786440 | tf_op jit(solution)/shard_map/ppermute | solution.py:604
  35.8 3.8 %filterbank.5 = (bf16[2,16,2,16,128]{4,3,2,1,0:T(8,128)(2,1)S(1)}, bf16[2,16,2,16,128]{4,3,2,1,0:T(8,128)(2,1)S(1)}, bf16[2,16,2,16,128]{4,3,2,1,0:T(8,128)(2,1)S(1)}, bf16[2,16,2,16,128]{4,3,2,1,0:T(8,128)(2,1)S(1)}) custom-call(s32[12]{0:T(128)S(1)} %concatenate.3.meta.refs_0_, bf16[2,2,512,128]{3,2,1,0:T(8,128)(2,1)S(1)} %get-tuple-element.68.refs_1_, ...), custom_call_target="tpu_custom_call" | custom-call | flops 1000000 | bytes 262144 | tf_op jit(solution)/shard_map/filterbank/pallas_call | solution.py:277
  39.6 3.5 %collective-permute-start.10 = (bf16[2,512,128]{2,1,0:T(8,128)(2,1)S(1)}, bf16[2,512,128]{2,1,0:T(8,128)(2,1)S(1)}, u32[]{:S(2)}, u32[]{:S(2)}) collective-permute-start(bf16[2,512,128]{2,1,0:T(8,128)(2,1)S(1)} %collective-permute-done.9.refs_3_), channel_id=1, source_target_pairs={{0,4},{4,8},{8,12},{1,5},{5,9},{9,13},{16,20},{20,24},{24,28},{17,... | collective-permute-start | bytes 786440 | tf_op jit(solution)/shard_map/ppermute | solution.py:604
  43.1 1.6 %collective-permute-start.5 = (bf16[2,16,2,16,128]{4,3,2,1,0:T(8,128)(2,1)S(1)}, bf16[2,16,2,16,128]{4,3,2,1,0:T(8,128)(2,1)S(1)}, u32[]{:S(2)}, u32[]{:S(2)}) collective-permute-start(bf16[2,16,2,16,128]{4,3,2,1,0:T(8,128)(2,1)S(1)} %get-tuple-element.77), channel_id=1, source_target_pairs={{0,1},{1,0},{2,3},{3,2},{4,5},{5,4},{6,7},{7,6},{8,9},{9,8},{10,11... | collective-permute-start | bytes 786440 | tf_op jit(solution)/shard_map/ppermute | solution.py:622
  44.7 2.0 %collective-permute-start.7 = (bf16[2,16,2,16,128]{4,3,2,1,0:T(8,128)(2,1)S(1)}, bf16[2,16,2,16,128]{4,3,2,1,0:T(8,128)(2,1)S(1)}, u32[]{:S(2)}, u32[]{:S(2)}) collective-permute-start(bf16[2,16,2,16,128]{4,3,2,1,0:T(8,128)(2,1)S(1)} %get-tuple-element.79), channel_id=1, source_target_pairs={{0,3},{1,2},{2,1},{3,0},{4,7},{5,6},{6,5},{7,4},{8,11},{9,10},{10,... | collective-permute-start | bytes 786440 | tf_op jit(solution)/shard_map/ppermute | solution.py:622
  46.7 3.8 %filterbank.6 = (bf16[1,16,2,16,128]{4,3,2,1,0:T(8,128)(2,1)S(1)}, bf16[1,16,2,16,128]{4,3,2,1,0:T(8,128)(2,1)S(1)}, bf16[1,16,2,16,128]{4,3,2,1,0:T(8,128)(2,1)S(1)}, bf16[1,16,2,16,128]{4,3,2,1,0:T(8,128)(2,1)S(1)}) custom-call(s32[12]{0:T(128)S(1)} %concatenate.3.meta.refs_0_, bf16[2,2,512,128]{3,2,1,0:T(8,128)(2,1)S(1)} %get-tuple-element.81.refs_1_, ...), custom_call_target="tpu_custom_call" | custom-call | flops 1000000 | bytes 262144 | tf_op jit(solution)/shard_map/filterbank/pallas_call | solution.py:277
  50.5 4.0 %filterbank.7 = (bf16[2,16,2,16,128]{4,3,2,1,0:T(8,128)(2,1)S(1)}, bf16[2,16,2,16,128]{4,3,2,1,0:T(8,128)(2,1)S(1)}, bf16[2,16,2,16,128]{4,3,2,1,0:T(8,128)(2,1)S(1)}, bf16[2,16,2,16,128]{4,3,2,1,0:T(8,128)(2,1)S(1)}) custom-call(s32[12]{0:T(128)S(1)} %concatenate.3.meta.refs_0_, bf16[2,2,512,128]{3,2,1,0:T(8,128)(2,1)S(1)} %get-tuple-element.81.refs_1_, ...), custom_call_target="tpu_custom_call" | custom-call | flops 1000000 | bytes 262144 | tf_op jit(solution)/shard_map/filterbank/pallas_call | solution.py:277
  54.6 0.5 collective-permute-start.17
  55.1 0.1 collective-permute-start.18
  55.2 0.4 collective-permute-start.19
  55.6 1.1 %collective-permute-start.15 = (bf16[2,16,2,16,128]{4,3,2,1,0:T(8,128)(2,1)S(1)}, bf16[2,16,2,16,128]{4,3,2,1,0:T(8,128)(2,1)S(1)}, u32[]{:S(2)}, u32[]{:S(2)}) collective-permute-start(bf16[2,16,2,16,128]{4,3,2,1,0:T(8,128)(2,1)S(1)} %get-tuple-element.100), channel_id=1, source_target_pairs={{0,3},{1,2},{2,1},{3,0},{4,7},{5,6},{6,5},{7,4},{8,11},{9,10},{10,... | collective-permute-start | bytes 786440 | tf_op jit(solution)/shard_map/ppermute | solution.py:622
  56.7 1.8 %collective-permute-start.14 = (bf16[2,16,2,16,128]{4,3,2,1,0:T(8,128)(2,1)S(1)}, bf16[2,16,2,16,128]{4,3,2,1,0:T(8,128)(2,1)S(1)}, u32[]{:S(2)}, u32[]{:S(2)}) collective-permute-start(bf16[2,16,2,16,128]{4,3,2,1,0:T(8,128)(2,1)S(1)} %get-tuple-element.98), channel_id=1, source_target_pairs={{0,2},{1,3},{2,0},{3,1},{4,6},{5,7},{6,4},{7,5},{8,10},{9,11},{10,... | collective-permute-start | bytes 786440 | tf_op jit(solution)/shard_map/ppermute | solution.py:622
  58.6 0.5 collective-permute-start.13
  59.1 4.5 %correlate_early.1 = (f32[272,128]{1,0:T(8,128)S(1)}, bf16[272,128]{1,0:T(8,128)(2,1)S(1)}, bf16[272,128]{1,0:T(8,128)(2,1)S(1)}, bf16[272,128]{1,0:T(8,128)(2,1)S(1)}) custom-call(s32[12]{0:T(128)S(1)} %concatenate.3.meta.refs_0_, bf16[2,16,2,16,128]{4,3,2,1,0:T(8,128)(2,1)S(1)} %get-tuple-element.101.refs_1_, ...), custom_call_target="tpu_custom_call" | custom-call | flops 1000000 | bytes 262144 | tf_op jit(solution)/shard_map/correlate_early/pallas_call | solution.py:445
  63.6 2.1 %collective-permute-done.15.refs_8_ = bf16[2,16,2,16,128]{4,3,2,1,0:T(8,128)(2,1)S(1)} collective-permute-done((bf16[2,16,2,16,128]{4,3,2,1,0:T(8,128)(2,1)S(1)}, bf16[2,16,2,16,128]{4,3,2,1,0:T(8,128)(2,1)S(1)}, u32[]{:S(2)}, u32[]{:S(2)}) %collective-permute-start.15) | collective-permute-done | bytes 262176 | tf_op jit(solution)/shard_map/ppermute | solution.py:622
  65.7 4.8 %collective-permute-done.14.refs_7_ = bf16[2,16,2,16,128]{4,3,2,1,0:T(8,128)(2,1)S(1)} collective-permute-done((bf16[2,16,2,16,128]{4,3,2,1,0:T(8,128)(2,1)S(1)}, bf16[2,16,2,16,128]{4,3,2,1,0:T(8,128)(2,1)S(1)}, u32[]{:S(2)}, u32[]{:S(2)}) %collective-permute-start.14) | collective-permute-done | bytes 262176 | tf_op jit(solution)/shard_map/ppermute | solution.py:622
  70.5 0.5 collective-permute-start.21
  71.0 0.5 collective-permute-start.23
  71.5 0.5 collective-permute-done.20.refs_13_
  72.0 0.4 collective-permute-done.21.refs_14_
  72.4 0.4 collective-permute-done.22.refs_15_
  72.8 0.4 collective-permute-done.23.refs_16_
  73.2 1.6 %collective-permute-start.25 = (bf16[272,128]{1,0:T(8,128)(2,1)S(1)}, bf16[272,128]{1,0:T(8,128)(2,1)S(1)}, u32[]{:S(2)}, u32[]{:S(2)}) collective-permute-start(bf16[272,128]{1,0:T(8,128)(2,1)S(1)} %get-tuple-element.113), channel_id=1, source_target_pairs={{0,8},{2,10},{4,12},{6,14},{8,0},{10,2},{12,4},{14,6},{1,9},{3,11}... | collective-permute-start | bytes 208904 | tf_op jit(solution)/shard_map/ppermute | solution.py:641
  74.7 0.5 collective-permute-start.24
  75.2 6.0 %correlate_own.1 = (f32[400,128]{1,0:T(8,128)S(1)}, bf16[400,128]{1,0:T(8,128)(2,1)S(1)}, bf16[400,128]{1,0:T(8,128)(2,1)S(1)}, bf16[400,128]{1,0:T(8,128)(2,1)S(1)}) custom-call(s32[12]{0:T(128)S(1)} %concatenate.3.meta.refs_0_, bf16[2,16,2,16,128]{4,3,2,1,0:T(8,128)(2,1)S(1)} %get-tuple-element.101.refs_1_, ...), custom_call_target="tpu_custom_call" | custom-call | flops 1000000 | bytes 262144 | tf_op jit(solution)/shard_map/correlate_own/pallas_call | solution.py:445
  81.2 3.4 %collective-permute-start.29 = (bf16[400,128]{1,0:T(8,128)(2,1)S(1)}, bf16[400,128]{1,0:T(8,128)(2,1)S(1)}, u32[]{:S(2)}, u32[]{:S(2)}) collective-permute-start(bf16[400,128]{1,0:T(8,128)(2,1)S(1)} %get-tuple-element.123), channel_id=1, source_target_pairs={{0,12},{2,14},{4,0},{6,2},{8,4},{10,6},{12,8},{14,10},{1,13},{3,15... | collective-permute-start | bytes 307208 | tf_op jit(solution)/shard_map/ppermute | solution.py:641
  84.6 1.6 %collective-permute-start.27 = (bf16[400,128]{1,0:T(8,128)(2,1)S(1)}, bf16[400,128]{1,0:T(8,128)(2,1)S(1)}, u32[]{:S(2)}, u32[]{:S(2)}) collective-permute-start(bf16[400,128]{1,0:T(8,128)(2,1)S(1)} %get-tuple-element.119), channel_id=1, source_target_pairs={{0,4},{2,6},{4,8},{6,10},{8,12},{10,14},{12,0},{14,2},{1,5},{3,7},... | collective-permute-start | bytes 307208 | tf_op jit(solution)/shard_map/ppermute | solution.py:641
  86.2 6.3 %correlate_cross.1 = (f32[384,128]{1,0:T(8,128)S(1)}, bf16[384,128]{1,0:T(8,128)(2,1)S(1)}, bf16[384,128]{1,0:T(8,128)(2,1)S(1)}, bf16[384,128]{1,0:T(8,128)(2,1)S(1)}, f32[272,128]{1,0:T(8,128)S(1)}) custom-call(s32[12]{0:T(128)S(1)} %concatenate.3.meta.refs_0_, bf16[2,16,2,16,128]{4,3,2,1,0:T(8,128)(2,1)S(1)} %get-tuple-element.101.refs_1_, ...), custom_call_target="tpu_custom_call" | custom-call | flops 1000000 | bytes 262144 | tf_op jit(solution)/shard_map/correlate_cross/pallas_call | solution.py:445
  92.6 2.3 %collective-permute-start.32 = (bf16[384,128]{1,0:T(8,128)(2,1)S(1)}, bf16[384,128]{1,0:T(8,128)(2,1)S(1)}, u32[]{:S(2)}, u32[]{:S(2)}) collective-permute-start(bf16[384,128]{1,0:T(8,128)(2,1)S(1)} %get-tuple-element.130), channel_id=1, source_target_pairs={{0,12},{2,14},{4,0},{6,2},{8,4},{10,6},{12,8},{14,10},{1,13},{3,15... | collective-permute-start | bytes 294920 | tf_op jit(solution)/shard_map/ppermute | solution.py:641
  94.9 1.1 collective-permute-start.31
  96.0 2.1 %collective-permute-done.32.refs_9_ = bf16[384,128]{1,0:T(8,128)(2,1)S(1)} collective-permute-done((bf16[384,128]{1,0:T(8,128)(2,1)S(1)}, bf16[384,128]{1,0:T(8,128)(2,1)S(1)}, u32[]{:S(2)}, u32[]{:S(2)}) %collective-permute-start.32) | collective-permute-done | bytes 98336 | tf_op jit(solution)/shard_map/ppermute | solution.py:641
  98.1 7.3 %collective-permute-done.31.refs_8_ = bf16[384,128]{1,0:T(8,128)(2,1)S(1)} collective-permute-done((bf16[384,128]{1,0:T(8,128)(2,1)S(1)}, bf16[384,128]{1,0:T(8,128)(2,1)S(1)}, u32[]{:S(2)}, u32[]{:S(2)}) %collective-permute-start.31) | collective-permute-done | bytes 98336 | tf_op jit(solution)/shard_map/ppermute | solution.py:641
  105.4 0.5 collective-permute-start.35
  105.9 0.8 collective-permute-done.36.refs_13_
  106.7 0.2 collective-permute-done.35.refs_12_
  106.9 3.6 %assemble.1 = f32[2,16,32,256]{3,2,1,0:T(8,128)} custom-call(s32[12]{0:T(128)S(1)} %concatenate.3.meta.refs_0_, f32[272,128]{1,0:T(8,128)S(1)} %get-tuple-element.116.refs_1_, f32[400,128]{1,0:T(8,128)S(1)} %get-tuple-element.117.refs_2_, bf16[400,128]{1,0:T(8,128)(2,1)S(1)} %collective-permute-done.27.refs_3_, ...), custom_call_target="tpu_custom_call" | custom-call | flops 1000000 | bytes 262144 | tf_op jit(solution)/shard_map/assemble/pallas_call | solution.py:529
  (50 shorter events, 0.4 us)
Async XLA Ops:
  0.0 27.9 %copy-start = (f32[16,64,128]{2,1,0:T(8,128)S(1)}, f32[16,64,128]{2,1,0:T(8,128)}, u32[]{:S(2)}) copy-start(f32[16,64,128]{2,1,0:T(8,128)} %constant.46.clone.refs_5_) | copy-start | bytes 1572868
  0.8 1.6 %copy-start.1 = (bf16[2,8,65536]{2,1,0:T(8,128)(2,1)S(1)}, bf16[2,8,65536]{2,1,0:T(8,128)(2,1)}, u32[]{:S(2)}) copy-start(bf16[2,8,65536]{2,1,0:T(8,128)(2,1)} %block.1) | copy-start | bytes 6291460
  2.4 25.5 %copy-start.2 = (bf16[2,4,32,128]{3,2,1,0:T(8,128)(2,1)S(1)}, bf16[2,4,32,128]{3,2,1,0:T(8,128)(2,1)}, u32[]{:S(2)}) copy-start(bf16[2,4,32,128]{3,2,1,0:T(8,128)(2,1)} %constant.50.clone.refs_9_) | copy-start | bytes 196612
  2.4 25.5 %copy-start.3 = (f32[64,128]{1,0:T(8,128)S(1)}, f32[64,128]{1,0:T(8,128)}, u32[]{:S(2)}) copy-start(f32[64,128]{1,0:T(8,128)} %constant.49.clone.refs_8_) | copy-start | bytes 98308
  2.4 25.5 %copy-start.4 = (f32[64,128]{1,0:T(8,128)S(1)}, f32[64,128]{1,0:T(8,128)}, u32[]{:S(2)}) copy-start(f32[64,128]{1,0:T(8,128)} %constant.48.clone.refs_7_) | copy-start | bytes 98308
  2.4 25.5 %copy-start.5 = (bf16[128,128]{1,0:T(8,128)(2,1)S(1)}, bf16[128,128]{1,0:T(8,128)(2,1)}, u32[]{:S(2)}) copy-start(bf16[128,128]{1,0:T(8,128)(2,1)} %constant.47.clone.refs_6_) | copy-start | bytes 98308
  4.7 22.4 %collective-permute-start = (bf16[2,2,512,128]{3,2,1,0:T(8,128)(2,1)S(1)}, bf16[2,2,512,128]{3,2,1,0:T(8,128)(2,1)S(1)}, u32[]{:S(2)}, u32[]{:S(2)}) collective-permute-start(bf16[2,2,512,128]{3,2,1,0:T(8,128)(2,1)S(1)} %get-tuple-element.68.refs_1_), channel_id=1, source_target_pairs={{2,6},{6,10},{10,14},{3,7},{7,11},{11,15},{18,22},{22,26},{26,30},... | collective-permute-start | bytes 1572872 | tf_op jit(solution)/shard_map/ppermute | solution.py:595
  5.4 13.0 %collective-permute-start.3 = (bf16[2,512,128]{2,1,0:T(8,128)(2,1)S(1)}, bf16[2,512,128]{2,1,0:T(8,128)(2,1)S(1)}, u32[]{:S(2)}, u32[]{:S(2)}) collective-permute-start(bf16[2,512,128]{2,1,0:T(8,128)(2,1)S(1)} %get-tuple-element.70), channel_id=1, source_target_pairs={{0,2},{2,0},{4,6},{6,4},{8,10},{10,8},{12,14},{14,12},{1,3},{3,1},... | collective-permute-start | bytes 786440 | tf_op jit(solution)/shard_map/ppermute | solution.py:591
  11.2 12.4 %collective-permute-start.1 = (bf16[2,512,128]{2,1,0:T(8,128)(2,1)S(1)}, bf16[2,512,128]{2,1,0:T(8,128)(2,1)S(1)}, u32[]{:S(2)}, u32[]{:S(2)}) collective-permute-start(bf16[2,512,128]{2,1,0:T(8,128)(2,1)S(1)} %get-tuple-element.69), channel_id=1, source_target_pairs={{0,2},{2,0},{4,6},{6,4},{8,10},{10,8},{12,14},{14,12},{1,3},{3,1},... | collective-permute-start | bytes 786440 | tf_op jit(solution)/shard_map/ppermute | solution.py:591
  18.4 9.5 %collective-permute-start.4 = (bf16[2,512,128]{2,1,0:T(8,128)(2,1)S(1)}, bf16[2,512,128]{2,1,0:T(8,128)(2,1)S(1)}, u32[]{:S(2)}, u32[]{:S(2)}) collective-permute-start(bf16[2,512,128]{2,1,0:T(8,128)(2,1)S(1)} %collective-permute-done.3.refs_3_), channel_id=1, source_target_pairs={{0,4},{4,8},{8,12},{1,5},{5,9},{9,13},{16,20},{20,24},{24,28},{17,... | collective-permute-start | bytes 786440 | tf_op jit(solution)/shard_map/ppermute | solution.py:604
  21.9 9.8 %collective-permute-start.11 = (bf16[2,512,128]{2,1,0:T(8,128)(2,1)S(1)}, bf16[2,512,128]{2,1,0:T(8,128)(2,1)S(1)}, u32[]{:S(2)}, u32[]{:S(2)}) collective-permute-start(bf16[2,512,128]{2,1,0:T(8,128)(2,1)S(1)} %get-tuple-element.86), channel_id=1, source_target_pairs={{0,2},{2,0},{4,6},{6,4},{8,10},{10,8},{12,14},{14,12},{1,3},{3,1},... | collective-permute-start | bytes 786440 | tf_op jit(solution)/shard_map/ppermute | solution.py:591
  23.6 8.1 %collective-permute-start.2 = (bf16[2,512,128]{2,1,0:T(8,128)(2,1)S(1)}, bf16[2,512,128]{2,1,0:T(8,128)(2,1)S(1)}, u32[]{:S(2)}, u32[]{:S(2)}) collective-permute-start(bf16[2,512,128]{2,1,0:T(8,128)(2,1)S(1)} %collective-permute-done.1.refs_3_), channel_id=1, source_target_pairs={{0,4},{4,8},{8,12},{1,5},{5,9},{9,13},{16,20},{20,24},{24,28},{17,... | collective-permute-start | bytes 786440 | tf_op jit(solution)/shard_map/ppermute | solution.py:604
  27.1 12.5 %collective-permute-start.9 = (bf16[2,512,128]{2,1,0:T(8,128)(2,1)S(1)}, bf16[2,512,128]{2,1,0:T(8,128)(2,1)S(1)}, u32[]{:S(2)}, u32[]{:S(2)}) collective-permute-start(bf16[2,512,128]{2,1,0:T(8,128)(2,1)S(1)} %get-tuple-element.83), channel_id=1, source_target_pairs={{0,2},{2,0},{4,6},{6,4},{8,10},{10,8},{12,14},{14,12},{1,3},{3,1},... | collective-permute-start | bytes 786440 | tf_op jit(solution)/shard_map/ppermute | solution.py:591
  27.2 19.5 %collective-permute-start.8 = (bf16[2,2,512,128]{3,2,1,0:T(8,128)(2,1)S(1)}, bf16[2,2,512,128]{3,2,1,0:T(8,128)(2,1)S(1)}, u32[]{:S(2)}, u32[]{:S(2)}) collective-permute-start(bf16[2,2,512,128]{3,2,1,0:T(8,128)(2,1)S(1)} %get-tuple-element.81.refs_1_), channel_id=1, source_target_pairs={{2,6},{6,10},{10,14},{3,7},{7,11},{11,15},{18,22},{22,26},{26,30},... | collective-permute-start | bytes 1572872 | tf_op jit(solution)/shard_map/ppermute | solution.py:595
  31.8 12.9 %collective-permute-start.12 = (bf16[2,512,128]{2,1,0:T(8,128)(2,1)S(1)}, bf16[2,512,128]{2,1,0:T(8,128)(2,1)S(1)}, u32[]{:S(2)}, u32[]{:S(2)}) collective-permute-start(bf16[2,512,128]{2,1,0:T(8,128)(2,1)S(1)} %collective-permute-done.11.refs_3_), channel_id=1, source_target_pairs={{0,4},{4,8},{8,12},{1,5},{5,9},{9,13},{16,20},{20,24},{24,28},{17,... | collective-permute-start | bytes 786440 | tf_op jit(solution)/shard_map/ppermute | solution.py:604
  39.6 10.9 %collective-permute-start.10 = (bf16[2,512,128]{2,1,0:T(8,128)(2,1)S(1)}, bf16[2,512,128]{2,1,0:T(8,128)(2,1)S(1)}, u32[]{:S(2)}, u32[]{:S(2)}) collective-permute-start(bf16[2,512,128]{2,1,0:T(8,128)(2,1)S(1)} %collective-permute-done.9.refs_3_), channel_id=1, source_target_pairs={{0,4},{4,8},{8,12},{1,5},{5,9},{9,13},{16,20},{20,24},{24,28},{17,... | collective-permute-start | bytes 786440 | tf_op jit(solution)/shard_map/ppermute | solution.py:604
  43.1 11.5 %collective-permute-start.5 = (bf16[2,16,2,16,128]{4,3,2,1,0:T(8,128)(2,1)S(1)}, bf16[2,16,2,16,128]{4,3,2,1,0:T(8,128)(2,1)S(1)}, u32[]{:S(2)}, u32[]{:S(2)}) collective-permute-start(bf16[2,16,2,16,128]{4,3,2,1,0:T(8,128)(2,1)S(1)} %get-tuple-element.77), channel_id=1, source_target_pairs={{0,1},{1,0},{2,3},{3,2},{4,5},{5,4},{6,7},{7,6},{8,9},{9,8},{10,11... | collective-permute-start | bytes 786440 | tf_op jit(solution)/shard_map/ppermute | solution.py:622
  44.7 10.4 %collective-permute-start.6 = (bf16[2,16,2,16,128]{4,3,2,1,0:T(8,128)(2,1)S(1)}, bf16[2,16,2,16,128]{4,3,2,1,0:T(8,128)(2,1)S(1)}, u32[]{:S(2)}, u32[]{:S(2)}) collective-permute-start(bf16[2,16,2,16,128]{4,3,2,1,0:T(8,128)(2,1)S(1)} %get-tuple-element.78), channel_id=1, source_target_pairs={{0,2},{1,3},{2,0},{3,1},{4,6},{5,7},{6,4},{7,5},{8,10},{9,11},{10,... | collective-permute-start | bytes 786440 | tf_op jit(solution)/shard_map/ppermute | solution.py:622
  44.7 10.4 %collective-permute-start.7 = (bf16[2,16,2,16,128]{4,3,2,1,0:T(8,128)(2,1)S(1)}, bf16[2,16,2,16,128]{4,3,2,1,0:T(8,128)(2,1)S(1)}, u32[]{:S(2)}, u32[]{:S(2)}) collective-permute-start(bf16[2,16,2,16,128]{4,3,2,1,0:T(8,128)(2,1)S(1)} %get-tuple-element.79), channel_id=1, source_target_pairs={{0,3},{1,2},{2,1},{3,0},{4,7},{5,6},{6,5},{7,4},{8,11},{9,10},{10,... | collective-permute-start | bytes 786440 | tf_op jit(solution)/shard_map/ppermute | solution.py:622
  54.5 2.2 %collective-permute-start.16 = (bf16[2,16,2,16,128]{4,3,2,1,0:T(8,128)(2,1)S(1)}, bf16[2,16,2,16,128]{4,3,2,1,0:T(8,128)(2,1)S(1)}, u32[]{:S(2)}, u32[]{:S(2)}) collective-permute-start(bf16[2,16,2,16,128]{4,3,2,1,0:T(8,128)(2,1)S(1)} %get-tuple-element.101.refs_1_), channel_id=1, source_target_pairs={{0,16},{16,0},{1,17},{17,1},{2,18},{18,2},{3,19},{19,3},{4,20},{20... | collective-permute-start | bytes 786440 | tf_op jit(solution)/shard_map/ppermute | solution.py:629
  54.6 4.0 %collective-permute-start.17 = (bf16[2,16,2,16,128]{4,3,2,1,0:T(8,128)(2,1)S(1)}, bf16[2,16,2,16,128]{4,3,2,1,0:T(8,128)(2,1)S(1)}, u32[]{:S(2)}, u32[]{:S(2)}) collective-permute-start(bf16[2,16,2,16,128]{4,3,2,1,0:T(8,128)(2,1)S(1)} %collective-permute-done.5.refs_2_), channel_id=1, source_target_pairs={{0,16},{16,0},{1,17},{17,1},{2,18},{18,2},{3,19},{19,3},{4,20},{20... | collective-permute-start | bytes 786440 | tf_op jit(solution)/shard_map/ppermute | solution.py:629
  55.1 4.0 %collective-permute-start.18 = (bf16[2,16,2,16,128]{4,3,2,1,0:T(8,128)(2,1)S(1)}, bf16[2,16,2,16,128]{4,3,2,1,0:T(8,128)(2,1)S(1)}, u32[]{:S(2)}, u32[]{:S(2)}) collective-permute-start(bf16[2,16,2,16,128]{4,3,2,1,0:T(8,128)(2,1)S(1)} %collective-permute-done.6.refs_3_), channel_id=1, source_target_pairs={{0,16},{16,0},{1,17},{17,1},{2,18},{18,2},{3,19},{19,3},{4,20},{20... | collective-permute-start | bytes 786440 | tf_op jit(solution)/shard_map/ppermute | solution.py:629
  55.2 3.9 %collective-permute-start.19 = (bf16[2,16,2,16,128]{4,3,2,1,0:T(8,128)(2,1)S(1)}, bf16[2,16,2,16,128]{4,3,2,1,0:T(8,128)(2,1)S(1)}, u32[]{:S(2)}, u32[]{:S(2)}) collective-permute-start(bf16[2,16,2,16,128]{4,3,2,1,0:T(8,128)(2,1)S(1)} %collective-permute-done.7.refs_4_), channel_id=1, source_target_pairs={{0,16},{16,0},{1,17},{17,1},{2,18},{18,2},{3,19},{19,3},{4,20},{20... | collective-permute-start | bytes 786440 | tf_op jit(solution)/shard_map/ppermute | solution.py:629
  55.6 10.1 %collective-permute-start.15 = (bf16[2,16,2,16,128]{4,3,2,1,0:T(8,128)(2,1)S(1)}, bf16[2,16,2,16,128]{4,3,2,1,0:T(8,128)(2,1)S(1)}, u32[]{:S(2)}, u32[]{:S(2)}) collective-permute-start(bf16[2,16,2,16,128]{4,3,2,1,0:T(8,128)(2,1)S(1)} %get-tuple-element.100), channel_id=1, source_target_pairs={{0,3},{1,2},{2,1},{3,0},{4,7},{5,6},{6,5},{7,4},{8,11},{9,10},{10,... | collective-permute-start | bytes 786440 | tf_op jit(solution)/shard_map/ppermute | solution.py:622
  56.7 13.8 %collective-permute-start.14 = (bf16[2,16,2,16,128]{4,3,2,1,0:T(8,128)(2,1)S(1)}, bf16[2,16,2,16,128]{4,3,2,1,0:T(8,128)(2,1)S(1)}, u32[]{:S(2)}, u32[]{:S(2)}) collective-permute-start(bf16[2,16,2,16,128]{4,3,2,1,0:T(8,128)(2,1)S(1)} %get-tuple-element.98), channel_id=1, source_target_pairs={{0,2},{1,3},{2,0},{3,1},{4,6},{5,7},{6,4},{7,5},{8,10},{9,11},{10,... | collective-permute-start | bytes 786440 | tf_op jit(solution)/shard_map/ppermute | solution.py:622
  58.6 11.9 %collective-permute-start.13 = (bf16[2,16,2,16,128]{4,3,2,1,0:T(8,128)(2,1)S(1)}, bf16[2,16,2,16,128]{4,3,2,1,0:T(8,128)(2,1)S(1)}, u32[]{:S(2)}, u32[]{:S(2)}) collective-permute-start(bf16[2,16,2,16,128]{4,3,2,1,0:T(8,128)(2,1)S(1)} %get-tuple-element.96), channel_id=1, source_target_pairs={{0,1},{1,0},{2,3},{3,2},{4,5},{5,4},{6,7},{7,6},{8,9},{9,8},{10,11... | collective-permute-start | bytes 786440 | tf_op jit(solution)/shard_map/ppermute | solution.py:622
  70.5 1.5 %collective-permute-start.20 = (bf16[2,16,2,16,128]{4,3,2,1,0:T(8,128)(2,1)S(1)}, bf16[2,16,2,16,128]{4,3,2,1,0:T(8,128)(2,1)S(1)}, u32[]{:S(2)}, u32[]{:S(2)}) collective-permute-start(bf16[2,16,2,16,128]{4,3,2,1,0:T(8,128)(2,1)S(1)} %get-tuple-element.106.refs_5_), channel_id=1, source_target_pairs={{0,16},{16,0},{1,17},{17,1},{2,18},{18,2},{3,19},{19,3},{4,20},{20... | collective-permute-start | bytes 786440 | tf_op jit(solution)/shard_map/ppermute | solution.py:634
  70.5 1.9 %collective-permute-start.21 = (bf16[2,16,2,16,128]{4,3,2,1,0:T(8,128)(2,1)S(1)}, bf16[2,16,2,16,128]{4,3,2,1,0:T(8,128)(2,1)S(1)}, u32[]{:S(2)}, u32[]{:S(2)}) collective-permute-start(bf16[2,16,2,16,128]{4,3,2,1,0:T(8,128)(2,1)S(1)} %collective-permute-done.13.refs_6_), channel_id=1, source_target_pairs={{0,16},{16,0},{1,17},{17,1},{2,18},{18,2},{3,19},{19,3},{4,20},{20... | collective-permute-start | bytes 786440 | tf_op jit(solution)/shard_map/ppermute | solution.py:634
  71.0 1.8 %collective-permute-start.22 = (bf16[2,16,2,16,128]{4,3,2,1,0:T(8,128)(2,1)S(1)}, bf16[2,16,2,16,128]{4,3,2,1,0:T(8,128)(2,1)S(1)}, u32[]{:S(2)}, u32[]{:S(2)}) collective-permute-start(bf16[2,16,2,16,128]{4,3,2,1,0:T(8,128)(2,1)S(1)} %collective-permute-done.14.refs_7_), channel_id=1, source_target_pairs={{0,16},{16,0},{1,17},{17,1},{2,18},{18,2},{3,19},{19,3},{4,20},{20... | collective-permute-start | bytes 786440 | tf_op jit(solution)/shard_map/ppermute | solution.py:634
  71.0 2.1 %collective-permute-start.23 = (bf16[2,16,2,16,128]{4,3,2,1,0:T(8,128)(2,1)S(1)}, bf16[2,16,2,16,128]{4,3,2,1,0:T(8,128)(2,1)S(1)}, u32[]{:S(2)}, u32[]{:S(2)}) collective-permute-start(bf16[2,16,2,16,128]{4,3,2,1,0:T(8,128)(2,1)S(1)} %collective-permute-done.15.refs_8_), channel_id=1, source_target_pairs={{0,16},{16,0},{1,17},{17,1},{2,18},{18,2},{3,19},{19,3},{4,20},{20... | collective-permute-start | bytes 786440 | tf_op jit(solution)/shard_map/ppermute | solution.py:634
  73.2 8.0 %collective-permute-start.26 = (bf16[272,128]{1,0:T(8,128)(2,1)S(1)}, bf16[272,128]{1,0:T(8,128)(2,1)S(1)}, u32[]{:S(2)}, u32[]{:S(2)}) collective-permute-start(bf16[272,128]{1,0:T(8,128)(2,1)S(1)} %get-tuple-element.115), channel_id=1, source_target_pairs={{0,12},{2,14},{4,0},{6,2},{8,4},{10,6},{12,8},{14,10},{1,13},{3,15... | collective-permute-start | bytes 208904 | tf_op jit(solution)/shard_map/ppermute | solution.py:641
  73.2 11.5 %collective-permute-start.25 = (bf16[272,128]{1,0:T(8,128)(2,1)S(1)}, bf16[272,128]{1,0:T(8,128)(2,1)S(1)}, u32[]{:S(2)}, u32[]{:S(2)}) collective-permute-start(bf16[272,128]{1,0:T(8,128)(2,1)S(1)} %get-tuple-element.113), channel_id=1, source_target_pairs={{0,8},{2,10},{4,12},{6,14},{8,0},{10,2},{12,4},{14,6},{1,9},{3,11}... | collective-permute-start | bytes 208904 | tf_op jit(solution)/shard_map/ppermute | solution.py:641
  74.7 9.9 %collective-permute-start.24 = (bf16[272,128]{1,0:T(8,128)(2,1)S(1)}, bf16[272,128]{1,0:T(8,128)(2,1)S(1)}, u32[]{:S(2)}, u32[]{:S(2)}) collective-permute-start(bf16[272,128]{1,0:T(8,128)(2,1)S(1)} %get-tuple-element.111), channel_id=1, source_target_pairs={{0,4},{2,6},{4,8},{6,10},{8,12},{10,14},{12,0},{14,2},{1,5},{3,7},... | collective-permute-start | bytes 208904 | tf_op jit(solution)/shard_map/ppermute | solution.py:641
  81.2 11.4 %collective-permute-start.29 = (bf16[400,128]{1,0:T(8,128)(2,1)S(1)}, bf16[400,128]{1,0:T(8,128)(2,1)S(1)}, u32[]{:S(2)}, u32[]{:S(2)}) collective-permute-start(bf16[400,128]{1,0:T(8,128)(2,1)S(1)} %get-tuple-element.123), channel_id=1, source_target_pairs={{0,12},{2,14},{4,0},{6,2},{8,4},{10,6},{12,8},{14,10},{1,13},{3,15... | collective-permute-start | bytes 307208 | tf_op jit(solution)/shard_map/ppermute | solution.py:641
  84.6 10.3 %collective-permute-start.28 = (bf16[400,128]{1,0:T(8,128)(2,1)S(1)}, bf16[400,128]{1,0:T(8,128)(2,1)S(1)}, u32[]{:S(2)}, u32[]{:S(2)}) collective-permute-start(bf16[400,128]{1,0:T(8,128)(2,1)S(1)} %get-tuple-element.121), channel_id=1, source_target_pairs={{0,8},{2,10},{4,12},{6,14},{8,0},{10,2},{12,4},{14,6},{1,9},{3,11}... | collective-permute-start | bytes 307208 | tf_op jit(solution)/shard_map/ppermute | solution.py:641
  84.6 11.4 %collective-permute-start.27 = (bf16[400,128]{1,0:T(8,128)(2,1)S(1)}, bf16[400,128]{1,0:T(8,128)(2,1)S(1)}, u32[]{:S(2)}, u32[]{:S(2)}) collective-permute-start(bf16[400,128]{1,0:T(8,128)(2,1)S(1)} %get-tuple-element.119), channel_id=1, source_target_pairs={{0,4},{2,6},{4,8},{6,10},{8,12},{10,14},{12,0},{14,2},{1,5},{3,7},... | collective-permute-start | bytes 307208 | tf_op jit(solution)/shard_map/ppermute | solution.py:641
  92.5 13.5 %collective-permute-start.34 = (f32[384,128]{1,0:T(8,128)S(1)}, f32[384,128]{1,0:T(8,128)S(1)}, u32[]{:S(2)}, u32[]{:S(2)}) collective-permute-start(f32[384,128]{1,0:T(8,128)S(1)} %get-tuple-element.124.refs_6_), channel_id=1, source_target_pairs={{0,16},{16,0},{1,17},{17,1},{2,18},{18,2},{3,19},{19,3},{4,20},{20... | collective-permute-start | bytes 589832 | tf_op jit(solution)/shard_map/ppermute | solution.py:651
  92.6 5.5 %collective-permute-start.32 = (bf16[384,128]{1,0:T(8,128)(2,1)S(1)}, bf16[384,128]{1,0:T(8,128)(2,1)S(1)}, u32[]{:S(2)}, u32[]{:S(2)}) collective-permute-start(bf16[384,128]{1,0:T(8,128)(2,1)S(1)} %get-tuple-element.130), channel_id=1, source_target_pairs={{0,12},{2,14},{4,0},{6,2},{8,4},{10,6},{12,8},{14,10},{1,13},{3,15... | collective-permute-start | bytes 294920 | tf_op jit(solution)/shard_map/ppermute | solution.py:641
  94.9 10.5 %collective-permute-start.31 = (bf16[384,128]{1,0:T(8,128)(2,1)S(1)}, bf16[384,128]{1,0:T(8,128)(2,1)S(1)}, u32[]{:S(2)}, u32[]{:S(2)}) collective-permute-start(bf16[384,128]{1,0:T(8,128)(2,1)S(1)} %get-tuple-element.128), channel_id=1, source_target_pairs={{0,8},{2,10},{4,12},{6,14},{8,0},{10,2},{12,4},{14,6},{1,9},{3,11}... | collective-permute-start | bytes 294920 | tf_op jit(solution)/shard_map/ppermute | solution.py:641
  96.0 9.4 %collective-permute-start.30 = (bf16[384,128]{1,0:T(8,128)(2,1)S(1)}, bf16[384,128]{1,0:T(8,128)(2,1)S(1)}, u32[]{:S(2)}, u32[]{:S(2)}) collective-permute-start(bf16[384,128]{1,0:T(8,128)(2,1)S(1)} %get-tuple-element.126), channel_id=1, source_target_pairs={{0,4},{2,6},{4,8},{6,10},{8,12},{10,14},{12,0},{14,2},{1,5},{3,7},... | collective-permute-start | bytes 294920 | tf_op jit(solution)/shard_map/ppermute | solution.py:641
  96.0 9.9 %collective-permute-start.33 = (f32[272,128]{1,0:T(8,128)S(1)}, f32[272,128]{1,0:T(8,128)S(1)}, u32[]{:S(2)}, u32[]{:S(2)}) collective-permute-start(f32[272,128]{1,0:T(8,128)S(1)} %get-tuple-element.116.refs_1_), channel_id=1, source_target_pairs={{0,16},{16,0},{1,17},{17,1},{2,18},{18,2},{3,19},{19,3},{4,20},{20... | collective-permute-start | bytes 417800 | tf_op jit(solution)/shard_map/ppermute | solution.py:651
  98.1 7.9 %collective-permute-start.37 = (bf16[384,128]{1,0:T(8,128)(2,1)S(1)}, bf16[384,128]{1,0:T(8,128)(2,1)S(1)}, u32[]{:S(2)}, u32[]{:S(2)}) collective-permute-start(bf16[384,128]{1,0:T(8,128)(2,1)S(1)} %collective-permute-done.32.refs_9_), channel_id=1, source_target_pairs={{0,16},{16,0},{1,17},{17,1},{2,18},{18,2},{3,19},{19,3},{4,20},{20... | collective-permute-start | bytes 294920 | tf_op jit(solution)/shard_map/ppermute | solution.py:651
  105.4 1.3 %collective-permute-start.36 = (bf16[384,128]{1,0:T(8,128)(2,1)S(1)}, bf16[384,128]{1,0:T(8,128)(2,1)S(1)}, u32[]{:S(2)}, u32[]{:S(2)}) collective-permute-start(bf16[384,128]{1,0:T(8,128)(2,1)S(1)} %collective-permute-done.31.refs_8_), channel_id=1, source_target_pairs={{0,16},{16,0},{1,17},{17,1},{2,18},{18,2},{3,19},{19,3},{4,20},{20... | collective-permute-start | bytes 294920 | tf_op jit(solution)/shard_map/ppermute | solution.py:651
  105.4 1.5 %collective-permute-start.35 = (bf16[384,128]{1,0:T(8,128)(2,1)S(1)}, bf16[384,128]{1,0:T(8,128)(2,1)S(1)}, u32[]{:S(2)}, u32[]{:S(2)}) collective-permute-start(bf16[384,128]{1,0:T(8,128)(2,1)S(1)} %collective-permute-done.30.refs_7_), channel_id=1, source_target_pairs={{0,16},{16,0},{1,17},{17,1},{2,18},{18,2},{3,19},{19,3},{4,20},{20... | collective-permute-start | bytes 294920 | tf_op jit(solution)/shard_map/ppermute | solution.py:651

commit v9 on v8

--- a/solution.py
+++ b/solution.py
@@ -99,8 +99,7 @@
     tall = 128
     for item in range(inputs):
         first = (1 - g) * half + item if item < half else g * half + item - half
-        kept = item - half
-        out = outs[item] if item < half else outs[half + kept // JOIN].at[kept % JOIN]
+        out = outs[item // JOIN].at[item % JOIN]
 
         def gather(n, carry, first=first, out=out):
             low = pl.multiple_of(n * tall, tall)
@@ -116,7 +115,7 @@
     _, inputs, samples = block.shape
     half = inputs // PAIR
     one = (2, samples // LANES, LANES)
-    shapes = [one] * half + [(JOIN,) + one] * (half // JOIN)
+    shapes = [(JOIN,) + one] * (inputs // JOIN)
     return pl.pallas_call(
         functools.partial(pick_kernel, half),
         out_shape=[jax.ShapeDtypeStruct(s, jnp.bfloat16) for s in shapes],
@@ -133,84 +132,89 @@
     return lax.optimization_barrier((block, after))[0]
 
 
-HALF = 16
 SOME = 4
 
 
-def filterbank_kernel(index, before, frames, dests, per_ct, half_count, *refs):
-    meta, keep, halo_own, recv, halo_far, coef, first, tw_cos, tw_sin, last = refs[:10]
-    earlier = refs[10 : 10 + dests * (before > 0)]
-    refs = refs[10 + len(earlier) :]
-    outs = refs[:dests]
-    raw, weights, grouped = refs[dests : dests + 3]
-    filtered = refs[dests + 3 :]
+def filterbank_kernel(late, part, frames, dests, per_ct, half_count, *refs):
+    meta, refs = refs[0], refs[1:]
+    me, ct = meta[G_AT], meta[CT_AT]
+    if late:
+        keep, recv = refs[:2]
+        refs = refs[2:]
+    else:
+        halo, keep, recv = refs[:3]
+        refs = refs[3:]
+    coef, first, tw_cos, tw_sin, last = refs[:5]
+    beside = () if late else refs[5 : 5 + dests]
+    outs = refs[5 + len(beside) :][:dests]
+    raw, weights, grouped = refs[5 + len(beside) + dests :][:3]
+    filtered = refs[5 + len(beside) + dests + 3 :]
     block_rows = frames * ROWS
-    total = PAIR * frames
-    me, ct = meta[G_AT], meta[CT_AT]
-    delay = meta[DELAY_AT + me * half_count + index]
-    down = delay // LANES
-    across = delay % LANES
     lane = lax.broadcasted_iota(jnp.int32, (1, LANES), 1)
-    inside = lane < LANES - across
-    turned_in = lane >= across
     high = lane < RADIX
 
     def bring(source, place):
         tall = 128
 
         def step(n, carry):
-            for part in range(2):
-                value = source[part, pl.ds(pl.multiple_of(n * tall, tall), tall), :]
-                at = pl.multiple_of(place * block_rows + n * tall, tall)
-                raw[part, pl.ds(at, tall), :] = value
+            low = pl.multiple_of(n * tall, tall)
+            at = pl.multiple_of(place * block_rows + n * tall, tall)
+            for item in range(JOIN):
+                for c in range(2):
+                    raw[item, c, pl.ds(at, tall), :] = source[item, c, pl.ds(low, tall), :]
             return carry
 
         lax.fori_loop(0, block_rows // tall, step, 0)
 
-    @pl.when(me == 0)
-    def _():
-        bring(halo_far, 0)
-
-    @pl.when(me != 0)
-    def _():
-        bring(halo_own.at[index % JOIN], 0)
-
-    bring(keep.at[index % JOIN], 1 + me)
-    bring(recv, 2 - me)
-
-    back = lax.rem(LANES - across, LANES)
-    for tap in range(TAPS):
-        here = coef[tap, pl.ds(down, ROWS), :]
-        after = coef[tap, pl.ds(down + 1, ROWS), :]
-        weights[tap] = pltpu.roll(jnp.where(turned_in, here, after), back, 1)
-    for dest, old in zip(outs, earlier):
-        dest[:before] = old[...]
-
-    def filt(half, low, high_frame, band, part):
-        size = high_frame - low
+    if late:
+        bring(keep, me)
+        bring(recv, 1 - me)
+    else:
+        bring(halo, 0)
+        pl.when(me == 0)(lambda: bring(keep, 1))
+        pl.when(me != 0)(lambda: bring(recv, 1))
+        for dest, block in zip(outs, beside):
+            dest[:, frames // 2 :] = block[...]
+
+    downs, acrosses = [], []
+    for item in range(JOIN):
+        delay = meta[DELAY_AT + me * half_count + part * JOIN + item]
+        down, across = delay // LANES, delay % LANES
+        downs.append(down)
+        acrosses.append(across)
+        back = lax.rem(LANES - across, LANES)
+        for tap in range(TAPS):
+            here = coef[tap, pl.ds(down, ROWS), :]
+            after = coef[tap, pl.ds(down + 1, ROWS), :]
+            turned = pltpu.roll(jnp.where(lane >= across, here, after), back, 1)
+            weights[item, tap] = turned
+
+    def filt(item, low, end, band, c):
+        size = end - low
         values = []
         for u in range(size + TAPS - 1):
-            at = (half * HALF + low + u + frames - TAPS) * ROWS + band * 16
-            values.append(raw[part, at : at + 16, :].astype(jnp.float32))
+            at = (low + u + frames - TAPS) * ROWS + band * 16
+            values.append(raw[item, c, at : at + 16, :].astype(jnp.float32))
         sums = [None] * size
         for tap in range(TAPS):
-            weight = weights[tap, band * 16 : band * 16 + 16, :]
+            weight = weights[item, tap, band * 16 : band * 16 + 16, :]
             for u in range(size):
                 term = weight * values[u + TAPS - 1 - tap]
                 sums[u] = term if sums[u] is None else sums[u] + term
         for u in range(size):
             at = (low + u) * ROWS + band * 16
-            filtered[half][part, at : at + 16, :] = sums[u]
-
-    twice = lax.rem(across + RADIX, LANES)
-
-    def place(half, u):
+            filtered[item][c, at : at + 16, :] = sums[u]
+
+    def place(item, u):
+        down, across = downs[item], acrosses[item]
+        twice = lax.rem(across + RADIX, LANES)
+        inside = lane < LANES - across
         for band in range(ROWS // 16):
             at = (u + 1) * ROWS + band * 16 - down
             moved, turned = [], []
-            for part in range(2):
-                here = filtered[half][part, pl.ds(at, 16), :]
-                above = filtered[half][part, pl.ds(at - 1, 16), :]
+            for c in range(2):
+                here = filtered[item][c, pl.ds(at, 16), :]
+                above = filtered[item][c, pl.ds(at - 1, 16), :]
                 value = jnp.where(inside, here, above)
                 moved.append(pltpu.roll(value, across, 1))
                 turned.append(pltpu.roll(value, twice, 1))
@@ -222,10 +226,14 @@
             )
             for which, value in enumerate(parts):
                 low = which * ROWS + band * 16
-                grouped[half * HALF + u, low : low + 16, :] = value.astype(jnp.bfloat16)
-
-    def turn(base):
-        wide = jnp.concatenate([grouped[base + u] for u in range(SOME)], axis=1)
+                grouped[item, u, low : low + 16, :] = value.astype(jnp.bfloat16)
+
+    rows_out = jnp.concatenate(
+        [last[me ^ dg, ct + dc] for dg in range(PAIR) for dc in range(per_ct)], axis=0
+    )
+
+    def turn(item, base):
+        wide = jnp.concatenate([grouped[item, base + u] for u in range(SOME)], axis=1)
         inner = jnp.dot(first[...], wide, preferred_element_type=jnp.float32)
         rows = []
         for u in range(SOME):
@@ -238,59 +246,55 @@
         ).astype(jnp.bfloat16)
         size = result.shape[0] // (2 * dests)
         for dest in range(dests):
-            for part in range(2):
-                low = (dest * 2 + part) * size
+            for c in range(2):
+                low = (dest * 2 + c) * size
                 for u in range(SOME // 2):
-                    outs[dest][before, base // 2 + u, part] = result[
+                    outs[dest][item, base // 2 + u, c] = result[
                         low : low + size, u * LANES : (u + 1) * LANES
                     ]
 
-    rows_out = jnp.concatenate(
-        [last[me ^ dg, ct + dc] for dg in range(PAIR) for dc in range(per_ct)], axis=0
-    )
     pieces = [
-        (low, high_frame, band, part)
-        for low, high_frame in ((0, 9), (9, HALF + 1))
+        (low, end, band, c)
+        for low, end in ((0, frames // 2 + 1), (frames // 2 + 1, frames + 1))
         for band in range(ROWS // 16)
-        for part in range(2)
+        for c in range(2)
     ]
-    each = len(pieces) // (HALF // SOME)
-    halves = total // HALF
-    for half in range(halves + 1):
-        for n in range(HALF // SOME):
-            if half < halves:
+    groups = frames // SOME
+    each = len(pieces) // groups
+    for item in range(JOIN + 1):
+        for n in range(groups):
+            if item < JOIN:
                 for piece in pieces[n * each : (n + 1) * each]:
-                    filt(half, *piece)
-            if half:
+                    filt(item, *piece)
+            if item:
                 for u in range(SOME):
-                    place(half - 1, n * SOME + u)
-                turn((half - 1) * HALF + n * SOME)
-
-
-def filterbank(index, half, meta, keep, halo_own, recv, halo_far, tables, earlier, dests):
-    frames = keep.shape[2] // ROWS
+                    place(item - 1, n * SOME + u)
+                turn(item - 1, n * SOME)
+
+
+def filterbank(part, half, meta, sources, tables, beside, dests):
+    late = not beside
+    frames = sources[0].shape[2] // ROWS
     size = tables[-1].shape[2] // 2
     per_ct = tables[-1].shape[1] // 2
-    before = earlier[0].shape[0] if earlier else 0
-    all_rows = (PAIR + 1) * frames * ROWS
-    shape = (before + 1, PAIR * frames // 2, 2, size, LANES)
+    pairs = frames // 2 if late else frames
+    shape = (JOIN, pairs, 2, size, LANES)
+    kernel = functools.partial(filterbank_kernel, late, part, frames, dests, per_ct, half)
     return pl.pallas_call(
-        functools.partial(
-            filterbank_kernel, index, before, frames, dests, per_ct, half
-        ),
+        kernel,
         out_shape=[jax.ShapeDtypeStruct(shape, jnp.bfloat16)] * dests,
-        in_specs=[SMEM] + [VMEM] * (9 + len(earlier)),
+        in_specs=[SMEM] + [VMEM] * (len(sources) + 5 + len(beside)),
         out_specs=[VMEM] * dests,
         scratch_shapes=[
-            pltpu.VMEM((2, all_rows, LANES), jnp.bfloat16),
-            pltpu.VMEM((TAPS, ROWS, LANES), jnp.float32),
-            pltpu.VMEM((PAIR * frames, LANES, LANES), jnp.bfloat16),
+            pltpu.VMEM((JOIN, 2, 2 * frames * ROWS, LANES), jnp.bfloat16),
+            pltpu.VMEM((JOIN, TAPS, ROWS, LANES), jnp.float32),
+            pltpu.VMEM((JOIN, frames, LANES, LANES), jnp.bfloat16),
         ]
-        + [pltpu.VMEM((2, (HALF + 1) * ROWS, LANES), jnp.float32)] * (PAIR * frames // HALF),
-        compiler_params=params(12),
+        + [pltpu.VMEM((2, (frames + 1) * ROWS, LANES), jnp.float32)] * JOIN,
+        compiler_params=params(14),
         cost_estimate=cost(10**6, 2**18),
-        name="filterbank",
-    )(meta, keep, halo_own, recv, halo_far, *tables, *earlier)
+        name="filterbank_late" if late else "filterbank_early",
+    )(meta, *sources, *tables, *beside)
 
 
 SQUARE = [(p, q) for p in range(TILE) for q in range(TILE)]
@@ -547,7 +551,7 @@
     own = in_count * per_ct
     return (
         frame_count >= TAPS
-        and frame_count % HALF == 0
+        and frame_count % (2 * SOME) == 0
         and span in (2, 4, 8)
         and outer * span % 16 == 0
         and own % (PAIR * JOIN * 2 * TILE // 4) == 0
@@ -582,34 +586,26 @@
     tables = [np.concatenate([filter_table()] * 2, axis=1), first_table(), *twiddle_tables()]
     tables = [jnp.asarray(t) for t in tables + [np.concatenate([base, base], axis=1)]]
 
+    parts = half // JOIN
     picked = pick(meta, voltages)
-    sends, keeps = picked[:half], picked[half:]
-    forward = [p for p in onward if p[0] % PAIR == 0]
-    recvs = []
-    for c in range(half):
-        block = follow(sends[c], recvs[c - 2]) if c >= 2 else sends[c]
-        recvs.append(lax.ppermute(block, "tm", swap))
-    ahead = [p for p in onward if p[0] % PAIR == 1]
-    halos = []
-    for block in keeps:
-        halos.append(lax.ppermute(follow(block, halos[-1]) if halos else block, "tm", ahead))
-
-    parts = half // JOIN
+    sends, keeps = picked[:parts], picked[parts:]
+    recvs = [lax.ppermute(block, "tm", swap) for block in sends]
+    halos, lates = [], []
+    for c in range(parts):
+        recv = follow(recvs[c], lates[-1]) if lates else recvs[c]
+        halos.append(lax.ppermute(jnp.where(g == 1, keeps[c], recv), "tm", onward))
+        sources = [keeps[c], follow(recvs[c], halos[c - 1]) if c else recvs[c]]
+        lates.append(filterbank(c, half, meta, sources, tables, [], len(dests)))
+
     sets = pair_sets(own, parts)
     sizes = (outer, span, per_ct)
     arrays, places = [], []
-    spectra, done = [], []
-    for c in range(half):
-        block = follow(recvs[c], done[c - 2]) if c >= 2 else recvs[c]
-        far = lax.ppermute(block, "tm", forward)
-        far = follow(far, done[c - 1]) if c else far
-        spectra = filterbank(
-            c, half, meta, keeps[c // JOIN], halos[c // JOIN], recvs[c], far, tables, spectra,
-            len(dests),
-        )
+    done = []
+    for c in range(parts):
+        halo = follow(halos[c], recvs[c + 1]) if c + 1 < parts else halos[c]
+        sources = [halo, keeps[c], recvs[c]]
+        spectra = filterbank(c, half, meta, sources, tables, lates[c], len(dests))
         done.append(spectra[0])
-        if c % JOIN < JOIN - 1:
-            continue
         for (dg, dc), block in zip(dests, spectra):
             route = []
             for i in range(tm):
@@ -621,8 +617,8 @@
                     block = follow(block, arrays[-len(dests)])
                 block = lax.ppermute(block, ("tm", "ct"), route)
             arrays.append(block)
-            places.append((dg, dc, c // JOIN))
-        spectra = []
+            places.append((dg, dc, c))
+
     near = [(False,) + place for place in places]
     far = [(True,) + place for place in places]
     count = len(dests)
@@ -631,7 +627,6 @@
         meta, arrays[:count] + others, near[:count] + far[:count], sets[0], own // parts, sizes,
         "correlate_early",
     )
-    others += [lax.ppermute(follow(block, early[0]), "stn", cores) for block in arrays[count:]]
     own_late = correlate(meta, arrays, near, sets[1], own, sizes, "correlate_own")
 
     def along(parts, after):
@@ -642,7 +637,8 @@
         return moved
 
     early = along(early, lambda r: others)
-    own_late = along(own_late, lambda r: early[r])
+    others += [lax.ppermute(follow(block, early), "stn", cores) for block in arrays[count:]]
+    own_late = along(own_late, lambda r: others)
     *cross_late, early = correlate(
         meta, arrays + others, near + far, sets[2], own, sizes, "correlate_cross", early
     )

time: 111 us -> 106 us (0.955)
  starting transfers between devices: 42 us -> 31.8 us
  waiting for transfers between devices: 27.7 us -> 32.3 us
    ppermute x14 -> x8, starting transfers between devices: 22.8 us -> 11.9 us  [the longest x2 7.85 us: fast(): halos.append(lax.ppermute(jnp.where(g == 1, keeps[c], recv), 'tm', onward))]
    ppermute x14 -> x8, waiting for transfers between devices: 10.4 us -> 15.4 us  [the longest x2 15.4 us: fast(): recvs = [lax.ppermute(block, 'tm', swap) for block in sends]]
    ppermute x6, waiting for transfers between devices: 6.88 us -> 2.46 us  [fast(): block = lax.ppermute(block, ('tm', 'ct'), route)]
    ppermute x9, waiting for transfers between devices: 9.43 us -> 13.5 us  [along(): moved.append(lax.ppermute(follow(parts[r], after(r)), 'tm', route))]
    ppermute x9, starting transfers between devices: 10.4 us -> 11.7 us  [along(): moved.append(lax.ppermute(follow(parts[r], after(r)), 'tm', route))]
  transfers between devices with their start and end apart: 38 -> 32, of which waited for: 12 -> 9; matrix products, arithmetic and copies ran while one was open for 0% -> 0% of each run, Pallas kernels for 29% -> 30%
where the time goes in v9:
time: 106 us
  Pallas kernels  38.7 us (37%)
  waiting for transfers between devices  32.3 us (30%)
  starting transfers between devices  31.8 us (30%)
  local copies, waits for them, and re-layouts  2.4 us (2%)
    pallas_call x3, Pallas kernels, correlate(): pl.pallas_call(functools.partial(correlate_kernel, layout), out_shape=sha...  16.8 us
    ppermute x2, waiting for transfers between devices, fast(): recvs = [lax.ppermute(block, 'tm', swap) for block in sends]  15.4 us
    pallas_call x4, Pallas kernels, filterbank(): pl.pallas_call(kernel, out_shape=[jax.ShapeDtypeStruct(shape, jnp.bfloat1...  15.2 us
    ppermute x9, waiting for transfers between devices, along(): moved.append(lax.ppermute(follow(parts[r], after(r)), 'tm', route))  13.5 us
    ppermute x9, starting transfers between devices, along(): moved.append(lax.ppermute(follow(parts[r], after(r)), 'tm', route))  11.7 us
    ppermute x2, starting transfers between devices, fast(): halos.append(lax.ppermute(jnp.where(g == 1, keeps[c], recv), 'tm', onward))  7.85 us
    ppermute x6, starting transfers between devices, fast(): block = lax.ppermute(block, ('tm', 'ct'), route)  7.04 us
    pallas_call x1, Pallas kernels, assemble(): pl.pallas_call(functools.partial(assemble_kernel, own, outer, span, scale...  3.65 us
  transfers between devices with their start and end apart: 32, of which 9 were waited for; matrix products, arithmetic and copies ran while one was open for 0% of the time, Pallas kernels for 30%

profile of v9, /device:TPU:0, one launch (start us, length us, event | category | flops | bytes accessed | tf_op | source)
XLA Modules:
  0.0 105.7 jit_solution(5440211190979776346)
XLA Ops:
  0.0 0.8 concatenate.3.meta.refs_0_
  0.8 1.6 %copy-done.1 = bf16[2,8,65536]{2,1,0:T(8,128)(2,1)S(1)} copy-done((bf16[2,8,65536]{2,1,0:T(8,128)(2,1)S(1)}, bf16[2,8,65536]{2,1,0:T(8,128)(2,1)}, u32[]{:S(2)}) %copy-start.1) | copy-done | bytes 2097176
  2.4 3.1 %pick.1 = (bf16[2,2,512,128]{3,2,1,0:T(8,128)(2,1)}, bf16[2,2,512,128]{3,2,1,0:T(8,128)(2,1)S(1)}, bf16[2,2,512,128]{3,2,1,0:T(8,128)(2,1)S(1)}, bf16[2,2,512,128]{3,2,1,0:T(8,128)(2,1)S(1)}) custom-call(s32[12]{0:T(128)S(1)} %concatenate.3.meta.refs_0_, bf16[2,8,65536]{2,1,0:T(8,128)(2,1)S(1)} %copy-done.1), custom_call_target="tpu_custom_call" | custom-call | flops 1000000 | bytes 262144 | tf_op jit(solution)/shard_map/pick/pallas_call | solution.py:119
  5.5 2.9 %collective-permute-start = (bf16[2,2,512,128]{3,2,1,0:T(8,128)(2,1)}, bf16[2,2,512,128]{3,2,1,0:T(8,128)(2,1)S(1)}, u32[]{:S(2)}, u32[]{:S(2)}) collective-permute-start(bf16[2,2,512,128]{3,2,1,0:T(8,128)(2,1)} %get-tuple-element.62), channel_id=1, source_target_pairs={{0,2},{2,0},{4,6},{6,4},{8,10},{10,8},{12,14},{14,12},{1,3},{3,1},... | collective-permute-start | bytes 1572872 | tf_op jit(solution)/shard_map/ppermute | solution.py:592
  8.4 0.0 collective-permute-start.2
  8.5 12.9 %collective-permute-done.refs_2_.refs_3_ = bf16[2,2,512,128]{3,2,1,0:T(8,128)(2,1)S(1)} collective-permute-done((bf16[2,2,512,128]{3,2,1,0:T(8,128)(2,1)}, bf16[2,2,512,128]{3,2,1,0:T(8,128)(2,1)S(1)}, u32[]{:S(2)}, u32[]{:S(2)}) %collective-permute-start) | collective-permute-done | bytes 524320 | tf_op jit(solution)/shard_map/ppermute | solution.py:592
  21.4 0.1 broadcast_select_fusion.1
  21.5 4.1 %collective-permute-start.1 = (bf16[2,2,512,128]{3,2,1,0:T(8,128)(2,1)S(1)}, bf16[2,2,512,128]{3,2,1,0:T(8,128)(2,1)S(1)}, u32[]{:S(2)}, u32[]{:S(2)}) collective-permute-start(bf16[2,2,512,128]{3,2,1,0:T(8,128)(2,1)S(1)} %broadcast_select_fusion.1), channel_id=1, source_target_pairs={{0,4},{2,6},{4,8},{6,10},{8,12},{10,14},{1,5},{3,7},{5,9},{7,11},{... | collective-permute-start | bytes 1572872 | tf_op jit(solution)/shard_map/ppermute | solution.py:596
  25.6 3.7 %filterbank_late.2 = (bf16[2,8,2,16,128]{4,3,2,1,0:T(8,128)(2,1)S(1)}, bf16[2,8,2,16,128]{4,3,2,1,0:T(8,128)(2,1)S(1)}, bf16[2,8,2,16,128]{4,3,2,1,0:T(8,128)(2,1)S(1)}, bf16[2,8,2,16,128]{4,3,2,1,0:T(8,128)(2,1)S(1)}) custom-call(s32[12]{0:T(128)S(1)} %concatenate.3.meta.refs_0_, bf16[2,2,512,128]{3,2,1,0:T(8,128)(2,1)S(1)} %get-tuple-element.61.refs_1_.refs_2_, ...), custom_call_target="tpu_custom_call" | custom-call | flops 1000000 | bytes 262144 | tf_op jit(solution)/shard_map/filterbank_late/pallas_call | solution.py:283
  29.3 2.5 %collective-permute-done.2.refs_2_.refs_3_ = bf16[2,2,512,128]{3,2,1,0:T(8,128)(2,1)S(1)} collective-permute-done((bf16[2,2,512,128]{3,2,1,0:T(8,128)(2,1)S(1)}, bf16[2,2,512,128]{3,2,1,0:T(8,128)(2,1)S(1)}, u32[]{:S(2)}, u32[]{:S(2)}) %collective-permute-start.2) | collective-permute-done | bytes 524320 | tf_op jit(solution)/shard_map/ppermute | solution.py:592
  31.8 0.1 broadcast_select_fusion
  31.9 3.8 %collective-permute-start.6 = (bf16[2,2,512,128]{3,2,1,0:T(8,128)(2,1)S(1)}, bf16[2,2,512,128]{3,2,1,0:T(8,128)(2,1)S(1)}, u32[]{:S(2)}, u32[]{:S(2)}) collective-permute-start(bf16[2,2,512,128]{3,2,1,0:T(8,128)(2,1)S(1)} %broadcast_select_fusion), channel_id=1, source_target_pairs={{0,4},{2,6},{4,8},{6,10},{8,12},{10,14},{1,5},{3,7},{5,9},{7,11},{... | collective-permute-start | bytes 1572872 | tf_op jit(solution)/shard_map/ppermute | solution.py:596
  35.7 3.8 %filterbank_early.2 = (bf16[2,16,2,16,128]{4,3,2,1,0:T(8,128)(2,1)S(1)}, bf16[2,16,2,16,128]{4,3,2,1,0:T(8,128)(2,1)S(1)}, bf16[2,16,2,16,128]{4,3,2,1,0:T(8,128)(2,1)S(1)}, bf16[2,16,2,16,128]{4,3,2,1,0:T(8,128)(2,1)S(1)}) custom-call(s32[12]{0:T(128)S(1)} %concatenate.3.meta.refs_0_, bf16[2,2,512,128]{3,2,1,0:T(8,128)(2,1)S(1)} %collective-permute-done.1.refs_1_, ...), custom_call_target="tpu_custom_call" | custom-call | flops 1000000 | bytes 262144 | tf_op jit(solution)/shard_map/filterbank_early/pallas_call | solution.py:283
  39.4 1.6 %collective-permute-start.3 = (bf16[2,16,2,16,128]{4,3,2,1,0:T(8,128)(2,1)S(1)}, bf16[2,16,2,16,128]{4,3,2,1,0:T(8,128)(2,1)S(1)}, u32[]{:S(2)}, u32[]{:S(2)}) collective-permute-start(bf16[2,16,2,16,128]{4,3,2,1,0:T(8,128)(2,1)S(1)} %get-tuple-element.70), channel_id=1, source_target_pairs={{0,1},{1,0},{2,3},{3,2},{4,5},{5,4},{6,7},{7,6},{8,9},{9,8},{10,11... | collective-permute-start | bytes 786440 | tf_op jit(solution)/shard_map/ppermute | solution.py:618
  41.0 1.4 %collective-permute-start.5 = (bf16[2,16,2,16,128]{4,3,2,1,0:T(8,128)(2,1)S(1)}, bf16[2,16,2,16,128]{4,3,2,1,0:T(8,128)(2,1)S(1)}, u32[]{:S(2)}, u32[]{:S(2)}) collective-permute-start(bf16[2,16,2,16,128]{4,3,2,1,0:T(8,128)(2,1)S(1)} %get-tuple-element.72), channel_id=1, source_target_pairs={{0,3},{1,2},{2,1},{3,0},{4,7},{5,6},{6,5},{7,4},{8,11},{9,10},{10,... | collective-permute-start | bytes 786440 | tf_op jit(solution)/shard_map/ppermute | solution.py:618
  42.5 0.5 collective-permute-start.4
  43.0 3.7 %filterbank_late.3 = (bf16[2,8,2,16,128]{4,3,2,1,0:T(8,128)(2,1)S(1)}, bf16[2,8,2,16,128]{4,3,2,1,0:T(8,128)(2,1)S(1)}, bf16[2,8,2,16,128]{4,3,2,1,0:T(8,128)(2,1)S(1)}, bf16[2,8,2,16,128]{4,3,2,1,0:T(8,128)(2,1)S(1)}) custom-call(s32[12]{0:T(128)S(1)} %concatenate.3.meta.refs_0_, bf16[2,2,512,128]{3,2,1,0:T(8,128)(2,1)S(1)} %get-tuple-element.73.refs_1_.refs_2_, ...), custom_call_target="tpu_custom_call" | custom-call | flops 1000000 | bytes 262144 | tf_op jit(solution)/shard_map/filterbank_late/pallas_call | solution.py:283
  46.7 4.0 %filterbank_early.3 = (bf16[2,16,2,16,128]{4,3,2,1,0:T(8,128)(2,1)S(1)}, bf16[2,16,2,16,128]{4,3,2,1,0:T(8,128)(2,1)S(1)}, bf16[2,16,2,16,128]{4,3,2,1,0:T(8,128)(2,1)S(1)}, bf16[2,16,2,16,128]{4,3,2,1,0:T(8,128)(2,1)S(1)}) custom-call(s32[12]{0:T(128)S(1)} %concatenate.3.meta.refs_0_, bf16[2,2,512,128]{3,2,1,0:T(8,128)(2,1)S(1)} %collective-permute-done.6.refs_1_, ...), custom_call_target="tpu_custom_call" | custom-call | flops 1000000 | bytes 262144 | tf_op jit(solution)/shard_map/filterbank_early/pallas_call | solution.py:283
  50.7 0.1 collective-permute-start.10
  50.8 1.2 %collective-permute-done.3.refs_2_ = bf16[2,16,2,16,128]{4,3,2,1,0:T(8,128)(2,1)S(1)} collective-permute-done((bf16[2,16,2,16,128]{4,3,2,1,0:T(8,128)(2,1)S(1)}, bf16[2,16,2,16,128]{4,3,2,1,0:T(8,128)(2,1)S(1)}, u32[]{:S(2)}, u32[]{:S(2)}) %collective-permute-start.3) | collective-permute-done | bytes 262176 | tf_op jit(solution)/shard_map/ppermute | solution.py:618
  52.0 1.2 %collective-permute-done.4.refs_3_ = bf16[2,16,2,16,128]{4,3,2,1,0:T(8,128)(2,1)S(1)} collective-permute-done((bf16[2,16,2,16,128]{4,3,2,1,0:T(8,128)(2,1)S(1)}, bf16[2,16,2,16,128]{4,3,2,1,0:T(8,128)(2,1)S(1)}, u32[]{:S(2)}, u32[]{:S(2)}) %collective-permute-start.4) | collective-permute-done | bytes 262176 | tf_op jit(solution)/shard_map/ppermute | solution.py:618
  53.2 0.5 collective-permute-start.13
  53.8 2.5 %collective-permute-start.9 = (bf16[2,16,2,16,128]{4,3,2,1,0:T(8,128)(2,1)S(1)}, bf16[2,16,2,16,128]{4,3,2,1,0:T(8,128)(2,1)S(1)}, u32[]{:S(2)}, u32[]{:S(2)}) collective-permute-start(bf16[2,16,2,16,128]{4,3,2,1,0:T(8,128)(2,1)S(1)} %get-tuple-element.86), channel_id=1, source_target_pairs={{0,3},{1,2},{2,1},{3,0},{4,7},{5,6},{6,5},{7,4},{8,11},{9,10},{10,... | collective-permute-start | bytes 786440 | tf_op jit(solution)/shard_map/ppermute | solution.py:618
  56.2 0.5 collective-permute-start.8
  56.7 0.5 collective-permute-start.7
  57.3 4.5 %correlate_early.1 = (f32[272,128]{1,0:T(8,128)S(1)}, bf16[272,128]{1,0:T(8,128)(2,1)S(1)}, bf16[272,128]{1,0:T(8,128)(2,1)S(1)}, bf16[272,128]{1,0:T(8,128)(2,1)S(1)}) custom-call(s32[12]{0:T(128)S(1)} %concatenate.3.meta.refs_0_, bf16[2,16,2,16,128]{4,3,2,1,0:T(8,128)(2,1)S(1)} %get-tuple-element.87.refs_1_, ...), custom_call_target="tpu_custom_call" | custom-call | flops 1000000 | bytes 262144 | tf_op jit(solution)/shard_map/correlate_early/pallas_call | solution.py:449
  61.8 1.8 %collective-permute-start.16 = (bf16[272,128]{1,0:T(8,128)(2,1)S(1)}, bf16[272,128]{1,0:T(8,128)(2,1)S(1)}, u32[]{:S(2)}, u32[]{:S(2)}) collective-permute-start(bf16[272,128]{1,0:T(8,128)(2,1)S(1)} %get-tuple-element.97), channel_id=1, source_target_pairs={{0,12},{2,14},{4,0},{6,2},{8,4},{10,6},{12,8},{14,10},{1,13},{3,15... | collective-permute-start | bytes 208904 | tf_op jit(solution)/shard_map/ppermute | solution.py:636
  63.6 1.2 %collective-permute-start.15 = (bf16[272,128]{1,0:T(8,128)(2,1)S(1)}, bf16[272,128]{1,0:T(8,128)(2,1)S(1)}, u32[]{:S(2)}, u32[]{:S(2)}) collective-permute-start(bf16[272,128]{1,0:T(8,128)(2,1)S(1)} %get-tuple-element.95), channel_id=1, source_target_pairs={{0,8},{2,10},{4,12},{6,14},{8,0},{10,2},{12,4},{14,6},{1,9},{3,11}... | collective-permute-start | bytes 208904 | tf_op jit(solution)/shard_map/ppermute | solution.py:636
  64.9 1.6 %collective-permute-start.14 = (bf16[272,128]{1,0:T(8,128)(2,1)S(1)}, bf16[272,128]{1,0:T(8,128)(2,1)S(1)}, u32[]{:S(2)}, u32[]{:S(2)}) collective-permute-start(bf16[272,128]{1,0:T(8,128)(2,1)S(1)} %get-tuple-element.93), channel_id=1, source_target_pairs={{0,4},{2,6},{4,8},{6,10},{8,12},{10,14},{12,0},{14,2},{1,5},{3,7},... | collective-permute-start | bytes 208904 | tf_op jit(solution)/shard_map/ppermute | solution.py:636
  66.4 5.0 %collective-permute-done.15.refs_19_ = bf16[272,128]{1,0:T(8,128)(2,1)S(1)} collective-permute-done((bf16[272,128]{1,0:T(8,128)(2,1)S(1)}, bf16[272,128]{1,0:T(8,128)(2,1)S(1)}, u32[]{:S(2)}, u32[]{:S(2)}) %collective-permute-start.15) | collective-permute-done | bytes 69664 | tf_op jit(solution)/shard_map/ppermute | solution.py:636
  71.4 0.1 collective-permute-start.17
  71.5 0.5 collective-permute-start.18
  72.0 0.1 collective-permute-start.19
  72.1 0.4 collective-permute-start.20
  72.5 6.0 %correlate_own.1 = (f32[400,128]{1,0:T(8,128)S(1)}, bf16[400,128]{1,0:T(8,128)(2,1)S(1)}, bf16[400,128]{1,0:T(8,128)(2,1)S(1)}, bf16[400,128]{1,0:T(8,128)(2,1)S(1)}) custom-call(s32[12]{0:T(128)S(1)} %concatenate.3.meta.refs_0_, bf16[2,16,2,16,128]{4,3,2,1,0:T(8,128)(2,1)S(1)} %get-tuple-element.87.refs_1_, ...), custom_call_target="tpu_custom_call" | custom-call | flops 1000000 | bytes 262144 | tf_op jit(solution)/shard_map/correlate_own/pallas_call | solution.py:449
  78.6 1.2 %collective-permute-start.23 = (bf16[400,128]{1,0:T(8,128)(2,1)S(1)}, bf16[400,128]{1,0:T(8,128)(2,1)S(1)}, u32[]{:S(2)}, u32[]{:S(2)}) collective-permute-start(bf16[400,128]{1,0:T(8,128)(2,1)S(1)} %get-tuple-element.109), channel_id=1, source_target_pairs={{0,12},{2,14},{4,0},{6,2},{8,4},{10,6},{12,8},{14,10},{1,13},{3,15... | collective-permute-start | bytes 307208 | tf_op jit(solution)/shard_map/ppermute | solution.py:636
  79.8 1.8 %collective-permute-start.21 = (bf16[400,128]{1,0:T(8,128)(2,1)S(1)}, bf16[400,128]{1,0:T(8,128)(2,1)S(1)}, u32[]{:S(2)}, u32[]{:S(2)}) collective-permute-start(bf16[400,128]{1,0:T(8,128)(2,1)S(1)} %get-tuple-element.105), channel_id=1, source_target_pairs={{0,4},{2,6},{4,8},{6,10},{8,12},{10,14},{12,0},{14,2},{1,5},{3,7},... | collective-permute-start | bytes 307208 | tf_op jit(solution)/shard_map/ppermute | solution.py:636
  81.6 6.3 %correlate_cross.1 = (f32[384,128]{1,0:T(8,128)S(1)}, bf16[384,128]{1,0:T(8,128)(2,1)S(1)}, bf16[384,128]{1,0:T(8,128)(2,1)S(1)}, bf16[384,128]{1,0:T(8,128)(2,1)S(1)}, f32[272,128]{1,0:T(8,128)S(1)}) custom-call(s32[12]{0:T(128)S(1)} %concatenate.3.meta.refs_0_, bf16[2,16,2,16,128]{4,3,2,1,0:T(8,128)(2,1)S(1)} %get-tuple-element.87.refs_1_, ...), custom_call_target="tpu_custom_call" | custom-call | flops 1000000 | bytes 262144 | tf_op jit(solution)/shard_map/correlate_cross/pallas_call | solution.py:449
  87.9 0.1 collective-permute-start.28
  88.0 2.0 %collective-permute-start.26 = (bf16[384,128]{1,0:T(8,128)(2,1)S(1)}, bf16[384,128]{1,0:T(8,128)(2,1)S(1)}, u32[]{:S(2)}, u32[]{:S(2)}) collective-permute-start(bf16[384,128]{1,0:T(8,128)(2,1)S(1)} %get-tuple-element.116), channel_id=1, source_target_pairs={{0,12},{2,14},{4,0},{6,2},{8,4},{10,6},{12,8},{14,10},{1,13},{3,15... | collective-permute-start | bytes 294920 | tf_op jit(solution)/shard_map/ppermute | solution.py:636
  90.0 1.1 %collective-permute-start.25 = (bf16[384,128]{1,0:T(8,128)(2,1)S(1)}, bf16[384,128]{1,0:T(8,128)(2,1)S(1)}, u32[]{:S(2)}, u32[]{:S(2)}) collective-permute-start(bf16[384,128]{1,0:T(8,128)(2,1)S(1)} %get-tuple-element.114), channel_id=1, source_target_pairs={{0,8},{2,10},{4,12},{6,14},{8,0},{10,2},{12,4},{14,6},{1,9},{3,11}... | collective-permute-start | bytes 294920 | tf_op jit(solution)/shard_map/ppermute | solution.py:636
  91.1 0.9 collective-permute-start.24
  92.0 1.2 %collective-permute-done.26.refs_9_ = bf16[384,128]{1,0:T(8,128)(2,1)S(1)} collective-permute-done((bf16[384,128]{1,0:T(8,128)(2,1)S(1)}, bf16[384,128]{1,0:T(8,128)(2,1)S(1)}, u32[]{:S(2)}, u32[]{:S(2)}) %collective-permute-start.26) | collective-permute-done | bytes 98336 | tf_op jit(solution)/shard_map/ppermute | solution.py:636
  93.2 7.4 %collective-permute-done.25.refs_8_ = bf16[384,128]{1,0:T(8,128)(2,1)S(1)} collective-permute-done((bf16[384,128]{1,0:T(8,128)(2,1)S(1)}, bf16[384,128]{1,0:T(8,128)(2,1)S(1)}, u32[]{:S(2)}, u32[]{:S(2)}) %collective-permute-start.25) | collective-permute-done | bytes 98336 | tf_op jit(solution)/shard_map/ppermute | solution.py:636
  100.6 0.5 collective-permute-start.29
  101.1 0.8 collective-permute-done.30.refs_13_
  101.9 0.2 collective-permute-done.29.refs_12_
  102.0 3.6 %assemble.1 = f32[2,16,32,256]{3,2,1,0:T(8,128)} custom-call(s32[12]{0:T(128)S(1)} %concatenate.3.meta.refs_0_, f32[272,128]{1,0:T(8,128)S(1)} %get-tuple-element.102.refs_1_, f32[400,128]{1,0:T(8,128)S(1)} %get-tuple-element.103.refs_2_, bf16[400,128]{1,0:T(8,128)(2,1)S(1)} %collective-permute-done.21.refs_3_, ...), custom_call_target="tpu_custom_call" | custom-call | flops 1000000 | bytes 262144 | tf_op jit(solution)/shard_map/assemble/pallas_call | solution.py:533
  (40 shorter events, 0.1 us)
Async XLA Ops:
  0.0 25.6 %copy-start = (f32[16,64,128]{2,1,0:T(8,128)S(1)}, f32[16,64,128]{2,1,0:T(8,128)}, u32[]{:S(2)}) copy-start(f32[16,64,128]{2,1,0:T(8,128)} %constant.47.clone.refs_3_.refs_4_) | copy-start | bytes 1572868
  0.8 1.6 %copy-start.1 = (bf16[2,8,65536]{2,1,0:T(8,128)(2,1)S(1)}, bf16[2,8,65536]{2,1,0:T(8,128)(2,1)}, u32[]{:S(2)}) copy-start(bf16[2,8,65536]{2,1,0:T(8,128)(2,1)} %block.1) | copy-start | bytes 6291460
  2.4 23.2 %copy-start.2 = (bf16[2,4,32,128]{3,2,1,0:T(8,128)(2,1)S(1)}, bf16[2,4,32,128]{3,2,1,0:T(8,128)(2,1)}, u32[]{:S(2)}) copy-start(bf16[2,4,32,128]{3,2,1,0:T(8,128)(2,1)} %constant.51.clone.refs_7_.refs_8_) | copy-start | bytes 196612
  2.4 23.2 %copy-start.3 = (f32[64,128]{1,0:T(8,128)S(1)}, f32[64,128]{1,0:T(8,128)}, u32[]{:S(2)}) copy-start(f32[64,128]{1,0:T(8,128)} %constant.50.clone.refs_6_.refs_7_) | copy-start | bytes 98308
  2.4 23.2 %copy-start.4 = (f32[64,128]{1,0:T(8,128)S(1)}, f32[64,128]{1,0:T(8,128)}, u32[]{:S(2)}) copy-start(f32[64,128]{1,0:T(8,128)} %constant.49.clone.refs_5_.refs_6_) | copy-start | bytes 98308
  2.4 23.2 %copy-start.5 = (bf16[128,128]{1,0:T(8,128)(2,1)S(1)}, bf16[128,128]{1,0:T(8,128)(2,1)}, u32[]{:S(2)}) copy-start(bf16[128,128]{1,0:T(8,128)(2,1)} %constant.48.clone.refs_4_.refs_5_) | copy-start | bytes 98308
  5.5 15.9 %collective-permute-start = (bf16[2,2,512,128]{3,2,1,0:T(8,128)(2,1)}, bf16[2,2,512,128]{3,2,1,0:T(8,128)(2,1)S(1)}, u32[]{:S(2)}, u32[]{:S(2)}) collective-permute-start(bf16[2,2,512,128]{3,2,1,0:T(8,128)(2,1)} %get-tuple-element.62), channel_id=1, source_target_pairs={{0,2},{2,0},{4,6},{6,4},{8,10},{10,8},{12,14},{14,12},{1,3},{3,1},... | collective-permute-start | bytes 1572872 | tf_op jit(solution)/shard_map/ppermute | solution.py:592
  8.4 23.4 %collective-permute-start.2 = (bf16[2,2,512,128]{3,2,1,0:T(8,128)(2,1)S(1)}, bf16[2,2,512,128]{3,2,1,0:T(8,128)(2,1)S(1)}, u32[]{:S(2)}, u32[]{:S(2)}) collective-permute-start(bf16[2,2,512,128]{3,2,1,0:T(8,128)(2,1)S(1)} %get-tuple-element.63), channel_id=1, source_target_pairs={{0,2},{2,0},{4,6},{6,4},{8,10},{10,8},{12,14},{14,12},{1,3},{3,1},... | collective-permute-start | bytes 1572872 | tf_op jit(solution)/shard_map/ppermute | solution.py:592
  21.5 14.2 %collective-permute-start.1 = (bf16[2,2,512,128]{3,2,1,0:T(8,128)(2,1)S(1)}, bf16[2,2,512,128]{3,2,1,0:T(8,128)(2,1)S(1)}, u32[]{:S(2)}, u32[]{:S(2)}) collective-permute-start(bf16[2,2,512,128]{3,2,1,0:T(8,128)(2,1)S(1)} %broadcast_select_fusion.1), channel_id=1, source_target_pairs={{0,4},{2,6},{4,8},{6,10},{8,12},{10,14},{1,5},{3,7},{5,9},{7,11},{... | collective-permute-start | bytes 1572872 | tf_op jit(solution)/shard_map/ppermute | solution.py:596
  31.9 14.9 %collective-permute-start.6 = (bf16[2,2,512,128]{3,2,1,0:T(8,128)(2,1)S(1)}, bf16[2,2,512,128]{3,2,1,0:T(8,128)(2,1)S(1)}, u32[]{:S(2)}, u32[]{:S(2)}) collective-permute-start(bf16[2,2,512,128]{3,2,1,0:T(8,128)(2,1)S(1)} %broadcast_select_fusion), channel_id=1, source_target_pairs={{0,4},{2,6},{4,8},{6,10},{8,12},{10,14},{1,5},{3,7},{5,9},{7,11},{... | collective-permute-start | bytes 1572872 | tf_op jit(solution)/shard_map/ppermute | solution.py:596
  39.4 12.6 %collective-permute-start.3 = (bf16[2,16,2,16,128]{4,3,2,1,0:T(8,128)(2,1)S(1)}, bf16[2,16,2,16,128]{4,3,2,1,0:T(8,128)(2,1)S(1)}, u32[]{:S(2)}, u32[]{:S(2)}) collective-permute-start(bf16[2,16,2,16,128]{4,3,2,1,0:T(8,128)(2,1)S(1)} %get-tuple-element.70), channel_id=1, source_target_pairs={{0,1},{1,0},{2,3},{3,2},{4,5},{5,4},{6,7},{7,6},{8,9},{9,8},{10,11... | collective-permute-start | bytes 786440 | tf_op jit(solution)/shard_map/ppermute | solution.py:618
  41.0 11.0 %collective-permute-start.5 = (bf16[2,16,2,16,128]{4,3,2,1,0:T(8,128)(2,1)S(1)}, bf16[2,16,2,16,128]{4,3,2,1,0:T(8,128)(2,1)S(1)}, u32[]{:S(2)}, u32[]{:S(2)}) collective-permute-start(bf16[2,16,2,16,128]{4,3,2,1,0:T(8,128)(2,1)S(1)} %get-tuple-element.72), channel_id=1, source_target_pairs={{0,3},{1,2},{2,1},{3,0},{4,7},{5,6},{6,5},{7,4},{8,11},{9,10},{10,... | collective-permute-start | bytes 786440 | tf_op jit(solution)/shard_map/ppermute | solution.py:618
  42.5 10.8 %collective-permute-start.4 = (bf16[2,16,2,16,128]{4,3,2,1,0:T(8,128)(2,1)S(1)}, bf16[2,16,2,16,128]{4,3,2,1,0:T(8,128)(2,1)S(1)}, u32[]{:S(2)}, u32[]{:S(2)}) collective-permute-start(bf16[2,16,2,16,128]{4,3,2,1,0:T(8,128)(2,1)S(1)} %get-tuple-element.71), channel_id=1, source_target_pairs={{0,2},{1,3},{2,0},{3,1},{4,6},{5,7},{6,4},{7,5},{8,10},{9,11},{10,... | collective-permute-start | bytes 786440 | tf_op jit(solution)/shard_map/ppermute | solution.py:618
  50.7 5.5 %collective-permute-start.10 = (bf16[2,16,2,16,128]{4,3,2,1,0:T(8,128)(2,1)S(1)}, bf16[2,16,2,16,128]{4,3,2,1,0:T(8,128)(2,1)S(1)}, u32[]{:S(2)}, u32[]{:S(2)}) collective-permute-start(bf16[2,16,2,16,128]{4,3,2,1,0:T(8,128)(2,1)S(1)} %get-tuple-element.87.refs_1_), channel_id=1, source_target_pairs={{0,16},{16,0},{1,17},{17,1},{2,18},{18,2},{3,19},{19,3},{4,20},{20... | collective-permute-start | bytes 786440 | tf_op jit(solution)/shard_map/ppermute | solution.py:625
  52.0 4.7 %collective-permute-start.11 = (bf16[2,16,2,16,128]{4,3,2,1,0:T(8,128)(2,1)S(1)}, bf16[2,16,2,16,128]{4,3,2,1,0:T(8,128)(2,1)S(1)}, u32[]{:S(2)}, u32[]{:S(2)}) collective-permute-start(bf16[2,16,2,16,128]{4,3,2,1,0:T(8,128)(2,1)S(1)} %collective-permute-done.3.refs_2_), channel_id=1, source_target_pairs={{0,16},{16,0},{1,17},{17,1},{2,18},{18,2},{3,19},{19,3},{4,20},{20... | collective-permute-start | bytes 786440 | tf_op jit(solution)/shard_map/ppermute | solution.py:625
  53.2 4.0 %collective-permute-start.12 = (bf16[2,16,2,16,128]{4,3,2,1,0:T(8,128)(2,1)S(1)}, bf16[2,16,2,16,128]{4,3,2,1,0:T(8,128)(2,1)S(1)}, u32[]{:S(2)}, u32[]{:S(2)}) collective-permute-start(bf16[2,16,2,16,128]{4,3,2,1,0:T(8,128)(2,1)S(1)} %collective-permute-done.4.refs_3_), channel_id=1, source_target_pairs={{0,16},{16,0},{1,17},{17,1},{2,18},{18,2},{3,19},{19,3},{4,20},{20... | collective-permute-start | bytes 786440 | tf_op jit(solution)/shard_map/ppermute | solution.py:625
  53.2 4.0 %collective-permute-start.13 = (bf16[2,16,2,16,128]{4,3,2,1,0:T(8,128)(2,1)S(1)}, bf16[2,16,2,16,128]{4,3,2,1,0:T(8,128)(2,1)S(1)}, u32[]{:S(2)}, u32[]{:S(2)}) collective-permute-start(bf16[2,16,2,16,128]{4,3,2,1,0:T(8,128)(2,1)S(1)} %collective-permute-done.5.refs_4_), channel_id=1, source_target_pairs={{0,16},{16,0},{1,17},{17,1},{2,18},{18,2},{3,19},{19,3},{4,20},{20... | collective-permute-start | bytes 786440 | tf_op jit(solution)/shard_map/ppermute | solution.py:625
  53.8 11.1 %collective-permute-start.9 = (bf16[2,16,2,16,128]{4,3,2,1,0:T(8,128)(2,1)S(1)}, bf16[2,16,2,16,128]{4,3,2,1,0:T(8,128)(2,1)S(1)}, u32[]{:S(2)}, u32[]{:S(2)}) collective-permute-start(bf16[2,16,2,16,128]{4,3,2,1,0:T(8,128)(2,1)S(1)} %get-tuple-element.86), channel_id=1, source_target_pairs={{0,3},{1,2},{2,1},{3,0},{4,7},{5,6},{6,5},{7,4},{8,11},{9,10},{10,... | collective-permute-start | bytes 786440 | tf_op jit(solution)/shard_map/ppermute | solution.py:618
  56.2 15.2 %collective-permute-start.8 = (bf16[2,16,2,16,128]{4,3,2,1,0:T(8,128)(2,1)S(1)}, bf16[2,16,2,16,128]{4,3,2,1,0:T(8,128)(2,1)S(1)}, u32[]{:S(2)}, u32[]{:S(2)}) collective-permute-start(bf16[2,16,2,16,128]{4,3,2,1,0:T(8,128)(2,1)S(1)} %get-tuple-element.84), channel_id=1, source_target_pairs={{0,2},{1,3},{2,0},{3,1},{4,6},{5,7},{6,4},{7,5},{8,10},{9,11},{10,... | collective-permute-start | bytes 786440 | tf_op jit(solution)/shard_map/ppermute | solution.py:618
  56.7 14.7 %collective-permute-start.7 = (bf16[2,16,2,16,128]{4,3,2,1,0:T(8,128)(2,1)S(1)}, bf16[2,16,2,16,128]{4,3,2,1,0:T(8,128)(2,1)S(1)}, u32[]{:S(2)}, u32[]{:S(2)}) collective-permute-start(bf16[2,16,2,16,128]{4,3,2,1,0:T(8,128)(2,1)S(1)} %get-tuple-element.82), channel_id=1, source_target_pairs={{0,1},{1,0},{2,3},{3,2},{4,5},{5,4},{6,7},{7,6},{8,9},{9,8},{10,11... | collective-permute-start | bytes 786440 | tf_op jit(solution)/shard_map/ppermute | solution.py:618
  61.8 4.7 %collective-permute-start.16 = (bf16[272,128]{1,0:T(8,128)(2,1)S(1)}, bf16[272,128]{1,0:T(8,128)(2,1)S(1)}, u32[]{:S(2)}, u32[]{:S(2)}) collective-permute-start(bf16[272,128]{1,0:T(8,128)(2,1)S(1)} %get-tuple-element.97), channel_id=1, source_target_pairs={{0,12},{2,14},{4,0},{6,2},{8,4},{10,6},{12,8},{14,10},{1,13},{3,15... | collective-permute-start | bytes 208904 | tf_op jit(solution)/shard_map/ppermute | solution.py:636
  63.6 7.8 %collective-permute-start.15 = (bf16[272,128]{1,0:T(8,128)(2,1)S(1)}, bf16[272,128]{1,0:T(8,128)(2,1)S(1)}, u32[]{:S(2)}, u32[]{:S(2)}) collective-permute-start(bf16[272,128]{1,0:T(8,128)(2,1)S(1)} %get-tuple-element.95), channel_id=1, source_target_pairs={{0,8},{2,10},{4,12},{6,14},{8,0},{10,2},{12,4},{14,6},{1,9},{3,11}... | collective-permute-start | bytes 208904 | tf_op jit(solution)/shard_map/ppermute | solution.py:636
  64.9 6.6 %collective-permute-start.14 = (bf16[272,128]{1,0:T(8,128)(2,1)S(1)}, bf16[272,128]{1,0:T(8,128)(2,1)S(1)}, u32[]{:S(2)}, u32[]{:S(2)}) collective-permute-start(bf16[272,128]{1,0:T(8,128)(2,1)S(1)} %get-tuple-element.93), channel_id=1, source_target_pairs={{0,4},{2,6},{4,8},{6,10},{8,12},{10,14},{12,0},{14,2},{1,5},{3,7},... | collective-permute-start | bytes 208904 | tf_op jit(solution)/shard_map/ppermute | solution.py:636
  71.4 7.1 %collective-permute-start.17 = (bf16[2,16,2,16,128]{4,3,2,1,0:T(8,128)(2,1)S(1)}, bf16[2,16,2,16,128]{4,3,2,1,0:T(8,128)(2,1)S(1)}, u32[]{:S(2)}, u32[]{:S(2)}) collective-permute-start(bf16[2,16,2,16,128]{4,3,2,1,0:T(8,128)(2,1)S(1)} %get-tuple-element.98.refs_5_), channel_id=1, source_target_pairs={{0,16},{16,0},{1,17},{17,1},{2,18},{18,2},{3,19},{19,3},{4,20},{20... | collective-permute-start | bytes 786440 | tf_op jit(solution)/shard_map/ppermute | solution.py:640
  71.5 7.0 %collective-permute-start.18 = (bf16[2,16,2,16,128]{4,3,2,1,0:T(8,128)(2,1)S(1)}, bf16[2,16,2,16,128]{4,3,2,1,0:T(8,128)(2,1)S(1)}, u32[]{:S(2)}, u32[]{:S(2)}) collective-permute-start(bf16[2,16,2,16,128]{4,3,2,1,0:T(8,128)(2,1)S(1)} %collective-permute-done.7.refs_6_), channel_id=1, source_target_pairs={{0,16},{16,0},{1,17},{17,1},{2,18},{18,2},{3,19},{19,3},{4,20},{20... | collective-permute-start | bytes 786440 | tf_op jit(solution)/shard_map/ppermute | solution.py:640
  72.0 6.5 %collective-permute-start.19 = (bf16[2,16,2,16,128]{4,3,2,1,0:T(8,128)(2,1)S(1)}, bf16[2,16,2,16,128]{4,3,2,1,0:T(8,128)(2,1)S(1)}, u32[]{:S(2)}, u32[]{:S(2)}) collective-permute-start(bf16[2,16,2,16,128]{4,3,2,1,0:T(8,128)(2,1)S(1)} %collective-permute-done.8.refs_7_), channel_id=1, source_target_pairs={{0,16},{16,0},{1,17},{17,1},{2,18},{18,2},{3,19},{19,3},{4,20},{20... | collective-permute-start | bytes 786440 | tf_op jit(solution)/shard_map/ppermute | solution.py:640
  72.1 6.5 %collective-permute-start.20 = (bf16[2,16,2,16,128]{4,3,2,1,0:T(8,128)(2,1)S(1)}, bf16[2,16,2,16,128]{4,3,2,1,0:T(8,128)(2,1)S(1)}, u32[]{:S(2)}, u32[]{:S(2)}) collective-permute-start(bf16[2,16,2,16,128]{4,3,2,1,0:T(8,128)(2,1)S(1)} %collective-permute-done.9.refs_8_), channel_id=1, source_target_pairs={{0,16},{16,0},{1,17},{17,1},{2,18},{18,2},{3,19},{19,3},{4,20},{20... | collective-permute-start | bytes 786440 | tf_op jit(solution)/shard_map/ppermute | solution.py:640
  78.6 9.4 %collective-permute-start.23 = (bf16[400,128]{1,0:T(8,128)(2,1)S(1)}, bf16[400,128]{1,0:T(8,128)(2,1)S(1)}, u32[]{:S(2)}, u32[]{:S(2)}) collective-permute-start(bf16[400,128]{1,0:T(8,128)(2,1)S(1)} %get-tuple-element.109), channel_id=1, source_target_pairs={{0,12},{2,14},{4,0},{6,2},{8,4},{10,6},{12,8},{14,10},{1,13},{3,15... | collective-permute-start | bytes 307208 | tf_op jit(solution)/shard_map/ppermute | solution.py:636
  79.8 10.2 %collective-permute-start.22 = (bf16[400,128]{1,0:T(8,128)(2,1)S(1)}, bf16[400,128]{1,0:T(8,128)(2,1)S(1)}, u32[]{:S(2)}, u32[]{:S(2)}) collective-permute-start(bf16[400,128]{1,0:T(8,128)(2,1)S(1)} %get-tuple-element.107), channel_id=1, source_target_pairs={{0,8},{2,10},{4,12},{6,14},{8,0},{10,2},{12,4},{14,6},{1,9},{3,11}... | collective-permute-start | bytes 307208 | tf_op jit(solution)/shard_map/ppermute | solution.py:636
  79.8 11.4 %collective-permute-start.21 = (bf16[400,128]{1,0:T(8,128)(2,1)S(1)}, bf16[400,128]{1,0:T(8,128)(2,1)S(1)}, u32[]{:S(2)}, u32[]{:S(2)}) collective-permute-start(bf16[400,128]{1,0:T(8,128)(2,1)S(1)} %get-tuple-element.105), channel_id=1, source_target_pairs={{0,4},{2,6},{4,8},{6,10},{8,12},{10,14},{12,0},{14,2},{1,5},{3,7},... | collective-permute-start | bytes 307208 | tf_op jit(solution)/shard_map/ppermute | solution.py:636
  87.9 13.2 %collective-permute-start.28 = (f32[384,128]{1,0:T(8,128)S(1)}, f32[384,128]{1,0:T(8,128)S(1)}, u32[]{:S(2)}, u32[]{:S(2)}) collective-permute-start(f32[384,128]{1,0:T(8,128)S(1)} %get-tuple-element.110.refs_6_), channel_id=1, source_target_pairs={{0,16},{16,0},{1,17},{17,1},{2,18},{18,2},{3,19},{19,3},{4,20},{20... | collective-permute-start | bytes 589832 | tf_op jit(solution)/shard_map/ppermute | solution.py:647
  88.0 5.2 %collective-permute-start.26 = (bf16[384,128]{1,0:T(8,128)(2,1)S(1)}, bf16[384,128]{1,0:T(8,128)(2,1)S(1)}, u32[]{:S(2)}, u32[]{:S(2)}) collective-permute-start(bf16[384,128]{1,0:T(8,128)(2,1)S(1)} %get-tuple-element.116), channel_id=1, source_target_pairs={{0,12},{2,14},{4,0},{6,2},{8,4},{10,6},{12,8},{14,10},{1,13},{3,15... | collective-permute-start | bytes 294920 | tf_op jit(solution)/shard_map/ppermute | solution.py:636
  90.0 10.6 %collective-permute-start.25 = (bf16[384,128]{1,0:T(8,128)(2,1)S(1)}, bf16[384,128]{1,0:T(8,128)(2,1)S(1)}, u32[]{:S(2)}, u32[]{:S(2)}) collective-permute-start(bf16[384,128]{1,0:T(8,128)(2,1)S(1)} %get-tuple-element.114), channel_id=1, source_target_pairs={{0,8},{2,10},{4,12},{6,14},{8,0},{10,2},{12,4},{14,6},{1,9},{3,11}... | collective-permute-start | bytes 294920 | tf_op jit(solution)/shard_map/ppermute | solution.py:636
  91.1 9.4 %collective-permute-start.24 = (bf16[384,128]{1,0:T(8,128)(2,1)S(1)}, bf16[384,128]{1,0:T(8,128)(2,1)S(1)}, u32[]{:S(2)}, u32[]{:S(2)}) collective-permute-start(bf16[384,128]{1,0:T(8,128)(2,1)S(1)} %get-tuple-element.112), channel_id=1, source_target_pairs={{0,4},{2,6},{4,8},{6,10},{8,12},{10,14},{12,0},{14,2},{1,5},{3,7},... | collective-permute-start | bytes 294920 | tf_op jit(solution)/shard_map/ppermute | solution.py:636
  92.0 9.1 %collective-permute-start.27 = (f32[272,128]{1,0:T(8,128)S(1)}, f32[272,128]{1,0:T(8,128)S(1)}, u32[]{:S(2)}, u32[]{:S(2)}) collective-permute-start(f32[272,128]{1,0:T(8,128)S(1)} %get-tuple-element.102.refs_1_), channel_id=1, source_target_pairs={{0,16},{16,0},{1,17},{17,1},{2,18},{18,2},{3,19},{19,3},{4,20},{20... | collective-permute-start | bytes 417800 | tf_op jit(solution)/shard_map/ppermute | solution.py:647
  93.2 7.9 %collective-permute-start.31 = (bf16[384,128]{1,0:T(8,128)(2,1)S(1)}, bf16[384,128]{1,0:T(8,128)(2,1)S(1)}, u32[]{:S(2)}, u32[]{:S(2)}) collective-permute-start(bf16[384,128]{1,0:T(8,128)(2,1)S(1)} %collective-permute-done.26.refs_9_), channel_id=1, source_target_pairs={{0,16},{16,0},{1,17},{17,1},{2,18},{18,2},{3,19},{19,3},{4,20},{20... | collective-permute-start | bytes 294920 | tf_op jit(solution)/shard_map/ppermute | solution.py:647
  100.6 1.3 %collective-permute-start.30 = (bf16[384,128]{1,0:T(8,128)(2,1)S(1)}, bf16[384,128]{1,0:T(8,128)(2,1)S(1)}, u32[]{:S(2)}, u32[]{:S(2)}) collective-permute-start(bf16[384,128]{1,0:T(8,128)(2,1)S(1)} %collective-permute-done.25.refs_8_), channel_id=1, source_target_pairs={{0,16},{16,0},{1,17},{17,1},{2,18},{18,2},{3,19},{19,3},{4,20},{20... | collective-permute-start | bytes 294920 | tf_op jit(solution)/shard_map/ppermute | solution.py:647
  100.6 1.5 %collective-permute-start.29 = (bf16[384,128]{1,0:T(8,128)(2,1)S(1)}, bf16[384,128]{1,0:T(8,128)(2,1)S(1)}, u32[]{:S(2)}, u32[]{:S(2)}) collective-permute-start(bf16[384,128]{1,0:T(8,128)(2,1)S(1)} %collective-permute-done.24.refs_7_), channel_id=1, source_target_pairs={{0,16},{16,0},{1,17},{17,1},{2,18},{18,2},{3,19},{19,3},{4,20},{20... | collective-permute-start | bytes 294920 | tf_op jit(solution)/shard_map/ppermute | solution.py:647

commit v10 on v9

--- a/solution.py
+++ b/solution.py
@@ -18,14 +18,17 @@
 TILE = 4
 JOIN = 2
 
-G_AT, O_AT, CORE_AT, CT_AT, DELAY_AT = range(5)
-
 VMEM = pl.BlockSpec(memory_space=pltpu.VMEM)
 SMEM = pl.BlockSpec(memory_space=pltpu.SMEM)
 
 
 def params(mib):
     return pltpu.CompilerParams(vmem_limit_bytes=mib * 2**20)
+
+
+def position():
+    place = lax.axis_index("tm")
+    return lax.axis_index("stn"), place // PAIR, place % PAIR, lax.axis_index("ct")
 
 
 def cost(flops, size):
@@ -80,64 +83,81 @@
     return np.concatenate([cosine, cosine], axis=1), np.concatenate([sine, sine], axis=1)
 
 
-def pick_kernel(half, meta, block, *refs):
+def pick_kernel(half, block, *refs):
     outs, rows = refs[:-1], refs[-1]
     inputs, samples = block.shape[1], block.shape[2]
+    tall = samples // LANES
     step = 16
     for part in range(2):
-
-        def spread(n, carry, part=part):
-            low = pl.multiple_of(n * step * LANES, step * LANES)
-            wide = block[part, :, pl.ds(low, step * LANES)].astype(jnp.float32)
+        for n in range(tall // step):
+            cut = slice(n * step * LANES, (n + 1) * step * LANES)
+            wide = block[part, :, cut].astype(jnp.float32)
             for u in range(step):
-                at = pl.multiple_of((n * step + u) * inputs, inputs)
-                rows[part, pl.ds(at, inputs), :] = wide[:, u * LANES : (u + 1) * LANES]
-            return carry
-
-        lax.fori_loop(0, samples // LANES // step, spread, 0)
-    g = meta[G_AT]
-    tall = 128
+                at = (n * step + u) * inputs
+                rows[part, at : at + inputs, :] = wide[:, u * LANES : (u + 1) * LANES]
+    g = position()[2]
     for item in range(inputs):
         first = (1 - g) * half + item if item < half else g * half + item - half
-        out = outs[item // JOIN].at[item % JOIN]
-
-        def gather(n, carry, first=first, out=out):
-            low = pl.multiple_of(n * tall, tall)
-            for part in range(2):
-                value = rows[part, pl.ds(low * inputs + first, tall, stride=inputs), :]
-                out[part, pl.ds(low, tall), :] = value.astype(jnp.bfloat16)
-            return carry
-
-        lax.fori_loop(0, samples // LANES // tall, gather, 0)
-
-
-def pick(meta, block):
+        for part in range(2):
+            value = rows[part, pl.ds(first, tall, stride=inputs), :]
+            outs[item // JOIN][item % JOIN, part] = value.astype(jnp.bfloat16)
+
+
+def pick(block):
     _, inputs, samples = block.shape
     half = inputs // PAIR
-    one = (2, samples // LANES, LANES)
-    shapes = [(JOIN,) + one] * (inputs // JOIN)
+    steps = 8
+    tall = samples // LANES // steps
+    shape = jax.ShapeDtypeStruct((JOIN, 2, samples // LANES, LANES), jnp.bfloat16)
     return pl.pallas_call(
         functools.partial(pick_kernel, half),
-        out_shape=[jax.ShapeDtypeStruct(s, jnp.bfloat16) for s in shapes],
-        in_specs=[SMEM, VMEM],
-        out_specs=[VMEM] * len(shapes),
-        scratch_shapes=[pltpu.VMEM((2, samples // LANES * inputs, LANES), jnp.float32)],
-        compiler_params=params(16),
+        grid=(steps,),
+        out_shape=[shape] * (inputs // JOIN),
+        in_specs=[pl.BlockSpec((2, inputs, samples // steps), lambda t: (0, 0, t))],
+        out_specs=[pl.BlockSpec((JOIN, 2, tall, LANES), lambda t: (0, 0, t, 0))] * (inputs // JOIN),
+        scratch_shapes=[pltpu.VMEM((2, tall * inputs, LANES), jnp.float32)],
+        compiler_params=params(56),
         cost_estimate=cost(10**6, 2**18),
         name="pick",
-    )(meta, block)
+    )(block)
 
 
 def follow(block, after):
     return lax.optimization_barrier((block, after))[0]
 
 
+def joined(blocks):
+    def kernel(*refs):
+        sources, out = refs[:-1], refs[-1]
+        for n, source in enumerate(sources):
+            size = source.shape[0]
+            for item in range(size):
+
+                def step(m, carry, n=n, source=source, size=size, item=item):
+                    cut = pl.ds(m * 4, 4)
+                    out[n * size + item, cut] = source[item, cut]
+                    return carry
+
+                lax.fori_loop(0, source.shape[1] // 4, step, 0)
+
+    shape = (sum(block.shape[0] for block in blocks),) + blocks[0].shape[1:]
+    return pl.pallas_call(
+        kernel,
+        out_shape=jax.ShapeDtypeStruct(shape, blocks[0].dtype),
+        in_specs=[VMEM] * len(blocks),
+        out_specs=VMEM,
+        compiler_params=params(8),
+        cost_estimate=cost(10**6, 2**18),
+        name="join",
+    )(*blocks)
+
+
 SOME = 4
 
 
 def filterbank_kernel(late, part, frames, dests, per_ct, half_count, *refs):
-    meta, refs = refs[0], refs[1:]
-    me, ct = meta[G_AT], meta[CT_AT]
+    delays, refs = refs[0], refs[1:]
+    _, _, me, ct = position()
     if late:
         keep, recv = refs[:2]
         refs = refs[2:]
@@ -178,7 +198,7 @@
 
     downs, acrosses = [], []
     for item in range(JOIN):
-        delay = meta[DELAY_AT + me * half_count + part * JOIN + item]
+        delay = delays[me * half_count + part * JOIN + item]
         down, across = delay // LANES, delay % LANES
         downs.append(down)
         acrosses.append(across)
@@ -272,7 +292,7 @@
                 turn(item - 1, n * SOME)
 
 
-def filterbank(part, half, meta, sources, tables, beside, dests):
+def filterbank(part, half, delays, sources, tables, beside, dests):
     late = not beside
     frames = sources[0].shape[2] // ROWS
     size = tables[-1].shape[2] // 2
@@ -294,7 +314,7 @@
         compiler_params=params(14),
         cost_estimate=cost(10**6, 2**18),
         name="filterbank_late" if late else "filterbank_early",
-    )(meta, *sources, *tables, *beside)
+    )(delays, *sources, *tables, *beside)
 
 
 SQUARE = [(p, q) for p in range(TILE) for q in range(TILE)]
@@ -331,43 +351,44 @@
 
 def correlate_kernel(layout, *refs):
     sources_at, blocks, own, terms, outer, span, per_ct = layout
-    meta, sources = refs[0], refs[1 : 1 + len(sources_at)]
-    rest = refs[1 + len(sources_at) :]
+    sources, rest = refs[: len(sources_at)], refs[len(sources_at) :]
     earlier, outs, (spectra, sums, held) = rest[:terms], rest[terms:-3], rest[-3:]
     steps = spectra.shape[1]
     some = 8
-    core, g, ct = meta[CORE_AT], meta[G_AT], meta[CT_AT]
+    core, o, g, ct = position()
     within = any(block[0] for block in blocks)
     across = any(not block[0] for block in blocks)
 
-    for source, (far, dg, dc, part) in zip(sources, sources_at):
-        device = lax.rem(ct - dc + per_ct, per_ct) * PAIR + (g ^ dg)
-        base = (part * per_ct * PAIR + device) * JOIN
-        wanted = None
-        if across:
-            side = 1 - core if far else core
-            wanted = (side == 1) | (lax.rem(base // TILE, 2) == core)
-            if within and not far:
-                wanted = None
-            base = base + side * own
-
-        def bring(source=source, base=base):
-            for item in range(source.shape[0]):
-
-                def spread(n, carry, item=item):
-                    for u in range(some):
-                        real = source[item, n * some + u, 0].astype(jnp.float32)
-                        imag = source[item, n * some + u, 1].astype(jnp.float32)
-                        for which, value in enumerate((real, imag, real + imag, imag - real)):
-                            spectra[base + item, n * some + u, which] = value
-                    return carry
-
-                lax.fori_loop(0, steps // some, spread, 0)
-
-        if wanted is None:
-            bring()
-        else:
-            pl.when(wanted)(bring)
+    for source, (far, part) in zip(sources, sources_at):
+        for n in range(PAIR * per_ct):
+            dg, dc = n // per_ct, n % per_ct
+            device = lax.rem(ct - dc + per_ct, per_ct) * PAIR + (g ^ dg)
+            base = (part * per_ct * PAIR + device) * JOIN
+            wanted = None
+            if across:
+                side = 1 - core if far else core
+                wanted = (side == 1) | (lax.rem(base // TILE, 2) == core)
+                if within and not far:
+                    wanted = None
+                base = base + side * own
+
+            def bring(source=source, base=base, n=n):
+                for item in range(JOIN):
+
+                    def spread(m, carry, item=item):
+                        for u in range(some):
+                            real = source[n * JOIN + item, m * some + u, 0].astype(jnp.float32)
+                            imag = source[n * JOIN + item, m * some + u, 1].astype(jnp.float32)
+                            for which, value in enumerate((real, imag, real + imag, imag - real)):
+                                spectra[base + item, m * some + u, which] = value
+                        return carry
+
+                    lax.fori_loop(0, steps // some, spread, 0)
+
+            if wanted is None:
+                bring()
+            else:
+                pl.when(wanted)(bring)
 
     high = lax.broadcasted_iota(jnp.int32, (1, LANES), 1) < RADIX
     rows_outer = pairs_in(blocks) * span
@@ -426,7 +447,7 @@
         done = end
 
     for r in range(outer):
-        base = pl.multiple_of(lax.rem(meta[O_AT] + r, outer) * rows_outer, 16)
+        base = pl.multiple_of(lax.rem(o + r, outer) * rows_outer, 16)
         outs[r][...] = sums[pl.ds(base, rows_outer), :].astype(outs[r].dtype)
     if terms:
         total = earlier[0][...].astype(jnp.float32)
@@ -435,7 +456,7 @@
         outs[outer][...] = total
 
 
-def correlate(meta, arrays, sources_at, blocks, own, sizes, name, earlier=()):
+def correlate(arrays, sources_at, blocks, own, sizes, name, earlier=()):
     outer, span, _ = sizes
     _, steps, _, size, _ = arrays[0].shape
     inputs = own if all(block[0] for block in blocks) else 2 * own
@@ -449,7 +470,7 @@
     return pl.pallas_call(
         functools.partial(correlate_kernel, layout),
         out_shape=shapes,
-        in_specs=[SMEM] + [VMEM] * (len(arrays) + len(earlier)),
+        in_specs=[VMEM] * (len(arrays) + len(earlier)),
         out_specs=[VMEM] * len(shapes),
         scratch_shapes=[
             pltpu.VMEM((inputs, steps, 4, size, LANES), jnp.float32),
@@ -459,13 +480,12 @@
         compiler_params=params(8 + inputs * steps * 4 * size * LANES * 4 // 2**20),
         cost_estimate=cost(10**6, 2**18),
         name=name,
-    )(meta, *arrays, *earlier)
+    )(*arrays, *earlier)
 
 
 def assemble_kernel(own, outer, span, scale, sets, order, counts, *refs):
-    meta = refs[0]
     out, joined = refs[-2:]
-    sources, at = [], 1
+    sources, at = [], 0
     for count in counts:
         sources.append(refs[at : at + count])
         at += count
@@ -473,7 +493,9 @@
     lane = lax.broadcasted_iota(jnp.int32, (1, LANES), 1)
     high = lane < RADIX
     mirror = jnp.where(high, 1.0, -1.0).astype(jnp.float32)
-    me = meta[CORE_AT]
+    me = position()[0]
+    across = 2 * own * span
+    mine_at = pl.multiple_of(me * own * span, 8)
 
     def added(parts, low, rows):
         total = parts[0][low : low + rows, :].astype(jnp.float32)
@@ -481,34 +503,51 @@
             total = total + part[low : low + rows, :].astype(jnp.float32)
         return total * scale
 
-    def put(value, row, col):
-        at = pl.multiple_of((row * 2 * own + col) * span, span)
-        joined[pl.ds(at, span), :] = value
-
-    sign = jnp.where(me == 0, jnp.ones_like(mirror), mirror)
-    for blocks, mine, others in zip(sets, near, far):
+    def put(value, places, base=0):
+        n = 0
+        while n < len(places):
+            wide = 1
+            if places[n] % 8 == 0 and places[n + 1 : n + 2] == [places[n] + span] and span < 8:
+                wide = 2
+            rows = value[n * span : (n + wide) * span]
+            joined[pl.ds(base + places[n], wide * span), :] = rows
+            n += wide
+
+    def inner(total, i, j, pairs):
+        direct = [order[i * TILE + p] * across + order[j * TILE + q] * span for p, q in pairs]
+        turned = [order[j * TILE + q] * across + order[i * TILE + p] * span for p, q in pairs]
+        put(total, direct, mine_at)
+        for n, (p, q) in enumerate(pairs):
+            if (i, p) != (j, q):
+                value = total[n * span : (n + 1) * span] * mirror
+                put(value, [turned[n]], mine_at)
+
+    def outer_pairs(core):
+        for blocks, mine, others in zip(sets, near, far):
+            low = 0
+            for within, i, j, pairs in blocks:
+                rows = len(pairs) * span
+                if not within:
+                    for parts, side in ((mine, core), (others, 1 - core)):
+                        total = added(parts, low, rows)
+                        a = [order[(i + side) * TILE + p] for p, _ in pairs]
+                        b = [order[j * TILE + q] for _, q in pairs]
+                        if core == 0:
+                            put(total, [x * across + (own + y) * span for x, y in zip(a, b)])
+                        else:
+                            total = total * mirror
+                            put(total, [y * across + x * span for x, y in zip(a, b)])
+                low += rows
+
+    for blocks, mine in zip(sets, near):
         low = 0
         for within, i, j, pairs in blocks:
             rows = len(pairs) * span
             if within:
-                total = added(mine, low, rows)
-                turned = total * mirror
-                for n, (p, q) in enumerate(pairs):
-                    cut = slice(n * span, (n + 1) * span)
-                    a, b = order[i * TILE + p], order[j * TILE + q]
-                    put(total[cut], a, me * own + b)
-                    if a != b:
-                        put(turned[cut], b, me * own + a)
-            else:
-                for parts, side in ((mine, me), (others, 1 - me)):
-                    total = added(parts, low, rows) * sign
-                    for n, (p, q) in enumerate(pairs):
-                        a = jnp.where(side == 0, order[i * TILE + p], order[(i + 1) * TILE + p])
-                        b = order[j * TILE + q]
-                        row = jnp.where(me == 0, a, b)
-                        col = jnp.where(me == 0, own + b, a)
-                        put(total[n * span : (n + 1) * span], row, col)
+                inner(added(mine, low, rows), i, j, pairs)
             low += rows
+    pl.when(me == 0)(lambda: outer_pairs(0))
+    pl.when(me != 0)(lambda: outer_pairs(1))
 
     def emit(a, carry):
         for tile in range(2 * own // 8):
@@ -523,23 +562,28 @@
                 out[1, a, tile * 8 : tile * 8 + 8, cut] = jnp.where(high, turned[0], loads[1])
         return carry
 
-    lax.fori_loop(0, own, emit, 0)
-
-
-def assemble(meta, near, far, sets, order, own, span, scale):
+    def emit_some(n, carry):
+        for u in range(4):
+            emit(n * 4 + u, carry)
+        return carry
+
+    lax.fori_loop(0, own // 4, emit_some, 0)
+
+
+def assemble(near, far, sets, order, own, span, scale):
     outer = len(near[1])
     counts = [len(arrays) for arrays in near + far]
     sources = [x for arrays in near + far for x in arrays]
     return pl.pallas_call(
         functools.partial(assemble_kernel, own, outer, span, scale, sets, order, counts),
         out_shape=jax.ShapeDtypeStruct((2, own, 2 * own, span * RADIX), jnp.float32),
-        in_specs=[SMEM] + [VMEM] * len(sources),
+        in_specs=[VMEM] * len(sources),
         out_specs=VMEM,
         scratch_shapes=[pltpu.VMEM((own * 2 * own * span, LANES), jnp.float32)],
         compiler_params=params(10),
         cost_estimate=cost(10**6, 2**18),
         name="assemble",
-    )(meta, *sources)
+    )(*sources)
 
 
 def fast_fits(in_count, frame_count):
@@ -570,16 +614,11 @@
     own = in_count * per_ct
     half = in_count // PAIR
     place_tm, place_ct = lax.axis_index("tm"), lax.axis_index("ct")
-    core = lax.axis_index("stn")
-    g, o = place_tm % PAIR, place_tm // PAIR
+    g = place_tm % PAIR
 
     swap = [(i, i ^ 1) for i in range(tm)]
     onward = [(i, i + PAIR) for i in range(tm - PAIR)]
     cores = [(0, 1), (1, 0)]
-
-    scalars = [None] * DELAY_AT
-    scalars[G_AT], scalars[O_AT], scalars[CORE_AT], scalars[CT_AT] = g, o, core, place_ct
-    meta = jnp.concatenate([jnp.stack(scalars).astype(jnp.int32), delays])
 
     dests = [(dg, dc) for dg in range(PAIR) for dc in range(per_ct)]
     base = last_table(outer, per_ct, span)
@@ -587,7 +626,7 @@
     tables = [jnp.asarray(t) for t in tables + [np.concatenate([base, base], axis=1)]]
 
     parts = half // JOIN
-    picked = pick(meta, voltages)
+    picked = pick(voltages)
     sends, keeps = picked[:parts], picked[parts:]
     recvs = [lax.ppermute(block, "tm", swap) for block in sends]
     halos, lates = [], []
@@ -595,39 +634,27 @@
         recv = follow(recvs[c], lates[-1]) if lates else recvs[c]
         halos.append(lax.ppermute(jnp.where(g == 1, keeps[c], recv), "tm", onward))
         sources = [keeps[c], follow(recvs[c], halos[c - 1]) if c else recvs[c]]
-        lates.append(filterbank(c, half, meta, sources, tables, [], len(dests)))
+        lates.append(filterbank(c, half, delays, sources, tables, [], len(dests)))
 
     sets = pair_sets(own, parts)
     sizes = (outer, span, per_ct)
-    arrays, places = [], []
-    done = []
+    received = []
     for c in range(parts):
         halo = follow(halos[c], recvs[c + 1]) if c + 1 < parts else halos[c]
         sources = [halo, keeps[c], recvs[c]]
-        spectra = filterbank(c, half, meta, sources, tables, lates[c], len(dests))
-        done.append(spectra[0])
-        for (dg, dc), block in zip(dests, spectra):
+        spectra = filterbank(c, half, delays, sources, tables, lates[c], len(dests))
+        arrays = []
+        for n, ((dg, dc), block) in enumerate(zip(dests, spectra)):
             route = []
             for i in range(tm):
                 for j in range(per_ct):
                     target = (i ^ dg) * per_ct + (j + dc) % per_ct
                     route.append((i * per_ct + j, target))
             if dg or dc:
-                if len(arrays) >= len(dests):
-                    block = follow(block, arrays[-len(dests)])
+                block = follow(block, received[-1][n]) if received else block
                 block = lax.ppermute(block, ("tm", "ct"), route)
             arrays.append(block)
-            places.append((dg, dc, c))
-
-    near = [(False,) + place for place in places]
-    far = [(True,) + place for place in places]
-    count = len(dests)
-    others = [lax.ppermute(follow(block, done[-1]), "stn", cores) for block in arrays[:count]]
-    early = correlate(
-        meta, arrays[:count] + others, near[:count] + far[:count], sets[0], own // parts, sizes,
-        "correlate_early",
-    )
-    own_late = correlate(meta, arrays, near, sets[1], own, sizes, "correlate_own")
+        received.append(arrays)
 
     def along(parts, after):
         moved = [parts[0]]
@@ -636,11 +663,19 @@
             moved.append(lax.ppermute(follow(parts[r], after(r)), "tm", route))
         return moved
 
-    early = along(early, lambda r: others)
-    others += [lax.ppermute(follow(block, early), "stn", cores) for block in arrays[count:]]
-    own_late = along(own_late, lambda r: others)
+    near = [joined([follow(block, spectra[0]) for block in received[0]])]
+    far = [lax.ppermute(near[0], "stn", cores)]
+    early = correlate(
+        near + far, [(False, 0), (True, 0)], sets[0], own // parts, sizes, "correlate_early"
+    )
+    early = along(early, lambda r: [])
+    near.append(joined([follow(block, early[1:3]) for block in received[1]]))
+    far.append(lax.ppermute(near[1], "stn", cores))
+    sources_at = [(False, c) for c in range(parts)] + [(True, c) for c in range(parts)]
+    own_late = correlate(near, sources_at[:parts], sets[1], own, sizes, "correlate_own")
+    own_late = along(own_late, lambda r: [far[1], early[r]])
     *cross_late, early = correlate(
-        meta, arrays + others, near + far, sets[2], own, sizes, "correlate_cross", early
+        near + far, sources_at, sets[2], own, sizes, "correlate_cross", early
     )
     cross_late = along(cross_late, lambda r: own_late[r])
     mine = [[early], own_late, cross_late]
@@ -652,7 +687,7 @@
             start = device // PAIR * in_count + device % PAIR * half + part * JOIN
             order += range(start, start + JOIN)
     scale = 1.0 / (tm * frame_count)
-    result = assemble(meta, mine, theirs, sets, order, own, span, scale)
+    result = assemble(mine, theirs, sets, order, own, span, scale)
     return result.transpose(0, 3, 1, 2)
 
 

time: 106 us -> 103 us (0.972)
  waiting for transfers between devices: 32.3 us -> 29.6 us
  local copies, waits for them, and re-layouts: 2.4 us -> 1.06 us
  starting transfers between devices: 31.8 us -> 33 us
    pallas_call x1 -> x3, Pallas kernels: 3.11 us -> 6.38 us  [the longest x1 6.01 us: pick(): pl.pallas_call(functools.partial(pick_kernel, half), grid=(steps,), out_s...]
    ppermute x9, starting transfers between devices: 11.7 us -> 13.7 us  [along(): moved.append(lax.ppermute(follow(parts[r], after(r)), 'tm', route))]
    pallas_call x1, Pallas kernels: 3.65 us -> 1.7 us  [assemble(): pl.pallas_call(functools.partial(assemble_kernel, own, outer, span, scale...]
    pallas_call x3, Pallas kernels: 16.8 us -> 15 us  [correlate(): pl.pallas_call(functools.partial(correlate_kernel, layout), out_shape=sha...]
    ppermute x8 -> x2, starting transfers between devices: 1.66 us -> 0.14 us  [the longest x1 0.07 us: fast(): far = [lax.ppermute(near[0], 'stn', cores)]]
    ppermute x9, waiting for transfers between devices: 13.5 us -> 12.4 us  [along(): moved.append(lax.ppermute(follow(parts[r], after(r)), 'tm', route))]
    ppermute x2, waiting for transfers between devices: 15.4 us -> 14.3 us  [fast(): recvs = [lax.ppermute(block, 'tm', swap) for block in sends]]
  transfers between devices with their start and end apart: 32 -> 26, of which waited for: 9 -> 10; matrix products, arithmetic and copies ran while one was open for 0% -> 0% of each run, Pallas kernels for 30% -> 30%
where the time goes in v10:
time: 103 us; the launch traced here: 102 us
  Pallas kernels  38.4 us (37%)
  starting transfers between devices  33 us (32%)
  waiting for transfers between devices  29.6 us (29%)
  local copies, waits for them, and re-layouts  1.06 us (1%)
    pallas_call x4, Pallas kernels, filterbank(): pl.pallas_call(kernel, out_shape=[jax.ShapeDtypeStruct(shape, jnp.bfloat1...  15.2 us
    pallas_call x3, Pallas kernels, correlate(): pl.pallas_call(functools.partial(correlate_kernel, layout), out_shape=sha...  15 us
    ppermute x2, waiting for transfers between devices, fast(): recvs = [lax.ppermute(block, 'tm', swap) for block in sends]  14.3 us
    ppermute x9, starting transfers between devices, along(): moved.append(lax.ppermute(follow(parts[r], after(r)), 'tm', route))  13.7 us
    ppermute x9, waiting for transfers between devices, along(): moved.append(lax.ppermute(follow(parts[r], after(r)), 'tm', route))  12.4 us
    ppermute x2, starting transfers between devices, fast(): halos.append(lax.ppermute(jnp.where(g == 1, keeps[c], recv), 'tm', onward))  7.84 us
    ppermute x6, starting transfers between devices, fast(): block = lax.ppermute(block, ('tm', 'ct'), route)  7.66 us
    pallas_call x1, Pallas kernels, pick(): pl.pallas_call(functools.partial(pick_kernel, half), grid=(steps,), out_s...  6.01 us
  transfers between devices with their start and end apart: 26, of which 10 were waited for; matrix products, arithmetic and copies ran while one was open for 0% of the time, Pallas kernels for 30%

profile of v10, /device:TPU:0, one launch (start us, length us, event | category | flops | bytes accessed | tf_op | source)
XLA Modules:
  0.0 102.3 jit_solution(7087641850308518861)
XLA Ops:
  0.0 6.0 %pick.1 = (bf16[2,2,512,128]{3,2,1,0:T(8,128)(2,1)}, bf16[2,2,512,128]{3,2,1,0:T(8,128)(2,1)}, bf16[2,2,512,128]{3,2,1,0:T(8,128)(2,1)}, bf16[2,2,512,128]{3,2,1,0:T(8,128)(2,1)}) custom-call(bf16[2,8,65536]{2,1,0:T(8,128)(2,1)} %block.1), custom_call_target="tpu_custom_call" | custom-call | flops 1000000 | bytes 262144 | tf_op jit(solution)/shard_map/pick/pallas_call | solution.py:112
  6.0 3.0 %collective-permute-start = (bf16[2,2,512,128]{3,2,1,0:T(8,128)(2,1)}, bf16[2,2,512,128]{3,2,1,0:T(8,128)(2,1)S(1)}, u32[]{:S(2)}, u32[]{:S(2)}) collective-permute-start(bf16[2,2,512,128]{3,2,1,0:T(8,128)(2,1)} %get-tuple-element.59), channel_id=1, source_target_pairs={{0,2},{2,0},{4,6},{6,4},{8,10},{10,8},{12,14},{14,12},{1,3},{3,1},... | collective-permute-start | bytes 1572872 | tf_op jit(solution)/shard_map/ppermute | solution.py:631
  9.0 0.1 collective-permute-start.2
  9.1 12.9 %collective-permute-done.refs_2_.refs_3_ = bf16[2,2,512,128]{3,2,1,0:T(8,128)(2,1)S(1)} collective-permute-done((bf16[2,2,512,128]{3,2,1,0:T(8,128)(2,1)}, bf16[2,2,512,128]{3,2,1,0:T(8,128)(2,1)S(1)}, u32[]{:S(2)}, u32[]{:S(2)}) %collective-permute-start) | collective-permute-done | bytes 524320 | tf_op jit(solution)/shard_map/ppermute | solution.py:631
  22.0 0.1 broadcast_select_fusion.1
  22.1 4.1 %collective-permute-start.1 = (bf16[2,2,512,128]{3,2,1,0:T(8,128)(2,1)S(1)}, bf16[2,2,512,128]{3,2,1,0:T(8,128)(2,1)S(1)}, u32[]{:S(2)}, u32[]{:S(2)}) collective-permute-start(bf16[2,2,512,128]{3,2,1,0:T(8,128)(2,1)S(1)} %broadcast_select_fusion.1), channel_id=1, source_target_pairs={{0,4},{2,6},{4,8},{6,10},{8,12},{10,14},{1,5},{3,7},{5,9},{7,11},{... | collective-permute-start | bytes 1572872 | tf_op jit(solution)/shard_map/ppermute | solution.py:635
  26.2 1.0 %copy-done.2 = bf16[2,2,512,128]{3,2,1,0:T(8,128)(2,1)S(1)} copy-done((bf16[2,2,512,128]{3,2,1,0:T(8,128)(2,1)S(1)}, bf16[2,2,512,128]{3,2,1,0:T(8,128)(2,1)}, u32[]{:S(2)}) %copy-start.2) | copy-done | bytes 524312
  27.2 3.7 %filterbank_late.2 = (bf16[2,8,2,16,128]{4,3,2,1,0:T(8,128)(2,1)S(1)}, bf16[2,8,2,16,128]{4,3,2,1,0:T(8,128)(2,1)S(1)}, bf16[2,8,2,16,128]{4,3,2,1,0:T(8,128)(2,1)S(1)}, bf16[2,8,2,16,128]{4,3,2,1,0:T(8,128)(2,1)S(1)}) custom-call(s32[8]{0:T(128)S(1)} %copy-done.7, bf16[2,2,512,128]{3,2,1,0:T(8,128)(2,1)S(1)} %copy-done.2, ...), custom_call_target="tpu_custom_call" | custom-call | flops 1000000 | bytes 262144 | tf_op jit(solution)/shard_map/filterbank_late/pallas_call | solution.py:303
  31.0 1.4 %collective-permute-done.2.refs_2_.refs_3_ = bf16[2,2,512,128]{3,2,1,0:T(8,128)(2,1)S(1)} collective-permute-done((bf16[2,2,512,128]{3,2,1,0:T(8,128)(2,1)}, bf16[2,2,512,128]{3,2,1,0:T(8,128)(2,1)S(1)}, u32[]{:S(2)}, u32[]{:S(2)}) %collective-permute-start.2) | collective-permute-done | bytes 524320 | tf_op jit(solution)/shard_map/ppermute | solution.py:631
  32.4 0.1 broadcast_select_fusion
  32.5 3.8 %collective-permute-start.3 = (bf16[2,2,512,128]{3,2,1,0:T(8,128)(2,1)S(1)}, bf16[2,2,512,128]{3,2,1,0:T(8,128)(2,1)S(1)}, u32[]{:S(2)}, u32[]{:S(2)}) collective-permute-start(bf16[2,2,512,128]{3,2,1,0:T(8,128)(2,1)S(1)} %broadcast_select_fusion), channel_id=1, source_target_pairs={{0,4},{2,6},{4,8},{6,10},{8,12},{10,14},{1,5},{3,7},{5,9},{7,11},{... | collective-permute-start | bytes 1572872 | tf_op jit(solution)/shard_map/ppermute | solution.py:635
  36.2 3.8 %filterbank_early.2 = (bf16[2,16,2,16,128]{4,3,2,1,0:T(8,128)(2,1)S(1)}, bf16[2,16,2,16,128]{4,3,2,1,0:T(8,128)(2,1)S(1)}, bf16[2,16,2,16,128]{4,3,2,1,0:T(8,128)(2,1)S(1)}, bf16[2,16,2,16,128]{4,3,2,1,0:T(8,128)(2,1)S(1)}) custom-call(s32[8]{0:T(128)S(1)} %copy-done.7, bf16[2,2,512,128]{3,2,1,0:T(8,128)(2,1)S(1)} %collective-permute-done.1.refs_1_, ...), custom_call_target="tpu_custom_call" | custom-call | flops 1000000 | bytes 262144 | tf_op jit(solution)/shard_map/filterbank_early/pallas_call | solution.py:303
  40.0 1.6 %collective-permute-start.4 = (bf16[2,16,2,16,128]{4,3,2,1,0:T(8,128)(2,1)S(1)}, bf16[2,16,2,16,128]{4,3,2,1,0:T(8,128)(2,1)S(1)}, u32[]{:S(2)}, u32[]{:S(2)}) collective-permute-start(bf16[2,16,2,16,128]{4,3,2,1,0:T(8,128)(2,1)S(1)} %get-tuple-element.76), channel_id=1, source_target_pairs={{0,1},{1,0},{2,3},{3,2},{4,5},{5,4},{6,7},{7,6},{8,9},{9,8},{10,11... | collective-permute-start | bytes 786440 | tf_op jit(solution)/shard_map/ppermute | solution.py:655
  41.6 2.5 %collective-permute-start.5 = (bf16[2,16,2,16,128]{4,3,2,1,0:T(8,128)(2,1)S(1)}, bf16[2,16,2,16,128]{4,3,2,1,0:T(8,128)(2,1)S(1)}, u32[]{:S(2)}, u32[]{:S(2)}) collective-permute-start(bf16[2,16,2,16,128]{4,3,2,1,0:T(8,128)(2,1)S(1)} %get-tuple-element.78), channel_id=1, source_target_pairs={{0,2},{1,3},{2,0},{3,1},{4,6},{5,7},{6,4},{7,5},{8,10},{9,11},{10,... | collective-permute-start | bytes 786440 | tf_op jit(solution)/shard_map/ppermute | solution.py:655
  44.1 3.7 %filterbank_late.3 = (bf16[2,8,2,16,128]{4,3,2,1,0:T(8,128)(2,1)S(1)}, bf16[2,8,2,16,128]{4,3,2,1,0:T(8,128)(2,1)S(1)}, bf16[2,8,2,16,128]{4,3,2,1,0:T(8,128)(2,1)S(1)}, bf16[2,8,2,16,128]{4,3,2,1,0:T(8,128)(2,1)S(1)}) custom-call(s32[8]{0:T(128)S(1)} %copy-done.7, bf16[2,2,512,128]{3,2,1,0:T(8,128)(2,1)S(1)} %copy-done.1, ...), custom_call_target="tpu_custom_call" | custom-call | flops 1000000 | bytes 262144 | tf_op jit(solution)/shard_map/filterbank_late/pallas_call | solution.py:303
  47.9 0.0 collective-permute-done.3.refs_1_
  47.9 4.0 %filterbank_early.3 = (bf16[2,16,2,16,128]{4,3,2,1,0:T(8,128)(2,1)S(1)}, bf16[2,16,2,16,128]{4,3,2,1,0:T(8,128)(2,1)S(1)}, bf16[2,16,2,16,128]{4,3,2,1,0:T(8,128)(2,1)S(1)}, bf16[2,16,2,16,128]{4,3,2,1,0:T(8,128)(2,1)S(1)}) custom-call(s32[8]{0:T(128)S(1)} %copy-done.7, bf16[2,2,512,128]{3,2,1,0:T(8,128)(2,1)S(1)} %collective-permute-done.3.refs_1_, ...), custom_call_target="tpu_custom_call" | custom-call | flops 1000000 | bytes 262144 | tf_op jit(solution)/shard_map/filterbank_early/pallas_call | solution.py:303
  51.9 0.0 collective-permute-done.4.refs_1_
  51.9 1.9 %collective-permute-done.6.refs_3_ = bf16[2,16,2,16,128]{4,3,2,1,0:T(8,128)(2,1)S(1)} collective-permute-done((bf16[2,16,2,16,128]{4,3,2,1,0:T(8,128)(2,1)S(1)}, bf16[2,16,2,16,128]{4,3,2,1,0:T(8,128)(2,1)S(1)}, u32[]{:S(2)}, u32[]{:S(2)}) %collective-permute-start.6) | collective-permute-done | bytes 262176 | tf_op jit(solution)/shard_map/ppermute | solution.py:655
  53.8 0.2 join.2.refs_0_
  54.0 0.1 collective-permute-start.7
  54.1 1.6 %collective-permute-start.10 = (bf16[2,16,2,16,128]{4,3,2,1,0:T(8,128)(2,1)S(1)}, bf16[2,16,2,16,128]{4,3,2,1,0:T(8,128)(2,1)S(1)}, u32[]{:S(2)}, u32[]{:S(2)}) collective-permute-start(bf16[2,16,2,16,128]{4,3,2,1,0:T(8,128)(2,1)S(1)} %get-tuple-element.86), channel_id=1, source_target_pairs={{0,1},{1,0},{2,3},{3,2},{4,5},{5,4},{6,7},{7,6},{8,9},{9,8},{10,11... | collective-permute-start | bytes 786440 | tf_op jit(solution)/shard_map/ppermute | solution.py:655
  55.7 1.5 %collective-permute-start.11 = (bf16[2,16,2,16,128]{4,3,2,1,0:T(8,128)(2,1)S(1)}, bf16[2,16,2,16,128]{4,3,2,1,0:T(8,128)(2,1)S(1)}, u32[]{:S(2)}, u32[]{:S(2)}) collective-permute-start(bf16[2,16,2,16,128]{4,3,2,1,0:T(8,128)(2,1)S(1)} %get-tuple-element.89), channel_id=1, source_target_pairs={{0,2},{1,3},{2,0},{3,1},{4,6},{5,7},{6,4},{7,5},{8,10},{9,11},{10,... | collective-permute-start | bytes 786440 | tf_op jit(solution)/shard_map/ppermute | solution.py:655
  57.1 0.5 collective-permute-start.12
  57.6 4.0 %correlate_early.1 = (f32[272,128]{1,0:T(8,128)S(1)}, bf16[272,128]{1,0:T(8,128)(2,1)S(1)}, bf16[272,128]{1,0:T(8,128)(2,1)S(1)}, bf16[272,128]{1,0:T(8,128)(2,1)S(1)}) custom-call(bf16[8,16,2,16,128]{4,3,2,1,0:T(8,128)(2,1)S(1)} %join.2.refs_0_, bf16[8,16,2,16,128]{4,3,2,1,0:T(8,128)(2,1)S(1)} %collective-permute-done.7.refs_1_.refs_2_), custom_call_target="tpu_custom_call" | custom-call | flops 1000000 | bytes 262144 | tf_op jit(solution)/shard_map/correlate_early/pallas_call | solution.py:470
  61.6 1.6 %collective-permute-start.8 = (bf16[272,128]{1,0:T(8,128)(2,1)S(1)}, bf16[272,128]{1,0:T(8,128)(2,1)S(1)}, u32[]{:S(2)}, u32[]{:S(2)}) collective-permute-start(bf16[272,128]{1,0:T(8,128)(2,1)S(1)} %get-tuple-element.82), channel_id=1, source_target_pairs={{0,4},{2,6},{4,8},{6,10},{8,12},{10,14},{12,0},{14,2},{1,5},{3,7},... | collective-permute-start | bytes 208904 | tf_op jit(solution)/shard_map/ppermute | solution.py:663
  63.2 1.6 %collective-permute-start.9 = (bf16[272,128]{1,0:T(8,128)(2,1)S(1)}, bf16[272,128]{1,0:T(8,128)(2,1)S(1)}, u32[]{:S(2)}, u32[]{:S(2)}) collective-permute-start(bf16[272,128]{1,0:T(8,128)(2,1)S(1)} %get-tuple-element.83), channel_id=1, source_target_pairs={{0,8},{2,10},{4,12},{6,14},{8,0},{10,2},{12,4},{14,6},{1,9},{3,11}... | collective-permute-start | bytes 208904 | tf_op jit(solution)/shard_map/ppermute | solution.py:663
  64.8 3.7 %collective-permute-done.8.refs_5_ = bf16[272,128]{1,0:T(8,128)(2,1)S(1)} collective-permute-done((bf16[272,128]{1,0:T(8,128)(2,1)S(1)}, bf16[272,128]{1,0:T(8,128)(2,1)S(1)}, u32[]{:S(2)}, u32[]{:S(2)}) %collective-permute-start.8) | collective-permute-done | bytes 69664 | tf_op jit(solution)/shard_map/ppermute | solution.py:663
  68.5 1.4 %collective-permute-done.9.refs_6_ = bf16[272,128]{1,0:T(8,128)(2,1)S(1)} collective-permute-done((bf16[272,128]{1,0:T(8,128)(2,1)S(1)}, bf16[272,128]{1,0:T(8,128)(2,1)S(1)}, u32[]{:S(2)}, u32[]{:S(2)}) %collective-permute-start.9) | collective-permute-done | bytes 69664 | tf_op jit(solution)/shard_map/ppermute | solution.py:663
  70.0 0.2 join.3.refs_1_
  70.2 0.1 collective-permute-start.13
  70.3 2.5 %collective-permute-start.14 = (bf16[272,128]{1,0:T(8,128)(2,1)S(1)}, bf16[272,128]{1,0:T(8,128)(2,1)S(1)}, u32[]{:S(2)}, u32[]{:S(2)}) collective-permute-start(bf16[272,128]{1,0:T(8,128)(2,1)S(1)} %get-tuple-element.95), channel_id=1, source_target_pairs={{0,12},{2,14},{4,0},{6,2},{8,4},{10,6},{12,8},{14,10},{1,13},{3,15... | collective-permute-start | bytes 208904 | tf_op jit(solution)/shard_map/ppermute | solution.py:663
  72.7 5.4 %correlate_own.1 = (f32[400,128]{1,0:T(8,128)S(1)}, bf16[400,128]{1,0:T(8,128)(2,1)S(1)}, bf16[400,128]{1,0:T(8,128)(2,1)S(1)}, bf16[400,128]{1,0:T(8,128)(2,1)S(1)}) custom-call(bf16[8,16,2,16,128]{4,3,2,1,0:T(8,128)(2,1)S(1)} %join.2.refs_0_, bf16[8,16,2,16,128]{4,3,2,1,0:T(8,128)(2,1)S(1)} %join.3.refs_1_), custom_call_target="tpu_custom_call" | custom-call | flops 1000000 | bytes 262144 | tf_op jit(solution)/shard_map/correlate_own/pallas_call | solution.py:470
  78.2 0.1 collective-permute-start.15
  78.3 1.8 %collective-permute-start.16 = (bf16[400,128]{1,0:T(8,128)(2,1)S(1)}, bf16[400,128]{1,0:T(8,128)(2,1)S(1)}, u32[]{:S(2)}, u32[]{:S(2)}) collective-permute-start(bf16[400,128]{1,0:T(8,128)(2,1)S(1)} %get-tuple-element.101), channel_id=1, source_target_pairs={{0,8},{2,10},{4,12},{6,14},{8,0},{10,2},{12,4},{14,6},{1,9},{3,11}... | collective-permute-start | bytes 307208 | tf_op jit(solution)/shard_map/ppermute | solution.py:663
  80.1 2.0 %collective-permute-start.17 = (bf16[400,128]{1,0:T(8,128)(2,1)S(1)}, bf16[400,128]{1,0:T(8,128)(2,1)S(1)}, u32[]{:S(2)}, u32[]{:S(2)}) collective-permute-start(bf16[400,128]{1,0:T(8,128)(2,1)S(1)} %get-tuple-element.103), channel_id=1, source_target_pairs={{0,12},{2,14},{4,0},{6,2},{8,4},{10,6},{12,8},{14,10},{1,13},{3,15... | collective-permute-start | bytes 307208 | tf_op jit(solution)/shard_map/ppermute | solution.py:663
  82.1 5.6 %correlate_cross.1 = (f32[384,128]{1,0:T(8,128)S(1)}, bf16[384,128]{1,0:T(8,128)(2,1)S(1)}, bf16[384,128]{1,0:T(8,128)(2,1)S(1)}, bf16[384,128]{1,0:T(8,128)(2,1)S(1)}, f32[272,128]{1,0:T(8,128)S(1)}) custom-call(bf16[8,16,2,16,128]{4,3,2,1,0:T(8,128)(2,1)S(1)} %join.2.refs_0_, bf16[8,16,2,16,128]{4,3,2,1,0:T(8,128)(2,1)S(1)} %join.3.refs_1_, ...), custom_call_target="tpu_custom_call" | custom-call | flops 1000000 | bytes 262144 | tf_op jit(solution)/shard_map/correlate_cross/pallas_call | solution.py:470
  87.7 0.1 collective-permute-start.22
  87.8 0.6 collective-permute-start.18
  88.4 0.9 collective-permute-done.16.refs_3_
  89.3 0.6 collective-permute-start.19
  90.0 2.8 %collective-permute-start.20 = (bf16[384,128]{1,0:T(8,128)(2,1)S(1)}, bf16[384,128]{1,0:T(8,128)(2,1)S(1)}, u32[]{:S(2)}, u32[]{:S(2)}) collective-permute-start(bf16[384,128]{1,0:T(8,128)(2,1)S(1)} %get-tuple-element.110), channel_id=1, source_target_pairs={{0,12},{2,14},{4,0},{6,2},{8,4},{10,6},{12,8},{14,10},{1,13},{3,15... | collective-permute-start | bytes 294920 | tf_op jit(solution)/shard_map/ppermute | solution.py:663
  92.8 2.5 %collective-permute-done.18.refs_6_ = bf16[384,128]{1,0:T(8,128)(2,1)S(1)} collective-permute-done((bf16[384,128]{1,0:T(8,128)(2,1)S(1)}, bf16[384,128]{1,0:T(8,128)(2,1)S(1)}, u32[]{:S(2)}, u32[]{:S(2)}) %collective-permute-start.18) | collective-permute-done | bytes 98336 | tf_op jit(solution)/shard_map/ppermute | solution.py:663
  95.4 3.8 %collective-permute-done.19.refs_7_ = bf16[384,128]{1,0:T(8,128)(2,1)S(1)} collective-permute-done((bf16[384,128]{1,0:T(8,128)(2,1)S(1)}, bf16[384,128]{1,0:T(8,128)(2,1)S(1)}, u32[]{:S(2)}, u32[]{:S(2)}) %collective-permute-start.19) | collective-permute-done | bytes 98336 | tf_op jit(solution)/shard_map/ppermute | solution.py:663
  99.2 0.5 collective-permute-start.25
  99.7 0.8 collective-permute-done.24.refs_12_
  100.5 0.2 collective-permute-done.25.refs_13_
  100.6 1.7 %assemble.1 = f32[2,16,32,256]{3,2,1,0:T(8,128)} custom-call(f32[272,128]{1,0:T(8,128)S(1)} %get-tuple-element.96.refs_0_, f32[400,128]{1,0:T(8,128)S(1)} %get-tuple-element.97.refs_1_, bf16[400,128]{1,0:T(8,128)(2,1)S(1)} %collective-permute-done.15.refs_2_, bf16[400,128]{1,0:T(8,128)(2,1)S(1)} %collective-permute-done.16.refs_3_, ...), custom_call_target="tpu_custom_call" | custom-call | flops 1000000 | bytes 262144 | tf_op jit(solution)/shard_map/assemble/pallas_call | solution.py:577
  (33 shorter events, 0.1 us)
Async XLA Ops:
  0.0 26.1 %copy-start = (f32[16,64,128]{2,1,0:T(8,128)S(1)}, f32[16,64,128]{2,1,0:T(8,128)}, u32[]{:S(2)}) copy-start(f32[16,64,128]{2,1,0:T(8,128)} %constant.30.clone.refs_3_.refs_4_) | copy-start | bytes 1572868
  0.0 26.2 %copy-start.4 = (bf16[128,128]{1,0:T(8,128)(2,1)S(1)}, bf16[128,128]{1,0:T(8,128)(2,1)}, u32[]{:S(2)}) copy-start(bf16[128,128]{1,0:T(8,128)(2,1)} %constant.31.clone.refs_4_.refs_5_) | copy-start | bytes 98308
  0.0 26.2 %copy-start.5 = (f32[64,128]{1,0:T(8,128)S(1)}, f32[64,128]{1,0:T(8,128)}, u32[]{:S(2)}) copy-start(f32[64,128]{1,0:T(8,128)} %constant.32.clone.refs_5_.refs_6_) | copy-start | bytes 98308
  0.0 26.2 %copy-start.6 = (f32[64,128]{1,0:T(8,128)S(1)}, f32[64,128]{1,0:T(8,128)}, u32[]{:S(2)}) copy-start(f32[64,128]{1,0:T(8,128)} %constant.33.clone.refs_6_.refs_7_) | copy-start | bytes 98308
  0.0 26.2 %copy-start.3 = (bf16[2,4,32,128]{3,2,1,0:T(8,128)(2,1)S(1)}, bf16[2,4,32,128]{3,2,1,0:T(8,128)(2,1)}, u32[]{:S(2)}) copy-start(bf16[2,4,32,128]{3,2,1,0:T(8,128)(2,1)} %constant.34.clone.refs_7_.refs_8_) | copy-start | bytes 196612
  0.0 26.2 %copy-start.7 = (s32[8]{0:T(128)S(1)}, s32[8]{0:T(128)}, u32[]{:S(2)}) copy-start(s32[8]{0:T(128)} %refs_0_.7) | copy-start | bytes 100
  6.0 26.4 %copy-start.1 = (bf16[2,2,512,128]{3,2,1,0:T(8,128)(2,1)S(1)}, bf16[2,2,512,128]{3,2,1,0:T(8,128)(2,1)}, u32[]{:S(2)}) copy-start(bf16[2,2,512,128]{3,2,1,0:T(8,128)(2,1)} %get-tuple-element.67.refs_1_.refs_2_) | copy-start | bytes 1572868
  6.0 15.9 %collective-permute-start = (bf16[2,2,512,128]{3,2,1,0:T(8,128)(2,1)}, bf16[2,2,512,128]{3,2,1,0:T(8,128)(2,1)S(1)}, u32[]{:S(2)}, u32[]{:S(2)}) collective-permute-start(bf16[2,2,512,128]{3,2,1,0:T(8,128)(2,1)} %get-tuple-element.59), channel_id=1, source_target_pairs={{0,2},{2,0},{4,6},{6,4},{8,10},{10,8},{12,14},{14,12},{1,3},{3,1},... | collective-permute-start | bytes 1572872 | tf_op jit(solution)/shard_map/ppermute | solution.py:631
  9.0 23.4 %collective-permute-start.2 = (bf16[2,2,512,128]{3,2,1,0:T(8,128)(2,1)}, bf16[2,2,512,128]{3,2,1,0:T(8,128)(2,1)S(1)}, u32[]{:S(2)}, u32[]{:S(2)}) collective-permute-start(bf16[2,2,512,128]{3,2,1,0:T(8,128)(2,1)} %get-tuple-element.60), channel_id=1, source_target_pairs={{0,2},{2,0},{4,6},{6,4},{8,10},{10,8},{12,14},{14,12},{1,3},{3,1},... | collective-permute-start | bytes 1572872 | tf_op jit(solution)/shard_map/ppermute | solution.py:631
  22.1 14.2 %collective-permute-start.1 = (bf16[2,2,512,128]{3,2,1,0:T(8,128)(2,1)S(1)}, bf16[2,2,512,128]{3,2,1,0:T(8,128)(2,1)S(1)}, u32[]{:S(2)}, u32[]{:S(2)}) collective-permute-start(bf16[2,2,512,128]{3,2,1,0:T(8,128)(2,1)S(1)} %broadcast_select_fusion.1), channel_id=1, source_target_pairs={{0,4},{2,6},{4,8},{6,10},{8,12},{10,14},{1,5},{3,7},{5,9},{7,11},{... | collective-permute-start | bytes 1572872 | tf_op jit(solution)/shard_map/ppermute | solution.py:635
  26.2 1.0 %copy-start.2 = (bf16[2,2,512,128]{3,2,1,0:T(8,128)(2,1)S(1)}, bf16[2,2,512,128]{3,2,1,0:T(8,128)(2,1)}, u32[]{:S(2)}) copy-start(bf16[2,2,512,128]{3,2,1,0:T(8,128)(2,1)} %get-tuple-element.58.refs_1_.refs_2_) | copy-start | bytes 1572868
  32.5 15.4 %collective-permute-start.3 = (bf16[2,2,512,128]{3,2,1,0:T(8,128)(2,1)S(1)}, bf16[2,2,512,128]{3,2,1,0:T(8,128)(2,1)S(1)}, u32[]{:S(2)}, u32[]{:S(2)}) collective-permute-start(bf16[2,2,512,128]{3,2,1,0:T(8,128)(2,1)S(1)} %broadcast_select_fusion), channel_id=1, source_target_pairs={{0,4},{2,6},{4,8},{6,10},{8,12},{10,14},{1,5},{3,7},{5,9},{7,11},{... | collective-permute-start | bytes 1572872 | tf_op jit(solution)/shard_map/ppermute | solution.py:635
  40.0 11.8 %collective-permute-start.4 = (bf16[2,16,2,16,128]{4,3,2,1,0:T(8,128)(2,1)S(1)}, bf16[2,16,2,16,128]{4,3,2,1,0:T(8,128)(2,1)S(1)}, u32[]{:S(2)}, u32[]{:S(2)}) collective-permute-start(bf16[2,16,2,16,128]{4,3,2,1,0:T(8,128)(2,1)S(1)} %get-tuple-element.76), channel_id=1, source_target_pairs={{0,1},{1,0},{2,3},{3,2},{4,5},{5,4},{6,7},{7,6},{8,9},{9,8},{10,11... | collective-permute-start | bytes 786440 | tf_op jit(solution)/shard_map/ppermute | solution.py:655
  41.6 10.3 %collective-permute-start.5 = (bf16[2,16,2,16,128]{4,3,2,1,0:T(8,128)(2,1)S(1)}, bf16[2,16,2,16,128]{4,3,2,1,0:T(8,128)(2,1)S(1)}, u32[]{:S(2)}, u32[]{:S(2)}) collective-permute-start(bf16[2,16,2,16,128]{4,3,2,1,0:T(8,128)(2,1)S(1)} %get-tuple-element.78), channel_id=1, source_target_pairs={{0,2},{1,3},{2,0},{3,1},{4,6},{5,7},{6,4},{7,5},{8,10},{9,11},{10,... | collective-permute-start | bytes 786440 | tf_op jit(solution)/shard_map/ppermute | solution.py:655
  44.1 9.7 %collective-permute-start.6 = (bf16[2,16,2,16,128]{4,3,2,1,0:T(8,128)(2,1)S(1)}, bf16[2,16,2,16,128]{4,3,2,1,0:T(8,128)(2,1)S(1)}, u32[]{:S(2)}, u32[]{:S(2)}) collective-permute-start(bf16[2,16,2,16,128]{4,3,2,1,0:T(8,128)(2,1)S(1)} %get-tuple-element.80), channel_id=1, source_target_pairs={{0,3},{1,2},{2,1},{3,0},{4,7},{5,6},{6,5},{7,4},{8,11},{9,10},{10,... | collective-permute-start | bytes 786440 | tf_op jit(solution)/shard_map/ppermute | solution.py:655
  54.0 3.6 %collective-permute-start.7 = (bf16[8,16,2,16,128]{4,3,2,1,0:T(8,128)(2,1)S(1)}, bf16[8,16,2,16,128]{4,3,2,1,0:T(8,128)(2,1)S(1)}, u32[]{:S(2)}, u32[]{:S(2)}) collective-permute-start(bf16[8,16,2,16,128]{4,3,2,1,0:T(8,128)(2,1)S(1)} %join.2.refs_0_), channel_id=1, source_target_pairs={{0,16},{16,0},{1,17},{17,1},{2,18},{18,2},{3,19},{19,3},{4,20},{20... | collective-permute-start | bytes 3145736 | tf_op jit(solution)/shard_map/ppermute | solution.py:667
  54.1 15.9 %collective-permute-start.10 = (bf16[2,16,2,16,128]{4,3,2,1,0:T(8,128)(2,1)S(1)}, bf16[2,16,2,16,128]{4,3,2,1,0:T(8,128)(2,1)S(1)}, u32[]{:S(2)}, u32[]{:S(2)}) collective-permute-start(bf16[2,16,2,16,128]{4,3,2,1,0:T(8,128)(2,1)S(1)} %get-tuple-element.86), channel_id=1, source_target_pairs={{0,1},{1,0},{2,3},{3,2},{4,5},{5,4},{6,7},{7,6},{8,9},{9,8},{10,11... | collective-permute-start | bytes 786440 | tf_op jit(solution)/shard_map/ppermute | solution.py:655
  55.7 14.3 %collective-permute-start.11 = (bf16[2,16,2,16,128]{4,3,2,1,0:T(8,128)(2,1)S(1)}, bf16[2,16,2,16,128]{4,3,2,1,0:T(8,128)(2,1)S(1)}, u32[]{:S(2)}, u32[]{:S(2)}) collective-permute-start(bf16[2,16,2,16,128]{4,3,2,1,0:T(8,128)(2,1)S(1)} %get-tuple-element.89), channel_id=1, source_target_pairs={{0,2},{1,3},{2,0},{3,1},{4,6},{5,7},{6,4},{7,5},{8,10},{9,11},{10,... | collective-permute-start | bytes 786440 | tf_op jit(solution)/shard_map/ppermute | solution.py:655
  57.1 12.8 %collective-permute-start.12 = (bf16[2,16,2,16,128]{4,3,2,1,0:T(8,128)(2,1)S(1)}, bf16[2,16,2,16,128]{4,3,2,1,0:T(8,128)(2,1)S(1)}, u32[]{:S(2)}, u32[]{:S(2)}) collective-permute-start(bf16[2,16,2,16,128]{4,3,2,1,0:T(8,128)(2,1)S(1)} %get-tuple-element.92), channel_id=1, source_target_pairs={{0,3},{1,2},{2,1},{3,0},{4,7},{5,6},{6,5},{7,4},{8,11},{9,10},{10,... | collective-permute-start | bytes 786440 | tf_op jit(solution)/shard_map/ppermute | solution.py:655
  61.6 6.9 %collective-permute-start.8 = (bf16[272,128]{1,0:T(8,128)(2,1)S(1)}, bf16[272,128]{1,0:T(8,128)(2,1)S(1)}, u32[]{:S(2)}, u32[]{:S(2)}) collective-permute-start(bf16[272,128]{1,0:T(8,128)(2,1)S(1)} %get-tuple-element.82), channel_id=1, source_target_pairs={{0,4},{2,6},{4,8},{6,10},{8,12},{10,14},{12,0},{14,2},{1,5},{3,7},... | collective-permute-start | bytes 208904 | tf_op jit(solution)/shard_map/ppermute | solution.py:663
  63.2 6.7 %collective-permute-start.9 = (bf16[272,128]{1,0:T(8,128)(2,1)S(1)}, bf16[272,128]{1,0:T(8,128)(2,1)S(1)}, u32[]{:S(2)}, u32[]{:S(2)}) collective-permute-start(bf16[272,128]{1,0:T(8,128)(2,1)S(1)} %get-tuple-element.83), channel_id=1, source_target_pairs={{0,8},{2,10},{4,12},{6,14},{8,0},{10,2},{12,4},{14,6},{1,9},{3,11}... | collective-permute-start | bytes 208904 | tf_op jit(solution)/shard_map/ppermute | solution.py:663
  70.2 8.0 %collective-permute-start.13 = (bf16[8,16,2,16,128]{4,3,2,1,0:T(8,128)(2,1)S(1)}, bf16[8,16,2,16,128]{4,3,2,1,0:T(8,128)(2,1)S(1)}, u32[]{:S(2)}, u32[]{:S(2)}) collective-permute-start(bf16[8,16,2,16,128]{4,3,2,1,0:T(8,128)(2,1)S(1)} %join.3.refs_1_), channel_id=1, source_target_pairs={{0,16},{16,0},{1,17},{17,1},{2,18},{18,2},{3,19},{19,3},{4,20},{20... | collective-permute-start | bytes 3145736 | tf_op jit(solution)/shard_map/ppermute | solution.py:673
  70.3 9.8 %collective-permute-start.14 = (bf16[272,128]{1,0:T(8,128)(2,1)S(1)}, bf16[272,128]{1,0:T(8,128)(2,1)S(1)}, u32[]{:S(2)}, u32[]{:S(2)}) collective-permute-start(bf16[272,128]{1,0:T(8,128)(2,1)S(1)} %get-tuple-element.95), channel_id=1, source_target_pairs={{0,12},{2,14},{4,0},{6,2},{8,4},{10,6},{12,8},{14,10},{1,13},{3,15... | collective-permute-start | bytes 208904 | tf_op jit(solution)/shard_map/ppermute | solution.py:663
  78.2 9.6 %collective-permute-start.15 = (bf16[400,128]{1,0:T(8,128)(2,1)S(1)}, bf16[400,128]{1,0:T(8,128)(2,1)S(1)}, u32[]{:S(2)}, u32[]{:S(2)}) collective-permute-start(bf16[400,128]{1,0:T(8,128)(2,1)S(1)} %get-tuple-element.99), channel_id=1, source_target_pairs={{0,4},{2,6},{4,8},{6,10},{8,12},{10,14},{12,0},{14,2},{1,5},{3,7},... | collective-permute-start | bytes 307208 | tf_op jit(solution)/shard_map/ppermute | solution.py:663
  78.3 11.1 %collective-permute-start.16 = (bf16[400,128]{1,0:T(8,128)(2,1)S(1)}, bf16[400,128]{1,0:T(8,128)(2,1)S(1)}, u32[]{:S(2)}, u32[]{:S(2)}) collective-permute-start(bf16[400,128]{1,0:T(8,128)(2,1)S(1)} %get-tuple-element.101), channel_id=1, source_target_pairs={{0,8},{2,10},{4,12},{6,14},{8,0},{10,2},{12,4},{14,6},{1,9},{3,11}... | collective-permute-start | bytes 307208 | tf_op jit(solution)/shard_map/ppermute | solution.py:663
  80.1 9.9 %collective-permute-start.17 = (bf16[400,128]{1,0:T(8,128)(2,1)S(1)}, bf16[400,128]{1,0:T(8,128)(2,1)S(1)}, u32[]{:S(2)}, u32[]{:S(2)}) collective-permute-start(bf16[400,128]{1,0:T(8,128)(2,1)S(1)} %get-tuple-element.103), channel_id=1, source_target_pairs={{0,12},{2,14},{4,0},{6,2},{8,4},{10,6},{12,8},{14,10},{1,13},{3,15... | collective-permute-start | bytes 307208 | tf_op jit(solution)/shard_map/ppermute | solution.py:663
  87.7 12.0 %collective-permute-start.22 = (f32[384,128]{1,0:T(8,128)S(1)}, f32[384,128]{1,0:T(8,128)S(1)}, u32[]{:S(2)}, u32[]{:S(2)}) collective-permute-start(f32[384,128]{1,0:T(8,128)S(1)} %get-tuple-element.104.refs_5_), channel_id=1, source_target_pairs={{0,16},{16,0},{1,17},{17,1},{2,18},{18,2},{3,19},{19,3},{4,20},{20... | collective-permute-start | bytes 589832 | tf_op jit(solution)/shard_map/ppermute | solution.py:682
  87.8 7.6 %collective-permute-start.18 = (bf16[384,128]{1,0:T(8,128)(2,1)S(1)}, bf16[384,128]{1,0:T(8,128)(2,1)S(1)}, u32[]{:S(2)}, u32[]{:S(2)}) collective-permute-start(bf16[384,128]{1,0:T(8,128)(2,1)S(1)} %get-tuple-element.106), channel_id=1, source_target_pairs={{0,4},{2,6},{4,8},{6,10},{8,12},{10,14},{12,0},{14,2},{1,5},{3,7},... | collective-permute-start | bytes 294920 | tf_op jit(solution)/shard_map/ppermute | solution.py:663
  89.3 9.8 %collective-permute-start.19 = (bf16[384,128]{1,0:T(8,128)(2,1)S(1)}, bf16[384,128]{1,0:T(8,128)(2,1)S(1)}, u32[]{:S(2)}, u32[]{:S(2)}) collective-permute-start(bf16[384,128]{1,0:T(8,128)(2,1)S(1)} %get-tuple-element.108), channel_id=1, source_target_pairs={{0,8},{2,10},{4,12},{6,14},{8,0},{10,2},{12,4},{14,6},{1,9},{3,11}... | collective-permute-start | bytes 294920 | tf_op jit(solution)/shard_map/ppermute | solution.py:663
  90.0 9.2 %collective-permute-start.20 = (bf16[384,128]{1,0:T(8,128)(2,1)S(1)}, bf16[384,128]{1,0:T(8,128)(2,1)S(1)}, u32[]{:S(2)}, u32[]{:S(2)}) collective-permute-start(bf16[384,128]{1,0:T(8,128)(2,1)S(1)} %get-tuple-element.110), channel_id=1, source_target_pairs={{0,12},{2,14},{4,0},{6,2},{8,4},{10,6},{12,8},{14,10},{1,13},{3,15... | collective-permute-start | bytes 294920 | tf_op jit(solution)/shard_map/ppermute | solution.py:663
  92.8 6.9 %collective-permute-start.21 = (f32[272,128]{1,0:T(8,128)S(1)}, f32[272,128]{1,0:T(8,128)S(1)}, u32[]{:S(2)}, u32[]{:S(2)}) collective-permute-start(f32[272,128]{1,0:T(8,128)S(1)} %get-tuple-element.96.refs_0_), channel_id=1, source_target_pairs={{0,16},{16,0},{1,17},{17,1},{2,18},{18,2},{3,19},{19,3},{4,20},{20... | collective-permute-start | bytes 417800 | tf_op jit(solution)/shard_map/ppermute | solution.py:682
  95.4 4.3 %collective-permute-start.23 = (bf16[384,128]{1,0:T(8,128)(2,1)S(1)}, bf16[384,128]{1,0:T(8,128)(2,1)S(1)}, u32[]{:S(2)}, u32[]{:S(2)}) collective-permute-start(bf16[384,128]{1,0:T(8,128)(2,1)S(1)} %collective-permute-done.18.refs_6_), channel_id=1, source_target_pairs={{0,16},{16,0},{1,17},{17,1},{2,18},{18,2},{3,19},{19,3},{4,20},{20... | collective-permute-start | bytes 294920 | tf_op jit(solution)/shard_map/ppermute | solution.py:682
  99.2 1.3 %collective-permute-start.24 = (bf16[384,128]{1,0:T(8,128)(2,1)S(1)}, bf16[384,128]{1,0:T(8,128)(2,1)S(1)}, u32[]{:S(2)}, u32[]{:S(2)}) collective-permute-start(bf16[384,128]{1,0:T(8,128)(2,1)S(1)} %collective-permute-done.19.refs_7_), channel_id=1, source_target_pairs={{0,16},{16,0},{1,17},{17,1},{2,18},{18,2},{3,19},{19,3},{4,20},{20... | collective-permute-start | bytes 294920 | tf_op jit(solution)/shard_map/ppermute | solution.py:682
  99.2 1.5 %collective-permute-start.25 = (bf16[384,128]{1,0:T(8,128)(2,1)S(1)}, bf16[384,128]{1,0:T(8,128)(2,1)S(1)}, u32[]{:S(2)}, u32[]{:S(2)}) collective-permute-start(bf16[384,128]{1,0:T(8,128)(2,1)S(1)} %collective-permute-done.20.refs_8_), channel_id=1, source_target_pairs={{0,16},{16,0},{1,17},{17,1},{2,18},{18,2},{3,19},{19,3},{4,20},{20... | collective-permute-start | bytes 294920 | tf_op jit(solution)/shard_map/ppermute | solution.py:682

commit v11 on v10

--- a/solution.py
+++ b/solution.py
@@ -83,40 +83,48 @@
     return np.concatenate([cosine, cosine], axis=1), np.concatenate([sine, sine], axis=1)
 
 
-def pick_kernel(half, block, *refs):
+def pick_kernel(half, own, block, *refs):
     outs, rows = refs[:-1], refs[-1]
     inputs, samples = block.shape[1], block.shape[2]
-    tall = samples // LANES
-    step = 16
+    step = 32
     for part in range(2):
-        for n in range(tall // step):
-            cut = slice(n * step * LANES, (n + 1) * step * LANES)
-            wide = block[part, :, cut].astype(jnp.float32)
+
+        def spread(n, carry, part=part):
+            low = pl.multiple_of(n * step * LANES, step * LANES)
+            wide = block[part, :, pl.ds(low, step * LANES)].astype(jnp.float32)
             for u in range(step):
-                at = (n * step + u) * inputs
-                rows[part, at : at + inputs, :] = wide[:, u * LANES : (u + 1) * LANES]
+                at = pl.multiple_of((n * step + u) * inputs, inputs)
+                rows[part, pl.ds(at, inputs), :] = wide[:, u * LANES : (u + 1) * LANES]
+            return carry
+
+        lax.fori_loop(0, samples // LANES // step, spread, 0)
     g = position()[2]
-    for item in range(inputs):
-        first = (1 - g) * half + item if item < half else g * half + item - half
-        for part in range(2):
-            value = rows[part, pl.ds(first, tall, stride=inputs), :]
-            outs[item // JOIN][item % JOIN, part] = value.astype(jnp.bfloat16)
-
-
-def pick(block):
+    first = (g if own else 1 - g) * half
+    tall = 64
+
+    def gather(n, carry):
+        low = pl.multiple_of(n * tall, tall)
+        for item in range(half):
+            for part in range(2):
+                at = low * inputs + first + item
+                value = rows[part, pl.ds(at, tall, stride=inputs), :].astype(jnp.bfloat16)
+                outs[item // JOIN][item % JOIN, part, pl.ds(low, tall), :] = value
+        return carry
+
+    lax.fori_loop(0, samples // LANES // tall, gather, 0)
+
+
+def pick(block, own):
     _, inputs, samples = block.shape
     half = inputs // PAIR
-    steps = 8
-    tall = samples // LANES // steps
     shape = jax.ShapeDtypeStruct((JOIN, 2, samples // LANES, LANES), jnp.bfloat16)
     return pl.pallas_call(
-        functools.partial(pick_kernel, half),
-        grid=(steps,),
-        out_shape=[shape] * (inputs // JOIN),
-        in_specs=[pl.BlockSpec((2, inputs, samples // steps), lambda t: (0, 0, t))],
-        out_specs=[pl.BlockSpec((JOIN, 2, tall, LANES), lambda t: (0, 0, t, 0))] * (inputs // JOIN),
-        scratch_shapes=[pltpu.VMEM((2, tall * inputs, LANES), jnp.float32)],
-        compiler_params=params(56),
+        functools.partial(pick_kernel, half, own),
+        out_shape=[shape] * (half // JOIN),
+        in_specs=[VMEM],
+        out_specs=[VMEM] * (half // JOIN),
+        scratch_shapes=[pltpu.VMEM((2, samples // LANES * inputs, LANES), jnp.float32)],
+        compiler_params=params(12),
         cost_estimate=cost(10**6, 2**18),
         name="pick",
     )(block)
@@ -155,7 +163,7 @@
 SOME = 4
 
 
-def filterbank_kernel(late, part, frames, dests, per_ct, half_count, *refs):
+def filterbank_kernel(late, before, part, frames, dests, per_ct, half_count, *refs):
     delays, refs = refs[0], refs[1:]
     _, _, me, ct = position()
     if late:
@@ -165,7 +173,7 @@
         halo, keep, recv = refs[:3]
         refs = refs[3:]
     coef, first, tw_cos, tw_sin, last = refs[:5]
-    beside = () if late else refs[5 : 5 + dests]
+    beside = refs[5 : 5 + dests] if before else ()
     outs = refs[5 + len(beside) :][:dests]
     raw, weights, grouped = refs[5 + len(beside) + dests :][:3]
     filtered = refs[5 + len(beside) + dests + 3 :]
@@ -193,8 +201,8 @@
         bring(halo, 0)
         pl.when(me == 0)(lambda: bring(keep, 1))
         pl.when(me != 0)(lambda: bring(recv, 1))
-        for dest, block in zip(outs, beside):
-            dest[:, frames // 2 :] = block[...]
+    for dest, block in zip(outs, beside):
+        dest[:before] = block[...]
 
     downs, acrosses = [], []
     for item in range(JOIN):
@@ -269,7 +277,7 @@
             for c in range(2):
                 low = (dest * 2 + c) * size
                 for u in range(SOME // 2):
-                    outs[dest][item, base // 2 + u, c] = result[
+                    outs[dest][before + item, base // 2 + u, c] = result[
                         low : low + size, u * LANES : (u + 1) * LANES
                     ]
 
@@ -293,13 +301,15 @@
 
 
 def filterbank(part, half, delays, sources, tables, beside, dests):
-    late = not beside
+    late = len(sources) == 2
     frames = sources[0].shape[2] // ROWS
     size = tables[-1].shape[2] // 2
     per_ct = tables[-1].shape[1] // 2
-    pairs = frames // 2 if late else frames
-    shape = (JOIN, pairs, 2, size, LANES)
-    kernel = functools.partial(filterbank_kernel, late, part, frames, dests, per_ct, half)
+    before = beside[0].shape[0] if beside else 0
+    shape = (before + JOIN, frames // 2, 2, size, LANES)
+    kernel = functools.partial(
+        filterbank_kernel, late, before, part, frames, dests, per_ct, half
+    )
     return pl.pallas_call(
         kernel,
         out_shape=[jax.ShapeDtypeStruct(shape, jnp.bfloat16)] * dests,
@@ -321,21 +331,12 @@
 CORNER = [(p, q) for p in range(TILE) for q in range(p, TILE)]
 
 
-def pair_sets(own, parts):
+def pair_sets(own):
     tiles = own // TILE
-    per = tiles // parts
     whole = [(True, i, j, SQUARE) for i in range(tiles) for j in range(i + 1, tiles)]
     corner = [(True, i, i, CORNER) for i in range(tiles)]
     across = [(False, i, j, SQUARE) for i in range(0, tiles, 2) for j in range(tiles)]
-
-    def early(block):
-        return block[1] < per and block[2] < per
-
-    def late(blocks):
-        return [block for block in blocks if not early(block)]
-
-    first = [block for block in whole + across + corner if early(block)]
-    return [first, late(whole + corner), late(across)]
+    return [whole + corner, across]
 
 
 def pairs_in(blocks):
@@ -350,45 +351,43 @@
 
 
 def correlate_kernel(layout, *refs):
-    sources_at, blocks, own, terms, outer, span, per_ct = layout
+    sources_at, blocks, own, added, outer, span, per_ct = layout
     sources, rest = refs[: len(sources_at)], refs[len(sources_at) :]
-    earlier, outs, (spectra, sums, held) = rest[:terms], rest[terms:-3], rest[-3:]
+    if added is None:
+        outs, (spectra, held), sums = (), rest[-2:], rest[0]
+    else:
+        first_sums, outs, (spectra, held, sums) = rest[0], rest[1:-3], rest[-3:]
     steps = spectra.shape[1]
-    some = 8
     core, o, g, ct = position()
     within = any(block[0] for block in blocks)
     across = any(not block[0] for block in blocks)
 
-    for source, (far, part) in zip(sources, sources_at):
+    for source, (far, groups) in zip(sources, sources_at):
         for n in range(PAIR * per_ct):
             dg, dc = n // per_ct, n % per_ct
             device = lax.rem(ct - dc + per_ct, per_ct) * PAIR + (g ^ dg)
-            base = (part * per_ct * PAIR + device) * JOIN
-            wanted = None
-            if across:
-                side = 1 - core if far else core
-                wanted = (side == 1) | (lax.rem(base // TILE, 2) == core)
-                if within and not far:
-                    wanted = None
-                base = base + side * own
-
-            def bring(source=source, base=base, n=n):
-                for item in range(JOIN):
-
-                    def spread(m, carry, item=item):
-                        for u in range(some):
-                            real = source[n * JOIN + item, m * some + u, 0].astype(jnp.float32)
-                            imag = source[n * JOIN + item, m * some + u, 1].astype(jnp.float32)
+            for at, part in enumerate(groups):
+                base = (part * per_ct * PAIR + device) * JOIN
+                wanted = None
+                if across:
+                    side = 1 - core if far else core
+                    wanted = (side == 1) | (lax.rem(base // TILE, 2) == core)
+                    if within and not far:
+                        wanted = None
+                    base = base + side * own
+
+                def bring(source=source, base=base, first=(n * len(groups) + at) * JOIN):
+                    for item in range(JOIN):
+                        for m in range(steps):
+                            real = source[first + item, m, 0].astype(jnp.float32)
+                            imag = source[first + item, m, 1].astype(jnp.float32)
                             for which, value in enumerate((real, imag, real + imag, imag - real)):
-                                spectra[base + item, m * some + u, which] = value
-                        return carry
-
-                    lax.fori_loop(0, steps // some, spread, 0)
-
-            if wanted is None:
-                bring()
-            else:
-                pl.when(wanted)(bring)
+                                spectra[base + item, m, which] = value
+
+                if wanted is None:
+                    bring()
+                else:
+                    pl.when(wanted)(bring)
 
     high = lax.broadcasted_iota(jnp.int32, (1, LANES), 1) < RADIX
     rows_outer = pairs_in(blocks) * span
@@ -446,41 +445,43 @@
         lax.fori_loop(0, len(run), step, 0)
         done = end
 
-    for r in range(outer):
-        base = pl.multiple_of(lax.rem(o + r, outer) * rows_outer, 16)
-        outs[r][...] = sums[pl.ds(base, rows_outer), :].astype(outs[r].dtype)
-    if terms:
-        total = earlier[0][...].astype(jnp.float32)
-        for term in earlier[1:]:
-            total = total + term[...].astype(jnp.float32)
-        outs[outer][...] = total
-
-
-def correlate(arrays, sources_at, blocks, own, sizes, name, earlier=()):
+    for r in range(len(outs)):
+        owner = lax.rem(o + r, outer)
+        value = sums[pl.ds(pl.multiple_of(owner * rows_outer, 16), rows_outer), :]
+        stride = first_sums.shape[0] // outer
+        at = pl.multiple_of(owner * stride + added, 16)
+        value = value + first_sums[pl.ds(at, rows_outer), :]
+        outs[r][...] = value.astype(outs[r].dtype)
+
+
+def correlate(arrays, sources_at, blocks, own, sizes, name, first_sums=None, added=None):
     outer, span, _ = sizes
     _, steps, _, size, _ = arrays[0].shape
     inputs = own if all(block[0] for block in blocks) else 2 * own
     rows = pairs_in(blocks) * span
-    shapes = []
-    for r in range(outer):
-        dtype = jnp.float32 if r == 0 else jnp.bfloat16
-        shapes.append(jax.ShapeDtypeStruct((rows, LANES), dtype))
-    shapes += [jax.ShapeDtypeStruct(x.shape, jnp.float32) for x in earlier[:1]]
-    layout = (sources_at, blocks, own, len(earlier)) + sizes
+    total = (outer * rows, LANES)
+    scratch = [
+        pltpu.VMEM((inputs, steps, 4, size, LANES), jnp.float32),
+        pltpu.VMEM((2, TILE * TILE, outer * span, LANES), jnp.float32),
+    ]
+    if first_sums is None:
+        shapes = [jax.ShapeDtypeStruct(total, jnp.float32)]
+    else:
+        types = [jnp.float32] + [jnp.bfloat16] * (outer - 1)
+        shapes = [jax.ShapeDtypeStruct((rows, LANES), dtype) for dtype in types]
+        arrays = [*arrays, first_sums]
+        scratch.append(pltpu.VMEM(total, jnp.float32))
+    layout = (sources_at, blocks, own, added) + sizes
     return pl.pallas_call(
         functools.partial(correlate_kernel, layout),
         out_shape=shapes,
-        in_specs=[VMEM] * (len(arrays) + len(earlier)),
+        in_specs=[VMEM] * len(arrays),
         out_specs=[VMEM] * len(shapes),
-        scratch_shapes=[
-            pltpu.VMEM((inputs, steps, 4, size, LANES), jnp.float32),
-            pltpu.VMEM((outer * rows, LANES), jnp.float32),
-            pltpu.VMEM((2, TILE * TILE, outer * span, LANES), jnp.float32),
-        ],
-        compiler_params=params(8 + inputs * steps * 4 * size * LANES * 4 // 2**20),
+        scratch_shapes=scratch,
+        compiler_params=params(12 + inputs * steps * 4 * size * LANES * 4 // 2**20),
         cost_estimate=cost(10**6, 2**18),
         name=name,
-    )(*arrays, *earlier)
+    )(*arrays)
 
 
 def assemble_kernel(own, outer, span, scale, sets, order, counts, *refs):
@@ -571,7 +572,7 @@
 
 
 def assemble(near, far, sets, order, own, span, scale):
-    outer = len(near[1])
+    outer = len(near[0])
     counts = [len(arrays) for arrays in near + far]
     sources = [x for arrays in near + far for x in arrays]
     return pl.pallas_call(
@@ -601,7 +602,7 @@
         and own % (PAIR * JOIN * 2 * TILE // 4) == 0
         and in_count == PAIR * JOIN * 2
         and per_ct * PAIR * JOIN % (2 * TILE) == 0
-        and all(pairs_in(s) * span % 16 == 0 for s in pair_sets(own, 2))
+        and all(pairs_in(s) * span % 16 == 0 for s in pair_sets(own))
     )
 
 
@@ -626,23 +627,17 @@
     tables = [jnp.asarray(t) for t in tables + [np.concatenate([base, base], axis=1)]]
 
     parts = half // JOIN
-    picked = pick(voltages)
-    sends, keeps = picked[:parts], picked[parts:]
+    sends = pick(voltages, False)
+    keeps = pick(follow(voltages, sends[0]), True)
     recvs = [lax.ppermute(block, "tm", swap) for block in sends]
-    halos, lates = [], []
+    count = len(dests)
+    late, halos = [], []
     for c in range(parts):
-        recv = follow(recvs[c], lates[-1]) if lates else recvs[c]
+        late = filterbank(c, half, delays, [keeps[c], recvs[c]], tables, late, count)
+        recv = follow(recvs[c], [late[0], halos[-1]]) if c else recvs[c]
         halos.append(lax.ppermute(jnp.where(g == 1, keeps[c], recv), "tm", onward))
-        sources = [keeps[c], follow(recvs[c], halos[c - 1]) if c else recvs[c]]
-        lates.append(filterbank(c, half, delays, sources, tables, [], len(dests)))
-
-    sets = pair_sets(own, parts)
-    sizes = (outer, span, per_ct)
-    received = []
-    for c in range(parts):
-        halo = follow(halos[c], recvs[c + 1]) if c + 1 < parts else halos[c]
-        sources = [halo, keeps[c], recvs[c]]
-        spectra = filterbank(c, half, delays, sources, tables, lates[c], len(dests))
+
+    def sent(spectra, after):
         arrays = []
         for n, ((dg, dc), block) in enumerate(zip(dests, spectra)):
             route = []
@@ -651,10 +646,17 @@
                     target = (i ^ dg) * per_ct + (j + dc) % per_ct
                     route.append((i * per_ct + j, target))
             if dg or dc:
-                block = follow(block, received[-1][n]) if received else block
-                block = lax.ppermute(block, ("tm", "ct"), route)
+                block = lax.ppermute(follow(block, after[n]) if after else block, ("tm", "ct"), route)
             arrays.append(block)
-        received.append(arrays)
+        return arrays
+
+    received = [sent(late, [])]
+    spectra = []
+    for c in range(parts):
+        halo = follow(halos[c], late[0]) if c == 0 else halos[c]
+        sources = [halo, keeps[c], recvs[c]]
+        spectra = filterbank(c, half, delays, sources, tables, spectra, count)
+    received.append(sent(spectra, received[0]))
 
     def along(parts, after):
         moved = [parts[0]]
@@ -663,24 +665,23 @@
             moved.append(lax.ppermute(follow(parts[r], after(r)), "tm", route))
         return moved
 
-    near = [joined([follow(block, spectra[0]) for block in received[0]])]
-    far = [lax.ppermute(near[0], "stn", cores)]
-    early = correlate(
-        near + far, [(False, 0), (True, 0)], sets[0], own // parts, sizes, "correlate_early"
+    sets = pair_sets(own)
+    sizes = (outer, span, per_ct)
+    both = [(False, range(parts)), (True, range(parts))]
+    near = joined([follow(block, spectra[0]) for block in received[0]])
+    far = lax.ppermute(near, "stn", cores)
+    (first_sums,) = correlate([near, far], both, sets[0] + sets[1], own, sizes, "correlate_late")
+    near = joined([follow(block, first_sums) for block in received[1]])
+    far = lax.ppermute(near, "stn", cores)
+    inner = correlate([near], both[:1], sets[0], own, sizes, "correlate_own", first_sums, 0)
+    inner = along(inner, lambda r: far)
+    cross = correlate(
+        [near, far], both, sets[1], own, sizes, "correlate_cross", first_sums,
+        pairs_in(sets[0]) * span,
     )
-    early = along(early, lambda r: [])
-    near.append(joined([follow(block, early[1:3]) for block in received[1]]))
-    far.append(lax.ppermute(near[1], "stn", cores))
-    sources_at = [(False, c) for c in range(parts)] + [(True, c) for c in range(parts)]
-    own_late = correlate(near, sources_at[:parts], sets[1], own, sizes, "correlate_own")
-    own_late = along(own_late, lambda r: [far[1], early[r]])
-    *cross_late, early = correlate(
-        near + far, sources_at, sets[2], own, sizes, "correlate_cross", early
-    )
-    cross_late = along(cross_late, lambda r: own_late[r])
-    mine = [[early], own_late, cross_late]
-    theirs = [[lax.ppermute(block, "stn", cores) for block in part] for part in (mine[0], mine[2])]
-    theirs.insert(1, [])
+    cross = along(cross, lambda r: inner[r])
+    mine = [inner, cross]
+    theirs = [[], [lax.ppermute(block, "stn", cores) for block in cross]]
     order = []
     for part in range(parts):
         for device in range(per_ct * PAIR):

time: 103 us -> 107 us (1.039)
  waiting for transfers between devices: 29.6 us -> 31.9 us
    pallas_call x1 -> x2, Pallas kernels: 6.01 us -> 2.49 us  [pick(): pl.pallas_call(functools.partial(pick_kernel, half, own), out_shape=[shap...]
    ppermute x2, waiting for transfers between devices: 0.01 us -> 2.94 us  [fast(): halos.append(lax.ppermute(jnp.where(g == 1, keeps[c], recv), 'tm', onward))]
    ppermute x9 -> x6, waiting for transfers between devices: 12.4 us -> 9.8 us  [along(): moved.append(lax.ppermute(follow(parts[r], after(r)), 'tm', route))]
    pallas_call x3, Pallas kernels: 15 us -> 17.5 us  [correlate(): pl.pallas_call(functools.partial(correlate_kernel, layout), out_shape=sha...]
    ppermute x13 -> x12, waiting for transfers between devices: 2.86 us -> 4.5 us  [the longest x6 3.2 us: sent(): lax.ppermute(follow(block, after[n]) if after else block, ('tm', 'ct'), r...]
    ppermute x9 -> x6, starting transfers between devices: 13.7 us -> 14.8 us  [along(): moved.append(lax.ppermute(follow(parts[r], after(r)), 'tm', route))]
    ppermute x13 -> x12, starting transfers between devices: 8.38 us -> 7.38 us  [the longest x6 7.11 us: sent(): lax.ppermute(follow(block, after[n]) if after else block, ('tm', 'ct'), r...]
  transfers between devices with their start and end apart: 26 -> 22, of which waited for: 10 -> 8; matrix products, arithmetic and copies ran while one was open for 0% -> 0% of each run, Pallas kernels for 30% -> 32%
where the time goes in v11:
time: 107 us; the launch traced here: 106 us
  Pallas kernels  38.4 us (36%)
  starting transfers between devices  33 us (31%)
  waiting for transfers between devices  31.9 us (30%)
  local copies, waits for them, and re-layouts  1.62 us (2%)
  other arithmetic  1.16 us (1%)
    pallas_call x3, Pallas kernels, correlate(): pl.pallas_call(functools.partial(correlate_kernel, layout), out_shape=sha...  17.5 us
    pallas_call x4, Pallas kernels, filterbank(): pl.pallas_call(kernel, out_shape=[jax.ShapeDtypeStruct(shape, jnp.bfloat1...  16.3 us
    ppermute x6, starting transfers between devices, along(): moved.append(lax.ppermute(follow(parts[r], after(r)), 'tm', route))  14.8 us
    ppermute x2, waiting for transfers between devices, fast(): recvs = [lax.ppermute(block, 'tm', swap) for block in sends]  14.7 us
    ppermute x6, waiting for transfers between devices, along(): moved.append(lax.ppermute(follow(parts[r], after(r)), 'tm', route))  9.8 us
    ppermute x2, starting transfers between devices, fast(): halos.append(lax.ppermute(jnp.where(g == 1, keeps[c], recv), 'tm', onward))  7.84 us
    ppermute x6, starting transfers between devices, sent(): lax.ppermute(follow(block, after[n]) if after else block, ('tm', 'ct'), r...  7.11 us
    ppermute x6, waiting for transfers between devices, sent(): lax.ppermute(follow(block, after[n]) if after else block, ('tm', 'ct'), r...  3.2 us
  transfers between devices with their start and end apart: 22, of which 8 were waited for; matrix products, arithmetic and copies ran while one was open for 0% of the time, Pallas kernels for 32%

profile of v11, /device:TPU:0, one launch (start us, length us, event | category | flops | bytes accessed | tf_op | source)
XLA Modules:
  0.0 106.4 jit_solution(12092623218356277472)
XLA Ops:
  0.0 1.6 %copy-done.1 = bf16[2,8,65536]{2,1,0:T(8,128)(2,1)S(1)} copy-done((bf16[2,8,65536]{2,1,0:T(8,128)(2,1)S(1)}, bf16[2,8,65536]{2,1,0:T(8,128)(2,1)}, u32[]{:S(2)}) %copy-start.1) | copy-done | bytes 2097176
  1.6 1.7 %pick.2 = (bf16[2,2,512,128]{3,2,1,0:T(8,128)(2,1)}, bf16[2,2,512,128]{3,2,1,0:T(8,128)(2,1)}) custom-call(bf16[2,8,65536]{2,1,0:T(8,128)(2,1)S(1)} %copy-done.1), custom_call_target="tpu_custom_call" | custom-call | flops 1000000 | bytes 262144 | tf_op jit(solution)/shard_map/pick/pallas_call | solution.py:121
  3.3 0.0 copy-start.6
  3.3 0.0 copy-start.7
  3.4 3.0 %collective-permute-start.1 = (bf16[2,2,512,128]{3,2,1,0:T(8,128)(2,1)}, bf16[2,2,512,128]{3,2,1,0:T(8,128)(2,1)S(1)}, u32[]{:S(2)}, u32[]{:S(2)}) collective-permute-start(bf16[2,2,512,128]{3,2,1,0:T(8,128)(2,1)} %get-tuple-element.53), channel_id=1, source_target_pairs={{0,2},{2,0},{4,6},{6,4},{8,10},{10,8},{12,14},{14,12},{1,3},{3,1},... | collective-permute-start | bytes 1572872 | tf_op jit(solution)/shard_map/ppermute | solution.py:632
  6.4 0.1 collective-permute-start
  6.4 0.8 pick.3
  7.2 12.1 %collective-permute-done.1.refs_2_.refs_3_ = bf16[2,2,512,128]{3,2,1,0:T(8,128)(2,1)S(1)} collective-permute-done((bf16[2,2,512,128]{3,2,1,0:T(8,128)(2,1)}, bf16[2,2,512,128]{3,2,1,0:T(8,128)(2,1)S(1)}, u32[]{:S(2)}, u32[]{:S(2)}) %collective-permute-start.1) | collective-permute-done | bytes 524320 | tf_op jit(solution)/shard_map/ppermute | solution.py:632
  19.3 0.1 broadcast_select_fusion.1
  19.4 4.1 %collective-permute-start.2 = (bf16[2,2,512,128]{3,2,1,0:T(8,128)(2,1)S(1)}, bf16[2,2,512,128]{3,2,1,0:T(8,128)(2,1)S(1)}, u32[]{:S(2)}, u32[]{:S(2)}) collective-permute-start(bf16[2,2,512,128]{3,2,1,0:T(8,128)(2,1)S(1)} %broadcast_select_fusion.1), channel_id=1, source_target_pairs={{0,4},{2,6},{4,8},{6,10},{8,12},{10,14},{1,5},{3,7},{5,9},{7,11},{... | collective-permute-start | bytes 1572872 | tf_op jit(solution)/shard_map/ppermute | solution.py:638
  23.5 3.8 %filterbank_late.2 = (bf16[2,8,2,16,128]{4,3,2,1,0:T(8,128)(2,1)S(1)}, bf16[2,8,2,16,128]{4,3,2,1,0:T(8,128)(2,1)S(1)}, bf16[2,8,2,16,128]{4,3,2,1,0:T(8,128)(2,1)S(1)}, bf16[2,8,2,16,128]{4,3,2,1,0:T(8,128)(2,1)S(1)}) custom-call(s32[8]{0:T(128)S(1)} %copy-done.7, bf16[2,2,512,128]{3,2,1,0:T(8,128)(2,1)S(1)} %get-tuple-element.57.refs_1_.refs_2_, ...), custom_call_target="tpu_custom_call" | custom-call | flops 1000000 | bytes 262144 | tf_op jit(solution)/shard_map/filterbank_late/pallas_call | solution.py:313
  27.3 2.5 %collective-permute-done.refs_2_.refs_3_ = bf16[2,2,512,128]{3,2,1,0:T(8,128)(2,1)} collective-permute-done((bf16[2,2,512,128]{3,2,1,0:T(8,128)(2,1)}, bf16[2,2,512,128]{3,2,1,0:T(8,128)(2,1)}, u32[]{:S(2)}, u32[]{:S(2)}) %collective-permute-start) | collective-permute-done | bytes 524320 | tf_op jit(solution)/shard_map/ppermute | solution.py:632
  29.8 4.3 %filterbank_late.3 = (bf16[4,8,2,16,128]{4,3,2,1,0:T(8,128)(2,1)S(1)}, bf16[4,8,2,16,128]{4,3,2,1,0:T(8,128)(2,1)S(1)}, bf16[4,8,2,16,128]{4,3,2,1,0:T(8,128)(2,1)S(1)}, bf16[4,8,2,16,128]{4,3,2,1,0:T(8,128)(2,1)S(1)}) custom-call(s32[8]{0:T(128)S(1)} %copy-done.7, bf16[2,2,512,128]{3,2,1,0:T(8,128)(2,1)S(1)} %get-tuple-element.55.refs_1_.refs_2_, ...), custom_call_target="tpu_custom_call" | custom-call | flops 1000000 | bytes 262144 | tf_op jit(solution)/shard_map/filterbank_late/pallas_call | solution.py:313
  34.1 0.0 collective-permute-done.2.refs_1_
  34.1 1.1 %broadcast_select_fusion = bf16[2,2,512,128]{3,2,1,0:T(8,128)(2,1)S(1)} fusion(bf16[2,2,512,128]{3,2,1,0:T(8,128)(2,1)S(1)} %get-tuple-element.55.refs_1_.refs_2_, bf16[2,2,512,128]{3,2,1,0:T(8,128)(2,1)} %collective-permute-done.refs_2_.refs_3_, pred[]{:T(512)S(6)} %eq.6), kind=kLoop, calls=%fused_computation | loop fusion | flops 262144 | bytes 1572865 | tf_op jit(solution)/shard_map/jit(_where)/select_n | solution.py:638
  35.2 3.8 %collective-permute-start.3 = (bf16[2,2,512,128]{3,2,1,0:T(8,128)(2,1)S(1)}, bf16[2,2,512,128]{3,2,1,0:T(8,128)(2,1)S(1)}, u32[]{:S(2)}, u32[]{:S(2)}) collective-permute-start(bf16[2,2,512,128]{3,2,1,0:T(8,128)(2,1)S(1)} %broadcast_select_fusion), channel_id=1, source_target_pairs={{0,4},{2,6},{4,8},{6,10},{8,12},{10,14},{1,5},{3,7},{5,9},{7,11},{... | collective-permute-start | bytes 1572872 | tf_op jit(solution)/shard_map/ppermute | solution.py:638
  39.0 1.5 %collective-permute-start.6 = (bf16[4,8,2,16,128]{4,3,2,1,0:T(8,128)(2,1)S(1)}, bf16[4,8,2,16,128]{4,3,2,1,0:T(8,128)(2,1)S(1)}, u32[]{:S(2)}, u32[]{:S(2)}) collective-permute-start(bf16[4,8,2,16,128]{4,3,2,1,0:T(8,128)(2,1)S(1)} %get-tuple-element.75), channel_id=1, source_target_pairs={{0,3},{1,2},{2,1},{3,0},{4,7},{5,6},{6,5},{7,4},{8,11},{9,10},{10,... | collective-permute-start | bytes 786440 | tf_op jit(solution)/shard_map/ppermute | solution.py:649
  40.5 1.6 %collective-permute-start.5 = (bf16[4,8,2,16,128]{4,3,2,1,0:T(8,128)(2,1)S(1)}, bf16[4,8,2,16,128]{4,3,2,1,0:T(8,128)(2,1)S(1)}, u32[]{:S(2)}, u32[]{:S(2)}) collective-permute-start(bf16[4,8,2,16,128]{4,3,2,1,0:T(8,128)(2,1)S(1)} %get-tuple-element.73), channel_id=1, source_target_pairs={{0,2},{1,3},{2,0},{3,1},{4,6},{5,7},{6,4},{7,5},{8,10},{9,11},{10,... | collective-permute-start | bytes 786440 | tf_op jit(solution)/shard_map/ppermute | solution.py:649
  42.1 0.5 collective-permute-start.4
  42.6 3.8 %filterbank_early.2 = (bf16[2,8,2,16,128]{4,3,2,1,0:T(8,128)(2,1)S(1)}, bf16[2,8,2,16,128]{4,3,2,1,0:T(8,128)(2,1)S(1)}, bf16[2,8,2,16,128]{4,3,2,1,0:T(8,128)(2,1)S(1)}, bf16[2,8,2,16,128]{4,3,2,1,0:T(8,128)(2,1)S(1)}) custom-call(s32[8]{0:T(128)S(1)} %copy-done.7, bf16[2,2,512,128]{3,2,1,0:T(8,128)(2,1)S(1)} %collective-permute-done.2.refs_1_, ...), custom_call_target="tpu_custom_call" | custom-call | flops 1000000 | bytes 262144 | tf_op jit(solution)/shard_map/filterbank_early/pallas_call | solution.py:313
  46.3 2.9 %collective-permute-done.3.refs_1_ = bf16[2,2,512,128]{3,2,1,0:T(8,128)(2,1)S(1)} collective-permute-done((bf16[2,2,512,128]{3,2,1,0:T(8,128)(2,1)S(1)}, bf16[2,2,512,128]{3,2,1,0:T(8,128)(2,1)S(1)}, u32[]{:S(2)}, u32[]{:S(2)}) %collective-permute-start.3) | collective-permute-done | bytes 524320 | tf_op jit(solution)/shard_map/ppermute | solution.py:638
  49.3 4.5 %filterbank_early.3 = (bf16[4,8,2,16,128]{4,3,2,1,0:T(8,128)(2,1)S(1)}, bf16[4,8,2,16,128]{4,3,2,1,0:T(8,128)(2,1)S(1)}, bf16[4,8,2,16,128]{4,3,2,1,0:T(8,128)(2,1)S(1)}, bf16[4,8,2,16,128]{4,3,2,1,0:T(8,128)(2,1)S(1)}) custom-call(s32[8]{0:T(128)S(1)} %copy-done.7, bf16[2,2,512,128]{3,2,1,0:T(8,128)(2,1)S(1)} %collective-permute-done.3.refs_1_, ...), custom_call_target="tpu_custom_call" | custom-call | flops 1000000 | bytes 262144 | tf_op jit(solution)/shard_map/filterbank_early/pallas_call | solution.py:313
  53.7 0.0 collective-permute-done.6.refs_3_
  53.8 0.0 collective-permute-done.5.refs_2_
  53.8 0.2 join.2.refs_0_
  54.0 0.1 collective-permute-start.7
  54.0 1.5 %collective-permute-start.10 = (bf16[4,8,2,16,128]{4,3,2,1,0:T(8,128)(2,1)S(1)}, bf16[4,8,2,16,128]{4,3,2,1,0:T(8,128)(2,1)S(1)}, u32[]{:S(2)}, u32[]{:S(2)}) collective-permute-start(bf16[4,8,2,16,128]{4,3,2,1,0:T(8,128)(2,1)S(1)} %get-tuple-element.85), channel_id=1, source_target_pairs={{0,3},{1,2},{2,1},{3,0},{4,7},{5,6},{6,5},{7,4},{8,11},{9,10},{10,... | collective-permute-start | bytes 786440 | tf_op jit(solution)/shard_map/ppermute | solution.py:649
  55.5 1.6 %collective-permute-start.9 = (bf16[4,8,2,16,128]{4,3,2,1,0:T(8,128)(2,1)S(1)}, bf16[4,8,2,16,128]{4,3,2,1,0:T(8,128)(2,1)S(1)}, u32[]{:S(2)}, u32[]{:S(2)}) collective-permute-start(bf16[4,8,2,16,128]{4,3,2,1,0:T(8,128)(2,1)S(1)} %get-tuple-element.82), channel_id=1, source_target_pairs={{0,2},{1,3},{2,0},{3,1},{4,6},{5,7},{6,4},{7,5},{8,10},{9,11},{10,... | collective-permute-start | bytes 786440 | tf_op jit(solution)/shard_map/ppermute | solution.py:649
  57.1 0.5 collective-permute-start.8
  57.6 8.6 %correlate_late.1.refs_1_.refs_2_ = f32[4224,128]{1,0:T(8,128)S(1)} custom-call(bf16[16,8,2,16,128]{4,3,2,1,0:T(8,128)(2,1)S(1)} %join.2.refs_0_, bf16[16,8,2,16,128]{4,3,2,1,0:T(8,128)(2,1)S(1)} %collective-permute-done.7.refs_1_), custom_call_target="tpu_custom_call" | custom-call | flops 1000000 | bytes 262144 | tf_op jit(solution)/shard_map/correlate_late/pallas_call | solution.py:475
  66.2 3.2 %collective-permute-done.9.refs_2_ = bf16[4,8,2,16,128]{4,3,2,1,0:T(8,128)(2,1)S(1)} collective-permute-done((bf16[4,8,2,16,128]{4,3,2,1,0:T(8,128)(2,1)S(1)}, bf16[4,8,2,16,128]{4,3,2,1,0:T(8,128)(2,1)S(1)}, u32[]{:S(2)}, u32[]{:S(2)}) %collective-permute-start.9) | collective-permute-done | bytes 262176 | tf_op jit(solution)/shard_map/ppermute | solution.py:649
  69.4 0.2 join.3.refs_0_
  69.6 0.1 collective-permute-start.11
  69.6 4.6 %correlate_own.1 = (f32[544,128]{1,0:T(8,128)S(1)}, bf16[544,128]{1,0:T(8,128)(2,1)S(1)}, bf16[544,128]{1,0:T(8,128)(2,1)S(1)}, bf16[544,128]{1,0:T(8,128)(2,1)S(1)}) custom-call(bf16[16,8,2,16,128]{4,3,2,1,0:T(8,128)(2,1)S(1)} %join.3.refs_0_, f32[4224,128]{1,0:T(8,128)S(1)} %correlate_late.1.refs_1_.refs_2_), custom_call_target="tpu_custom_call" | custom-call | flops 1000000 | bytes 262144 | tf_op jit(solution)/shard_map/correlate_own/pallas_call | solution.py:475
  74.2 2.5 %collective-permute-start.12 = (bf16[544,128]{1,0:T(8,128)(2,1)S(1)}, bf16[544,128]{1,0:T(8,128)(2,1)S(1)}, u32[]{:S(2)}, u32[]{:S(2)}) collective-permute-start(bf16[544,128]{1,0:T(8,128)(2,1)S(1)} %get-tuple-element.89), channel_id=1, source_target_pairs={{0,4},{2,6},{4,8},{6,10},{8,12},{10,14},{12,0},{14,2},{1,5},{3,7},... | collective-permute-start | bytes 417800 | tf_op jit(solution)/shard_map/ppermute | solution.py:665
  76.7 2.6 %collective-permute-start.13 = (bf16[544,128]{1,0:T(8,128)(2,1)S(1)}, bf16[544,128]{1,0:T(8,128)(2,1)S(1)}, u32[]{:S(2)}, u32[]{:S(2)}) collective-permute-start(bf16[544,128]{1,0:T(8,128)(2,1)S(1)} %get-tuple-element.91), channel_id=1, source_target_pairs={{0,8},{2,10},{4,12},{6,14},{8,0},{10,2},{12,4},{14,6},{1,9},{3,11}... | collective-permute-start | bytes 417800 | tf_op jit(solution)/shard_map/ppermute | solution.py:665
  79.3 1.3 %collective-permute-start.14 = (bf16[544,128]{1,0:T(8,128)(2,1)S(1)}, bf16[544,128]{1,0:T(8,128)(2,1)S(1)}, u32[]{:S(2)}, u32[]{:S(2)}) collective-permute-start(bf16[544,128]{1,0:T(8,128)(2,1)S(1)} %get-tuple-element.93), channel_id=1, source_target_pairs={{0,12},{2,14},{4,0},{6,2},{8,4},{10,6},{12,8},{14,10},{1,13},{3,15... | collective-permute-start | bytes 417800 | tf_op jit(solution)/shard_map/ppermute | solution.py:665
  80.7 4.4 %correlate_cross.1 = (f32[512,128]{1,0:T(8,128)S(1)}, bf16[512,128]{1,0:T(8,128)(2,1)S(1)}, bf16[512,128]{1,0:T(8,128)(2,1)S(1)}, bf16[512,128]{1,0:T(8,128)(2,1)S(1)}) custom-call(bf16[16,8,2,16,128]{4,3,2,1,0:T(8,128)(2,1)S(1)} %join.3.refs_0_, bf16[16,8,2,16,128]{4,3,2,1,0:T(8,128)(2,1)S(1)} %collective-permute-done.11.refs_1_, ...), custom_call_target="tpu_custom_call" | custom-call | flops 1000000 | bytes 262144 | tf_op jit(solution)/shard_map/correlate_cross/pallas_call | solution.py:475
  85.1 0.1 collective-permute-start.18
  85.2 3.0 %collective-permute-start.15 = (bf16[512,128]{1,0:T(8,128)(2,1)S(1)}, bf16[512,128]{1,0:T(8,128)(2,1)S(1)}, u32[]{:S(2)}, u32[]{:S(2)}) collective-permute-start(bf16[512,128]{1,0:T(8,128)(2,1)S(1)} %get-tuple-element.96), channel_id=1, source_target_pairs={{0,4},{2,6},{4,8},{6,10},{8,12},{10,14},{12,0},{14,2},{1,5},{3,7},... | collective-permute-start | bytes 393224 | tf_op jit(solution)/shard_map/ppermute | solution.py:665
  88.2 1.0 collective-permute-done.13.refs_2_
  89.1 1.1 %collective-permute-start.16 = (bf16[512,128]{1,0:T(8,128)(2,1)S(1)}, bf16[512,128]{1,0:T(8,128)(2,1)S(1)}, u32[]{:S(2)}, u32[]{:S(2)}) collective-permute-start(bf16[512,128]{1,0:T(8,128)(2,1)S(1)} %get-tuple-element.98), channel_id=1, source_target_pairs={{0,8},{2,10},{4,12},{6,14},{8,0},{10,2},{12,4},{14,6},{1,9},{3,11}... | collective-permute-start | bytes 393224 | tf_op jit(solution)/shard_map/ppermute | solution.py:665
  90.2 4.2 %collective-permute-start.17 = (bf16[512,128]{1,0:T(8,128)(2,1)S(1)}, bf16[512,128]{1,0:T(8,128)(2,1)S(1)}, u32[]{:S(2)}, u32[]{:S(2)}) collective-permute-start(bf16[512,128]{1,0:T(8,128)(2,1)S(1)} %get-tuple-element.100), channel_id=1, source_target_pairs={{0,12},{2,14},{4,0},{6,2},{8,4},{10,6},{12,8},{14,10},{1,13},{3,15... | collective-permute-start | bytes 393224 | tf_op jit(solution)/shard_map/ppermute | solution.py:665
  94.4 6.1 %collective-permute-done.16.refs_6_ = bf16[512,128]{1,0:T(8,128)(2,1)S(1)} collective-permute-done((bf16[512,128]{1,0:T(8,128)(2,1)S(1)}, bf16[512,128]{1,0:T(8,128)(2,1)S(1)}, u32[]{:S(2)}, u32[]{:S(2)}) %collective-permute-start.16) | collective-permute-done | bytes 131104 | tf_op jit(solution)/shard_map/ppermute | solution.py:665
  100.6 2.7 %collective-permute-done.17.refs_7_ = bf16[512,128]{1,0:T(8,128)(2,1)S(1)} collective-permute-done((bf16[512,128]{1,0:T(8,128)(2,1)S(1)}, bf16[512,128]{1,0:T(8,128)(2,1)S(1)}, u32[]{:S(2)}, u32[]{:S(2)}) %collective-permute-start.17) | collective-permute-done | bytes 131104 | tf_op jit(solution)/shard_map/ppermute | solution.py:665
  103.3 0.0 collective-permute-start.21
  103.3 1.3 %collective-permute-done.21.refs_11_ = bf16[512,128]{1,0:T(8,128)(2,1)S(1)} collective-permute-done((bf16[512,128]{1,0:T(8,128)(2,1)S(1)}, bf16[512,128]{1,0:T(8,128)(2,1)S(1)}, u32[]{:S(2)}, u32[]{:S(2)}) %collective-permute-start.21) | collective-permute-done | bytes 131104 | tf_op jit(solution)/shard_map/ppermute | solution.py:684
  104.6 1.7 %assemble.1 = f32[2,16,32,256]{3,2,1,0:T(8,128)} custom-call(f32[544,128]{1,0:T(8,128)S(1)} %get-tuple-element.87.refs_0_, bf16[544,128]{1,0:T(8,128)(2,1)S(1)} %collective-permute-done.12.refs_1_, bf16[544,128]{1,0:T(8,128)(2,1)S(1)} %collective-permute-done.13.refs_2_, bf16[544,128]{1,0:T(8,128)(2,1)S(1)} %collective-permute-done.14.refs_3_, ...), custom_call_target="tpu_custom_call" | custom-call | flops 1000000 | bytes 262144 | tf_op jit(solution)/shard_map/assemble/pallas_call | solution.py:578
  (26 shorter events, 0.1 us)
Async XLA Ops:
  0.0 1.6 %copy-start.1 = (bf16[2,8,65536]{2,1,0:T(8,128)(2,1)S(1)}, bf16[2,8,65536]{2,1,0:T(8,128)(2,1)}, u32[]{:S(2)}) copy-start(bf16[2,8,65536]{2,1,0:T(8,128)(2,1)} %block.2) | copy-start | bytes 6291460
  1.6 4.8 %copy-start.2 = (bf16[2,8,65536]{2,1,0:T(8,128)(2,1)S(1)}, bf16[2,8,65536]{2,1,0:T(8,128)(2,1)}, u32[]{:S(2)}) copy-start(bf16[2,8,65536]{2,1,0:T(8,128)(2,1)} %block.2) | copy-start | bytes 6291460
  3.3 20.2 %copy-start = (f32[16,64,128]{2,1,0:T(8,128)S(1)}, f32[16,64,128]{2,1,0:T(8,128)}, u32[]{:S(2)}) copy-start(f32[16,64,128]{2,1,0:T(8,128)} %constant.30.clone.refs_3_.refs_4_) | copy-start | bytes 1572868
  3.3 20.2 %copy-start.3 = (bf16[2,4,32,128]{3,2,1,0:T(8,128)(2,1)S(1)}, bf16[2,4,32,128]{3,2,1,0:T(8,128)(2,1)}, u32[]{:S(2)}) copy-start(bf16[2,4,32,128]{3,2,1,0:T(8,128)(2,1)} %constant.34.clone.refs_7_.refs_8_) | copy-start | bytes 196612
  3.3 20.2 %copy-start.4 = (f32[64,128]{1,0:T(8,128)S(1)}, f32[64,128]{1,0:T(8,128)}, u32[]{:S(2)}) copy-start(f32[64,128]{1,0:T(8,128)} %constant.33.clone.refs_6_.refs_7_) | copy-start | bytes 98308
  3.3 20.2 %copy-start.5 = (f32[64,128]{1,0:T(8,128)S(1)}, f32[64,128]{1,0:T(8,128)}, u32[]{:S(2)}) copy-start(f32[64,128]{1,0:T(8,128)} %constant.32.clone.refs_5_.refs_6_) | copy-start | bytes 98308
  3.3 20.2 %copy-start.6 = (bf16[128,128]{1,0:T(8,128)(2,1)S(1)}, bf16[128,128]{1,0:T(8,128)(2,1)}, u32[]{:S(2)}) copy-start(bf16[128,128]{1,0:T(8,128)(2,1)} %constant.31.clone.refs_4_.refs_5_) | copy-start | bytes 98308
  3.3 20.2 %copy-start.7 = (s32[8]{0:T(128)S(1)}, s32[8]{0:T(128)}, u32[]{:S(2)}) copy-start(s32[8]{0:T(128)} %refs_0_.7) | copy-start | bytes 100
  3.4 16.0 %collective-permute-start.1 = (bf16[2,2,512,128]{3,2,1,0:T(8,128)(2,1)}, bf16[2,2,512,128]{3,2,1,0:T(8,128)(2,1)S(1)}, u32[]{:S(2)}, u32[]{:S(2)}) collective-permute-start(bf16[2,2,512,128]{3,2,1,0:T(8,128)(2,1)} %get-tuple-element.53), channel_id=1, source_target_pairs={{0,2},{2,0},{4,6},{6,4},{8,10},{10,8},{12,14},{14,12},{1,3},{3,1},... | collective-permute-start | bytes 1572872 | tf_op jit(solution)/shard_map/ppermute | solution.py:632
  6.4 23.5 %collective-permute-start = (bf16[2,2,512,128]{3,2,1,0:T(8,128)(2,1)}, bf16[2,2,512,128]{3,2,1,0:T(8,128)(2,1)}, u32[]{:S(2)}, u32[]{:S(2)}) collective-permute-start(bf16[2,2,512,128]{3,2,1,0:T(8,128)(2,1)} %get-tuple-element.56), channel_id=1, source_target_pairs={{0,2},{2,0},{4,6},{6,4},{8,10},{10,8},{12,14},{14,12},{1,3},{3,1},... | collective-permute-start | bytes 1572872 | tf_op jit(solution)/shard_map/ppermute | solution.py:632
  19.4 14.7 %collective-permute-start.2 = (bf16[2,2,512,128]{3,2,1,0:T(8,128)(2,1)S(1)}, bf16[2,2,512,128]{3,2,1,0:T(8,128)(2,1)S(1)}, u32[]{:S(2)}, u32[]{:S(2)}) collective-permute-start(bf16[2,2,512,128]{3,2,1,0:T(8,128)(2,1)S(1)} %broadcast_select_fusion.1), channel_id=1, source_target_pairs={{0,4},{2,6},{4,8},{6,10},{8,12},{10,14},{1,5},{3,7},{5,9},{7,11},{... | collective-permute-start | bytes 1572872 | tf_op jit(solution)/shard_map/ppermute | solution.py:638
  35.2 14.0 %collective-permute-start.3 = (bf16[2,2,512,128]{3,2,1,0:T(8,128)(2,1)S(1)}, bf16[2,2,512,128]{3,2,1,0:T(8,128)(2,1)S(1)}, u32[]{:S(2)}, u32[]{:S(2)}) collective-permute-start(bf16[2,2,512,128]{3,2,1,0:T(8,128)(2,1)S(1)} %broadcast_select_fusion), channel_id=1, source_target_pairs={{0,4},{2,6},{4,8},{6,10},{8,12},{10,14},{1,5},{3,7},{5,9},{7,11},{... | collective-permute-start | bytes 1572872 | tf_op jit(solution)/shard_map/ppermute | solution.py:638
  39.0 14.7 %collective-permute-start.6 = (bf16[4,8,2,16,128]{4,3,2,1,0:T(8,128)(2,1)S(1)}, bf16[4,8,2,16,128]{4,3,2,1,0:T(8,128)(2,1)S(1)}, u32[]{:S(2)}, u32[]{:S(2)}) collective-permute-start(bf16[4,8,2,16,128]{4,3,2,1,0:T(8,128)(2,1)S(1)} %get-tuple-element.75), channel_id=1, source_target_pairs={{0,3},{1,2},{2,1},{3,0},{4,7},{5,6},{6,5},{7,4},{8,11},{9,10},{10,... | collective-permute-start | bytes 786440 | tf_op jit(solution)/shard_map/ppermute | solution.py:649
  40.5 13.3 %collective-permute-start.5 = (bf16[4,8,2,16,128]{4,3,2,1,0:T(8,128)(2,1)S(1)}, bf16[4,8,2,16,128]{4,3,2,1,0:T(8,128)(2,1)S(1)}, u32[]{:S(2)}, u32[]{:S(2)}) collective-permute-start(bf16[4,8,2,16,128]{4,3,2,1,0:T(8,128)(2,1)S(1)} %get-tuple-element.73), channel_id=1, source_target_pairs={{0,2},{1,3},{2,0},{3,1},{4,6},{5,7},{6,4},{7,5},{8,10},{9,11},{10,... | collective-permute-start | bytes 786440 | tf_op jit(solution)/shard_map/ppermute | solution.py:649
  42.1 11.7 %collective-permute-start.4 = (bf16[4,8,2,16,128]{4,3,2,1,0:T(8,128)(2,1)S(1)}, bf16[4,8,2,16,128]{4,3,2,1,0:T(8,128)(2,1)S(1)}, u32[]{:S(2)}, u32[]{:S(2)}) collective-permute-start(bf16[4,8,2,16,128]{4,3,2,1,0:T(8,128)(2,1)S(1)} %get-tuple-element.71), channel_id=1, source_target_pairs={{0,1},{1,0},{2,3},{3,2},{4,5},{5,4},{6,7},{7,6},{8,9},{9,8},{10,11... | collective-permute-start | bytes 786440 | tf_op jit(solution)/shard_map/ppermute | solution.py:649
  54.0 3.6 %collective-permute-start.7 = (bf16[16,8,2,16,128]{4,3,2,1,0:T(8,128)(2,1)S(1)}, bf16[16,8,2,16,128]{4,3,2,1,0:T(8,128)(2,1)S(1)}, u32[]{:S(2)}, u32[]{:S(2)}) collective-permute-start(bf16[16,8,2,16,128]{4,3,2,1,0:T(8,128)(2,1)S(1)} %join.2.refs_0_), channel_id=1, source_target_pairs={{0,16},{16,0},{1,17},{17,1},{2,18},{18,2},{3,19},{19,3},{4,20},{20... | collective-permute-start | bytes 3145736 | tf_op jit(solution)/shard_map/ppermute | solution.py:672
  54.0 12.1 %collective-permute-start.10 = (bf16[4,8,2,16,128]{4,3,2,1,0:T(8,128)(2,1)S(1)}, bf16[4,8,2,16,128]{4,3,2,1,0:T(8,128)(2,1)S(1)}, u32[]{:S(2)}, u32[]{:S(2)}) collective-permute-start(bf16[4,8,2,16,128]{4,3,2,1,0:T(8,128)(2,1)S(1)} %get-tuple-element.85), channel_id=1, source_target_pairs={{0,3},{1,2},{2,1},{3,0},{4,7},{5,6},{6,5},{7,4},{8,11},{9,10},{10,... | collective-permute-start | bytes 786440 | tf_op jit(solution)/shard_map/ppermute | solution.py:649
  55.5 13.9 %collective-permute-start.9 = (bf16[4,8,2,16,128]{4,3,2,1,0:T(8,128)(2,1)S(1)}, bf16[4,8,2,16,128]{4,3,2,1,0:T(8,128)(2,1)S(1)}, u32[]{:S(2)}, u32[]{:S(2)}) collective-permute-start(bf16[4,8,2,16,128]{4,3,2,1,0:T(8,128)(2,1)S(1)} %get-tuple-element.82), channel_id=1, source_target_pairs={{0,2},{1,3},{2,0},{3,1},{4,6},{5,7},{6,4},{7,5},{8,10},{9,11},{10,... | collective-permute-start | bytes 786440 | tf_op jit(solution)/shard_map/ppermute | solution.py:649
  57.1 12.3 %collective-permute-start.8 = (bf16[4,8,2,16,128]{4,3,2,1,0:T(8,128)(2,1)S(1)}, bf16[4,8,2,16,128]{4,3,2,1,0:T(8,128)(2,1)S(1)}, u32[]{:S(2)}, u32[]{:S(2)}) collective-permute-start(bf16[4,8,2,16,128]{4,3,2,1,0:T(8,128)(2,1)S(1)} %get-tuple-element.79), channel_id=1, source_target_pairs={{0,1},{1,0},{2,3},{3,2},{4,5},{5,4},{6,7},{7,6},{8,9},{9,8},{10,11... | collective-permute-start | bytes 786440 | tf_op jit(solution)/shard_map/ppermute | solution.py:649
  69.6 4.6 %collective-permute-start.11 = (bf16[16,8,2,16,128]{4,3,2,1,0:T(8,128)(2,1)S(1)}, bf16[16,8,2,16,128]{4,3,2,1,0:T(8,128)(2,1)S(1)}, u32[]{:S(2)}, u32[]{:S(2)}) collective-permute-start(bf16[16,8,2,16,128]{4,3,2,1,0:T(8,128)(2,1)S(1)} %join.3.refs_0_), channel_id=1, source_target_pairs={{0,16},{16,0},{1,17},{17,1},{2,18},{18,2},{3,19},{19,3},{4,20},{20... | collective-permute-start | bytes 3145736 | tf_op jit(solution)/shard_map/ppermute | solution.py:675
  74.2 11.0 %collective-permute-start.12 = (bf16[544,128]{1,0:T(8,128)(2,1)S(1)}, bf16[544,128]{1,0:T(8,128)(2,1)S(1)}, u32[]{:S(2)}, u32[]{:S(2)}) collective-permute-start(bf16[544,128]{1,0:T(8,128)(2,1)S(1)} %get-tuple-element.89), channel_id=1, source_target_pairs={{0,4},{2,6},{4,8},{6,10},{8,12},{10,14},{12,0},{14,2},{1,5},{3,7},... | collective-permute-start | bytes 417800 | tf_op jit(solution)/shard_map/ppermute | solution.py:665
  76.7 12.4 %collective-permute-start.13 = (bf16[544,128]{1,0:T(8,128)(2,1)S(1)}, bf16[544,128]{1,0:T(8,128)(2,1)S(1)}, u32[]{:S(2)}, u32[]{:S(2)}) collective-permute-start(bf16[544,128]{1,0:T(8,128)(2,1)S(1)} %get-tuple-element.91), channel_id=1, source_target_pairs={{0,8},{2,10},{4,12},{6,14},{8,0},{10,2},{12,4},{14,6},{1,9},{3,11}... | collective-permute-start | bytes 417800 | tf_op jit(solution)/shard_map/ppermute | solution.py:665
  79.3 10.9 %collective-permute-start.14 = (bf16[544,128]{1,0:T(8,128)(2,1)S(1)}, bf16[544,128]{1,0:T(8,128)(2,1)S(1)}, u32[]{:S(2)}, u32[]{:S(2)}) collective-permute-start(bf16[544,128]{1,0:T(8,128)(2,1)S(1)} %get-tuple-element.93), channel_id=1, source_target_pairs={{0,12},{2,14},{4,0},{6,2},{8,4},{10,6},{12,8},{14,10},{1,13},{3,15... | collective-permute-start | bytes 417800 | tf_op jit(solution)/shard_map/ppermute | solution.py:665
  85.1 18.2 %collective-permute-start.18 = (f32[512,128]{1,0:T(8,128)S(1)}, f32[512,128]{1,0:T(8,128)S(1)}, u32[]{:S(2)}, u32[]{:S(2)}) collective-permute-start(f32[512,128]{1,0:T(8,128)S(1)} %get-tuple-element.94.refs_4_), channel_id=1, source_target_pairs={{0,16},{16,0},{1,17},{17,1},{2,18},{18,2},{3,19},{19,3},{4,20},{20... | collective-permute-start | bytes 786440 | tf_op jit(solution)/shard_map/ppermute | solution.py:684
  85.2 9.3 %collective-permute-start.15 = (bf16[512,128]{1,0:T(8,128)(2,1)S(1)}, bf16[512,128]{1,0:T(8,128)(2,1)S(1)}, u32[]{:S(2)}, u32[]{:S(2)}) collective-permute-start(bf16[512,128]{1,0:T(8,128)(2,1)S(1)} %get-tuple-element.96), channel_id=1, source_target_pairs={{0,4},{2,6},{4,8},{6,10},{8,12},{10,14},{12,0},{14,2},{1,5},{3,7},... | collective-permute-start | bytes 393224 | tf_op jit(solution)/shard_map/ppermute | solution.py:665
  89.1 11.4 %collective-permute-start.16 = (bf16[512,128]{1,0:T(8,128)(2,1)S(1)}, bf16[512,128]{1,0:T(8,128)(2,1)S(1)}, u32[]{:S(2)}, u32[]{:S(2)}) collective-permute-start(bf16[512,128]{1,0:T(8,128)(2,1)S(1)} %get-tuple-element.98), channel_id=1, source_target_pairs={{0,8},{2,10},{4,12},{6,14},{8,0},{10,2},{12,4},{14,6},{1,9},{3,11}... | collective-permute-start | bytes 393224 | tf_op jit(solution)/shard_map/ppermute | solution.py:665
  90.2 13.0 %collective-permute-start.17 = (bf16[512,128]{1,0:T(8,128)(2,1)S(1)}, bf16[512,128]{1,0:T(8,128)(2,1)S(1)}, u32[]{:S(2)}, u32[]{:S(2)}) collective-permute-start(bf16[512,128]{1,0:T(8,128)(2,1)S(1)} %get-tuple-element.100), channel_id=1, source_target_pairs={{0,12},{2,14},{4,0},{6,2},{8,4},{10,6},{12,8},{14,10},{1,13},{3,15... | collective-permute-start | bytes 393224 | tf_op jit(solution)/shard_map/ppermute | solution.py:665
  94.4 8.9 %collective-permute-start.19 = (bf16[512,128]{1,0:T(8,128)(2,1)S(1)}, bf16[512,128]{1,0:T(8,128)(2,1)S(1)}, u32[]{:S(2)}, u32[]{:S(2)}) collective-permute-start(bf16[512,128]{1,0:T(8,128)(2,1)S(1)} %collective-permute-done.15.refs_5_), channel_id=1, source_target_pairs={{0,16},{16,0},{1,17},{17,1},{2,18},{18,2},{3,19},{19,3},{4,20},{20... | collective-permute-start | bytes 393224 | tf_op jit(solution)/shard_map/ppermute | solution.py:684
  100.6 2.8 %collective-permute-start.20 = (bf16[512,128]{1,0:T(8,128)(2,1)S(1)}, bf16[512,128]{1,0:T(8,128)(2,1)S(1)}, u32[]{:S(2)}, u32[]{:S(2)}) collective-permute-start(bf16[512,128]{1,0:T(8,128)(2,1)S(1)} %collective-permute-done.16.refs_6_), channel_id=1, source_target_pairs={{0,16},{16,0},{1,17},{17,1},{2,18},{18,2},{3,19},{19,3},{4,20},{20... | collective-permute-start | bytes 393224 | tf_op jit(solution)/shard_map/ppermute | solution.py:684
  103.3 1.3 %collective-permute-start.21 = (bf16[512,128]{1,0:T(8,128)(2,1)S(1)}, bf16[512,128]{1,0:T(8,128)(2,1)S(1)}, u32[]{:S(2)}, u32[]{:S(2)}) collective-permute-start(bf16[512,128]{1,0:T(8,128)(2,1)S(1)} %collective-permute-done.17.refs_7_), channel_id=1, source_target_pairs={{0,16},{16,0},{1,17},{17,1},{2,18},{18,2},{3,19},{19,3},{4,20},{20... | collective-permute-start | bytes 393224 | tf_op jit(solution)/shard_map/ppermute | solution.py:684

commit v12 on v10

--- a/solution.py
+++ b/solution.py
@@ -83,40 +83,48 @@
     return np.concatenate([cosine, cosine], axis=1), np.concatenate([sine, sine], axis=1)
 
 
-def pick_kernel(half, block, *refs):
+def pick_kernel(half, own, block, *refs):
     outs, rows = refs[:-1], refs[-1]
     inputs, samples = block.shape[1], block.shape[2]
-    tall = samples // LANES
-    step = 16
+    step = 32
     for part in range(2):
-        for n in range(tall // step):
-            cut = slice(n * step * LANES, (n + 1) * step * LANES)
-            wide = block[part, :, cut].astype(jnp.float32)
+
+        def spread(n, carry, part=part):
+            low = pl.multiple_of(n * step * LANES, step * LANES)
+            wide = block[part, :, pl.ds(low, step * LANES)].astype(jnp.float32)
             for u in range(step):
-                at = (n * step + u) * inputs
-                rows[part, at : at + inputs, :] = wide[:, u * LANES : (u + 1) * LANES]
+                at = pl.multiple_of((n * step + u) * inputs, inputs)
+                rows[part, pl.ds(at, inputs), :] = wide[:, u * LANES : (u + 1) * LANES]
+            return carry
+
+        lax.fori_loop(0, samples // LANES // step, spread, 0)
     g = position()[2]
-    for item in range(inputs):
-        first = (1 - g) * half + item if item < half else g * half + item - half
-        for part in range(2):
-            value = rows[part, pl.ds(first, tall, stride=inputs), :]
-            outs[item // JOIN][item % JOIN, part] = value.astype(jnp.bfloat16)
-
-
-def pick(block):
+    first = (g if own else 1 - g) * half
+    tall = 64
+
+    def gather(n, carry):
+        low = pl.multiple_of(n * tall, tall)
+        for item in range(half):
+            for part in range(2):
+                at = low * inputs + first + item
+                value = rows[part, pl.ds(at, tall, stride=inputs), :].astype(jnp.bfloat16)
+                outs[item // JOIN][item % JOIN, part, pl.ds(low, tall), :] = value
+        return carry
+
+    lax.fori_loop(0, samples // LANES // tall, gather, 0)
+
+
+def pick(block, own):
     _, inputs, samples = block.shape
     half = inputs // PAIR
-    steps = 8
-    tall = samples // LANES // steps
     shape = jax.ShapeDtypeStruct((JOIN, 2, samples // LANES, LANES), jnp.bfloat16)
     return pl.pallas_call(
-        functools.partial(pick_kernel, half),
-        grid=(steps,),
-        out_shape=[shape] * (inputs // JOIN),
-        in_specs=[pl.BlockSpec((2, inputs, samples // steps), lambda t: (0, 0, t))],
-        out_specs=[pl.BlockSpec((JOIN, 2, tall, LANES), lambda t: (0, 0, t, 0))] * (inputs // JOIN),
-        scratch_shapes=[pltpu.VMEM((2, tall * inputs, LANES), jnp.float32)],
-        compiler_params=params(56),
+        functools.partial(pick_kernel, half, own),
+        out_shape=[shape] * (half // JOIN),
+        in_specs=[VMEM],
+        out_specs=[VMEM] * (half // JOIN),
+        scratch_shapes=[pltpu.VMEM((2, samples // LANES * inputs, LANES), jnp.float32)],
+        compiler_params=params(12),
         cost_estimate=cost(10**6, 2**18),
         name="pick",
     )(block)
@@ -335,7 +343,7 @@
         return [block for block in blocks if not early(block)]
 
     first = [block for block in whole + across + corner if early(block)]
-    return [first, late(whole + corner), late(across)]
+    return [first, late(whole + corner + across)]
 
 
 def pairs_in(blocks):
@@ -350,12 +358,14 @@
 
 
 def correlate_kernel(layout, *refs):
-    sources_at, blocks, own, terms, outer, span, per_ct = layout
+    sources_at, blocks, own, owners, outer, span, per_ct = layout
     sources, rest = refs[: len(sources_at)], refs[len(sources_at) :]
-    earlier, outs, (spectra, sums, held) = rest[:terms], rest[terms:-3], rest[-3:]
-    steps = spectra.shape[1]
-    some = 8
+    outs, (spectra, sums, held) = rest[-3 - len(owners) : -3], rest[-3:]
+    earlier = rest[: -3 - len(owners)]
+    steps, size = spectra.shape[1], spectra.shape[3]
     core, o, g, ct = position()
+    whole = size == outer * span
+    base_owner = 0 if whole else (o // 2 if 0 in owners else 1 - o // 2) * 2
     within = any(block[0] for block in blocks)
     across = any(not block[0] for block in blocks)
 
@@ -365,25 +375,28 @@
             device = lax.rem(ct - dc + per_ct, per_ct) * PAIR + (g ^ dg)
             base = (part * per_ct * PAIR + device) * JOIN
             wanted = None
-            if across:
-                side = 1 - core if far else core
+            side = 1 - core if far else core
+            if far:
                 wanted = (side == 1) | (lax.rem(base // TILE, 2) == core)
-                if within and not far:
-                    wanted = None
-                base = base + side * own
+            base = base + side * own
 
             def bring(source=source, base=base, n=n):
                 for item in range(JOIN):
 
                     def spread(m, carry, item=item):
-                        for u in range(some):
-                            real = source[n * JOIN + item, m * some + u, 0].astype(jnp.float32)
-                            imag = source[n * JOIN + item, m * some + u, 1].astype(jnp.float32)
+                        for u in range(8):
+                            parts = []
+                            for c in range(2):
+                                value = source[n * JOIN + item, m * 8 + u, c].astype(jnp.float32)
+                                if not whole:
+                                    value = jnp.where(base_owner == 0, value[:size], value[size:])
+                                parts.append(value)
+                            real, imag = parts
                             for which, value in enumerate((real, imag, real + imag, imag - real)):
-                                spectra[base + item, m * some + u, which] = value
+                                spectra[base + item, m * 8 + u, which] = value
                         return carry
 
-                    lax.fori_loop(0, steps // some, spread, 0)
+                    lax.fori_loop(0, steps // 8, spread, 0)
 
             if wanted is None:
                 bring()
@@ -392,8 +405,7 @@
 
     high = lax.broadcasted_iota(jnp.int32, (1, LANES), 1) < RADIX
     rows_outer = pairs_in(blocks) * span
-    size = outer * span
-    unroll = 4
+    unroll = 4 if whole else 8
 
     def block(left, right, pairs, first_row):
         def over(one, two, acc, sign):
@@ -420,9 +432,9 @@
         for at in range(count):
             folded = imag[at] + pltpu.roll(imag[at], RADIX, 1)
             both = jnp.where(high, held[1, at], folded)
-            for o in range(outer):
-                row = o * rows_outer + first_row + at * span
-                sums[pl.ds(pl.multiple_of(row, span), span), :] = both[o * span : (o + 1) * span]
+            for u in range(size // span):
+                row = u * rows_outer + first_row + at * span
+                sums[pl.ds(pl.multiple_of(row, span), span), :] = both[u * span : (u + 1) * span]
 
     done = 0
     while done < len(blocks):
@@ -436,60 +448,72 @@
             left, right = chosen(t, [b[1] for b in run]), chosen(t, [b[2] for b in run])
             if not kind[0]:
                 left, right = TILE * (left + core), own + TILE * right
-            elif across:
+            else:
                 left, right = core * own + TILE * left, core * own + TILE * right
-            else:
-                left, right = TILE * left, TILE * right
             block(left, right, kind[1], row + t * len(kind[1]) * span)
             return carry
 
         lax.fori_loop(0, len(run), step, 0)
         done = end
 
-    for r in range(outer):
-        base = pl.multiple_of(lax.rem(o + r, outer) * rows_outer, 16)
-        outs[r][...] = sums[pl.ds(base, rows_outer), :].astype(outs[r].dtype)
-    if terms:
-        total = earlier[0][...].astype(jnp.float32)
-        for term in earlier[1:]:
-            total = total + term[...].astype(jnp.float32)
-        outs[outer][...] = total
-
-
-def correlate(arrays, sources_at, blocks, own, sizes, name, earlier=()):
+    before = earlier[0].shape[0] if earlier else 0
+    for n, x in enumerate(owners):
+        at = pl.multiple_of(((o ^ x) - base_owner) * rows_outer, 16)
+        outs[n][before:, :] = sums[pl.ds(at, rows_outer), :].astype(outs[n].dtype)
+        if earlier:
+            outs[n][:before, :] = earlier[n][...]
+
+
+def correlate(arrays, sources_at, blocks, own, owners, sizes, name, earlier=()):
     outer, span, _ = sizes
     _, steps, _, size, _ = arrays[0].shape
-    inputs = own if all(block[0] for block in blocks) else 2 * own
+    if len(owners) < outer:
+        size = 2 * span
     rows = pairs_in(blocks) * span
-    shapes = []
-    for r in range(outer):
-        dtype = jnp.float32 if r == 0 else jnp.bfloat16
-        shapes.append(jax.ShapeDtypeStruct((rows, LANES), dtype))
-    shapes += [jax.ShapeDtypeStruct(x.shape, jnp.float32) for x in earlier[:1]]
-    layout = (sources_at, blocks, own, len(earlier)) + sizes
+    before = earlier[0].shape[0] if earlier else 0
+    types = [jnp.bfloat16 if x else jnp.float32 for x in owners]
+    scratch = pltpu.VMEM((2 * own, steps, 4, size, LANES), jnp.float32)
+    layout = (sources_at, blocks, own, owners) + sizes
     return pl.pallas_call(
         functools.partial(correlate_kernel, layout),
-        out_shape=shapes,
+        out_shape=[jax.ShapeDtypeStruct((before + rows, LANES), dtype) for dtype in types],
         in_specs=[VMEM] * (len(arrays) + len(earlier)),
-        out_specs=[VMEM] * len(shapes),
+        out_specs=[VMEM] * len(owners),
         scratch_shapes=[
-            pltpu.VMEM((inputs, steps, 4, size, LANES), jnp.float32),
-            pltpu.VMEM((outer * rows, LANES), jnp.float32),
-            pltpu.VMEM((2, TILE * TILE, outer * span, LANES), jnp.float32),
+            scratch,
+            pltpu.VMEM((size // span * rows, LANES), jnp.float32),
+            pltpu.VMEM((2, TILE * TILE, size, LANES), jnp.float32),
         ],
-        compiler_params=params(8 + inputs * steps * 4 * size * LANES * 4 // 2**20),
+        compiler_params=params(12 + 2 * own * steps * 4 * size * LANES * 4 // 2**20),
         cost_estimate=cost(10**6, 2**18),
         name=name,
     )(*arrays, *earlier)
 
 
-def assemble_kernel(own, outer, span, scale, sets, order, counts, *refs):
+def summed(early, late):
+    def kernel(*refs):
+        out = refs[-1]
+        split = refs[0].shape[0]
+        out[:split, :] = refs[0][...].astype(jnp.float32) + refs[1][...].astype(jnp.float32)
+        out[split:, :] = refs[2][...].astype(jnp.float32) + refs[3][...].astype(jnp.float32)
+
+    rows = early[0].shape[0] + late[0].shape[0]
+    return pl.pallas_call(
+        kernel,
+        out_shape=jax.ShapeDtypeStruct((rows, LANES), jnp.float32),
+        in_specs=[VMEM] * 4,
+        out_specs=VMEM,
+        compiler_params=params(8),
+        cost_estimate=cost(10**6, 36 * 2**20),
+        name="sum_far",
+    )(*early, *late)
+
+
+def assemble_kernel(own, span, scale, sets, order, terms, *refs):
     out, joined = refs[-2:]
-    sources, at = [], 0
-    for count in counts:
-        sources.append(refs[at : at + count])
-        at += count
-    near, far = sources[: len(sets)], sources[len(sets) :]
+    count = len(refs) // 2 - 1
+    near = [[(refs[n], low) for n, low in term] for term in terms]
+    far = [[(refs[count + n], low) for n, low in term] for term in terms]
     lane = lax.broadcasted_iota(jnp.int32, (1, LANES), 1)
     high = lane < RADIX
     mirror = jnp.where(high, 1.0, -1.0).astype(jnp.float32)
@@ -498,9 +522,10 @@
     mine_at = pl.multiple_of(me * own * span, 8)
 
     def added(parts, low, rows):
-        total = parts[0][low : low + rows, :].astype(jnp.float32)
-        for part in parts[1:]:
-            total = total + part[low : low + rows, :].astype(jnp.float32)
+        total = None
+        for ref, first in parts:
+            term = ref[first + low : first + low + rows, :].astype(jnp.float32)
+            total = term if total is None else total + term
         return total * scale
 
     def put(value, places, base=0):
@@ -570,20 +595,17 @@
     lax.fori_loop(0, own // 4, emit_some, 0)
 
 
-def assemble(near, far, sets, order, own, span, scale):
-    outer = len(near[1])
-    counts = [len(arrays) for arrays in near + far]
-    sources = [x for arrays in near + far for x in arrays]
+def assemble(near, far, terms, sets, order, own, span, scale):
     return pl.pallas_call(
-        functools.partial(assemble_kernel, own, outer, span, scale, sets, order, counts),
+        functools.partial(assemble_kernel, own, span, scale, sets, order, terms),
         out_shape=jax.ShapeDtypeStruct((2, own, 2 * own, span * RADIX), jnp.float32),
-        in_specs=[VMEM] * len(sources),
+        in_specs=[VMEM] * (len(near) + len(far)),
         out_specs=VMEM,
         scratch_shapes=[pltpu.VMEM((own * 2 * own * span, LANES), jnp.float32)],
-        compiler_params=params(10),
+        compiler_params=params(12),
         cost_estimate=cost(10**6, 2**18),
         name="assemble",
-    )(*sources)
+    )(*near, *far)
 
 
 def fast_fits(in_count, frame_count):
@@ -596,7 +618,8 @@
     return (
         frame_count >= TAPS
         and frame_count % (2 * SOME) == 0
-        and span in (2, 4, 8)
+        and outer == 4
+        and span == 4
         and outer * span % 16 == 0
         and own % (PAIR * JOIN * 2 * TILE // 4) == 0
         and in_count == PAIR * JOIN * 2
@@ -626,8 +649,8 @@
     tables = [jnp.asarray(t) for t in tables + [np.concatenate([base, base], axis=1)]]
 
     parts = half // JOIN
-    picked = pick(voltages)
-    sends, keeps = picked[:parts], picked[parts:]
+    sends = pick(voltages, False)
+    keeps = pick(follow(voltages, sends[0]), True)
     recvs = [lax.ppermute(block, "tm", swap) for block in sends]
     halos, lates = [], []
     for c in range(parts):
@@ -656,38 +679,40 @@
             arrays.append(block)
         received.append(arrays)
 
-    def along(parts, after):
-        moved = [parts[0]]
-        for r in range(1, outer):
-            route = [(i, (i + r * PAIR) % tm) for i in range(tm)]
-            moved.append(lax.ppermute(follow(parts[r], after(r)), "tm", route))
-        return moved
+    def along(block, x):
+        route = [(i, ((i // PAIR) ^ x) * PAIR + i % PAIR) for i in range(tm)]
+        return lax.ppermute(block, "tm", route)
 
     near = [joined([follow(block, spectra[0]) for block in received[0]])]
     far = [lax.ppermute(near[0], "stn", cores)]
     early = correlate(
-        near + far, [(False, 0), (True, 0)], sets[0], own // parts, sizes, "correlate_early"
+        near + far, [(False, 0), (True, 0)], sets[0], own // parts, (0, 1, 2, 3), sizes,
+        "correlate_early",
     )
-    early = along(early, lambda r: [])
-    near.append(joined([follow(block, early[1:3]) for block in received[1]]))
+    early = [*early[:2], *[along(early[x], x) for x in (2, 3)]]
+    near.append(joined([follow(block, early[2:]) for block in received[1]]))
     far.append(lax.ppermute(near[1], "stn", cores))
     sources_at = [(False, c) for c in range(parts)] + [(True, c) for c in range(parts)]
-    own_late = correlate(near, sources_at[:parts], sets[1], own, sizes, "correlate_own")
-    own_late = along(own_late, lambda r: [far[1], early[r]])
-    *cross_late, early = correlate(
-        near + far, sources_at, sets[2], own, sizes, "correlate_cross", early
+    beyond = correlate(near + far, sources_at, sets[1], own, (2, 3), sizes, "correlate_far")
+    near[0] = follow(near[0], beyond[0])
+    kept, beside = correlate(
+        near + far, sources_at, sets[1], own, (0, 1), sizes, "correlate_near", early[:2]
     )
-    cross_late = along(cross_late, lambda r: own_late[r])
-    mine = [[early], own_late, cross_late]
-    theirs = [[lax.ppermute(block, "stn", cores) for block in part] for part in (mine[0], mine[2])]
-    theirs.insert(1, [])
+    beyond = [along(block, x) for block, x in zip(beyond, (2, 3))]
+    beside = along(beside, 1)
+    beyond = summed(early[2:], beyond)
+    mine = [kept, beside, beyond]
+    after = [kept, follow(beside, beyond), beyond]
+    theirs = [lax.ppermute(block, "stn", cores) for block in after]
+    first = pairs_in(sets[0]) * span
+    terms = [[(n, low) for n in range(3)] for low in (0, first)]
     order = []
     for part in range(parts):
         for device in range(per_ct * PAIR):
             start = device // PAIR * in_count + device % PAIR * half + part * JOIN
             order += range(start, start + JOIN)
     scale = 1.0 / (tm * frame_count)
-    result = assemble(mine, theirs, sets, order, own, span, scale)
+    result = assemble(mine, theirs, terms, sets, order, own, span, scale)
     return result.transpose(0, 3, 1, 2)
 
 

time: 103 us -> 114 us (1.11)
  waiting for transfers between devices: 29.6 us -> 46.8 us
  starting transfers between devices: 33 us -> 27.5 us
  Pallas kernels: 38.4 us -> 36.7 us
    ppermute x2, waiting for transfers between devices: 0.01 us -> 8.77 us  [fast(): halos.append(lax.ppermute(jnp.where(g == 1, keeps[c], recv), 'tm', onward))]
    ppermute x14 -> x8, starting transfers between devices: 14.3 us -> 9.99 us  [the longest x5 9.43 us: along(): return lax.ppermute(block, 'tm', route)]
    ppermute x2, waiting for transfers between devices: 14.3 us -> 18.3 us  [fast(): recvs = [lax.ppermute(block, 'tm', swap) for block in sends]]
    ppermute x14 -> x8, waiting for transfers between devices: 13.3 us -> 17.1 us  [the longest x5 15.3 us: along(): return lax.ppermute(block, 'tm', route)]
    pallas_call x5 -> x7, Pallas kernels: 22.8 us -> 20.1 us  [the longest x3 15.8 us: correlate(): pl.pallas_call(functools.partial(correlate_kernel, layout), out_shape=[ja...]
    ppermute x1, waiting for transfers between devices: 0.01 us -> 2.65 us  [fast(): far.append(lax.ppermute(near[1], 'stn', cores))]
    ppermute x6, waiting for transfers between devices: 1.92 us -> 0.02 us  [fast(): block = lax.ppermute(block, ('tm', 'ct'), route)]
  transfers between devices with their start and end apart: 26 -> 20, of which waited for: 10 -> 8; matrix products, arithmetic and copies ran while one was open for 0% -> 0% of each run, Pallas kernels for 30% -> 24%
where the time goes in v12:
time: 114 us
  waiting for transfers between devices  46.8 us (41%)
  Pallas kernels  36.7 us (32%)
  starting transfers between devices  27.5 us (24%)
  local copies, waits for them, and re-layouts  1.62 us (1%)
  other arithmetic  1.16 us (1%)
    ppermute x2, waiting for transfers between devices, fast(): recvs = [lax.ppermute(block, 'tm', swap) for block in sends]  18.3 us
    pallas_call x4, Pallas kernels, filterbank(): pl.pallas_call(kernel, out_shape=[jax.ShapeDtypeStruct(shape, jnp.bfloat1...  16.3 us
    pallas_call x3, Pallas kernels, correlate(): pl.pallas_call(functools.partial(correlate_kernel, layout), out_shape=[ja...  15.8 us
    ppermute x5, waiting for transfers between devices, along(): return lax.ppermute(block, 'tm', route)  15.3 us
    ppermute x5, starting transfers between devices, along(): return lax.ppermute(block, 'tm', route)  9.43 us
    ppermute x2, waiting for transfers between devices, fast(): halos.append(lax.ppermute(jnp.where(g == 1, keeps[c], recv), 'tm', onward))  8.77 us
    ppermute x2, starting transfers between devices, fast(): halos.append(lax.ppermute(jnp.where(g == 1, keeps[c], recv), 'tm', onward))  7.25 us
    ppermute x6, starting transfers between devices, fast(): block = lax.ppermute(block, ('tm', 'ct'), route)  7.11 us
  transfers between devices with their start and end apart: 20, of which 8 were waited for; matrix products, arithmetic and copies ran while one was open for 0% of the time, Pallas kernels for 24%

profile of v12, /device:TPU:0, one launch (start us, length us, event | category | flops | bytes accessed | tf_op | source)
XLA Modules:
  0.0 113.9 jit_solution(12791618005007635319)
XLA Ops:
  0.0 1.6 %copy-done = bf16[2,8,65536]{2,1,0:T(8,128)(2,1)S(1)} copy-done((bf16[2,8,65536]{2,1,0:T(8,128)(2,1)S(1)}, bf16[2,8,65536]{2,1,0:T(8,128)(2,1)}, u32[]{:S(2)}) %copy-start) | copy-done | bytes 2097176
  1.6 0.0 copy-start.5
  1.6 0.0 copy-start.6
  1.6 1.7 %pick.2 = (bf16[2,2,512,128]{3,2,1,0:T(8,128)(2,1)}, bf16[2,2,512,128]{3,2,1,0:T(8,128)(2,1)}) custom-call(bf16[2,8,65536]{2,1,0:T(8,128)(2,1)S(1)} %copy-done), custom_call_target="tpu_custom_call" | custom-call | flops 1000000 | bytes 262144 | tf_op jit(solution)/shard_map/pick/pallas_call | solution.py:121
  3.4 2.9 %collective-permute-start = (bf16[2,2,512,128]{3,2,1,0:T(8,128)(2,1)}, bf16[2,2,512,128]{3,2,1,0:T(8,128)(2,1)}, u32[]{:S(2)}, u32[]{:S(2)}) collective-permute-start(bf16[2,2,512,128]{3,2,1,0:T(8,128)(2,1)} %get-tuple-element.50), channel_id=1, source_target_pairs={{0,2},{2,0},{4,6},{6,4},{8,10},{10,8},{12,14},{14,12},{1,3},{3,1},... | collective-permute-start | bytes 1572872 | tf_op jit(solution)/shard_map/ppermute | solution.py:654
  6.3 0.0 collective-permute-start.2
  6.4 0.8 pick.3
  7.1 12.3 %collective-permute-done.refs_2_.refs_3_ = bf16[2,2,512,128]{3,2,1,0:T(8,128)(2,1)} collective-permute-done((bf16[2,2,512,128]{3,2,1,0:T(8,128)(2,1)}, bf16[2,2,512,128]{3,2,1,0:T(8,128)(2,1)}, u32[]{:S(2)}, u32[]{:S(2)}) %collective-permute-start) | collective-permute-done | bytes 524320 | tf_op jit(solution)/shard_map/ppermute | solution.py:654
  19.4 4.3 %filterbank_late.2 = (bf16[2,8,2,16,128]{4,3,2,1,0:T(8,128)(2,1)S(1)}, bf16[2,8,2,16,128]{4,3,2,1,0:T(8,128)(2,1)S(1)}, bf16[2,8,2,16,128]{4,3,2,1,0:T(8,128)(2,1)S(1)}, bf16[2,8,2,16,128]{4,3,2,1,0:T(8,128)(2,1)S(1)}) custom-call(s32[8]{0:T(128)S(1)} %copy-done.7, bf16[2,2,512,128]{3,2,1,0:T(8,128)(2,1)S(1)} %get-tuple-element.52.refs_1_.refs_2_, ...), custom_call_target="tpu_custom_call" | custom-call | flops 1000000 | bytes 262144 | tf_op jit(solution)/shard_map/filterbank_late/pallas_call | solution.py:311
  23.7 6.0 %collective-permute-done.2.refs_2_.refs_3_ = bf16[2,2,512,128]{3,2,1,0:T(8,128)(2,1)S(1)} collective-permute-done((bf16[2,2,512,128]{3,2,1,0:T(8,128)(2,1)}, bf16[2,2,512,128]{3,2,1,0:T(8,128)(2,1)S(1)}, u32[]{:S(2)}, u32[]{:S(2)}) %collective-permute-start.2) | collective-permute-done | bytes 524320 | tf_op jit(solution)/shard_map/ppermute | solution.py:654
  29.7 1.1 broadcast_select_fusion.1
  30.8 3.8 %collective-permute-start.1 = (bf16[2,2,512,128]{3,2,1,0:T(8,128)(2,1)S(1)}, bf16[2,2,512,128]{3,2,1,0:T(8,128)(2,1)S(1)}, u32[]{:S(2)}, u32[]{:S(2)}) collective-permute-start(bf16[2,2,512,128]{3,2,1,0:T(8,128)(2,1)S(1)} %broadcast_select_fusion.1), channel_id=1, source_target_pairs={{0,4},{2,6},{4,8},{6,10},{8,12},{10,14},{1,5},{3,7},{5,9},{7,11},{... | collective-permute-start | bytes 1572872 | tf_op jit(solution)/shard_map/ppermute | solution.py:658
  34.6 0.1 broadcast_select_fusion
  34.6 3.5 %collective-permute-start.3 = (bf16[2,2,512,128]{3,2,1,0:T(8,128)(2,1)S(1)}, bf16[2,2,512,128]{3,2,1,0:T(8,128)(2,1)S(1)}, u32[]{:S(2)}, u32[]{:S(2)}) collective-permute-start(bf16[2,2,512,128]{3,2,1,0:T(8,128)(2,1)S(1)} %broadcast_select_fusion), channel_id=1, source_target_pairs={{0,4},{2,6},{4,8},{6,10},{8,12},{10,14},{1,5},{3,7},{5,9},{7,11},{... | collective-permute-start | bytes 1572872 | tf_op jit(solution)/shard_map/ppermute | solution.py:658
  38.1 8.8 %collective-permute-done.1.refs_1_ = bf16[2,2,512,128]{3,2,1,0:T(8,128)(2,1)S(1)} collective-permute-done((bf16[2,2,512,128]{3,2,1,0:T(8,128)(2,1)S(1)}, bf16[2,2,512,128]{3,2,1,0:T(8,128)(2,1)S(1)}, u32[]{:S(2)}, u32[]{:S(2)}) %collective-permute-start.1) | collective-permute-done | bytes 524320 | tf_op jit(solution)/shard_map/ppermute | solution.py:658
  46.9 4.3 %filterbank_early.2 = (bf16[2,16,2,16,128]{4,3,2,1,0:T(8,128)(2,1)S(1)}, bf16[2,16,2,16,128]{4,3,2,1,0:T(8,128)(2,1)S(1)}, bf16[2,16,2,16,128]{4,3,2,1,0:T(8,128)(2,1)S(1)}, bf16[2,16,2,16,128]{4,3,2,1,0:T(8,128)(2,1)S(1)}) custom-call(s32[8]{0:T(128)S(1)} %copy-done.7, bf16[2,2,512,128]{3,2,1,0:T(8,128)(2,1)S(1)} %collective-permute-done.1.refs_1_, ...), custom_call_target="tpu_custom_call" | custom-call | flops 1000000 | bytes 262144 | tf_op jit(solution)/shard_map/filterbank_early/pallas_call | solution.py:311
  51.2 1.5 %collective-permute-start.6 = (bf16[2,16,2,16,128]{4,3,2,1,0:T(8,128)(2,1)S(1)}, bf16[2,16,2,16,128]{4,3,2,1,0:T(8,128)(2,1)S(1)}, u32[]{:S(2)}, u32[]{:S(2)}) collective-permute-start(bf16[2,16,2,16,128]{4,3,2,1,0:T(8,128)(2,1)S(1)} %get-tuple-element.73), channel_id=1, source_target_pairs={{0,3},{1,2},{2,1},{3,0},{4,7},{5,6},{6,5},{7,4},{8,11},{9,10},{10,... | collective-permute-start | bytes 786440 | tf_op jit(solution)/shard_map/ppermute | solution.py:678
  52.7 1.6 %collective-permute-start.5 = (bf16[2,16,2,16,128]{4,3,2,1,0:T(8,128)(2,1)S(1)}, bf16[2,16,2,16,128]{4,3,2,1,0:T(8,128)(2,1)S(1)}, u32[]{:S(2)}, u32[]{:S(2)}) collective-permute-start(bf16[2,16,2,16,128]{4,3,2,1,0:T(8,128)(2,1)S(1)} %get-tuple-element.71), channel_id=1, source_target_pairs={{0,2},{1,3},{2,0},{3,1},{4,6},{5,7},{6,4},{7,5},{8,10},{9,11},{10,... | collective-permute-start | bytes 786440 | tf_op jit(solution)/shard_map/ppermute | solution.py:678
  54.2 0.5 collective-permute-start.4
  54.7 3.7 %filterbank_late.3 = (bf16[2,8,2,16,128]{4,3,2,1,0:T(8,128)(2,1)S(1)}, bf16[2,8,2,16,128]{4,3,2,1,0:T(8,128)(2,1)S(1)}, bf16[2,8,2,16,128]{4,3,2,1,0:T(8,128)(2,1)S(1)}, bf16[2,8,2,16,128]{4,3,2,1,0:T(8,128)(2,1)S(1)}) custom-call(s32[8]{0:T(128)S(1)} %copy-done.7, bf16[2,2,512,128]{3,2,1,0:T(8,128)(2,1)S(1)} %get-tuple-element.60.refs_1_.refs_2_, ...), custom_call_target="tpu_custom_call" | custom-call | flops 1000000 | bytes 262144 | tf_op jit(solution)/shard_map/filterbank_late/pallas_call | solution.py:311
  58.5 0.0 collective-permute-done.3.refs_1_
  58.5 4.0 %filterbank_early.3 = (bf16[2,16,2,16,128]{4,3,2,1,0:T(8,128)(2,1)S(1)}, bf16[2,16,2,16,128]{4,3,2,1,0:T(8,128)(2,1)S(1)}, bf16[2,16,2,16,128]{4,3,2,1,0:T(8,128)(2,1)S(1)}, bf16[2,16,2,16,128]{4,3,2,1,0:T(8,128)(2,1)S(1)}) custom-call(s32[8]{0:T(128)S(1)} %copy-done.7, bf16[2,2,512,128]{3,2,1,0:T(8,128)(2,1)S(1)} %collective-permute-done.3.refs_1_, ...), custom_call_target="tpu_custom_call" | custom-call | flops 1000000 | bytes 262144 | tf_op jit(solution)/shard_map/filterbank_early/pallas_call | solution.py:311
  62.5 0.0 collective-permute-done.6.refs_3_
  62.5 0.2 join.2.refs_0_
  62.7 0.1 collective-permute-start.7
  62.8 1.5 %collective-permute-start.12 = (bf16[2,16,2,16,128]{4,3,2,1,0:T(8,128)(2,1)S(1)}, bf16[2,16,2,16,128]{4,3,2,1,0:T(8,128)(2,1)S(1)}, u32[]{:S(2)}, u32[]{:S(2)}) collective-permute-start(bf16[2,16,2,16,128]{4,3,2,1,0:T(8,128)(2,1)S(1)} %get-tuple-element.85), channel_id=1, source_target_pairs={{0,3},{1,2},{2,1},{3,0},{4,7},{5,6},{6,5},{7,4},{8,11},{9,10},{10,... | collective-permute-start | bytes 786440 | tf_op jit(solution)/shard_map/ppermute | solution.py:678
  64.3 1.6 %collective-permute-start.11 = (bf16[2,16,2,16,128]{4,3,2,1,0:T(8,128)(2,1)S(1)}, bf16[2,16,2,16,128]{4,3,2,1,0:T(8,128)(2,1)S(1)}, u32[]{:S(2)}, u32[]{:S(2)}) collective-permute-start(bf16[2,16,2,16,128]{4,3,2,1,0:T(8,128)(2,1)S(1)} %get-tuple-element.82), channel_id=1, source_target_pairs={{0,2},{1,3},{2,0},{3,1},{4,6},{5,7},{6,4},{7,5},{8,10},{9,11},{10,... | collective-permute-start | bytes 786440 | tf_op jit(solution)/shard_map/ppermute | solution.py:678
  65.8 0.5 collective-permute-start.10
  66.3 4.0 %correlate_early.1 = (f32[272,128]{1,0:T(8,128)S(1)}, bf16[272,128]{1,0:T(8,128)(2,1)S(1)}, bf16[272,128]{1,0:T(8,128)(2,1)S(1)}, bf16[272,128]{1,0:T(8,128)(2,1)S(1)}) custom-call(bf16[8,16,2,16,128]{4,3,2,1,0:T(8,128)(2,1)S(1)} %join.2.refs_0_, bf16[8,16,2,16,128]{4,3,2,1,0:T(8,128)(2,1)S(1)} %collective-permute-done.7.refs_1_.refs_2_), custom_call_target="tpu_custom_call" | custom-call | flops 1000000 | bytes 262144 | tf_op jit(solution)/shard_map/correlate_early/pallas_call | solution.py:477
  70.3 3.6 %collective-permute-start.8 = (bf16[272,128]{1,0:T(8,128)(2,1)S(1)}, bf16[272,128]{1,0:T(8,128)(2,1)S(1)}, u32[]{:S(2)}, u32[]{:S(2)}) collective-permute-start(bf16[272,128]{1,0:T(8,128)(2,1)S(1)} %get-tuple-element.75), channel_id=1, source_target_pairs={{0,8},{2,10},{4,12},{6,14},{8,0},{10,2},{12,4},{14,6},{1,9},{3,11}... | collective-permute-start | bytes 208904 | tf_op jit(solution)/shard_map/ppermute | solution.py:684
  73.9 1.3 %collective-permute-start.9 = (bf16[272,128]{1,0:T(8,128)(2,1)S(1)}, bf16[272,128]{1,0:T(8,128)(2,1)S(1)}, u32[]{:S(2)}, u32[]{:S(2)}) collective-permute-start(bf16[272,128]{1,0:T(8,128)(2,1)S(1)} %get-tuple-element.76), channel_id=1, source_target_pairs={{0,12},{2,14},{4,8},{6,10},{8,4},{10,6},{12,0},{14,2},{1,13},{3,15... | collective-permute-start | bytes 208904 | tf_op jit(solution)/shard_map/ppermute | solution.py:684
  75.2 1.6 %collective-permute-done.8.refs_0_ = bf16[272,128]{1,0:T(8,128)(2,1)S(1)} collective-permute-done((bf16[272,128]{1,0:T(8,128)(2,1)S(1)}, bf16[272,128]{1,0:T(8,128)(2,1)S(1)}, u32[]{:S(2)}, u32[]{:S(2)}) %collective-permute-start.8) | collective-permute-done | bytes 69664 | tf_op jit(solution)/shard_map/ppermute | solution.py:684
  76.8 3.3 %collective-permute-done.9.refs_1_ = bf16[272,128]{1,0:T(8,128)(2,1)S(1)} collective-permute-done((bf16[272,128]{1,0:T(8,128)(2,1)S(1)}, bf16[272,128]{1,0:T(8,128)(2,1)S(1)}, u32[]{:S(2)}, u32[]{:S(2)}) %collective-permute-start.9) | collective-permute-done | bytes 69664 | tf_op jit(solution)/shard_map/ppermute | solution.py:684
  80.1 0.2 join.3.refs_1_
  80.3 0.1 collective-permute-start.13
  80.4 2.6 %collective-permute-done.13.refs_3_ = bf16[8,16,2,16,128]{4,3,2,1,0:T(8,128)(2,1)S(1)} collective-permute-done((bf16[8,16,2,16,128]{4,3,2,1,0:T(8,128)(2,1)S(1)}, bf16[8,16,2,16,128]{4,3,2,1,0:T(8,128)(2,1)S(1)}, u32[]{:S(2)}, u32[]{:S(2)}) %collective-permute-start.13) | collective-permute-done | bytes 1048608 | tf_op jit(solution)/shard_map/ppermute | solution.py:694
  83.0 5.9 %correlate_far.1 = (bf16[784,128]{1,0:T(8,128)(2,1)S(1)}, bf16[784,128]{1,0:T(8,128)(2,1)S(1)}) custom-call(bf16[8,16,2,16,128]{4,3,2,1,0:T(8,128)(2,1)S(1)} %join.2.refs_0_, bf16[8,16,2,16,128]{4,3,2,1,0:T(8,128)(2,1)S(1)} %join.3.refs_1_, bf16[8,16,2,16,128]{4,3,2,1,0:T(8,128)(2,1)S(1)} %collective-permute-done.7.refs_1_.refs_2_, ...), custom_call_target="tpu_custom_call" | custom-call | flops 1000000 | bytes 262144 | tf_op jit(solution)/shard_map/correlate_far/pallas_call | solution.py:477
  88.9 2.6 %collective-permute-start.16 = (bf16[784,128]{1,0:T(8,128)(2,1)S(1)}, bf16[784,128]{1,0:T(8,128)(2,1)S(1)}, u32[]{:S(2)}, u32[]{:S(2)}) collective-permute-start(bf16[784,128]{1,0:T(8,128)(2,1)S(1)} %get-tuple-element.93), channel_id=1, source_target_pairs={{0,12},{2,14},{4,8},{6,10},{8,4},{10,6},{12,0},{14,2},{1,13},{3,15... | collective-permute-start | bytes 602120 | tf_op jit(solution)/shard_map/ppermute | solution.py:684
  91.6 0.2 collective-permute-start.15
  91.8 5.9 %correlate_near.1 = (f32[1056,128]{1,0:T(8,128)S(1)}, bf16[1056,128]{1,0:T(8,128)(2,1)S(1)}) custom-call(bf16[8,16,2,16,128]{4,3,2,1,0:T(8,128)(2,1)S(1)} %join.2.refs_0_, bf16[8,16,2,16,128]{4,3,2,1,0:T(8,128)(2,1)S(1)} %join.3.refs_1_, bf16[8,16,2,16,128]{4,3,2,1,0:T(8,128)(2,1)S(1)} %collective-permute-done.7.refs_1_.refs_2_, ...), custom_call_target="tpu_custom_call" | custom-call | flops 1000000 | bytes 262144 | tf_op jit(solution)/shard_map/correlate_near/pallas_call | solution.py:477
  97.7 1.7 %collective-permute-start.14 = (bf16[1056,128]{1,0:T(8,128)(2,1)S(1)}, bf16[1056,128]{1,0:T(8,128)(2,1)S(1)}, u32[]{:S(2)}, u32[]{:S(2)}) collective-permute-start(bf16[1056,128]{1,0:T(8,128)(2,1)S(1)} %get-tuple-element.92), channel_id=1, source_target_pairs={{0,4},{2,6},{4,0},{6,2},{8,12},{10,14},{12,8},{14,10},{1,5},{3,7},... | collective-permute-start | bytes 811016 | tf_op jit(solution)/shard_map/ppermute | solution.py:684
  99.4 10.4 %collective-permute-done.15.refs_2_ = bf16[784,128]{1,0:T(8,128)(2,1)S(1)} collective-permute-done((bf16[784,128]{1,0:T(8,128)(2,1)S(1)}, bf16[784,128]{1,0:T(8,128)(2,1)S(1)}, u32[]{:S(2)}, u32[]{:S(2)}) %collective-permute-start.15) | collective-permute-done | bytes 200736 | tf_op jit(solution)/shard_map/ppermute | solution.py:684
  109.8 0.1 sum_far.1.refs_2_
  109.9 0.1 collective-permute-start.19
  110.0 0.0 collective-permute-done.14.refs_1_
  110.0 0.5 collective-permute-start.18
  110.5 1.8 %collective-permute-done.18.refs_4_ = bf16[1056,128]{1,0:T(8,128)(2,1)S(1)} collective-permute-done((bf16[1056,128]{1,0:T(8,128)(2,1)S(1)}, bf16[1056,128]{1,0:T(8,128)(2,1)S(1)}, u32[]{:S(2)}, u32[]{:S(2)}) %collective-permute-start.18) | collective-permute-done | bytes 270368 | tf_op jit(solution)/shard_map/ppermute | solution.py:706
  112.3 1.7 %assemble.1 = f32[2,16,32,256]{3,2,1,0:T(8,128)} custom-call(f32[1056,128]{1,0:T(8,128)S(1)} %get-tuple-element.91.refs_0_, bf16[1056,128]{1,0:T(8,128)(2,1)S(1)} %collective-permute-done.14.refs_1_, f32[1056,128]{1,0:T(8,128)S(1)} %sum_far.1.refs_2_, f32[1056,128]{1,0:T(8,128)S(1)} %collective-permute-done.17.refs_3_, ...), custom_call_target="tpu_custom_call" | custom-call | flops 1000000 | bytes 262144 | tf_op jit(solution)/shard_map/assemble/pallas_call | solution.py:599
  (23 shorter events, 0.1 us)
Async XLA Ops:
  0.0 1.6 %copy-start = (bf16[2,8,65536]{2,1,0:T(8,128)(2,1)S(1)}, bf16[2,8,65536]{2,1,0:T(8,128)(2,1)}, u32[]{:S(2)}) copy-start(bf16[2,8,65536]{2,1,0:T(8,128)(2,1)} %block.2) | copy-start | bytes 6291460
  1.6 4.8 %copy-start.1 = (bf16[2,8,65536]{2,1,0:T(8,128)(2,1)S(1)}, bf16[2,8,65536]{2,1,0:T(8,128)(2,1)}, u32[]{:S(2)}) copy-start(bf16[2,8,65536]{2,1,0:T(8,128)(2,1)} %block.2) | copy-start | bytes 6291460
  1.6 17.8 %copy-start.2 = (f32[16,64,128]{2,1,0:T(8,128)S(1)}, f32[16,64,128]{2,1,0:T(8,128)}, u32[]{:S(2)}) copy-start(f32[16,64,128]{2,1,0:T(8,128)} %constant.30.clone.refs_3_.refs_4_) | copy-start | bytes 1572868
  1.6 17.8 %copy-start.3 = (bf16[2,4,32,128]{3,2,1,0:T(8,128)(2,1)S(1)}, bf16[2,4,32,128]{3,2,1,0:T(8,128)(2,1)}, u32[]{:S(2)}) copy-start(bf16[2,4,32,128]{3,2,1,0:T(8,128)(2,1)} %constant.34.clone.refs_7_.refs_8_) | copy-start | bytes 196612
  1.6 17.8 %copy-start.4 = (f32[64,128]{1,0:T(8,128)S(1)}, f32[64,128]{1,0:T(8,128)}, u32[]{:S(2)}) copy-start(f32[64,128]{1,0:T(8,128)} %constant.33.clone.refs_6_.refs_7_) | copy-start | bytes 98308
  1.6 17.8 %copy-start.5 = (f32[64,128]{1,0:T(8,128)S(1)}, f32[64,128]{1,0:T(8,128)}, u32[]{:S(2)}) copy-start(f32[64,128]{1,0:T(8,128)} %constant.32.clone.refs_5_.refs_6_) | copy-start | bytes 98308
  1.6 17.8 %copy-start.6 = (bf16[128,128]{1,0:T(8,128)(2,1)S(1)}, bf16[128,128]{1,0:T(8,128)(2,1)}, u32[]{:S(2)}) copy-start(bf16[128,128]{1,0:T(8,128)(2,1)} %constant.31.clone.refs_4_.refs_5_) | copy-start | bytes 98308
  1.6 17.8 %copy-start.7 = (s32[8]{0:T(128)S(1)}, s32[8]{0:T(128)}, u32[]{:S(2)}) copy-start(s32[8]{0:T(128)} %refs_0_.7) | copy-start | bytes 100
  3.4 16.0 %collective-permute-start = (bf16[2,2,512,128]{3,2,1,0:T(8,128)(2,1)}, bf16[2,2,512,128]{3,2,1,0:T(8,128)(2,1)}, u32[]{:S(2)}, u32[]{:S(2)}) collective-permute-start(bf16[2,2,512,128]{3,2,1,0:T(8,128)(2,1)} %get-tuple-element.50), channel_id=1, source_target_pairs={{0,2},{2,0},{4,6},{6,4},{8,10},{10,8},{12,14},{14,12},{1,3},{3,1},... | collective-permute-start | bytes 1572872 | tf_op jit(solution)/shard_map/ppermute | solution.py:654
  6.3 23.4 %collective-permute-start.2 = (bf16[2,2,512,128]{3,2,1,0:T(8,128)(2,1)}, bf16[2,2,512,128]{3,2,1,0:T(8,128)(2,1)S(1)}, u32[]{:S(2)}, u32[]{:S(2)}) collective-permute-start(bf16[2,2,512,128]{3,2,1,0:T(8,128)(2,1)} %get-tuple-element.53), channel_id=1, source_target_pairs={{0,2},{2,0},{4,6},{6,4},{8,10},{10,8},{12,14},{14,12},{1,3},{3,1},... | collective-permute-start | bytes 1572872 | tf_op jit(solution)/shard_map/ppermute | solution.py:654
  30.8 16.1 %collective-permute-start.1 = (bf16[2,2,512,128]{3,2,1,0:T(8,128)(2,1)S(1)}, bf16[2,2,512,128]{3,2,1,0:T(8,128)(2,1)S(1)}, u32[]{:S(2)}, u32[]{:S(2)}) collective-permute-start(bf16[2,2,512,128]{3,2,1,0:T(8,128)(2,1)S(1)} %broadcast_select_fusion.1), channel_id=1, source_target_pairs={{0,4},{2,6},{4,8},{6,10},{8,12},{10,14},{1,5},{3,7},{5,9},{7,11},{... | collective-permute-start | bytes 1572872 | tf_op jit(solution)/shard_map/ppermute | solution.py:658
  34.6 23.9 %collective-permute-start.3 = (bf16[2,2,512,128]{3,2,1,0:T(8,128)(2,1)S(1)}, bf16[2,2,512,128]{3,2,1,0:T(8,128)(2,1)S(1)}, u32[]{:S(2)}, u32[]{:S(2)}) collective-permute-start(bf16[2,2,512,128]{3,2,1,0:T(8,128)(2,1)S(1)} %broadcast_select_fusion), channel_id=1, source_target_pairs={{0,4},{2,6},{4,8},{6,10},{8,12},{10,14},{1,5},{3,7},{5,9},{7,11},{... | collective-permute-start | bytes 1572872 | tf_op jit(solution)/shard_map/ppermute | solution.py:658
  51.2 11.3 %collective-permute-start.6 = (bf16[2,16,2,16,128]{4,3,2,1,0:T(8,128)(2,1)S(1)}, bf16[2,16,2,16,128]{4,3,2,1,0:T(8,128)(2,1)S(1)}, u32[]{:S(2)}, u32[]{:S(2)}) collective-permute-start(bf16[2,16,2,16,128]{4,3,2,1,0:T(8,128)(2,1)S(1)} %get-tuple-element.73), channel_id=1, source_target_pairs={{0,3},{1,2},{2,1},{3,0},{4,7},{5,6},{6,5},{7,4},{8,11},{9,10},{10,... | collective-permute-start | bytes 786440 | tf_op jit(solution)/shard_map/ppermute | solution.py:678
  52.7 9.8 %collective-permute-start.5 = (bf16[2,16,2,16,128]{4,3,2,1,0:T(8,128)(2,1)S(1)}, bf16[2,16,2,16,128]{4,3,2,1,0:T(8,128)(2,1)S(1)}, u32[]{:S(2)}, u32[]{:S(2)}) collective-permute-start(bf16[2,16,2,16,128]{4,3,2,1,0:T(8,128)(2,1)S(1)} %get-tuple-element.71), channel_id=1, source_target_pairs={{0,2},{1,3},{2,0},{3,1},{4,6},{5,7},{6,4},{7,5},{8,10},{9,11},{10,... | collective-permute-start | bytes 786440 | tf_op jit(solution)/shard_map/ppermute | solution.py:678
  54.2 8.3 %collective-permute-start.4 = (bf16[2,16,2,16,128]{4,3,2,1,0:T(8,128)(2,1)S(1)}, bf16[2,16,2,16,128]{4,3,2,1,0:T(8,128)(2,1)S(1)}, u32[]{:S(2)}, u32[]{:S(2)}) collective-permute-start(bf16[2,16,2,16,128]{4,3,2,1,0:T(8,128)(2,1)S(1)} %get-tuple-element.69), channel_id=1, source_target_pairs={{0,1},{1,0},{2,3},{3,2},{4,5},{5,4},{6,7},{7,6},{8,9},{9,8},{10,11... | collective-permute-start | bytes 786440 | tf_op jit(solution)/shard_map/ppermute | solution.py:678
  62.7 3.6 %collective-permute-start.7 = (bf16[8,16,2,16,128]{4,3,2,1,0:T(8,128)(2,1)S(1)}, bf16[8,16,2,16,128]{4,3,2,1,0:T(8,128)(2,1)S(1)}, u32[]{:S(2)}, u32[]{:S(2)}) collective-permute-start(bf16[8,16,2,16,128]{4,3,2,1,0:T(8,128)(2,1)S(1)} %join.2.refs_0_), channel_id=1, source_target_pairs={{0,16},{16,0},{1,17},{17,1},{2,18},{18,2},{3,19},{19,3},{4,20},{20... | collective-permute-start | bytes 3145736 | tf_op jit(solution)/shard_map/ppermute | solution.py:687
  62.8 12.4 %collective-permute-start.12 = (bf16[2,16,2,16,128]{4,3,2,1,0:T(8,128)(2,1)S(1)}, bf16[2,16,2,16,128]{4,3,2,1,0:T(8,128)(2,1)S(1)}, u32[]{:S(2)}, u32[]{:S(2)}) collective-permute-start(bf16[2,16,2,16,128]{4,3,2,1,0:T(8,128)(2,1)S(1)} %get-tuple-element.85), channel_id=1, source_target_pairs={{0,3},{1,2},{2,1},{3,0},{4,7},{5,6},{6,5},{7,4},{8,11},{9,10},{10,... | collective-permute-start | bytes 786440 | tf_op jit(solution)/shard_map/ppermute | solution.py:678
  64.3 15.8 %collective-permute-start.11 = (bf16[2,16,2,16,128]{4,3,2,1,0:T(8,128)(2,1)S(1)}, bf16[2,16,2,16,128]{4,3,2,1,0:T(8,128)(2,1)S(1)}, u32[]{:S(2)}, u32[]{:S(2)}) collective-permute-start(bf16[2,16,2,16,128]{4,3,2,1,0:T(8,128)(2,1)S(1)} %get-tuple-element.82), channel_id=1, source_target_pairs={{0,2},{1,3},{2,0},{3,1},{4,6},{5,7},{6,4},{7,5},{8,10},{9,11},{10,... | collective-permute-start | bytes 786440 | tf_op jit(solution)/shard_map/ppermute | solution.py:678
  65.8 14.3 %collective-permute-start.10 = (bf16[2,16,2,16,128]{4,3,2,1,0:T(8,128)(2,1)S(1)}, bf16[2,16,2,16,128]{4,3,2,1,0:T(8,128)(2,1)S(1)}, u32[]{:S(2)}, u32[]{:S(2)}) collective-permute-start(bf16[2,16,2,16,128]{4,3,2,1,0:T(8,128)(2,1)S(1)} %get-tuple-element.79), channel_id=1, source_target_pairs={{0,1},{1,0},{2,3},{3,2},{4,5},{5,4},{6,7},{7,6},{8,9},{9,8},{10,11... | collective-permute-start | bytes 786440 | tf_op jit(solution)/shard_map/ppermute | solution.py:678
  70.3 6.5 %collective-permute-start.8 = (bf16[272,128]{1,0:T(8,128)(2,1)S(1)}, bf16[272,128]{1,0:T(8,128)(2,1)S(1)}, u32[]{:S(2)}, u32[]{:S(2)}) collective-permute-start(bf16[272,128]{1,0:T(8,128)(2,1)S(1)} %get-tuple-element.75), channel_id=1, source_target_pairs={{0,8},{2,10},{4,12},{6,14},{8,0},{10,2},{12,4},{14,6},{1,9},{3,11}... | collective-permute-start | bytes 208904 | tf_op jit(solution)/shard_map/ppermute | solution.py:684
  73.9 6.2 %collective-permute-start.9 = (bf16[272,128]{1,0:T(8,128)(2,1)S(1)}, bf16[272,128]{1,0:T(8,128)(2,1)S(1)}, u32[]{:S(2)}, u32[]{:S(2)}) collective-permute-start(bf16[272,128]{1,0:T(8,128)(2,1)S(1)} %get-tuple-element.76), channel_id=1, source_target_pairs={{0,12},{2,14},{4,8},{6,10},{8,4},{10,6},{12,0},{14,2},{1,13},{3,15... | collective-permute-start | bytes 208904 | tf_op jit(solution)/shard_map/ppermute | solution.py:684
  80.3 2.7 %collective-permute-start.13 = (bf16[8,16,2,16,128]{4,3,2,1,0:T(8,128)(2,1)S(1)}, bf16[8,16,2,16,128]{4,3,2,1,0:T(8,128)(2,1)S(1)}, u32[]{:S(2)}, u32[]{:S(2)}) collective-permute-start(bf16[8,16,2,16,128]{4,3,2,1,0:T(8,128)(2,1)S(1)} %join.3.refs_1_), channel_id=1, source_target_pairs={{0,16},{16,0},{1,17},{17,1},{2,18},{18,2},{3,19},{19,3},{4,20},{20... | collective-permute-start | bytes 3145736 | tf_op jit(solution)/shard_map/ppermute | solution.py:694
  88.9 10.5 %collective-permute-start.16 = (bf16[784,128]{1,0:T(8,128)(2,1)S(1)}, bf16[784,128]{1,0:T(8,128)(2,1)S(1)}, u32[]{:S(2)}, u32[]{:S(2)}) collective-permute-start(bf16[784,128]{1,0:T(8,128)(2,1)S(1)} %get-tuple-element.93), channel_id=1, source_target_pairs={{0,12},{2,14},{4,8},{6,10},{8,4},{10,6},{12,0},{14,2},{1,13},{3,15... | collective-permute-start | bytes 602120 | tf_op jit(solution)/shard_map/ppermute | solution.py:684
  91.6 18.3 %collective-permute-start.15 = (bf16[784,128]{1,0:T(8,128)(2,1)S(1)}, bf16[784,128]{1,0:T(8,128)(2,1)S(1)}, u32[]{:S(2)}, u32[]{:S(2)}) collective-permute-start(bf16[784,128]{1,0:T(8,128)(2,1)S(1)} %get-tuple-element.87), channel_id=1, source_target_pairs={{0,8},{2,10},{4,12},{6,14},{8,0},{10,2},{12,4},{14,6},{1,9},{3,11}... | collective-permute-start | bytes 602120 | tf_op jit(solution)/shard_map/ppermute | solution.py:684
  97.7 12.2 %collective-permute-start.14 = (bf16[1056,128]{1,0:T(8,128)(2,1)S(1)}, bf16[1056,128]{1,0:T(8,128)(2,1)S(1)}, u32[]{:S(2)}, u32[]{:S(2)}) collective-permute-start(bf16[1056,128]{1,0:T(8,128)(2,1)S(1)} %get-tuple-element.92), channel_id=1, source_target_pairs={{0,4},{2,6},{4,0},{6,2},{8,12},{10,14},{12,8},{14,10},{1,5},{3,7},... | collective-permute-start | bytes 811016 | tf_op jit(solution)/shard_map/ppermute | solution.py:684
  99.4 12.9 %collective-permute-start.17 = (f32[1056,128]{1,0:T(8,128)S(1)}, f32[1056,128]{1,0:T(8,128)S(1)}, u32[]{:S(2)}, u32[]{:S(2)}) collective-permute-start(f32[1056,128]{1,0:T(8,128)S(1)} %get-tuple-element.91.refs_0_), channel_id=1, source_target_pairs={{0,16},{16,0},{1,17},{17,1},{2,18},{18,2},{3,19},{19,3},{4,20},{20... | collective-permute-start | bytes 1622024 | tf_op jit(solution)/shard_map/ppermute | solution.py:706
  109.9 2.4 %collective-permute-start.19 = (f32[1056,128]{1,0:T(8,128)S(1)}, f32[1056,128]{1,0:T(8,128)S(1)}, u32[]{:S(2)}, u32[]{:S(2)}) collective-permute-start(f32[1056,128]{1,0:T(8,128)S(1)} %sum_far.1.refs_2_), channel_id=1, source_target_pairs={{0,16},{16,0},{1,17},{17,1},{2,18},{18,2},{3,19},{19,3},{4,20},{20... | collective-permute-start | bytes 1622024 | tf_op jit(solution)/shard_map/ppermute | solution.py:706
  110.0 2.3 %collective-permute-start.18 = (bf16[1056,128]{1,0:T(8,128)(2,1)S(1)}, bf16[1056,128]{1,0:T(8,128)(2,1)S(1)}, u32[]{:S(2)}, u32[]{:S(2)}) collective-permute-start(bf16[1056,128]{1,0:T(8,128)(2,1)S(1)} %collective-permute-done.14.refs_1_), channel_id=1, source_target_pairs={{0,16},{16,0},{1,17},{17,1},{2,18},{18,2},{3,19},{19,3},{4,20},{20... | collective-permute-start | bytes 811016 | tf_op jit(solution)/shard_map/ppermute | solution.py:706

commit v13 on v12

--- a/solution.py
+++ b/solution.py
@@ -654,7 +654,7 @@
     recvs = [lax.ppermute(block, "tm", swap) for block in sends]
     halos, lates = [], []
     for c in range(parts):
-        recv = follow(recvs[c], lates[-1]) if lates else recvs[c]
+        recv = follow(recvs[c], [lates[-1][0], halos[-1]]) if lates else recvs[c]
         halos.append(lax.ppermute(jnp.where(g == 1, keeps[c], recv), "tm", onward))
         sources = [keeps[c], follow(recvs[c], halos[c - 1]) if c else recvs[c]]
         lates.append(filterbank(c, half, delays, sources, tables, [], len(dests)))

time: 114 us -> 104 us (0.912)
  waiting for transfers between devices: 46.8 us -> 36.6 us
    ppermute x2, waiting for transfers between devices: 18.3 us -> 13 us  [fast(): recvs = [lax.ppermute(block, 'tm', swap) for block in sends]]
    ppermute x2, waiting for transfers between devices: 8.77 us -> 4 us  [fast(): halos.append(lax.ppermute(jnp.where(g == 1, keeps[c], recv), 'tm', onward))]
    ppermute x2, starting transfers between devices: 7.25 us -> 8.5 us  [fast(): halos.append(lax.ppermute(jnp.where(g == 1, keeps[c], recv), 'tm', onward))]
  transfers between devices with their start and end apart: 20 -> 20, of which waited for: 8 -> 10; matrix products, arithmetic and copies ran while one was open for 0% -> 1% of each run, Pallas kernels for 24% -> 26%
where the time goes in v13:
time: 104 us
  Pallas kernels  36.7 us (35%)
  waiting for transfers between devices  36.6 us (35%)
  starting transfers between devices  27.5 us (26%)
  local copies, waits for them, and re-layouts  1.62 us (2%)
  other arithmetic  1.15 us (1%)
    pallas_call x4, Pallas kernels, filterbank(): pl.pallas_call(kernel, out_shape=[jax.ShapeDtypeStruct(shape, jnp.bfloat1...  16.3 us
    pallas_call x3, Pallas kernels, correlate(): pl.pallas_call(functools.partial(correlate_kernel, layout), out_shape=[ja...  15.8 us
    ppermute x5, waiting for transfers between devices, along(): return lax.ppermute(block, 'tm', route)  14.9 us
    ppermute x2, waiting for transfers between devices, fast(): recvs = [lax.ppermute(block, 'tm', swap) for block in sends]  13 us
    ppermute x2, starting transfers between devices, fast(): halos.append(lax.ppermute(jnp.where(g == 1, keeps[c], recv), 'tm', onward))  8.5 us
    ppermute x5, starting transfers between devices, along(): return lax.ppermute(block, 'tm', route)  8.5 us
    ppermute x6, starting transfers between devices, fast(): block = lax.ppermute(block, ('tm', 'ct'), route)  7.11 us
    ppermute x2, waiting for transfers between devices, fast(): halos.append(lax.ppermute(jnp.where(g == 1, keeps[c], recv), 'tm', onward))  4 us
  transfers between devices with their start and end apart: 20, of which 10 were waited for; matrix products, arithmetic and copies ran while one was open for 1% of the time, Pallas kernels for 26%

profile of v13, /device:TPU:0, one launch (start us, length us, event | category | flops | bytes accessed | tf_op | source)
XLA Modules:
  0.0 103.8 jit_solution(7330087001428101111)
XLA Ops:
  0.0 1.6 %copy-done = bf16[2,8,65536]{2,1,0:T(8,128)(2,1)S(1)} copy-done((bf16[2,8,65536]{2,1,0:T(8,128)(2,1)S(1)}, bf16[2,8,65536]{2,1,0:T(8,128)(2,1)}, u32[]{:S(2)}) %copy-start) | copy-done | bytes 2097176
  1.6 1.7 %pick.2 = (bf16[2,2,512,128]{3,2,1,0:T(8,128)(2,1)}, bf16[2,2,512,128]{3,2,1,0:T(8,128)(2,1)}) custom-call(bf16[2,8,65536]{2,1,0:T(8,128)(2,1)S(1)} %copy-done), custom_call_target="tpu_custom_call" | custom-call | flops 1000000 | bytes 262144 | tf_op jit(solution)/shard_map/pick/pallas_call | solution.py:121
  3.3 0.0 copy-start.6
  3.3 0.0 copy-start.7
  3.4 3.0 %collective-permute-start = (bf16[2,2,512,128]{3,2,1,0:T(8,128)(2,1)}, bf16[2,2,512,128]{3,2,1,0:T(8,128)(2,1)}, u32[]{:S(2)}, u32[]{:S(2)}) collective-permute-start(bf16[2,2,512,128]{3,2,1,0:T(8,128)(2,1)} %get-tuple-element.50), channel_id=1, source_target_pairs={{0,2},{2,0},{4,6},{6,4},{8,10},{10,8},{12,14},{14,12},{1,3},{3,1},... | collective-permute-start | bytes 1572872 | tf_op jit(solution)/shard_map/ppermute | solution.py:654
  6.4 0.1 collective-permute-start.2
  6.4 0.8 pick.3
  7.2 12.2 %collective-permute-done.refs_2_.refs_3_ = bf16[2,2,512,128]{3,2,1,0:T(8,128)(2,1)} collective-permute-done((bf16[2,2,512,128]{3,2,1,0:T(8,128)(2,1)}, bf16[2,2,512,128]{3,2,1,0:T(8,128)(2,1)}, u32[]{:S(2)}, u32[]{:S(2)}) %collective-permute-start) | collective-permute-done | bytes 524320 | tf_op jit(solution)/shard_map/ppermute | solution.py:654
  19.4 1.1 %broadcast_select_fusion.1 = bf16[2,2,512,128]{3,2,1,0:T(8,128)(2,1)S(1)} fusion(bf16[2,2,512,128]{3,2,1,0:T(8,128)(2,1)S(1)} %get-tuple-element.52.refs_1_.refs_2_, bf16[2,2,512,128]{3,2,1,0:T(8,128)(2,1)} %collective-permute-done.refs_2_.refs_3_, pred[]{:T(512)S(6)} %eq.6), kind=kLoop, calls=%fused_computation.1 | loop fusion | flops 262144 | bytes 1572865 | tf_op jit(solution)/shard_map/jit(_where)/select_n | solution.py:658
  20.5 4.1 %collective-permute-start.1 = (bf16[2,2,512,128]{3,2,1,0:T(8,128)(2,1)S(1)}, bf16[2,2,512,128]{3,2,1,0:T(8,128)(2,1)S(1)}, u32[]{:S(2)}, u32[]{:S(2)}) collective-permute-start(bf16[2,2,512,128]{3,2,1,0:T(8,128)(2,1)S(1)} %broadcast_select_fusion.1), channel_id=1, source_target_pairs={{0,4},{2,6},{4,8},{6,10},{8,12},{10,14},{1,5},{3,7},{5,9},{7,11},{... | collective-permute-start | bytes 1572872 | tf_op jit(solution)/shard_map/ppermute | solution.py:658
  24.7 4.3 %filterbank_late.2 = (bf16[2,8,2,16,128]{4,3,2,1,0:T(8,128)(2,1)S(1)}, bf16[2,8,2,16,128]{4,3,2,1,0:T(8,128)(2,1)S(1)}, bf16[2,8,2,16,128]{4,3,2,1,0:T(8,128)(2,1)S(1)}, bf16[2,8,2,16,128]{4,3,2,1,0:T(8,128)(2,1)S(1)}) custom-call(s32[8]{0:T(128)S(1)} %copy-done.7, bf16[2,2,512,128]{3,2,1,0:T(8,128)(2,1)S(1)} %get-tuple-element.52.refs_1_.refs_2_, ...), custom_call_target="tpu_custom_call" | custom-call | flops 1000000 | bytes 262144 | tf_op jit(solution)/shard_map/filterbank_late/pallas_call | solution.py:311
  29.0 0.8 collective-permute-done.2.refs_2_.refs_3_
  29.7 4.0 %collective-permute-done.1.refs_1_ = bf16[2,2,512,128]{3,2,1,0:T(8,128)(2,1)S(1)} collective-permute-done((bf16[2,2,512,128]{3,2,1,0:T(8,128)(2,1)S(1)}, bf16[2,2,512,128]{3,2,1,0:T(8,128)(2,1)S(1)}, u32[]{:S(2)}, u32[]{:S(2)}) %collective-permute-start.1) | collective-permute-done | bytes 524320 | tf_op jit(solution)/shard_map/ppermute | solution.py:658
  33.7 0.1 broadcast_select_fusion
  33.8 4.4 %collective-permute-start.3 = (bf16[2,2,512,128]{3,2,1,0:T(8,128)(2,1)S(1)}, bf16[2,2,512,128]{3,2,1,0:T(8,128)(2,1)S(1)}, u32[]{:S(2)}, u32[]{:S(2)}) collective-permute-start(bf16[2,2,512,128]{3,2,1,0:T(8,128)(2,1)S(1)} %broadcast_select_fusion), channel_id=1, source_target_pairs={{0,4},{2,6},{4,8},{6,10},{8,12},{10,14},{1,5},{3,7},{5,9},{7,11},{... | collective-permute-start | bytes 1572872 | tf_op jit(solution)/shard_map/ppermute | solution.py:658
  38.2 4.3 %filterbank_early.2 = (bf16[2,16,2,16,128]{4,3,2,1,0:T(8,128)(2,1)S(1)}, bf16[2,16,2,16,128]{4,3,2,1,0:T(8,128)(2,1)S(1)}, bf16[2,16,2,16,128]{4,3,2,1,0:T(8,128)(2,1)S(1)}, bf16[2,16,2,16,128]{4,3,2,1,0:T(8,128)(2,1)S(1)}) custom-call(s32[8]{0:T(128)S(1)} %copy-done.7, bf16[2,2,512,128]{3,2,1,0:T(8,128)(2,1)S(1)} %collective-permute-done.1.refs_1_, ...), custom_call_target="tpu_custom_call" | custom-call | flops 1000000 | bytes 262144 | tf_op jit(solution)/shard_map/filterbank_early/pallas_call | solution.py:311
  42.5 1.5 %collective-permute-start.6 = (bf16[2,16,2,16,128]{4,3,2,1,0:T(8,128)(2,1)S(1)}, bf16[2,16,2,16,128]{4,3,2,1,0:T(8,128)(2,1)S(1)}, u32[]{:S(2)}, u32[]{:S(2)}) collective-permute-start(bf16[2,16,2,16,128]{4,3,2,1,0:T(8,128)(2,1)S(1)} %get-tuple-element.73), channel_id=1, source_target_pairs={{0,3},{1,2},{2,1},{3,0},{4,7},{5,6},{6,5},{7,4},{8,11},{9,10},{10,... | collective-permute-start | bytes 786440 | tf_op jit(solution)/shard_map/ppermute | solution.py:678
  44.0 1.6 %collective-permute-start.5 = (bf16[2,16,2,16,128]{4,3,2,1,0:T(8,128)(2,1)S(1)}, bf16[2,16,2,16,128]{4,3,2,1,0:T(8,128)(2,1)S(1)}, u32[]{:S(2)}, u32[]{:S(2)}) collective-permute-start(bf16[2,16,2,16,128]{4,3,2,1,0:T(8,128)(2,1)S(1)} %get-tuple-element.71), channel_id=1, source_target_pairs={{0,2},{1,3},{2,0},{3,1},{4,6},{5,7},{6,4},{7,5},{8,10},{9,11},{10,... | collective-permute-start | bytes 786440 | tf_op jit(solution)/shard_map/ppermute | solution.py:678
  45.6 0.5 collective-permute-start.4
  46.1 3.7 %filterbank_late.3 = (bf16[2,8,2,16,128]{4,3,2,1,0:T(8,128)(2,1)S(1)}, bf16[2,8,2,16,128]{4,3,2,1,0:T(8,128)(2,1)S(1)}, bf16[2,8,2,16,128]{4,3,2,1,0:T(8,128)(2,1)S(1)}, bf16[2,8,2,16,128]{4,3,2,1,0:T(8,128)(2,1)S(1)}) custom-call(s32[8]{0:T(128)S(1)} %copy-done.7, bf16[2,2,512,128]{3,2,1,0:T(8,128)(2,1)S(1)} %get-tuple-element.60.refs_1_.refs_2_, ...), custom_call_target="tpu_custom_call" | custom-call | flops 1000000 | bytes 262144 | tf_op jit(solution)/shard_map/filterbank_late/pallas_call | solution.py:311
  49.8 4.0 %filterbank_early.3 = (bf16[2,16,2,16,128]{4,3,2,1,0:T(8,128)(2,1)S(1)}, bf16[2,16,2,16,128]{4,3,2,1,0:T(8,128)(2,1)S(1)}, bf16[2,16,2,16,128]{4,3,2,1,0:T(8,128)(2,1)S(1)}, bf16[2,16,2,16,128]{4,3,2,1,0:T(8,128)(2,1)S(1)}) custom-call(s32[8]{0:T(128)S(1)} %copy-done.7, bf16[2,2,512,128]{3,2,1,0:T(8,128)(2,1)S(1)} %collective-permute-done.3.refs_1_, ...), custom_call_target="tpu_custom_call" | custom-call | flops 1000000 | bytes 262144 | tf_op jit(solution)/shard_map/filterbank_early/pallas_call | solution.py:311
  53.8 0.2 collective-permute-done.5.refs_2_
  54.1 0.0 collective-permute-done.4.refs_1_
  54.1 0.2 join.2.refs_0_
  54.3 0.1 collective-permute-start.7
  54.3 1.3 %collective-permute-start.12 = (bf16[2,16,2,16,128]{4,3,2,1,0:T(8,128)(2,1)S(1)}, bf16[2,16,2,16,128]{4,3,2,1,0:T(8,128)(2,1)S(1)}, u32[]{:S(2)}, u32[]{:S(2)}) collective-permute-start(bf16[2,16,2,16,128]{4,3,2,1,0:T(8,128)(2,1)S(1)} %get-tuple-element.85), channel_id=1, source_target_pairs={{0,3},{1,2},{2,1},{3,0},{4,7},{5,6},{6,5},{7,4},{8,11},{9,10},{10,... | collective-permute-start | bytes 786440 | tf_op jit(solution)/shard_map/ppermute | solution.py:678
  55.7 1.6 %collective-permute-start.11 = (bf16[2,16,2,16,128]{4,3,2,1,0:T(8,128)(2,1)S(1)}, bf16[2,16,2,16,128]{4,3,2,1,0:T(8,128)(2,1)S(1)}, u32[]{:S(2)}, u32[]{:S(2)}) collective-permute-start(bf16[2,16,2,16,128]{4,3,2,1,0:T(8,128)(2,1)S(1)} %get-tuple-element.82), channel_id=1, source_target_pairs={{0,2},{1,3},{2,0},{3,1},{4,6},{5,7},{6,4},{7,5},{8,10},{9,11},{10,... | collective-permute-start | bytes 786440 | tf_op jit(solution)/shard_map/ppermute | solution.py:678
  57.2 0.7 collective-permute-start.10
  57.9 4.0 %correlate_early.1 = (f32[272,128]{1,0:T(8,128)S(1)}, bf16[272,128]{1,0:T(8,128)(2,1)S(1)}, bf16[272,128]{1,0:T(8,128)(2,1)S(1)}, bf16[272,128]{1,0:T(8,128)(2,1)S(1)}) custom-call(bf16[8,16,2,16,128]{4,3,2,1,0:T(8,128)(2,1)S(1)} %join.2.refs_0_, bf16[8,16,2,16,128]{4,3,2,1,0:T(8,128)(2,1)S(1)} %collective-permute-done.7.refs_1_.refs_2_), custom_call_target="tpu_custom_call" | custom-call | flops 1000000 | bytes 262144 | tf_op jit(solution)/shard_map/correlate_early/pallas_call | solution.py:477
  61.9 2.6 %collective-permute-start.8 = (bf16[272,128]{1,0:T(8,128)(2,1)S(1)}, bf16[272,128]{1,0:T(8,128)(2,1)S(1)}, u32[]{:S(2)}, u32[]{:S(2)}) collective-permute-start(bf16[272,128]{1,0:T(8,128)(2,1)S(1)} %get-tuple-element.75), channel_id=1, source_target_pairs={{0,8},{2,10},{4,12},{6,14},{8,0},{10,2},{12,4},{14,6},{1,9},{3,11}... | collective-permute-start | bytes 208904 | tf_op jit(solution)/shard_map/ppermute | solution.py:684
  64.5 1.3 %collective-permute-start.9 = (bf16[272,128]{1,0:T(8,128)(2,1)S(1)}, bf16[272,128]{1,0:T(8,128)(2,1)S(1)}, u32[]{:S(2)}, u32[]{:S(2)}) collective-permute-start(bf16[272,128]{1,0:T(8,128)(2,1)S(1)} %get-tuple-element.76), channel_id=1, source_target_pairs={{0,12},{2,14},{4,8},{6,10},{8,4},{10,6},{12,0},{14,2},{1,13},{3,15... | collective-permute-start | bytes 208904 | tf_op jit(solution)/shard_map/ppermute | solution.py:684
  65.9 3.5 %collective-permute-done.8.refs_0_ = bf16[272,128]{1,0:T(8,128)(2,1)S(1)} collective-permute-done((bf16[272,128]{1,0:T(8,128)(2,1)S(1)}, bf16[272,128]{1,0:T(8,128)(2,1)S(1)}, u32[]{:S(2)}, u32[]{:S(2)}) %collective-permute-start.8) | collective-permute-done | bytes 69664 | tf_op jit(solution)/shard_map/ppermute | solution.py:684
  69.4 1.4 %collective-permute-done.9.refs_1_ = bf16[272,128]{1,0:T(8,128)(2,1)S(1)} collective-permute-done((bf16[272,128]{1,0:T(8,128)(2,1)S(1)}, bf16[272,128]{1,0:T(8,128)(2,1)S(1)}, u32[]{:S(2)}, u32[]{:S(2)}) %collective-permute-start.9) | collective-permute-done | bytes 69664 | tf_op jit(solution)/shard_map/ppermute | solution.py:684
  70.7 0.2 join.3.refs_1_
  70.9 0.1 collective-permute-start.13
  71.0 2.6 %collective-permute-done.13.refs_3_ = bf16[8,16,2,16,128]{4,3,2,1,0:T(8,128)(2,1)S(1)} collective-permute-done((bf16[8,16,2,16,128]{4,3,2,1,0:T(8,128)(2,1)S(1)}, bf16[8,16,2,16,128]{4,3,2,1,0:T(8,128)(2,1)S(1)}, u32[]{:S(2)}, u32[]{:S(2)}) %collective-permute-start.13) | collective-permute-done | bytes 1048608 | tf_op jit(solution)/shard_map/ppermute | solution.py:694
  73.6 5.9 %correlate_far.1 = (bf16[784,128]{1,0:T(8,128)(2,1)S(1)}, bf16[784,128]{1,0:T(8,128)(2,1)S(1)}) custom-call(bf16[8,16,2,16,128]{4,3,2,1,0:T(8,128)(2,1)S(1)} %join.2.refs_0_, bf16[8,16,2,16,128]{4,3,2,1,0:T(8,128)(2,1)S(1)} %join.3.refs_1_, bf16[8,16,2,16,128]{4,3,2,1,0:T(8,128)(2,1)S(1)} %collective-permute-done.7.refs_1_.refs_2_, ...), custom_call_target="tpu_custom_call" | custom-call | flops 1000000 | bytes 262144 | tf_op jit(solution)/shard_map/correlate_far/pallas_call | solution.py:477
  79.6 1.4 %collective-permute-start.16 = (bf16[784,128]{1,0:T(8,128)(2,1)S(1)}, bf16[784,128]{1,0:T(8,128)(2,1)S(1)}, u32[]{:S(2)}, u32[]{:S(2)}) collective-permute-start(bf16[784,128]{1,0:T(8,128)(2,1)S(1)} %get-tuple-element.93), channel_id=1, source_target_pairs={{0,12},{2,14},{4,8},{6,10},{8,4},{10,6},{12,0},{14,2},{1,13},{3,15... | collective-permute-start | bytes 602120 | tf_op jit(solution)/shard_map/ppermute | solution.py:684
  80.9 0.9 collective-permute-start.15
  81.8 5.9 %correlate_near.1 = (f32[1056,128]{1,0:T(8,128)S(1)}, bf16[1056,128]{1,0:T(8,128)(2,1)S(1)}) custom-call(bf16[8,16,2,16,128]{4,3,2,1,0:T(8,128)(2,1)S(1)} %join.2.refs_0_, bf16[8,16,2,16,128]{4,3,2,1,0:T(8,128)(2,1)S(1)} %join.3.refs_1_, bf16[8,16,2,16,128]{4,3,2,1,0:T(8,128)(2,1)S(1)} %collective-permute-done.7.refs_1_.refs_2_, ...), custom_call_target="tpu_custom_call" | custom-call | flops 1000000 | bytes 262144 | tf_op jit(solution)/shard_map/correlate_near/pallas_call | solution.py:477
  87.8 2.3 %collective-permute-start.14 = (bf16[1056,128]{1,0:T(8,128)(2,1)S(1)}, bf16[1056,128]{1,0:T(8,128)(2,1)S(1)}, u32[]{:S(2)}, u32[]{:S(2)}) collective-permute-start(bf16[1056,128]{1,0:T(8,128)(2,1)S(1)} %get-tuple-element.92), channel_id=1, source_target_pairs={{0,4},{2,6},{4,0},{6,2},{8,12},{10,14},{12,8},{14,10},{1,5},{3,7},... | collective-permute-start | bytes 811016 | tf_op jit(solution)/shard_map/ppermute | solution.py:684
  90.1 9.6 %collective-permute-done.15.refs_2_ = bf16[784,128]{1,0:T(8,128)(2,1)S(1)} collective-permute-done((bf16[784,128]{1,0:T(8,128)(2,1)S(1)}, bf16[784,128]{1,0:T(8,128)(2,1)S(1)}, u32[]{:S(2)}, u32[]{:S(2)}) %collective-permute-start.15) | collective-permute-done | bytes 200736 | tf_op jit(solution)/shard_map/ppermute | solution.py:684
  99.6 0.1 sum_far.1.refs_2_
  99.7 0.1 collective-permute-start.19
  99.8 0.4 collective-permute-done.14.refs_1_
  100.2 0.1 collective-permute-start.18
  100.3 1.8 %collective-permute-done.18.refs_4_ = bf16[1056,128]{1,0:T(8,128)(2,1)S(1)} collective-permute-done((bf16[1056,128]{1,0:T(8,128)(2,1)S(1)}, bf16[1056,128]{1,0:T(8,128)(2,1)S(1)}, u32[]{:S(2)}, u32[]{:S(2)}) %collective-permute-start.18) | collective-permute-done | bytes 270368 | tf_op jit(solution)/shard_map/ppermute | solution.py:706
  102.1 1.7 %assemble.1 = f32[2,16,32,256]{3,2,1,0:T(8,128)} custom-call(f32[1056,128]{1,0:T(8,128)S(1)} %get-tuple-element.91.refs_0_, bf16[1056,128]{1,0:T(8,128)(2,1)S(1)} %collective-permute-done.14.refs_1_, f32[1056,128]{1,0:T(8,128)S(1)} %sum_far.1.refs_2_, f32[1056,128]{1,0:T(8,128)S(1)} %collective-permute-done.17.refs_3_, ...), custom_call_target="tpu_custom_call" | custom-call | flops 1000000 | bytes 262144 | tf_op jit(solution)/shard_map/assemble/pallas_call | solution.py:599
  (23 shorter events, 0.1 us)
Async XLA Ops:
  0.0 1.6 %copy-start = (bf16[2,8,65536]{2,1,0:T(8,128)(2,1)S(1)}, bf16[2,8,65536]{2,1,0:T(8,128)(2,1)}, u32[]{:S(2)}) copy-start(bf16[2,8,65536]{2,1,0:T(8,128)(2,1)} %block.2) | copy-start | bytes 6291460
  1.6 4.9 %copy-start.1 = (bf16[2,8,65536]{2,1,0:T(8,128)(2,1)S(1)}, bf16[2,8,65536]{2,1,0:T(8,128)(2,1)}, u32[]{:S(2)}) copy-start(bf16[2,8,65536]{2,1,0:T(8,128)(2,1)} %block.2) | copy-start | bytes 6291460
  3.3 21.3 %copy-start.2 = (f32[16,64,128]{2,1,0:T(8,128)S(1)}, f32[16,64,128]{2,1,0:T(8,128)}, u32[]{:S(2)}) copy-start(f32[16,64,128]{2,1,0:T(8,128)} %constant.30.clone.refs_3_.refs_4_) | copy-start | bytes 1572868
  3.3 21.3 %copy-start.3 = (bf16[2,4,32,128]{3,2,1,0:T(8,128)(2,1)S(1)}, bf16[2,4,32,128]{3,2,1,0:T(8,128)(2,1)}, u32[]{:S(2)}) copy-start(bf16[2,4,32,128]{3,2,1,0:T(8,128)(2,1)} %constant.34.clone.refs_7_.refs_8_) | copy-start | bytes 196612
  3.3 21.3 %copy-start.4 = (f32[64,128]{1,0:T(8,128)S(1)}, f32[64,128]{1,0:T(8,128)}, u32[]{:S(2)}) copy-start(f32[64,128]{1,0:T(8,128)} %constant.33.clone.refs_6_.refs_7_) | copy-start | bytes 98308
  3.3 21.3 %copy-start.5 = (f32[64,128]{1,0:T(8,128)S(1)}, f32[64,128]{1,0:T(8,128)}, u32[]{:S(2)}) copy-start(f32[64,128]{1,0:T(8,128)} %constant.32.clone.refs_5_.refs_6_) | copy-start | bytes 98308
  3.3 21.3 %copy-start.6 = (bf16[128,128]{1,0:T(8,128)(2,1)S(1)}, bf16[128,128]{1,0:T(8,128)(2,1)}, u32[]{:S(2)}) copy-start(bf16[128,128]{1,0:T(8,128)(2,1)} %constant.31.clone.refs_4_.refs_5_) | copy-start | bytes 98308
  3.3 21.3 %copy-start.7 = (s32[8]{0:T(128)S(1)}, s32[8]{0:T(128)}, u32[]{:S(2)}) copy-start(s32[8]{0:T(128)} %refs_0_.7) | copy-start | bytes 100
  3.4 16.1 %collective-permute-start = (bf16[2,2,512,128]{3,2,1,0:T(8,128)(2,1)}, bf16[2,2,512,128]{3,2,1,0:T(8,128)(2,1)}, u32[]{:S(2)}, u32[]{:S(2)}) collective-permute-start(bf16[2,2,512,128]{3,2,1,0:T(8,128)(2,1)} %get-tuple-element.50), channel_id=1, source_target_pairs={{0,2},{2,0},{4,6},{6,4},{8,10},{10,8},{12,14},{14,12},{1,3},{3,1},... | collective-permute-start | bytes 1572872 | tf_op jit(solution)/shard_map/ppermute | solution.py:654
  6.4 23.4 %collective-permute-start.2 = (bf16[2,2,512,128]{3,2,1,0:T(8,128)(2,1)}, bf16[2,2,512,128]{3,2,1,0:T(8,128)(2,1)S(1)}, u32[]{:S(2)}, u32[]{:S(2)}) collective-permute-start(bf16[2,2,512,128]{3,2,1,0:T(8,128)(2,1)} %get-tuple-element.53), channel_id=1, source_target_pairs={{0,2},{2,0},{4,6},{6,4},{8,10},{10,8},{12,14},{14,12},{1,3},{3,1},... | collective-permute-start | bytes 1572872 | tf_op jit(solution)/shard_map/ppermute | solution.py:654
  20.5 13.2 %collective-permute-start.1 = (bf16[2,2,512,128]{3,2,1,0:T(8,128)(2,1)S(1)}, bf16[2,2,512,128]{3,2,1,0:T(8,128)(2,1)S(1)}, u32[]{:S(2)}, u32[]{:S(2)}) collective-permute-start(bf16[2,2,512,128]{3,2,1,0:T(8,128)(2,1)S(1)} %broadcast_select_fusion.1), channel_id=1, source_target_pairs={{0,4},{2,6},{4,8},{6,10},{8,12},{10,14},{1,5},{3,7},{5,9},{7,11},{... | collective-permute-start | bytes 1572872 | tf_op jit(solution)/shard_map/ppermute | solution.py:658
  33.8 16.0 %collective-permute-start.3 = (bf16[2,2,512,128]{3,2,1,0:T(8,128)(2,1)S(1)}, bf16[2,2,512,128]{3,2,1,0:T(8,128)(2,1)S(1)}, u32[]{:S(2)}, u32[]{:S(2)}) collective-permute-start(bf16[2,2,512,128]{3,2,1,0:T(8,128)(2,1)S(1)} %broadcast_select_fusion), channel_id=1, source_target_pairs={{0,4},{2,6},{4,8},{6,10},{8,12},{10,14},{1,5},{3,7},{5,9},{7,11},{... | collective-permute-start | bytes 1572872 | tf_op jit(solution)/shard_map/ppermute | solution.py:658
  42.5 11.3 %collective-permute-start.6 = (bf16[2,16,2,16,128]{4,3,2,1,0:T(8,128)(2,1)S(1)}, bf16[2,16,2,16,128]{4,3,2,1,0:T(8,128)(2,1)S(1)}, u32[]{:S(2)}, u32[]{:S(2)}) collective-permute-start(bf16[2,16,2,16,128]{4,3,2,1,0:T(8,128)(2,1)S(1)} %get-tuple-element.73), channel_id=1, source_target_pairs={{0,3},{1,2},{2,1},{3,0},{4,7},{5,6},{6,5},{7,4},{8,11},{9,10},{10,... | collective-permute-start | bytes 786440 | tf_op jit(solution)/shard_map/ppermute | solution.py:678
  44.0 10.1 %collective-permute-start.5 = (bf16[2,16,2,16,128]{4,3,2,1,0:T(8,128)(2,1)S(1)}, bf16[2,16,2,16,128]{4,3,2,1,0:T(8,128)(2,1)S(1)}, u32[]{:S(2)}, u32[]{:S(2)}) collective-permute-start(bf16[2,16,2,16,128]{4,3,2,1,0:T(8,128)(2,1)S(1)} %get-tuple-element.71), channel_id=1, source_target_pairs={{0,2},{1,3},{2,0},{3,1},{4,6},{5,7},{6,4},{7,5},{8,10},{9,11},{10,... | collective-permute-start | bytes 786440 | tf_op jit(solution)/shard_map/ppermute | solution.py:678
  45.6 8.5 %collective-permute-start.4 = (bf16[2,16,2,16,128]{4,3,2,1,0:T(8,128)(2,1)S(1)}, bf16[2,16,2,16,128]{4,3,2,1,0:T(8,128)(2,1)S(1)}, u32[]{:S(2)}, u32[]{:S(2)}) collective-permute-start(bf16[2,16,2,16,128]{4,3,2,1,0:T(8,128)(2,1)S(1)} %get-tuple-element.69), channel_id=1, source_target_pairs={{0,1},{1,0},{2,3},{3,2},{4,5},{5,4},{6,7},{7,6},{8,9},{9,8},{10,11... | collective-permute-start | bytes 786440 | tf_op jit(solution)/shard_map/ppermute | solution.py:678
  54.3 3.6 %collective-permute-start.7 = (bf16[8,16,2,16,128]{4,3,2,1,0:T(8,128)(2,1)S(1)}, bf16[8,16,2,16,128]{4,3,2,1,0:T(8,128)(2,1)S(1)}, u32[]{:S(2)}, u32[]{:S(2)}) collective-permute-start(bf16[8,16,2,16,128]{4,3,2,1,0:T(8,128)(2,1)S(1)} %join.2.refs_0_), channel_id=1, source_target_pairs={{0,16},{16,0},{1,17},{17,1},{2,18},{18,2},{3,19},{19,3},{4,20},{20... | collective-permute-start | bytes 3145736 | tf_op jit(solution)/shard_map/ppermute | solution.py:687
  54.3 11.5 %collective-permute-start.12 = (bf16[2,16,2,16,128]{4,3,2,1,0:T(8,128)(2,1)S(1)}, bf16[2,16,2,16,128]{4,3,2,1,0:T(8,128)(2,1)S(1)}, u32[]{:S(2)}, u32[]{:S(2)}) collective-permute-start(bf16[2,16,2,16,128]{4,3,2,1,0:T(8,128)(2,1)S(1)} %get-tuple-element.85), channel_id=1, source_target_pairs={{0,3},{1,2},{2,1},{3,0},{4,7},{5,6},{6,5},{7,4},{8,11},{9,10},{10,... | collective-permute-start | bytes 786440 | tf_op jit(solution)/shard_map/ppermute | solution.py:678
  55.7 15.1 %collective-permute-start.11 = (bf16[2,16,2,16,128]{4,3,2,1,0:T(8,128)(2,1)S(1)}, bf16[2,16,2,16,128]{4,3,2,1,0:T(8,128)(2,1)S(1)}, u32[]{:S(2)}, u32[]{:S(2)}) collective-permute-start(bf16[2,16,2,16,128]{4,3,2,1,0:T(8,128)(2,1)S(1)} %get-tuple-element.82), channel_id=1, source_target_pairs={{0,2},{1,3},{2,0},{3,1},{4,6},{5,7},{6,4},{7,5},{8,10},{9,11},{10,... | collective-permute-start | bytes 786440 | tf_op jit(solution)/shard_map/ppermute | solution.py:678
  57.2 13.5 %collective-permute-start.10 = (bf16[2,16,2,16,128]{4,3,2,1,0:T(8,128)(2,1)S(1)}, bf16[2,16,2,16,128]{4,3,2,1,0:T(8,128)(2,1)S(1)}, u32[]{:S(2)}, u32[]{:S(2)}) collective-permute-start(bf16[2,16,2,16,128]{4,3,2,1,0:T(8,128)(2,1)S(1)} %get-tuple-element.79), channel_id=1, source_target_pairs={{0,1},{1,0},{2,3},{3,2},{4,5},{5,4},{6,7},{7,6},{8,9},{9,8},{10,11... | collective-permute-start | bytes 786440 | tf_op jit(solution)/shard_map/ppermute | solution.py:678
  61.9 7.5 %collective-permute-start.8 = (bf16[272,128]{1,0:T(8,128)(2,1)S(1)}, bf16[272,128]{1,0:T(8,128)(2,1)S(1)}, u32[]{:S(2)}, u32[]{:S(2)}) collective-permute-start(bf16[272,128]{1,0:T(8,128)(2,1)S(1)} %get-tuple-element.75), channel_id=1, source_target_pairs={{0,8},{2,10},{4,12},{6,14},{8,0},{10,2},{12,4},{14,6},{1,9},{3,11}... | collective-permute-start | bytes 208904 | tf_op jit(solution)/shard_map/ppermute | solution.py:684
  64.5 6.2 %collective-permute-start.9 = (bf16[272,128]{1,0:T(8,128)(2,1)S(1)}, bf16[272,128]{1,0:T(8,128)(2,1)S(1)}, u32[]{:S(2)}, u32[]{:S(2)}) collective-permute-start(bf16[272,128]{1,0:T(8,128)(2,1)S(1)} %get-tuple-element.76), channel_id=1, source_target_pairs={{0,12},{2,14},{4,8},{6,10},{8,4},{10,6},{12,0},{14,2},{1,13},{3,15... | collective-permute-start | bytes 208904 | tf_op jit(solution)/shard_map/ppermute | solution.py:684
  70.9 2.7 %collective-permute-start.13 = (bf16[8,16,2,16,128]{4,3,2,1,0:T(8,128)(2,1)S(1)}, bf16[8,16,2,16,128]{4,3,2,1,0:T(8,128)(2,1)S(1)}, u32[]{:S(2)}, u32[]{:S(2)}) collective-permute-start(bf16[8,16,2,16,128]{4,3,2,1,0:T(8,128)(2,1)S(1)} %join.3.refs_1_), channel_id=1, source_target_pairs={{0,16},{16,0},{1,17},{17,1},{2,18},{18,2},{3,19},{19,3},{4,20},{20... | collective-permute-start | bytes 3145736 | tf_op jit(solution)/shard_map/ppermute | solution.py:694
  79.6 10.5 %collective-permute-start.16 = (bf16[784,128]{1,0:T(8,128)(2,1)S(1)}, bf16[784,128]{1,0:T(8,128)(2,1)S(1)}, u32[]{:S(2)}, u32[]{:S(2)}) collective-permute-start(bf16[784,128]{1,0:T(8,128)(2,1)S(1)} %get-tuple-element.93), channel_id=1, source_target_pairs={{0,12},{2,14},{4,8},{6,10},{8,4},{10,6},{12,0},{14,2},{1,13},{3,15... | collective-permute-start | bytes 602120 | tf_op jit(solution)/shard_map/ppermute | solution.py:684
  80.9 18.7 %collective-permute-start.15 = (bf16[784,128]{1,0:T(8,128)(2,1)S(1)}, bf16[784,128]{1,0:T(8,128)(2,1)S(1)}, u32[]{:S(2)}, u32[]{:S(2)}) collective-permute-start(bf16[784,128]{1,0:T(8,128)(2,1)S(1)} %get-tuple-element.87), channel_id=1, source_target_pairs={{0,8},{2,10},{4,12},{6,14},{8,0},{10,2},{12,4},{14,6},{1,9},{3,11}... | collective-permute-start | bytes 602120 | tf_op jit(solution)/shard_map/ppermute | solution.py:684
  87.8 12.4 %collective-permute-start.14 = (bf16[1056,128]{1,0:T(8,128)(2,1)S(1)}, bf16[1056,128]{1,0:T(8,128)(2,1)S(1)}, u32[]{:S(2)}, u32[]{:S(2)}) collective-permute-start(bf16[1056,128]{1,0:T(8,128)(2,1)S(1)} %get-tuple-element.92), channel_id=1, source_target_pairs={{0,4},{2,6},{4,0},{6,2},{8,12},{10,14},{12,8},{14,10},{1,5},{3,7},... | collective-permute-start | bytes 811016 | tf_op jit(solution)/shard_map/ppermute | solution.py:684
  90.1 12.0 %collective-permute-start.17 = (f32[1056,128]{1,0:T(8,128)S(1)}, f32[1056,128]{1,0:T(8,128)S(1)}, u32[]{:S(2)}, u32[]{:S(2)}) collective-permute-start(f32[1056,128]{1,0:T(8,128)S(1)} %get-tuple-element.91.refs_0_), channel_id=1, source_target_pairs={{0,16},{16,0},{1,17},{17,1},{2,18},{18,2},{3,19},{19,3},{4,20},{20... | collective-permute-start | bytes 1622024 | tf_op jit(solution)/shard_map/ppermute | solution.py:706
  99.7 2.4 %collective-permute-start.19 = (f32[1056,128]{1,0:T(8,128)S(1)}, f32[1056,128]{1,0:T(8,128)S(1)}, u32[]{:S(2)}, u32[]{:S(2)}) collective-permute-start(f32[1056,128]{1,0:T(8,128)S(1)} %sum_far.1.refs_2_), channel_id=1, source_target_pairs={{0,16},{16,0},{1,17},{17,1},{2,18},{18,2},{3,19},{19,3},{4,20},{20... | collective-permute-start | bytes 1622024 | tf_op jit(solution)/shard_map/ppermute | solution.py:706
  100.2 1.9 %collective-permute-start.18 = (bf16[1056,128]{1,0:T(8,128)(2,1)S(1)}, bf16[1056,128]{1,0:T(8,128)(2,1)S(1)}, u32[]{:S(2)}, u32[]{:S(2)}) collective-permute-start(bf16[1056,128]{1,0:T(8,128)(2,1)S(1)} %collective-permute-done.14.refs_1_), channel_id=1, source_target_pairs={{0,16},{16,0},{1,17},{17,1},{2,18},{18,2},{3,19},{19,3},{4,20},{20... | collective-permute-start | bytes 811016 | tf_op jit(solution)/shard_map/ppermute | solution.py:706

commit v14 on v12

--- a/solution.py
+++ b/solution.py
@@ -83,7 +83,7 @@
     return np.concatenate([cosine, cosine], axis=1), np.concatenate([sine, sine], axis=1)
 
 
-def pick_kernel(half, own, block, *refs):
+def pick_kernel(half, block, *refs):
     outs, rows = refs[:-1], refs[-1]
     inputs, samples = block.shape[1], block.shape[2]
     step = 32
@@ -99,14 +99,14 @@
 
         lax.fori_loop(0, samples // LANES // step, spread, 0)
     g = position()[2]
-    first = (g if own else 1 - g) * half
     tall = 64
 
     def gather(n, carry):
         low = pl.multiple_of(n * tall, tall)
-        for item in range(half):
+        for item in range(inputs):
+            first = (1 - g) * half + item if item < half else g * half + item - half
             for part in range(2):
-                at = low * inputs + first + item
+                at = low * inputs + first
                 value = rows[part, pl.ds(at, tall, stride=inputs), :].astype(jnp.bfloat16)
                 outs[item // JOIN][item % JOIN, part, pl.ds(low, tall), :] = value
         return carry
@@ -114,17 +114,16 @@
     lax.fori_loop(0, samples // LANES // tall, gather, 0)
 
 
-def pick(block, own):
+def pick(block):
     _, inputs, samples = block.shape
-    half = inputs // PAIR
     shape = jax.ShapeDtypeStruct((JOIN, 2, samples // LANES, LANES), jnp.bfloat16)
     return pl.pallas_call(
-        functools.partial(pick_kernel, half, own),
-        out_shape=[shape] * (half // JOIN),
+        functools.partial(pick_kernel, inputs // PAIR),
+        out_shape=[shape] * (inputs // JOIN),
         in_specs=[VMEM],
-        out_specs=[VMEM] * (half // JOIN),
+        out_specs=[VMEM] * (inputs // JOIN),
         scratch_shapes=[pltpu.VMEM((2, samples // LANES * inputs, LANES), jnp.float32)],
-        compiler_params=params(12),
+        compiler_params=params(16),
         cost_estimate=cost(10**6, 2**18),
         name="pick",
     )(block)
@@ -649,8 +648,8 @@
     tables = [jnp.asarray(t) for t in tables + [np.concatenate([base, base], axis=1)]]
 
     parts = half // JOIN
-    sends = pick(voltages, False)
-    keeps = pick(follow(voltages, sends[0]), True)
+    picked = pick(voltages)
+    sends, keeps = picked[:parts], picked[parts:]
     recvs = [lax.ppermute(block, "tm", swap) for block in sends]
     halos, lates = [], []
     for c in range(parts):

time: 114 us -> 101 us (0.89)
  waiting for transfers between devices: 46.8 us -> 37 us
  Pallas kernels: 36.7 us -> 35.1 us
    ppermute x2, waiting for transfers between devices: 8.77 us -> 0.01 us  [fast(): halos.append(lax.ppermute(jnp.where(g == 1, keeps[c], recv), 'tm', onward))]
    ppermute x2, waiting for transfers between devices: 18.3 us -> 15.4 us  [fast(): recvs = [lax.ppermute(block, 'tm', swap) for block in sends]]
    ppermute x6, waiting for transfers between devices: 0.02 us -> 2.28 us  [fast(): block = lax.ppermute(block, ('tm', 'ct'), route)]
    pallas_call x2 -> x1, Pallas kernels: 2.5 us -> 1.89 us  [pick(): pl.pallas_call(functools.partial(pick_kernel, inputs // PAIR), out_shape=...]
  transfers between devices with their start and end apart: 20 -> 20, of which waited for: 8 -> 9; matrix products, arithmetic and copies ran while one was open for 0% -> 0% of each run, Pallas kernels for 24% -> 25%
where the time goes in v14:
time: 101 us
  waiting for transfers between devices  37 us (37%)
  Pallas kernels  35.1 us (35%)
  starting transfers between devices  26.7 us (26%)
  local copies, waits for them, and re-layouts  1.67 us (2%)
    pallas_call x3, Pallas kernels, correlate(): pl.pallas_call(functools.partial(correlate_kernel, layout), out_shape=[ja...  15.8 us
    ppermute x2, waiting for transfers between devices, fast(): recvs = [lax.ppermute(block, 'tm', swap) for block in sends]  15.4 us
    pallas_call x4, Pallas kernels, filterbank(): pl.pallas_call(kernel, out_shape=[jax.ShapeDtypeStruct(shape, jnp.bfloat1...  15.3 us
    ppermute x5, waiting for transfers between devices, along(): return lax.ppermute(block, 'tm', route)  14.9 us
    ppermute x5, starting transfers between devices, along(): return lax.ppermute(block, 'tm', route)  8.5 us
    ppermute x2, starting transfers between devices, fast(): halos.append(lax.ppermute(jnp.where(g == 1, keeps[c], recv), 'tm', onward))  7.85 us
    ppermute x6, starting transfers between devices, fast(): block = lax.ppermute(block, ('tm', 'ct'), route)  7.11 us
    ppermute x2, starting transfers between devices, fast(): recvs = [lax.ppermute(block, 'tm', swap) for block in sends]  2.97 us
  transfers between devices with their start and end apart: 20, of which 9 were waited for; matrix products, arithmetic and copies ran while one was open for 0% of the time, Pallas kernels for 25%

profile of v14, /device:TPU:0, one launch (start us, length us, event | category | flops | bytes accessed | tf_op | source)
XLA Modules:
  0.0 100.8 jit_solution(13191301579332118035)
XLA Ops:
  0.0 1.6 %copy-done.1 = bf16[2,8,65536]{2,1,0:T(8,128)(2,1)S(1)} copy-done((bf16[2,8,65536]{2,1,0:T(8,128)(2,1)S(1)}, bf16[2,8,65536]{2,1,0:T(8,128)(2,1)}, u32[]{:S(2)}) %copy-start.1) | copy-done | bytes 2097176
  1.7 1.9 %pick.1 = (bf16[2,2,512,128]{3,2,1,0:T(8,128)(2,1)}, bf16[2,2,512,128]{3,2,1,0:T(8,128)(2,1)S(1)}, bf16[2,2,512,128]{3,2,1,0:T(8,128)(2,1)S(1)}, bf16[2,2,512,128]{3,2,1,0:T(8,128)(2,1)S(1)}) custom-call(bf16[2,8,65536]{2,1,0:T(8,128)(2,1)S(1)} %copy-done.1), custom_call_target="tpu_custom_call" | custom-call | flops 1000000 | bytes 262144 | tf_op jit(solution)/shard_map/pick/pallas_call | solution.py:120
  3.6 2.9 %collective-permute-start = (bf16[2,2,512,128]{3,2,1,0:T(8,128)(2,1)}, bf16[2,2,512,128]{3,2,1,0:T(8,128)(2,1)S(1)}, u32[]{:S(2)}, u32[]{:S(2)}) collective-permute-start(bf16[2,2,512,128]{3,2,1,0:T(8,128)(2,1)} %get-tuple-element.50), channel_id=1, source_target_pairs={{0,2},{2,0},{4,6},{6,4},{8,10},{10,8},{12,14},{14,12},{1,3},{3,1},... | collective-permute-start | bytes 1572872 | tf_op jit(solution)/shard_map/ppermute | solution.py:653
  6.5 0.0 collective-permute-start.2
  6.5 12.9 %collective-permute-done.refs_2_.refs_3_ = bf16[2,2,512,128]{3,2,1,0:T(8,128)(2,1)S(1)} collective-permute-done((bf16[2,2,512,128]{3,2,1,0:T(8,128)(2,1)}, bf16[2,2,512,128]{3,2,1,0:T(8,128)(2,1)S(1)}, u32[]{:S(2)}, u32[]{:S(2)}) %collective-permute-start) | collective-permute-done | bytes 524320 | tf_op jit(solution)/shard_map/ppermute | solution.py:653
  19.5 0.1 broadcast_select_fusion.1
  19.5 4.1 %collective-permute-start.1 = (bf16[2,2,512,128]{3,2,1,0:T(8,128)(2,1)S(1)}, bf16[2,2,512,128]{3,2,1,0:T(8,128)(2,1)S(1)}, u32[]{:S(2)}, u32[]{:S(2)}) collective-permute-start(bf16[2,2,512,128]{3,2,1,0:T(8,128)(2,1)S(1)} %broadcast_select_fusion.1), channel_id=1, source_target_pairs={{0,4},{2,6},{4,8},{6,10},{8,12},{10,14},{1,5},{3,7},{5,9},{7,11},{... | collective-permute-start | bytes 1572872 | tf_op jit(solution)/shard_map/ppermute | solution.py:657
  23.7 3.8 %filterbank_late.2 = (bf16[2,8,2,16,128]{4,3,2,1,0:T(8,128)(2,1)S(1)}, bf16[2,8,2,16,128]{4,3,2,1,0:T(8,128)(2,1)S(1)}, bf16[2,8,2,16,128]{4,3,2,1,0:T(8,128)(2,1)S(1)}, bf16[2,8,2,16,128]{4,3,2,1,0:T(8,128)(2,1)S(1)}) custom-call(s32[8]{0:T(128)S(1)} %copy-done.6, bf16[2,2,512,128]{3,2,1,0:T(8,128)(2,1)S(1)} %get-tuple-element.49.refs_1_.refs_2_, ...), custom_call_target="tpu_custom_call" | custom-call | flops 1000000 | bytes 262144 | tf_op jit(solution)/shard_map/filterbank_late/pallas_call | solution.py:310
  27.4 2.4 %collective-permute-done.2.refs_2_.refs_3_ = bf16[2,2,512,128]{3,2,1,0:T(8,128)(2,1)S(1)} collective-permute-done((bf16[2,2,512,128]{3,2,1,0:T(8,128)(2,1)S(1)}, bf16[2,2,512,128]{3,2,1,0:T(8,128)(2,1)S(1)}, u32[]{:S(2)}, u32[]{:S(2)}) %collective-permute-start.2) | collective-permute-done | bytes 524320 | tf_op jit(solution)/shard_map/ppermute | solution.py:653
  29.9 0.1 broadcast_select_fusion
  29.9 3.8 %collective-permute-start.3 = (bf16[2,2,512,128]{3,2,1,0:T(8,128)(2,1)S(1)}, bf16[2,2,512,128]{3,2,1,0:T(8,128)(2,1)S(1)}, u32[]{:S(2)}, u32[]{:S(2)}) collective-permute-start(bf16[2,2,512,128]{3,2,1,0:T(8,128)(2,1)S(1)} %broadcast_select_fusion), channel_id=1, source_target_pairs={{0,4},{2,6},{4,8},{6,10},{8,12},{10,14},{1,5},{3,7},{5,9},{7,11},{... | collective-permute-start | bytes 1572872 | tf_op jit(solution)/shard_map/ppermute | solution.py:657
  33.7 3.8 %filterbank_early.2 = (bf16[2,16,2,16,128]{4,3,2,1,0:T(8,128)(2,1)S(1)}, bf16[2,16,2,16,128]{4,3,2,1,0:T(8,128)(2,1)S(1)}, bf16[2,16,2,16,128]{4,3,2,1,0:T(8,128)(2,1)S(1)}, bf16[2,16,2,16,128]{4,3,2,1,0:T(8,128)(2,1)S(1)}) custom-call(s32[8]{0:T(128)S(1)} %copy-done.6, bf16[2,2,512,128]{3,2,1,0:T(8,128)(2,1)S(1)} %collective-permute-done.1.refs_1_, ...), custom_call_target="tpu_custom_call" | custom-call | flops 1000000 | bytes 262144 | tf_op jit(solution)/shard_map/filterbank_early/pallas_call | solution.py:310
  37.5 2.5 %collective-permute-start.6 = (bf16[2,16,2,16,128]{4,3,2,1,0:T(8,128)(2,1)S(1)}, bf16[2,16,2,16,128]{4,3,2,1,0:T(8,128)(2,1)S(1)}, u32[]{:S(2)}, u32[]{:S(2)}) collective-permute-start(bf16[2,16,2,16,128]{4,3,2,1,0:T(8,128)(2,1)S(1)} %get-tuple-element.71), channel_id=1, source_target_pairs={{0,3},{1,2},{2,1},{3,0},{4,7},{5,6},{6,5},{7,4},{8,11},{9,10},{10,... | collective-permute-start | bytes 786440 | tf_op jit(solution)/shard_map/ppermute | solution.py:677
  40.0 0.5 collective-permute-start.5
  40.6 0.5 collective-permute-start.4
  41.1 3.7 %filterbank_late.3 = (bf16[2,8,2,16,128]{4,3,2,1,0:T(8,128)(2,1)S(1)}, bf16[2,8,2,16,128]{4,3,2,1,0:T(8,128)(2,1)S(1)}, bf16[2,8,2,16,128]{4,3,2,1,0:T(8,128)(2,1)S(1)}, bf16[2,8,2,16,128]{4,3,2,1,0:T(8,128)(2,1)S(1)}) custom-call(s32[8]{0:T(128)S(1)} %copy-done.6, bf16[2,2,512,128]{3,2,1,0:T(8,128)(2,1)S(1)} %get-tuple-element.58.refs_1_.refs_2_, ...), custom_call_target="tpu_custom_call" | custom-call | flops 1000000 | bytes 262144 | tf_op jit(solution)/shard_map/filterbank_late/pallas_call | solution.py:310
  44.8 0.0 collective-permute-done.3.refs_1_
  44.8 4.0 %filterbank_early.3 = (bf16[2,16,2,16,128]{4,3,2,1,0:T(8,128)(2,1)S(1)}, bf16[2,16,2,16,128]{4,3,2,1,0:T(8,128)(2,1)S(1)}, bf16[2,16,2,16,128]{4,3,2,1,0:T(8,128)(2,1)S(1)}, bf16[2,16,2,16,128]{4,3,2,1,0:T(8,128)(2,1)S(1)}) custom-call(s32[8]{0:T(128)S(1)} %copy-done.6, bf16[2,2,512,128]{3,2,1,0:T(8,128)(2,1)S(1)} %collective-permute-done.3.refs_1_, ...), custom_call_target="tpu_custom_call" | custom-call | flops 1000000 | bytes 262144 | tf_op jit(solution)/shard_map/filterbank_early/pallas_call | solution.py:310
  48.8 0.0 collective-permute-done.6.refs_3_
  48.8 2.3 %collective-permute-done.5.refs_2_ = bf16[2,16,2,16,128]{4,3,2,1,0:T(8,128)(2,1)S(1)} collective-permute-done((bf16[2,16,2,16,128]{4,3,2,1,0:T(8,128)(2,1)S(1)}, bf16[2,16,2,16,128]{4,3,2,1,0:T(8,128)(2,1)S(1)}, u32[]{:S(2)}, u32[]{:S(2)}) %collective-permute-start.5) | collective-permute-done | bytes 262176 | tf_op jit(solution)/shard_map/ppermute | solution.py:677
  51.1 0.0 collective-permute-done.4.refs_1_
  51.1 0.2 join.2.refs_0_
  51.3 0.1 collective-permute-start.7
  51.4 2.4 %collective-permute-start.12 = (bf16[2,16,2,16,128]{4,3,2,1,0:T(8,128)(2,1)S(1)}, bf16[2,16,2,16,128]{4,3,2,1,0:T(8,128)(2,1)S(1)}, u32[]{:S(2)}, u32[]{:S(2)}) collective-permute-start(bf16[2,16,2,16,128]{4,3,2,1,0:T(8,128)(2,1)S(1)} %get-tuple-element.83), channel_id=1, source_target_pairs={{0,3},{1,2},{2,1},{3,0},{4,7},{5,6},{6,5},{7,4},{8,11},{9,10},{10,... | collective-permute-start | bytes 786440 | tf_op jit(solution)/shard_map/ppermute | solution.py:677
  53.8 0.5 collective-permute-start.11
  54.3 0.6 collective-permute-start.10
  54.9 0.0 collective-permute-done.7.refs_1_.refs_2_
  54.9 4.0 %correlate_early.1 = (f32[272,128]{1,0:T(8,128)S(1)}, bf16[272,128]{1,0:T(8,128)(2,1)S(1)}, bf16[272,128]{1,0:T(8,128)(2,1)S(1)}, bf16[272,128]{1,0:T(8,128)(2,1)S(1)}) custom-call(bf16[8,16,2,16,128]{4,3,2,1,0:T(8,128)(2,1)S(1)} %join.2.refs_0_, bf16[8,16,2,16,128]{4,3,2,1,0:T(8,128)(2,1)S(1)} %collective-permute-done.7.refs_1_.refs_2_), custom_call_target="tpu_custom_call" | custom-call | flops 1000000 | bytes 262144 | tf_op jit(solution)/shard_map/correlate_early/pallas_call | solution.py:476
  58.9 2.6 %collective-permute-start.8 = (bf16[272,128]{1,0:T(8,128)(2,1)S(1)}, bf16[272,128]{1,0:T(8,128)(2,1)S(1)}, u32[]{:S(2)}, u32[]{:S(2)}) collective-permute-start(bf16[272,128]{1,0:T(8,128)(2,1)S(1)} %get-tuple-element.73), channel_id=1, source_target_pairs={{0,8},{2,10},{4,12},{6,14},{8,0},{10,2},{12,4},{14,6},{1,9},{3,11}... | collective-permute-start | bytes 208904 | tf_op jit(solution)/shard_map/ppermute | solution.py:683
  61.5 1.3 %collective-permute-start.9 = (bf16[272,128]{1,0:T(8,128)(2,1)S(1)}, bf16[272,128]{1,0:T(8,128)(2,1)S(1)}, u32[]{:S(2)}, u32[]{:S(2)}) collective-permute-start(bf16[272,128]{1,0:T(8,128)(2,1)S(1)} %get-tuple-element.74), channel_id=1, source_target_pairs={{0,12},{2,14},{4,8},{6,10},{8,4},{10,6},{12,0},{14,2},{1,13},{3,15... | collective-permute-start | bytes 208904 | tf_op jit(solution)/shard_map/ppermute | solution.py:683
  62.9 3.5 %collective-permute-done.8.refs_0_ = bf16[272,128]{1,0:T(8,128)(2,1)S(1)} collective-permute-done((bf16[272,128]{1,0:T(8,128)(2,1)S(1)}, bf16[272,128]{1,0:T(8,128)(2,1)S(1)}, u32[]{:S(2)}, u32[]{:S(2)}) %collective-permute-start.8) | collective-permute-done | bytes 69664 | tf_op jit(solution)/shard_map/ppermute | solution.py:683
  66.4 1.4 %collective-permute-done.9.refs_1_ = bf16[272,128]{1,0:T(8,128)(2,1)S(1)} collective-permute-done((bf16[272,128]{1,0:T(8,128)(2,1)S(1)}, bf16[272,128]{1,0:T(8,128)(2,1)S(1)}, u32[]{:S(2)}, u32[]{:S(2)}) %collective-permute-start.9) | collective-permute-done | bytes 69664 | tf_op jit(solution)/shard_map/ppermute | solution.py:683
  67.7 0.0 collective-permute-done.11.refs_2_
  67.7 0.2 join.3.refs_1_
  67.9 0.1 collective-permute-start.13
  68.0 2.6 %collective-permute-done.13.refs_3_ = bf16[8,16,2,16,128]{4,3,2,1,0:T(8,128)(2,1)S(1)} collective-permute-done((bf16[8,16,2,16,128]{4,3,2,1,0:T(8,128)(2,1)S(1)}, bf16[8,16,2,16,128]{4,3,2,1,0:T(8,128)(2,1)S(1)}, u32[]{:S(2)}, u32[]{:S(2)}) %collective-permute-start.13) | collective-permute-done | bytes 1048608 | tf_op jit(solution)/shard_map/ppermute | solution.py:693
  70.7 5.9 %correlate_far.1 = (bf16[784,128]{1,0:T(8,128)(2,1)S(1)}, bf16[784,128]{1,0:T(8,128)(2,1)S(1)}) custom-call(bf16[8,16,2,16,128]{4,3,2,1,0:T(8,128)(2,1)S(1)} %join.2.refs_0_, bf16[8,16,2,16,128]{4,3,2,1,0:T(8,128)(2,1)S(1)} %join.3.refs_1_, bf16[8,16,2,16,128]{4,3,2,1,0:T(8,128)(2,1)S(1)} %collective-permute-done.7.refs_1_.refs_2_, ...), custom_call_target="tpu_custom_call" | custom-call | flops 1000000 | bytes 262144 | tf_op jit(solution)/shard_map/correlate_far/pallas_call | solution.py:476
  76.6 1.4 %collective-permute-start.16 = (bf16[784,128]{1,0:T(8,128)(2,1)S(1)}, bf16[784,128]{1,0:T(8,128)(2,1)S(1)}, u32[]{:S(2)}, u32[]{:S(2)}) collective-permute-start(bf16[784,128]{1,0:T(8,128)(2,1)S(1)} %get-tuple-element.91), channel_id=1, source_target_pairs={{0,12},{2,14},{4,8},{6,10},{8,4},{10,6},{12,0},{14,2},{1,13},{3,15... | collective-permute-start | bytes 602120 | tf_op jit(solution)/shard_map/ppermute | solution.py:683
  78.0 0.9 collective-permute-start.15
  78.8 5.9 %correlate_near.1 = (f32[1056,128]{1,0:T(8,128)S(1)}, bf16[1056,128]{1,0:T(8,128)(2,1)S(1)}) custom-call(bf16[8,16,2,16,128]{4,3,2,1,0:T(8,128)(2,1)S(1)} %join.2.refs_0_, bf16[8,16,2,16,128]{4,3,2,1,0:T(8,128)(2,1)S(1)} %join.3.refs_1_, bf16[8,16,2,16,128]{4,3,2,1,0:T(8,128)(2,1)S(1)} %collective-permute-done.7.refs_1_.refs_2_, ...), custom_call_target="tpu_custom_call" | custom-call | flops 1000000 | bytes 262144 | tf_op jit(solution)/shard_map/correlate_near/pallas_call | solution.py:476
  84.8 2.3 %collective-permute-start.14 = (bf16[1056,128]{1,0:T(8,128)(2,1)S(1)}, bf16[1056,128]{1,0:T(8,128)(2,1)S(1)}, u32[]{:S(2)}, u32[]{:S(2)}) collective-permute-start(bf16[1056,128]{1,0:T(8,128)(2,1)S(1)} %get-tuple-element.90), channel_id=1, source_target_pairs={{0,4},{2,6},{4,0},{6,2},{8,12},{10,14},{12,8},{14,10},{1,5},{3,7},... | collective-permute-start | bytes 811016 | tf_op jit(solution)/shard_map/ppermute | solution.py:683
  87.1 9.6 %collective-permute-done.15.refs_2_ = bf16[784,128]{1,0:T(8,128)(2,1)S(1)} collective-permute-done((bf16[784,128]{1,0:T(8,128)(2,1)S(1)}, bf16[784,128]{1,0:T(8,128)(2,1)S(1)}, u32[]{:S(2)}, u32[]{:S(2)}) %collective-permute-start.15) | collective-permute-done | bytes 200736 | tf_op jit(solution)/shard_map/ppermute | solution.py:683
  96.6 0.1 sum_far.1.refs_2_
  96.7 0.1 collective-permute-start.19
  96.8 0.4 collective-permute-done.14.refs_1_
  97.2 0.1 collective-permute-start.18
  97.3 1.8 %collective-permute-done.18.refs_4_ = bf16[1056,128]{1,0:T(8,128)(2,1)S(1)} collective-permute-done((bf16[1056,128]{1,0:T(8,128)(2,1)S(1)}, bf16[1056,128]{1,0:T(8,128)(2,1)S(1)}, u32[]{:S(2)}, u32[]{:S(2)}) %collective-permute-start.18) | collective-permute-done | bytes 270368 | tf_op jit(solution)/shard_map/ppermute | solution.py:705
  99.1 1.7 %assemble.1 = f32[2,16,32,256]{3,2,1,0:T(8,128)} custom-call(f32[1056,128]{1,0:T(8,128)S(1)} %get-tuple-element.89.refs_0_, bf16[1056,128]{1,0:T(8,128)(2,1)S(1)} %collective-permute-done.14.refs_1_, f32[1056,128]{1,0:T(8,128)S(1)} %sum_far.1.refs_2_, f32[1056,128]{1,0:T(8,128)S(1)} %collective-permute-done.17.refs_3_, ...), custom_call_target="tpu_custom_call" | custom-call | flops 1000000 | bytes 262144 | tf_op jit(solution)/shard_map/assemble/pallas_call | solution.py:598
  (20 shorter events, 0.0 us)
Async XLA Ops:
  0.0 23.6 %copy-start = (f32[16,64,128]{2,1,0:T(8,128)S(1)}, f32[16,64,128]{2,1,0:T(8,128)}, u32[]{:S(2)}) copy-start(f32[16,64,128]{2,1,0:T(8,128)} %constant.30.clone.refs_3_.refs_4_) | copy-start | bytes 1572868
  0.0 1.6 %copy-start.1 = (bf16[2,8,65536]{2,1,0:T(8,128)(2,1)S(1)}, bf16[2,8,65536]{2,1,0:T(8,128)(2,1)}, u32[]{:S(2)}) copy-start(bf16[2,8,65536]{2,1,0:T(8,128)(2,1)} %block.1) | copy-start | bytes 6291460
  1.7 22.0 %copy-start.2 = (bf16[2,4,32,128]{3,2,1,0:T(8,128)(2,1)S(1)}, bf16[2,4,32,128]{3,2,1,0:T(8,128)(2,1)}, u32[]{:S(2)}) copy-start(bf16[2,4,32,128]{3,2,1,0:T(8,128)(2,1)} %constant.34.clone.refs_7_.refs_8_) | copy-start | bytes 196612
  1.7 22.0 %copy-start.3 = (f32[64,128]{1,0:T(8,128)S(1)}, f32[64,128]{1,0:T(8,128)}, u32[]{:S(2)}) copy-start(f32[64,128]{1,0:T(8,128)} %constant.33.clone.refs_6_.refs_7_) | copy-start | bytes 98308
  1.7 22.0 %copy-start.4 = (f32[64,128]{1,0:T(8,128)S(1)}, f32[64,128]{1,0:T(8,128)}, u32[]{:S(2)}) copy-start(f32[64,128]{1,0:T(8,128)} %constant.32.clone.refs_5_.refs_6_) | copy-start | bytes 98308
  1.7 22.0 %copy-start.5 = (bf16[128,128]{1,0:T(8,128)(2,1)S(1)}, bf16[128,128]{1,0:T(8,128)(2,1)}, u32[]{:S(2)}) copy-start(bf16[128,128]{1,0:T(8,128)(2,1)} %constant.31.clone.refs_4_.refs_5_) | copy-start | bytes 98308
  1.7 22.0 %copy-start.6 = (s32[8]{0:T(128)S(1)}, s32[8]{0:T(128)}, u32[]{:S(2)}) copy-start(s32[8]{0:T(128)} %refs_0_.7) | copy-start | bytes 100
  3.6 15.9 %collective-permute-start = (bf16[2,2,512,128]{3,2,1,0:T(8,128)(2,1)}, bf16[2,2,512,128]{3,2,1,0:T(8,128)(2,1)S(1)}, u32[]{:S(2)}, u32[]{:S(2)}) collective-permute-start(bf16[2,2,512,128]{3,2,1,0:T(8,128)(2,1)} %get-tuple-element.50), channel_id=1, source_target_pairs={{0,2},{2,0},{4,6},{6,4},{8,10},{10,8},{12,14},{14,12},{1,3},{3,1},... | collective-permute-start | bytes 1572872 | tf_op jit(solution)/shard_map/ppermute | solution.py:653
  6.5 23.4 %collective-permute-start.2 = (bf16[2,2,512,128]{3,2,1,0:T(8,128)(2,1)S(1)}, bf16[2,2,512,128]{3,2,1,0:T(8,128)(2,1)S(1)}, u32[]{:S(2)}, u32[]{:S(2)}) collective-permute-start(bf16[2,2,512,128]{3,2,1,0:T(8,128)(2,1)S(1)} %get-tuple-element.51), channel_id=1, source_target_pairs={{0,2},{2,0},{4,6},{6,4},{8,10},{10,8},{12,14},{14,12},{1,3},{3,1},... | collective-permute-start | bytes 1572872 | tf_op jit(solution)/shard_map/ppermute | solution.py:653
  19.5 14.2 %collective-permute-start.1 = (bf16[2,2,512,128]{3,2,1,0:T(8,128)(2,1)S(1)}, bf16[2,2,512,128]{3,2,1,0:T(8,128)(2,1)S(1)}, u32[]{:S(2)}, u32[]{:S(2)}) collective-permute-start(bf16[2,2,512,128]{3,2,1,0:T(8,128)(2,1)S(1)} %broadcast_select_fusion.1), channel_id=1, source_target_pairs={{0,4},{2,6},{4,8},{6,10},{8,12},{10,14},{1,5},{3,7},{5,9},{7,11},{... | collective-permute-start | bytes 1572872 | tf_op jit(solution)/shard_map/ppermute | solution.py:657
  29.9 14.9 %collective-permute-start.3 = (bf16[2,2,512,128]{3,2,1,0:T(8,128)(2,1)S(1)}, bf16[2,2,512,128]{3,2,1,0:T(8,128)(2,1)S(1)}, u32[]{:S(2)}, u32[]{:S(2)}) collective-permute-start(bf16[2,2,512,128]{3,2,1,0:T(8,128)(2,1)S(1)} %broadcast_select_fusion), channel_id=1, source_target_pairs={{0,4},{2,6},{4,8},{6,10},{8,12},{10,14},{1,5},{3,7},{5,9},{7,11},{... | collective-permute-start | bytes 1572872 | tf_op jit(solution)/shard_map/ppermute | solution.py:657
  37.5 11.3 %collective-permute-start.6 = (bf16[2,16,2,16,128]{4,3,2,1,0:T(8,128)(2,1)S(1)}, bf16[2,16,2,16,128]{4,3,2,1,0:T(8,128)(2,1)S(1)}, u32[]{:S(2)}, u32[]{:S(2)}) collective-permute-start(bf16[2,16,2,16,128]{4,3,2,1,0:T(8,128)(2,1)S(1)} %get-tuple-element.71), channel_id=1, source_target_pairs={{0,3},{1,2},{2,1},{3,0},{4,7},{5,6},{6,5},{7,4},{8,11},{9,10},{10,... | collective-permute-start | bytes 786440 | tf_op jit(solution)/shard_map/ppermute | solution.py:677
  40.0 11.1 %collective-permute-start.5 = (bf16[2,16,2,16,128]{4,3,2,1,0:T(8,128)(2,1)S(1)}, bf16[2,16,2,16,128]{4,3,2,1,0:T(8,128)(2,1)S(1)}, u32[]{:S(2)}, u32[]{:S(2)}) collective-permute-start(bf16[2,16,2,16,128]{4,3,2,1,0:T(8,128)(2,1)S(1)} %get-tuple-element.69), channel_id=1, source_target_pairs={{0,2},{1,3},{2,0},{3,1},{4,6},{5,7},{6,4},{7,5},{8,10},{9,11},{10,... | collective-permute-start | bytes 786440 | tf_op jit(solution)/shard_map/ppermute | solution.py:677
  40.6 10.5 %collective-permute-start.4 = (bf16[2,16,2,16,128]{4,3,2,1,0:T(8,128)(2,1)S(1)}, bf16[2,16,2,16,128]{4,3,2,1,0:T(8,128)(2,1)S(1)}, u32[]{:S(2)}, u32[]{:S(2)}) collective-permute-start(bf16[2,16,2,16,128]{4,3,2,1,0:T(8,128)(2,1)S(1)} %get-tuple-element.67), channel_id=1, source_target_pairs={{0,1},{1,0},{2,3},{3,2},{4,5},{5,4},{6,7},{7,6},{8,9},{9,8},{10,11... | collective-permute-start | bytes 786440 | tf_op jit(solution)/shard_map/ppermute | solution.py:677
  51.3 3.6 %collective-permute-start.7 = (bf16[8,16,2,16,128]{4,3,2,1,0:T(8,128)(2,1)S(1)}, bf16[8,16,2,16,128]{4,3,2,1,0:T(8,128)(2,1)S(1)}, u32[]{:S(2)}, u32[]{:S(2)}) collective-permute-start(bf16[8,16,2,16,128]{4,3,2,1,0:T(8,128)(2,1)S(1)} %join.2.refs_0_), channel_id=1, source_target_pairs={{0,16},{16,0},{1,17},{17,1},{2,18},{18,2},{3,19},{19,3},{4,20},{20... | collective-permute-start | bytes 3145736 | tf_op jit(solution)/shard_map/ppermute | solution.py:686
  51.4 11.5 %collective-permute-start.12 = (bf16[2,16,2,16,128]{4,3,2,1,0:T(8,128)(2,1)S(1)}, bf16[2,16,2,16,128]{4,3,2,1,0:T(8,128)(2,1)S(1)}, u32[]{:S(2)}, u32[]{:S(2)}) collective-permute-start(bf16[2,16,2,16,128]{4,3,2,1,0:T(8,128)(2,1)S(1)} %get-tuple-element.83), channel_id=1, source_target_pairs={{0,3},{1,2},{2,1},{3,0},{4,7},{5,6},{6,5},{7,4},{8,11},{9,10},{10,... | collective-permute-start | bytes 786440 | tf_op jit(solution)/shard_map/ppermute | solution.py:677
  53.8 14.0 %collective-permute-start.11 = (bf16[2,16,2,16,128]{4,3,2,1,0:T(8,128)(2,1)S(1)}, bf16[2,16,2,16,128]{4,3,2,1,0:T(8,128)(2,1)S(1)}, u32[]{:S(2)}, u32[]{:S(2)}) collective-permute-start(bf16[2,16,2,16,128]{4,3,2,1,0:T(8,128)(2,1)S(1)} %get-tuple-element.80), channel_id=1, source_target_pairs={{0,2},{1,3},{2,0},{3,1},{4,6},{5,7},{6,4},{7,5},{8,10},{9,11},{10,... | collective-permute-start | bytes 786440 | tf_op jit(solution)/shard_map/ppermute | solution.py:677
  54.3 13.4 %collective-permute-start.10 = (bf16[2,16,2,16,128]{4,3,2,1,0:T(8,128)(2,1)S(1)}, bf16[2,16,2,16,128]{4,3,2,1,0:T(8,128)(2,1)S(1)}, u32[]{:S(2)}, u32[]{:S(2)}) collective-permute-start(bf16[2,16,2,16,128]{4,3,2,1,0:T(8,128)(2,1)S(1)} %get-tuple-element.77), channel_id=1, source_target_pairs={{0,1},{1,0},{2,3},{3,2},{4,5},{5,4},{6,7},{7,6},{8,9},{9,8},{10,11... | collective-permute-start | bytes 786440 | tf_op jit(solution)/shard_map/ppermute | solution.py:677
  58.9 7.5 %collective-permute-start.8 = (bf16[272,128]{1,0:T(8,128)(2,1)S(1)}, bf16[272,128]{1,0:T(8,128)(2,1)S(1)}, u32[]{:S(2)}, u32[]{:S(2)}) collective-permute-start(bf16[272,128]{1,0:T(8,128)(2,1)S(1)} %get-tuple-element.73), channel_id=1, source_target_pairs={{0,8},{2,10},{4,12},{6,14},{8,0},{10,2},{12,4},{14,6},{1,9},{3,11}... | collective-permute-start | bytes 208904 | tf_op jit(solution)/shard_map/ppermute | solution.py:683
  61.5 6.2 %collective-permute-start.9 = (bf16[272,128]{1,0:T(8,128)(2,1)S(1)}, bf16[272,128]{1,0:T(8,128)(2,1)S(1)}, u32[]{:S(2)}, u32[]{:S(2)}) collective-permute-start(bf16[272,128]{1,0:T(8,128)(2,1)S(1)} %get-tuple-element.74), channel_id=1, source_target_pairs={{0,12},{2,14},{4,8},{6,10},{8,4},{10,6},{12,0},{14,2},{1,13},{3,15... | collective-permute-start | bytes 208904 | tf_op jit(solution)/shard_map/ppermute | solution.py:683
  67.9 2.7 %collective-permute-start.13 = (bf16[8,16,2,16,128]{4,3,2,1,0:T(8,128)(2,1)S(1)}, bf16[8,16,2,16,128]{4,3,2,1,0:T(8,128)(2,1)S(1)}, u32[]{:S(2)}, u32[]{:S(2)}) collective-permute-start(bf16[8,16,2,16,128]{4,3,2,1,0:T(8,128)(2,1)S(1)} %join.3.refs_1_), channel_id=1, source_target_pairs={{0,16},{16,0},{1,17},{17,1},{2,18},{18,2},{3,19},{19,3},{4,20},{20... | collective-permute-start | bytes 3145736 | tf_op jit(solution)/shard_map/ppermute | solution.py:693
  76.6 10.5 %collective-permute-start.16 = (bf16[784,128]{1,0:T(8,128)(2,1)S(1)}, bf16[784,128]{1,0:T(8,128)(2,1)S(1)}, u32[]{:S(2)}, u32[]{:S(2)}) collective-permute-start(bf16[784,128]{1,0:T(8,128)(2,1)S(1)} %get-tuple-element.91), channel_id=1, source_target_pairs={{0,12},{2,14},{4,8},{6,10},{8,4},{10,6},{12,0},{14,2},{1,13},{3,15... | collective-permute-start | bytes 602120 | tf_op jit(solution)/shard_map/ppermute | solution.py:683
  78.0 18.7 %collective-permute-start.15 = (bf16[784,128]{1,0:T(8,128)(2,1)S(1)}, bf16[784,128]{1,0:T(8,128)(2,1)S(1)}, u32[]{:S(2)}, u32[]{:S(2)}) collective-permute-start(bf16[784,128]{1,0:T(8,128)(2,1)S(1)} %get-tuple-element.85), channel_id=1, source_target_pairs={{0,8},{2,10},{4,12},{6,14},{8,0},{10,2},{12,4},{14,6},{1,9},{3,11}... | collective-permute-start | bytes 602120 | tf_op jit(solution)/shard_map/ppermute | solution.py:683
  84.8 12.4 %collective-permute-start.14 = (bf16[1056,128]{1,0:T(8,128)(2,1)S(1)}, bf16[1056,128]{1,0:T(8,128)(2,1)S(1)}, u32[]{:S(2)}, u32[]{:S(2)}) collective-permute-start(bf16[1056,128]{1,0:T(8,128)(2,1)S(1)} %get-tuple-element.90), channel_id=1, source_target_pairs={{0,4},{2,6},{4,0},{6,2},{8,12},{10,14},{12,8},{14,10},{1,5},{3,7},... | collective-permute-start | bytes 811016 | tf_op jit(solution)/shard_map/ppermute | solution.py:683
  87.1 12.0 %collective-permute-start.17 = (f32[1056,128]{1,0:T(8,128)S(1)}, f32[1056,128]{1,0:T(8,128)S(1)}, u32[]{:S(2)}, u32[]{:S(2)}) collective-permute-start(f32[1056,128]{1,0:T(8,128)S(1)} %get-tuple-element.89.refs_0_), channel_id=1, source_target_pairs={{0,16},{16,0},{1,17},{17,1},{2,18},{18,2},{3,19},{19,3},{4,20},{20... | collective-permute-start | bytes 1622024 | tf_op jit(solution)/shard_map/ppermute | solution.py:705
  96.7 2.4 %collective-permute-start.19 = (f32[1056,128]{1,0:T(8,128)S(1)}, f32[1056,128]{1,0:T(8,128)S(1)}, u32[]{:S(2)}, u32[]{:S(2)}) collective-permute-start(f32[1056,128]{1,0:T(8,128)S(1)} %sum_far.1.refs_2_), channel_id=1, source_target_pairs={{0,16},{16,0},{1,17},{17,1},{2,18},{18,2},{3,19},{19,3},{4,20},{20... | collective-permute-start | bytes 1622024 | tf_op jit(solution)/shard_map/ppermute | solution.py:705
  97.2 1.9 %collective-permute-start.18 = (bf16[1056,128]{1,0:T(8,128)(2,1)S(1)}, bf16[1056,128]{1,0:T(8,128)(2,1)S(1)}, u32[]{:S(2)}, u32[]{:S(2)}) collective-permute-start(bf16[1056,128]{1,0:T(8,128)(2,1)S(1)} %collective-permute-done.14.refs_1_), channel_id=1, source_target_pairs={{0,16},{16,0},{1,17},{17,1},{2,18},{18,2},{3,19},{19,3},{4,20},{20... | collective-permute-start | bytes 811016 | tf_op jit(solution)/shard_map/ppermute | solution.py:705

commit v15 on v14

--- a/solution.py
+++ b/solution.py
@@ -342,7 +342,7 @@
         return [block for block in blocks if not early(block)]
 
     first = [block for block in whole + across + corner if early(block)]
-    return [first, late(whole + corner + across)]
+    return [first, late(whole + corner), late(across)]
 
 
 def pairs_in(blocks):
@@ -375,7 +375,7 @@
             base = (part * per_ct * PAIR + device) * JOIN
             wanted = None
             side = 1 - core if far else core
-            if far:
+            if far or not within:
                 wanted = (side == 1) | (lax.rem(base // TILE, 2) == core)
             base = base + side * own
 
@@ -692,7 +692,11 @@
     near.append(joined([follow(block, early[2:]) for block in received[1]]))
     far.append(lax.ppermute(near[1], "stn", cores))
     sources_at = [(False, c) for c in range(parts)] + [(True, c) for c in range(parts)]
-    beyond = correlate(near + far, sources_at, sets[1], own, (2, 3), sizes, "correlate_far")
+    beyond = correlate(near, sources_at[:parts], sets[1], own, (2, 3), sizes, "far_own")
+    beyond = correlate(
+        near + far, sources_at, sets[2], own, (2, 3), sizes, "far_cross", beyond
+    )
+    sets = [sets[0], sets[1] + sets[2]]
     near[0] = follow(near[0], beyond[0])
     kept, beside = correlate(
         near + far, sources_at, sets[1], own, (0, 1), sizes, "correlate_near", early[:2]

time: 101 us -> 99.2 us (0.982)
  waiting for transfers between devices: 37 us -> 34.9 us
    ppermute x1, waiting for transfers between devices: 2.65 us -> 0.01 us  [fast(): far.append(lax.ppermute(near[1], 'stn', cores))]
    pallas_call x3 -> x4, Pallas kernels: 15.8 us -> 16.2 us  [correlate(): pl.pallas_call(functools.partial(correlate_kernel, layout), out_shape=[ja...]
  transfers between devices with their start and end apart: 20 -> 20, of which waited for: 9 -> 8; matrix products, arithmetic and copies ran while one was open for 0% -> 0% of each run, Pallas kernels for 25% -> 29%
where the time goes in v15:
time: 99.2 us; the launch traced here: 99 us
  Pallas kernels  35.4 us (36%)
  waiting for transfers between devices  34.9 us (35%)
  starting transfers between devices  26.7 us (27%)
  local copies, waits for them, and re-layouts  1.67 us (2%)
    pallas_call x4, Pallas kernels, correlate(): pl.pallas_call(functools.partial(correlate_kernel, layout), out_shape=[ja...  16.2 us
    ppermute x5, waiting for transfers between devices, along(): return lax.ppermute(block, 'tm', route)  15.4 us
    ppermute x2, waiting for transfers between devices, fast(): recvs = [lax.ppermute(block, 'tm', swap) for block in sends]  15.4 us
    pallas_call x4, Pallas kernels, filterbank(): pl.pallas_call(kernel, out_shape=[jax.ShapeDtypeStruct(shape, jnp.bfloat1...  15.2 us
    ppermute x5, starting transfers between devices, along(): return lax.ppermute(block, 'tm', route)  8.49 us
    ppermute x2, starting transfers between devices, fast(): halos.append(lax.ppermute(jnp.where(g == 1, keeps[c], recv), 'tm', onward))  7.85 us
    ppermute x6, starting transfers between devices, fast(): block = lax.ppermute(block, ('tm', 'ct'), route)  7.11 us
    ppermute x2, starting transfers between devices, fast(): recvs = [lax.ppermute(block, 'tm', swap) for block in sends]  2.97 us
  transfers between devices with their start and end apart: 20, of which 8 were waited for; matrix products, arithmetic and copies ran while one was open for 0% of the time, Pallas kernels for 29%

profile of v15, /device:TPU:0, one launch (start us, length us, event | category | flops | bytes accessed | tf_op | source)
XLA Modules:
  0.0 99.0 jit_solution(17408997948832653726)
XLA Ops:
  0.0 1.6 %copy-done.1 = bf16[2,8,65536]{2,1,0:T(8,128)(2,1)S(1)} copy-done((bf16[2,8,65536]{2,1,0:T(8,128)(2,1)S(1)}, bf16[2,8,65536]{2,1,0:T(8,128)(2,1)}, u32[]{:S(2)}) %copy-start.1) | copy-done | bytes 2097176
  1.7 1.9 %pick.1 = (bf16[2,2,512,128]{3,2,1,0:T(8,128)(2,1)}, bf16[2,2,512,128]{3,2,1,0:T(8,128)(2,1)S(1)}, bf16[2,2,512,128]{3,2,1,0:T(8,128)(2,1)S(1)}, bf16[2,2,512,128]{3,2,1,0:T(8,128)(2,1)S(1)}) custom-call(bf16[2,8,65536]{2,1,0:T(8,128)(2,1)S(1)} %copy-done.1), custom_call_target="tpu_custom_call" | custom-call | flops 1000000 | bytes 262144 | tf_op jit(solution)/shard_map/pick/pallas_call | solution.py:120
  3.6 2.9 %collective-permute-start = (bf16[2,2,512,128]{3,2,1,0:T(8,128)(2,1)}, bf16[2,2,512,128]{3,2,1,0:T(8,128)(2,1)S(1)}, u32[]{:S(2)}, u32[]{:S(2)}) collective-permute-start(bf16[2,2,512,128]{3,2,1,0:T(8,128)(2,1)} %get-tuple-element.52), channel_id=1, source_target_pairs={{0,2},{2,0},{4,6},{6,4},{8,10},{10,8},{12,14},{14,12},{1,3},{3,1},... | collective-permute-start | bytes 1572872 | tf_op jit(solution)/shard_map/ppermute | solution.py:653
  6.5 0.0 collective-permute-start.2
  6.5 12.9 %collective-permute-done.refs_2_.refs_3_ = bf16[2,2,512,128]{3,2,1,0:T(8,128)(2,1)S(1)} collective-permute-done((bf16[2,2,512,128]{3,2,1,0:T(8,128)(2,1)}, bf16[2,2,512,128]{3,2,1,0:T(8,128)(2,1)S(1)}, u32[]{:S(2)}, u32[]{:S(2)}) %collective-permute-start) | collective-permute-done | bytes 524320 | tf_op jit(solution)/shard_map/ppermute | solution.py:653
  19.5 0.1 broadcast_select_fusion.1
  19.5 4.1 %collective-permute-start.1 = (bf16[2,2,512,128]{3,2,1,0:T(8,128)(2,1)S(1)}, bf16[2,2,512,128]{3,2,1,0:T(8,128)(2,1)S(1)}, u32[]{:S(2)}, u32[]{:S(2)}) collective-permute-start(bf16[2,2,512,128]{3,2,1,0:T(8,128)(2,1)S(1)} %broadcast_select_fusion.1), channel_id=1, source_target_pairs={{0,4},{2,6},{4,8},{6,10},{8,12},{10,14},{1,5},{3,7},{5,9},{7,11},{... | collective-permute-start | bytes 1572872 | tf_op jit(solution)/shard_map/ppermute | solution.py:657
  23.7 3.8 %filterbank_late.2 = (bf16[2,8,2,16,128]{4,3,2,1,0:T(8,128)(2,1)S(1)}, bf16[2,8,2,16,128]{4,3,2,1,0:T(8,128)(2,1)S(1)}, bf16[2,8,2,16,128]{4,3,2,1,0:T(8,128)(2,1)S(1)}, bf16[2,8,2,16,128]{4,3,2,1,0:T(8,128)(2,1)S(1)}) custom-call(s32[8]{0:T(128)S(1)} %copy-done.6, bf16[2,2,512,128]{3,2,1,0:T(8,128)(2,1)S(1)} %get-tuple-element.51.refs_1_.refs_2_, ...), custom_call_target="tpu_custom_call" | custom-call | flops 1000000 | bytes 262144 | tf_op jit(solution)/shard_map/filterbank_late/pallas_call | solution.py:310
  27.4 2.4 %collective-permute-done.2.refs_2_.refs_3_ = bf16[2,2,512,128]{3,2,1,0:T(8,128)(2,1)S(1)} collective-permute-done((bf16[2,2,512,128]{3,2,1,0:T(8,128)(2,1)S(1)}, bf16[2,2,512,128]{3,2,1,0:T(8,128)(2,1)S(1)}, u32[]{:S(2)}, u32[]{:S(2)}) %collective-permute-start.2) | collective-permute-done | bytes 524320 | tf_op jit(solution)/shard_map/ppermute | solution.py:653
  29.9 0.1 broadcast_select_fusion
  29.9 3.8 %collective-permute-start.3 = (bf16[2,2,512,128]{3,2,1,0:T(8,128)(2,1)S(1)}, bf16[2,2,512,128]{3,2,1,0:T(8,128)(2,1)S(1)}, u32[]{:S(2)}, u32[]{:S(2)}) collective-permute-start(bf16[2,2,512,128]{3,2,1,0:T(8,128)(2,1)S(1)} %broadcast_select_fusion), channel_id=1, source_target_pairs={{0,4},{2,6},{4,8},{6,10},{8,12},{10,14},{1,5},{3,7},{5,9},{7,11},{... | collective-permute-start | bytes 1572872 | tf_op jit(solution)/shard_map/ppermute | solution.py:657
  33.7 0.0 collective-permute-done.1.refs_1_
  33.7 3.8 %filterbank_early.2 = (bf16[2,16,2,16,128]{4,3,2,1,0:T(8,128)(2,1)S(1)}, bf16[2,16,2,16,128]{4,3,2,1,0:T(8,128)(2,1)S(1)}, bf16[2,16,2,16,128]{4,3,2,1,0:T(8,128)(2,1)S(1)}, bf16[2,16,2,16,128]{4,3,2,1,0:T(8,128)(2,1)S(1)}) custom-call(s32[8]{0:T(128)S(1)} %copy-done.6, bf16[2,2,512,128]{3,2,1,0:T(8,128)(2,1)S(1)} %collective-permute-done.1.refs_1_, ...), custom_call_target="tpu_custom_call" | custom-call | flops 1000000 | bytes 262144 | tf_op jit(solution)/shard_map/filterbank_early/pallas_call | solution.py:310
  37.5 2.5 %collective-permute-start.6 = (bf16[2,16,2,16,128]{4,3,2,1,0:T(8,128)(2,1)S(1)}, bf16[2,16,2,16,128]{4,3,2,1,0:T(8,128)(2,1)S(1)}, u32[]{:S(2)}, u32[]{:S(2)}) collective-permute-start(bf16[2,16,2,16,128]{4,3,2,1,0:T(8,128)(2,1)S(1)} %get-tuple-element.73), channel_id=1, source_target_pairs={{0,3},{1,2},{2,1},{3,0},{4,7},{5,6},{6,5},{7,4},{8,11},{9,10},{10,... | collective-permute-start | bytes 786440 | tf_op jit(solution)/shard_map/ppermute | solution.py:677
  40.0 0.5 collective-permute-start.5
  40.6 0.5 collective-permute-start.4
  41.1 3.7 %filterbank_late.3 = (bf16[2,8,2,16,128]{4,3,2,1,0:T(8,128)(2,1)S(1)}, bf16[2,8,2,16,128]{4,3,2,1,0:T(8,128)(2,1)S(1)}, bf16[2,8,2,16,128]{4,3,2,1,0:T(8,128)(2,1)S(1)}, bf16[2,8,2,16,128]{4,3,2,1,0:T(8,128)(2,1)S(1)}) custom-call(s32[8]{0:T(128)S(1)} %copy-done.6, bf16[2,2,512,128]{3,2,1,0:T(8,128)(2,1)S(1)} %get-tuple-element.60.refs_1_.refs_2_, ...), custom_call_target="tpu_custom_call" | custom-call | flops 1000000 | bytes 262144 | tf_op jit(solution)/shard_map/filterbank_late/pallas_call | solution.py:310
  44.8 4.0 %filterbank_early.3 = (bf16[2,16,2,16,128]{4,3,2,1,0:T(8,128)(2,1)S(1)}, bf16[2,16,2,16,128]{4,3,2,1,0:T(8,128)(2,1)S(1)}, bf16[2,16,2,16,128]{4,3,2,1,0:T(8,128)(2,1)S(1)}, bf16[2,16,2,16,128]{4,3,2,1,0:T(8,128)(2,1)S(1)}) custom-call(s32[8]{0:T(128)S(1)} %copy-done.6, bf16[2,2,512,128]{3,2,1,0:T(8,128)(2,1)S(1)} %collective-permute-done.3.refs_1_, ...), custom_call_target="tpu_custom_call" | custom-call | flops 1000000 | bytes 262144 | tf_op jit(solution)/shard_map/filterbank_early/pallas_call | solution.py:310
  48.8 2.3 %collective-permute-done.5.refs_2_ = bf16[2,16,2,16,128]{4,3,2,1,0:T(8,128)(2,1)S(1)} collective-permute-done((bf16[2,16,2,16,128]{4,3,2,1,0:T(8,128)(2,1)S(1)}, bf16[2,16,2,16,128]{4,3,2,1,0:T(8,128)(2,1)S(1)}, u32[]{:S(2)}, u32[]{:S(2)}) %collective-permute-start.5) | collective-permute-done | bytes 262176 | tf_op jit(solution)/shard_map/ppermute | solution.py:677
  51.1 0.2 join.2.refs_0_
  51.3 0.1 collective-permute-start.7
  51.4 2.4 %collective-permute-start.12 = (bf16[2,16,2,16,128]{4,3,2,1,0:T(8,128)(2,1)S(1)}, bf16[2,16,2,16,128]{4,3,2,1,0:T(8,128)(2,1)S(1)}, u32[]{:S(2)}, u32[]{:S(2)}) collective-permute-start(bf16[2,16,2,16,128]{4,3,2,1,0:T(8,128)(2,1)S(1)} %get-tuple-element.85), channel_id=1, source_target_pairs={{0,3},{1,2},{2,1},{3,0},{4,7},{5,6},{6,5},{7,4},{8,11},{9,10},{10,... | collective-permute-start | bytes 786440 | tf_op jit(solution)/shard_map/ppermute | solution.py:677
  53.8 0.5 collective-permute-start.11
  54.3 0.6 collective-permute-start.10
  54.9 0.0 collective-permute-done.7.refs_1_.refs_2_
  54.9 4.0 %correlate_early.1 = (f32[272,128]{1,0:T(8,128)S(1)}, bf16[272,128]{1,0:T(8,128)(2,1)S(1)}, bf16[272,128]{1,0:T(8,128)(2,1)S(1)}, bf16[272,128]{1,0:T(8,128)(2,1)S(1)}) custom-call(bf16[8,16,2,16,128]{4,3,2,1,0:T(8,128)(2,1)S(1)} %join.2.refs_0_, bf16[8,16,2,16,128]{4,3,2,1,0:T(8,128)(2,1)S(1)} %collective-permute-done.7.refs_1_.refs_2_), custom_call_target="tpu_custom_call" | custom-call | flops 1000000 | bytes 262144 | tf_op jit(solution)/shard_map/correlate_early/pallas_call | solution.py:476
  58.9 2.6 %collective-permute-start.8 = (bf16[272,128]{1,0:T(8,128)(2,1)S(1)}, bf16[272,128]{1,0:T(8,128)(2,1)S(1)}, u32[]{:S(2)}, u32[]{:S(2)}) collective-permute-start(bf16[272,128]{1,0:T(8,128)(2,1)S(1)} %get-tuple-element.75), channel_id=1, source_target_pairs={{0,8},{2,10},{4,12},{6,14},{8,0},{10,2},{12,4},{14,6},{1,9},{3,11}... | collective-permute-start | bytes 208904 | tf_op jit(solution)/shard_map/ppermute | solution.py:683
  61.5 1.3 %collective-permute-start.9 = (bf16[272,128]{1,0:T(8,128)(2,1)S(1)}, bf16[272,128]{1,0:T(8,128)(2,1)S(1)}, u32[]{:S(2)}, u32[]{:S(2)}) collective-permute-start(bf16[272,128]{1,0:T(8,128)(2,1)S(1)} %get-tuple-element.76), channel_id=1, source_target_pairs={{0,12},{2,14},{4,8},{6,10},{8,4},{10,6},{12,0},{14,2},{1,13},{3,15... | collective-permute-start | bytes 208904 | tf_op jit(solution)/shard_map/ppermute | solution.py:683
  62.9 0.0 collective-permute-done.12.refs_3_
  62.9 3.5 %collective-permute-done.8.refs_0_ = bf16[272,128]{1,0:T(8,128)(2,1)S(1)} collective-permute-done((bf16[272,128]{1,0:T(8,128)(2,1)S(1)}, bf16[272,128]{1,0:T(8,128)(2,1)S(1)}, u32[]{:S(2)}, u32[]{:S(2)}) %collective-permute-start.8) | collective-permute-done | bytes 69664 | tf_op jit(solution)/shard_map/ppermute | solution.py:683
  66.4 1.3 %collective-permute-done.9.refs_1_ = bf16[272,128]{1,0:T(8,128)(2,1)S(1)} collective-permute-done((bf16[272,128]{1,0:T(8,128)(2,1)S(1)}, bf16[272,128]{1,0:T(8,128)(2,1)S(1)}, u32[]{:S(2)}, u32[]{:S(2)}) %collective-permute-start.9) | collective-permute-done | bytes 69664 | tf_op jit(solution)/shard_map/ppermute | solution.py:683
  67.7 0.0 collective-permute-done.11.refs_2_
  67.7 0.0 collective-permute-done.10.refs_1_
  67.7 0.2 join.3.refs_1_
  67.9 0.1 collective-permute-start.13
  68.0 3.1 %far_own.1 = (bf16[400,128]{1,0:T(8,128)(2,1)S(1)}, bf16[400,128]{1,0:T(8,128)(2,1)S(1)}) custom-call(bf16[8,16,2,16,128]{4,3,2,1,0:T(8,128)(2,1)S(1)} %join.2.refs_0_, bf16[8,16,2,16,128]{4,3,2,1,0:T(8,128)(2,1)S(1)} %join.3.refs_1_), custom_call_target="tpu_custom_call" | custom-call | flops 1000000 | bytes 262144 | tf_op jit(solution)/shard_map/far_own/pallas_call | solution.py:476
  71.1 3.2 %far_cross.1 = (bf16[784,128]{1,0:T(8,128)(2,1)S(1)}, bf16[784,128]{1,0:T(8,128)(2,1)S(1)}) custom-call(bf16[8,16,2,16,128]{4,3,2,1,0:T(8,128)(2,1)S(1)} %join.2.refs_0_, bf16[8,16,2,16,128]{4,3,2,1,0:T(8,128)(2,1)S(1)} %join.3.refs_1_, bf16[8,16,2,16,128]{4,3,2,1,0:T(8,128)(2,1)S(1)} %collective-permute-done.7.refs_1_.refs_2_, ...), custom_call_target="tpu_custom_call" | custom-call | flops 1000000 | bytes 262144 | tf_op jit(solution)/shard_map/far_cross/pallas_call | solution.py:476
  74.3 1.4 %collective-permute-start.16 = (bf16[784,128]{1,0:T(8,128)(2,1)S(1)}, bf16[784,128]{1,0:T(8,128)(2,1)S(1)}, u32[]{:S(2)}, u32[]{:S(2)}) collective-permute-start(bf16[784,128]{1,0:T(8,128)(2,1)S(1)} %get-tuple-element.95), channel_id=1, source_target_pairs={{0,12},{2,14},{4,8},{6,10},{8,4},{10,6},{12,0},{14,2},{1,13},{3,15... | collective-permute-start | bytes 602120 | tf_op jit(solution)/shard_map/ppermute | solution.py:683
  75.7 0.9 collective-permute-start.15
  76.5 5.9 %correlate_near.1 = (f32[1056,128]{1,0:T(8,128)S(1)}, bf16[1056,128]{1,0:T(8,128)(2,1)S(1)}) custom-call(bf16[8,16,2,16,128]{4,3,2,1,0:T(8,128)(2,1)S(1)} %join.2.refs_0_, bf16[8,16,2,16,128]{4,3,2,1,0:T(8,128)(2,1)S(1)} %join.3.refs_1_, bf16[8,16,2,16,128]{4,3,2,1,0:T(8,128)(2,1)S(1)} %collective-permute-done.7.refs_1_.refs_2_, ...), custom_call_target="tpu_custom_call" | custom-call | flops 1000000 | bytes 262144 | tf_op jit(solution)/shard_map/correlate_near/pallas_call | solution.py:476
  82.5 2.3 %collective-permute-start.14 = (bf16[1056,128]{1,0:T(8,128)(2,1)S(1)}, bf16[1056,128]{1,0:T(8,128)(2,1)S(1)}, u32[]{:S(2)}, u32[]{:S(2)}) collective-permute-start(bf16[1056,128]{1,0:T(8,128)(2,1)S(1)} %get-tuple-element.94), channel_id=1, source_target_pairs={{0,4},{2,6},{4,0},{6,2},{8,12},{10,14},{12,8},{14,10},{1,5},{3,7},... | collective-permute-start | bytes 811016 | tf_op jit(solution)/shard_map/ppermute | solution.py:683
  84.8 10.1 %collective-permute-done.15.refs_2_ = bf16[784,128]{1,0:T(8,128)(2,1)S(1)} collective-permute-done((bf16[784,128]{1,0:T(8,128)(2,1)S(1)}, bf16[784,128]{1,0:T(8,128)(2,1)S(1)}, u32[]{:S(2)}, u32[]{:S(2)}) %collective-permute-start.15) | collective-permute-done | bytes 200736 | tf_op jit(solution)/shard_map/ppermute | solution.py:683
  94.9 0.1 sum_far.1.refs_2_
  94.9 0.1 collective-permute-start.19
  95.0 0.4 collective-permute-done.14.refs_1_
  95.4 0.1 collective-permute-start.18
  95.5 1.8 %collective-permute-done.18.refs_4_ = bf16[1056,128]{1,0:T(8,128)(2,1)S(1)} collective-permute-done((bf16[1056,128]{1,0:T(8,128)(2,1)S(1)}, bf16[1056,128]{1,0:T(8,128)(2,1)S(1)}, u32[]{:S(2)}, u32[]{:S(2)}) %collective-permute-start.18) | collective-permute-done | bytes 270368 | tf_op jit(solution)/shard_map/ppermute | solution.py:709
  97.3 1.7 %assemble.1 = f32[2,16,32,256]{3,2,1,0:T(8,128)} custom-call(f32[1056,128]{1,0:T(8,128)S(1)} %get-tuple-element.93.refs_0_, bf16[1056,128]{1,0:T(8,128)(2,1)S(1)} %collective-permute-done.14.refs_1_, f32[1056,128]{1,0:T(8,128)S(1)} %sum_far.1.refs_2_, f32[1056,128]{1,0:T(8,128)S(1)} %collective-permute-done.17.refs_3_, ...), custom_call_target="tpu_custom_call" | custom-call | flops 1000000 | bytes 262144 | tf_op jit(solution)/shard_map/assemble/pallas_call | solution.py:598
  (21 shorter events, 0.0 us)
Async XLA Ops:
  0.0 23.6 %copy-start = (f32[16,64,128]{2,1,0:T(8,128)S(1)}, f32[16,64,128]{2,1,0:T(8,128)}, u32[]{:S(2)}) copy-start(f32[16,64,128]{2,1,0:T(8,128)} %constant.30.clone.refs_3_.refs_4_) | copy-start | bytes 1572868
  0.0 1.6 %copy-start.1 = (bf16[2,8,65536]{2,1,0:T(8,128)(2,1)S(1)}, bf16[2,8,65536]{2,1,0:T(8,128)(2,1)}, u32[]{:S(2)}) copy-start(bf16[2,8,65536]{2,1,0:T(8,128)(2,1)} %block.1) | copy-start | bytes 6291460
  1.7 22.0 %copy-start.2 = (bf16[2,4,32,128]{3,2,1,0:T(8,128)(2,1)S(1)}, bf16[2,4,32,128]{3,2,1,0:T(8,128)(2,1)}, u32[]{:S(2)}) copy-start(bf16[2,4,32,128]{3,2,1,0:T(8,128)(2,1)} %constant.34.clone.refs_7_.refs_8_) | copy-start | bytes 196612
  1.7 22.0 %copy-start.3 = (f32[64,128]{1,0:T(8,128)S(1)}, f32[64,128]{1,0:T(8,128)}, u32[]{:S(2)}) copy-start(f32[64,128]{1,0:T(8,128)} %constant.33.clone.refs_6_.refs_7_) | copy-start | bytes 98308
  1.7 22.0 %copy-start.4 = (f32[64,128]{1,0:T(8,128)S(1)}, f32[64,128]{1,0:T(8,128)}, u32[]{:S(2)}) copy-start(f32[64,128]{1,0:T(8,128)} %constant.32.clone.refs_5_.refs_6_) | copy-start | bytes 98308
  1.7 22.0 %copy-start.5 = (bf16[128,128]{1,0:T(8,128)(2,1)S(1)}, bf16[128,128]{1,0:T(8,128)(2,1)}, u32[]{:S(2)}) copy-start(bf16[128,128]{1,0:T(8,128)(2,1)} %constant.31.clone.refs_4_.refs_5_) | copy-start | bytes 98308
  1.7 22.0 %copy-start.6 = (s32[8]{0:T(128)S(1)}, s32[8]{0:T(128)}, u32[]{:S(2)}) copy-start(s32[8]{0:T(128)} %refs_0_.7) | copy-start | bytes 100
  3.6 15.9 %collective-permute-start = (bf16[2,2,512,128]{3,2,1,0:T(8,128)(2,1)}, bf16[2,2,512,128]{3,2,1,0:T(8,128)(2,1)S(1)}, u32[]{:S(2)}, u32[]{:S(2)}) collective-permute-start(bf16[2,2,512,128]{3,2,1,0:T(8,128)(2,1)} %get-tuple-element.52), channel_id=1, source_target_pairs={{0,2},{2,0},{4,6},{6,4},{8,10},{10,8},{12,14},{14,12},{1,3},{3,1},... | collective-permute-start | bytes 1572872 | tf_op jit(solution)/shard_map/ppermute | solution.py:653
  6.5 23.4 %collective-permute-start.2 = (bf16[2,2,512,128]{3,2,1,0:T(8,128)(2,1)S(1)}, bf16[2,2,512,128]{3,2,1,0:T(8,128)(2,1)S(1)}, u32[]{:S(2)}, u32[]{:S(2)}) collective-permute-start(bf16[2,2,512,128]{3,2,1,0:T(8,128)(2,1)S(1)} %get-tuple-element.53), channel_id=1, source_target_pairs={{0,2},{2,0},{4,6},{6,4},{8,10},{10,8},{12,14},{14,12},{1,3},{3,1},... | collective-permute-start | bytes 1572872 | tf_op jit(solution)/shard_map/ppermute | solution.py:653
  19.5 14.2 %collective-permute-start.1 = (bf16[2,2,512,128]{3,2,1,0:T(8,128)(2,1)S(1)}, bf16[2,2,512,128]{3,2,1,0:T(8,128)(2,1)S(1)}, u32[]{:S(2)}, u32[]{:S(2)}) collective-permute-start(bf16[2,2,512,128]{3,2,1,0:T(8,128)(2,1)S(1)} %broadcast_select_fusion.1), channel_id=1, source_target_pairs={{0,4},{2,6},{4,8},{6,10},{8,12},{10,14},{1,5},{3,7},{5,9},{7,11},{... | collective-permute-start | bytes 1572872 | tf_op jit(solution)/shard_map/ppermute | solution.py:657
  29.9 14.9 %collective-permute-start.3 = (bf16[2,2,512,128]{3,2,1,0:T(8,128)(2,1)S(1)}, bf16[2,2,512,128]{3,2,1,0:T(8,128)(2,1)S(1)}, u32[]{:S(2)}, u32[]{:S(2)}) collective-permute-start(bf16[2,2,512,128]{3,2,1,0:T(8,128)(2,1)S(1)} %broadcast_select_fusion), channel_id=1, source_target_pairs={{0,4},{2,6},{4,8},{6,10},{8,12},{10,14},{1,5},{3,7},{5,9},{7,11},{... | collective-permute-start | bytes 1572872 | tf_op jit(solution)/shard_map/ppermute | solution.py:657
  37.5 11.3 %collective-permute-start.6 = (bf16[2,16,2,16,128]{4,3,2,1,0:T(8,128)(2,1)S(1)}, bf16[2,16,2,16,128]{4,3,2,1,0:T(8,128)(2,1)S(1)}, u32[]{:S(2)}, u32[]{:S(2)}) collective-permute-start(bf16[2,16,2,16,128]{4,3,2,1,0:T(8,128)(2,1)S(1)} %get-tuple-element.73), channel_id=1, source_target_pairs={{0,3},{1,2},{2,1},{3,0},{4,7},{5,6},{6,5},{7,4},{8,11},{9,10},{10,... | collective-permute-start | bytes 786440 | tf_op jit(solution)/shard_map/ppermute | solution.py:677
  40.0 11.1 %collective-permute-start.5 = (bf16[2,16,2,16,128]{4,3,2,1,0:T(8,128)(2,1)S(1)}, bf16[2,16,2,16,128]{4,3,2,1,0:T(8,128)(2,1)S(1)}, u32[]{:S(2)}, u32[]{:S(2)}) collective-permute-start(bf16[2,16,2,16,128]{4,3,2,1,0:T(8,128)(2,1)S(1)} %get-tuple-element.71), channel_id=1, source_target_pairs={{0,2},{1,3},{2,0},{3,1},{4,6},{5,7},{6,4},{7,5},{8,10},{9,11},{10,... | collective-permute-start | bytes 786440 | tf_op jit(solution)/shard_map/ppermute | solution.py:677
  40.6 10.5 %collective-permute-start.4 = (bf16[2,16,2,16,128]{4,3,2,1,0:T(8,128)(2,1)S(1)}, bf16[2,16,2,16,128]{4,3,2,1,0:T(8,128)(2,1)S(1)}, u32[]{:S(2)}, u32[]{:S(2)}) collective-permute-start(bf16[2,16,2,16,128]{4,3,2,1,0:T(8,128)(2,1)S(1)} %get-tuple-element.69), channel_id=1, source_target_pairs={{0,1},{1,0},{2,3},{3,2},{4,5},{5,4},{6,7},{7,6},{8,9},{9,8},{10,11... | collective-permute-start | bytes 786440 | tf_op jit(solution)/shard_map/ppermute | solution.py:677
  51.3 3.6 %collective-permute-start.7 = (bf16[8,16,2,16,128]{4,3,2,1,0:T(8,128)(2,1)S(1)}, bf16[8,16,2,16,128]{4,3,2,1,0:T(8,128)(2,1)S(1)}, u32[]{:S(2)}, u32[]{:S(2)}) collective-permute-start(bf16[8,16,2,16,128]{4,3,2,1,0:T(8,128)(2,1)S(1)} %join.2.refs_0_), channel_id=1, source_target_pairs={{0,16},{16,0},{1,17},{17,1},{2,18},{18,2},{3,19},{19,3},{4,20},{20... | collective-permute-start | bytes 3145736 | tf_op jit(solution)/shard_map/ppermute | solution.py:686
  51.4 11.5 %collective-permute-start.12 = (bf16[2,16,2,16,128]{4,3,2,1,0:T(8,128)(2,1)S(1)}, bf16[2,16,2,16,128]{4,3,2,1,0:T(8,128)(2,1)S(1)}, u32[]{:S(2)}, u32[]{:S(2)}) collective-permute-start(bf16[2,16,2,16,128]{4,3,2,1,0:T(8,128)(2,1)S(1)} %get-tuple-element.85), channel_id=1, source_target_pairs={{0,3},{1,2},{2,1},{3,0},{4,7},{5,6},{6,5},{7,4},{8,11},{9,10},{10,... | collective-permute-start | bytes 786440 | tf_op jit(solution)/shard_map/ppermute | solution.py:677
  53.8 14.0 %collective-permute-start.11 = (bf16[2,16,2,16,128]{4,3,2,1,0:T(8,128)(2,1)S(1)}, bf16[2,16,2,16,128]{4,3,2,1,0:T(8,128)(2,1)S(1)}, u32[]{:S(2)}, u32[]{:S(2)}) collective-permute-start(bf16[2,16,2,16,128]{4,3,2,1,0:T(8,128)(2,1)S(1)} %get-tuple-element.82), channel_id=1, source_target_pairs={{0,2},{1,3},{2,0},{3,1},{4,6},{5,7},{6,4},{7,5},{8,10},{9,11},{10,... | collective-permute-start | bytes 786440 | tf_op jit(solution)/shard_map/ppermute | solution.py:677
  54.3 13.4 %collective-permute-start.10 = (bf16[2,16,2,16,128]{4,3,2,1,0:T(8,128)(2,1)S(1)}, bf16[2,16,2,16,128]{4,3,2,1,0:T(8,128)(2,1)S(1)}, u32[]{:S(2)}, u32[]{:S(2)}) collective-permute-start(bf16[2,16,2,16,128]{4,3,2,1,0:T(8,128)(2,1)S(1)} %get-tuple-element.79), channel_id=1, source_target_pairs={{0,1},{1,0},{2,3},{3,2},{4,5},{5,4},{6,7},{7,6},{8,9},{9,8},{10,11... | collective-permute-start | bytes 786440 | tf_op jit(solution)/shard_map/ppermute | solution.py:677
  58.9 7.5 %collective-permute-start.8 = (bf16[272,128]{1,0:T(8,128)(2,1)S(1)}, bf16[272,128]{1,0:T(8,128)(2,1)S(1)}, u32[]{:S(2)}, u32[]{:S(2)}) collective-permute-start(bf16[272,128]{1,0:T(8,128)(2,1)S(1)} %get-tuple-element.75), channel_id=1, source_target_pairs={{0,8},{2,10},{4,12},{6,14},{8,0},{10,2},{12,4},{14,6},{1,9},{3,11}... | collective-permute-start | bytes 208904 | tf_op jit(solution)/shard_map/ppermute | solution.py:683
  61.5 6.2 %collective-permute-start.9 = (bf16[272,128]{1,0:T(8,128)(2,1)S(1)}, bf16[272,128]{1,0:T(8,128)(2,1)S(1)}, u32[]{:S(2)}, u32[]{:S(2)}) collective-permute-start(bf16[272,128]{1,0:T(8,128)(2,1)S(1)} %get-tuple-element.76), channel_id=1, source_target_pairs={{0,12},{2,14},{4,8},{6,10},{8,4},{10,6},{12,0},{14,2},{1,13},{3,15... | collective-permute-start | bytes 208904 | tf_op jit(solution)/shard_map/ppermute | solution.py:683
  67.9 3.1 %collective-permute-start.13 = (bf16[8,16,2,16,128]{4,3,2,1,0:T(8,128)(2,1)S(1)}, bf16[8,16,2,16,128]{4,3,2,1,0:T(8,128)(2,1)S(1)}, u32[]{:S(2)}, u32[]{:S(2)}) collective-permute-start(bf16[8,16,2,16,128]{4,3,2,1,0:T(8,128)(2,1)S(1)} %join.3.refs_1_), channel_id=1, source_target_pairs={{0,16},{16,0},{1,17},{17,1},{2,18},{18,2},{3,19},{19,3},{4,20},{20... | collective-permute-start | bytes 3145736 | tf_op jit(solution)/shard_map/ppermute | solution.py:693
  74.3 10.5 %collective-permute-start.16 = (bf16[784,128]{1,0:T(8,128)(2,1)S(1)}, bf16[784,128]{1,0:T(8,128)(2,1)S(1)}, u32[]{:S(2)}, u32[]{:S(2)}) collective-permute-start(bf16[784,128]{1,0:T(8,128)(2,1)S(1)} %get-tuple-element.95), channel_id=1, source_target_pairs={{0,12},{2,14},{4,8},{6,10},{8,4},{10,6},{12,0},{14,2},{1,13},{3,15... | collective-permute-start | bytes 602120 | tf_op jit(solution)/shard_map/ppermute | solution.py:683
  75.7 19.2 %collective-permute-start.15 = (bf16[784,128]{1,0:T(8,128)(2,1)S(1)}, bf16[784,128]{1,0:T(8,128)(2,1)S(1)}, u32[]{:S(2)}, u32[]{:S(2)}) collective-permute-start(bf16[784,128]{1,0:T(8,128)(2,1)S(1)} %get-tuple-element.89), channel_id=1, source_target_pairs={{0,8},{2,10},{4,12},{6,14},{8,0},{10,2},{12,4},{14,6},{1,9},{3,11}... | collective-permute-start | bytes 602120 | tf_op jit(solution)/shard_map/ppermute | solution.py:683
  82.5 12.9 %collective-permute-start.14 = (bf16[1056,128]{1,0:T(8,128)(2,1)S(1)}, bf16[1056,128]{1,0:T(8,128)(2,1)S(1)}, u32[]{:S(2)}, u32[]{:S(2)}) collective-permute-start(bf16[1056,128]{1,0:T(8,128)(2,1)S(1)} %get-tuple-element.94), channel_id=1, source_target_pairs={{0,4},{2,6},{4,0},{6,2},{8,12},{10,14},{12,8},{14,10},{1,5},{3,7},... | collective-permute-start | bytes 811016 | tf_op jit(solution)/shard_map/ppermute | solution.py:683
  84.8 12.6 %collective-permute-start.17 = (f32[1056,128]{1,0:T(8,128)S(1)}, f32[1056,128]{1,0:T(8,128)S(1)}, u32[]{:S(2)}, u32[]{:S(2)}) collective-permute-start(f32[1056,128]{1,0:T(8,128)S(1)} %get-tuple-element.93.refs_0_), channel_id=1, source_target_pairs={{0,16},{16,0},{1,17},{17,1},{2,18},{18,2},{3,19},{19,3},{4,20},{20... | collective-permute-start | bytes 1622024 | tf_op jit(solution)/shard_map/ppermute | solution.py:709
  94.9 2.4 %collective-permute-start.19 = (f32[1056,128]{1,0:T(8,128)S(1)}, f32[1056,128]{1,0:T(8,128)S(1)}, u32[]{:S(2)}, u32[]{:S(2)}) collective-permute-start(f32[1056,128]{1,0:T(8,128)S(1)} %sum_far.1.refs_2_), channel_id=1, source_target_pairs={{0,16},{16,0},{1,17},{17,1},{2,18},{18,2},{3,19},{19,3},{4,20},{20... | collective-permute-start | bytes 1622024 | tf_op jit(solution)/shard_map/ppermute | solution.py:709
  95.4 1.9 %collective-permute-start.18 = (bf16[1056,128]{1,0:T(8,128)(2,1)S(1)}, bf16[1056,128]{1,0:T(8,128)(2,1)S(1)}, u32[]{:S(2)}, u32[]{:S(2)}) collective-permute-start(bf16[1056,128]{1,0:T(8,128)(2,1)S(1)} %collective-permute-done.14.refs_1_), channel_id=1, source_target_pairs={{0,16},{16,0},{1,17},{17,1},{2,18},{18,2},{3,19},{19,3},{4,20},{20... | collective-permute-start | bytes 811016 | tf_op jit(solution)/shard_map/ppermute | solution.py:709

commit v16 on v15

--- a/solution.py
+++ b/solution.py
@@ -689,10 +689,11 @@
         "correlate_early",
     )
     early = [*early[:2], *[along(early[x], x) for x in (2, 3)]]
-    near.append(joined([follow(block, early[2:]) for block in received[1]]))
+    near.append(joined([follow(block, early[3]) for block in received[1]]))
     far.append(lax.ppermute(near[1], "stn", cores))
     sources_at = [(False, c) for c in range(parts)] + [(True, c) for c in range(parts)]
     beyond = correlate(near, sources_at[:parts], sets[1], own, (2, 3), sizes, "far_own")
+    far[1] = follow(far[1], early[2])
     beyond = correlate(
         near + far, sources_at, sets[2], own, (2, 3), sizes, "far_cross", beyond
     )

time: 99.2 us -> 100 us (level)
    ppermute x6, waiting for transfers between devices: 2.3 us -> 4.59 us  [fast(): block = lax.ppermute(block, ('tm', 'ct'), route)]
    ppermute x5, waiting for transfers between devices: 15.4 us -> 14.1 us  [along(): return lax.ppermute(block, 'tm', route)]
  transfers between devices with their start and end apart: 20 -> 20, of which waited for: 8 -> 10; matrix products, arithmetic and copies ran while one was open for 0% -> 0% of each run, Pallas kernels for 29% -> 28%
where the time goes in v16:
time: 100 us
  waiting for transfers between devices  35.8 us (36%)
  Pallas kernels  35.3 us (35%)
  starting transfers between devices  27.2 us (27%)
  local copies, waits for them, and re-layouts  1.67 us (2%)
    pallas_call x4, Pallas kernels, correlate(): pl.pallas_call(functools.partial(correlate_kernel, layout), out_shape=[ja...  16.1 us
    ppermute x2, waiting for transfers between devices, fast(): recvs = [lax.ppermute(block, 'tm', swap) for block in sends]  15.4 us
    pallas_call x4, Pallas kernels, filterbank(): pl.pallas_call(kernel, out_shape=[jax.ShapeDtypeStruct(shape, jnp.bfloat1...  15.2 us
    ppermute x5, waiting for transfers between devices, along(): return lax.ppermute(block, 'tm', route)  14.1 us
    ppermute x5, starting transfers between devices, along(): return lax.ppermute(block, 'tm', route)  8.96 us
    ppermute x2, starting transfers between devices, fast(): halos.append(lax.ppermute(jnp.where(g == 1, keeps[c], recv), 'tm', onward))  7.85 us
    ppermute x6, starting transfers between devices, fast(): block = lax.ppermute(block, ('tm', 'ct'), route)  7.11 us
    ppermute x6, waiting for transfers between devices, fast(): block = lax.ppermute(block, ('tm', 'ct'), route)  4.59 us
  transfers between devices with their start and end apart: 20, of which 10 were waited for; matrix products, arithmetic and copies ran while one was open for 0% of the time, Pallas kernels for 28%

profile of v16, /device:TPU:0, one launch (start us, length us, event | category | flops | bytes accessed | tf_op | source)
XLA Modules:
  0.0 100.3 jit_solution(3471178887680654197)
XLA Ops:
  0.0 1.6 %copy-done.1 = bf16[2,8,65536]{2,1,0:T(8,128)(2,1)S(1)} copy-done((bf16[2,8,65536]{2,1,0:T(8,128)(2,1)S(1)}, bf16[2,8,65536]{2,1,0:T(8,128)(2,1)}, u32[]{:S(2)}) %copy-start.1) | copy-done | bytes 2097176
  1.7 1.9 %pick.1 = (bf16[2,2,512,128]{3,2,1,0:T(8,128)(2,1)}, bf16[2,2,512,128]{3,2,1,0:T(8,128)(2,1)S(1)}, bf16[2,2,512,128]{3,2,1,0:T(8,128)(2,1)S(1)}, bf16[2,2,512,128]{3,2,1,0:T(8,128)(2,1)S(1)}) custom-call(bf16[2,8,65536]{2,1,0:T(8,128)(2,1)S(1)} %copy-done.1), custom_call_target="tpu_custom_call" | custom-call | flops 1000000 | bytes 262144 | tf_op jit(solution)/shard_map/pick/pallas_call | solution.py:120
  3.6 2.9 %collective-permute-start = (bf16[2,2,512,128]{3,2,1,0:T(8,128)(2,1)}, bf16[2,2,512,128]{3,2,1,0:T(8,128)(2,1)S(1)}, u32[]{:S(2)}, u32[]{:S(2)}) collective-permute-start(bf16[2,2,512,128]{3,2,1,0:T(8,128)(2,1)} %get-tuple-element.53), channel_id=1, source_target_pairs={{0,2},{2,0},{4,6},{6,4},{8,10},{10,8},{12,14},{14,12},{1,3},{3,1},... | collective-permute-start | bytes 1572872 | tf_op jit(solution)/shard_map/ppermute | solution.py:653
  6.5 0.0 collective-permute-start.2
  6.5 12.9 %collective-permute-done.refs_2_.refs_3_ = bf16[2,2,512,128]{3,2,1,0:T(8,128)(2,1)S(1)} collective-permute-done((bf16[2,2,512,128]{3,2,1,0:T(8,128)(2,1)}, bf16[2,2,512,128]{3,2,1,0:T(8,128)(2,1)S(1)}, u32[]{:S(2)}, u32[]{:S(2)}) %collective-permute-start) | collective-permute-done | bytes 524320 | tf_op jit(solution)/shard_map/ppermute | solution.py:653
  19.5 0.1 broadcast_select_fusion.1
  19.5 4.1 %collective-permute-start.1 = (bf16[2,2,512,128]{3,2,1,0:T(8,128)(2,1)S(1)}, bf16[2,2,512,128]{3,2,1,0:T(8,128)(2,1)S(1)}, u32[]{:S(2)}, u32[]{:S(2)}) collective-permute-start(bf16[2,2,512,128]{3,2,1,0:T(8,128)(2,1)S(1)} %broadcast_select_fusion.1), channel_id=1, source_target_pairs={{0,4},{2,6},{4,8},{6,10},{8,12},{10,14},{1,5},{3,7},{5,9},{7,11},{... | collective-permute-start | bytes 1572872 | tf_op jit(solution)/shard_map/ppermute | solution.py:657
  23.7 3.8 %filterbank_late.2 = (bf16[2,8,2,16,128]{4,3,2,1,0:T(8,128)(2,1)S(1)}, bf16[2,8,2,16,128]{4,3,2,1,0:T(8,128)(2,1)S(1)}, bf16[2,8,2,16,128]{4,3,2,1,0:T(8,128)(2,1)S(1)}, bf16[2,8,2,16,128]{4,3,2,1,0:T(8,128)(2,1)S(1)}) custom-call(s32[8]{0:T(128)S(1)} %copy-done.6, bf16[2,2,512,128]{3,2,1,0:T(8,128)(2,1)S(1)} %get-tuple-element.52.refs_1_.refs_2_, ...), custom_call_target="tpu_custom_call" | custom-call | flops 1000000 | bytes 262144 | tf_op jit(solution)/shard_map/filterbank_late/pallas_call | solution.py:310
  27.4 2.4 %collective-permute-done.2.refs_2_.refs_3_ = bf16[2,2,512,128]{3,2,1,0:T(8,128)(2,1)S(1)} collective-permute-done((bf16[2,2,512,128]{3,2,1,0:T(8,128)(2,1)S(1)}, bf16[2,2,512,128]{3,2,1,0:T(8,128)(2,1)S(1)}, u32[]{:S(2)}, u32[]{:S(2)}) %collective-permute-start.2) | collective-permute-done | bytes 524320 | tf_op jit(solution)/shard_map/ppermute | solution.py:653
  29.9 0.1 broadcast_select_fusion
  29.9 3.8 %collective-permute-start.3 = (bf16[2,2,512,128]{3,2,1,0:T(8,128)(2,1)S(1)}, bf16[2,2,512,128]{3,2,1,0:T(8,128)(2,1)S(1)}, u32[]{:S(2)}, u32[]{:S(2)}) collective-permute-start(bf16[2,2,512,128]{3,2,1,0:T(8,128)(2,1)S(1)} %broadcast_select_fusion), channel_id=1, source_target_pairs={{0,4},{2,6},{4,8},{6,10},{8,12},{10,14},{1,5},{3,7},{5,9},{7,11},{... | collective-permute-start | bytes 1572872 | tf_op jit(solution)/shard_map/ppermute | solution.py:657
  33.7 0.0 collective-permute-done.1.refs_1_
  33.7 3.8 %filterbank_early.2 = (bf16[2,16,2,16,128]{4,3,2,1,0:T(8,128)(2,1)S(1)}, bf16[2,16,2,16,128]{4,3,2,1,0:T(8,128)(2,1)S(1)}, bf16[2,16,2,16,128]{4,3,2,1,0:T(8,128)(2,1)S(1)}, bf16[2,16,2,16,128]{4,3,2,1,0:T(8,128)(2,1)S(1)}) custom-call(s32[8]{0:T(128)S(1)} %copy-done.6, bf16[2,2,512,128]{3,2,1,0:T(8,128)(2,1)S(1)} %collective-permute-done.1.refs_1_, ...), custom_call_target="tpu_custom_call" | custom-call | flops 1000000 | bytes 262144 | tf_op jit(solution)/shard_map/filterbank_early/pallas_call | solution.py:310
  37.5 2.5 %collective-permute-start.6 = (bf16[2,16,2,16,128]{4,3,2,1,0:T(8,128)(2,1)S(1)}, bf16[2,16,2,16,128]{4,3,2,1,0:T(8,128)(2,1)S(1)}, u32[]{:S(2)}, u32[]{:S(2)}) collective-permute-start(bf16[2,16,2,16,128]{4,3,2,1,0:T(8,128)(2,1)S(1)} %get-tuple-element.74), channel_id=1, source_target_pairs={{0,3},{1,2},{2,1},{3,0},{4,7},{5,6},{6,5},{7,4},{8,11},{9,10},{10,... | collective-permute-start | bytes 786440 | tf_op jit(solution)/shard_map/ppermute | solution.py:677
  40.0 0.5 collective-permute-start.5
  40.6 0.5 collective-permute-start.4
  41.1 3.7 %filterbank_late.3 = (bf16[2,8,2,16,128]{4,3,2,1,0:T(8,128)(2,1)S(1)}, bf16[2,8,2,16,128]{4,3,2,1,0:T(8,128)(2,1)S(1)}, bf16[2,8,2,16,128]{4,3,2,1,0:T(8,128)(2,1)S(1)}, bf16[2,8,2,16,128]{4,3,2,1,0:T(8,128)(2,1)S(1)}) custom-call(s32[8]{0:T(128)S(1)} %copy-done.6, bf16[2,2,512,128]{3,2,1,0:T(8,128)(2,1)S(1)} %get-tuple-element.61.refs_1_.refs_2_, ...), custom_call_target="tpu_custom_call" | custom-call | flops 1000000 | bytes 262144 | tf_op jit(solution)/shard_map/filterbank_late/pallas_call | solution.py:310
  44.8 4.0 %filterbank_early.3 = (bf16[2,16,2,16,128]{4,3,2,1,0:T(8,128)(2,1)S(1)}, bf16[2,16,2,16,128]{4,3,2,1,0:T(8,128)(2,1)S(1)}, bf16[2,16,2,16,128]{4,3,2,1,0:T(8,128)(2,1)S(1)}, bf16[2,16,2,16,128]{4,3,2,1,0:T(8,128)(2,1)S(1)}) custom-call(s32[8]{0:T(128)S(1)} %copy-done.6, bf16[2,2,512,128]{3,2,1,0:T(8,128)(2,1)S(1)} %collective-permute-done.3.refs_1_, ...), custom_call_target="tpu_custom_call" | custom-call | flops 1000000 | bytes 262144 | tf_op jit(solution)/shard_map/filterbank_early/pallas_call | solution.py:310
  48.8 2.3 %collective-permute-done.5.refs_2_ = bf16[2,16,2,16,128]{4,3,2,1,0:T(8,128)(2,1)S(1)} collective-permute-done((bf16[2,16,2,16,128]{4,3,2,1,0:T(8,128)(2,1)S(1)}, bf16[2,16,2,16,128]{4,3,2,1,0:T(8,128)(2,1)S(1)}, u32[]{:S(2)}, u32[]{:S(2)}) %collective-permute-start.5) | collective-permute-done | bytes 262176 | tf_op jit(solution)/shard_map/ppermute | solution.py:677
  51.1 0.2 join.2.refs_0_
  51.3 0.1 collective-permute-start.7
  51.4 2.4 %collective-permute-start.11 = (bf16[2,16,2,16,128]{4,3,2,1,0:T(8,128)(2,1)S(1)}, bf16[2,16,2,16,128]{4,3,2,1,0:T(8,128)(2,1)S(1)}, u32[]{:S(2)}, u32[]{:S(2)}) collective-permute-start(bf16[2,16,2,16,128]{4,3,2,1,0:T(8,128)(2,1)S(1)} %get-tuple-element.85), channel_id=1, source_target_pairs={{0,3},{1,2},{2,1},{3,0},{4,7},{5,6},{6,5},{7,4},{8,11},{9,10},{10,... | collective-permute-start | bytes 786440 | tf_op jit(solution)/shard_map/ppermute | solution.py:677
  53.8 0.5 collective-permute-start.10
  54.3 0.6 collective-permute-start.9
  54.9 0.0 collective-permute-done.7.refs_1_.refs_2_
  54.9 4.0 %correlate_early.1 = (f32[272,128]{1,0:T(8,128)S(1)}, bf16[272,128]{1,0:T(8,128)(2,1)S(1)}, bf16[272,128]{1,0:T(8,128)(2,1)S(1)}, bf16[272,128]{1,0:T(8,128)(2,1)S(1)}) custom-call(bf16[8,16,2,16,128]{4,3,2,1,0:T(8,128)(2,1)S(1)} %join.2.refs_0_, bf16[8,16,2,16,128]{4,3,2,1,0:T(8,128)(2,1)S(1)} %collective-permute-done.7.refs_1_.refs_2_), custom_call_target="tpu_custom_call" | custom-call | flops 1000000 | bytes 262144 | tf_op jit(solution)/shard_map/correlate_early/pallas_call | solution.py:476
  58.9 1.8 %collective-permute-start.8 = (bf16[272,128]{1,0:T(8,128)(2,1)S(1)}, bf16[272,128]{1,0:T(8,128)(2,1)S(1)}, u32[]{:S(2)}, u32[]{:S(2)}) collective-permute-start(bf16[272,128]{1,0:T(8,128)(2,1)S(1)} %get-tuple-element.76), channel_id=1, source_target_pairs={{0,12},{2,14},{4,8},{6,10},{8,4},{10,6},{12,0},{14,2},{1,13},{3,15... | collective-permute-start | bytes 208904 | tf_op jit(solution)/shard_map/ppermute | solution.py:683
  60.7 0.8 collective-permute-done.11.refs_3_
  61.5 3.6 %collective-permute-done.8.refs_1_ = bf16[272,128]{1,0:T(8,128)(2,1)S(1)} collective-permute-done((bf16[272,128]{1,0:T(8,128)(2,1)S(1)}, bf16[272,128]{1,0:T(8,128)(2,1)S(1)}, u32[]{:S(2)}, u32[]{:S(2)}) %collective-permute-start.8) | collective-permute-done | bytes 69664 | tf_op jit(solution)/shard_map/ppermute | solution.py:683
  65.1 1.5 %collective-permute-done.10.refs_2_ = bf16[2,16,2,16,128]{4,3,2,1,0:T(8,128)(2,1)S(1)} collective-permute-done((bf16[2,16,2,16,128]{4,3,2,1,0:T(8,128)(2,1)S(1)}, bf16[2,16,2,16,128]{4,3,2,1,0:T(8,128)(2,1)S(1)}, u32[]{:S(2)}, u32[]{:S(2)}) %collective-permute-start.10) | collective-permute-done | bytes 262176 | tf_op jit(solution)/shard_map/ppermute | solution.py:677
  66.6 0.0 collective-permute-done.9.refs_1_
  66.6 0.2 join.3.refs_1_
  66.8 0.1 collective-permute-start.12
  66.9 2.6 %collective-permute-start.13 = (bf16[272,128]{1,0:T(8,128)(2,1)S(1)}, bf16[272,128]{1,0:T(8,128)(2,1)S(1)}, u32[]{:S(2)}, u32[]{:S(2)}) collective-permute-start(bf16[272,128]{1,0:T(8,128)(2,1)S(1)} %get-tuple-element.87), channel_id=1, source_target_pairs={{0,8},{2,10},{4,12},{6,14},{8,0},{10,2},{12,4},{14,6},{1,9},{3,11}... | collective-permute-start | bytes 208904 | tf_op jit(solution)/shard_map/ppermute | solution.py:683
  69.5 3.0 %far_own.1 = (bf16[400,128]{1,0:T(8,128)(2,1)S(1)}, bf16[400,128]{1,0:T(8,128)(2,1)S(1)}) custom-call(bf16[8,16,2,16,128]{4,3,2,1,0:T(8,128)(2,1)S(1)} %join.2.refs_0_, bf16[8,16,2,16,128]{4,3,2,1,0:T(8,128)(2,1)S(1)} %join.3.refs_1_), custom_call_target="tpu_custom_call" | custom-call | flops 1000000 | bytes 262144 | tf_op jit(solution)/shard_map/far_own/pallas_call | solution.py:476
  72.5 1.3 %collective-permute-done.13.refs_0_ = bf16[272,128]{1,0:T(8,128)(2,1)S(1)} collective-permute-done((bf16[272,128]{1,0:T(8,128)(2,1)S(1)}, bf16[272,128]{1,0:T(8,128)(2,1)S(1)}, u32[]{:S(2)}, u32[]{:S(2)}) %collective-permute-start.13) | collective-permute-done | bytes 69664 | tf_op jit(solution)/shard_map/ppermute | solution.py:683
  73.9 3.2 %far_cross.1 = (bf16[784,128]{1,0:T(8,128)(2,1)S(1)}, bf16[784,128]{1,0:T(8,128)(2,1)S(1)}) custom-call(bf16[8,16,2,16,128]{4,3,2,1,0:T(8,128)(2,1)S(1)} %join.2.refs_0_, bf16[8,16,2,16,128]{4,3,2,1,0:T(8,128)(2,1)S(1)} %join.3.refs_1_, bf16[8,16,2,16,128]{4,3,2,1,0:T(8,128)(2,1)S(1)} %collective-permute-done.7.refs_1_.refs_2_, ...), custom_call_target="tpu_custom_call" | custom-call | flops 1000000 | bytes 262144 | tf_op jit(solution)/shard_map/far_cross/pallas_call | solution.py:476
  77.0 0.3 collective-permute-start.16
  77.4 1.3 %collective-permute-start.15 = (bf16[784,128]{1,0:T(8,128)(2,1)S(1)}, bf16[784,128]{1,0:T(8,128)(2,1)S(1)}, u32[]{:S(2)}, u32[]{:S(2)}) collective-permute-start(bf16[784,128]{1,0:T(8,128)(2,1)S(1)} %get-tuple-element.91), channel_id=1, source_target_pairs={{0,8},{2,10},{4,12},{6,14},{8,0},{10,2},{12,4},{14,6},{1,9},{3,11}... | collective-permute-start | bytes 602120 | tf_op jit(solution)/shard_map/ppermute | solution.py:683
  78.7 5.9 %correlate_near.1 = (f32[1056,128]{1,0:T(8,128)S(1)}, bf16[1056,128]{1,0:T(8,128)(2,1)S(1)}) custom-call(bf16[8,16,2,16,128]{4,3,2,1,0:T(8,128)(2,1)S(1)} %join.2.refs_0_, bf16[8,16,2,16,128]{4,3,2,1,0:T(8,128)(2,1)S(1)} %join.3.refs_1_, bf16[8,16,2,16,128]{4,3,2,1,0:T(8,128)(2,1)S(1)} %collective-permute-done.7.refs_1_.refs_2_, ...), custom_call_target="tpu_custom_call" | custom-call | flops 1000000 | bytes 262144 | tf_op jit(solution)/shard_map/correlate_near/pallas_call | solution.py:476
  84.7 2.8 %collective-permute-start.14 = (bf16[1056,128]{1,0:T(8,128)(2,1)S(1)}, bf16[1056,128]{1,0:T(8,128)(2,1)S(1)}, u32[]{:S(2)}, u32[]{:S(2)}) collective-permute-start(bf16[1056,128]{1,0:T(8,128)(2,1)S(1)} %get-tuple-element.96), channel_id=1, source_target_pairs={{0,4},{2,6},{4,0},{6,2},{8,12},{10,14},{12,8},{14,10},{1,5},{3,7},... | collective-permute-start | bytes 811016 | tf_op jit(solution)/shard_map/ppermute | solution.py:683
  87.5 8.7 %collective-permute-done.15.refs_2_ = bf16[784,128]{1,0:T(8,128)(2,1)S(1)} collective-permute-done((bf16[784,128]{1,0:T(8,128)(2,1)S(1)}, bf16[784,128]{1,0:T(8,128)(2,1)S(1)}, u32[]{:S(2)}, u32[]{:S(2)}) %collective-permute-start.15) | collective-permute-done | bytes 200736 | tf_op jit(solution)/shard_map/ppermute | solution.py:683
  96.2 0.1 sum_far.1.refs_2_
  96.3 0.1 collective-permute-start.19
  96.3 0.4 collective-permute-done.14.refs_1_
  96.8 0.1 collective-permute-start.18
  96.8 1.8 %collective-permute-done.18.refs_4_ = bf16[1056,128]{1,0:T(8,128)(2,1)S(1)} collective-permute-done((bf16[1056,128]{1,0:T(8,128)(2,1)S(1)}, bf16[1056,128]{1,0:T(8,128)(2,1)S(1)}, u32[]{:S(2)}, u32[]{:S(2)}) %collective-permute-start.18) | collective-permute-done | bytes 270368 | tf_op jit(solution)/shard_map/ppermute | solution.py:710
  98.6 1.7 %assemble.1 = f32[2,16,32,256]{3,2,1,0:T(8,128)} custom-call(f32[1056,128]{1,0:T(8,128)S(1)} %get-tuple-element.95.refs_0_, bf16[1056,128]{1,0:T(8,128)(2,1)S(1)} %collective-permute-done.14.refs_1_, f32[1056,128]{1,0:T(8,128)S(1)} %sum_far.1.refs_2_, f32[1056,128]{1,0:T(8,128)S(1)} %collective-permute-done.17.refs_3_, ...), custom_call_target="tpu_custom_call" | custom-call | flops 1000000 | bytes 262144 | tf_op jit(solution)/shard_map/assemble/pallas_call | solution.py:598
  (21 shorter events, 0.0 us)
Async XLA Ops:
  0.0 23.6 %copy-start = (f32[16,64,128]{2,1,0:T(8,128)S(1)}, f32[16,64,128]{2,1,0:T(8,128)}, u32[]{:S(2)}) copy-start(f32[16,64,128]{2,1,0:T(8,128)} %constant.30.clone.refs_3_.refs_4_) | copy-start | bytes 1572868
  0.0 1.6 %copy-start.1 = (bf16[2,8,65536]{2,1,0:T(8,128)(2,1)S(1)}, bf16[2,8,65536]{2,1,0:T(8,128)(2,1)}, u32[]{:S(2)}) copy-start(bf16[2,8,65536]{2,1,0:T(8,128)(2,1)} %block.1) | copy-start | bytes 6291460
  1.7 22.0 %copy-start.2 = (bf16[2,4,32,128]{3,2,1,0:T(8,128)(2,1)S(1)}, bf16[2,4,32,128]{3,2,1,0:T(8,128)(2,1)}, u32[]{:S(2)}) copy-start(bf16[2,4,32,128]{3,2,1,0:T(8,128)(2,1)} %constant.34.clone.refs_7_.refs_8_) | copy-start | bytes 196612
  1.7 22.0 %copy-start.3 = (f32[64,128]{1,0:T(8,128)S(1)}, f32[64,128]{1,0:T(8,128)}, u32[]{:S(2)}) copy-start(f32[64,128]{1,0:T(8,128)} %constant.33.clone.refs_6_.refs_7_) | copy-start | bytes 98308
  1.7 22.0 %copy-start.4 = (f32[64,128]{1,0:T(8,128)S(1)}, f32[64,128]{1,0:T(8,128)}, u32[]{:S(2)}) copy-start(f32[64,128]{1,0:T(8,128)} %constant.32.clone.refs_5_.refs_6_) | copy-start | bytes 98308
  1.7 22.0 %copy-start.5 = (bf16[128,128]{1,0:T(8,128)(2,1)S(1)}, bf16[128,128]{1,0:T(8,128)(2,1)}, u32[]{:S(2)}) copy-start(bf16[128,128]{1,0:T(8,128)(2,1)} %constant.31.clone.refs_4_.refs_5_) | copy-start | bytes 98308
  1.7 22.0 %copy-start.6 = (s32[8]{0:T(128)S(1)}, s32[8]{0:T(128)}, u32[]{:S(2)}) copy-start(s32[8]{0:T(128)} %refs_0_.7) | copy-start | bytes 100
  3.6 15.9 %collective-permute-start = (bf16[2,2,512,128]{3,2,1,0:T(8,128)(2,1)}, bf16[2,2,512,128]{3,2,1,0:T(8,128)(2,1)S(1)}, u32[]{:S(2)}, u32[]{:S(2)}) collective-permute-start(bf16[2,2,512,128]{3,2,1,0:T(8,128)(2,1)} %get-tuple-element.53), channel_id=1, source_target_pairs={{0,2},{2,0},{4,6},{6,4},{8,10},{10,8},{12,14},{14,12},{1,3},{3,1},... | collective-permute-start | bytes 1572872 | tf_op jit(solution)/shard_map/ppermute | solution.py:653
  6.5 23.4 %collective-permute-start.2 = (bf16[2,2,512,128]{3,2,1,0:T(8,128)(2,1)S(1)}, bf16[2,2,512,128]{3,2,1,0:T(8,128)(2,1)S(1)}, u32[]{:S(2)}, u32[]{:S(2)}) collective-permute-start(bf16[2,2,512,128]{3,2,1,0:T(8,128)(2,1)S(1)} %get-tuple-element.54), channel_id=1, source_target_pairs={{0,2},{2,0},{4,6},{6,4},{8,10},{10,8},{12,14},{14,12},{1,3},{3,1},... | collective-permute-start | bytes 1572872 | tf_op jit(solution)/shard_map/ppermute | solution.py:653
  19.5 14.2 %collective-permute-start.1 = (bf16[2,2,512,128]{3,2,1,0:T(8,128)(2,1)S(1)}, bf16[2,2,512,128]{3,2,1,0:T(8,128)(2,1)S(1)}, u32[]{:S(2)}, u32[]{:S(2)}) collective-permute-start(bf16[2,2,512,128]{3,2,1,0:T(8,128)(2,1)S(1)} %broadcast_select_fusion.1), channel_id=1, source_target_pairs={{0,4},{2,6},{4,8},{6,10},{8,12},{10,14},{1,5},{3,7},{5,9},{7,11},{... | collective-permute-start | bytes 1572872 | tf_op jit(solution)/shard_map/ppermute | solution.py:657
  29.9 14.9 %collective-permute-start.3 = (bf16[2,2,512,128]{3,2,1,0:T(8,128)(2,1)S(1)}, bf16[2,2,512,128]{3,2,1,0:T(8,128)(2,1)S(1)}, u32[]{:S(2)}, u32[]{:S(2)}) collective-permute-start(bf16[2,2,512,128]{3,2,1,0:T(8,128)(2,1)S(1)} %broadcast_select_fusion), channel_id=1, source_target_pairs={{0,4},{2,6},{4,8},{6,10},{8,12},{10,14},{1,5},{3,7},{5,9},{7,11},{... | collective-permute-start | bytes 1572872 | tf_op jit(solution)/shard_map/ppermute | solution.py:657
  37.5 11.3 %collective-permute-start.6 = (bf16[2,16,2,16,128]{4,3,2,1,0:T(8,128)(2,1)S(1)}, bf16[2,16,2,16,128]{4,3,2,1,0:T(8,128)(2,1)S(1)}, u32[]{:S(2)}, u32[]{:S(2)}) collective-permute-start(bf16[2,16,2,16,128]{4,3,2,1,0:T(8,128)(2,1)S(1)} %get-tuple-element.74), channel_id=1, source_target_pairs={{0,3},{1,2},{2,1},{3,0},{4,7},{5,6},{6,5},{7,4},{8,11},{9,10},{10,... | collective-permute-start | bytes 786440 | tf_op jit(solution)/shard_map/ppermute | solution.py:677
  40.0 11.1 %collective-permute-start.5 = (bf16[2,16,2,16,128]{4,3,2,1,0:T(8,128)(2,1)S(1)}, bf16[2,16,2,16,128]{4,3,2,1,0:T(8,128)(2,1)S(1)}, u32[]{:S(2)}, u32[]{:S(2)}) collective-permute-start(bf16[2,16,2,16,128]{4,3,2,1,0:T(8,128)(2,1)S(1)} %get-tuple-element.72), channel_id=1, source_target_pairs={{0,2},{1,3},{2,0},{3,1},{4,6},{5,7},{6,4},{7,5},{8,10},{9,11},{10,... | collective-permute-start | bytes 786440 | tf_op jit(solution)/shard_map/ppermute | solution.py:677
  40.6 10.5 %collective-permute-start.4 = (bf16[2,16,2,16,128]{4,3,2,1,0:T(8,128)(2,1)S(1)}, bf16[2,16,2,16,128]{4,3,2,1,0:T(8,128)(2,1)S(1)}, u32[]{:S(2)}, u32[]{:S(2)}) collective-permute-start(bf16[2,16,2,16,128]{4,3,2,1,0:T(8,128)(2,1)S(1)} %get-tuple-element.70), channel_id=1, source_target_pairs={{0,1},{1,0},{2,3},{3,2},{4,5},{5,4},{6,7},{7,6},{8,9},{9,8},{10,11... | collective-permute-start | bytes 786440 | tf_op jit(solution)/shard_map/ppermute | solution.py:677
  51.3 3.6 %collective-permute-start.7 = (bf16[8,16,2,16,128]{4,3,2,1,0:T(8,128)(2,1)S(1)}, bf16[8,16,2,16,128]{4,3,2,1,0:T(8,128)(2,1)S(1)}, u32[]{:S(2)}, u32[]{:S(2)}) collective-permute-start(bf16[8,16,2,16,128]{4,3,2,1,0:T(8,128)(2,1)S(1)} %join.2.refs_0_), channel_id=1, source_target_pairs={{0,16},{16,0},{1,17},{17,1},{2,18},{18,2},{3,19},{19,3},{4,20},{20... | collective-permute-start | bytes 3145736 | tf_op jit(solution)/shard_map/ppermute | solution.py:686
  51.4 10.1 %collective-permute-start.11 = (bf16[2,16,2,16,128]{4,3,2,1,0:T(8,128)(2,1)S(1)}, bf16[2,16,2,16,128]{4,3,2,1,0:T(8,128)(2,1)S(1)}, u32[]{:S(2)}, u32[]{:S(2)}) collective-permute-start(bf16[2,16,2,16,128]{4,3,2,1,0:T(8,128)(2,1)S(1)} %get-tuple-element.85), channel_id=1, source_target_pairs={{0,3},{1,2},{2,1},{3,0},{4,7},{5,6},{6,5},{7,4},{8,11},{9,10},{10,... | collective-permute-start | bytes 786440 | tf_op jit(solution)/shard_map/ppermute | solution.py:677
  53.8 12.8 %collective-permute-start.10 = (bf16[2,16,2,16,128]{4,3,2,1,0:T(8,128)(2,1)S(1)}, bf16[2,16,2,16,128]{4,3,2,1,0:T(8,128)(2,1)S(1)}, u32[]{:S(2)}, u32[]{:S(2)}) collective-permute-start(bf16[2,16,2,16,128]{4,3,2,1,0:T(8,128)(2,1)S(1)} %get-tuple-element.82), channel_id=1, source_target_pairs={{0,2},{1,3},{2,0},{3,1},{4,6},{5,7},{6,4},{7,5},{8,10},{9,11},{10,... | collective-permute-start | bytes 786440 | tf_op jit(solution)/shard_map/ppermute | solution.py:677
  54.3 12.3 %collective-permute-start.9 = (bf16[2,16,2,16,128]{4,3,2,1,0:T(8,128)(2,1)S(1)}, bf16[2,16,2,16,128]{4,3,2,1,0:T(8,128)(2,1)S(1)}, u32[]{:S(2)}, u32[]{:S(2)}) collective-permute-start(bf16[2,16,2,16,128]{4,3,2,1,0:T(8,128)(2,1)S(1)} %get-tuple-element.79), channel_id=1, source_target_pairs={{0,1},{1,0},{2,3},{3,2},{4,5},{5,4},{6,7},{7,6},{8,9},{9,8},{10,11... | collective-permute-start | bytes 786440 | tf_op jit(solution)/shard_map/ppermute | solution.py:677
  58.9 6.2 %collective-permute-start.8 = (bf16[272,128]{1,0:T(8,128)(2,1)S(1)}, bf16[272,128]{1,0:T(8,128)(2,1)S(1)}, u32[]{:S(2)}, u32[]{:S(2)}) collective-permute-start(bf16[272,128]{1,0:T(8,128)(2,1)S(1)} %get-tuple-element.76), channel_id=1, source_target_pairs={{0,12},{2,14},{4,8},{6,10},{8,4},{10,6},{12,0},{14,2},{1,13},{3,15... | collective-permute-start | bytes 208904 | tf_op jit(solution)/shard_map/ppermute | solution.py:683
  66.8 7.1 %collective-permute-start.12 = (bf16[8,16,2,16,128]{4,3,2,1,0:T(8,128)(2,1)S(1)}, bf16[8,16,2,16,128]{4,3,2,1,0:T(8,128)(2,1)S(1)}, u32[]{:S(2)}, u32[]{:S(2)}) collective-permute-start(bf16[8,16,2,16,128]{4,3,2,1,0:T(8,128)(2,1)S(1)} %join.3.refs_1_), channel_id=1, source_target_pairs={{0,16},{16,0},{1,17},{17,1},{2,18},{18,2},{3,19},{19,3},{4,20},{20... | collective-permute-start | bytes 3145736 | tf_op jit(solution)/shard_map/ppermute | solution.py:693
  66.9 7.0 %collective-permute-start.13 = (bf16[272,128]{1,0:T(8,128)(2,1)S(1)}, bf16[272,128]{1,0:T(8,128)(2,1)S(1)}, u32[]{:S(2)}, u32[]{:S(2)}) collective-permute-start(bf16[272,128]{1,0:T(8,128)(2,1)S(1)} %get-tuple-element.87), channel_id=1, source_target_pairs={{0,8},{2,10},{4,12},{6,14},{8,0},{10,2},{12,4},{14,6},{1,9},{3,11}... | collective-permute-start | bytes 208904 | tf_op jit(solution)/shard_map/ppermute | solution.py:683
  77.0 10.5 %collective-permute-start.16 = (bf16[784,128]{1,0:T(8,128)(2,1)S(1)}, bf16[784,128]{1,0:T(8,128)(2,1)S(1)}, u32[]{:S(2)}, u32[]{:S(2)}) collective-permute-start(bf16[784,128]{1,0:T(8,128)(2,1)S(1)} %get-tuple-element.97), channel_id=1, source_target_pairs={{0,12},{2,14},{4,8},{6,10},{8,4},{10,6},{12,0},{14,2},{1,13},{3,15... | collective-permute-start | bytes 602120 | tf_op jit(solution)/shard_map/ppermute | solution.py:683
  77.4 18.8 %collective-permute-start.15 = (bf16[784,128]{1,0:T(8,128)(2,1)S(1)}, bf16[784,128]{1,0:T(8,128)(2,1)S(1)}, u32[]{:S(2)}, u32[]{:S(2)}) collective-permute-start(bf16[784,128]{1,0:T(8,128)(2,1)S(1)} %get-tuple-element.91), channel_id=1, source_target_pairs={{0,8},{2,10},{4,12},{6,14},{8,0},{10,2},{12,4},{14,6},{1,9},{3,11}... | collective-permute-start | bytes 602120 | tf_op jit(solution)/shard_map/ppermute | solution.py:683
  84.7 12.1 %collective-permute-start.14 = (bf16[1056,128]{1,0:T(8,128)(2,1)S(1)}, bf16[1056,128]{1,0:T(8,128)(2,1)S(1)}, u32[]{:S(2)}, u32[]{:S(2)}) collective-permute-start(bf16[1056,128]{1,0:T(8,128)(2,1)S(1)} %get-tuple-element.96), channel_id=1, source_target_pairs={{0,4},{2,6},{4,0},{6,2},{8,12},{10,14},{12,8},{14,10},{1,5},{3,7},... | collective-permute-start | bytes 811016 | tf_op jit(solution)/shard_map/ppermute | solution.py:683
  87.5 11.1 %collective-permute-start.17 = (f32[1056,128]{1,0:T(8,128)S(1)}, f32[1056,128]{1,0:T(8,128)S(1)}, u32[]{:S(2)}, u32[]{:S(2)}) collective-permute-start(f32[1056,128]{1,0:T(8,128)S(1)} %get-tuple-element.95.refs_0_), channel_id=1, source_target_pairs={{0,16},{16,0},{1,17},{17,1},{2,18},{18,2},{3,19},{19,3},{4,20},{20... | collective-permute-start | bytes 1622024 | tf_op jit(solution)/shard_map/ppermute | solution.py:710
  96.3 2.4 %collective-permute-start.19 = (f32[1056,128]{1,0:T(8,128)S(1)}, f32[1056,128]{1,0:T(8,128)S(1)}, u32[]{:S(2)}, u32[]{:S(2)}) collective-permute-start(f32[1056,128]{1,0:T(8,128)S(1)} %sum_far.1.refs_2_), channel_id=1, source_target_pairs={{0,16},{16,0},{1,17},{17,1},{2,18},{18,2},{3,19},{19,3},{4,20},{20... | collective-permute-start | bytes 1622024 | tf_op jit(solution)/shard_map/ppermute | solution.py:710
  96.8 1.9 %collective-permute-start.18 = (bf16[1056,128]{1,0:T(8,128)(2,1)S(1)}, bf16[1056,128]{1,0:T(8,128)(2,1)S(1)}, u32[]{:S(2)}, u32[]{:S(2)}) collective-permute-start(bf16[1056,128]{1,0:T(8,128)(2,1)S(1)} %collective-permute-done.14.refs_1_), channel_id=1, source_target_pairs={{0,16},{16,0},{1,17},{17,1},{2,18},{18,2},{3,19},{19,3},{4,20},{20... | collective-permute-start | bytes 811016 | tf_op jit(solution)/shard_map/ppermute | solution.py:710
